TPU v7x, 32 devices: a whole 2x2x4 slice. The times are simulated.
32 devices in a mesh: span: 16 (over z, y, x), width: 2 (over core).
Axes of the slice: x: 2, y: 2, z: 4, core: 2. Of those that a mesh axis runs over, the one named last changes fastest.
Arguments:
- right_side: float32 [32, 128, 1024], P(None, 'span', 'width'), may hold values from -6 to 6
- diffusivity: float32 [32, 128, 1024], P(None, 'span', 'width'), may hold values from 0.2 to 5
- reaction: float32 [32, 128, 1024], P(None, 'span', 'width'), may hold values from 0.01 to 0.2
Outputs:
- correction: float32 [32, 128, 1024], P(None, 'span', 'width')
All inputs are finite; a program needn't handle non-finite values.
Results may differ from a plain program's by a relative error of at most 0.0003.
Values sent between devices are 32-bit elements; how exact they have to be, the bound alone decides.
No kernel may reach another device: no remote copies, remote signals or barrier semaphores. Data moves between devices by JAX's collectives and lax.ppermute only.
A program may use at most 128 MiB of HBM per device.

v0:
```python
import jax
import jax.numpy as jnp
from jax import lax
from jax.sharding import PartitionSpec as P

LEVELS = 6
COARSE_SWEEPS = 3


relax_weight = 0.8


def with_halo(cells, sides, width):
    for axis, dim in sides:
        count = lax.axis_size(axis)
        ends = count - 1
        head = lax.slice_in_dim(cells, 0, width, axis=dim)
        tail = lax.slice_in_dim(cells, cells.shape[dim] - width, cells.shape[dim], axis=dim)
        cells = jnp.concatenate(
            [
                lax.ppermute(tail, axis, [(i, (i + 1) % count) for i in range(ends)]),
                cells,
                lax.ppermute(head, axis, [((i + 1) % count, i) for i in range(ends)]),
            ],
            axis=dim,
        )
    return cells


def from_behind(value, axis, steps):
    count = lax.axis_size(axis)
    initial, last = (max(0, -steps), min(count, count - steps))
    return lax.ppermute(value, axis, [(source, source + steps) for source in range(initial, last)])


def partner_2(block, axis, distance):
    count = lax.axis_size(axis)
    route = []
    for low in range(count):
        high = low | 1 << distance
        if high != low and high < count:
            route += [(low, high), (high, low)]
    return lax.ppermute(block, axis, route)


def harmonic(first, second):
    return 2.0 * first * second / (first + second)


def level_group(cells_x, grid_level):
    return max(1, 4 * 2**grid_level // cells_x)


def layout(cells_x, grid_level, span_count):
    group_size = level_group(cells_x, grid_level)
    span_whole = group_size >= span_count
    return (group_size, span_whole, False)


def extend(field, grid_level, cells_x, span_count):
    group_size, span_whole, width_whole = layout(cells_x, grid_level, span_count)
    if group_size == 1 and (not span_whole) and (not width_whole):
        return with_halo(field, (("span", 1), ("width", 2)), 1)
    widened = with_halo(field, (("width", 2),), 1)
    if span_whole:
        return jnp.pad(widened, ((0, 0), (1, 1), (0, 0)))
    below_plane = from_behind(widened[:, -1:, :], "span", group_size)
    above_plane = from_behind(widened[:, :1, :], "span", -group_size)
    return jnp.concatenate([below_plane, widened, above_plane], axis=1)


def face_terms(conduct, binding, grid_level, cells_x, span_count):
    padded = extend(conduct, grid_level, cells_x, span_count)
    depth_pad = jnp.pad(conduct, ((1, 1), (0, 0), (0, 0)))
    face_scale = 0.25**grid_level
    west = face_scale * harmonic(conduct, padded[:, :-2, 1:-1])
    east = face_scale * harmonic(conduct, padded[:, 2:, 1:-1])
    south = face_scale * harmonic(conduct, padded[:, 1:-1, :-2])
    north = face_scale * harmonic(conduct, padded[:, 1:-1, 2:])
    upward = face_scale * harmonic(conduct, depth_pad[:-2])
    downward = face_scale * harmonic(conduct, depth_pad[2:])
    diagonal = west + east + south + north + upward + downward + face_scale * binding
    return (west, east, south, north, upward, downward, diagonal)


def operate(field, coeffs, grid_level, cells_x, span_count):
    padded = extend(field, grid_level, cells_x, span_count)
    depth_pad = jnp.pad(field, ((1, 1), (0, 0), (0, 0)))
    beside = coeffs[0] * padded[:, :-2, 1:-1] + coeffs[1] * padded[:, 2:, 1:-1]
    beside = beside + coeffs[2] * padded[:, 1:-1, :-2] + coeffs[3] * padded[:, 1:-1, 2:]
    beside = beside + coeffs[4] * depth_pad[:-2] + coeffs[5] * depth_pad[2:]
    return coeffs[6] * field - beside


def restrict(field):
    depth, first, second = field.shape
    return jnp.mean(field.reshape(depth, first // 2, 2, second // 2, 2), axis=(2, 4))


def pair_up(fields, group_size):
    bit_index = group_size.bit_length() - 1
    stacked = jnp.stack(fields)
    partner = partner_2(stacked, "span", bit_index)
    upper_half = lax.axis_index("span") // group_size % 2 == 1
    joined = jnp.where(
        upper_half,
        jnp.concatenate([partner, stacked], axis=2),
        jnp.concatenate([stacked, partner], axis=2),
    )
    return tuple((joined[position] for position in range(len(fields))))


def descend(fields, grid_level, cells_x):
    coarse = tuple((restrict(field) for field in fields))
    group_now = level_group(cells_x, grid_level)
    group_next = level_group(cells_x, grid_level + 1)
    if group_next > group_now:
        coarse = pair_up(coarse, group_now)
    return tuple(coarse)


def prolong(coarse, fine_shape, grid_level, cells_x, span_count):
    group_fine, whole_fine, width_fine = layout(cells_x, grid_level, span_count)
    group_coarse, whole_coarse, width_coarse = layout(cells_x, grid_level + 1, span_count)
    group_coarse = span_count if whole_coarse else group_coarse
    depth, extent_x, extent_y = fine_shape
    span_at = lax.axis_index("span")
    offset_x = span_at // group_fine * (extent_x // 2) - span_at // group_coarse * coarse.shape[1]
    offset_y = jnp.zeros((), jnp.int32)
    coarse_part = lax.dynamic_slice(
        coarse,
        (jnp.zeros((), jnp.int32), offset_x, offset_y),
        (depth, extent_x // 2, extent_y // 2),
    )
    return jnp.repeat(jnp.repeat(coarse_part, 2, axis=1), 2, axis=2)


def on_device(right_side, diffusivity, reaction):
    cells_x = diffusivity.shape[1]
    span_count = lax.axis_size("span")
    conduct = diffusivity
    binding = reaction
    all_coeffs = []
    for grid_level in range(LEVELS):
        all_coeffs.append(face_terms(conduct, binding, grid_level, cells_x, span_count))
        if grid_level < LEVELS - 1:
            conduct, binding = descend((conduct, binding), grid_level, cells_x)
    source = right_side
    saved = []
    for grid_level in range(LEVELS - 1):
        coeffs = all_coeffs[grid_level]
        smooth_one = relax_weight * source / coeffs[6]
        defect = source - operate(smooth_one, coeffs, grid_level, cells_x, span_count)
        saved.append((source, smooth_one))
        source = descend((defect,), grid_level, cells_x)[0]
    coeffs = all_coeffs[LEVELS - 1]
    iterate = relax_weight * source / coeffs[6]
    for sweep_index in range(COARSE_SWEEPS - 1):
        iterate = (
            iterate
            + relax_weight
            * (source - operate(iterate, coeffs, LEVELS - 1, cells_x, span_count))
            / coeffs[6]
        )
    for grid_level in range(LEVELS - 2, -1, -1):
        source, smooth_one = saved[grid_level]
        coeffs = all_coeffs[grid_level]
        lifted = smooth_one + prolong(iterate, smooth_one.shape, grid_level, cells_x, span_count)
        iterate = (
            lifted
            + relax_weight
            * (source - operate(lifted, coeffs, grid_level, cells_x, span_count))
            / coeffs[6]
        )
    return iterate


def solution(mesh):
    in_specs = (P(None, "span", "width"), P(None, "span", "width"), P(None, "span", "width"))
    out_specs = P(None, "span", "width")
    return jax.shard_map(
        on_device, mesh=mesh, in_specs=in_specs, out_specs=out_specs, check_vma=False
    )
```

profile of v0, /device:TPU:0, one launch (start us, length us, event | category | flops | bytes accessed | tf_op | source)
XLA Modules:
  0.0 386.1 jit_solution(13410028284701376200)
XLA Ops:
  2.0 4.8 %collective-permute-start = (f32[32,1,512]{2,1,0:T(1,128)}, f32[32,1,512]{2,1,0:T(1,128)S(1)}, u32[]{:S(2)}, u32[]{:S(2)}) collective-permute-start(f32[32,1,512]{2,1,0:T(1,128)} %get-tuple-element.43), channel_id=1, source_target_pairs={{0,2},{2,4},{4,6},{6,8},{8,10},{10,12},{12,14},{14,16},{16,18},{18... | collective-permute-start | bytes 196616 | tf_op jit(solution)/shard_map/ppermute | solution.py:21
  12.4 5.1 %collective-permute-start.8 = (f32[32,1,256]{2,0,1:T(8,128)}, f32[32,1,256]{2,0,1:T(8,128)}, u32[]{:S(2)}, u32[]{:S(2)}) collective-permute-start(f32[32,1,256]{2,0,1:T(8,128)} %get-tuple-element.90), channel_id=1, source_target_pairs={{0,2},{2,4},{4,6},{6,8},{8,10},{10,12},{12,14},{14,16},{16,18},{18... | collective-permute-start | bytes 98312 | tf_op jit(solution)/shard_map/ppermute | solution.py:21
  24.9 3.3 reduce_sum.137
  32.9 4.6 %collective-permute-start.4 = (f32[32,1,512]{2,1,0:T(1,128)S(1)}, f32[32,1,512]{2,1,0:T(1,128)S(1)}, u32[]{:S(2)}, u32[]{:S(2)}) collective-permute-start(f32[32,1,512]{2,1,0:T(1,128)S(1)} %get-tuple-element.40), channel_id=1, source_target_pairs={{0,2},{2,4},{4,6},{6,8},{8,10},{10,12},{12,14},{14,16},{16,18},{18... | collective-permute-start | bytes 196616 | tf_op jit(solution)/shard_map/ppermute | solution.py:21
  39.9 5.2 %collective-permute-done.5 = f32[32,1,512]{2,1,0:T(1,128)S(1)} collective-permute-done((f32[32,1,512]{2,1,0:T(1,128)S(1)}, f32[32,1,512]{2,1,0:T(1,128)S(1)}, u32[]{:S(2)}, u32[]{:S(2)}) %collective-permute-start.5) | collective-permute-done | bytes 65568 | tf_op jit(solution)/shard_map/ppermute | solution.py:23
  60.3 4.1 %reduce_sum.135 = f32[32,4,256]{0,2,1:T(8,128)} reduce(f32[32,4,2,256,2]{0,4,3,2,1:T(2,128)} %bitcast.108, f32[]{:T(128)} %constant.153.clone.1), dimensions={2,4}, to_apply=%region_0.1 | reduce | flops 98304 | bytes 655364 | tf_op jit(solution)/shard_map/reduce_sum | solution.py:97
  69.8 4.7 %collective-permute-start.12 = (f32[32,1,256]{2,0,1:T(8,128)}, f32[32,1,256]{2,0,1:T(8,128)S(1)}, u32[]{:S(2)}, u32[]{:S(2)}) collective-permute-start(f32[32,1,256]{2,0,1:T(8,128)} %get-tuple-element.87), channel_id=1, source_target_pairs={{0,2},{2,4},{4,6},{6,8},{8,10},{10,12},{12,14},{14,16},{16,18},{18... | collective-permute-start | bytes 98312 | tf_op jit(solution)/shard_map/ppermute | solution.py:21
  108.9 5.9 %collective-permute-start.20 = (f32[32,1,130]{2,0,1:T(8,128)S(1)}, f32[32,1,130]{2,0,1:T(8,128)S(1)}, u32[]{:S(2)}, u32[]{:S(2)}) collective-permute-start(f32[32,1,130]{2,0,1:T(8,128)S(1)} %get-tuple-element.69), channel_id=1, source_target_pairs={{0,4},{2,6},{4,8},{6,10},{8,12},{10,14},{12,16},{14,18},{16,20},{1... | collective-permute-start | bytes 49928 | tf_op jit(solution)/shard_map/ppermute | solution.py:33
  117.0 3.7 collective-permute-done.21
  130.7 3.4 collective-permute-start.24
  150.0 3.9 %collective-permute-start.37 = (f32[2,32,2,32]{1,3,2,0:T(8,128)}, f32[2,32,2,32]{1,3,2,0:T(8,128)}, u32[]{:S(2)}, u32[]{:S(2)}) collective-permute-start(f32[2,32,2,32]{1,3,2,0:T(8,128)} %pad_maximum_fusion.113), channel_id=1, source_target_pairs={{0,8},{8,0},{2,10},{10,2},{4,12},{12,4},{6,14},{14,6},{16,24},{24,... | collective-permute-start | bytes 49160 | tf_op jit(solution)/shard_map/ppermute | solution.py:43
  186.2 4.2 %collective-permute-start.32 = (f32[32,4,1]{0,2,1:T(1,128)}, f32[32,4,1]{0,2,1:T(1,128)}, u32[]{:S(2)}, u32[]{:S(2)}) collective-permute-start(f32[32,4,1]{0,2,1:T(1,128)} %get-tuple-element.80), channel_id=1, source_target_pairs={{0,1},{2,3},{4,5},{6,7},{8,9},{10,11},{12,13},{14,15},{16,17},{18,... | collective-permute-start | bytes 1544 | tf_op jit(solution)/shard_map/ppermute | solution.py:21
  200.1 4.2 %collective-permute-start.34 = (f32[32,1,66]{2,0,1:T(8,128)S(1)}, f32[32,1,66]{2,0,1:T(8,128)S(1)}, u32[]{:S(2)}, u32[]{:S(2)}) collective-permute-start(f32[32,1,66]{2,0,1:T(8,128)S(1)} %get-tuple-element.59), channel_id=1, source_target_pairs={{0,8},{2,10},{4,12},{6,14},{8,16},{10,18},{12,20},{14,22},{16,24},... | collective-permute-start | bytes 25352 | tf_op jit(solution)/shard_map/ppermute | solution.py:33
  207.0 4.6 %collective-permute-start.40 = (f32[32,1,34]{0,2,1:T(8,128)}, f32[32,1,34]{0,2,1:T(8,128)}, u32[]{:S(2)}, u32[]{:S(2)}) collective-permute-start(f32[32,1,34]{0,2,1:T(8,128)} %get-tuple-element.96), channel_id=1, source_target_pairs={{0,16},{2,18},{4,20},{6,22},{8,24},{10,26},{12,28},{14,30},{1,17},... | collective-permute-start | bytes 13064 | tf_op jit(solution)/shard_map/ppermute | solution.py:33
  233.5 5.0 %collective-permute-start.44 = (f32[32,1,34]{0,2,1:T(8,128)S(1)}, f32[32,1,34]{0,2,1:T(8,128)S(1)}, u32[]{:S(2)}, u32[]{:S(2)}) collective-permute-start(f32[32,1,34]{0,2,1:T(8,128)S(1)} %get-tuple-element.94), channel_id=1, source_target_pairs={{0,16},{2,18},{4,20},{6,22},{8,24},{10,26},{12,28},{14,30},{1,17},... | collective-permute-start | bytes 13064 | tf_op jit(solution)/shard_map/ppermute | solution.py:33
  279.6 4.3 %collective-permute-start.56 = (f32[32,1,34]{0,2,1:T(8,128)S(1)}, f32[32,1,34]{0,2,1:T(8,128)S(1)}, u32[]{:S(2)}, u32[]{:S(2)}) collective-permute-start(f32[32,1,34]{0,2,1:T(8,128)S(1)} %get-tuple-element.92), channel_id=1, source_target_pairs={{0,16},{2,18},{4,20},{6,22},{8,24},{10,26},{12,28},{14,30},{1,17},... | collective-permute-start | bytes 13064 | tf_op jit(solution)/shard_map/ppermute | solution.py:33
  286.1 4.3 %collective-permute-done.57 = f32[32,1,34]{0,2,1:T(8,128)S(1)} collective-permute-done((f32[32,1,34]{0,2,1:T(8,128)S(1)}, f32[32,1,34]{0,2,1:T(8,128)S(1)}, u32[]{:S(2)}, u32[]{:S(2)}) %collective-permute-start.57) | collective-permute-done | bytes 4384 | tf_op jit(solution)/shard_map/ppermute | solution.py:33
  302.0 3.5 collective-permute-start.60
  306.8 4.7 %collective-permute-done.61 = f32[32,1,66]{2,0,1:T(8,128)} collective-permute-done((f32[32,1,66]{2,0,1:T(8,128)}, f32[32,1,66]{2,0,1:T(8,128)}, u32[]{:S(2)}, u32[]{:S(2)}) %collective-permute-start.61) | collective-permute-done | bytes 8480 | tf_op jit(solution)/shard_map/ppermute | solution.py:33
  328.1 3.6 collective-permute-start.64
  333.2 4.2 %collective-permute-done.65 = f32[32,1,130]{2,0,1:T(8,128)S(1)} collective-permute-done((f32[32,1,130]{2,0,1:T(8,128)S(1)}, f32[32,1,130]{2,0,1:T(8,128)S(1)}, u32[]{:S(2)}, u32[]{:S(2)}) %collective-permute-start.65) | collective-permute-done | bytes 16672 | tf_op jit(solution)/shard_map/ppermute | solution.py:33
  349.0 4.2 %collective-permute-done.67 = f32[32,1,256]{2,0,1:T(8,128)S(1)} collective-permute-done((f32[32,1,256]{2,0,1:T(8,128)S(1)}, f32[32,1,256]{2,0,1:T(8,128)S(1)}, u32[]{:S(2)}, u32[]{:S(2)}) %collective-permute-start.67) | collective-permute-done | bytes 32800 | tf_op jit(solution)/shard_map/ppermute | solution.py:23
  367.5 4.6 %collective-permute-start.70 = (f32[32,1,512]{2,1,0:T(1,128)S(1)}, f32[32,1,512]{2,1,0:T(1,128)S(1)}, u32[]{:S(2)}, u32[]{:S(2)}) collective-permute-start(f32[32,1,512]{2,1,0:T(1,128)S(1)} %get-tuple-element.38), channel_id=1, source_target_pairs={{0,2},{2,4},{4,6},{6,8},{8,10},{10,12},{12,14},{14,16},{16,18},{18... | collective-permute-start | bytes 196616 | tf_op jit(solution)/shard_map/ppermute | solution.py:21
  374.3 4.0 %collective-permute-done.71 = f32[32,1,512]{2,1,0:T(1,128)S(1)} collective-permute-done((f32[32,1,512]{2,1,0:T(1,128)S(1)}, f32[32,1,512]{2,1,0:T(1,128)S(1)}, u32[]{:S(2)}, u32[]{:S(2)}) %collective-permute-start.71) | collective-permute-done | bytes 65568 | tf_op jit(solution)/shard_map/ppermute | solution.py:23
  (369 shorter events, 280.4 us)
Async XLA Ops:
  2.0 17.1 %collective-permute-start = (f32[32,1,512]{2,1,0:T(1,128)}, f32[32,1,512]{2,1,0:T(1,128)S(1)}, u32[]{:S(2)}, u32[]{:S(2)}) collective-permute-start(f32[32,1,512]{2,1,0:T(1,128)} %get-tuple-element.43), channel_id=1, source_target_pairs={{0,2},{2,4},{4,6},{6,8},{8,10},{10,12},{12,14},{14,16},{16,18},{18... | collective-permute-start | bytes 196616 | tf_op jit(solution)/shard_map/ppermute | solution.py:21
  6.8 12.6 %collective-permute-start.1 = (f32[32,1,512]{2,1,0:T(1,128)}, f32[32,1,512]{2,1,0:T(1,128)S(1)}, u32[]{:S(2)}, u32[]{:S(2)}) collective-permute-start(f32[32,1,512]{2,1,0:T(1,128)} %get-tuple-element.42), channel_id=1, source_target_pairs={{2,0},{4,2},{6,4},{8,6},{10,8},{12,10},{14,12},{16,14},{18,16},{20... | collective-permute-start | bytes 196616 | tf_op jit(solution)/shard_map/ppermute | solution.py:23
  12.4 25.1 %collective-permute-start.8 = (f32[32,1,256]{2,0,1:T(8,128)}, f32[32,1,256]{2,0,1:T(8,128)}, u32[]{:S(2)}, u32[]{:S(2)}) collective-permute-start(f32[32,1,256]{2,0,1:T(8,128)} %get-tuple-element.90), channel_id=1, source_target_pairs={{0,2},{2,4},{4,6},{6,8},{8,10},{10,12},{12,14},{14,16},{16,18},{18... | collective-permute-start | bytes 98312 | tf_op jit(solution)/shard_map/ppermute | solution.py:21
  17.6 19.9 %collective-permute-start.9 = (f32[32,1,256]{2,0,1:T(8,128)}, f32[32,1,256]{2,0,1:T(8,128)}, u32[]{:S(2)}, u32[]{:S(2)}) collective-permute-start(f32[32,1,256]{2,0,1:T(8,128)} %get-tuple-element.91), channel_id=1, source_target_pairs={{2,0},{4,2},{6,4},{8,6},{10,8},{12,10},{14,12},{16,14},{18,16},{20... | collective-permute-start | bytes 98312 | tf_op jit(solution)/shard_map/ppermute | solution.py:23
  19.6 10.5 %collective-permute-start.2 = (f32[32,10,1]{2,0,1:T(8,128)S(1)}, f32[32,10,1]{2,0,1:T(8,128)}, u32[]{:S(2)}, u32[]{:S(2)}) collective-permute-start(f32[32,10,1]{2,0,1:T(8,128)S(1)} %get-tuple-element.37), channel_id=1, source_target_pairs={{0,1},{2,3},{4,5},{6,7},{8,9},{10,11},{12,13},{14,15},{16,17},{18,... | collective-permute-start | bytes 3848 | tf_op jit(solution)/shard_map/ppermute | solution.py:21
  49.8 16.4 %collective-permute-start.10 = (f32[32,6,1]{2,0,1:T(8,128)}, f32[32,6,1]{2,0,1:T(8,128)S(1)}, u32[]{:S(2)}, u32[]{:S(2)}) collective-permute-start(f32[32,6,1]{2,0,1:T(8,128)} %get-tuple-element.72), channel_id=1, source_target_pairs={{0,1},{2,3},{4,5},{6,7},{8,9},{10,11},{12,13},{14,15},{16,17},{18,... | collective-permute-start | bytes 2312 | tf_op jit(solution)/shard_map/ppermute | solution.py:21
  52.8 14.0 %collective-permute-start.11 = (f32[32,6,1]{2,0,1:T(8,128)}, f32[32,6,1]{2,0,1:T(8,128)}, u32[]{:S(2)}, u32[]{:S(2)}) collective-permute-start(f32[32,6,1]{2,0,1:T(8,128)} %get-tuple-element.71), channel_id=1, source_target_pairs={{1,0},{3,2},{5,4},{7,6},{9,8},{11,10},{13,12},{15,14},{17,16},{19,... | collective-permute-start | bytes 2312 | tf_op jit(solution)/shard_map/ppermute | solution.py:23
  69.8 12.4 %collective-permute-start.12 = (f32[32,1,256]{2,0,1:T(8,128)}, f32[32,1,256]{2,0,1:T(8,128)S(1)}, u32[]{:S(2)}, u32[]{:S(2)}) collective-permute-start(f32[32,1,256]{2,0,1:T(8,128)} %get-tuple-element.87), channel_id=1, source_target_pairs={{0,2},{2,4},{4,6},{6,8},{8,10},{10,12},{12,14},{14,16},{16,18},{18... | collective-permute-start | bytes 98312 | tf_op jit(solution)/shard_map/ppermute | solution.py:21
  96.2 20.8 %collective-permute-start.16 = (f32[1,32,2,128]{3,1,2,0:T(8,128)}, f32[1,32,2,128]{3,1,2,0:T(8,128)}, u32[]{:S(2)}, u32[]{:S(2)}) collective-permute-start(f32[1,32,2,128]{3,1,2,0:T(8,128)} %get-tuple-element.123), channel_id=1, source_target_pairs={{0,2},{2,0},{4,6},{6,4},{8,10},{10,8},{12,14},{14,12},{16,18},{18,... | collective-permute-start | bytes 98312 | tf_op jit(solution)/shard_map/ppermute | solution.py:43
  130.7 29.9 %collective-permute-start.24 = (f32[32,1,130]{2,0,1:T(8,128)}, f32[32,1,130]{2,0,1:T(8,128)}, u32[]{:S(2)}, u32[]{:S(2)}) collective-permute-start(f32[32,1,130]{2,0,1:T(8,128)} %get-tuple-element.61), channel_id=1, source_target_pairs={{0,4},{2,6},{4,8},{6,10},{8,12},{10,14},{12,16},{14,18},{16,20},{1... | collective-permute-start | bytes 49928 | tf_op jit(solution)/shard_map/ppermute | solution.py:33
  134.1 26.6 %collective-permute-start.25 = (f32[32,1,130]{2,0,1:T(8,128)}, f32[32,1,130]{2,0,1:T(8,128)}, u32[]{:S(2)}, u32[]{:S(2)}) collective-permute-start(f32[32,1,130]{2,0,1:T(8,128)} %get-tuple-element.62), channel_id=1, source_target_pairs={{4,0},{6,2},{8,4},{10,6},{12,8},{14,10},{16,12},{18,14},{20,16},{2... | collective-permute-start | bytes 49928 | tf_op jit(solution)/shard_map/ppermute | solution.py:33
  137.8 16.1 %collective-permute-start.28 = (f32[32,4,1]{0,2,1:T(1,128)S(1)}, f32[32,4,1]{0,2,1:T(1,128)S(1)}, u32[]{:S(2)}, u32[]{:S(2)}) collective-permute-start(f32[32,4,1]{0,2,1:T(1,128)S(1)} %get-tuple-element.82), channel_id=1, source_target_pairs={{0,1},{2,3},{4,5},{6,7},{8,9},{10,11},{12,13},{14,15},{16,17},{18,... | collective-permute-start | bytes 1544 | tf_op jit(solution)/shard_map/ppermute | solution.py:21
  139.7 15.0 %collective-permute-start.29 = (f32[32,4,1]{0,2,1:T(1,128)S(1)}, f32[32,4,1]{0,2,1:T(1,128)S(1)}, u32[]{:S(2)}, u32[]{:S(2)}) collective-permute-start(f32[32,4,1]{0,2,1:T(1,128)S(1)} %get-tuple-element.83), channel_id=1, source_target_pairs={{1,0},{3,2},{5,4},{7,6},{9,8},{11,10},{13,12},{15,14},{17,16},{19,... | collective-permute-start | bytes 1544 | tf_op jit(solution)/shard_map/ppermute | solution.py:23
  150.0 21.1 %collective-permute-start.37 = (f32[2,32,2,32]{1,3,2,0:T(8,128)}, f32[2,32,2,32]{1,3,2,0:T(8,128)}, u32[]{:S(2)}, u32[]{:S(2)}) collective-permute-start(f32[2,32,2,32]{1,3,2,0:T(8,128)} %pad_maximum_fusion.113), channel_id=1, source_target_pairs={{0,8},{8,0},{2,10},{10,2},{4,12},{12,4},{6,14},{14,6},{16,24},{24,... | collective-permute-start | bytes 49160 | tf_op jit(solution)/shard_map/ppermute | solution.py:43
  156.9 10.1 %collective-permute-start.30 = (f32[32,1,66]{2,0,1:T(8,128)}, f32[32,1,66]{2,0,1:T(8,128)}, u32[]{:S(2)}, u32[]{:S(2)}) collective-permute-start(f32[32,1,66]{2,0,1:T(8,128)} %get-tuple-element.65), channel_id=1, source_target_pairs={{0,8},{2,10},{4,12},{6,14},{8,16},{10,18},{12,20},{14,22},{16,24},... | collective-permute-start | bytes 25352 | tf_op jit(solution)/shard_map/ppermute | solution.py:33
  166.2 16.3 %collective-permute-start.26 = (f32[1,32,2,64]{1,3,2,0:T(8,128)}, f32[1,32,2,64]{1,3,2,0:T(8,128)}, u32[]{:S(2)}, u32[]{:S(2)}) collective-permute-start(f32[1,32,2,64]{1,3,2,0:T(8,128)} %get-tuple-element.109), channel_id=1, source_target_pairs={{0,4},{4,0},{2,6},{6,2},{8,12},{12,8},{10,14},{14,10},{16,20},{20,... | collective-permute-start | bytes 49160 | tf_op jit(solution)/shard_map/ppermute | solution.py:43
  173.9 31.7 %collective-permute-start.38 = (f32[32,4,1]{0,2,1:T(1,128)}, f32[32,4,1]{0,2,1:T(1,128)}, u32[]{:S(2)}, u32[]{:S(2)}) collective-permute-start(f32[32,4,1]{0,2,1:T(1,128)} %get-tuple-element.106), channel_id=1, source_target_pairs={{0,1},{2,3},{4,5},{6,7},{8,9},{10,11},{12,13},{14,15},{16,17},{18,... | collective-permute-start | bytes 1544 | tf_op jit(solution)/shard_map/ppermute | solution.py:21
  176.7 28.9 %collective-permute-start.39 = (f32[32,4,1]{0,2,1:T(1,128)}, f32[32,4,1]{0,2,1:T(1,128)}, u32[]{:S(2)}, u32[]{:S(2)}) collective-permute-start(f32[32,4,1]{0,2,1:T(1,128)} %get-tuple-element.107), channel_id=1, source_target_pairs={{1,0},{3,2},{5,4},{7,6},{9,8},{11,10},{13,12},{15,14},{17,16},{19,... | collective-permute-start | bytes 1544 | tf_op jit(solution)/shard_map/ppermute | solution.py:23
  186.2 10.2 %collective-permute-start.32 = (f32[32,4,1]{0,2,1:T(1,128)}, f32[32,4,1]{0,2,1:T(1,128)}, u32[]{:S(2)}, u32[]{:S(2)}) collective-permute-start(f32[32,4,1]{0,2,1:T(1,128)} %get-tuple-element.80), channel_id=1, source_target_pairs={{0,1},{2,3},{4,5},{6,7},{8,9},{10,11},{12,13},{14,15},{16,17},{18,... | collective-permute-start | bytes 1544 | tf_op jit(solution)/shard_map/ppermute | solution.py:21
  192.3 32.1 %collective-permute-start.47 = (f32[2,32,2,16]{1,3,2,0:T(8,128)}, f32[2,32,2,16]{1,3,2,0:T(8,128)}, u32[]{:S(2)}, u32[]{:S(2)}) collective-permute-start(f32[2,32,2,16]{1,3,2,0:T(8,128)} %pad_maximum_fusion.129), channel_id=1, source_target_pairs={{0,16},{16,0},{2,18},{18,2},{4,20},{20,4},{6,22},{22,6},{8,24},{24... | collective-permute-start | bytes 24584 | tf_op jit(solution)/shard_map/ppermute | solution.py:43
  200.1 13.0 %collective-permute-start.34 = (f32[32,1,66]{2,0,1:T(8,128)S(1)}, f32[32,1,66]{2,0,1:T(8,128)S(1)}, u32[]{:S(2)}, u32[]{:S(2)}) collective-permute-start(f32[32,1,66]{2,0,1:T(8,128)S(1)} %get-tuple-element.59), channel_id=1, source_target_pairs={{0,8},{2,10},{4,12},{6,14},{8,16},{10,18},{12,20},{14,22},{16,24},... | collective-permute-start | bytes 25352 | tf_op jit(solution)/shard_map/ppermute | solution.py:33
  207.0 18.3 %collective-permute-start.40 = (f32[32,1,34]{0,2,1:T(8,128)}, f32[32,1,34]{0,2,1:T(8,128)}, u32[]{:S(2)}, u32[]{:S(2)}) collective-permute-start(f32[32,1,34]{0,2,1:T(8,128)} %get-tuple-element.96), channel_id=1, source_target_pairs={{0,16},{2,18},{4,20},{6,22},{8,24},{10,26},{12,28},{14,30},{1,17},... | collective-permute-start | bytes 13064 | tf_op jit(solution)/shard_map/ppermute | solution.py:33
  211.6 13.7 %collective-permute-start.41 = (f32[32,1,34]{0,2,1:T(8,128)}, f32[32,1,34]{0,2,1:T(8,128)}, u32[]{:S(2)}, u32[]{:S(2)}) collective-permute-start(f32[32,1,34]{0,2,1:T(8,128)} %get-tuple-element.97), channel_id=1, source_target_pairs={{16,0},{18,2},{20,4},{22,6},{24,8},{26,10},{28,12},{30,14},{17,1},... | collective-permute-start | bytes 13064 | tf_op jit(solution)/shard_map/ppermute | solution.py:33
  233.5 10.6 %collective-permute-start.44 = (f32[32,1,34]{0,2,1:T(8,128)S(1)}, f32[32,1,34]{0,2,1:T(8,128)S(1)}, u32[]{:S(2)}, u32[]{:S(2)}) collective-permute-start(f32[32,1,34]{0,2,1:T(8,128)S(1)} %get-tuple-element.94), channel_id=1, source_target_pairs={{0,16},{2,18},{4,20},{6,22},{8,24},{10,26},{12,28},{14,30},{1,17},... | collective-permute-start | bytes 13064 | tf_op jit(solution)/shard_map/ppermute | solution.py:33
  (89 other events, 828.9 us)
where the time goes:
time: 392 us; the launch traced here: 386 us
  starting transfers between devices  164 us (42%)
  other arithmetic  101 us (26%)
  local copies, waits for them, and re-layouts  70.7 us (18%)
  waiting for transfers between devices  49.5 us (13%)
    ppermute x24, starting transfers between devices, with_halo(): lax.ppermute(tail, axis, [(i, (i + 1) % count) for i in range(ends)])  66.6 us
    ppermute x18, starting transfers between devices, from_behind(): lax.ppermute(value, axis, [(source, source + steps) for source in range(i...  48.7 us
    ppermute x24, starting transfers between devices, with_halo(): lax.ppermute(head, axis, [((i + 1) % count, i) for i in range(ends)])  31.1 us
    ppermute x24, waiting for transfers between devices, with_halo(): lax.ppermute(head, axis, [((i + 1) % count, i) for i in range(ends)])  26.6 us
    reduce_sum x15, other arithmetic, restrict(): jnp.mean(field.reshape(depth, first // 2, 2, second // 2, 2), axis=(2, 4))  24.7 us
    unnamed x92, local copies, waits for them, and re-layouts  19 us
    ppermute x18, waiting for transfers between devices, from_behind(): lax.ppermute(value, axis, [(source, source + steps) for source in range(i...  18.2 us
    ppermute x8, starting transfers between devices, partner_2(): return lax.ppermute(block, axis, route)  17.2 us
  transfers between devices with their start and end apart: 74, of which 20 were waited for; matrix products, arithmetic and copies ran while one was open for 29% of the time, Pallas kernels for 0%

commit v1 on v0

v1 whole, which is shorter than its diff:
```python
import functools

import jax
import jax.numpy as jnp
from jax import lax
from jax.experimental import pallas as pl
from jax.experimental.pallas import tpu as pltpu
from jax.sharding import PartitionSpec as P

LEVELS = 6
COARSE_SWEEPS = 3
LANES = 128
BORDER = 128
relax_weight = 0.8
f32 = jnp.float32
VMEM_LIMIT = 40 * 1024 * 1024


class Sizes:
    def __init__(self, depth, extent_x, extent_y, span_count, width_count):
        self.depth, self.extent_x, self.extent_y = depth, extent_x, extent_y
        self.span_count, self.width_count = span_count, width_count
        self.sides = min(width_count - 1, 2)
        self.used = [(extent_y + self.sides * BORDER) >> level for level in range(LEVELS)]
        self.held = [-(-used // LANES) * LANES for used in self.used]
        self.tiles = [held // LANES for held in self.held]
        self.slots = []
        start = 0
        for level in (0, 1, 1, 1, 2, 2, 2):
            self.slots.append((start, self.tiles[level]))
            start += self.tiles[level]
        self.message = (start, depth, LANES)


def put(message, slot, row):
    start, tiles = slot
    for tile in range(tiles):
        message[start + tile] = row[:, tile * LANES : (tile + 1) * LANES]


def get(message, slot):
    start, tiles = slot
    return jnp.concatenate([message[start + tile] for tile in range(tiles)], axis=1)


def roll(value, steps, axis):
    return pltpu.roll(value, steps % value.shape[axis], axis=axis)


def reciprocal(value):
    return pltpu.reciprocal(value, approx=True)


def harmonic(first, second, guard):
    total = first + second
    if guard:
        total = jnp.maximum(total, 1e-3)
    return (2.0 * first) * second * reciprocal(total)


def split(value):
    high = value.astype(jnp.bfloat16)
    return high, (value - high.astype(f32)).astype(jnp.bfloat16)


def pairs(fine, coarse, weight):
    fine_at = lax.broadcasted_iota(jnp.int32, (fine, coarse), 0)
    coarse_at = lax.broadcasted_iota(jnp.int32, (fine, coarse), 1)
    return jnp.where(fine_at // 2 == coarse_at, weight, 0.0).astype(jnp.bfloat16)


def pairs_up(coarse, fine, weight):
    coarse_at = lax.broadcasted_iota(jnp.int32, (coarse, fine), 0)
    fine_at = lax.broadcasted_iota(jnp.int32, (coarse, fine), 1)
    return jnp.where(fine_at // 2 == coarse_at, weight, 0.0).astype(jnp.bfloat16)


def dot(first, second):
    return jnp.dot(first, second, preferred_element_type=f32)


def narrow(sums, target, rows):
    depth, held = sums.shape[1], sums.shape[2]
    high, low = split(sums[0:rows].reshape(rows * depth, held))
    table = pairs(min(held, 2 * LANES), LANES, 0.25)
    for tile in range(target.shape[2] // LANES):
        start, stop = 2 * LANES * tile, min(2 * LANES * (tile + 1), held)
        part = table[: stop - start]
        result = dot(high[:, start:stop], part) + dot(low[:, start:stop], part)
        target[0:rows, :, tile * LANES : (tile + 1) * LANES] = result.reshape(rows, depth, LANES)


def widen(coarse, target, rows):
    depth, held = coarse.shape[1], target.shape[2]
    high, low = split(coarse.reshape(rows * depth, coarse.shape[2]))
    table = pairs_up(LANES, min(held, 2 * LANES), 4.0)
    for tile in range(coarse.shape[2] // LANES):
        start, stop = 2 * LANES * tile, min(2 * LANES * (tile + 1), held)
        if start >= stop:
            break
        part = table[:, : stop - start]
        mine = slice(tile * LANES, (tile + 1) * LANES)
        result = dot(high[:, mine], part) + dot(low[:, mine], part)
        target[0:rows, :, start:stop] = result.reshape(rows, depth, stop - start)


def coefficients(count, conduct, binding, fx, fy, fz, weight, used, guard):
    for row in range(1, count):
        fx[row - 1] = harmonic(conduct(row - 1), conduct(row), guard)
    for row in range(1, count - 1):
        mine = conduct(row)
        shape = mine.shape
        south = harmonic(mine, roll(mine, 1, 1), guard)
        if used == shape[1]:
            south = jnp.where(lax.broadcasted_iota(jnp.int32, shape, 1) == 0, 0.0, south)
        below = harmonic(mine, roll(mine, 1, 0), guard)
        below = jnp.where(lax.broadcasted_iota(jnp.int32, shape, 0) == 0, 0.0, below)
        diagonal = fx[row - 1] + fx[row] + binding(row)
        diagonal = diagonal + (south + roll(south, -1, 1)) + (below + roll(below, -1, 0))
        if guard:
            diagonal = jnp.maximum(diagonal, 1e-6)
        fy[row - 1] = south
        fz[row - 1] = below
        weight[row - 1] = relax_weight * reciprocal(diagonal)


def sweep(count, field, binding, fx, fy, fz, emit):
    lower = fx[0] * (field(1) - field(0))
    for row in range(1, count - 1):
        mine = field(row)
        upper = fx[row] * (field(row + 1) - mine)
        south = fy[row - 1] * (mine - roll(mine, 1, 1))
        below = fz[row - 1] * (mine - roll(mine, 1, 0))
        across = (south - roll(south, -1, 1)) + (below - roll(below, -1, 0))
        emit(row, binding(row) * mine + (lower - upper) + across)
        lower = upper


def own_defect(count, smooth, source, binding, fx, fy, fz, sums, first):
    zero = jnp.zeros(smooth.shape[1:], f32)

    def field(row):
        return smooth[row - 1] if 0 < row < count - 1 else zero

    def add(row, value):
        slot = (row + first) // 2
        if (row + first) % 2 == 0 or row == 0:
            sums[slot] = value
        else:
            sums[slot] = sums[slot] + value

    add(0, fx[0] * field(1))
    sweep(count, field, binding, fx, fy, fz, lambda row, result: add(row, source(row) - result))
    add(count - 1, fx[count - 2] * field(count - 2))


def start_kernel(sizes, place, right_side, conduct, binding, *out):
    rows, sends = out[:3], out[3:]
    last = sizes.extent_y - BORDER
    for index, array in enumerate((conduct, binding, right_side)):
        turned = jnp.swapaxes(array[...], 0, 1)
        rows[index][...] = turned
        if sizes.width_count == 2:

            @pl.when(place[1] == 0)
            def _():
                sends[0][index] = turned[:, :, last:]

            @pl.when(place[1] == 1)
            def _():
                sends[0][index] = turned[:, :, :BORDER]

        elif sizes.width_count > 2:
            sends[0][index] = turned[:, :, last:]
            sends[1][index] = turned[:, :, :BORDER]


def border_kernel(sizes, place, conduct, binding, right_side, *refs):
    borders, refs = refs[: sizes.sides], refs[sizes.sides :]
    wide, refs = refs[:3], refs[3:]
    conducts, bindings, to_next, to_prev, sums = refs[0:3], refs[3:6], refs[6], refs[7], refs[8]
    for index, (array, target) in enumerate(zip((conduct, binding, right_side), wide)):
        if sizes.sides == 0:
            target[...] = array[...]
        elif sizes.sides == 1:

            @pl.when(place[1] == 0)
            def _():
                target[:, :, : sizes.extent_y] = array[...]
                target[:, :, sizes.extent_y :] = borders[0][index]

            @pl.when(place[1] == 1)
            def _():
                target[:, :, :BORDER] = borders[0][index]
                target[:, :, BORDER:] = array[...]

        else:
            target[:, :, :BORDER] = borders[0][index]
            target[:, :, BORDER : BORDER + sizes.extent_y] = array[...]
            target[:, :, BORDER + sizes.extent_y :] = borders[1][index]
    for fine, coarse in ((wide[0], conducts), (wide[1], bindings)):
        for level in range(3):
            count = coarse[level].shape[0]
            held = fine.shape[2]
            for row in range(count):
                sums[row, :, :held] = fine[2 * row] + fine[2 * row + 1]
            narrow(sums.at[:, :, :held], coarse[level], count)
            fine = coarse[level]
    c1, c2 = conducts[0], conducts[1]
    b1, b2 = bindings[0], bindings[1]
    high = sizes.extent_x - 1
    half = sizes.extent_x // 2 - 1
    for message, rows in (
        (to_next, (wide[0][high], c1[half - 1], c1[half], b1[half], c2[0], c2[1], b2[1])),
        (to_prev, (wide[0][0], c1[0], c1[1], b1[0], c2[0], c2[1], b2[0])),
    ):
        for slot, row in zip(sizes.slots, rows):
            put(message, slot, row)


def down_kernel(sizes, *refs):
    (source0, c0, b0, c1, b1, c2, b2, c3, b3, from_prev, from_next), refs = refs[:11], refs[11:]
    gathered, to_next, to_prev, to_next_2, to_prev_2 = refs[:5]
    v0, level0, level1, level2 = refs[5], refs[6:10], refs[10:17], refs[17:24]
    sums = refs[24]
    slots = sizes.slots
    guard = sizes.sides > 1
    n0, n1, n2 = (sizes.extent_x >> level for level in range(3))

    def conduct0(row):
        if row == 0:
            return get(from_prev, slots[0])
        if row == n0 + 1:
            return get(from_next, slots[0])
        return c0[row - 1]

    def bordered(array, count, first, second):
        def at(row):
            if row < 2:
                return get(from_prev, slots[first + row])
            if row >= count + 2:
                return get(from_next, slots[first + row - count - 2])
            return array[row - 2]

        return at

    def single(array, count, slot):
        def at(row):
            if row == 1:
                return get(from_prev, slots[slot])
            if row == count + 2:
                return get(from_next, slots[slot])
            return array[row - 2]

        return at

    fx, fy, fz, weight = level0
    coefficients(n0 + 2, conduct0, lambda row: b0[row - 1], fx, fy, fz, weight, sizes.used[0], guard)
    for row in range(n0):
        v0[row] = weight[row] * source0[row]
    own_defect(n0 + 2, v0, lambda row: source0[row - 1], lambda row: b0[row - 1], fx, fy, fz, sums, 1)
    fine_held = sizes.held[0]
    count = n1 + 2
    for level, n, array, bind, refs_of, slot in (
        (1, n1, c1, b1, level1, 1),
        (2, n2, c2, b2, level2, 4),
    ):
        fx, fy, fz, weight, binding, source, smooth = refs_of
        held = sizes.held[level]
        narrow(sums.at[:, :, :fine_held], source, n + 2)
        lookup = single(bind, n, slot + 2)
        for row in range(1, n + 3):
            binding[row - 1] = lookup(row)
        bound = lambda row, binding=binding: binding[row - 1]
        coefficients(n + 4, bordered(array, n, slot, slot + 1), bound, fx, fy, fz, weight, sizes.used[level], True)
        for row in range(n + 2):
            smooth[row] = weight[row] * source[row]
        own_defect(
            n + 4, smooth, lambda row, source=source: source[row - 1], bound, fx, fy, fz, sums.at[:, :, :held], 0
        )
        fine_held = held
    narrow(sums.at[:, :, :fine_held], gathered, 3)
    gathered[3] = c3[0]
    gathered[4] = b3[0]
    s1, v1 = level1[5], level1[6]
    s2, v2 = level2[5], level2[6]
    for message, rows in (
        (to_next, (v0[n0 - 1], s1[n1], s1[n1 + 1], v1[n1 - 1], s2[n2], s2[n2 + 1], v2[n2 - 1])),
        (to_prev, (v0[0], s1[1], s1[0], v1[2], s2[1], s2[0], v2[2])),
    ):
        for slot, row in zip(slots, rows):
            put(message, slot, row)
    put(to_next_2, (0, sizes.tiles[2]), v2[n2 + 1])
    put(to_prev_2, (0, sizes.tiles[2]), v2[0])


def up_kernel(sizes, place, gathered, from_prev, from_next, from_prev_2, from_next_2, source0, b0, v0, *refs):
    level0, level1, level2, out, scratch = refs[0:4], refs[4:11], refs[11:18], refs[18], refs[19:]
    slots = sizes.slots
    n0, n1, n2 = (sizes.extent_x >> level for level in range(3))
    total = sizes.span_count
    sums = scratch[0]
    coarse = [scratch[1 + 9 * index : 10 + 9 * index] for index in range(3)]
    wide2, wide1, wide0, lift2, lift1, lift0, it2, it1, it0 = scratch[28:37]
    zero = jnp.zeros(gathered.shape[2:], f32)

    for index in range(3):
        level = 3 + index
        fx, fy, fz, weight, conduct, binding, source, smooth, iterate = coarse[index]
        count = total >> index
        for array in (conduct, smooth, iterate):
            array[0] = zero
            array[count + 1] = zero
        if index == 0:
            for row in range(count):
                conduct[row + 1] = gathered[row, 3]
                binding[row] = gathered[row, 4]
                value = gathered[row, 1]
                if row > 0:
                    value = value + gathered[row - 1, 2]
                if row < count - 1:
                    value = value + gathered[row + 1, 0]
                source[row] = value
        bound = lambda row, binding=binding: binding[row - 1]
        coefficients(
            count + 2, lambda row, conduct=conduct: conduct[row], bound, fx, fy, fz, weight, sizes.used[level], True
        )
        for row in range(count):
            smooth[row + 1] = weight[row] * source[row]
        if index < 2:
            _, _, _, _, conduct_next, binding_next, source_next = coarse[index + 1][:7]
            for row in range(count // 2):
                sums[row, :, :LANES] = conduct[2 * row + 1] + conduct[2 * row + 2]
            narrow(sums.at[:, :, :LANES], conduct_next.at[1 : count // 2 + 1], count // 2)
            for row in range(count // 2):
                sums[row, :, :LANES] = binding[2 * row] + binding[2 * row + 1]
            narrow(sums.at[:, :, :LANES], binding_next, count // 2)

            def add(row, result, source=source):
                value = source[row - 1] - result
                slot = (row - 1) // 2
                if row % 2 == 1:
                    sums[slot, :, :LANES] = value
                else:
                    sums[slot, :, :LANES] = sums[slot, :, :LANES] + value

            sweep(count + 2, lambda row, smooth=smooth: smooth[row], bound, fx, fy, fz, add)
            narrow(sums.at[:, :, :LANES], source_next, count // 2)

    fx, fy, fz, weight, conduct, binding, source, smooth, iterate = coarse[2]
    held, other = smooth, iterate
    for _ in range(COARSE_SWEEPS - 1):

        def relax(row, result, held=held, other=other):
            other[row] = held[row] + weight[row - 1] * (source[row - 1] - result)

        sweep((total >> 2) + 2, lambda row, held=held: held[row], lambda row: binding[row - 1], fx, fy, fz, relax)
        held, other = other, held
    for index in (1, 0):
        fx, fy, fz, weight, conduct, binding, source, smooth, iterate = coarse[index]
        count = total >> index
        widen(held[1 : count // 2 + 1], sums.at[:, :, :LANES], count // 2)
        for row in range(count):
            smooth[row + 1] = smooth[row + 1] + sums[row // 2, :, :LANES]

        def relax(row, result, smooth=smooth, iterate=iterate, weight=weight, source=source):
            iterate[row] = smooth[row] + weight[row - 1] * (source[row - 1] - result)

        sweep(
            count + 2,
            lambda row, smooth=smooth: smooth[row],
            lambda row, binding=binding: binding[row - 1],
            fx,
            fy,
            fz,
            relax,
        )
        held = iterate

    widen(held[pl.ds(place[0], 3)], wide2, 3)
    for level, n, refs_of, slot, wide, lift, result_rows, upper in (
        (2, n2, level2, 4, wide2, lift2, it2, wide1),
        (1, n1, level1, 1, wide1, lift1, it1, wide0),
    ):
        fx, fy, fz, weight, binding, own, smooth = refs_of

        def source(row, own=own, slot=slot, n=n):
            value = own[row - 1]
            if row in (1, 2):
                value = value + get(from_prev, slots[slot + row - 1])
            if row in (n + 1, n + 2):
                value = value + get(from_next, slots[slot + n + 2 - row])
            return value

        for row in range(n + 4):
            if row == 0:
                value = get(from_prev, slots[slot + 2])
                if level == 2:
                    value = value + get(from_prev_2, (0, sizes.tiles[2]))
            elif row == n + 3:
                value = get(from_next, slots[slot + 2])
                if level == 2:
                    value = value + get(from_next_2, (0, sizes.tiles[2]))
            elif row in (1, 2, n + 1, n + 2):
                value = weight[row - 1] * source(row)
            else:
                value = smooth[row - 1]
            lift[row] = value + wide[row // 2]

        def relax(row, result, lift=lift, weight=weight, source=source, result_rows=result_rows):
            result_rows[row - 1] = lift[row] + weight[row - 1] * (source(row) - result)

        sweep(
            n + 4,
            lambda row, lift=lift: lift[row],
            lambda row, binding=binding: binding[row - 1],
            fx,
            fy,
            fz,
            relax,
        )
        widen(result_rows[...], upper, n + 2)

    fx, fy, fz, weight = level0
    lift0[0] = get(from_prev, slots[0]) + wide0[0]
    lift0[n0 + 1] = get(from_next, slots[0]) + wide0[n1 + 1]
    for row in range(1, n0 + 1):
        lift0[row] = v0[row - 1] + wide0[(row + 1) // 2]

    def relax0(row, result):
        it0[row - 1] = lift0[row] + weight[row - 1] * (source0[row - 1] - result)

    sweep(n0 + 2, lambda row: lift0[row], lambda row: b0[row - 1], fx, fy, fz, relax0)
    if sizes.sides == 1:

        @pl.when(place[1] == 0)
        def _():
            out[...] = jnp.swapaxes(it0[:, :, : sizes.extent_y], 0, 1)

        @pl.when(place[1] == 1)
        def _():
            out[...] = jnp.swapaxes(it0[:, :, BORDER:], 0, 1)

    else:
        start = BORDER if sizes.sides else 0
        out[...] = jnp.swapaxes(it0[:, :, start : start + sizes.extent_y], 0, 1)


def call(body, sizes, name, outputs, scratch, inputs, scalars=0):
    in_specs = [pl.BlockSpec(memory_space=pltpu.SMEM)] * scalars
    in_specs += [pl.BlockSpec(memory_space=pltpu.VMEM)] * (len(inputs) - scalars)
    return pl.pallas_call(
        functools.partial(body, sizes),
        name=name,
        out_shape=[jax.ShapeDtypeStruct(shape, f32) for shape in outputs],
        in_specs=in_specs,
        out_specs=[pl.BlockSpec(memory_space=pltpu.VMEM)] * len(outputs),
        scratch_shapes=[pltpu.VMEM(shape, f32) for shape in scratch],
        compiler_params=pltpu.CompilerParams(vmem_limit_bytes=VMEM_LIMIT),
    )(*inputs)


def along(value, axis, steps):
    count = lax.axis_size(axis)
    initial, last = max(0, -steps), min(count, count - steps)
    return lax.ppermute(value, axis, [(source, source + steps) for source in range(initial, last)])


def on_device(right_side, diffusivity, reaction):
    depth, extent_x, extent_y = diffusivity.shape
    sizes = Sizes(depth, extent_x, extent_y, lax.axis_size("span"), lax.axis_size("width"))
    place = jnp.stack([lax.axis_index("span"), lax.axis_index("width")]).astype(jnp.int32)
    own = (extent_x, depth, extent_y)
    edge = (3, extent_x, depth, BORDER)
    started = call(
        start_kernel,
        sizes,
        "start",
        [own] * 3 + [edge] * sizes.sides,
        [],
        [place, right_side, diffusivity, reaction],
        1,
    )
    if sizes.sides == 0:
        borders = []
    elif sizes.sides == 1:
        borders = [lax.ppermute(started[3], "width", [(0, 1), (1, 0)])]
    else:
        borders = [along(started[3], "width", 1), along(started[4], "width", -1)]

    def shape(level, rows):
        return (rows, depth, sizes.held[level])

    n0, n1, n2, n3 = (extent_x >> level for level in range(4))
    coarse = [shape(1, n1), shape(2, n2), shape(3, n3)]
    bordered = call(
        border_kernel,
        sizes,
        "border",
        [shape(0, n0)] * 3 + coarse * 2 + [sizes.message] * 2,
        [shape(0, n1)],
        [place, *started[:3], *borders],
        1,
    )
    (c0, b0, r0), (c1, c2, c3), (b1, b2, b3) = bordered[0:3], bordered[3:6], bordered[6:9]
    from_prev = along(bordered[9], "span", 1)
    from_next = along(bordered[10], "span", -1)

    def level_shapes(level, n):
        return [shape(level, n + 3)] + [shape(level, n + 2)] * 6

    far = (sizes.tiles[2], depth, LANES)
    part = (5, depth, LANES)
    coefficient_shapes = [shape(0, n0 + 1)] + [shape(0, n0)] * 3
    coefficient_shapes += level_shapes(1, n1) + level_shapes(2, n2)
    downs = call(
        down_kernel,
        sizes,
        "down",
        [part, sizes.message, sizes.message, far, far, shape(0, n0)] + coefficient_shapes,
        [shape(0, n1 + 2)],
        [r0, c0, b0, c1, b1, c2, b2, c3, b3, from_prev, from_next],
    )
    gathered = lax.all_gather(downs[0], "span", axis=0, tiled=False)
    from_prev = along(downs[1], "span", 1)
    from_next = along(downs[2], "span", -1)
    from_prev_2 = along(downs[3], "span", 2)
    from_next_2 = along(downs[4], "span", -2)
    scratch = [(max(sizes.span_count, n1 + 2), depth, sizes.held[0])]
    for index in range(3):
        count = sizes.span_count >> index
        scratch += [(count + 1, depth, LANES)] + [(count, depth, LANES)] * 3
        scratch += [(count + 2, depth, LANES), (count, depth, LANES), (count, depth, LANES)]
        scratch += [(count + 2, depth, LANES)] * 2
    scratch += [shape(2, n3 + 2), shape(1, n2 + 2), shape(0, n1 + 2)]
    scratch += [shape(2, n2 + 4), shape(1, n1 + 4), shape(0, n0 + 2)]
    scratch += [shape(2, n2 + 2), shape(1, n1 + 2), shape(0, n0)]
    (correction,) = call(
        up_kernel,
        sizes,
        "up",
        [diffusivity.shape],
        scratch,
        [place, gathered, from_prev, from_next, from_prev_2, from_next_2, r0, b0, *downs[5:]],
        1,
    )
    return correction


def solution(mesh):
    in_specs = (P(None, "span", "width"),) * 3
    return jax.shard_map(
        on_device, mesh=mesh, in_specs=in_specs, out_specs=P(None, "span", "width"), check_vma=False
    )
```

time: 392 us -> 146 us (0.37); the launches traced: 386 us -> 145 us
  starting transfers between devices: 164 us -> 16.6 us
  other arithmetic: 101 us -> 0.07 us
  local copies, waits for them, and re-layouts: 70.7 us -> 38.1 us
  waiting for transfers between devices: 49.5 us -> 66.7 us
  between operations: 1.61 us -> 13.5 us
  Pallas kernels: 0 us -> 10.3 us
    ppermute x74 -> x7, starting transfers between devices: 164 us -> 16.6 us  [the longest x6 16.1 us: along(): lax.ppermute(value, axis, [(source, source + steps) for source in range(i...]
    all_gather x0 -> x1, waiting for transfers between devices: none -> 43.3 us  [on_device(): gathered = lax.all_gather(downs[0], 'span', axis=0, tiled=False)]
    ppermute x74 -> x7, waiting for transfers between devices: 49.5 us -> 23.4 us  [the longest x6 22 us: along(): lax.ppermute(value, axis, [(source, source + steps) for source in range(i...]
    reduce_sum x15 -> x0, other arithmetic: 24.7 us -> none  [restrict(): jnp.mean(field.reshape(depth, first // 2, 2, second // 2, 2), axis=(2, 4))]
    add x16 -> x0, other arithmetic: 19.1 us -> none  [the longest x5 6.71 us: on_device(): lifted + relax_weight * (source - operate(lifted, coeffs, grid_level, cel...]
    div x18 -> x0, other arithmetic: 19.1 us -> none  [the longest x12 8.77 us: restrict(): jnp.mean(field.reshape(depth, first // 2, 2, second // 2, 2), axis=(2, 4))]
    unnamed x92 -> x94, local copies, waits for them, and re-layouts: 19 us -> 38.1 us
    slice x29 -> x0, local copies, waits for them, and re-layouts: 13.8 us -> none  [the longest x21 6.97 us: with_halo(): lax.slice_in_dim(cells, cells.shape[dim] - width, cells.shape[dim], axis=...]
  transfers between devices with their start and end apart: 74 -> 8, of which waited for: 20 -> 7; matrix products, arithmetic and copies ran while one was open for 29% -> 0% of each run, Pallas kernels for 0% -> 0%
where the time goes in v1:
time: 146 us; the launch traced here: 145 us
  waiting for transfers between devices  66.7 us (46%)
  local copies, waits for them, and re-layouts  38.1 us (26%)
  starting transfers between devices  16.6 us (11%)
  between operations  13.5 us (9%)
  Pallas kernels  10.3 us (7%)
    all_gather x1, waiting for transfers between devices, on_device(): gathered = lax.all_gather(downs[0], 'span', axis=0, tiled=False)  43.3 us
    unnamed x94, local copies, waits for them, and re-layouts  38.1 us
    ppermute x6, waiting for transfers between devices, along(): lax.ppermute(value, axis, [(source, source + steps) for source in range(i...  22 us
    ppermute x6, starting transfers between devices, along(): lax.ppermute(value, axis, [(source, source + steps) for source in range(i...  16.1 us
    pallas_call x4, Pallas kernels, call(): pl.pallas_call(functools.partial(body, sizes), name=name, out_shape=[jax....  10.3 us
  transfers between devices with their start and end apart: 8, of which 7 were waited for; matrix products, arithmetic and copies ran while one was open for 0% of the time, Pallas kernels for 0%

profile of v1, /device:TPU:0, one launch (start us, length us, event | category | flops | bytes accessed | tf_op | source)
XLA Modules:
  0.0 145.2 jit_solution(9343556930192694684)
XLA Ops:
  6.6 1.0 copy-done.5
  7.7 1.0 copy-done.6
  8.7 1.0 copy-done.7
  11.2 1.3 collective-permute-done.refs_0_
  12.6 1.6 %border.1 = (f32[8,32,640]{2,1,0:T(8,128)S(1)}, f32[8,32,640]{2,1,0:T(8,128)S(1)}, f32[8,32,640]{2,1,0:T(8,128)S(1)}, f32[4,32,384]{2,1,0:T(8,128)S(1)}, f32[2,3...) custom-call(s32[2]{0:T(128)S(1)} %pad_add_fusion.place, ...), custom_call_target="tpu_custom_call" | custom-call | tf_op jit(solution)/shard_map/border/pallas_call | solution.py:452
  14.2 4.8 %collective-permute-start.1 = (f32[20,32,128]{2,1,0:T(8,128)S(1)}, f32[20,32,128]{2,1,0:T(8,128)S(1)}, u32[]{:S(2)}, u32[]{:S(2)}) collective-permute-start(f32[20,32,128]{2,1,0:T(8,128)S(1)} %get-tuple-element.57), channel_id=1, source_target_pairs={{0,2},{2,4},{4,6},{6,8},{8,10},{10,12},{12,14},{14,16},{16,18},{18... | collective-permute-start | bytes 983048 | tf_op jit(solution)/shard_map/ppermute | solution.py:466
  19.0 1.3 collective-permute-start.2
  20.3 13.0 %collective-permute-done.1.refs_9_ = f32[20,32,128]{2,1,0:T(8,128)S(1)} collective-permute-done((f32[20,32,128]{2,1,0:T(8,128)S(1)}, f32[20,32,128]{2,1,0:T(8,128)S(1)}, u32[]{:S(2)}, u32[]{:S(2)}) %collective-permute-start.1) | collective-permute-done | bytes 327712 | tf_op jit(solution)/shard_map/ppermute | solution.py:466
  33.2 1.9 %collective-permute-done.2.refs_10_ = f32[20,32,128]{2,1,0:T(8,128)S(1)} collective-permute-done((f32[20,32,128]{2,1,0:T(8,128)S(1)}, f32[20,32,128]{2,1,0:T(8,128)S(1)}, u32[]{:S(2)}, u32[]{:S(2)}) %collective-permute-start.2) | collective-permute-done | bytes 327712 | tf_op jit(solution)/shard_map/ppermute | solution.py:466
  35.2 2.7 %down.1 = (f32[5,32,128]{2,1,0:T(8,128)S(1)}, f32[20,32,128]{2,1,0:T(8,128)S(1)}, f32[20,32,128]{2,1,0:T(8,128)S(1)}, f32[2,32,128]{2,1,0:T(8,128)S(1)}, f32[2,3...) custom-call(f32[8,32,640]{2,1,0:T(8,128)S(1)} %get-tuple-element.48., ...), custom_call_target="tpu_custom_call" | custom-call | tf_op jit(solution)/shard_map/down/pallas_call | solution.py:452
  51.8 3.4 %collective-permute-start.3 = (f32[20,32,128]{2,1,0:T(8,128)}, f32[20,32,128]{2,1,0:T(8,128)S(1)}, u32[]{:S(2)}, u32[]{:S(2)}) collective-permute-start(f32[20,32,128]{2,1,0:T(8,128)} %copy-done.44), channel_id=1, source_target_pairs={{0,2},{2,4},{4,6},{6,8},{8,10},{10,12},{12,14},{14,16},{16,18},{18... | collective-permute-start | bytes 983048 | tf_op jit(solution)/shard_map/ppermute | solution.py:466
  55.2 1.3 collective-permute-start.4
  56.5 4.0 %collective-permute-start.5 = (f32[2,32,128]{2,1,0:T(8,128)}, f32[2,32,128]{2,1,0:T(8,128)S(1)}, u32[]{:S(2)}, u32[]{:S(2)}) collective-permute-start(f32[2,32,128]{2,1,0:T(8,128)} %copy-done.46), channel_id=1, source_target_pairs={{0,4},{2,6},{4,8},{6,10},{8,12},{10,14},{12,16},{14,18},{16,20},{1... | collective-permute-start | bytes 98312 | tf_op jit(solution)/shard_map/ppermute | solution.py:466
  60.5 1.3 collective-permute-start.6
  61.8 1.0 collective-permute-done.5.from_prev_2
  62.8 5.6 %collective-permute-done.6.from_next_2 = f32[2,32,128]{2,1,0:T(8,128)S(1)} collective-permute-done((f32[2,32,128]{2,1,0:T(8,128)}, f32[2,32,128]{2,1,0:T(8,128)S(1)}, u32[]{:S(2)}, u32[]{:S(2)}) %collective-permute-start.6) | collective-permute-done | bytes 32800 | tf_op jit(solution)/shard_map/ppermute | solution.py:466
  71.0 43.3 %all-gather.3.cloned.1.call-done = f32[80,32,128]{2,1,0:T(8,128)} async-done(((f32[5,32,128]{2,1,0:T(8,128)}), f32[80,32,128]{2,1,0:T(8,128)}) %all-gather.3.cloned.1.call-update) | async-done | bytes 1310736 | tf_op jit(solution)/shard_map/all_gather | solution.py:524
  114.3 1.3 copy-done
  115.6 1.1 copy-done.2
  116.7 1.1 copy-done.4
  117.8 1.0 copy-done.9
  118.8 1.0 copy-done.11
  119.7 1.0 copy-done.13
  133.3 5.1 %up.1 = f32[32,8,512]{2,1,0:T(8,128)} custom-call(s32[2]{0:T(128)S(1)} %copy-done.42, f32[16,5,32,128]{3,2,1,0:T(8,128)S(1)} %bitcast.3, f32[20,32,128]{2,1,0:T(8,128)S(1)} %copy-done.11, f32[20,32,128]{2,1,0:T(8,128)S(1)} %copy-done.13, f32[2,32,128]{2,1,0:T(8,128)S(1)} %collective-permute-done.5.from_prev_2, f32[2,32,128]{2,1,0:T(8,128)S(1)} %copy-done.40, ...), custom_call_target="tpu_custom_call" | custom-call | tf_op jit(solution)/shard_map/up/pallas_call | solution.py:452
  (92 shorter events, 30.6 us)
Async XLA Ops:
  6.5 107.8 %all-gather.3.cloned.1.call-start = ((), (), s32[]{:S(2)}) async-start(), calls=%async_computation | async-start | bytes 1392640 | tf_op jit(solution)/shard_map/all_gather | solution.py:524
  6.6 1.0 copy-start.5
  7.7 1.0 copy-start.6
  8.7 1.0 copy-start.7
  9.7 4.4 %copy-start.41 = (s32[2]{0:T(128)}, s32[2]{0:T(128)S(1)}, u32[]{:S(2)}) copy-start(s32[2]{0:T(128)S(1)} %pad_add_fusion.place) | copy-start | bytes 28
  10.7 1.9 %collective-permute-start = (f32[3,8,32,128]{3,2,1,0:T(8,128)S(1)}, f32[3,8,32,128]{3,2,1,0:T(8,128)S(1)}, u32[]{:S(2)}, u32[]{:S(2)}) collective-permute-start(f32[3,8,32,128]{3,2,1,0:T(8,128)S(1)} %get-tuple-element.47), channel_id=1, source_target_pairs={{0,1},{1,0},{2,3},{3,2},{4,5},{5,4},{6,7},{7,6},{8,9},{9,8},{10,11... | collective-permute-start | bytes 1179656 | tf_op jit(solution)/shard_map/ppermute | solution.py:487
  14.2 19.1 %collective-permute-start.1 = (f32[20,32,128]{2,1,0:T(8,128)S(1)}, f32[20,32,128]{2,1,0:T(8,128)S(1)}, u32[]{:S(2)}, u32[]{:S(2)}) collective-permute-start(f32[20,32,128]{2,1,0:T(8,128)S(1)} %get-tuple-element.57), channel_id=1, source_target_pairs={{0,2},{2,4},{4,6},{6,8},{8,10},{10,12},{12,14},{14,16},{16,18},{18... | collective-permute-start | bytes 983048 | tf_op jit(solution)/shard_map/ppermute | solution.py:466
  19.0 16.2 %collective-permute-start.2 = (f32[20,32,128]{2,1,0:T(8,128)S(1)}, f32[20,32,128]{2,1,0:T(8,128)S(1)}, u32[]{:S(2)}, u32[]{:S(2)}) collective-permute-start(f32[20,32,128]{2,1,0:T(8,128)S(1)} %get-tuple-element.58), channel_id=1, source_target_pairs={{2,0},{4,2},{6,4},{8,6},{10,8},{12,10},{14,12},{16,14},{18,16},{20... | collective-permute-start | bytes 983048 | tf_op jit(solution)/shard_map/ppermute | solution.py:466
  51.8 17.8 %collective-permute-start.3 = (f32[20,32,128]{2,1,0:T(8,128)}, f32[20,32,128]{2,1,0:T(8,128)S(1)}, u32[]{:S(2)}, u32[]{:S(2)}) collective-permute-start(f32[20,32,128]{2,1,0:T(8,128)} %copy-done.44), channel_id=1, source_target_pairs={{0,2},{2,4},{4,6},{6,8},{8,10},{10,12},{12,14},{14,16},{16,18},{18... | collective-permute-start | bytes 983048 | tf_op jit(solution)/shard_map/ppermute | solution.py:466
  55.2 15.1 %collective-permute-start.4 = (f32[20,32,128]{2,1,0:T(8,128)}, f32[20,32,128]{2,1,0:T(8,128)S(1)}, u32[]{:S(2)}, u32[]{:S(2)}) collective-permute-start(f32[20,32,128]{2,1,0:T(8,128)} %copy-done.43), channel_id=1, source_target_pairs={{2,0},{4,2},{6,4},{8,6},{10,8},{12,10},{14,12},{16,14},{18,16},{20... | collective-permute-start | bytes 983048 | tf_op jit(solution)/shard_map/ppermute | solution.py:466
  56.5 6.3 %collective-permute-start.5 = (f32[2,32,128]{2,1,0:T(8,128)}, f32[2,32,128]{2,1,0:T(8,128)S(1)}, u32[]{:S(2)}, u32[]{:S(2)}) collective-permute-start(f32[2,32,128]{2,1,0:T(8,128)} %copy-done.46), channel_id=1, source_target_pairs={{0,4},{2,6},{4,8},{6,10},{8,12},{10,14},{12,16},{14,18},{16,20},{1... | collective-permute-start | bytes 98312 | tf_op jit(solution)/shard_map/ppermute | solution.py:466
  60.5 7.9 %collective-permute-start.6 = (f32[2,32,128]{2,1,0:T(8,128)}, f32[2,32,128]{2,1,0:T(8,128)S(1)}, u32[]{:S(2)}, u32[]{:S(2)}) collective-permute-start(f32[2,32,128]{2,1,0:T(8,128)} %copy-done.45), channel_id=1, source_target_pairs={{4,0},{6,2},{8,4},{10,6},{12,8},{14,10},{16,12},{18,14},{20,16},{2... | collective-permute-start | bytes 98312 | tf_op jit(solution)/shard_map/ppermute | solution.py:466
  114.3 1.3 copy-start
  115.6 1.1 copy-start.2
  116.7 1.1 copy-start.4
  117.8 1.0 copy-start.9
  118.8 1.0 copy-start.11
  119.7 1.0 copy-start.13
  120.7 1.0 copy-start.15
  121.7 1.0 copy-start.17
  122.6 1.0 copy-start.19
  123.6 1.0 copy-start.21
  124.6 1.0 copy-start.23
  125.5 1.0 copy-start.25
  (31 other events, 22.8 us)
Sparse Core Ops, SparseCore 0:
  51.9 62.3 all-gather.2

commit v2 on v0

v2 whole, which is shorter than its diff:
```python
import functools

import jax
import jax.numpy as jnp
from jax import lax
from jax.experimental import pallas as pl
from jax.experimental.pallas import tpu as pltpu
from jax.sharding import PartitionSpec as P

LEVELS = 6
COARSE_SWEEPS = 3
LANES = 128
BORDER = 128
FRINGE = 4
SPREAD = 16
relax_weight = 0.8
f32 = jnp.float32
VMEM_LIMIT = 40 * 1024 * 1024


class Sizes:
    def __init__(self, depth, extent_x, extent_y, span_count, width_count):
        self.depth, self.extent_x, self.extent_y = depth, extent_x, extent_y
        self.span_count, self.width_count = span_count, width_count
        self.sides = min(width_count - 1, 2)
        self.own = [(extent_y >> level) // LANES for level in range(3)]
        self.border = [self.sides, min(self.sides, 1), min(self.sides, 1)]
        self.held = [(self.own[level] + self.border[level]) * LANES for level in range(3)] + [LANES] * 3
        self.rows = [extent_x >> level for level in range(4)]
        self.slots = []
        start = 0
        for level in (0, 1, 1, 1, 2, 2, 2):
            self.slots.append((start, self.own[level]))
            start += self.own[level]
        self.tiles = start


class Copies:
    def __init__(self, semaphores):
        self.semaphores, self.used = semaphores, 0

    def start(self, source, target):
        copy = pltpu.make_async_copy(source, target, self.semaphores.at[self.used])
        self.used += 1
        copy.start()
        return copy


def wait(copies):
    for copy in copies:
        copy.wait()


def put(message, slot, row):
    start, tiles = slot
    for tile in range(tiles):
        message[start + tile] = row[:, tile * LANES : (tile + 1) * LANES]


def get(message, slot):
    start, tiles = slot
    return [message[start + tile] for tile in range(tiles)]


def lane_at(shape):
    return lax.broadcasted_iota(jnp.int32, shape, len(shape) - 1)


def roll(value, steps, axis):
    return pltpu.roll(value, steps % value.shape[axis], axis=axis)


def reciprocal(value):
    return pltpu.reciprocal(value, approx=True)


def harmonic(first, second, guard):
    total = first + second
    if guard:
        total = jnp.maximum(total, 1e-3)
    return (2.0 * first) * second * reciprocal(total)


def split(value):
    high = value.astype(jnp.bfloat16)
    return high, (value - high.astype(f32)).astype(jnp.bfloat16)


def dot(halves, table):
    high, low = halves
    return jnp.dot(high, table, preferred_element_type=f32) + jnp.dot(low, table, preferred_element_type=f32)


def pair_table(fine, fine_dim, turn, weight):
    shape = (fine, LANES) if fine_dim == 0 else (LANES, fine)
    fine_at = lax.broadcasted_iota(jnp.int32, shape, fine_dim)
    coarse_at = lax.broadcasted_iota(jnp.int32, shape, 1 - fine_dim)
    if turn is not None:
        coarse_at = coarse_at - jnp.where(fine_at >= turn, LANES // 2, 0)
    return jnp.where(fine_at // 2 == coarse_at, weight, 0.0).astype(jnp.bfloat16)


def turns(sizes, place, level):
    if sizes.sides == 0:
        return []
    if level == 0:
        return [jnp.where(place[1] == 0, LANES, 0)] if sizes.sides == 1 else [LANES, 0]
    return [LANES // 2]


def transfer_plan(sizes, place, level, part):
    plan = []
    if level >= 3:
        return [((0, LANES), 0, 3 * LANES // 4)]
    if level == 2:
        return [((0, sizes.held[2]), 0, None)]
    own = sizes.own[level]
    if part != "border":
        plan += [((2 * LANES * tile, 2 * LANES * (tile + 1)), tile, None) for tile in range(own // 2)]
    if part != "own":
        for index, turn in enumerate(turns(sizes, place, level)):
            start = (own + index) * LANES
            plan.append(((start, start + LANES), own // 2, turn))
    return plan


def narrow(sizes, place, level, sums, target, rows, part="all", shift=0):
    depth = sums.shape[1]
    done = {}
    for (start, stop), tile, turn in transfer_plan(sizes, place, level, part):
        start, stop, tile = start - shift, stop - shift, tile - shift // (2 * LANES)
        columns = split(sums[0:rows, :, start:stop].reshape(rows * depth, stop - start))
        result = dot(columns, pair_table(stop - start, 0, turn, 0.25)).reshape(rows, depth, LANES)
        done[tile] = done[tile] + result if tile in done else result
    for tile, result in done.items():
        target[0:rows, :, tile * LANES : (tile + 1) * LANES] = result


def widen(sizes, place, level, coarse, target, rows):
    depth = coarse.shape[1]
    for (start, stop), tile, turn in transfer_plan(sizes, place, level, "all"):
        columns = split(coarse[0:rows, :, tile * LANES : (tile + 1) * LANES].reshape(rows * depth, LANES))
        result = dot(columns, pair_table(stop - start, 1, turn, 4.0))
        target[0:rows, :, start:stop] = result.reshape(rows, depth, stop - start)


def coefficients(sizes, place, level, count, conduct, binding, fx, fy, fz, weight):
    guard = level > 0 or sizes.sides > 1
    for row in range(1, count):
        fx[row - 1] = harmonic(conduct(row - 1), conduct(row), guard)
    for row in range(1, count - 1):
        mine = conduct(row)
        south = harmonic(mine, roll(mine, 1, 1), guard)
        if level == 0 and sizes.sides < 2:
            cut = 0 if sizes.sides == 0 else jnp.where(place[1] == 0, 0, sizes.extent_y)
            south = jnp.where(lane_at(mine.shape) == cut, 0.0, south)
        below = harmonic(mine, roll(mine, 1, 0), guard)
        below = jnp.where(lax.broadcasted_iota(jnp.int32, mine.shape, 0) == 0, 0.0, below)
        diagonal = fx[row - 1] + fx[row] + binding(row)
        diagonal = diagonal + (south + roll(south, -1, 1)) + (below + roll(below, -1, 0))
        if guard:
            diagonal = jnp.maximum(diagonal, 1e-6)
        fy[row - 1] = south
        fz[row - 1] = below
        weight[row - 1] = relax_weight * reciprocal(diagonal)


def sweep(count, field, binding, fx, fy, fz, emit):
    lower = fx[0] * (field(1) - field(0))
    for row in range(1, count - 1):
        mine = field(row)
        upper = fx[row] * (field(row + 1) - mine)
        south = fy[row - 1] * (mine - roll(mine, 1, 1))
        below = fz[row - 1] * (mine - roll(mine, 1, 0))
        across = (south - roll(south, -1, 1)) + (below - roll(below, -1, 0))
        emit(row, binding(row) * mine + (lower - upper) + across)
        lower = upper


def own_defect(count, smooth, source, binding, fx, fy, fz, sums, first):
    zero = jnp.zeros(smooth.shape[1:], f32)

    def field(row):
        return smooth[row - 1] if 0 < row < count - 1 else zero

    def add(row, value):
        slot = (row + first) // 2
        if (row + first) % 2 == 0 or row == 0:
            sums[slot] = value
        else:
            sums[slot] = sums[slot] + value

    add(0, fx[0] * field(1))
    sweep(count, field, binding, fx, fy, fz, lambda row, result: add(row, source(row) - result))
    add(count - 1, fx[count - 2] * field(count - 2))


def parts(array, counts):
    views, start = [], 0
    for count in counts:
        views.append(array.at[start : start + count])
        start += count
    return views


def coefficient_rows(sizes, level):
    n = sizes.rows[level]
    if level == 0:
        return [n + 1, n, n, n, n]
    return [n + 3] + [n + 2] * 6


def start_kernel(sizes, place, right_side, conduct, binding, own0, own1, own2, to_next, to_prev, *refs):
    sends, refs = refs[: sizes.sides], refs[sizes.sides :]
    inputs, turned, level1, level2, next_out, prev_out = refs[:6]
    edges, sums, semaphores = refs[6 : 6 + sizes.sides], refs[-2], refs[-1]
    copies = Copies(semaphores)
    loads = [copies.start(array, inputs.at[at]) for at, array in enumerate((conduct, binding, right_side))]
    n0, n1, n2 = sizes.rows[:3]
    last = sizes.extent_y - BORDER

    def turn(at):
        loads[at].wait()
        turned[at] = jnp.swapaxes(inputs[at], 0, 1)

    for at in (0, 1):
        turn(at)
        for row in range(n1):
            sums[row] = turned[at, 2 * row] + turned[at, 2 * row + 1]
        narrow(sizes, place, 0, sums, level1.at[at], n1, "own")
        for row in range(n2):
            sums[row, :, : sizes.own[1] * LANES] = level1[at, 2 * row] + level1[at, 2 * row + 1]
        narrow(sizes, place, 1, sums, level2.at[at], n2, "own")
    for message, low, at1, at0 in ((next_out, n1 - 2, n1 - 1, n0 - 1), (prev_out, 0, 0, 0)):
        edge = n2 - 1 if at0 else 0
        rows = (turned[0, at0], level1[0, low], level1[0, low + 1], level1[1, at1])
        rows += (level2[0, n2 - 2], level2[0, n2 - 1], level2[1, edge])
        for slot, row in zip(sizes.slots, rows):
            put(message, slot, row)
    out = [copies.start(next_out, to_next), copies.start(prev_out, to_prev)]
    turn(2)
    out += [copies.start(turned, own0), copies.start(level1, own1), copies.start(level2, own2)]
    if sizes.sides == 1:
        at = pl.multiple_of(jnp.where(place[1] == 0, last, 0), LANES)
        edges[0][...] = turned[:, :, :, pl.ds(at, BORDER)]
    elif sizes.sides == 2:
        edges[0][...] = turned[:, :, :, last:]
        edges[1][...] = turned[:, :, :, :BORDER]
    for edge, send in zip(edges, sends):
        out.append(copies.start(edge, send))
    wait(out)


def border_kernel(sizes, place, own2, *refs):
    borders, refs = refs[: sizes.sides], refs[sizes.sides :]
    border1, border2, top = refs[:3]
    fine, level1, whole2, level3, sums, semaphores = refs[3:]
    copies = Copies(semaphores)
    n1, n2 = sizes.rows[1:3]
    own = sizes.own[2] * LANES
    loads = [copies.start(array.at[0:2], fine.at[side]) for side, array in enumerate(borders)]
    loads.append(copies.start(own2, whole2.at[:, :, :, :own]))
    wait(loads)
    out = []
    for at in (0, 1):
        if sizes.sides:
            for row in range(n1):
                for side in range(sizes.sides):
                    columns = slice(side * LANES, (side + 1) * LANES)
                    sums[row, :, columns] = fine[side, at, 2 * row] + fine[side, at, 2 * row + 1]
            narrow(sizes, place, 0, sums, level1.at[at], n1, "border", sizes.own[0] * LANES)
            for row in range(n2):
                sums[row, :, :LANES] = level1[at, 2 * row] + level1[at, 2 * row + 1]
            narrow(sizes, place, 1, sums, whole2.at[at, :, :, own:], n2, "border", sizes.own[1] * LANES)
        sums[0, :, : sizes.held[2]] = whole2[at, 0] + whole2[at, 1]
        narrow(sizes, place, 2, sums, level3.at[at : at + 1], 1)
    out.append(copies.start(level3, top))
    if sizes.sides:
        out.append(copies.start(level1, border1))
        out.append(copies.start(whole2.at[:, :, :, own:], border2))
    wait(out)


def message_row(sizes, place, level, slot, message, beside):
    start, tiles = slot
    row = get(message, slot)
    if sizes.sides == 1:
        left = place[1] != 0
        tile = beside[0][start + jnp.where(left, tiles - 1, 0)]
        if level > 0:
            reach = BORDER >> level
            lane = lane_at(tile.shape)
            first = jnp.where(left, LANES - reach, 0)
            tile = jnp.where((lane >= first) & (lane < first + reach), tile, 0.0)
        row.append(tile)
    elif sizes.sides == 2:
        right, left = beside[0][start], beside[1][start + tiles - 1]
        if level == 0:
            row += [right, left]
        else:
            reach = BORDER >> level
            lane = lane_at(right.shape)
            row.append(jnp.where(lane < reach, right, jnp.where(lane >= LANES - reach, left, 0.0)))
    return jnp.concatenate(row, axis=1)


def fringe_lanes(shape):
    lane = lane_at(shape)
    return (lane < FRINGE) | (lane >= LANES - FRINGE)


def put_fringes(sizes, message, rows):
    total = None
    for index, (level, row) in enumerate(rows):
        tile = row[:, sizes.own[level] * LANES :]
        tile = jnp.where(fringe_lanes(tile.shape), tile, 0.0)
        tile = roll(tile, SPREAD * index + SPREAD // 2, 1)
        total = tile if total is None else total + tile
    message[sizes.tiles] = total


def fringed_row(sizes, level, index, message):
    row = get(message, sizes.slots[index])
    if sizes.border[level]:
        if level == 0:
            row += [jnp.zeros(row[0].shape, f32)] * sizes.border[0]
        else:
            tile = roll(message[sizes.tiles], -(SPREAD * (index - 1) + SPREAD // 2), 1)
            row.append(jnp.where(fringe_lanes(tile.shape), tile, 0.0))
    return jnp.concatenate(row, axis=1)


def down_kernel(sizes, place, *refs):
    s = sizes.sides
    own0, own1, own2 = refs[:3]
    borders0, refs = refs[3 : 3 + s], refs[3 + s :]
    if s:
        (border1, border2), refs = refs[:2], refs[2:]
    halo_refs, refs = refs[: 2 * (1 + s)], refs[2 * (1 + s) :]
    coefs, contribution, ups, fars, refs = refs[:3], refs[3], refs[4:6], refs[6:8], refs[8:]
    wides, halos, refs = refs[:3], refs[3], refs[4:]
    rows_of, level3, up_rows, far_rows, sums, semaphores = refs[:3], refs[3], refs[4], refs[5], refs[6], refs[7]
    copies = Copies(semaphores)
    slots = sizes.slots
    n0, n1, n2 = sizes.rows[:3]

    def load(level, own, borders):
        width = sizes.own[level] * LANES
        started = [copies.start(own, wides[level].at[:, :, :, :width])]
        for index, border in enumerate(borders):
            start = width + index * LANES
            started.append(copies.start(border, wides[level].at[:, :, :, start : start + LANES]))
        return started

    loads = [copies.start(array, halos.at[at]) for at, array in enumerate(halo_refs)]
    loads += load(0, own0, borders0)
    later = load(1, own1, (border1,) if s else ()) + load(2, own2, (border2,) if s else ())
    wait(loads)
    from_prev, beside_prev = halos.at[0], [halos.at[2 + 2 * side] for side in range(s)]
    from_next, beside_next = halos.at[1], [halos.at[3 + 2 * side] for side in range(s)]
    c0, b0, r0 = (wides[0].at[at] for at in range(3))

    def prev_row(level, index):
        return message_row(sizes, place, level, slots[index], from_prev, beside_prev)

    def next_row(level, index):
        return message_row(sizes, place, level, slots[index], from_next, beside_next)

    def conduct0(row):
        if row == 0:
            return prev_row(0, 0)
        if row == n0 + 1:
            return next_row(0, 0)
        return c0[row - 1]

    fx, fy, fz, weight, v0 = parts(rows_of[0], coefficient_rows(sizes, 0))
    coefficients(sizes, place, 0, n0 + 2, conduct0, lambda row: b0[row - 1], fx, fy, fz, weight)
    for row in range(n0):
        v0[row] = weight[row] * r0[row]
    out = [copies.start(rows_of[0], coefs[0])]
    own_defect(n0 + 2, v0, lambda row: r0[row - 1], lambda row: b0[row - 1], fx, fy, fz, sums, 1)
    wait(later)
    smooths, sources = [], []
    for level, first in ((1, 1), (2, 4)):
        n = sizes.rows[level]
        conducts, bindings = wides[level].at[0], wides[level].at[1]
        fx, fy, fz, weight, binding, source, smooth = parts(rows_of[level], coefficient_rows(sizes, level))
        held = sizes.held[level]
        narrow(sizes, place, level - 1, sums.at[:, :, : sizes.held[level - 1]], source, n + 2)
        binding[0] = prev_row(level, first + 2)
        binding[n + 1] = next_row(level, first + 2)
        for row in range(n):
            binding[row + 1] = bindings[row]

        def conduct(row, n=n, level=level, first=first, conducts=conducts):
            if row < 2:
                return prev_row(level, first + row)
            if row >= n + 2:
                return next_row(level, first + row - n - 2)
            return conducts[row - 2]

        bound = lambda row, binding=binding: binding[row - 1]
        coefficients(sizes, place, level, n + 4, conduct, bound, fx, fy, fz, weight)
        for row in range(n + 2):
            smooth[row] = weight[row] * source[row]
        out.append(copies.start(rows_of[level], coefs[level]))
        mine = lambda row, source=source: source[row - 1]
        own_defect(n + 4, smooth, mine, bound, fx, fy, fz, sums.at[:, :, :held], 0)
        smooths.append(smooth)
        sources.append(source)
    narrow(sizes, place, 2, sums.at[:, :, : sizes.held[2]], level3, 3)
    out.append(copies.start(level3, contribution))
    (s1, s2), (v1, v2) = sources, smooths
    for at, rows in enumerate(
        (
            (v0[n0 - 1], s1[n1], s1[n1 + 1], v1[n1 - 1], s2[n2], s2[n2 + 1], v2[n2 - 1]),
            (v0[0], s1[1], s1[0], v1[2], s2[1], s2[0], v2[2]),
        )
    ):
        message = up_rows.at[at]
        for slot, row in zip(slots, rows):
            put(message, slot, row)
        if s:
            put_fringes(sizes, message, list(zip((1, 1, 1, 2, 2, 2), rows[1:])))
        out.append(copies.start(message, ups[at]))
        put(far_rows.at[at], (0, sizes.held[2] // LANES), v2[n2 + 1 if at == 0 else 0])
        out.append(copies.start(far_rows.at[at], fars[at]))
    wait(out)


def merge_into(place, stride, radix, arrays, target):
    position = (place[0] // stride) % radix
    target[...] = jnp.zeros(target.shape, f32)
    for step, array in enumerate(arrays):
        at = (position ^ step) * stride
        rows = pl.ds(at, stride + 2)
        target[rows] = target[rows] + array[...]


def merge_kernel(sizes, stride, radix, place, *refs):
    inputs, out, refs = refs[:radix], refs[radix], refs[radix + 1 :]
    arrays, total, semaphores = refs[:radix], refs[radix], refs[radix + 1]
    copies = Copies(semaphores)
    wait([copies.start(source, target) for source, target in zip(inputs, arrays)])
    merge_into(place, stride, radix, arrays, total)
    wait([copies.start(total, out)])


def up_kernel(sizes, stride, radix, place, *refs):
    s = sizes.sides
    sources, refs = refs[:radix], refs[radix:]
    tops, refs = refs[:radix], refs[radix:]
    halos, coefs, own0, borders0, out = refs[:4], refs[4:7], refs[7], refs[8 : 8 + s], refs[8 + s]
    scratch = refs[9 + s :]
    source_rows, top_rows, messages, fars, rows0, wide0, rows1, rows2, merged, sums, result = scratch[:11]
    coarse = [scratch[11 + 9 * index : 20 + 9 * index] for index in range(3)]
    over2, over1, over0, lift2, lift1, lift0, it2, it1, it0 = scratch[38:47]
    semaphores = scratch[47]
    copies = Copies(semaphores)
    slots = sizes.slots
    n0, n1, n2 = sizes.rows[:3]
    total = sizes.span_count
    loads = [copies.start(array, source_rows.at[step]) for step, array in enumerate(sources)]
    loads += [copies.start(array, top_rows.at[step]) for step, array in enumerate(tops)]
    later = [copies.start(array, messages.at[at]) for at, array in enumerate(halos[:2])]
    later += [copies.start(array, fars.at[at]) for at, array in enumerate(halos[2:])]
    for level in (2, 1, 0):
        later.append(copies.start(coefs[level], (rows0, rows1, rows2)[level]))
    width = sizes.own[0] * LANES
    later.append(copies.start(own0.at[1:3], wide0.at[:, :, :, :width]))
    for index, border in enumerate(borders0):
        start = width + index * LANES
        later.append(copies.start(border.at[1:3], wide0.at[:, :, :, start : start + LANES]))
    wait(loads)
    merge_into(place, stride, radix, [source_rows.at[step] for step in range(radix)], merged)

    zero = jnp.zeros((sizes.depth, LANES), f32)
    for index in range(3):
        level = 3 + index
        fx, fy, fz, weight, conduct, binding, source, smooth, iterate = coarse[index]
        count = total >> index
        for array in (conduct, smooth, iterate):
            array[0] = zero
            array[count + 1] = zero
        if index == 0:
            source = merged.at[1 : count + 1]
            for row in range(count):
                at = row ^ place[0]
                conduct[row + 1] = top_rows[at // stride, at % stride, 0]
                binding[row] = top_rows[at // stride, at % stride, 1]
        bound = lambda row, binding=binding: binding[row - 1]
        at_row = lambda row, conduct=conduct: conduct[row]
        coefficients(sizes, place, level, count + 2, at_row, bound, fx, fy, fz, weight)
        for row in range(count):
            smooth[row + 1] = weight[row] * source[row]
        if index < 2:
            conduct_next, binding_next, source_next = coarse[index + 1][4:7]
            half = count // 2
            for row in range(half):
                sums[row, :, :LANES] = conduct[2 * row + 1] + conduct[2 * row + 2]
            narrow(sizes, place, level, sums, conduct_next.at[1 : half + 1], half)
            for row in range(half):
                sums[row, :, :LANES] = binding[2 * row] + binding[2 * row + 1]
            narrow(sizes, place, level, sums, binding_next, half)

            def add(row, value, source=source):
                value = source[row - 1] - value
                slot = (row - 1) // 2
                if row % 2 == 1:
                    sums[slot, :, :LANES] = value
                else:
                    sums[slot, :, :LANES] = sums[slot, :, :LANES] + value

            sweep(count + 2, lambda row, smooth=smooth: smooth[row], bound, fx, fy, fz, add)
            narrow(sizes, place, level, sums, source_next, half)

    def relax(count, field, refs_of, source, target):
        fx, fy, fz, weight, binding = refs_of

        def update(row, value):
            target(row, field(row) + weight[row - 1] * (source(row) - value))

        sweep(count, field, lambda row: binding[row - 1], fx, fy, fz, update)

    def store(array, first):
        def put_row(row, value):
            array[row - first] = value

        return put_row

    fx, fy, fz, weight, conduct, binding, source, smooth, iterate = coarse[2]
    held, other = smooth, iterate
    for _ in range(COARSE_SWEEPS - 1):
        field = lambda row, held=held: held[row]
        mine = lambda row: source[row - 1]
        relax((total >> 2) + 2, field, (fx, fy, fz, weight, binding), mine, store(other, 0))
        held, other = other, held
    for index in (1, 0):
        fx, fy, fz, weight, conduct, binding, source, smooth, iterate = coarse[index]
        if index == 0:
            source = merged.at[1 : total + 1]
        count = total >> index
        widen(sizes, place, 3 + index, held.at[1 : count // 2 + 1], sums, count // 2)
        for row in range(count):
            smooth[row + 1] = smooth[row + 1] + sums[row // 2, :, :LANES]
        field = lambda row, smooth=smooth: smooth[row]
        mine = lambda row, source=source: source[row - 1]
        relax(count + 2, field, (fx, fy, fz, weight, binding), mine, store(iterate, 0))
        held = iterate

    wait(later)
    from_prev, from_next = messages.at[0], messages.at[1]
    widen(sizes, place, 2, held.at[pl.ds(place[0], 3)], over2, 3)
    for level, array, first, over, lift, target, upper in (
        (2, rows2, 4, over2, lift2, it2, over1),
        (1, rows1, 1, over1, lift1, it1, over0),
    ):
        n = sizes.rows[level]
        fx, fy, fz, weight, binding, own, smooth = parts(array, coefficient_rows(sizes, level))
        edge = {}
        for row, message, index in (
            (1, from_prev, first),
            (2, from_prev, first + 1),
            (n + 2, from_next, first),
            (n + 1, from_next, first + 1),
        ):
            value = edge.get(row, own[row - 1])
            edge[row] = value + fringed_row(sizes, level, index, message)
        for row, value in edge.items():
            own[row - 1] = value
        for row in range(n + 4):
            if row in (0, n + 3):
                value = fringed_row(sizes, level, first + 2, from_next if row else from_prev)
                if level == 2:
                    far = fars.at[1 if row else 0]
                    value = value + jnp.concatenate(get(far, (0, sizes.held[2] // LANES)), axis=1)
            elif row in edge:
                value = weight[row - 1] * own[row - 1]
            else:
                value = smooth[row - 1]
            lift[row] = value + over[row // 2]
        field = lambda row, lift=lift: lift[row]
        mine = lambda row, own=own: own[row - 1]
        relax(n + 4, field, (fx, fy, fz, weight, binding), mine, store(target, 1))
        widen(sizes, place, level - 1, target, upper, n + 2)

    b0, r0 = wide0.at[0], wide0.at[1]
    fx, fy, fz, weight, v0 = parts(rows0, coefficient_rows(sizes, 0))
    lift0[0] = fringed_row(sizes, 0, 0, from_prev) + over0[0]
    lift0[n0 + 1] = fringed_row(sizes, 0, 0, from_next) + over0[n1 + 1]
    for row in range(1, n0 + 1):
        lift0[row] = v0[row - 1] + over0[(row + 1) // 2]
    field = lambda row: lift0[row]
    mine = lambda row: r0[row - 1]
    relax(n0 + 2, field, (fx, fy, fz, weight, b0), mine, store(it0, 1))
    result[...] = jnp.swapaxes(it0[:, :, :width], 0, 1)
    wait([copies.start(result, out)])


def call(body, name, outputs, scratch, copies, place, inputs):
    return pl.pallas_call(
        body,
        name=name,
        out_shape=[jax.ShapeDtypeStruct(shape, f32) for shape in outputs],
        in_specs=[pl.BlockSpec(memory_space=pltpu.SMEM)] + [pl.BlockSpec(memory_space=pl.ANY)] * len(inputs),
        out_specs=[pl.BlockSpec(memory_space=pl.ANY)] * len(outputs),
        scratch_shapes=[pltpu.VMEM(shape, f32) for shape in scratch] + [pltpu.SemaphoreType.DMA((copies,))],
        compiler_params=pltpu.CompilerParams(vmem_limit_bytes=VMEM_LIMIT),
    )(place, *inputs)


def along(value, axis, steps):
    count = lax.axis_size(axis)
    initial, last = max(0, -steps), min(count, count - steps)
    return lax.ppermute(value, axis, [(source, source + steps) for source in range(initial, last)])


def beside(values, sizes):
    if sizes.sides == 1:
        return [[lax.ppermute(value, "width", [(0, 1), (1, 0)]) for value in values]]
    if sizes.sides == 2:
        return [[along(value, "width", steps) for value in values] for steps in (-1, 1)]
    return []


def stages(count):
    stride = 1
    while stride < count:
        radix = 4 if count // stride % 4 == 0 else 2
        yield stride, radix
        stride *= radix


def swap(value, stride, radix):
    count = lax.axis_size("span")
    others = range(1, radix)
    return [value] + [
        lax.ppermute(value, "span", [(device, device ^ step * stride) for device in range(count)]) for step in others
    ]


def on_device(right_side, diffusivity, reaction):
    depth, extent_x, extent_y = diffusivity.shape
    sizes = Sizes(depth, extent_x, extent_y, lax.axis_size("span"), lax.axis_size("width"))
    place = jnp.stack([lax.axis_index("span"), lax.axis_index("width")]).astype(jnp.int32)
    n0, n1, n2, n3 = sizes.rows
    s = sizes.sides

    def columns(count):
        return (depth, count * LANES)

    own = [columns(count) for count in sizes.own]
    held = [(depth, count) for count in sizes.held]
    down_message = (sizes.tiles, depth, LANES)
    up_message = (sizes.tiles + 1, depth, LANES)
    edge = (3, n0, depth, BORDER)

    outputs = [(3, n0, *own[0]), (2, n1, *own[1]), (2, n2, *own[2]), down_message, down_message] + [edge] * s
    own0, own1, own2, to_next, to_prev, *edges = call(
        functools.partial(start_kernel, sizes),
        "start",
        outputs,
        [(3, *diffusivity.shape), *outputs, (n1, *own[0])],
        8 + s,
        place,
        [right_side, diffusivity, reaction],
    )
    halos = [along(to_next, "span", 1), along(to_prev, "span", -1)]
    if s == 1:
        borders = [lax.ppermute(edges[0], "width", [(0, 1), (1, 0)])]
    elif s == 2:
        borders = [along(edges[1], "width", -1), along(edges[0], "width", 1)]
    else:
        borders = []

    outputs = [(2, n1, depth, LANES), (2, n2, depth, LANES), (2, depth, LANES)]
    border1, border2, top = call(
        functools.partial(border_kernel, sizes),
        "border",
        outputs,
        [(max(s, 1), 2, n0, depth, BORDER), outputs[0], (2, n2, *held[2]), outputs[2], (n1, depth, 2 * LANES)],
        4 + s,
        place,
        [own2, *borders],
    )
    plan = list(stages(sizes.span_count))
    for stride, radix in plan[:-1]:
        top = jnp.concatenate(swap(top.reshape(stride, 2, depth, LANES), stride, radix))
    stride, radix = plan[-1]
    tops = swap(top.reshape(stride, 2, depth, LANES), stride, radix)

    sides = beside(halos, sizes)
    lengths = [sum(coefficient_rows(sizes, level)) for level in range(3)]
    far = (sizes.held[2] // LANES, depth, LANES)
    coefs = [(lengths[level], *held[level]) for level in range(3)]
    downs = call(
        functools.partial(down_kernel, sizes),
        "down",
        [*coefs, (3, depth, LANES), up_message, up_message, far, far],
        [
            *((3 if level == 0 else 2, sizes.rows[level], *held[level]) for level in range(3)),
            (2 * (1 + s), *down_message),
            *coefs,
            (3, depth, LANES),
            (2, *up_message),
            (2, *far),
            (n1 + 2, *held[0]),
        ],
        20 + 4 * s,
        place,
        [own0, own1, own2, *borders, *([border1, border2] if s else []), *halos, *sum(sides, [])],
    )
    coefs_out, source, ups, fars = downs[:3], downs[3], downs[4:6], downs[6:8]
    for stride, radix in plan[:-1]:
        merged = (stride * radix + 2, depth, LANES)
        parts_of = swap(source, stride, radix)
        (source,) = call(
            functools.partial(merge_kernel, sizes, stride, radix),
            "merge",
            [merged],
            [(stride + 2, depth, LANES)] * radix + [merged],
            radix + 1,
            place,
            parts_of,
        )
    stride, radix = plan[-1]
    sources = swap(source, stride, radix)
    received = [along(ups[0], "span", 1), along(ups[1], "span", -1)]
    received += [along(fars[0], "span", 2), along(fars[1], "span", -2)]
    scratch = [
        (radix, stride + 2, depth, LANES),
        (radix, stride, 2, depth, LANES),
        (2, *up_message),
        (2, *far),
        coefs[0],
        (2, n0, *held[0]),
        coefs[1],
        coefs[2],
        (sizes.span_count + 2, depth, LANES),
        (max(sizes.span_count // 2, 2), depth, LANES),
        diffusivity.shape,
    ]
    for index in range(3):
        count = sizes.span_count >> index
        scratch += [(count + 1, depth, LANES)] + [(count, depth, LANES)] * 3
        scratch += [(count + 2, depth, LANES), (count, depth, LANES), (count, depth, LANES)]
        scratch += [(count + 2, depth, LANES)] * 2
    scratch += [(n3 + 2, *held[2]), (n2 + 2, *held[1]), (n1 + 2, *held[0])]
    scratch += [(n2 + 4, *held[2]), (n1 + 4, *held[1]), (n0 + 2, *held[0])]
    scratch += [(n2 + 2, *held[2]), (n1 + 2, *held[1]), (n0, *held[0])]
    (correction,) = call(
        functools.partial(up_kernel, sizes, stride, radix),
        "up",
        [diffusivity.shape],
        scratch,
        2 * radix + 9 + s,
        place,
        [*sources, *tops, *received, *coefs_out, own0, *borders],
    )
    return correction


def solution(mesh):
    in_specs = (P(None, "span", "width"),) * 3
    return jax.shard_map(
        on_device, mesh=mesh, in_specs=in_specs, out_specs=P(None, "span", "width"), check_vma=False
    )
```

time: 392 us -> 80.2 us (0.20); the launches traced: 386 us -> 79.8 us
  starting transfers between devices: 164 us -> 38 us
  other arithmetic: 101 us -> 0.09 us
  local copies, waits for them, and re-layouts: 70.7 us -> 3.12 us
  waiting for transfers between devices: 49.5 us -> 18.1 us
  Pallas kernels: 0 us -> 20.4 us
    ppermute x74 -> x21, starting transfers between devices: 164 us -> 38 us  [the longest x12 23.8 us: swap(): lax.ppermute(value, 'span', [(device, device ^ step * stride) for device...]
    ppermute x74 -> x21, waiting for transfers between devices: 49.5 us -> 18.1 us  [the longest x6 10.2 us: along(): lax.ppermute(value, axis, [(source, source + steps) for source in range(i...]
    reduce_sum x15 -> x0, other arithmetic: 24.7 us -> none  [restrict(): jnp.mean(field.reshape(depth, first // 2, 2, second // 2, 2), axis=(2, 4))]
    pallas_call x0 -> x5, Pallas kernels: none -> 20.4 us  [call(): pl.pallas_call(body, name=name, out_shape=[jax.ShapeDtypeStruct(shape, f3...]
    add x16 -> x0, other arithmetic: 19.1 us -> none  [the longest x5 6.71 us: on_device(): lifted + relax_weight * (source - operate(lifted, coeffs, grid_level, cel...]
    div x18 -> x0, other arithmetic: 19.1 us -> none  [the longest x12 8.77 us: restrict(): jnp.mean(field.reshape(depth, first // 2, 2, second // 2, 2), axis=(2, 4))]
    unnamed x92 -> x6, local copies, waits for them, and re-layouts: 19 us -> 3.12 us
    slice x29 -> x0, local copies, waits for them, and re-layouts: 13.8 us -> none  [the longest x21 6.97 us: with_halo(): lax.slice_in_dim(cells, cells.shape[dim] - width, cells.shape[dim], axis=...]
  transfers between devices with their start and end apart: 74 -> 21, of which waited for: 20 -> 6; matrix products, arithmetic and copies ran while one was open for 29% -> 0% of each run, Pallas kernels for 0% -> 12%
where the time goes in v2:
time: 80.2 us; the launch traced here: 79.8 us
  starting transfers between devices  38 us (47%)
  Pallas kernels  20.4 us (25%)
  waiting for transfers between devices  18.1 us (23%)
  local copies, waits for them, and re-layouts  3.12 us (4%)
    ppermute x12, starting transfers between devices, swap(): lax.ppermute(value, 'span', [(device, device ^ step * stride) for device...  23.8 us
    pallas_call x5, Pallas kernels, call(): pl.pallas_call(body, name=name, out_shape=[jax.ShapeDtypeStruct(shape, f3...  20.4 us
    ppermute x6, starting transfers between devices, along(): lax.ppermute(value, axis, [(source, source + steps) for source in range(i...  14.1 us
    ppermute x6, waiting for transfers between devices, along(): lax.ppermute(value, axis, [(source, source + steps) for source in range(i...  10.2 us
    ppermute x12, waiting for transfers between devices, swap(): lax.ppermute(value, 'span', [(device, device ^ step * stride) for device...  7.86 us
    unnamed x6, local copies, waits for them, and re-layouts  3.12 us
  transfers between devices with their start and end apart: 21, of which 6 were waited for; matrix products, arithmetic and copies ran while one was open for 0% of the time, Pallas kernels for 12%

profile of v2, /device:TPU:0, one launch (start us, length us, event | category | flops | bytes accessed | tf_op | source)
XLA Modules:
  0.0 79.8 jit_solution(5646927982677244478)
XLA Ops:
  0.1 1.0 %copy-done = f32[32,8,512]{2,1,0:T(8,128)S(1)} copy-done((f32[32,8,512]{2,1,0:T(8,128)S(1)}, f32[32,8,512]{2,1,0:T(8,128)}, u32[]{:S(2)}) %copy-start) | copy-done | bytes 524312
  3.2 2.7 %start.1 = (f32[3,8,32,512]{3,2,1,0:T(8,128)S(1)}, f32[2,4,32,256]{3,2,1,0:T(8,128)S(1)}, f32[2,2,32,128]{3,2,1,0:T(8,128)S(1)}, f32[13,32,128]{2,1,0:T(8,128)S(...) custom-call(s32[2]{0:T(128)S(1)} %pad_add_fusion.place, f32[32,8,512]{2,1,0:T(8,128)S(1)} %copy-done, ...), custom_call_target="tpu_custom_call" | custom-call | tf_op jit(solution)/shard_map/start/pallas_call | solution.py:601
  5.9 4.9 %collective-permute-start.1 = (f32[13,32,128]{2,1,0:T(8,128)S(1)}, f32[13,32,128]{2,1,0:T(8,128)S(1)}, u32[]{:S(2)}, u32[]{:S(2)}) collective-permute-start(f32[13,32,128]{2,1,0:T(8,128)S(1)} %get-tuple-element.28), channel_id=1, source_target_pairs={{0,2},{2,4},{4,6},{6,8},{8,10},{10,12},{12,14},{14,16},{16,18},{18... | collective-permute-start | bytes 638984 | tf_op jit(solution)/shard_map/ppermute | solution.py:615
  10.7 1.3 %collective-permute-start.2 = (f32[13,32,128]{2,1,0:T(8,128)S(1)}, f32[13,32,128]{2,1,0:T(8,128)S(1)}, u32[]{:S(2)}, u32[]{:S(2)}) collective-permute-start(f32[13,32,128]{2,1,0:T(8,128)S(1)} %get-tuple-element.29), channel_id=1, source_target_pairs={{2,0},{4,2},{6,4},{8,6},{10,8},{12,10},{14,12},{16,14},{18,16},{20... | collective-permute-start | bytes 638984 | tf_op jit(solution)/shard_map/ppermute | solution.py:615
  12.1 3.1 %collective-permute-done.1.refs_6_ = f32[13,32,128]{2,1,0:T(8,128)S(1)} collective-permute-done((f32[13,32,128]{2,1,0:T(8,128)S(1)}, f32[13,32,128]{2,1,0:T(8,128)S(1)}, u32[]{:S(2)}, u32[]{:S(2)}) %collective-permute-start.1) | collective-permute-done | bytes 213024 | tf_op jit(solution)/shard_map/ppermute | solution.py:615
  15.2 6.5 %collective-permute-done.2.refs_7_ = f32[13,32,128]{2,1,0:T(8,128)S(1)} collective-permute-done((f32[13,32,128]{2,1,0:T(8,128)S(1)}, f32[13,32,128]{2,1,0:T(8,128)S(1)}, u32[]{:S(2)}, u32[]{:S(2)}) %collective-permute-start.2) | collective-permute-done | bytes 213024 | tf_op jit(solution)/shard_map/ppermute | solution.py:615
  21.7 1.6 %border.1 = (f32[2,4,32,128]{3,2,1,0:T(8,128)S(1)}, f32[2,2,32,128]{3,2,1,0:T(8,128)S(1)}, f32[2,32,128]{2,1,0:T(8,128)S(1)}) custom-call(s32[2]{0:T(128)S(1)} %pad_add_fusion.place, f32[2,2,32,128]{3,2,1,0:T(8,128)S(1)} %get-tuple-element.24.own2.refs_2_, f32[3,8,32,128]{3,2,1,0:T(8,128)S(1)} %collective-permute-done.refs_0_.refs_3_.refs_16_), custom_call_target="tpu_custom_call" | custom-call | tf_op jit(solution)/shard_map/border/pallas_call | solution.py:601
  23.3 1.9 %collective-permute-start.13 = (f32[1,2,32,128]{3,2,1,0:T(8,128)S(1)}, f32[1,2,32,128]{3,2,1,0:T(8,128)S(1)}, u32[]{:S(2)}, u32[]{:S(2)}) collective-permute-start(f32[1,2,32,128]{3,2,1,0:T(8,128)S(1)} %bitcast.3), channel_id=1, source_target_pairs={{0,6},{2,4},{4,2},{6,0},{8,14},{10,12},{12,10},{14,8},{16,22},{18,... | collective-permute-start | bytes 98312 | tf_op jit(solution)/shard_map/ppermute | solution.py:638
  25.2 1.1 %collective-permute-start.12 = (f32[1,2,32,128]{3,2,1,0:T(8,128)S(1)}, f32[1,2,32,128]{3,2,1,0:T(8,128)S(1)}, u32[]{:S(2)}, u32[]{:S(2)}) collective-permute-start(f32[1,2,32,128]{3,2,1,0:T(8,128)S(1)} %bitcast.4), channel_id=1, source_target_pairs={{0,4},{2,6},{4,0},{6,2},{8,12},{10,14},{12,8},{14,10},{16,20},{18,... | collective-permute-start | bytes 98312 | tf_op jit(solution)/shard_map/ppermute | solution.py:638
  26.9 7.0 %down.1 = (f32[41,32,640]{2,1,0:T(8,128)S(1)}, f32[43,32,384]{2,1,0:T(8,128)S(1)}, f32[29,32,256]{2,1,0:T(8,128)S(1)}, f32[3,32,128]{2,1,0:T(8,128)S(1)}, f32[14...) custom-call(s32[2]{0:T(128)S(1)} %pad_add_fusion.place, ...), custom_call_target="tpu_custom_call" | custom-call | tf_op jit(solution)/shard_map/down/pallas_call | solution.py:601
  33.9 1.6 %collective-permute-start.5 = (f32[3,32,128]{2,1,0:T(8,128)S(1)}, f32[3,32,128]{2,1,0:T(8,128)S(1)}, u32[]{:S(2)}, u32[]{:S(2)}) collective-permute-start(f32[3,32,128]{2,1,0:T(8,128)S(1)} %get-tuple-element.30.refs_0_), channel_id=1, source_target_pairs={{0,2},{2,0},{4,6},{6,4},{8,10},{10,8},{12,14},{14,12},{16,18},{18,... | collective-permute-start | bytes 147464 | tf_op jit(solution)/shard_map/ppermute | solution.py:638
  36.4 1.1 %collective-permute-start.7 = (f32[3,32,128]{2,1,0:T(8,128)S(1)}, f32[3,32,128]{2,1,0:T(8,128)S(1)}, u32[]{:S(2)}, u32[]{:S(2)}) collective-permute-start(f32[3,32,128]{2,1,0:T(8,128)S(1)} %get-tuple-element.30.refs_0_), channel_id=1, source_target_pairs={{0,6},{2,4},{4,2},{6,0},{8,14},{10,12},{12,10},{14,8},{16,22},{18,... | collective-permute-start | bytes 147464 | tf_op jit(solution)/shard_map/ppermute | solution.py:638
  37.5 2.4 %collective-permute-start.19 = (f32[2,32,128]{2,1,0:T(8,128)S(1)}, f32[2,32,128]{2,1,0:T(8,128)S(1)}, u32[]{:S(2)}, u32[]{:S(2)}) collective-permute-start(f32[2,32,128]{2,1,0:T(8,128)S(1)} %get-tuple-element.34), channel_id=1, source_target_pairs={{0,4},{2,6},{4,8},{6,10},{8,12},{10,14},{12,16},{14,18},{16,20},{1... | collective-permute-start | bytes 98312 | tf_op jit(solution)/shard_map/ppermute | solution.py:615
  39.8 1.3 %collective-permute-start.20 = (f32[2,32,128]{2,1,0:T(8,128)S(1)}, f32[2,32,128]{2,1,0:T(8,128)S(1)}, u32[]{:S(2)}, u32[]{:S(2)}) collective-permute-start(f32[2,32,128]{2,1,0:T(8,128)S(1)} %get-tuple-element.35), channel_id=1, source_target_pairs={{4,0},{6,2},{8,4},{10,6},{12,8},{14,10},{16,12},{18,14},{20,16},{2... | collective-permute-start | bytes 98312 | tf_op jit(solution)/shard_map/ppermute | solution.py:615
  41.4 4.5 %collective-permute-start.14 = (f32[4,2,32,128]{3,2,1,0:T(8,128)S(1)}, f32[4,2,32,128]{3,2,1,0:T(8,128)S(1)}, u32[]{:S(2)}, u32[]{:S(2)}) collective-permute-start(f32[4,2,32,128]{3,2,1,0:T(8,128)S(1)} %pad_maximum_fusion.refs_4_), channel_id=1, source_target_pairs={{0,8},{2,10},{4,12},{6,14},{8,0},{10,2},{12,4},{14,6},{16,24},{18,... | collective-permute-start | bytes 393224 | tf_op jit(solution)/shard_map/ppermute | solution.py:638
  46.2 3.0 %collective-permute-start.15 = (f32[4,2,32,128]{3,2,1,0:T(8,128)S(1)}, f32[4,2,32,128]{3,2,1,0:T(8,128)S(1)}, u32[]{:S(2)}, u32[]{:S(2)}) collective-permute-start(f32[4,2,32,128]{3,2,1,0:T(8,128)S(1)} %pad_maximum_fusion.refs_4_), channel_id=1, source_target_pairs={{0,16},{2,18},{4,20},{6,22},{8,24},{10,26},{12,28},{14,30},{16,0},... | collective-permute-start | bytes 393224 | tf_op jit(solution)/shard_map/ppermute | solution.py:638
  49.2 1.4 %collective-permute-start.16 = (f32[4,2,32,128]{3,2,1,0:T(8,128)S(1)}, f32[4,2,32,128]{3,2,1,0:T(8,128)S(1)}, u32[]{:S(2)}, u32[]{:S(2)}) collective-permute-start(f32[4,2,32,128]{3,2,1,0:T(8,128)S(1)} %pad_maximum_fusion.refs_4_), channel_id=1, source_target_pairs={{0,24},{2,26},{4,28},{6,30},{8,16},{10,18},{12,20},{14,22},{16,8},... | collective-permute-start | bytes 393224 | tf_op jit(solution)/shard_map/ppermute | solution.py:638
  50.5 3.0 %collective-permute-start.17 = (f32[14,32,128]{2,1,0:T(8,128)S(1)}, f32[14,32,128]{2,1,0:T(8,128)S(1)}, u32[]{:S(2)}, u32[]{:S(2)}) collective-permute-start(f32[14,32,128]{2,1,0:T(8,128)S(1)} %get-tuple-element.32), channel_id=1, source_target_pairs={{0,2},{2,4},{4,6},{6,8},{8,10},{10,12},{12,14},{14,16},{16,18},{18... | collective-permute-start | bytes 688136 | tf_op jit(solution)/shard_map/ppermute | solution.py:615
  53.6 1.3 %collective-permute-start.18 = (f32[14,32,128]{2,1,0:T(8,128)S(1)}, f32[14,32,128]{2,1,0:T(8,128)S(1)}, u32[]{:S(2)}, u32[]{:S(2)}) collective-permute-start(f32[14,32,128]{2,1,0:T(8,128)S(1)} %get-tuple-element.33), channel_id=1, source_target_pairs={{2,0},{4,2},{6,4},{8,6},{10,8},{12,10},{14,12},{16,14},{18,16},{20... | collective-permute-start | bytes 688136 | tf_op jit(solution)/shard_map/ppermute | solution.py:615
  55.9 5.5 %collective-permute-start.8 = (f32[6,32,128]{2,1,0:T(8,128)S(1)}, f32[6,32,128]{2,1,0:T(8,128)S(1)}, u32[]{:S(2)}, u32[]{:S(2)}) collective-permute-start(f32[6,32,128]{2,1,0:T(8,128)S(1)} %merge.1.refs_0_), channel_id=1, source_target_pairs={{0,8},{2,10},{4,12},{6,14},{8,0},{10,2},{12,4},{14,6},{16,24},{18,... | collective-permute-start | bytes 294920 | tf_op jit(solution)/shard_map/ppermute | solution.py:638
  62.3 1.5 %collective-permute-start.10 = (f32[6,32,128]{2,1,0:T(8,128)S(1)}, f32[6,32,128]{2,1,0:T(8,128)S(1)}, u32[]{:S(2)}, u32[]{:S(2)}) collective-permute-start(f32[6,32,128]{2,1,0:T(8,128)S(1)} %merge.1.refs_0_), channel_id=1, source_target_pairs={{0,24},{2,26},{4,28},{6,30},{8,16},{10,18},{12,20},{14,22},{16,8},... | collective-permute-start | bytes 294920 | tf_op jit(solution)/shard_map/ppermute | solution.py:638
  63.8 3.6 %collective-permute-done.8.refs_1_ = f32[6,32,128]{2,1,0:T(8,128)S(1)} collective-permute-done((f32[6,32,128]{2,1,0:T(8,128)S(1)}, f32[6,32,128]{2,1,0:T(8,128)S(1)}, u32[]{:S(2)}, u32[]{:S(2)}) %collective-permute-start.8) | collective-permute-done | bytes 98336 | tf_op jit(solution)/shard_map/ppermute | solution.py:638
  67.4 4.2 %collective-permute-done.9.refs_2_ = f32[6,32,128]{2,1,0:T(8,128)S(1)} collective-permute-done((f32[6,32,128]{2,1,0:T(8,128)S(1)}, f32[6,32,128]{2,1,0:T(8,128)S(1)}, u32[]{:S(2)}, u32[]{:S(2)}) %collective-permute-start.9) | collective-permute-done | bytes 98336 | tf_op jit(solution)/shard_map/ppermute | solution.py:638
  71.7 8.2 %up.1 = f32[32,8,512]{2,1,0:T(8,128)} custom-call(s32[2]{0:T(128)S(1)} %pad_add_fusion.place, f32[6,32,128]{2,1,0:T(8,128)S(1)} %merge.1.refs_0_, f32[6,32,128]{2,1,0:T(8,128)S(1)} %collective-permute-done.8.refs_1_, f32[6,32,128]{2,1,0:T(8,128)S(1)} %collective-permute-done.9.refs_2_, f32[6,32,128]{2,1,0:T(8,128)S(1)} %collective-permute-done.10.refs_3_, ...), custom_call_target="tpu_custom_call" | custom-call | tf_op jit(solution)/shard_map/up/pallas_call | solution.py:601
  (31 shorter events, 6.3 us)
Async XLA Ops:
  0.1 1.0 %copy-start = (f32[32,8,512]{2,1,0:T(8,128)S(1)}, f32[32,8,512]{2,1,0:T(8,128)}, u32[]{:S(2)}) copy-start(f32[32,8,512]{2,1,0:T(8,128)} %right_side.1) | copy-start | bytes 1572868
  1.1 1.0 %copy-start.1 = (f32[32,8,512]{2,1,0:T(8,128)S(1)}, f32[32,8,512]{2,1,0:T(8,128)}, u32[]{:S(2)}) copy-start(f32[32,8,512]{2,1,0:T(8,128)} %conduct.1) | copy-start | bytes 1572868
  2.2 1.0 %copy-start.2 = (f32[32,8,512]{2,1,0:T(8,128)S(1)}, f32[32,8,512]{2,1,0:T(8,128)}, u32[]{:S(2)}) copy-start(f32[32,8,512]{2,1,0:T(8,128)} %binding.1) | copy-start | bytes 1572868
  5.9 9.3 %collective-permute-start.1 = (f32[13,32,128]{2,1,0:T(8,128)S(1)}, f32[13,32,128]{2,1,0:T(8,128)S(1)}, u32[]{:S(2)}, u32[]{:S(2)}) collective-permute-start(f32[13,32,128]{2,1,0:T(8,128)S(1)} %get-tuple-element.28), channel_id=1, source_target_pairs={{0,2},{2,4},{4,6},{6,8},{8,10},{10,12},{12,14},{14,16},{16,18},{18... | collective-permute-start | bytes 638984 | tf_op jit(solution)/shard_map/ppermute | solution.py:615
  10.7 11.0 %collective-permute-start.2 = (f32[13,32,128]{2,1,0:T(8,128)S(1)}, f32[13,32,128]{2,1,0:T(8,128)S(1)}, u32[]{:S(2)}, u32[]{:S(2)}) collective-permute-start(f32[13,32,128]{2,1,0:T(8,128)S(1)} %get-tuple-element.29), channel_id=1, source_target_pairs={{2,0},{4,2},{6,4},{8,6},{10,8},{12,10},{14,12},{16,14},{18,16},{20... | collective-permute-start | bytes 638984 | tf_op jit(solution)/shard_map/ppermute | solution.py:615
  12.0 9.7 %collective-permute-start = (f32[3,8,32,128]{3,2,1,0:T(8,128)S(1)}, f32[3,8,32,128]{3,2,1,0:T(8,128)S(1)}, u32[]{:S(2)}, u32[]{:S(2)}) collective-permute-start(f32[3,8,32,128]{3,2,1,0:T(8,128)S(1)} %get-tuple-element.25), channel_id=1, source_target_pairs={{0,1},{1,0},{2,3},{3,2},{4,5},{5,4},{6,7},{7,6},{8,9},{9,8},{10,11... | collective-permute-start | bytes 1179656 | tf_op jit(solution)/shard_map/ppermute | solution.py:670
  15.2 11.7 %collective-permute-start.3 = (f32[13,32,128]{2,1,0:T(8,128)S(1)}, f32[13,32,128]{2,1,0:T(8,128)S(1)}, u32[]{:S(2)}, u32[]{:S(2)}) collective-permute-start(f32[13,32,128]{2,1,0:T(8,128)S(1)} %collective-permute-done.1.refs_6_), channel_id=1, source_target_pairs={{0,1},{1,0},{2,3},{3,2},{4,5},{5,4},{6,7},{7,6},{8,9},{9,8},{10,11... | collective-permute-start | bytes 638984 | tf_op jit(solution)/shard_map/ppermute | solution.py:620
  21.7 5.1 %collective-permute-start.4 = (f32[13,32,128]{2,1,0:T(8,128)S(1)}, f32[13,32,128]{2,1,0:T(8,128)S(1)}, u32[]{:S(2)}, u32[]{:S(2)}) collective-permute-start(f32[13,32,128]{2,1,0:T(8,128)S(1)} %collective-permute-done.2.refs_7_), channel_id=1, source_target_pairs={{0,1},{1,0},{2,3},{3,2},{4,5},{5,4},{6,7},{7,6},{8,9},{9,8},{10,11... | collective-permute-start | bytes 638984 | tf_op jit(solution)/shard_map/ppermute | solution.py:620
  23.3 13.1 %collective-permute-start.13 = (f32[1,2,32,128]{3,2,1,0:T(8,128)S(1)}, f32[1,2,32,128]{3,2,1,0:T(8,128)S(1)}, u32[]{:S(2)}, u32[]{:S(2)}) collective-permute-start(f32[1,2,32,128]{3,2,1,0:T(8,128)S(1)} %bitcast.3), channel_id=1, source_target_pairs={{0,6},{2,4},{4,2},{6,0},{8,14},{10,12},{12,10},{14,8},{16,22},{18,... | collective-permute-start | bytes 98312 | tf_op jit(solution)/shard_map/ppermute | solution.py:638
  25.2 12.2 %collective-permute-start.12 = (f32[1,2,32,128]{3,2,1,0:T(8,128)S(1)}, f32[1,2,32,128]{3,2,1,0:T(8,128)S(1)}, u32[]{:S(2)}, u32[]{:S(2)}) collective-permute-start(f32[1,2,32,128]{3,2,1,0:T(8,128)S(1)} %bitcast.4), channel_id=1, source_target_pairs={{0,4},{2,6},{4,0},{6,2},{8,12},{10,14},{12,8},{14,10},{16,20},{18,... | collective-permute-start | bytes 98312 | tf_op jit(solution)/shard_map/ppermute | solution.py:638
  26.3 13.5 %collective-permute-start.11 = (f32[1,2,32,128]{3,2,1,0:T(8,128)S(1)}, f32[1,2,32,128]{3,2,1,0:T(8,128)S(1)}, u32[]{:S(2)}, u32[]{:S(2)}) collective-permute-start(f32[1,2,32,128]{3,2,1,0:T(8,128)S(1)} %bitcast.5), channel_id=1, source_target_pairs={{0,2},{2,0},{4,6},{6,4},{8,10},{10,8},{12,14},{14,12},{16,18},{18,... | collective-permute-start | bytes 98312 | tf_op jit(solution)/shard_map/ppermute | solution.py:638
  33.9 15.3 %collective-permute-start.5 = (f32[3,32,128]{2,1,0:T(8,128)S(1)}, f32[3,32,128]{2,1,0:T(8,128)S(1)}, u32[]{:S(2)}, u32[]{:S(2)}) collective-permute-start(f32[3,32,128]{2,1,0:T(8,128)S(1)} %get-tuple-element.30.refs_0_), channel_id=1, source_target_pairs={{0,2},{2,0},{4,6},{6,4},{8,10},{10,8},{12,14},{14,12},{16,18},{18,... | collective-permute-start | bytes 147464 | tf_op jit(solution)/shard_map/ppermute | solution.py:638
  35.4 15.1 %collective-permute-start.6 = (f32[3,32,128]{2,1,0:T(8,128)S(1)}, f32[3,32,128]{2,1,0:T(8,128)S(1)}, u32[]{:S(2)}, u32[]{:S(2)}) collective-permute-start(f32[3,32,128]{2,1,0:T(8,128)S(1)} %get-tuple-element.30.refs_0_), channel_id=1, source_target_pairs={{0,4},{2,6},{4,0},{6,2},{8,12},{10,14},{12,8},{14,10},{16,20},{18,... | collective-permute-start | bytes 147464 | tf_op jit(solution)/shard_map/ppermute | solution.py:638
  36.4 17.2 %collective-permute-start.7 = (f32[3,32,128]{2,1,0:T(8,128)S(1)}, f32[3,32,128]{2,1,0:T(8,128)S(1)}, u32[]{:S(2)}, u32[]{:S(2)}) collective-permute-start(f32[3,32,128]{2,1,0:T(8,128)S(1)} %get-tuple-element.30.refs_0_), channel_id=1, source_target_pairs={{0,6},{2,4},{4,2},{6,0},{8,14},{10,12},{12,10},{14,8},{16,22},{18,... | collective-permute-start | bytes 147464 | tf_op jit(solution)/shard_map/ppermute | solution.py:638
  37.5 4.0 %collective-permute-start.19 = (f32[2,32,128]{2,1,0:T(8,128)S(1)}, f32[2,32,128]{2,1,0:T(8,128)S(1)}, u32[]{:S(2)}, u32[]{:S(2)}) collective-permute-start(f32[2,32,128]{2,1,0:T(8,128)S(1)} %get-tuple-element.34), channel_id=1, source_target_pairs={{0,4},{2,6},{4,8},{6,10},{8,12},{10,14},{12,16},{14,18},{16,20},{1... | collective-permute-start | bytes 98312 | tf_op jit(solution)/shard_map/ppermute | solution.py:615
  39.8 6.4 %collective-permute-start.20 = (f32[2,32,128]{2,1,0:T(8,128)S(1)}, f32[2,32,128]{2,1,0:T(8,128)S(1)}, u32[]{:S(2)}, u32[]{:S(2)}) collective-permute-start(f32[2,32,128]{2,1,0:T(8,128)S(1)} %get-tuple-element.35), channel_id=1, source_target_pairs={{4,0},{6,2},{8,4},{10,6},{12,8},{14,10},{16,12},{18,14},{20,16},{2... | collective-permute-start | bytes 98312 | tf_op jit(solution)/shard_map/ppermute | solution.py:615
  41.4 14.5 %collective-permute-start.14 = (f32[4,2,32,128]{3,2,1,0:T(8,128)S(1)}, f32[4,2,32,128]{3,2,1,0:T(8,128)S(1)}, u32[]{:S(2)}, u32[]{:S(2)}) collective-permute-start(f32[4,2,32,128]{3,2,1,0:T(8,128)S(1)} %pad_maximum_fusion.refs_4_), channel_id=1, source_target_pairs={{0,8},{2,10},{4,12},{6,14},{8,0},{10,2},{12,4},{14,6},{16,24},{18,... | collective-permute-start | bytes 393224 | tf_op jit(solution)/shard_map/ppermute | solution.py:638
  46.2 15.1 %collective-permute-start.15 = (f32[4,2,32,128]{3,2,1,0:T(8,128)S(1)}, f32[4,2,32,128]{3,2,1,0:T(8,128)S(1)}, u32[]{:S(2)}, u32[]{:S(2)}) collective-permute-start(f32[4,2,32,128]{3,2,1,0:T(8,128)S(1)} %pad_maximum_fusion.refs_4_), channel_id=1, source_target_pairs={{0,16},{2,18},{4,20},{6,22},{8,24},{10,26},{12,28},{14,30},{16,0},... | collective-permute-start | bytes 393224 | tf_op jit(solution)/shard_map/ppermute | solution.py:638
  49.2 13.1 %collective-permute-start.16 = (f32[4,2,32,128]{3,2,1,0:T(8,128)S(1)}, f32[4,2,32,128]{3,2,1,0:T(8,128)S(1)}, u32[]{:S(2)}, u32[]{:S(2)}) collective-permute-start(f32[4,2,32,128]{3,2,1,0:T(8,128)S(1)} %pad_maximum_fusion.refs_4_), channel_id=1, source_target_pairs={{0,24},{2,26},{4,28},{6,30},{8,16},{10,18},{12,20},{14,22},{16,8},... | collective-permute-start | bytes 393224 | tf_op jit(solution)/shard_map/ppermute | solution.py:638
  50.5 21.1 %collective-permute-start.17 = (f32[14,32,128]{2,1,0:T(8,128)S(1)}, f32[14,32,128]{2,1,0:T(8,128)S(1)}, u32[]{:S(2)}, u32[]{:S(2)}) collective-permute-start(f32[14,32,128]{2,1,0:T(8,128)S(1)} %get-tuple-element.32), channel_id=1, source_target_pairs={{0,2},{2,4},{4,6},{6,8},{8,10},{10,12},{12,14},{14,16},{16,18},{18... | collective-permute-start | bytes 688136 | tf_op jit(solution)/shard_map/ppermute | solution.py:615
  53.6 18.1 %collective-permute-start.18 = (f32[14,32,128]{2,1,0:T(8,128)S(1)}, f32[14,32,128]{2,1,0:T(8,128)S(1)}, u32[]{:S(2)}, u32[]{:S(2)}) collective-permute-start(f32[14,32,128]{2,1,0:T(8,128)S(1)} %get-tuple-element.33), channel_id=1, source_target_pairs={{2,0},{4,2},{6,4},{8,6},{10,8},{12,10},{14,12},{16,14},{18,16},{20... | collective-permute-start | bytes 688136 | tf_op jit(solution)/shard_map/ppermute | solution.py:615
  55.9 11.5 %collective-permute-start.8 = (f32[6,32,128]{2,1,0:T(8,128)S(1)}, f32[6,32,128]{2,1,0:T(8,128)S(1)}, u32[]{:S(2)}, u32[]{:S(2)}) collective-permute-start(f32[6,32,128]{2,1,0:T(8,128)S(1)} %merge.1.refs_0_), channel_id=1, source_target_pairs={{0,8},{2,10},{4,12},{6,14},{8,0},{10,2},{12,4},{14,6},{16,24},{18,... | collective-permute-start | bytes 294920 | tf_op jit(solution)/shard_map/ppermute | solution.py:638
  61.4 10.3 %collective-permute-start.9 = (f32[6,32,128]{2,1,0:T(8,128)S(1)}, f32[6,32,128]{2,1,0:T(8,128)S(1)}, u32[]{:S(2)}, u32[]{:S(2)}) collective-permute-start(f32[6,32,128]{2,1,0:T(8,128)S(1)} %merge.1.refs_0_), channel_id=1, source_target_pairs={{0,16},{2,18},{4,20},{6,22},{8,24},{10,26},{12,28},{14,30},{16,0},... | collective-permute-start | bytes 294920 | tf_op jit(solution)/shard_map/ppermute | solution.py:638
  62.3 9.3 %collective-permute-start.10 = (f32[6,32,128]{2,1,0:T(8,128)S(1)}, f32[6,32,128]{2,1,0:T(8,128)S(1)}, u32[]{:S(2)}, u32[]{:S(2)}) collective-permute-start(f32[6,32,128]{2,1,0:T(8,128)S(1)} %merge.1.refs_0_), channel_id=1, source_target_pairs={{0,24},{2,26},{4,28},{6,30},{8,16},{10,18},{12,20},{14,22},{16,8},... | collective-permute-start | bytes 294920 | tf_op jit(solution)/shard_map/ppermute | solution.py:638

commit v3 on v2

v3 whole, which is shorter than its diff:
```python
import functools

import jax
import jax.numpy as jnp
from jax import lax
from jax.experimental import pallas as pl
from jax.experimental.pallas import tpu as pltpu
from jax.sharding import PartitionSpec as P

LEVELS = 6
COARSE_SWEEPS = 3
LANES = 128
BORDER = 128
FRINGE = 4
SPREAD = 16
relax_weight = 0.8
f32 = jnp.float32
VMEM_LIMIT = 40 * 1024 * 1024
START_LIMIT = 58 * 1024 * 1024
CHUNKS = 4


class Sizes:
    def __init__(self, depth, extent_x, extent_y, span_count, width_count):
        self.depth, self.extent_x, self.extent_y = depth, extent_x, extent_y
        self.span_count, self.width_count = span_count, width_count
        self.sides = min(width_count - 1, 2)
        self.own = [(extent_y >> level) // LANES for level in range(3)]
        self.border = [self.sides, min(self.sides, 1), min(self.sides, 1)]
        self.held = [(self.own[level] + self.border[level]) * LANES for level in range(3)] + [LANES] * 3
        self.rows = [extent_x >> level for level in range(4)]
        self.slots = []
        start = 0
        for level in (0, 1, 1, 1, 2, 2, 2):
            self.slots.append((start, self.own[level]))
            start += self.own[level]
        self.tiles = start


def put(message, slot, row):
    start, tiles = slot
    for tile in range(tiles):
        message[start + tile] = row[:, tile * LANES : (tile + 1) * LANES]


def get(message, slot):
    start, tiles = slot
    return [message[start + tile] for tile in range(tiles)]


def lane_at(shape):
    return lax.broadcasted_iota(jnp.int32, shape, len(shape) - 1)


def roll(value, steps, axis):
    return pltpu.roll(value, steps % value.shape[axis], axis=axis)


def reciprocal(value):
    return pltpu.reciprocal(value, approx=True)


def harmonic(first, second, guard):
    total = first + second
    if guard:
        total = jnp.maximum(total, 1e-3)
    return (2.0 * first) * second * reciprocal(total)


def split(value):
    high = value.astype(jnp.bfloat16)
    return high, (value - high.astype(f32)).astype(jnp.bfloat16)


def dot(halves, table):
    high, low = halves
    return jnp.dot(high, table, preferred_element_type=f32) + jnp.dot(low, table, preferred_element_type=f32)


def pair_table(fine, fine_dim, turn, weight):
    shape = (fine, LANES) if fine_dim == 0 else (LANES, fine)
    fine_at = lax.broadcasted_iota(jnp.int32, shape, fine_dim)
    coarse_at = lax.broadcasted_iota(jnp.int32, shape, 1 - fine_dim)
    if turn is not None:
        coarse_at = coarse_at - jnp.where(fine_at >= turn, LANES // 2, 0)
    return jnp.where(fine_at // 2 == coarse_at, weight, 0.0).astype(jnp.bfloat16)


def turns(sizes, place, level):
    if sizes.sides == 0:
        return []
    if level == 0:
        return [jnp.where(place[1] == 0, LANES, 0)] if sizes.sides == 1 else [LANES, 0]
    return [LANES // 2]


def transfer_plan(sizes, place, level, part):
    plan = []
    if level >= 3:
        return [((0, LANES), 0, 3 * LANES // 4)]
    if level == 2:
        return [((0, sizes.held[2]), 0, None)]
    own = sizes.own[level]
    if part != "border":
        plan += [((2 * LANES * tile, 2 * LANES * (tile + 1)), tile, None) for tile in range(own // 2)]
    if part != "own":
        for index, turn in enumerate(turns(sizes, place, level)):
            start = (own + index) * LANES
            plan.append(((start, start + LANES), own // 2, turn))
    return plan


def narrow(sizes, place, level, sums, target, rows, part="all", shift=0):
    depth = sums.shape[1]
    done = {}
    for (start, stop), tile, turn in transfer_plan(sizes, place, level, part):
        start, stop, tile = start - shift, stop - shift, tile - shift // (2 * LANES)
        columns = split(sums[0:rows, :, start:stop].reshape(rows * depth, stop - start))
        result = dot(columns, pair_table(stop - start, 0, turn, 0.25)).reshape(rows, depth, LANES)
        done[tile] = done[tile] + result if tile in done else result
    for tile, result in done.items():
        target[0:rows, :, tile * LANES : (tile + 1) * LANES] = result


def widen(sizes, place, level, coarse, target, rows):
    depth = coarse.shape[1]
    for (start, stop), tile, turn in transfer_plan(sizes, place, level, "all"):
        columns = split(coarse[0:rows, :, tile * LANES : (tile + 1) * LANES].reshape(rows * depth, LANES))
        result = dot(columns, pair_table(stop - start, 1, turn, 4.0))
        target[0:rows, :, start:stop] = result.reshape(rows, depth, stop - start)


def coefficients(sizes, place, level, count, conduct, binding, fx, fy, fz, weight):
    guard = level > 0 or sizes.sides > 1
    for row in range(1, count):
        fx[row - 1] = harmonic(conduct(row - 1), conduct(row), guard)
    for row in range(1, count - 1):
        mine = conduct(row)
        south = harmonic(mine, roll(mine, 1, 1), guard)
        if level == 0 and sizes.sides < 2:
            cut = 0 if sizes.sides == 0 else jnp.where(place[1] == 0, 0, sizes.extent_y)
            south = jnp.where(lane_at(mine.shape) == cut, 0.0, south)
        below = harmonic(mine, roll(mine, 1, 0), guard)
        below = jnp.where(lax.broadcasted_iota(jnp.int32, mine.shape, 0) == 0, 0.0, below)
        diagonal = fx[row - 1] + fx[row] + binding(row)
        diagonal = diagonal + (south + roll(south, -1, 1)) + (below + roll(below, -1, 0))
        if guard:
            diagonal = jnp.maximum(diagonal, 1e-6)
        fy[row - 1] = south
        fz[row - 1] = below
        weight[row - 1] = relax_weight * reciprocal(diagonal)


def sweep(count, field, binding, fx, fy, fz, emit):
    lower = fx[0] * (field(1) - field(0))
    for row in range(1, count - 1):
        mine = field(row)
        upper = fx[row] * (field(row + 1) - mine)
        south = fy[row - 1] * (mine - roll(mine, 1, 1))
        below = fz[row - 1] * (mine - roll(mine, 1, 0))
        across = (south - roll(south, -1, 1)) + (below - roll(below, -1, 0))
        emit(row, binding(row) * mine + (lower - upper) + across)
        lower = upper


def own_defect(count, smooth, source, binding, fx, fy, fz, sums, first):
    zero = jnp.zeros(smooth.shape[1:], f32)

    def field(row):
        return smooth[row - 1] if 0 < row < count - 1 else zero

    def add(row, value):
        slot = (row + first) // 2
        if (row + first) % 2 == 0 or row == 0:
            sums[slot] = value
        else:
            sums[slot] = sums[slot] + value

    add(0, fx[0] * field(1))
    sweep(count, field, binding, fx, fy, fz, lambda row, result: add(row, source(row) - result))
    add(count - 1, fx[count - 2] * field(count - 2))


def parts(array, counts):
    views, start = [], 0
    for count in counts:
        views.append(array.at[start : start + count])
        start += count
    return views


def coefficient_rows(sizes, level):
    n = sizes.rows[level]
    if level == 0:
        return [n + 1, n, n, n, n]
    return [n + 3] + [n + 2] * 6


def start_kernel(sizes, place, right_side, conduct, binding, own0, own1, own2, to_next, to_prev, top, *refs):
    edges, (inputs, sums, semaphores) = refs[: sizes.sides], refs[sizes.sides :]
    n0, n1, n2 = sizes.rows[:3]
    step = sizes.depth // CHUNKS
    loads = [[], [], []]
    for at, array in enumerate((conduct, binding, right_side)):
        for chunk in range(CHUNKS):
            part = pl.ds(chunk * step, step)
            copy = pltpu.make_async_copy(array.at[part], inputs.at[at, part], semaphores.at[at * CHUNKS + chunk])
            copy.start()
            loads[at].append(copy)

    def turn(at):
        for copy in loads[at]:
            copy.wait()
        own0[at] = jnp.swapaxes(inputs[at], 0, 1)

    tops = []
    for at in (0, 1):
        turn(at)
        for row in range(n1):
            sums[row] = own0[at, 2 * row] + own0[at, 2 * row + 1]
        narrow(sizes, place, 0, sums, own1.at[at], n1, "own")
        for row in range(n2):
            sums[row, :, : sizes.own[1] * LANES] = own1[at, 2 * row] + own1[at, 2 * row + 1]
        narrow(sizes, place, 1, sums, own2.at[at], n2, "own")
        tops.append(dot(split(own2[at, 0] + own2[at, 1]), pair_table(LANES, 0, None, 0.25)))
    for message, low, at1, at0 in ((to_next, n1 - 2, n1 - 1, n0 - 1), (to_prev, 0, 0, 0)):
        edge = n2 - 1 if at0 else 0
        rows = (own0[0, at0], own1[0, low], own1[0, low + 1], own1[1, at1])
        rows += (own2[0, n2 - 2], own2[0, n2 - 1], own2[1, edge])
        for slot, row in zip(sizes.slots, rows):
            put(message, slot, row)
    block = tops[0] + roll(tops[1], LANES // 2, 1)
    for device in range(sizes.span_count):
        top[device] = block
    turn(2)
    last = sizes.extent_y - BORDER
    if sizes.sides == 1:
        at = pl.multiple_of(jnp.where(place[1] == 0, last, 0), LANES)
        edges[0][...] = own0[:, :, :, pl.ds(at, BORDER)]
    elif sizes.sides == 2:
        edges[0][...] = own0[:, :, :, last:]
        edges[1][...] = own0[:, :, :, :BORDER]


def message_row(sizes, place, level, slot, message, beside):
    start, tiles = slot
    row = get(message, slot)
    if sizes.sides == 1:
        left = place[1] != 0
        tile = beside[0][start + jnp.where(left, tiles - 1, 0)]
        if level > 0:
            reach = BORDER >> level
            lane = lane_at(tile.shape)
            first = jnp.where(left, LANES - reach, 0)
            tile = jnp.where((lane >= first) & (lane < first + reach), tile, 0.0)
        row.append(tile)
    elif sizes.sides == 2:
        right, left = beside[0][start], beside[1][start + tiles - 1]
        if level == 0:
            row += [right, left]
        else:
            reach = BORDER >> level
            lane = lane_at(right.shape)
            row.append(jnp.where(lane < reach, right, jnp.where(lane >= LANES - reach, left, 0.0)))
    return jnp.concatenate(row, axis=1)


def fringe_lanes(shape):
    lane = lane_at(shape)
    return (lane < FRINGE) | (lane >= LANES - FRINGE)


def put_fringes(sizes, message, rows):
    total = None
    for index, (level, row) in enumerate(rows):
        tile = row[:, sizes.own[level] * LANES :]
        tile = jnp.where(fringe_lanes(tile.shape), tile, 0.0)
        tile = roll(tile, SPREAD * index + SPREAD // 2, 1)
        total = tile if total is None else total + tile
    message[sizes.tiles] = total


def fringed_row(sizes, level, index, message):
    row = get(message, sizes.slots[index])
    if sizes.border[level]:
        if level == 0:
            row += [jnp.zeros(row[0].shape, f32)] * sizes.border[0]
        else:
            tile = roll(message[sizes.tiles], -(SPREAD * (index - 1) + SPREAD // 2), 1)
            row.append(jnp.where(fringe_lanes(tile.shape), tile, 0.0))
    return jnp.concatenate(row, axis=1)


def pack_edges(sizes, place, rows, target):
    if sizes.sides != 1:
        for index, row in enumerate(rows):
            target(index, row)
        return
    half, reach = LANES // 2, BORDER >> 3
    lane = lane_at(rows[0].shape)
    target(0, jnp.where(lane < half, rows[0], pltpu.roll(rows[1], half, axis=1)))
    mixed = jnp.where(lane < half, rows[2], 0.0)
    for index, row in enumerate(rows):
        first = half + index * reach
        moved = pltpu.roll(row, border_turn(place, index), axis=1)
        mixed = jnp.where((lane >= first) & (lane < first + reach), moved, mixed)
    target(1, mixed)


def border_turn(place, index):
    reach = BORDER >> 3
    return jnp.where(place[1] == 0, index * reach, LANES // 2 + (index + 1) * reach)


def unpack_edges(sizes, place, blocks, row, count):
    total = None
    if sizes.sides != 1:
        for index, device in ((2, row - 1), (1, row), (0, row + 1)):
            if 0 <= device < count:
                value = blocks[device, index]
                total = value if total is None else total + value
        return total
    half, reach = LANES // 2, BORDER >> 3
    own = pltpu.roll(blocks[row, 0], half, axis=1)
    border = turned = None
    for index, device in ((2, row - 1), (1, row), (0, row + 1)):
        if 0 <= device < count:
            if index != 1:
                own = own + blocks[device, 0 if index == 0 else 1]
            back = lax.rem(LANES - border_turn(place, index), LANES)
            value = pltpu.roll(blocks[device, 1], back, axis=1)
            border = value if border is None else border + value
    lane = lane_at(own.shape)
    first = jnp.where(place[1] == 0, half, LANES - reach)
    return jnp.where(lane < half, own, jnp.where((lane >= first) & (lane < first + reach), border, 0.0))


def top_row(sizes, place, top, beside, row):
    half, reach = LANES // 2, BORDER >> 3
    block = top[row]
    lane = lane_at(block.shape)
    values = [jnp.where(lane < half, block, 0.0), jnp.where(lane < half, pltpu.roll(block, half, axis=1), 0.0)]
    right = (lane >= half) & (lane < half + reach)
    left = lane >= LANES - reach
    for side in range(sizes.sides):
        other = beside[side][row]
        if sizes.sides == 2:
            here = left if side else right
        else:
            first = jnp.where(place[1] == 0, half, LANES - reach)
            here = (lane >= first) & (lane < first + reach)
        values[0] = jnp.where(here, pltpu.roll(other, half, axis=1), values[0])
        values[1] = jnp.where(here, other, values[1])
    return values


def down_kernel(sizes, place, *refs):
    s = sizes.sides
    owns, refs = refs[:3], refs[3:]
    borders0, refs = refs[:s], refs[s:]
    from_prev, from_next, refs = refs[0], refs[1], refs[2:]
    beside_prev, beside_next, refs = refs[: 2 * s : 2], refs[1 : 2 * s : 2], refs[2 * s :]
    coefs, contribution, ups, fars, refs = refs[:3], refs[3], refs[4:6], refs[6:8], refs[8:]
    border1, border2, level3, sums = refs
    slots = sizes.slots
    n0, n1, n2 = sizes.rows[:3]

    if s:
        for at in (0, 1):
            for row in range(n1):
                for side in range(s):
                    columns = slice(side * LANES, (side + 1) * LANES)
                    sums[row, :, columns] = borders0[side][at, 2 * row] + borders0[side][at, 2 * row + 1]
            narrow(sizes, place, 0, sums, border1.at[at], n1, "border", sizes.own[0] * LANES)
            for row in range(n2):
                sums[row, :, :LANES] = border1[at, 2 * row] + border1[at, 2 * row + 1]
            narrow(sizes, place, 1, sums, border2.at[at], n2, "border", sizes.own[1] * LANES)
    borders = [borders0, [border1][:s], [border2][:s]]

    def held_row(level, at, row):
        return jnp.concatenate([owns[level][at, row], *(array[at, row] for array in borders[level])], axis=1)

    def prev_row(level, index):
        return message_row(sizes, place, level, slots[index], from_prev, beside_prev)

    def next_row(level, index):
        return message_row(sizes, place, level, slots[index], from_next, beside_next)

    def conduct0(row):
        if row == 0:
            return prev_row(0, 0)
        if row == n0 + 1:
            return next_row(0, 0)
        return held_row(0, 0, row - 1)

    bound0 = lambda row: held_row(0, 1, row - 1)
    fx, fy, fz, weight, v0 = parts(coefs[0], coefficient_rows(sizes, 0))
    coefficients(sizes, place, 0, n0 + 2, conduct0, bound0, fx, fy, fz, weight)
    for row in range(n0):
        v0[row] = weight[row] * held_row(0, 2, row)
    own_defect(n0 + 2, v0, lambda row: held_row(0, 2, row - 1), bound0, fx, fy, fz, sums, 1)
    smooths, sources = [], []
    for level, first in ((1, 1), (2, 4)):
        n = sizes.rows[level]
        fx, fy, fz, weight, binding, source, smooth = parts(coefs[level], coefficient_rows(sizes, level))
        held = sizes.held[level]
        narrow(sizes, place, level - 1, sums.at[:, :, : sizes.held[level - 1]], source, n + 2)
        binding[0] = prev_row(level, first + 2)
        binding[n + 1] = next_row(level, first + 2)
        for row in range(n):
            binding[row + 1] = held_row(level, 1, row)

        def conduct(row, n=n, level=level, first=first):
            if row < 2:
                return prev_row(level, first + row)
            if row >= n + 2:
                return next_row(level, first + row - n - 2)
            return held_row(level, 0, row - 2)

        bound = lambda row, binding=binding: binding[row - 1]
        coefficients(sizes, place, level, n + 4, conduct, bound, fx, fy, fz, weight)
        for row in range(n + 2):
            smooth[row] = weight[row] * source[row]
        mine = lambda row, source=source: source[row - 1]
        own_defect(n + 4, smooth, mine, bound, fx, fy, fz, sums.at[:, :, :held], 0)
        smooths.append(smooth)
        sources.append(source)
    narrow(sizes, place, 2, sums.at[:, :, : sizes.held[2]], level3, 3)

    def send(index, value):
        for device in range(sizes.span_count):
            contribution[device, index] = value

    pack_edges(sizes, place, [level3[row] for row in range(3)], send)
    (s1, s2), (v1, v2) = sources, smooths
    for at, rows in enumerate(
        (
            (v0[n0 - 1], s1[n1], s1[n1 + 1], v1[n1 - 1], s2[n2], s2[n2 + 1], v2[n2 - 1]),
            (v0[0], s1[1], s1[0], v1[2], s2[1], s2[0], v2[2]),
        )
    ):
        for slot, row in zip(slots, rows):
            put(ups[at], slot, row)
        if s:
            put_fringes(sizes, ups[at], list(zip((1, 1, 1, 2, 2, 2), rows[1:])))
        put(fars[at], (0, sizes.held[2] // LANES), v2[n2 + 1 if at == 0 else 0])


def up_kernel(sizes, place, blocks, top, *refs):
    s = sizes.sides
    tops, refs = refs[:s], refs[s:]
    (from_prev, from_next), fars, coefs, own0 = refs[:2], refs[2:4], refs[4:7], refs[7]
    borders0, out, refs = refs[8 : 8 + s], refs[8 + s], refs[9 + s :]
    total1, total2, sums, result = refs[:4]
    coarse = [refs[4 + 9 * index : 13 + 9 * index] for index in range(3)]
    over2, over1, over0, lift2, lift1, lift0, it2, it1, it0, semaphores = refs[31:]
    slots = sizes.slots
    n0, n1, n2 = sizes.rows[:3]
    total = sizes.span_count
    width = sizes.own[0] * LANES

    zero = jnp.zeros((sizes.depth, LANES), f32)
    for index in range(3):
        level = 3 + index
        fx, fy, fz, weight, conduct, binding, source, smooth, iterate = coarse[index]
        count = total >> index
        for array in (conduct, smooth, iterate):
            array[0] = zero
            array[count + 1] = zero
        if index == 0:
            for row in range(count):
                conduct[row + 1], binding[row] = top_row(sizes, place, top, tops, row)
                source[row] = unpack_edges(sizes, place, blocks, row, count)
        bound = lambda row, binding=binding: binding[row - 1]
        at_row = lambda row, conduct=conduct: conduct[row]
        coefficients(sizes, place, level, count + 2, at_row, bound, fx, fy, fz, weight)
        for row in range(count):
            smooth[row + 1] = weight[row] * source[row]
        if index < 2:
            conduct_next, binding_next, source_next = coarse[index + 1][4:7]
            half = count // 2
            for row in range(half):
                sums[row, :, :LANES] = conduct[2 * row + 1] + conduct[2 * row + 2]
            narrow(sizes, place, level, sums, conduct_next.at[1 : half + 1], half)
            for row in range(half):
                sums[row, :, :LANES] = binding[2 * row] + binding[2 * row + 1]
            narrow(sizes, place, level, sums, binding_next, half)

            def add(row, value, source=source):
                value = source[row - 1] - value
                slot = (row - 1) // 2
                if row % 2 == 1:
                    sums[slot, :, :LANES] = value
                else:
                    sums[slot, :, :LANES] = sums[slot, :, :LANES] + value

            sweep(count + 2, lambda row, smooth=smooth: smooth[row], bound, fx, fy, fz, add)
            narrow(sizes, place, level, sums, source_next, half)

    def relax(count, field, refs_of, source, target):
        fx, fy, fz, weight, binding = refs_of

        def update(row, value):
            target(row, field(row) + weight[row - 1] * (source(row) - value))

        sweep(count, field, binding, fx, fy, fz, update)

    def store(array, first):
        def put_row(row, value):
            array[row - first] = value

        return put_row

    fx, fy, fz, weight, conduct, binding, source, smooth, iterate = coarse[2]
    held, other = smooth, iterate
    for _ in range(COARSE_SWEEPS - 1):
        field = lambda row, held=held: held[row]
        mine = lambda row: source[row - 1]
        bound = lambda row: binding[row - 1]
        relax((total >> 2) + 2, field, (fx, fy, fz, weight, bound), mine, store(other, 0))
        held, other = other, held
    for index in (1, 0):
        fx, fy, fz, weight, conduct, binding, source, smooth, iterate = coarse[index]
        count = total >> index
        widen(sizes, place, 3 + index, held.at[1 : count // 2 + 1], sums, count // 2)
        for row in range(count):
            smooth[row + 1] = smooth[row + 1] + sums[row // 2, :, :LANES]
        field = lambda row, smooth=smooth: smooth[row]
        mine = lambda row, source=source: source[row - 1]
        bound = lambda row, binding=binding: binding[row - 1]
        relax(count + 2, field, (fx, fy, fz, weight, bound), mine, store(iterate, 0))
        held = iterate

    widen(sizes, place, 2, held.at[pl.ds(place[0], 3)], over2, 3)
    for level, array, first, totals, over, lift, target, upper in (
        (2, coefs[2], 4, total2, over2, lift2, it2, over1),
        (1, coefs[1], 1, total1, over1, lift1, it1, over0),
    ):
        n = sizes.rows[level]
        fx, fy, fz, weight, binding, own, smooth = parts(array, coefficient_rows(sizes, level))
        edge = {}
        for row, message, index in (
            (1, from_prev, first),
            (2, from_prev, first + 1),
            (n + 2, from_next, first),
            (n + 1, from_next, first + 1),
        ):
            value = edge.get(row, own[row - 1])
            edge[row] = value + fringed_row(sizes, level, index, message)
        for row, value in edge.items():
            totals[row - 1] = value
        for row in range(n + 4):
            if row in (0, n + 3):
                value = fringed_row(sizes, level, first + 2, from_next if row else from_prev)
                if level == 2:
                    far = fars[1 if row else 0]
                    value = value + jnp.concatenate(get(far, (0, sizes.held[2] // LANES)), axis=1)
            elif row in edge:
                value = weight[row - 1] * totals[row - 1]
            else:
                value = smooth[row - 1]
            lift[row] = value + over[row // 2]
        field = lambda row, lift=lift: lift[row]
        mine = lambda row, own=own, totals=totals, edge=edge: (totals if row in edge else own)[row - 1]
        bound = lambda row, binding=binding: binding[row - 1]
        relax(n + 4, field, (fx, fy, fz, weight, bound), mine, store(target, 1))
        widen(sizes, place, level - 1, target, upper, n + 2)

    def held_row(at, row):
        return jnp.concatenate([own0[at, row - 1], *(array[at, row - 1] for array in borders0)], axis=1)

    fx, fy, fz, weight, v0 = parts(coefs[0], coefficient_rows(sizes, 0))
    lift0[0] = fringed_row(sizes, 0, 0, from_prev) + over0[0]
    lift0[n0 + 1] = fringed_row(sizes, 0, 0, from_next) + over0[n1 + 1]
    for row in range(1, n0 + 1):
        lift0[row] = v0[row - 1] + over0[(row + 1) // 2]
    field = lambda row: lift0[row]
    bound = lambda row: held_row(1, row)
    relax(n0 + 2, field, (fx, fy, fz, weight, bound), lambda row: held_row(2, row), store(it0, 1))
    step = sizes.depth // CHUNKS
    copies = []
    for chunk in range(CHUNKS):
        part = slice(chunk * step, (chunk + 1) * step)
        result[part] = jnp.swapaxes(it0[:, part, :width], 0, 1)
        copies.append(pltpu.make_async_copy(result.at[part], out.at[part], semaphores.at[chunk]))
        copies[-1].start()
    for copy in copies:
        copy.wait()


def call(body, name, outputs, scratch, place, inputs, limit=VMEM_LIMIT, copies=0, far_in=False, far_out=False):
    near, far = pl.BlockSpec(memory_space=pltpu.VMEM), pl.BlockSpec(memory_space=pl.ANY)
    scratch = [pltpu.VMEM(shape, f32) for shape in scratch]
    if copies:
        scratch.append(pltpu.SemaphoreType.DMA((copies,)))
    return pl.pallas_call(
        body,
        name=name,
        out_shape=[jax.ShapeDtypeStruct(shape, f32) for shape in outputs],
        in_specs=[pl.BlockSpec(memory_space=pltpu.SMEM)] + [far if far_in else near] * len(inputs),
        out_specs=[far if far_out else near] * len(outputs),
        scratch_shapes=scratch,
        compiler_params=pltpu.CompilerParams(vmem_limit_bytes=limit),
    )(place, *inputs)


def along(value, axis, steps):
    count = lax.axis_size(axis)
    initial, last = max(0, -steps), min(count, count - steps)
    return lax.ppermute(value, axis, [(source, source + steps) for source in range(initial, last)])


def beside(values, sizes):
    if sizes.sides == 1:
        return [[lax.ppermute(value, "width", [(0, 1), (1, 0)]) for value in values]]
    if sizes.sides == 2:
        return [[along(value, "width", steps) for value in values] for steps in (-1, 1)]
    return []


def to_all(value):
    return lax.all_to_all(value, "span", split_axis=0, concat_axis=0, tiled=True)


def on_device(right_side, diffusivity, reaction):
    depth, extent_x, extent_y = diffusivity.shape
    sizes = Sizes(depth, extent_x, extent_y, lax.axis_size("span"), lax.axis_size("width"))
    place = jnp.stack([lax.axis_index("span"), lax.axis_index("width")]).astype(jnp.int32)
    n0, n1, n2, n3 = sizes.rows
    s = sizes.sides
    tile = (depth, LANES)
    own = [(depth, count * LANES) for count in sizes.own]
    held = [(depth, count) for count in sizes.held]
    down_message = (sizes.tiles, *tile)
    up_message = (sizes.tiles + 1, *tile)
    own0, own1, own2, to_next, to_prev, top, *edges = call(
        functools.partial(start_kernel, sizes),
        "start",
        [(3, n0, *own[0]), (2, n1, *own[1]), (2, n2, *own[2]), down_message, down_message]
        + [(sizes.span_count, *tile)]
        + [(3, n0, depth, BORDER)] * s,
        [(3, *diffusivity.shape), (n1, *own[0])],
        place,
        [right_side, diffusivity, reaction],
        limit=START_LIMIT,
        copies=3 * CHUNKS,
        far_in=True,
    )
    halos = [along(to_next, "span", 1), along(to_prev, "span", -1)]
    if s == 1:
        borders = [lax.ppermute(edges[0], "width", [(0, 1), (1, 0)])]
    elif s == 2:
        borders = [along(edges[1], "width", -1), along(edges[0], "width", 1)]
    else:
        borders = []
    top, *halos = lax.optimization_barrier((top, *halos))
    sides = beside(halos, sizes)
    top = to_all(top)

    lengths = [sum(coefficient_rows(sizes, level)) for level in range(3)]
    far = (sizes.held[2] // LANES, *tile)
    coefs = [(lengths[level], *held[level]) for level in range(3)]
    downs = call(
        functools.partial(down_kernel, sizes),
        "down",
        [*coefs, (sizes.span_count, 2 if s == 1 else 3, *tile), up_message, up_message, far, far],
        [(2, n1, *tile), (2, n2, *tile), (3, *tile), (n1 + 2, *held[0])],
        place,
        [own0, own1, own2, *borders, *halos, *sum(sides, [])],
    )
    coefs_out, blocks, ups, fars = downs[:3], downs[3], downs[4:6], downs[6:8]
    blocks = to_all(blocks)
    tops = [side[0] for side in beside([top], sizes)]
    received = [along(ups[0], "span", 1), along(ups[1], "span", -1)]
    received += [along(fars[0], "span", 2), along(fars[1], "span", -2)]
    scratch = [(n1 + 2, *held[1]), (n2 + 2, *held[2]), (max(sizes.span_count // 2, 2), *tile), diffusivity.shape]
    for index in range(3):
        count = sizes.span_count >> index
        scratch += [(count + 1, *tile)] + [(count, *tile)] * 3 + [(count + 2, *tile)] + [(count, *tile)] * 2
        scratch += [(count + 2, *tile)] * 2
    scratch += [(n3 + 2, *held[2]), (n2 + 2, *held[1]), (n1 + 2, *held[0])]
    scratch += [(n2 + 4, *held[2]), (n1 + 4, *held[1]), (n0 + 2, *held[0])]
    scratch += [(n2 + 2, *held[2]), (n1 + 2, *held[1]), (n0, *held[0])]
    (correction,) = call(
        functools.partial(up_kernel, sizes),
        "up",
        [diffusivity.shape],
        scratch,
        place,
        [blocks, top, *tops, *received, *coefs_out, own0, *borders],
        copies=CHUNKS,
        far_out=True,
    )
    return correction


def solution(mesh):
    in_specs = (P(None, "span", "width"),) * 3
    return jax.shard_map(
        on_device, mesh=mesh, in_specs=in_specs, out_specs=P(None, "span", "width"), check_vma=False
    )
```

time: 80.2 us -> 81.5 us (1.016)
  local copies, waits for them, and re-layouts: 3.12 us -> 13.9 us
  starting transfers between devices: 38 us -> 31.5 us
  Pallas kernels: 20.4 us -> 14.6 us
  waiting for transfers between devices: 18.1 us -> 19.9 us
    ppermute x12 -> x0, starting transfers between devices: 23.8 us -> none  [swap(): lax.ppermute(value, 'span', [(device, device ^ step * stride) for device...]
    all_to_all x0 -> x2, starting transfers between devices: none -> 12.8 us  [to_all(): lax.all_to_all(value, 'span', split_axis=0, concat_axis=0, tiled=True)]
    unnamed x6 -> x28, local copies, waits for them, and re-layouts: 3.12 us -> 13.9 us
    ppermute x6, waiting for transfers between devices: 10.2 us -> 18.2 us  [along(): lax.ppermute(value, axis, [(source, source + steps) for source in range(i...]
    ppermute x12 -> x0, waiting for transfers between devices: 7.86 us -> none  [swap(): lax.ppermute(value, 'span', [(device, device ^ step * stride) for device...]
    pallas_call x5 -> x3, Pallas kernels: 20.4 us -> 14.6 us  [call(): pl.pallas_call(body, name=name, out_shape=[jax.ShapeDtypeStruct(shape, f3...]
    ppermute x6, starting transfers between devices: 14.1 us -> 17.9 us  [along(): lax.ppermute(value, axis, [(source, source + steps) for source in range(i...]
    ppermute x1, waiting for transfers between devices: 0.01 us -> 1.34 us  [on_device(): borders = [lax.ppermute(edges[0], 'width', [(0, 1), (1, 0)])]]
  transfers between devices with their start and end apart: 21 -> 12, of which waited for: 6 -> 9; matrix products, arithmetic and copies ran while one was open for 0% -> 0% of each run, Pallas kernels for 12% -> 6%
where the time goes in v3:
time: 81.5 us; the launch traced here: 80.8 us
  starting transfers between devices  31.5 us (39%)
  waiting for transfers between devices  19.9 us (24%)
  Pallas kernels  14.6 us (18%)
  local copies, waits for them, and re-layouts  13.9 us (17%)
    ppermute x6, waiting for transfers between devices, along(): lax.ppermute(value, axis, [(source, source + steps) for source in range(i...  18.2 us
    ppermute x6, starting transfers between devices, along(): lax.ppermute(value, axis, [(source, source + steps) for source in range(i...  17.9 us
    pallas_call x3, Pallas kernels, call(): pl.pallas_call(body, name=name, out_shape=[jax.ShapeDtypeStruct(shape, f3...  14.6 us
    unnamed x28, local copies, waits for them, and re-layouts  13.9 us
    all_to_all x2, starting transfers between devices, to_all(): lax.all_to_all(value, 'span', split_axis=0, concat_axis=0, tiled=True)  12.8 us
  transfers between devices with their start and end apart: 12, of which 9 were waited for; matrix products, arithmetic and copies ran while one was open for 0% of the time, Pallas kernels for 6%

profile of v3, /device:TPU:0, one launch (start us, length us, event | category | flops | bytes accessed | tf_op | source)
XLA Modules:
  0.0 80.8 jit_solution(13659901746518426015)
XLA Ops:
  0.7 4.7 %start.1 = (f32[3,8,32,512]{3,2,1,0:T(8,128)}, f32[2,4,32,256]{3,2,1,0:T(8,128)}, f32[2,2,32,128]{3,2,1,0:T(8,128)}, f32[13,32,128]{2,1,0:T(8,128)}, f32[13,32,1...) custom-call(s32[2]{0:T(128)} %pad_add_fusion.place, f32[32,8,512]{2,1,0:T(8,128)} %right_side.1, ...), custom_call_target="tpu_custom_call" | custom-call | tf_op jit(solution)/shard_map/start/pallas_call | solution.py:596
  5.3 4.9 %collective-permute-start.1 = (f32[13,32,128]{2,1,0:T(8,128)}, f32[13,32,128]{2,1,0:T(8,128)S(1)}, u32[]{:S(2)}, u32[]{:S(2)}) collective-permute-start(f32[13,32,128]{2,1,0:T(8,128)} %get-tuple-element.28), channel_id=1, source_target_pairs={{0,2},{2,4},{4,6},{6,8},{8,10},{10,12},{12,14},{14,16},{16,18},{18... | collective-permute-start | bytes 638984 | tf_op jit(solution)/shard_map/ppermute | solution.py:610
  10.2 1.3 %collective-permute-start.2 = (f32[13,32,128]{2,1,0:T(8,128)}, f32[13,32,128]{2,1,0:T(8,128)S(1)}, u32[]{:S(2)}, u32[]{:S(2)}) collective-permute-start(f32[13,32,128]{2,1,0:T(8,128)} %get-tuple-element.29), channel_id=1, source_target_pairs={{2,0},{4,2},{6,4},{8,6},{10,8},{12,10},{14,12},{16,14},{18,16},{20... | collective-permute-start | bytes 638984 | tf_op jit(solution)/shard_map/ppermute | solution.py:610
  11.5 3.5 %collective-permute-done.1.refs_4_ = f32[13,32,128]{2,1,0:T(8,128)S(1)} collective-permute-done((f32[13,32,128]{2,1,0:T(8,128)}, f32[13,32,128]{2,1,0:T(8,128)S(1)}, u32[]{:S(2)}, u32[]{:S(2)}) %collective-permute-start.1) | collective-permute-done | bytes 213024 | tf_op jit(solution)/shard_map/ppermute | solution.py:610
  15.0 6.4 %collective-permute-done.2.refs_5_ = f32[13,32,128]{2,1,0:T(8,128)S(1)} collective-permute-done((f32[13,32,128]{2,1,0:T(8,128)}, f32[13,32,128]{2,1,0:T(8,128)S(1)}, u32[]{:S(2)}, u32[]{:S(2)}) %collective-permute-start.2) | collective-permute-done | bytes 213024 | tf_op jit(solution)/shard_map/ppermute | solution.py:610
  21.4 5.9 %all-to-all-start.1 = ((f32[16,32,128]{2,1,0:T(8,128)}), f32[16,32,128]{2,1,0:T(8,128)S(1)}, u32[]{:S(2)}, u32[]{:S(2)}) async-start(f32[16,32,128]{2,1,0:T(8,128)} %get-tuple-element.33), calls=%async_computation.1 | async-start | bytes 524288 | tf_op jit(solution)/shard_map/all_to_all | solution.py:622
  28.0 1.3 %collective-permute-done.refs_3_.refs_9_ = f32[3,8,32,128]{3,2,1,0:T(8,128)S(1)} collective-permute-done((f32[3,8,32,128]{3,2,1,0:T(8,128)}, f32[3,8,32,128]{3,2,1,0:T(8,128)S(1)}, u32[]{:S(2)}, u32[]{:S(2)}) %collective-permute-start) | collective-permute-done | bytes 393248 | tf_op jit(solution)/shard_map/ppermute | solution.py:651
  29.7 1.4 %copy-done = f32[3,8,32,512]{3,2,1,0:T(8,128)S(1)} copy-done((f32[3,8,32,512]{3,2,1,0:T(8,128)S(1)}, f32[3,8,32,512]{3,2,1,0:T(8,128)}, u32[]{:S(2)}) %copy-start) | copy-done | bytes 1572888
  33.6 4.6 %down.1 = (f32[41,32,640]{2,1,0:T(8,128)S(1)}, f32[43,32,384]{2,1,0:T(8,128)S(1)}, f32[29,32,256]{2,1,0:T(8,128)S(1)}, f32[16,2,32,128]{3,2,1,0:T(8,128)}, f32[1...) custom-call(s32[2]{0:T(128)S(1)} %copy-done.10, ...), custom_call_target="tpu_custom_call" | custom-call | tf_op jit(solution)/shard_map/down/pallas_call | solution.py:596
  38.2 1.7 %copy-done.2 = f32[41,32,640]{2,1,0:T(8,128)} copy-done((f32[41,32,640]{2,1,0:T(8,128)}, f32[41,32,640]{2,1,0:T(8,128)S(1)}, u32[]{:S(2)}) %copy-start.2) | copy-done | bytes 3358744
  39.9 1.3 %copy-done.4 = f32[43,32,384]{2,1,0:T(8,128)} copy-done((f32[43,32,384]{2,1,0:T(8,128)}, f32[43,32,384]{2,1,0:T(8,128)S(1)}, u32[]{:S(2)}) %copy-start.4) | copy-done | bytes 2113560
  43.5 6.9 %all-to-all-start = ((f32[16,2,32,128]{3,2,1,0:T(8,128)}), f32[16,2,32,128]{3,2,1,0:T(8,128)S(1)}, u32[]{:S(2)}, u32[]{:S(2)}) async-start(f32[16,2,32,128]{3,2,1,0:T(8,128)} %get-tuple-element.32), calls=%async_computation | async-start | bytes 1048576 | tf_op jit(solution)/shard_map/all_to_all | solution.py:622
  50.5 3.8 %collective-permute-start.6 = (f32[14,32,128]{2,1,0:T(8,128)}, f32[14,32,128]{2,1,0:T(8,128)S(1)}, u32[]{:S(2)}, u32[]{:S(2)}) collective-permute-start(f32[14,32,128]{2,1,0:T(8,128)} %get-tuple-element.34), channel_id=1, source_target_pairs={{0,2},{2,4},{4,6},{6,8},{8,10},{10,12},{12,14},{14,16},{16,18},{18... | collective-permute-start | bytes 688136 | tf_op jit(solution)/shard_map/ppermute | solution.py:610
  54.3 1.3 %collective-permute-start.7 = (f32[14,32,128]{2,1,0:T(8,128)}, f32[14,32,128]{2,1,0:T(8,128)S(1)}, u32[]{:S(2)}, u32[]{:S(2)}) collective-permute-start(f32[14,32,128]{2,1,0:T(8,128)} %copy-done.12), channel_id=1, source_target_pairs={{2,0},{4,2},{6,4},{8,6},{10,8},{12,10},{14,12},{16,14},{18,16},{20... | collective-permute-start | bytes 688136 | tf_op jit(solution)/shard_map/ppermute | solution.py:610
  55.6 5.4 %collective-permute-start.8 = (f32[2,32,128]{2,1,0:T(8,128)}, f32[2,32,128]{2,1,0:T(8,128)S(1)}, u32[]{:S(2)}, u32[]{:S(2)}) collective-permute-start(f32[2,32,128]{2,1,0:T(8,128)} %get-tuple-element.36), channel_id=1, source_target_pairs={{0,4},{2,6},{4,8},{6,10},{8,12},{10,14},{12,16},{14,18},{16,20},{1... | collective-permute-start | bytes 98312 | tf_op jit(solution)/shard_map/ppermute | solution.py:610
  61.0 1.3 %collective-permute-start.9 = (f32[2,32,128]{2,1,0:T(8,128)}, f32[2,32,128]{2,1,0:T(8,128)S(1)}, u32[]{:S(2)}, u32[]{:S(2)}) collective-permute-start(f32[2,32,128]{2,1,0:T(8,128)} %copy-done.13), channel_id=1, source_target_pairs={{4,0},{6,2},{8,4},{10,6},{12,8},{14,10},{16,12},{18,14},{20,16},{2... | collective-permute-start | bytes 98312 | tf_op jit(solution)/shard_map/ppermute | solution.py:610
  62.3 2.6 %collective-permute-done.8.refs_3_ = f32[2,32,128]{2,1,0:T(8,128)S(1)} collective-permute-done((f32[2,32,128]{2,1,0:T(8,128)}, f32[2,32,128]{2,1,0:T(8,128)S(1)}, u32[]{:S(2)}, u32[]{:S(2)}) %collective-permute-start.8) | collective-permute-done | bytes 32800 | tf_op jit(solution)/shard_map/ppermute | solution.py:610
  64.9 2.5 %collective-permute-done.9.refs_4_ = f32[2,32,128]{2,1,0:T(8,128)S(1)} collective-permute-done((f32[2,32,128]{2,1,0:T(8,128)}, f32[2,32,128]{2,1,0:T(8,128)S(1)}, u32[]{:S(2)}, u32[]{:S(2)}) %collective-permute-start.9) | collective-permute-done | bytes 32800 | tf_op jit(solution)/shard_map/ppermute | solution.py:610
  67.4 1.2 %collective-permute-done.6.refs_1_ = f32[14,32,128]{2,1,0:T(8,128)S(1)} collective-permute-done((f32[14,32,128]{2,1,0:T(8,128)}, f32[14,32,128]{2,1,0:T(8,128)S(1)}, u32[]{:S(2)}, u32[]{:S(2)}) %collective-permute-start.6) | collective-permute-done | bytes 229408 | tf_op jit(solution)/shard_map/ppermute | solution.py:610
  68.6 2.0 %collective-permute-done.7.refs_2_ = f32[14,32,128]{2,1,0:T(8,128)S(1)} collective-permute-done((f32[14,32,128]{2,1,0:T(8,128)}, f32[14,32,128]{2,1,0:T(8,128)S(1)}, u32[]{:S(2)}, u32[]{:S(2)}) %collective-permute-start.7) | collective-permute-done | bytes 229408 | tf_op jit(solution)/shard_map/ppermute | solution.py:610
  70.6 1.9 %copy-done.3 = f32[41,32,640]{2,1,0:T(8,128)S(1)} copy-done((f32[41,32,640]{2,1,0:T(8,128)S(1)}, f32[41,32,640]{2,1,0:T(8,128)}, u32[]{:S(2)}) %copy-start.3) | copy-done | bytes 3358744
  72.5 1.6 %copy-done.5 = f32[43,32,384]{2,1,0:T(8,128)S(1)} copy-done((f32[43,32,384]{2,1,0:T(8,128)S(1)}, f32[43,32,384]{2,1,0:T(8,128)}, u32[]{:S(2)}) %copy-start.5) | copy-done | bytes 2113560
  74.1 1.2 %copy-done.7 = f32[29,32,256]{2,1,0:T(8,128)S(1)} copy-done((f32[29,32,256]{2,1,0:T(8,128)S(1)}, f32[29,32,256]{2,1,0:T(8,128)}, u32[]{:S(2)}) %copy-start.7) | copy-done | bytes 950296
  75.3 5.4 %up.1 = f32[32,8,512]{2,1,0:T(8,128)} custom-call(s32[2]{0:T(128)S(1)} %copy-done.11, f32[16,2,32,128]{3,2,1,0:T(8,128)S(1)} %all-to-all-done.blocks, f32[16,32,128]{2,1,0:T(8,128)S(1)} %all-to-all-done.1.top, f32[16,32,128]{2,1,0:T(8,128)S(1)} %collective-permute-done.5.refs_0_, f32[14,32,128]{2,1,0:T(8,128)S(1)} %collective-permute-done.6.refs_1_, ...), custom_call_target="tpu_custom_call" | custom-call | tf_op jit(solution)/shard_map/up/pallas_call | solution.py:596
  (32 shorter events, 6.5 us)
Async XLA Ops:
  5.3 9.7 %collective-permute-start.1 = (f32[13,32,128]{2,1,0:T(8,128)}, f32[13,32,128]{2,1,0:T(8,128)S(1)}, u32[]{:S(2)}, u32[]{:S(2)}) collective-permute-start(f32[13,32,128]{2,1,0:T(8,128)} %get-tuple-element.28), channel_id=1, source_target_pairs={{0,2},{2,4},{4,6},{6,8},{8,10},{10,12},{12,14},{14,16},{16,18},{18... | collective-permute-start | bytes 638984 | tf_op jit(solution)/shard_map/ppermute | solution.py:610
  10.2 11.2 %collective-permute-start.2 = (f32[13,32,128]{2,1,0:T(8,128)}, f32[13,32,128]{2,1,0:T(8,128)S(1)}, u32[]{:S(2)}, u32[]{:S(2)}) collective-permute-start(f32[13,32,128]{2,1,0:T(8,128)} %get-tuple-element.29), channel_id=1, source_target_pairs={{2,0},{4,2},{6,4},{8,6},{10,8},{12,10},{14,12},{16,14},{18,16},{20... | collective-permute-start | bytes 638984 | tf_op jit(solution)/shard_map/ppermute | solution.py:610
  21.4 22.1 %all-to-all-start.1 = ((f32[16,32,128]{2,1,0:T(8,128)}), f32[16,32,128]{2,1,0:T(8,128)S(1)}, u32[]{:S(2)}, u32[]{:S(2)}) async-start(f32[16,32,128]{2,1,0:T(8,128)} %get-tuple-element.33), calls=%async_computation.1 | async-start | bytes 524288 | tf_op jit(solution)/shard_map/all_to_all | solution.py:622
  27.3 43.3 %copy-start.11 = (s32[2]{0:T(128)S(1)}, s32[2]{0:T(128)}, u32[]{:S(2)}) copy-start(s32[2]{0:T(128)} %pad_add_fusion.place) | copy-start | bytes 28
  27.3 2.0 %collective-permute-start = (f32[3,8,32,128]{3,2,1,0:T(8,128)}, f32[3,8,32,128]{3,2,1,0:T(8,128)S(1)}, u32[]{:S(2)}, u32[]{:S(2)}) collective-permute-start(f32[3,8,32,128]{3,2,1,0:T(8,128)} %get-tuple-element.26), channel_id=1, source_target_pairs={{0,1},{1,0},{2,3},{3,2},{4,5},{5,4},{6,7},{7,6},{8,9},{9,8},{10,11... | collective-permute-start | bytes 1179656 | tf_op jit(solution)/shard_map/ppermute | solution.py:651
  27.4 2.0 %collective-permute-start.3 = (f32[13,32,128]{2,1,0:T(8,128)S(1)}, f32[13,32,128]{2,1,0:T(8,128)S(1)}, u32[]{:S(2)}, u32[]{:S(2)}) collective-permute-start(f32[13,32,128]{2,1,0:T(8,128)S(1)} %collective-permute-done.1.refs_4_), channel_id=1, source_target_pairs={{0,1},{1,0},{2,3},{3,2},{4,5},{5,4},{6,7},{7,6},{8,9},{9,8},{10,11... | collective-permute-start | bytes 638984 | tf_op jit(solution)/shard_map/ppermute | solution.py:615
  27.9 1.8 %collective-permute-start.4 = (f32[13,32,128]{2,1,0:T(8,128)S(1)}, f32[13,32,128]{2,1,0:T(8,128)S(1)}, u32[]{:S(2)}, u32[]{:S(2)}) collective-permute-start(f32[13,32,128]{2,1,0:T(8,128)S(1)} %collective-permute-done.2.refs_5_), channel_id=1, source_target_pairs={{0,1},{1,0},{2,3},{3,2},{4,5},{5,4},{6,7},{7,6},{8,9},{9,8},{10,11... | collective-permute-start | bytes 638984 | tf_op jit(solution)/shard_map/ppermute | solution.py:615
  29.7 1.4 %copy-start = (f32[3,8,32,512]{3,2,1,0:T(8,128)S(1)}, f32[3,8,32,512]{3,2,1,0:T(8,128)}, u32[]{:S(2)}) copy-start(f32[3,8,32,512]{3,2,1,0:T(8,128)} %get-tuple-element.23.refs_0_.refs_8_) | copy-start | bytes 4718596
  31.1 0.9 %copy-start.8 = (f32[2,4,32,256]{3,2,1,0:T(8,128)S(1)}, f32[2,4,32,256]{3,2,1,0:T(8,128)}, u32[]{:S(2)}) copy-start(f32[2,4,32,256]{3,2,1,0:T(8,128)} %get-tuple-element.24.refs_1_) | copy-start | bytes 786436
  32.1 0.8 %copy-start.9 = (f32[2,2,32,128]{3,2,1,0:T(8,128)S(1)}, f32[2,2,32,128]{3,2,1,0:T(8,128)}, u32[]{:S(2)}) copy-start(f32[2,2,32,128]{3,2,1,0:T(8,128)} %get-tuple-element.25.refs_2_) | copy-start | bytes 196612
  33.6 37.0 %copy-start.1 = (f32[3,8,32,512]{3,2,1,0:T(8,128)S(1)}, f32[3,8,32,512]{3,2,1,0:T(8,128)}, u32[]{:S(2)}) copy-start(f32[3,8,32,512]{3,2,1,0:T(8,128)} %get-tuple-element.23.refs_0_.refs_8_) | copy-start | bytes 4718596
  38.2 1.7 %copy-start.2 = (f32[41,32,640]{2,1,0:T(8,128)}, f32[41,32,640]{2,1,0:T(8,128)S(1)}, u32[]{:S(2)}) copy-start(f32[41,32,640]{2,1,0:T(8,128)S(1)} %get-tuple-element.38.refs_5_) | copy-start | bytes 10076164
  39.9 1.3 %copy-start.4 = (f32[43,32,384]{2,1,0:T(8,128)}, f32[43,32,384]{2,1,0:T(8,128)S(1)}, u32[]{:S(2)}) copy-start(f32[43,32,384]{2,1,0:T(8,128)S(1)} %get-tuple-element.39.refs_6_) | copy-start | bytes 6340612
  41.2 1.0 %copy-start.6 = (f32[29,32,256]{2,1,0:T(8,128)}, f32[29,32,256]{2,1,0:T(8,128)S(1)}, u32[]{:S(2)}) copy-start(f32[29,32,256]{2,1,0:T(8,128)S(1)} %get-tuple-element.40.refs_7_) | copy-start | bytes 2850820
  42.2 0.7 copy-start.12
  43.5 27.1 %all-to-all-start = ((f32[16,2,32,128]{3,2,1,0:T(8,128)}), f32[16,2,32,128]{3,2,1,0:T(8,128)S(1)}, u32[]{:S(2)}, u32[]{:S(2)}) async-start(f32[16,2,32,128]{3,2,1,0:T(8,128)} %get-tuple-element.32), calls=%async_computation | async-start | bytes 1048576 | tf_op jit(solution)/shard_map/all_to_all | solution.py:622
  50.4 20.2 %collective-permute-start.5 = (f32[16,32,128]{2,1,0:T(8,128)S(1)}, f32[16,32,128]{2,1,0:T(8,128)S(1)}, u32[]{:S(2)}, u32[]{:S(2)}) collective-permute-start(f32[16,32,128]{2,1,0:T(8,128)S(1)} %all-to-all-done.1.top), channel_id=1, source_target_pairs={{0,1},{1,0},{2,3},{3,2},{4,5},{5,4},{6,7},{7,6},{8,9},{9,8},{10,11... | collective-permute-start | bytes 786440 | tf_op jit(solution)/shard_map/ppermute | solution.py:615
  50.5 18.1 %collective-permute-start.6 = (f32[14,32,128]{2,1,0:T(8,128)}, f32[14,32,128]{2,1,0:T(8,128)S(1)}, u32[]{:S(2)}, u32[]{:S(2)}) collective-permute-start(f32[14,32,128]{2,1,0:T(8,128)} %get-tuple-element.34), channel_id=1, source_target_pairs={{0,2},{2,4},{4,6},{6,8},{8,10},{10,12},{12,14},{14,16},{16,18},{18... | collective-permute-start | bytes 688136 | tf_op jit(solution)/shard_map/ppermute | solution.py:610
  54.3 16.3 %collective-permute-start.7 = (f32[14,32,128]{2,1,0:T(8,128)}, f32[14,32,128]{2,1,0:T(8,128)S(1)}, u32[]{:S(2)}, u32[]{:S(2)}) collective-permute-start(f32[14,32,128]{2,1,0:T(8,128)} %copy-done.12), channel_id=1, source_target_pairs={{2,0},{4,2},{6,4},{8,6},{10,8},{12,10},{14,12},{16,14},{18,16},{20... | collective-permute-start | bytes 688136 | tf_op jit(solution)/shard_map/ppermute | solution.py:610
  55.6 9.3 %collective-permute-start.8 = (f32[2,32,128]{2,1,0:T(8,128)}, f32[2,32,128]{2,1,0:T(8,128)S(1)}, u32[]{:S(2)}, u32[]{:S(2)}) collective-permute-start(f32[2,32,128]{2,1,0:T(8,128)} %get-tuple-element.36), channel_id=1, source_target_pairs={{0,4},{2,6},{4,8},{6,10},{8,12},{10,14},{12,16},{14,18},{16,20},{1... | collective-permute-start | bytes 98312 | tf_op jit(solution)/shard_map/ppermute | solution.py:610
  61.0 6.4 %collective-permute-start.9 = (f32[2,32,128]{2,1,0:T(8,128)}, f32[2,32,128]{2,1,0:T(8,128)S(1)}, u32[]{:S(2)}, u32[]{:S(2)}) collective-permute-start(f32[2,32,128]{2,1,0:T(8,128)} %copy-done.13), channel_id=1, source_target_pairs={{4,0},{6,2},{8,4},{10,6},{12,8},{14,10},{16,12},{18,14},{20,16},{2... | collective-permute-start | bytes 98312 | tf_op jit(solution)/shard_map/ppermute | solution.py:610
  70.6 2.0 %copy-start.3 = (f32[41,32,640]{2,1,0:T(8,128)S(1)}, f32[41,32,640]{2,1,0:T(8,128)}, u32[]{:S(2)}) copy-start(f32[41,32,640]{2,1,0:T(8,128)} %copy-done.2) | copy-start | bytes 10076164
  72.5 1.6 %copy-start.5 = (f32[43,32,384]{2,1,0:T(8,128)S(1)}, f32[43,32,384]{2,1,0:T(8,128)}, u32[]{:S(2)}) copy-start(f32[43,32,384]{2,1,0:T(8,128)} %copy-done.4) | copy-start | bytes 6340612
  74.1 1.2 %copy-start.7 = (f32[29,32,256]{2,1,0:T(8,128)S(1)}, f32[29,32,256]{2,1,0:T(8,128)}, u32[]{:S(2)}) copy-start(f32[29,32,256]{2,1,0:T(8,128)} %copy-done.6) | copy-start | bytes 2850820
  (2 other events, 1.3 us)

commit v4 on v3

--- a/solution.py
+++ b/solution.py
@@ -15,8 +15,7 @@
 SPREAD = 16
 relax_weight = 0.8
 f32 = jnp.float32
-VMEM_LIMIT = 40 * 1024 * 1024
-START_LIMIT = 58 * 1024 * 1024
+VMEM_LIMIT = 32 * 1024 * 1024
 CHUNKS = 4
 
 
@@ -197,42 +196,26 @@
 
 
 def start_kernel(sizes, place, right_side, conduct, binding, own0, own1, own2, to_next, to_prev, top, *refs):
-    edges, (inputs, sums, semaphores) = refs[: sizes.sides], refs[sizes.sides :]
+    edges, sums = refs[: sizes.sides], refs[-1]
     n0, n1, n2 = sizes.rows[:3]
-    step = sizes.depth // CHUNKS
-    loads = [[], [], []]
     for at, array in enumerate((conduct, binding, right_side)):
-        for chunk in range(CHUNKS):
-            part = pl.ds(chunk * step, step)
-            copy = pltpu.make_async_copy(array.at[part], inputs.at[at, part], semaphores.at[at * CHUNKS + chunk])
-            copy.start()
-            loads[at].append(copy)
-
-    def turn(at):
-        for copy in loads[at]:
-            copy.wait()
-        own0[at] = jnp.swapaxes(inputs[at], 0, 1)
-
-    tops = []
+        own0[at] = jnp.swapaxes(array[...], 0, 1)
     for at in (0, 1):
-        turn(at)
         for row in range(n1):
-            sums[row] = own0[at, 2 * row] + own0[at, 2 * row + 1]
-        narrow(sizes, place, 0, sums, own1.at[at], n1, "own")
-        for row in range(n2):
-            sums[row, :, : sizes.own[1] * LANES] = own1[at, 2 * row] + own1[at, 2 * row + 1]
-        narrow(sizes, place, 1, sums, own2.at[at], n2, "own")
-        tops.append(dot(split(own2[at, 0] + own2[at, 1]), pair_table(LANES, 0, None, 0.25)))
+            sums[at * n1 + row] = own0[at, 2 * row] + own0[at, 2 * row + 1]
+    narrow(sizes, place, 0, sums, own1, 2 * n1, "own")
+    for row in range(2 * n2):
+        sums[row, :, : sizes.own[1] * LANES] = own1[2 * row] + own1[2 * row + 1]
+    narrow(sizes, place, 1, sums, own2, 2 * n2, "own")
+    last = jnp.concatenate([own2[0] + own2[1], own2[n2] + own2[n2 + 1]], axis=0)
+    last = dot(split(last), pair_table(LANES, 0, None, 0.25))
+    top[0] = last[: sizes.depth] + roll(last[sizes.depth :], LANES // 2, 1)
     for message, low, at1, at0 in ((to_next, n1 - 2, n1 - 1, n0 - 1), (to_prev, 0, 0, 0)):
         edge = n2 - 1 if at0 else 0
-        rows = (own0[0, at0], own1[0, low], own1[0, low + 1], own1[1, at1])
-        rows += (own2[0, n2 - 2], own2[0, n2 - 1], own2[1, edge])
+        rows = (own0[0, at0], own1[low], own1[low + 1], own1[n1 + at1])
+        rows += (own2[n2 - 2], own2[n2 - 1], own2[n2 + edge])
         for slot, row in zip(sizes.slots, rows):
             put(message, slot, row)
-    block = tops[0] + roll(tops[1], LANES // 2, 1)
-    for device in range(sizes.span_count):
-        top[device] = block
-    turn(2)
     last = sizes.extent_y - BORDER
     if sizes.sides == 1:
         at = pl.multiple_of(jnp.where(place[1] == 0, last, 0), LANES)
@@ -291,59 +274,86 @@
     return jnp.concatenate(row, axis=1)
 
 
-def pack_edges(sizes, place, rows, target):
-    if sizes.sides != 1:
+def packing(sizes, count):
+    half, reach = LANES // 2, BORDER >> 3
+    pairs = -(-count // 2)
+    if sizes.sides != 1 or count * reach > LANES:
+        return False, count, None, None
+    if count % 2 and count * reach <= half:
+        return True, pairs, pairs - 1, half
+    return True, pairs + 1, pairs, 0
+
+
+def border_turn(place, first, index):
+    reach = BORDER >> 3
+    goal = first + index * reach
+    return jnp.where(place[1] == 0, (goal - LANES // 2) % LANES, (goal + reach) % LANES)
+
+
+def pack_rows(sizes, place, rows, target):
+    packed, tiles, border, first = packing(sizes, len(rows))
+    if not packed:
         for index, row in enumerate(rows):
-            target(index, row)
+            target[index] = row
         return
     half, reach = LANES // 2, BORDER >> 3
     lane = lane_at(rows[0].shape)
-    target(0, jnp.where(lane < half, rows[0], pltpu.roll(rows[1], half, axis=1)))
-    mixed = jnp.where(lane < half, rows[2], 0.0)
+    held = [jnp.zeros(rows[0].shape, f32)] * tiles
     for index, row in enumerate(rows):
-        first = half + index * reach
-        moved = pltpu.roll(row, border_turn(place, index), axis=1)
-        mixed = jnp.where((lane >= first) & (lane < first + reach), moved, mixed)
-    target(1, mixed)
-
-
-def border_turn(place, index):
-    reach = BORDER >> 3
-    return jnp.where(place[1] == 0, index * reach, LANES // 2 + (index + 1) * reach)
-
-
-def unpack_edges(sizes, place, blocks, row, count):
-    total = None
-    if sizes.sides != 1:
-        for index, device in ((2, row - 1), (1, row), (0, row + 1)):
-            if 0 <= device < count:
-                value = blocks[device, index]
-                total = value if total is None else total + value
-        return total
+        if index % 2 == 0:
+            held[index // 2] = jnp.where(lane < half, row, 0.0)
+        else:
+            held[index // 2] = jnp.where(lane < half, held[index // 2], pltpu.roll(row, half, axis=1))
+    for index, row in enumerate(rows):
+        start = first + index * reach
+        moved = pltpu.roll(row, border_turn(place, first, index), axis=1)
+        held[border] = jnp.where((lane >= start) & (lane < start + reach), moved, held[border])
+    for index, tile in enumerate(held):
+        target[index] = tile
+
+
+def unpack_rows(sizes, place, blocks, count):
+    packed, _, border, first = packing(sizes, count)
+    if not packed:
+        return [blocks[index] for index in range(count)]
     half, reach = LANES // 2, BORDER >> 3
-    own = pltpu.roll(blocks[row, 0], half, axis=1)
-    border = turned = None
-    for index, device in ((2, row - 1), (1, row), (0, row + 1)):
-        if 0 <= device < count:
-            if index != 1:
-                own = own + blocks[device, 0 if index == 0 else 1]
-            back = lax.rem(LANES - border_turn(place, index), LANES)
-            value = pltpu.roll(blocks[device, 1], back, axis=1)
-            border = value if border is None else border + value
-    lane = lane_at(own.shape)
-    first = jnp.where(place[1] == 0, half, LANES - reach)
-    return jnp.where(lane < half, own, jnp.where((lane >= first) & (lane < first + reach), border, 0.0))
-
-
-def top_row(sizes, place, top, beside, row):
+    rows = []
+    for index in range(count):
+        own = blocks[index // 2]
+        lane = lane_at(own.shape)
+        if index % 2:
+            own = pltpu.roll(own, half, axis=1)
+        back = lax.rem(LANES - border_turn(place, first, index), LANES)
+        beside = pltpu.roll(blocks[border], back, axis=1)
+        start = jnp.where(place[1] == 0, half, LANES - reach)
+        here = (lane >= start) & (lane < start + reach)
+        rows.append(jnp.where(lane < half, own, jnp.where(here, beside, 0.0)))
+    return rows
+
+
+def merge_into(sizes, place, stride, radix, arrays, target):
+    position = (place[0] // stride) % radix
+    target[...] = jnp.zeros(target.shape, f32)
+    for step, array in enumerate(arrays):
+        at = (position ^ step) * stride
+        for index, row in enumerate(unpack_rows(sizes, place, array, stride + 2)):
+            target[at + index] = target[at + index] + row
+
+
+def merge_kernel(sizes, stride, radix, place, *refs):
+    arrays, out, total = refs[:radix], refs[radix], refs[radix + 1]
+    merge_into(sizes, place, stride, radix, arrays, total)
+    pack_rows(sizes, place, [total[row] for row in range(stride * radix + 2)], out)
+
+
+def top_row(sizes, place, block, beside):
     half, reach = LANES // 2, BORDER >> 3
-    block = top[row]
     lane = lane_at(block.shape)
     values = [jnp.where(lane < half, block, 0.0), jnp.where(lane < half, pltpu.roll(block, half, axis=1), 0.0)]
     right = (lane >= half) & (lane < half + reach)
     left = lane >= LANES - reach
     for side in range(sizes.sides):
-        other = beside[side][row]
+        other = beside[side]
         if sizes.sides == 2:
             here = left if side else right
         else:
@@ -366,19 +376,23 @@
     n0, n1, n2 = sizes.rows[:3]
 
     if s:
-        for at in (0, 1):
-            for row in range(n1):
-                for side in range(s):
-                    columns = slice(side * LANES, (side + 1) * LANES)
-                    sums[row, :, columns] = borders0[side][at, 2 * row] + borders0[side][at, 2 * row + 1]
-            narrow(sizes, place, 0, sums, border1.at[at], n1, "border", sizes.own[0] * LANES)
-            for row in range(n2):
-                sums[row, :, :LANES] = border1[at, 2 * row] + border1[at, 2 * row + 1]
-            narrow(sizes, place, 1, sums, border2.at[at], n2, "border", sizes.own[1] * LANES)
-    borders = [borders0, [border1][:s], [border2][:s]]
+        for row in range(2 * n1):
+            for side in range(s):
+                columns = slice(side * LANES, (side + 1) * LANES)
+                at, low = row // n1, 2 * (row % n1)
+                sums[row, :, columns] = borders0[side][at, low] + borders0[side][at, low + 1]
+        narrow(sizes, place, 0, sums, border1, 2 * n1, "border", sizes.own[0] * LANES)
+        for row in range(2 * n2):
+            sums[row, :, :LANES] = border1[2 * row] + border1[2 * row + 1]
+        narrow(sizes, place, 1, sums, border2, 2 * n2, "border", sizes.own[1] * LANES)
 
     def held_row(level, at, row):
-        return jnp.concatenate([owns[level][at, row], *(array[at, row] for array in borders[level])], axis=1)
+        if level == 0:
+            tiles = [owns[0][at, row], *(array[at, row] for array in borders0)]
+        else:
+            row = at * sizes.rows[level] + row
+            tiles = [owns[level][row], *([(border1, border2)[level - 1][row]] if s else [])]
+        return jnp.concatenate(tiles, axis=1)
 
     def prev_row(level, index):
         return message_row(sizes, place, level, slots[index], from_prev, beside_prev)
@@ -427,11 +441,7 @@
         sources.append(source)
     narrow(sizes, place, 2, sums.at[:, :, : sizes.held[2]], level3, 3)
 
-    def send(index, value):
-        for device in range(sizes.span_count):
-            contribution[device, index] = value
-
-    pack_edges(sizes, place, [level3[row] for row in range(3)], send)
+    pack_rows(sizes, place, [level3[row] for row in range(3)], contribution)
     (s1, s2), (v1, v2) = sources, smooths
     for at, rows in enumerate(
         (
@@ -446,19 +456,30 @@
         put(fars[at], (0, sizes.held[2] // LANES), v2[n2 + 1 if at == 0 else 0])
 
 
-def up_kernel(sizes, place, blocks, top, *refs):
+def relax(count, field, refs_of, source, target):
+    fx, fy, fz, weight, binding = refs_of
+
+    def update(row, value):
+        target(row, field(row) + weight[row - 1] * (source(row) - value))
+
+    sweep(count, field, binding, fx, fy, fz, update)
+
+
+def store(array, first):
+    def put_row(row, value):
+        array[row - first] = value
+
+    return put_row
+
+
+def coarse_kernel(sizes, stride, radix, place, *refs):
     s = sizes.sides
-    tops, refs = refs[:s], refs[s:]
-    (from_prev, from_next), fars, coefs, own0 = refs[:2], refs[2:4], refs[4:7], refs[7]
-    borders0, out, refs = refs[8 : 8 + s], refs[8 + s], refs[9 + s :]
-    total1, total2, sums, result = refs[:4]
-    coarse = [refs[4 + 9 * index : 13 + 9 * index] for index in range(3)]
-    over2, over1, over0, lift2, lift1, lift0, it2, it1, it0, semaphores = refs[31:]
-    slots = sizes.slots
-    n0, n1, n2 = sizes.rows[:3]
+    blocks, tops, refs = refs[:radix], refs[radix : 2 * radix], refs[2 * radix :]
+    beside, refs = [refs[side * radix : (side + 1) * radix] for side in range(s)], refs[s * radix :]
+    out, merged, sums = refs[:3]
+    coarse = [refs[3 + 9 * index : 12 + 9 * index] for index in range(3)]
     total = sizes.span_count
-    width = sizes.own[0] * LANES
-
+    merge_into(sizes, place, stride, radix, blocks, merged)
     zero = jnp.zeros((sizes.depth, LANES), f32)
     for index in range(3):
         level = 3 + index
@@ -468,9 +489,13 @@
             array[0] = zero
             array[count + 1] = zero
         if index == 0:
-            for row in range(count):
-                conduct[row + 1], binding[row] = top_row(sizes, place, top, tops, row)
-                source[row] = unpack_edges(sizes, place, blocks, row, count)
+            source = merged.at[1 : count + 1]
+            base = place[0] // stride % radix
+            for step in range(radix):
+                for low in range(stride):
+                    row = ((base ^ step) * stride) + ((place[0] % stride) ^ low)
+                    others = [arrays[step][low] for arrays in beside]
+                    conduct[row + 1], binding[row] = top_row(sizes, place, tops[step][low], others)
         bound = lambda row, binding=binding: binding[row - 1]
         at_row = lambda row, conduct=conduct: conduct[row]
         coefficients(sizes, place, level, count + 2, at_row, bound, fx, fy, fz, weight)
@@ -497,20 +522,6 @@
             sweep(count + 2, lambda row, smooth=smooth: smooth[row], bound, fx, fy, fz, add)
             narrow(sizes, place, level, sums, source_next, half)
 
-    def relax(count, field, refs_of, source, target):
-        fx, fy, fz, weight, binding = refs_of
-
-        def update(row, value):
-            target(row, field(row) + weight[row - 1] * (source(row) - value))
-
-        sweep(count, field, binding, fx, fy, fz, update)
-
-    def store(array, first):
-        def put_row(row, value):
-            array[row - first] = value
-
-        return put_row
-
     fx, fy, fz, weight, conduct, binding, source, smooth, iterate = coarse[2]
     held, other = smooth, iterate
     for _ in range(COARSE_SWEEPS - 1):
@@ -521,6 +532,8 @@
         held, other = other, held
     for index in (1, 0):
         fx, fy, fz, weight, conduct, binding, source, smooth, iterate = coarse[index]
+        if index == 0:
+            source = merged.at[1 : total + 1]
         count = total >> index
         widen(sizes, place, 3 + index, held.at[1 : count // 2 + 1], sums, count // 2)
         for row in range(count):
@@ -531,7 +544,20 @@
         relax(count + 2, field, (fx, fy, fz, weight, bound), mine, store(iterate, 0))
         held = iterate
 
-    widen(sizes, place, 2, held.at[pl.ds(place[0], 3)], over2, 3)
+    out[...] = held[pl.ds(place[0], 3)]
+
+
+def up_kernel(sizes, place, coarse, *refs):
+    s = sizes.sides
+    (from_prev, from_next), fars, coefs, own0 = refs[:2], refs[2:4], refs[4:7], refs[7]
+    borders0, out, refs = refs[8 : 8 + s], refs[8 + s], refs[9 + s :]
+    total1, total2, result = refs[:3]
+    over2, over1, over0, lift2, lift1, lift0, it2, it1, it0, semaphores = refs[3:]
+    slots = sizes.slots
+    n0, n1, n2 = sizes.rows[:3]
+    width = sizes.own[0] * LANES
+
+    widen(sizes, place, 2, coarse, over2, 3)
     for level, array, first, totals, over, lift, target, upper in (
         (2, coefs[2], 4, total2, over2, lift2, it2, over1),
         (1, coefs[1], 1, total1, over1, lift1, it1, over0),
@@ -588,7 +614,7 @@
         copy.wait()
 
 
-def call(body, name, outputs, scratch, place, inputs, limit=VMEM_LIMIT, copies=0, far_in=False, far_out=False):
+def call(body, name, outputs, scratch, place, inputs, copies=0, far_out=False):
     near, far = pl.BlockSpec(memory_space=pltpu.VMEM), pl.BlockSpec(memory_space=pl.ANY)
     scratch = [pltpu.VMEM(shape, f32) for shape in scratch]
     if copies:
@@ -597,10 +623,10 @@
         body,
         name=name,
         out_shape=[jax.ShapeDtypeStruct(shape, f32) for shape in outputs],
-        in_specs=[pl.BlockSpec(memory_space=pltpu.SMEM)] + [far if far_in else near] * len(inputs),
+        in_specs=[pl.BlockSpec(memory_space=pltpu.SMEM)] + [near] * len(inputs),
         out_specs=[far if far_out else near] * len(outputs),
         scratch_shapes=scratch,
-        compiler_params=pltpu.CompilerParams(vmem_limit_bytes=limit),
+        compiler_params=pltpu.CompilerParams(vmem_limit_bytes=VMEM_LIMIT),
     )(place, *inputs)
 
 
@@ -618,8 +644,20 @@
     return []
 
 
-def to_all(value):
-    return lax.all_to_all(value, "span", split_axis=0, concat_axis=0, tiled=True)
+def stages(count):
+    stride = 1
+    while stride < count:
+        radix = 4 if count // stride % 4 == 0 else 2
+        yield stride, radix
+        stride *= radix
+
+
+def swap(value, stride, radix):
+    count = lax.axis_size("span")
+    return [value] + [
+        lax.ppermute(value, "span", [(device, device ^ step * stride) for device in range(count)])
+        for step in range(1, radix)
+    ]
 
 
 def on_device(right_side, diffusivity, reaction):
@@ -636,15 +674,12 @@
     own0, own1, own2, to_next, to_prev, top, *edges = call(
         functools.partial(start_kernel, sizes),
         "start",
-        [(3, n0, *own[0]), (2, n1, *own[1]), (2, n2, *own[2]), down_message, down_message]
-        + [(sizes.span_count, *tile)]
+        [(3, n0, *own[0]), (2 * n1, *own[1]), (2 * n2, *own[2]), down_message, down_message]
+        + [(1, *tile)]
         + [(3, n0, depth, BORDER)] * s,
-        [(3, *diffusivity.shape), (n1, *own[0])],
+        [(2 * n1, *own[0])],
         place,
         [right_side, diffusivity, reaction],
-        limit=START_LIMIT,
-        copies=3 * CHUNKS,
-        far_in=True,
     )
     halos = [along(to_next, "span", 1), along(to_prev, "span", -1)]
     if s == 1:
@@ -653,9 +688,13 @@
         borders = [along(edges[1], "width", -1), along(edges[0], "width", 1)]
     else:
         borders = []
-    top, *halos = lax.optimization_barrier((top, *halos))
+    plan = list(stages(sizes.span_count))
+    for stride, radix in plan[:-1]:
+        top = jnp.concatenate(swap(top, stride, radix))
     sides = beside(halos, sizes)
-    top = to_all(top)
+    tops = swap(top, *plan[-1])
+    beside_tops = beside(tops, sizes)
+    halos, sides, tops, beside_tops = lax.optimization_barrier((halos, sides, tops, beside_tops))
 
     lengths = [sum(coefficient_rows(sizes, level)) for level in range(3)]
     far = (sizes.held[2] // LANES, *tile)
@@ -663,21 +702,41 @@
     downs = call(
         functools.partial(down_kernel, sizes),
         "down",
-        [*coefs, (sizes.span_count, 2 if s == 1 else 3, *tile), up_message, up_message, far, far],
-        [(2, n1, *tile), (2, n2, *tile), (3, *tile), (n1 + 2, *held[0])],
+        [*coefs, (packing(sizes, 3)[1], *tile), up_message, up_message, far, far],
+        [(2 * n1, *tile), (2 * n2, *tile), (3, *tile), (max(2 * n1, n1 + 2), *held[0])],
         place,
         [own0, own1, own2, *borders, *halos, *sum(sides, [])],
     )
     coefs_out, blocks, ups, fars = downs[:3], downs[3], downs[4:6], downs[6:8]
-    blocks = to_all(blocks)
-    tops = [side[0] for side in beside([top], sizes)]
-    received = [along(ups[0], "span", 1), along(ups[1], "span", -1)]
-    received += [along(fars[0], "span", 2), along(fars[1], "span", -2)]
-    scratch = [(n1 + 2, *held[1]), (n2 + 2, *held[2]), (max(sizes.span_count // 2, 2), *tile), diffusivity.shape]
+    for stride, radix in plan[:-1]:
+        rows = stride * radix + 2
+        (blocks,) = call(
+            functools.partial(merge_kernel, sizes, stride, radix),
+            "merge",
+            [(packing(sizes, rows)[1], *tile)],
+            [(rows, *tile)],
+            place,
+            swap(blocks, stride, radix),
+        )
+    blocks, *sent = lax.optimization_barrier((blocks, *ups, *fars))
+    stride, radix = plan[-1]
+    blocks = swap(blocks, stride, radix)
+    received = [along(sent[0], "span", 1), along(sent[1], "span", -1)]
+    received += [along(sent[2], "span", 2), along(sent[3], "span", -2)]
+    scratch = [(sizes.span_count + 2, *tile), (max(sizes.span_count // 2, 2), *tile)]
     for index in range(3):
         count = sizes.span_count >> index
         scratch += [(count + 1, *tile)] + [(count, *tile)] * 3 + [(count + 2, *tile)] + [(count, *tile)] * 2
         scratch += [(count + 2, *tile)] * 2
+    (coarse,) = call(
+        functools.partial(coarse_kernel, sizes, stride, radix),
+        "coarse",
+        [(n3 + 2, *tile)],
+        scratch,
+        place,
+        [*blocks, *tops, *sum(beside_tops, [])],
+    )
+    scratch = [(n1 + 2, *held[1]), (n2 + 2, *held[2]), diffusivity.shape]
     scratch += [(n3 + 2, *held[2]), (n2 + 2, *held[1]), (n1 + 2, *held[0])]
     scratch += [(n2 + 4, *held[2]), (n1 + 4, *held[1]), (n0 + 2, *held[0])]
     scratch += [(n2 + 2, *held[2]), (n1 + 2, *held[1]), (n0, *held[0])]
@@ -687,7 +746,7 @@
         [diffusivity.shape],
         scratch,
         place,
-        [blocks, top, *tops, *received, *coefs_out, own0, *borders],
+        [coarse, *received, *coefs_out, own0, *borders],
         copies=CHUNKS,
         far_out=True,
     )

time: 81.5 us -> 77.3 us (0.948)
  local copies, waits for them, and re-layouts: 13.9 us -> 3.14 us
  waiting for transfers between devices: 19.9 us -> 27.1 us
  starting transfers between devices: 31.5 us -> 34.7 us
  Pallas kernels: 14.6 us -> 11.8 us
    ppermute x0 -> x12, starting transfers between devices: none -> 22.2 us  [swap(): lax.ppermute(value, 'span', [(device, device ^ step * stride) for device...]
    ppermute x0 -> x12, waiting for transfers between devices: none -> 15.1 us  [swap(): lax.ppermute(value, 'span', [(device, device ^ step * stride) for device...]
    all_to_all x2 -> x0, starting transfers between devices: 12.8 us -> none  [to_all(): lax.all_to_all(value, 'span', split_axis=0, concat_axis=0, tiled=True)]
    unnamed x28 -> x9, local copies, waits for them, and re-layouts: 13.9 us -> 3.13 us
    ppermute x6, waiting for transfers between devices: 18.2 us -> 11 us  [along(): lax.ppermute(value, axis, [(source, source + steps) for source in range(i...]
    ppermute x6, starting transfers between devices: 17.9 us -> 11.4 us  [along(): lax.ppermute(value, axis, [(source, source + steps) for source in range(i...]
    pallas_call x3 -> x5, Pallas kernels: 14.6 us -> 11.8 us  [call(): pl.pallas_call(body, name=name, out_shape=[jax.ShapeDtypeStruct(shape, f3...]
    ppermute x1, waiting for transfers between devices: 1.34 us -> 0.01 us  [on_device(): borders = [lax.ppermute(edges[0], 'width', [(0, 1), (1, 0)])]]
  transfers between devices with their start and end apart: 12 -> 25, of which waited for: 9 -> 13; matrix products, arithmetic and copies ran while one was open for 0% -> 0% of each run, Pallas kernels for 6% -> 4%
where the time goes in v4:
time: 77.3 us; the launch traced here: 77 us
  starting transfers between devices  34.7 us (45%)
  waiting for transfers between devices  27.1 us (35%)
  Pallas kernels  11.8 us (15%)
  local copies, waits for them, and re-layouts  3.14 us (4%)
    ppermute x12, starting transfers between devices, swap(): lax.ppermute(value, 'span', [(device, device ^ step * stride) for device...  22.2 us
    ppermute x12, waiting for transfers between devices, swap(): lax.ppermute(value, 'span', [(device, device ^ step * stride) for device...  15.1 us
    pallas_call x5, Pallas kernels, call(): pl.pallas_call(body, name=name, out_shape=[jax.ShapeDtypeStruct(shape, f3...  11.8 us
    ppermute x6, starting transfers between devices, along(): lax.ppermute(value, axis, [(source, source + steps) for source in range(i...  11.4 us
    ppermute x6, waiting for transfers between devices, along(): lax.ppermute(value, axis, [(source, source + steps) for source in range(i...  11 us
    unnamed x9, local copies, waits for them, and re-layouts  3.13 us
  transfers between devices with their start and end apart: 25, of which 13 were waited for; matrix products, arithmetic and copies ran while one was open for 0% of the time, Pallas kernels for 4%

profile of v4, /device:TPU:0, one launch (start us, length us, event | category | flops | bytes accessed | tf_op | source)
XLA Modules:
  0.0 77.0 jit_solution(2801684448925160329)
XLA Ops:
  3.2 1.4 %start.1 = (f32[3,8,32,512]{3,2,1,0:T(8,128)S(1)}, f32[8,32,256]{2,1,0:T(8,128)S(1)}, f32[4,32,128]{2,1,0:T(8,128)S(1)}, f32[13,32,128]{2,1,0:T(8,128)S(1)}, f32...) custom-call(s32[2]{0:T(128)S(1)} %pad_add_fusion.place, ...), custom_call_target="tpu_custom_call" | custom-call | tf_op jit(solution)/shard_map/start/pallas_call | solution.py:622
  4.6 3.9 %collective-permute-start.7 = (f32[1,32,128]{2,1,0:T(8,128)S(1)}, f32[1,32,128]{2,1,0:T(8,128)S(1)}, u32[]{:S(2)}, u32[]{:S(2)}) collective-permute-start(f32[1,32,128]{2,1,0:T(8,128)S(1)} %get-tuple-element.43), channel_id=1, source_target_pairs={{0,6},{2,4},{4,2},{6,0},{8,14},{10,12},{12,10},{14,8},{16,22},{18,... | collective-permute-start | bytes 49160 | tf_op jit(solution)/shard_map/ppermute | solution.py:658
  9.2 3.8 %collective-permute-start.1 = (f32[13,32,128]{2,1,0:T(8,128)S(1)}, f32[13,32,128]{2,1,0:T(8,128)S(1)}, u32[]{:S(2)}, u32[]{:S(2)}) collective-permute-start(f32[13,32,128]{2,1,0:T(8,128)S(1)} %get-tuple-element.41), channel_id=1, source_target_pairs={{0,2},{2,4},{4,6},{6,8},{8,10},{10,12},{12,14},{14,16},{16,18},{18... | collective-permute-start | bytes 638984 | tf_op jit(solution)/shard_map/ppermute | solution.py:636
  13.0 1.3 %collective-permute-start.2 = (f32[13,32,128]{2,1,0:T(8,128)S(1)}, f32[13,32,128]{2,1,0:T(8,128)S(1)}, u32[]{:S(2)}, u32[]{:S(2)}) collective-permute-start(f32[13,32,128]{2,1,0:T(8,128)S(1)} %get-tuple-element.42), channel_id=1, source_target_pairs={{2,0},{4,2},{6,4},{8,6},{10,8},{12,10},{14,12},{16,14},{18,16},{20... | collective-permute-start | bytes 638984 | tf_op jit(solution)/shard_map/ppermute | solution.py:636
  15.0 1.6 %collective-permute-done.1.refs_4_ = f32[13,32,128]{2,1,0:T(8,128)S(1)} collective-permute-done((f32[13,32,128]{2,1,0:T(8,128)S(1)}, f32[13,32,128]{2,1,0:T(8,128)S(1)}, u32[]{:S(2)}, u32[]{:S(2)}) %collective-permute-start.1) | collective-permute-done | bytes 213024 | tf_op jit(solution)/shard_map/ppermute | solution.py:636
  16.6 6.5 %collective-permute-done.2.refs_5_ = f32[13,32,128]{2,1,0:T(8,128)S(1)} collective-permute-done((f32[13,32,128]{2,1,0:T(8,128)S(1)}, f32[13,32,128]{2,1,0:T(8,128)S(1)}, u32[]{:S(2)}, u32[]{:S(2)}) %collective-permute-start.2) | collective-permute-done | bytes 213024 | tf_op jit(solution)/shard_map/ppermute | solution.py:636
  23.2 3.6 %collective-permute-start.10 = (f32[4,32,128]{2,1,0:T(8,128)S(1)}, f32[4,32,128]{2,1,0:T(8,128)S(1)}, u32[]{:S(2)}, u32[]{:S(2)}) collective-permute-start(f32[4,32,128]{2,1,0:T(8,128)S(1)} %constant_dynamic-update-slice_fusion.refs_4_), channel_id=1, source_target_pairs={{0,24},{2,26},{4,28},{6,30},{8,16},{10,18},{12,20},{14,22},{16,8},... | collective-permute-start | bytes 196616 | tf_op jit(solution)/shard_map/ppermute | solution.py:658
  26.8 3.0 %collective-permute-done.10.refs_7_ = f32[4,32,128]{2,1,0:T(8,128)S(1)} collective-permute-done((f32[4,32,128]{2,1,0:T(8,128)S(1)}, f32[4,32,128]{2,1,0:T(8,128)S(1)}, u32[]{:S(2)}, u32[]{:S(2)}) %collective-permute-start.10) | collective-permute-done | bytes 65568 | tf_op jit(solution)/shard_map/ppermute | solution.py:658
  29.7 2.7 %collective-permute-start.8 = (f32[4,32,128]{2,1,0:T(8,128)S(1)}, f32[4,32,128]{2,1,0:T(8,128)S(1)}, u32[]{:S(2)}, u32[]{:S(2)}) collective-permute-start(f32[4,32,128]{2,1,0:T(8,128)S(1)} %constant_dynamic-update-slice_fusion.refs_4_), channel_id=1, source_target_pairs={{0,8},{2,10},{4,12},{6,14},{8,0},{10,2},{12,4},{14,6},{16,24},{18,... | collective-permute-start | bytes 196616 | tf_op jit(solution)/shard_map/ppermute | solution.py:658
  32.9 1.8 %collective-permute-done.8.refs_5_ = f32[4,32,128]{2,1,0:T(8,128)S(1)} collective-permute-done((f32[4,32,128]{2,1,0:T(8,128)S(1)}, f32[4,32,128]{2,1,0:T(8,128)S(1)}, u32[]{:S(2)}, u32[]{:S(2)}) %collective-permute-start.8) | collective-permute-done | bytes 65568 | tf_op jit(solution)/shard_map/ppermute | solution.py:658
  36.1 3.7 %down.1 = (f32[41,32,640]{2,1,0:T(8,128)S(1)}, f32[43,32,384]{2,1,0:T(8,128)S(1)}, f32[29,32,256]{2,1,0:T(8,128)S(1)}, f32[2,32,128]{2,1,0:T(8,128)S(1)}, f32[14...) custom-call(s32[2]{0:T(128)S(1)} %pad_add_fusion.place, ...), custom_call_target="tpu_custom_call" | custom-call | tf_op jit(solution)/shard_map/down/pallas_call | solution.py:622
  39.8 1.9 %collective-permute-start.17 = (f32[2,32,128]{2,1,0:T(8,128)S(1)}, f32[2,32,128]{2,1,0:T(8,128)S(1)}, u32[]{:S(2)}, u32[]{:S(2)}) collective-permute-start(f32[2,32,128]{2,1,0:T(8,128)S(1)} %get-tuple-element.48.refs_0_), channel_id=1, source_target_pairs={{0,6},{2,4},{4,2},{6,0},{8,14},{10,12},{12,10},{14,8},{16,22},{18,... | collective-permute-start | bytes 98312 | tf_op jit(solution)/shard_map/ppermute | solution.py:658
  41.7 1.1 %collective-permute-start.16 = (f32[2,32,128]{2,1,0:T(8,128)S(1)}, f32[2,32,128]{2,1,0:T(8,128)S(1)}, u32[]{:S(2)}, u32[]{:S(2)}) collective-permute-start(f32[2,32,128]{2,1,0:T(8,128)S(1)} %get-tuple-element.48.refs_0_), channel_id=1, source_target_pairs={{0,4},{2,6},{4,0},{6,2},{8,12},{10,14},{12,8},{14,10},{16,20},{18,... | collective-permute-start | bytes 98312 | tf_op jit(solution)/shard_map/ppermute | solution.py:658
  43.3 1.4 %collective-permute-done.17.refs_3_ = f32[2,32,128]{2,1,0:T(8,128)S(1)} collective-permute-done((f32[2,32,128]{2,1,0:T(8,128)S(1)}, f32[2,32,128]{2,1,0:T(8,128)S(1)}, u32[]{:S(2)}, u32[]{:S(2)}) %collective-permute-start.17) | collective-permute-done | bytes 32800 | tf_op jit(solution)/shard_map/ppermute | solution.py:658
  45.6 1.1 %collective-permute-done.15.refs_1_ = f32[2,32,128]{2,1,0:T(8,128)S(1)} collective-permute-done((f32[2,32,128]{2,1,0:T(8,128)S(1)}, f32[2,32,128]{2,1,0:T(8,128)S(1)}, u32[]{:S(2)}, u32[]{:S(2)}) %collective-permute-start.15) | collective-permute-done | bytes 32800 | tf_op jit(solution)/shard_map/ppermute | solution.py:658
  47.5 2.5 %collective-permute-start.21 = (f32[14,32,128]{2,1,0:T(8,128)S(1)}, f32[14,32,128]{2,1,0:T(8,128)S(1)}, u32[]{:S(2)}, u32[]{:S(2)}) collective-permute-start(f32[14,32,128]{2,1,0:T(8,128)S(1)} %get-tuple-element.62), channel_id=1, source_target_pairs={{0,2},{2,4},{4,6},{6,8},{8,10},{10,12},{12,14},{14,16},{16,18},{18... | collective-permute-start | bytes 688136 | tf_op jit(solution)/shard_map/ppermute | solution.py:636
  49.9 1.3 %collective-permute-start.22 = (f32[14,32,128]{2,1,0:T(8,128)S(1)}, f32[14,32,128]{2,1,0:T(8,128)S(1)}, u32[]{:S(2)}, u32[]{:S(2)}) collective-permute-start(f32[14,32,128]{2,1,0:T(8,128)S(1)} %get-tuple-element.63), channel_id=1, source_target_pairs={{2,0},{4,2},{6,4},{8,6},{10,8},{12,10},{14,12},{16,14},{18,16},{20... | collective-permute-start | bytes 688136 | tf_op jit(solution)/shard_map/ppermute | solution.py:636
  51.2 7.1 %collective-permute-start.20 = (f32[4,32,128]{2,1,0:T(8,128)S(1)}, f32[4,32,128]{2,1,0:T(8,128)S(1)}, u32[]{:S(2)}, u32[]{:S(2)}) collective-permute-start(f32[4,32,128]{2,1,0:T(8,128)S(1)} %merge.1.refs_0_), channel_id=1, source_target_pairs={{0,24},{2,26},{4,28},{6,30},{8,16},{10,18},{12,20},{14,22},{16,8},... | collective-permute-start | bytes 196616 | tf_op jit(solution)/shard_map/ppermute | solution.py:658
  59.0 6.0 %collective-permute-done.20.refs_3_ = f32[4,32,128]{2,1,0:T(8,128)S(1)} collective-permute-done((f32[4,32,128]{2,1,0:T(8,128)S(1)}, f32[4,32,128]{2,1,0:T(8,128)S(1)}, u32[]{:S(2)}, u32[]{:S(2)}) %collective-permute-start.20) | collective-permute-done | bytes 65568 | tf_op jit(solution)/shard_map/ppermute | solution.py:658
  65.0 1.3 %collective-permute-start.23 = (f32[2,32,128]{2,1,0:T(8,128)S(1)}, f32[2,32,128]{2,1,0:T(8,128)S(1)}, u32[]{:S(2)}, u32[]{:S(2)}) collective-permute-start(f32[2,32,128]{2,1,0:T(8,128)S(1)} %get-tuple-element.64), channel_id=1, source_target_pairs={{0,4},{2,6},{4,8},{6,10},{8,12},{10,14},{12,16},{14,18},{16,20},{1... | collective-permute-start | bytes 98312 | tf_op jit(solution)/shard_map/ppermute | solution.py:636
  66.8 1.3 %collective-permute-start.24 = (f32[2,32,128]{2,1,0:T(8,128)S(1)}, f32[2,32,128]{2,1,0:T(8,128)S(1)}, u32[]{:S(2)}, u32[]{:S(2)}) collective-permute-start(f32[2,32,128]{2,1,0:T(8,128)S(1)} %get-tuple-element.65), channel_id=1, source_target_pairs={{4,0},{6,2},{8,4},{10,6},{12,8},{14,10},{16,12},{18,14},{20,16},{2... | collective-permute-start | bytes 98312 | tf_op jit(solution)/shard_map/ppermute | solution.py:636
  68.1 2.8 %coarse.1 = f32[3,32,128]{2,1,0:T(8,128)S(1)} custom-call(s32[2]{0:T(128)S(1)} %pad_add_fusion.place, f32[4,32,128]{2,1,0:T(8,128)S(1)} %merge.1.refs_0_, f32[4,32,128]{2,1,0:T(8,128)S(1)} %collective-permute-done.18.refs_1_, f32[4,32,128]{2,1,0:T(8,128)S(1)} %collective-permute-done.19.refs_2_, f32[4,32,128]{2,1,0:T(8,128)S(1)} %collective-permute-done.20.refs_3_, ...), custom_call_target="tpu_custom_call" | custom-call | tf_op jit(solution)/shard_map/coarse/pallas_call | solution.py:622
  71.0 2.9 %collective-permute-done.24.refs_3_ = f32[2,32,128]{2,1,0:T(8,128)S(1)} collective-permute-done((f32[2,32,128]{2,1,0:T(8,128)S(1)}, f32[2,32,128]{2,1,0:T(8,128)S(1)}, u32[]{:S(2)}, u32[]{:S(2)}) %collective-permute-start.24) | collective-permute-done | bytes 32800 | tf_op jit(solution)/shard_map/ppermute | solution.py:636
  73.9 3.1 %up.1 = f32[32,8,512]{2,1,0:T(8,128)} custom-call(s32[2]{0:T(128)S(1)} %pad_add_fusion.place, f32[3,32,128]{2,1,0:T(8,128)S(1)} %coarse.1, f32[14,32,128]{2,1,0:T(8,128)S(1)} %collective-permute-done.21.refs_0_, f32[14,32,128]{2,1,0:T(8,128)S(1)} %collective-permute-done.22.refs_1_, f32[2,32,128]{2,1,0:T(8,128)S(1)} %collective-permute-done.23.refs_2_, ...), custom_call_target="tpu_custom_call" | custom-call | tf_op jit(solution)/shard_map/up/pallas_call | solution.py:622
  (42 shorter events, 9.8 us)
Async XLA Ops:
  4.6 9.8 %collective-permute-start.7 = (f32[1,32,128]{2,1,0:T(8,128)S(1)}, f32[1,32,128]{2,1,0:T(8,128)S(1)}, u32[]{:S(2)}, u32[]{:S(2)}) collective-permute-start(f32[1,32,128]{2,1,0:T(8,128)S(1)} %get-tuple-element.43), channel_id=1, source_target_pairs={{0,6},{2,4},{4,2},{6,0},{8,14},{10,12},{12,10},{14,8},{16,22},{18,... | collective-permute-start | bytes 49160 | tf_op jit(solution)/shard_map/ppermute | solution.py:658
  8.6 5.9 %collective-permute-start.6 = (f32[1,32,128]{2,1,0:T(8,128)S(1)}, f32[1,32,128]{2,1,0:T(8,128)S(1)}, u32[]{:S(2)}, u32[]{:S(2)}) collective-permute-start(f32[1,32,128]{2,1,0:T(8,128)S(1)} %get-tuple-element.43), channel_id=1, source_target_pairs={{0,4},{2,6},{4,0},{6,2},{8,12},{10,14},{12,8},{14,10},{16,20},{18,... | collective-permute-start | bytes 49160 | tf_op jit(solution)/shard_map/ppermute | solution.py:658
  9.1 5.3 %collective-permute-start.5 = (f32[1,32,128]{2,1,0:T(8,128)S(1)}, f32[1,32,128]{2,1,0:T(8,128)S(1)}, u32[]{:S(2)}, u32[]{:S(2)}) collective-permute-start(f32[1,32,128]{2,1,0:T(8,128)S(1)} %get-tuple-element.43), channel_id=1, source_target_pairs={{0,2},{2,0},{4,6},{6,4},{8,10},{10,8},{12,14},{14,12},{16,18},{18,... | collective-permute-start | bytes 49160 | tf_op jit(solution)/shard_map/ppermute | solution.py:658
  9.2 7.4 %collective-permute-start.1 = (f32[13,32,128]{2,1,0:T(8,128)S(1)}, f32[13,32,128]{2,1,0:T(8,128)S(1)}, u32[]{:S(2)}, u32[]{:S(2)}) collective-permute-start(f32[13,32,128]{2,1,0:T(8,128)S(1)} %get-tuple-element.41), channel_id=1, source_target_pairs={{0,2},{2,4},{4,6},{6,8},{8,10},{10,12},{12,14},{14,16},{16,18},{18... | collective-permute-start | bytes 638984 | tf_op jit(solution)/shard_map/ppermute | solution.py:636
  13.0 10.2 %collective-permute-start.2 = (f32[13,32,128]{2,1,0:T(8,128)S(1)}, f32[13,32,128]{2,1,0:T(8,128)S(1)}, u32[]{:S(2)}, u32[]{:S(2)}) collective-permute-start(f32[13,32,128]{2,1,0:T(8,128)S(1)} %get-tuple-element.42), channel_id=1, source_target_pairs={{2,0},{4,2},{6,4},{8,6},{10,8},{12,10},{14,12},{16,14},{18,16},{20... | collective-permute-start | bytes 638984 | tf_op jit(solution)/shard_map/ppermute | solution.py:636
  14.3 21.8 %collective-permute-start = (f32[3,8,32,128]{3,2,1,0:T(8,128)S(1)}, f32[3,8,32,128]{3,2,1,0:T(8,128)S(1)}, u32[]{:S(2)}, u32[]{:S(2)}) collective-permute-start(f32[3,8,32,128]{3,2,1,0:T(8,128)S(1)} %get-tuple-element.40), channel_id=1, source_target_pairs={{0,1},{1,0},{2,3},{3,2},{4,5},{5,4},{6,7},{7,6},{8,9},{9,8},{10,11... | collective-permute-start | bytes 1179656 | tf_op jit(solution)/shard_map/ppermute | solution.py:686
  14.5 12.3 %collective-permute-start.11 = (f32[4,32,128]{2,1,0:T(8,128)S(1)}, f32[4,32,128]{2,1,0:T(8,128)S(1)}, u32[]{:S(2)}, u32[]{:S(2)}) collective-permute-start(f32[4,32,128]{2,1,0:T(8,128)S(1)} %constant_dynamic-update-slice_fusion.refs_4_), channel_id=1, source_target_pairs={{0,1},{1,0},{2,3},{3,2},{4,5},{5,4},{6,7},{7,6},{8,9},{9,8},{10,11... | collective-permute-start | bytes 196616 | tf_op jit(solution)/shard_map/ppermute | solution.py:641
  16.6 19.5 %collective-permute-start.3 = (f32[13,32,128]{2,1,0:T(8,128)S(1)}, f32[13,32,128]{2,1,0:T(8,128)S(1)}, u32[]{:S(2)}, u32[]{:S(2)}) collective-permute-start(f32[13,32,128]{2,1,0:T(8,128)S(1)} %collective-permute-done.1.refs_4_), channel_id=1, source_target_pairs={{0,1},{1,0},{2,3},{3,2},{4,5},{5,4},{6,7},{7,6},{8,9},{9,8},{10,11... | collective-permute-start | bytes 638984 | tf_op jit(solution)/shard_map/ppermute | solution.py:641
  23.2 12.9 %collective-permute-start.4 = (f32[13,32,128]{2,1,0:T(8,128)S(1)}, f32[13,32,128]{2,1,0:T(8,128)S(1)}, u32[]{:S(2)}, u32[]{:S(2)}) collective-permute-start(f32[13,32,128]{2,1,0:T(8,128)S(1)} %collective-permute-done.2.refs_5_), channel_id=1, source_target_pairs={{0,1},{1,0},{2,3},{3,2},{4,5},{5,4},{6,7},{7,6},{8,9},{9,8},{10,11... | collective-permute-start | bytes 638984 | tf_op jit(solution)/shard_map/ppermute | solution.py:641
  23.2 6.6 %collective-permute-start.10 = (f32[4,32,128]{2,1,0:T(8,128)S(1)}, f32[4,32,128]{2,1,0:T(8,128)S(1)}, u32[]{:S(2)}, u32[]{:S(2)}) collective-permute-start(f32[4,32,128]{2,1,0:T(8,128)S(1)} %constant_dynamic-update-slice_fusion.refs_4_), channel_id=1, source_target_pairs={{0,24},{2,26},{4,28},{6,30},{8,16},{10,18},{12,20},{14,22},{16,8},... | collective-permute-start | bytes 196616 | tf_op jit(solution)/shard_map/ppermute | solution.py:658
  26.8 6.2 %collective-permute-start.9 = (f32[4,32,128]{2,1,0:T(8,128)S(1)}, f32[4,32,128]{2,1,0:T(8,128)S(1)}, u32[]{:S(2)}, u32[]{:S(2)}) collective-permute-start(f32[4,32,128]{2,1,0:T(8,128)S(1)} %constant_dynamic-update-slice_fusion.refs_4_), channel_id=1, source_target_pairs={{0,16},{2,18},{4,20},{6,22},{8,24},{10,26},{12,28},{14,30},{16,0},... | collective-permute-start | bytes 196616 | tf_op jit(solution)/shard_map/ppermute | solution.py:658
  29.7 4.9 %collective-permute-start.8 = (f32[4,32,128]{2,1,0:T(8,128)S(1)}, f32[4,32,128]{2,1,0:T(8,128)S(1)}, u32[]{:S(2)}, u32[]{:S(2)}) collective-permute-start(f32[4,32,128]{2,1,0:T(8,128)S(1)} %constant_dynamic-update-slice_fusion.refs_4_), channel_id=1, source_target_pairs={{0,8},{2,10},{4,12},{6,14},{8,0},{10,2},{12,4},{14,6},{16,24},{18,... | collective-permute-start | bytes 196616 | tf_op jit(solution)/shard_map/ppermute | solution.py:658
  32.9 1.8 %collective-permute-start.14 = (f32[4,32,128]{2,1,0:T(8,128)S(1)}, f32[4,32,128]{2,1,0:T(8,128)S(1)}, u32[]{:S(2)}, u32[]{:S(2)}) collective-permute-start(f32[4,32,128]{2,1,0:T(8,128)S(1)} %collective-permute-done.10.refs_7_), channel_id=1, source_target_pairs={{0,1},{1,0},{2,3},{3,2},{4,5},{5,4},{6,7},{7,6},{8,9},{9,8},{10,11... | collective-permute-start | bytes 196616 | tf_op jit(solution)/shard_map/ppermute | solution.py:641
  34.7 1.4 %collective-permute-start.12 = (f32[4,32,128]{2,1,0:T(8,128)S(1)}, f32[4,32,128]{2,1,0:T(8,128)S(1)}, u32[]{:S(2)}, u32[]{:S(2)}) collective-permute-start(f32[4,32,128]{2,1,0:T(8,128)S(1)} %collective-permute-done.8.refs_5_), channel_id=1, source_target_pairs={{0,1},{1,0},{2,3},{3,2},{4,5},{5,4},{6,7},{7,6},{8,9},{9,8},{10,11... | collective-permute-start | bytes 196616 | tf_op jit(solution)/shard_map/ppermute | solution.py:641
  39.8 4.9 %collective-permute-start.17 = (f32[2,32,128]{2,1,0:T(8,128)S(1)}, f32[2,32,128]{2,1,0:T(8,128)S(1)}, u32[]{:S(2)}, u32[]{:S(2)}) collective-permute-start(f32[2,32,128]{2,1,0:T(8,128)S(1)} %get-tuple-element.48.refs_0_), channel_id=1, source_target_pairs={{0,6},{2,4},{4,2},{6,0},{8,14},{10,12},{12,10},{14,8},{16,22},{18,... | collective-permute-start | bytes 98312 | tf_op jit(solution)/shard_map/ppermute | solution.py:658
  41.7 3.9 %collective-permute-start.16 = (f32[2,32,128]{2,1,0:T(8,128)S(1)}, f32[2,32,128]{2,1,0:T(8,128)S(1)}, u32[]{:S(2)}, u32[]{:S(2)}) collective-permute-start(f32[2,32,128]{2,1,0:T(8,128)S(1)} %get-tuple-element.48.refs_0_), channel_id=1, source_target_pairs={{0,4},{2,6},{4,0},{6,2},{8,12},{10,14},{12,8},{14,10},{16,20},{18,... | collective-permute-start | bytes 98312 | tf_op jit(solution)/shard_map/ppermute | solution.py:658
  42.8 3.9 %collective-permute-start.15 = (f32[2,32,128]{2,1,0:T(8,128)S(1)}, f32[2,32,128]{2,1,0:T(8,128)S(1)}, u32[]{:S(2)}, u32[]{:S(2)}) collective-permute-start(f32[2,32,128]{2,1,0:T(8,128)S(1)} %get-tuple-element.48.refs_0_), channel_id=1, source_target_pairs={{0,2},{2,0},{4,6},{6,4},{8,10},{10,8},{12,14},{14,12},{16,18},{18,... | collective-permute-start | bytes 98312 | tf_op jit(solution)/shard_map/ppermute | solution.py:658
  47.5 26.4 %collective-permute-start.21 = (f32[14,32,128]{2,1,0:T(8,128)S(1)}, f32[14,32,128]{2,1,0:T(8,128)S(1)}, u32[]{:S(2)}, u32[]{:S(2)}) collective-permute-start(f32[14,32,128]{2,1,0:T(8,128)S(1)} %get-tuple-element.62), channel_id=1, source_target_pairs={{0,2},{2,4},{4,6},{6,8},{8,10},{10,12},{12,14},{14,16},{16,18},{18... | collective-permute-start | bytes 688136 | tf_op jit(solution)/shard_map/ppermute | solution.py:636
  49.9 23.9 %collective-permute-start.22 = (f32[14,32,128]{2,1,0:T(8,128)S(1)}, f32[14,32,128]{2,1,0:T(8,128)S(1)}, u32[]{:S(2)}, u32[]{:S(2)}) collective-permute-start(f32[14,32,128]{2,1,0:T(8,128)S(1)} %get-tuple-element.63), channel_id=1, source_target_pairs={{2,0},{4,2},{6,4},{8,6},{10,8},{12,10},{14,12},{16,14},{18,16},{20... | collective-permute-start | bytes 688136 | tf_op jit(solution)/shard_map/ppermute | solution.py:636
  51.2 13.8 %collective-permute-start.20 = (f32[4,32,128]{2,1,0:T(8,128)S(1)}, f32[4,32,128]{2,1,0:T(8,128)S(1)}, u32[]{:S(2)}, u32[]{:S(2)}) collective-permute-start(f32[4,32,128]{2,1,0:T(8,128)S(1)} %merge.1.refs_0_), channel_id=1, source_target_pairs={{0,24},{2,26},{4,28},{6,30},{8,16},{10,18},{12,20},{14,22},{16,8},... | collective-permute-start | bytes 196616 | tf_op jit(solution)/shard_map/ppermute | solution.py:658
  58.3 8.5 %collective-permute-start.19 = (f32[4,32,128]{2,1,0:T(8,128)S(1)}, f32[4,32,128]{2,1,0:T(8,128)S(1)}, u32[]{:S(2)}, u32[]{:S(2)}) collective-permute-start(f32[4,32,128]{2,1,0:T(8,128)S(1)} %merge.1.refs_0_), channel_id=1, source_target_pairs={{0,16},{2,18},{4,20},{6,22},{8,24},{10,26},{12,28},{14,30},{16,0},... | collective-permute-start | bytes 196616 | tf_op jit(solution)/shard_map/ppermute | solution.py:658
  58.7 9.4 %collective-permute-start.18 = (f32[4,32,128]{2,1,0:T(8,128)S(1)}, f32[4,32,128]{2,1,0:T(8,128)S(1)}, u32[]{:S(2)}, u32[]{:S(2)}) collective-permute-start(f32[4,32,128]{2,1,0:T(8,128)S(1)} %merge.1.refs_0_), channel_id=1, source_target_pairs={{0,8},{2,10},{4,12},{6,14},{8,0},{10,2},{12,4},{14,6},{16,24},{18,... | collective-permute-start | bytes 196616 | tf_op jit(solution)/shard_map/ppermute | solution.py:658
  65.0 6.0 %collective-permute-start.23 = (f32[2,32,128]{2,1,0:T(8,128)S(1)}, f32[2,32,128]{2,1,0:T(8,128)S(1)}, u32[]{:S(2)}, u32[]{:S(2)}) collective-permute-start(f32[2,32,128]{2,1,0:T(8,128)S(1)} %get-tuple-element.64), channel_id=1, source_target_pairs={{0,4},{2,6},{4,8},{6,10},{8,12},{10,14},{12,16},{14,18},{16,20},{1... | collective-permute-start | bytes 98312 | tf_op jit(solution)/shard_map/ppermute | solution.py:636
  66.8 7.0 %collective-permute-start.24 = (f32[2,32,128]{2,1,0:T(8,128)S(1)}, f32[2,32,128]{2,1,0:T(8,128)S(1)}, u32[]{:S(2)}, u32[]{:S(2)}) collective-permute-start(f32[2,32,128]{2,1,0:T(8,128)S(1)} %get-tuple-element.65), channel_id=1, source_target_pairs={{4,0},{6,2},{8,4},{10,6},{12,8},{14,10},{16,12},{18,14},{20,16},{2... | collective-permute-start | bytes 98312 | tf_op jit(solution)/shard_map/ppermute | solution.py:636
  (4 other events, 4.4 us)

commit v5 on v4

--- a/solution.py
+++ b/solution.py
@@ -195,10 +195,9 @@
     return [n + 3] + [n + 2] * 6
 
 
-def start_kernel(sizes, place, right_side, conduct, binding, own0, own1, own2, to_next, to_prev, top, *refs):
-    edges, sums = refs[: sizes.sides], refs[-1]
+def start_kernel(sizes, place, conduct, binding, own0, own1, own2, to_next, to_prev, sums):
     n0, n1, n2 = sizes.rows[:3]
-    for at, array in enumerate((conduct, binding, right_side)):
+    for at, array in enumerate((conduct, binding)):
         own0[at] = jnp.swapaxes(array[...], 0, 1)
     for at in (0, 1):
         for row in range(n1):
@@ -207,22 +206,24 @@
     for row in range(2 * n2):
         sums[row, :, : sizes.own[1] * LANES] = own1[2 * row] + own1[2 * row + 1]
     narrow(sizes, place, 1, sums, own2, 2 * n2, "own")
-    last = jnp.concatenate([own2[0] + own2[1], own2[n2] + own2[n2 + 1]], axis=0)
-    last = dot(split(last), pair_table(LANES, 0, None, 0.25))
-    top[0] = last[: sizes.depth] + roll(last[sizes.depth :], LANES // 2, 1)
     for message, low, at1, at0 in ((to_next, n1 - 2, n1 - 1, n0 - 1), (to_prev, 0, 0, 0)):
         edge = n2 - 1 if at0 else 0
         rows = (own0[0, at0], own1[low], own1[low + 1], own1[n1 + at1])
         rows += (own2[n2 - 2], own2[n2 - 1], own2[n2 + edge])
         for slot, row in zip(sizes.slots, rows):
             put(message, slot, row)
+
+
+def turn_kernel(sizes, place, right_side, own0, turned, *edges):
+    turned[...] = jnp.swapaxes(right_side[...], 0, 1)
     last = sizes.extent_y - BORDER
-    if sizes.sides == 1:
-        at = pl.multiple_of(jnp.where(place[1] == 0, last, 0), LANES)
-        edges[0][...] = own0[:, :, :, pl.ds(at, BORDER)]
-    elif sizes.sides == 2:
-        edges[0][...] = own0[:, :, :, last:]
-        edges[1][...] = own0[:, :, :, :BORDER]
+    for index, array in enumerate((own0.at[0], own0.at[1], turned)):
+        if sizes.sides == 1:
+            at = pl.multiple_of(jnp.where(place[1] == 0, last, 0), LANES)
+            edges[0][index] = array[:, :, pl.ds(at, BORDER)]
+        elif sizes.sides == 2:
+            edges[0][index] = array[:, :, last:]
+            edges[1][index] = array[:, :, :BORDER]
 
 
 def message_row(sizes, place, level, slot, message, beside):
@@ -275,98 +276,83 @@
 
 
 def packing(sizes, count):
-    half, reach = LANES // 2, BORDER >> 3
-    pairs = -(-count // 2)
-    if sizes.sides != 1 or count * reach > LANES:
-        return False, count, None, None
-    if count % 2 and count * reach <= half:
-        return True, pairs, pairs - 1, half
-    return True, pairs + 1, pairs, 0
-
-
-def border_turn(place, first, index):
-    reach = BORDER >> 3
-    goal = first + index * reach
-    return jnp.where(place[1] == 0, (goal - LANES // 2) % LANES, (goal + reach) % LANES)
+    if sizes.sides != 1:
+        return False, count, count
+    own = -(-count // 2)
+    return True, own, own - (-count * (BORDER >> 3) // LANES)
+
+
+def border_turn(place, goal):
+    return jnp.where(place[1] == 0, (goal - LANES // 2) % LANES, (goal + (BORDER >> 3)) % LANES)
 
 
 def pack_rows(sizes, place, rows, target):
-    packed, tiles, border, first = packing(sizes, len(rows))
+    packed, own, tiles = packing(sizes, len(rows))
     if not packed:
         for index, row in enumerate(rows):
             target[index] = row
         return
     half, reach = LANES // 2, BORDER >> 3
     lane = lane_at(rows[0].shape)
-    held = [jnp.zeros(rows[0].shape, f32)] * tiles
-    for index, row in enumerate(rows):
-        if index % 2 == 0:
-            held[index // 2] = jnp.where(lane < half, row, 0.0)
-        else:
-            held[index // 2] = jnp.where(lane < half, held[index // 2], pltpu.roll(row, half, axis=1))
-    for index, row in enumerate(rows):
-        start = first + index * reach
-        moved = pltpu.roll(row, border_turn(place, first, index), axis=1)
-        held[border] = jnp.where((lane >= start) & (lane < start + reach), moved, held[border])
-    for index, tile in enumerate(held):
-        target[index] = tile
+    for index in range(own):
+        held = rows[2 * index]
+        other = rows[2 * index + 1] if 2 * index + 1 < len(rows) else jnp.zeros(held.shape, f32)
+        target[index] = jnp.where(lane < half, held, pltpu.roll(other, half, axis=1))
+    for index in range(own, tiles):
+        held = jnp.zeros(rows[0].shape, f32)
+        some = rows[(index - own) * (LANES // reach) :][: LANES // reach]
+        for place_at, row in enumerate(some):
+            goal = place_at * reach
+            moved = pltpu.roll(row, border_turn(place, goal), axis=1)
+            held = jnp.where((lane >= goal) & (lane < goal + reach), moved, held)
+        target[index] = held
 
 
 def unpack_rows(sizes, place, blocks, count):
-    packed, _, border, first = packing(sizes, count)
+    packed, own, _ = packing(sizes, count)
     if not packed:
         return [blocks[index] for index in range(count)]
     half, reach = LANES // 2, BORDER >> 3
     rows = []
     for index in range(count):
-        own = blocks[index // 2]
-        lane = lane_at(own.shape)
+        held = blocks[index // 2]
+        lane = lane_at(held.shape)
         if index % 2:
-            own = pltpu.roll(own, half, axis=1)
-        back = lax.rem(LANES - border_turn(place, first, index), LANES)
-        beside = pltpu.roll(blocks[border], back, axis=1)
+            held = pltpu.roll(held, half, axis=1)
+        at, goal = index // (LANES // reach), index % (LANES // reach) * reach
+        back = lax.rem(LANES - border_turn(place, goal), LANES)
+        beside = pltpu.roll(blocks[own + at], back, axis=1)
         start = jnp.where(place[1] == 0, half, LANES - reach)
         here = (lane >= start) & (lane < start + reach)
-        rows.append(jnp.where(lane < half, own, jnp.where(here, beside, 0.0)))
+        rows.append(jnp.where(lane < half, held, jnp.where(here, beside, 0.0)))
     return rows
 
 
-def merge_into(sizes, place, stride, radix, arrays, target):
+def merge_into(sizes, place, stride, radix, arrays, source, conduct, binding, first):
     position = (place[0] // stride) % radix
-    target[...] = jnp.zeros(target.shape, f32)
+    source[...] = jnp.zeros(source.shape, f32)
     for step, array in enumerate(arrays):
         at = (position ^ step) * stride
-        for index, row in enumerate(unpack_rows(sizes, place, array, stride + 2)):
-            target[at + index] = target[at + index] + row
+        rows = unpack_rows(sizes, place, array, 3 * stride + 2)
+        for index, row in enumerate(rows[: stride + 2]):
+            source[at + index] = source[at + index] + row
+        for index in range(stride):
+            conduct[at + index + first] = rows[stride + 2 + index]
+            binding[at + index] = rows[2 * stride + 2 + index]
 
 
 def merge_kernel(sizes, stride, radix, place, *refs):
-    arrays, out, total = refs[:radix], refs[radix], refs[radix + 1]
-    merge_into(sizes, place, stride, radix, arrays, total)
-    pack_rows(sizes, place, [total[row] for row in range(stride * radix + 2)], out)
-
-
-def top_row(sizes, place, block, beside):
-    half, reach = LANES // 2, BORDER >> 3
-    lane = lane_at(block.shape)
-    values = [jnp.where(lane < half, block, 0.0), jnp.where(lane < half, pltpu.roll(block, half, axis=1), 0.0)]
-    right = (lane >= half) & (lane < half + reach)
-    left = lane >= LANES - reach
-    for side in range(sizes.sides):
-        other = beside[side]
-        if sizes.sides == 2:
-            here = left if side else right
-        else:
-            first = jnp.where(place[1] == 0, half, LANES - reach)
-            here = (lane >= first) & (lane < first + reach)
-        values[0] = jnp.where(here, pltpu.roll(other, half, axis=1), values[0])
-        values[1] = jnp.where(here, other, values[1])
-    return values
+    arrays, out, (source, conduct, binding) = refs[:radix], refs[radix], refs[radix + 1 :]
+    merge_into(sizes, place, stride, radix, arrays, source, conduct, binding, 0)
+    count = stride * radix
+    rows = [source[row] for row in range(count + 2)]
+    rows += [conduct[row] for row in range(count)] + [binding[row] for row in range(count)]
+    pack_rows(sizes, place, rows, out)
 
 
 def down_kernel(sizes, place, *refs):
     s = sizes.sides
-    owns, refs = refs[:3], refs[3:]
+    owns, turned, refs = refs[:3], refs[3], refs[4:]
     borders0, refs = refs[:s], refs[s:]
     from_prev, from_next, refs = refs[0], refs[1], refs[2:]
     beside_prev, beside_next, refs = refs[: 2 * s : 2], refs[1 : 2 * s : 2], refs[2 * s :]
@@ -388,7 +374,7 @@
 
     def held_row(level, at, row):
         if level == 0:
-            tiles = [owns[0][at, row], *(array[at, row] for array in borders0)]
+            tiles = [turned[row] if at == 2 else owns[0][at, row], *(array[at, row] for array in borders0)]
         else:
             row = at * sizes.rows[level] + row
             tiles = [owns[level][row], *([(border1, border2)[level - 1][row]] if s else [])]
@@ -441,7 +427,10 @@
         sources.append(source)
     narrow(sizes, place, 2, sums.at[:, :, : sizes.held[2]], level3, 3)
 
-    pack_rows(sizes, place, [level3[row] for row in range(3)], contribution)
+    for at in (0, 1):
+        sums[at, :, : sizes.held[2]] = held_row(2, at, 0) + held_row(2, at, 1)
+    narrow(sizes, place, 2, sums.at[:, :, : sizes.held[2]], level3.at[3:5], 2)
+    pack_rows(sizes, place, [level3[row] for row in range(5)], contribution)
     (s1, s2), (v1, v2) = sources, smooths
     for at, rows in enumerate(
         (
@@ -473,13 +462,11 @@
 
 
 def coarse_kernel(sizes, stride, radix, place, *refs):
-    s = sizes.sides
-    blocks, tops, refs = refs[:radix], refs[radix : 2 * radix], refs[2 * radix :]
-    beside, refs = [refs[side * radix : (side + 1) * radix] for side in range(s)], refs[s * radix :]
+    blocks, refs = refs[:radix], refs[radix:]
     out, merged, sums = refs[:3]
     coarse = [refs[3 + 9 * index : 12 + 9 * index] for index in range(3)]
     total = sizes.span_count
-    merge_into(sizes, place, stride, radix, blocks, merged)
+    merge_into(sizes, place, stride, radix, blocks, merged, coarse[0][4], coarse[0][5], 1)
     zero = jnp.zeros((sizes.depth, LANES), f32)
     for index in range(3):
         level = 3 + index
@@ -490,12 +477,6 @@
             array[count + 1] = zero
         if index == 0:
             source = merged.at[1 : count + 1]
-            base = place[0] // stride % radix
-            for step in range(radix):
-                for low in range(stride):
-                    row = ((base ^ step) * stride) + ((place[0] % stride) ^ low)
-                    others = [arrays[step][low] for arrays in beside]
-                    conduct[row + 1], binding[row] = top_row(sizes, place, tops[step][low], others)
         bound = lambda row, binding=binding: binding[row - 1]
         at_row = lambda row, conduct=conduct: conduct[row]
         coefficients(sizes, place, level, count + 2, at_row, bound, fx, fy, fz, weight)
@@ -549,8 +530,8 @@
 
 def up_kernel(sizes, place, coarse, *refs):
     s = sizes.sides
-    (from_prev, from_next), fars, coefs, own0 = refs[:2], refs[2:4], refs[4:7], refs[7]
-    borders0, out, refs = refs[8 : 8 + s], refs[8 + s], refs[9 + s :]
+    (from_prev, from_next), fars, coefs, (own0, turned) = refs[:2], refs[2:4], refs[4:7], refs[7:9]
+    borders0, out, refs = refs[9 : 9 + s], refs[9 + s], refs[10 + s :]
     total1, total2, result = refs[:3]
     over2, over1, over0, lift2, lift1, lift0, it2, it1, it0, semaphores = refs[3:]
     slots = sizes.slots
@@ -593,7 +574,8 @@
         widen(sizes, place, level - 1, target, upper, n + 2)
 
     def held_row(at, row):
-        return jnp.concatenate([own0[at, row - 1], *(array[at, row - 1] for array in borders0)], axis=1)
+        own = turned[row - 1] if at == 2 else own0[at, row - 1]
+        return jnp.concatenate([own, *(array[at, row - 1] for array in borders0)], axis=1)
 
     fx, fy, fz, weight, v0 = parts(coefs[0], coefficient_rows(sizes, 0))
     lift0[0] = fringed_row(sizes, 0, 0, from_prev) + over0[0]
@@ -671,17 +653,23 @@
     held = [(depth, count) for count in sizes.held]
     down_message = (sizes.tiles, *tile)
     up_message = (sizes.tiles + 1, *tile)
-    own0, own1, own2, to_next, to_prev, top, *edges = call(
+    own0, own1, own2, to_next, to_prev = call(
         functools.partial(start_kernel, sizes),
         "start",
-        [(3, n0, *own[0]), (2 * n1, *own[1]), (2 * n2, *own[2]), down_message, down_message]
-        + [(1, *tile)]
-        + [(3, n0, depth, BORDER)] * s,
+        [(2, n0, *own[0]), (2 * n1, *own[1]), (2 * n2, *own[2]), down_message, down_message],
         [(2 * n1, *own[0])],
         place,
-        [right_side, diffusivity, reaction],
+        [diffusivity, reaction],
     )
     halos = [along(to_next, "span", 1), along(to_prev, "span", -1)]
+    turned, *edges = call(
+        functools.partial(turn_kernel, sizes),
+        "turn",
+        [(n0, *own[0])] + [(3, n0, depth, BORDER)] * s,
+        [],
+        place,
+        [right_side, own0],
+    )
     if s == 1:
         borders = [lax.ppermute(edges[0], "width", [(0, 1), (1, 0)])]
     elif s == 2:
@@ -689,12 +677,7 @@
     else:
         borders = []
     plan = list(stages(sizes.span_count))
-    for stride, radix in plan[:-1]:
-        top = jnp.concatenate(swap(top, stride, radix))
     sides = beside(halos, sizes)
-    tops = swap(top, *plan[-1])
-    beside_tops = beside(tops, sizes)
-    halos, sides, tops, beside_tops = lax.optimization_barrier((halos, sides, tops, beside_tops))
 
     lengths = [sum(coefficient_rows(sizes, level)) for level in range(3)]
     far = (sizes.held[2] // LANES, *tile)
@@ -702,19 +685,19 @@
     downs = call(
         functools.partial(down_kernel, sizes),
         "down",
-        [*coefs, (packing(sizes, 3)[1], *tile), up_message, up_message, far, far],
-        [(2 * n1, *tile), (2 * n2, *tile), (3, *tile), (max(2 * n1, n1 + 2), *held[0])],
+        [*coefs, (packing(sizes, 5)[2], *tile), up_message, up_message, far, far],
+        [(2 * n1, *tile), (2 * n2, *tile), (5, *tile), (max(2 * n1, n1 + 2), *held[0])],
         place,
-        [own0, own1, own2, *borders, *halos, *sum(sides, [])],
+        [own0, own1, own2, turned, *borders, *halos, *sum(sides, [])],
     )
     coefs_out, blocks, ups, fars = downs[:3], downs[3], downs[4:6], downs[6:8]
     for stride, radix in plan[:-1]:
-        rows = stride * radix + 2
+        count = stride * radix
         (blocks,) = call(
             functools.partial(merge_kernel, sizes, stride, radix),
             "merge",
-            [(packing(sizes, rows)[1], *tile)],
-            [(rows, *tile)],
+            [(packing(sizes, 3 * count + 2)[2], *tile)],
+            [(count + 2, *tile), (count, *tile), (count, *tile)],
             place,
             swap(blocks, stride, radix),
         )
@@ -734,7 +717,7 @@
         [(n3 + 2, *tile)],
         scratch,
         place,
-        [*blocks, *tops, *sum(beside_tops, [])],
+        blocks,
     )
     scratch = [(n1 + 2, *held[1]), (n2 + 2, *held[2]), diffusivity.shape]
     scratch += [(n3 + 2, *held[2]), (n2 + 2, *held[1]), (n1 + 2, *held[0])]
@@ -746,7 +729,7 @@
         [diffusivity.shape],
         scratch,
         place,
-        [coarse, *received, *coefs_out, own0, *borders],
+        [coarse, *received, *coefs_out, own0, turned, *borders],
         copies=CHUNKS,
         far_out=True,
     )

time: 77.3 us -> 69.1 us (0.89)
  starting transfers between devices: 34.7 us -> 24.3 us
  waiting for transfers between devices: 27.1 us -> 28.8 us
    ppermute x12 -> x6, starting transfers between devices: 22.2 us -> 11.8 us  [swap(): lax.ppermute(value, 'span', [(device, device ^ step * stride) for device...]
    ppermute x12 -> x6, waiting for transfers between devices: 15.1 us -> 17.6 us  [swap(): lax.ppermute(value, 'span', [(device, device ^ step * stride) for device...]
    ppermute x6, waiting for transfers between devices: 11 us -> 9.71 us  [along(): lax.ppermute(value, axis, [(source, source + steps) for source in range(i...]
    ppermute x6, starting transfers between devices: 11.4 us -> 12.5 us  [along(): lax.ppermute(value, axis, [(source, source + steps) for source in range(i...]
    ppermute x6 -> x2, starting transfers between devices: 1.06 us -> 0.01 us  [beside(): lax.ppermute(value, 'width', [(0, 1), (1, 0)])]
    pallas_call x5 -> x6, Pallas kernels: 11.8 us -> 12.3 us  [call(): pl.pallas_call(body, name=name, out_shape=[jax.ShapeDtypeStruct(shape, f3...]
    unnamed x9 -> x6, local copies, waits for them, and re-layouts: 3.13 us -> 3.12 us
  transfers between devices with their start and end apart: 25 -> 15, of which waited for: 13 -> 9; matrix products, arithmetic and copies ran while one was open for 0% -> 0% of each run, Pallas kernels for 4% -> 5%
where the time goes in v5:
time: 69.1 us; the launch traced here: 68.7 us
  waiting for transfers between devices  28.8 us (42%)
  starting transfers between devices  24.3 us (35%)
  Pallas kernels  12.3 us (18%)
  local copies, waits for them, and re-layouts  3.12 us (5%)
    ppermute x6, waiting for transfers between devices, swap(): lax.ppermute(value, 'span', [(device, device ^ step * stride) for device...  17.6 us
    ppermute x6, starting transfers between devices, along(): lax.ppermute(value, axis, [(source, source + steps) for source in range(i...  12.5 us
    pallas_call x6, Pallas kernels, call(): pl.pallas_call(body, name=name, out_shape=[jax.ShapeDtypeStruct(shape, f3...  12.3 us
    ppermute x6, starting transfers between devices, swap(): lax.ppermute(value, 'span', [(device, device ^ step * stride) for device...  11.8 us
    ppermute x6, waiting for transfers between devices, along(): lax.ppermute(value, axis, [(source, source + steps) for source in range(i...  9.71 us
    unnamed x6, local copies, waits for them, and re-layouts  3.12 us
    ppermute x2, waiting for transfers between devices, beside(): lax.ppermute(value, 'width', [(0, 1), (1, 0)])  1.46 us
  transfers between devices with their start and end apart: 15, of which 9 were waited for; matrix products, arithmetic and copies ran while one was open for 0% of the time, Pallas kernels for 5%

profile of v5, /device:TPU:0, one launch (start us, length us, event | category | flops | bytes accessed | tf_op | source)
XLA Modules:
  0.0 68.7 jit_solution(14926818260043861196)
XLA Ops:
  0.1 1.0 %copy-done.1 = f32[32,8,512]{2,1,0:T(8,128)S(1)} copy-done((f32[32,8,512]{2,1,0:T(8,128)S(1)}, f32[32,8,512]{2,1,0:T(8,128)}, u32[]{:S(2)}) %copy-start.1) | copy-done | bytes 524312
  1.1 1.0 %copy-done.2 = f32[32,8,512]{2,1,0:T(8,128)S(1)} copy-done((f32[32,8,512]{2,1,0:T(8,128)S(1)}, f32[32,8,512]{2,1,0:T(8,128)}, u32[]{:S(2)}) %copy-start.2) | copy-done | bytes 524312
  2.2 1.1 %start.1 = (f32[2,8,32,512]{3,2,1,0:T(8,128)S(1)}, f32[8,32,256]{2,1,0:T(8,128)S(1)}, f32[4,32,128]{2,1,0:T(8,128)S(1)}, f32[13,32,128]{2,1,0:T(8,128)S(1)}, f32[13,32,128]{2,1,0:T(8,128)S(1)}) custom-call(s32[2]{0:T(128)S(1)} %pad_add_fusion.place, f32[32,8,512]{2,1,0:T(8,128)S(1)} %copy-done.1, f32[32,8,512]{2,1,0:T(8,128)S(1)} %copy-done.2), custom_call_target="tpu_custom_call" | custom-call | tf_op jit(solution)/shard_map/start/pallas_call | solution.py:604
  3.3 4.9 %collective-permute-start.1 = (f32[13,32,128]{2,1,0:T(8,128)S(1)}, f32[13,32,128]{2,1,0:T(8,128)S(1)}, u32[]{:S(2)}, u32[]{:S(2)}) collective-permute-start(f32[13,32,128]{2,1,0:T(8,128)S(1)} %get-tuple-element.30), channel_id=1, source_target_pairs={{0,2},{2,4},{4,6},{6,8},{8,10},{10,12},{12,14},{14,16},{16,18},{18... | collective-permute-start | bytes 638984 | tf_op jit(solution)/shard_map/ppermute | solution.py:618
  8.1 1.3 %collective-permute-start.2 = (f32[13,32,128]{2,1,0:T(8,128)S(1)}, f32[13,32,128]{2,1,0:T(8,128)S(1)}, u32[]{:S(2)}, u32[]{:S(2)}) collective-permute-start(f32[13,32,128]{2,1,0:T(8,128)S(1)} %get-tuple-element.31), channel_id=1, source_target_pairs={{2,0},{4,2},{6,4},{8,6},{10,8},{12,10},{14,12},{16,14},{18,16},{20... | collective-permute-start | bytes 638984 | tf_op jit(solution)/shard_map/ppermute | solution.py:618
  9.4 1.0 %copy-done = f32[32,8,512]{2,1,0:T(8,128)S(1)} copy-done((f32[32,8,512]{2,1,0:T(8,128)S(1)}, f32[32,8,512]{2,1,0:T(8,128)}, u32[]{:S(2)}) %copy-start) | copy-done | bytes 524312
  11.2 1.4 %collective-permute-done.1.refs_5_ = f32[13,32,128]{2,1,0:T(8,128)S(1)} collective-permute-done((f32[13,32,128]{2,1,0:T(8,128)S(1)}, f32[13,32,128]{2,1,0:T(8,128)S(1)}, u32[]{:S(2)}, u32[]{:S(2)}) %collective-permute-start.1) | collective-permute-done | bytes 213024 | tf_op jit(solution)/shard_map/ppermute | solution.py:618
  12.6 6.5 %collective-permute-done.2.refs_6_ = f32[13,32,128]{2,1,0:T(8,128)S(1)} collective-permute-done((f32[13,32,128]{2,1,0:T(8,128)S(1)}, f32[13,32,128]{2,1,0:T(8,128)S(1)}, u32[]{:S(2)}, u32[]{:S(2)}) %collective-permute-start.2) | collective-permute-done | bytes 213024 | tf_op jit(solution)/shard_map/ppermute | solution.py:618
  19.1 1.5 %collective-permute-done.4.refs_8_ = f32[13,32,128]{2,1,0:T(8,128)S(1)} collective-permute-done((f32[13,32,128]{2,1,0:T(8,128)S(1)}, f32[13,32,128]{2,1,0:T(8,128)S(1)}, u32[]{:S(2)}, u32[]{:S(2)}) %collective-permute-start.4) | collective-permute-done | bytes 213024 | tf_op jit(solution)/shard_map/ppermute | solution.py:623
  20.6 3.7 %down.1 = (f32[41,32,640]{2,1,0:T(8,128)S(1)}, f32[43,32,384]{2,1,0:T(8,128)S(1)}, f32[29,32,256]{2,1,0:T(8,128)S(1)}, f32[4,32,128]{2,1,0:T(8,128)S(1)}, f32[14...) custom-call(s32[2]{0:T(128)S(1)} %pad_add_fusion.place, ...), custom_call_target="tpu_custom_call" | custom-call | tf_op jit(solution)/shard_map/down/pallas_call | solution.py:604
  24.3 1.9 %collective-permute-start.7 = (f32[4,32,128]{2,1,0:T(8,128)S(1)}, f32[4,32,128]{2,1,0:T(8,128)S(1)}, u32[]{:S(2)}, u32[]{:S(2)}) collective-permute-start(f32[4,32,128]{2,1,0:T(8,128)S(1)} %get-tuple-element.32.refs_0_), channel_id=1, source_target_pairs={{0,6},{2,4},{4,2},{6,0},{8,14},{10,12},{12,10},{14,8},{16,22},{18,... | collective-permute-start | bytes 196616 | tf_op jit(solution)/shard_map/ppermute | solution.py:640
  26.2 1.1 %collective-permute-start.6 = (f32[4,32,128]{2,1,0:T(8,128)S(1)}, f32[4,32,128]{2,1,0:T(8,128)S(1)}, u32[]{:S(2)}, u32[]{:S(2)}) collective-permute-start(f32[4,32,128]{2,1,0:T(8,128)S(1)} %get-tuple-element.32.refs_0_), channel_id=1, source_target_pairs={{0,4},{2,6},{4,0},{6,2},{8,12},{10,14},{12,8},{14,10},{16,20},{18,... | collective-permute-start | bytes 196616 | tf_op jit(solution)/shard_map/ppermute | solution.py:640
  27.8 1.7 %collective-permute-done.7.refs_3_ = f32[4,32,128]{2,1,0:T(8,128)S(1)} collective-permute-done((f32[4,32,128]{2,1,0:T(8,128)S(1)}, f32[4,32,128]{2,1,0:T(8,128)S(1)}, u32[]{:S(2)}, u32[]{:S(2)}) %collective-permute-start.7) | collective-permute-done | bytes 65568 | tf_op jit(solution)/shard_map/ppermute | solution.py:640
  29.6 1.2 %collective-permute-done.6.refs_2_ = f32[4,32,128]{2,1,0:T(8,128)S(1)} collective-permute-done((f32[4,32,128]{2,1,0:T(8,128)S(1)}, f32[4,32,128]{2,1,0:T(8,128)S(1)}, u32[]{:S(2)}, u32[]{:S(2)}) %collective-permute-start.6) | collective-permute-done | bytes 65568 | tf_op jit(solution)/shard_map/ppermute | solution.py:640
  32.4 2.5 %collective-permute-start.11 = (f32[14,32,128]{2,1,0:T(8,128)S(1)}, f32[14,32,128]{2,1,0:T(8,128)S(1)}, u32[]{:S(2)}, u32[]{:S(2)}) collective-permute-start(f32[14,32,128]{2,1,0:T(8,128)S(1)} %get-tuple-element.38), channel_id=1, source_target_pairs={{0,2},{2,4},{4,6},{6,8},{8,10},{10,12},{12,14},{14,16},{16,18},{18... | collective-permute-start | bytes 688136 | tf_op jit(solution)/shard_map/ppermute | solution.py:618
  34.9 1.3 %collective-permute-start.12 = (f32[14,32,128]{2,1,0:T(8,128)S(1)}, f32[14,32,128]{2,1,0:T(8,128)S(1)}, u32[]{:S(2)}, u32[]{:S(2)}) collective-permute-start(f32[14,32,128]{2,1,0:T(8,128)S(1)} %get-tuple-element.39), channel_id=1, source_target_pairs={{2,0},{4,2},{6,4},{8,6},{10,8},{12,10},{14,12},{16,14},{18,16},{20... | collective-permute-start | bytes 688136 | tf_op jit(solution)/shard_map/ppermute | solution.py:618
  36.2 7.6 %collective-permute-start.10 = (f32[9,32,128]{2,1,0:T(8,128)S(1)}, f32[9,32,128]{2,1,0:T(8,128)S(1)}, u32[]{:S(2)}, u32[]{:S(2)}) collective-permute-start(f32[9,32,128]{2,1,0:T(8,128)S(1)} %merge.1.refs_0_), channel_id=1, source_target_pairs={{0,24},{2,26},{4,28},{6,30},{8,16},{10,18},{12,20},{14,22},{16,8},... | collective-permute-start | bytes 442376 | tf_op jit(solution)/shard_map/ppermute | solution.py:640
  44.4 9.0 %collective-permute-done.10.refs_3_ = f32[9,32,128]{2,1,0:T(8,128)S(1)} collective-permute-done((f32[9,32,128]{2,1,0:T(8,128)S(1)}, f32[9,32,128]{2,1,0:T(8,128)S(1)}, u32[]{:S(2)}, u32[]{:S(2)}) %collective-permute-start.10) | collective-permute-done | bytes 147488 | tf_op jit(solution)/shard_map/ppermute | solution.py:640
  53.4 1.3 %collective-permute-start.13 = (f32[2,32,128]{2,1,0:T(8,128)S(1)}, f32[2,32,128]{2,1,0:T(8,128)S(1)}, u32[]{:S(2)}, u32[]{:S(2)}) collective-permute-start(f32[2,32,128]{2,1,0:T(8,128)S(1)} %get-tuple-element.40), channel_id=1, source_target_pairs={{0,4},{2,6},{4,8},{6,10},{8,12},{10,14},{12,16},{14,18},{16,20},{1... | collective-permute-start | bytes 98312 | tf_op jit(solution)/shard_map/ppermute | solution.py:618
  54.7 4.9 %collective-permute-done.9.refs_2_ = f32[9,32,128]{2,1,0:T(8,128)S(1)} collective-permute-done((f32[9,32,128]{2,1,0:T(8,128)S(1)}, f32[9,32,128]{2,1,0:T(8,128)S(1)}, u32[]{:S(2)}, u32[]{:S(2)}) %collective-permute-start.9) | collective-permute-done | bytes 147488 | tf_op jit(solution)/shard_map/ppermute | solution.py:640
  59.6 1.3 %collective-permute-start.14 = (f32[2,32,128]{2,1,0:T(8,128)S(1)}, f32[2,32,128]{2,1,0:T(8,128)S(1)}, u32[]{:S(2)}, u32[]{:S(2)}) collective-permute-start(f32[2,32,128]{2,1,0:T(8,128)S(1)} %get-tuple-element.41), channel_id=1, source_target_pairs={{4,0},{6,2},{8,4},{10,6},{12,8},{14,10},{16,12},{18,14},{20,16},{2... | collective-permute-start | bytes 98312 | tf_op jit(solution)/shard_map/ppermute | solution.py:618
  60.9 2.9 %coarse.1 = f32[3,32,128]{2,1,0:T(8,128)S(1)} custom-call(s32[2]{0:T(128)S(1)} %pad_add_fusion.place, f32[9,32,128]{2,1,0:T(8,128)S(1)} %merge.1.refs_0_, f32[9,32,128]{2,1,0:T(8,128)S(1)} %collective-permute-done.8.refs_1_, f32[9,32,128]{2,1,0:T(8,128)S(1)} %collective-permute-done.9.refs_2_, f32[9,32,128]{2,1,0:T(8,128)S(1)} %collective-permute-done.10.refs_3_), custom_call_target="tpu_custom_call" | custom-call | tf_op jit(solution)/shard_map/coarse/pallas_call | solution.py:604
  63.8 1.8 %collective-permute-done.14.refs_3_ = f32[2,32,128]{2,1,0:T(8,128)S(1)} collective-permute-done((f32[2,32,128]{2,1,0:T(8,128)S(1)}, f32[2,32,128]{2,1,0:T(8,128)S(1)}, u32[]{:S(2)}, u32[]{:S(2)}) %collective-permute-start.14) | collective-permute-done | bytes 32800 | tf_op jit(solution)/shard_map/ppermute | solution.py:618
  65.7 3.1 %up.1 = f32[32,8,512]{2,1,0:T(8,128)} custom-call(s32[2]{0:T(128)S(1)} %pad_add_fusion.place, f32[3,32,128]{2,1,0:T(8,128)S(1)} %coarse.1, f32[14,32,128]{2,1,0:T(8,128)S(1)} %collective-permute-done.11.refs_0_, f32[14,32,128]{2,1,0:T(8,128)S(1)} %collective-permute-done.12.refs_1_, f32[2,32,128]{2,1,0:T(8,128)S(1)} %collective-permute-done.13.refs_2_, ...), custom_call_target="tpu_custom_call" | custom-call | tf_op jit(solution)/shard_map/up/pallas_call | solution.py:604
  (19 shorter events, 3.7 us)
Async XLA Ops:
  0.1 1.0 %copy-start.1 = (f32[32,8,512]{2,1,0:T(8,128)S(1)}, f32[32,8,512]{2,1,0:T(8,128)}, u32[]{:S(2)}) copy-start(f32[32,8,512]{2,1,0:T(8,128)} %conduct.1) | copy-start | bytes 1572868
  1.1 1.0 %copy-start.2 = (f32[32,8,512]{2,1,0:T(8,128)S(1)}, f32[32,8,512]{2,1,0:T(8,128)}, u32[]{:S(2)}) copy-start(f32[32,8,512]{2,1,0:T(8,128)} %binding.1) | copy-start | bytes 1572868
  3.3 9.3 %collective-permute-start.1 = (f32[13,32,128]{2,1,0:T(8,128)S(1)}, f32[13,32,128]{2,1,0:T(8,128)S(1)}, u32[]{:S(2)}, u32[]{:S(2)}) collective-permute-start(f32[13,32,128]{2,1,0:T(8,128)S(1)} %get-tuple-element.30), channel_id=1, source_target_pairs={{0,2},{2,4},{4,6},{6,8},{8,10},{10,12},{12,14},{14,16},{16,18},{18... | collective-permute-start | bytes 638984 | tf_op jit(solution)/shard_map/ppermute | solution.py:618
  8.1 11.0 %collective-permute-start.2 = (f32[13,32,128]{2,1,0:T(8,128)S(1)}, f32[13,32,128]{2,1,0:T(8,128)S(1)}, u32[]{:S(2)}, u32[]{:S(2)}) collective-permute-start(f32[13,32,128]{2,1,0:T(8,128)S(1)} %get-tuple-element.31), channel_id=1, source_target_pairs={{2,0},{4,2},{6,4},{8,6},{10,8},{12,10},{14,12},{16,14},{18,16},{20... | collective-permute-start | bytes 638984 | tf_op jit(solution)/shard_map/ppermute | solution.py:618
  9.4 1.0 %copy-start = (f32[32,8,512]{2,1,0:T(8,128)S(1)}, f32[32,8,512]{2,1,0:T(8,128)}, u32[]{:S(2)}) copy-start(f32[32,8,512]{2,1,0:T(8,128)} %right_side.1) | copy-start | bytes 1572868
  11.2 8.0 %collective-permute-start = (f32[3,8,32,128]{3,2,1,0:T(8,128)S(1)}, f32[3,8,32,128]{3,2,1,0:T(8,128)S(1)}, u32[]{:S(2)}, u32[]{:S(2)}) collective-permute-start(f32[3,8,32,128]{3,2,1,0:T(8,128)S(1)} %get-tuple-element.29), channel_id=1, source_target_pairs={{0,1},{1,0},{2,3},{3,2},{4,5},{5,4},{6,7},{7,6},{8,9},{9,8},{10,11... | collective-permute-start | bytes 1179656 | tf_op jit(solution)/shard_map/ppermute | solution.py:674
  12.6 6.5 %collective-permute-start.3 = (f32[13,32,128]{2,1,0:T(8,128)S(1)}, f32[13,32,128]{2,1,0:T(8,128)S(1)}, u32[]{:S(2)}, u32[]{:S(2)}) collective-permute-start(f32[13,32,128]{2,1,0:T(8,128)S(1)} %collective-permute-done.1.refs_5_), channel_id=1, source_target_pairs={{0,1},{1,0},{2,3},{3,2},{4,5},{5,4},{6,7},{7,6},{8,9},{9,8},{10,11... | collective-permute-start | bytes 638984 | tf_op jit(solution)/shard_map/ppermute | solution.py:623
  19.1 1.5 %collective-permute-start.4 = (f32[13,32,128]{2,1,0:T(8,128)S(1)}, f32[13,32,128]{2,1,0:T(8,128)S(1)}, u32[]{:S(2)}, u32[]{:S(2)}) collective-permute-start(f32[13,32,128]{2,1,0:T(8,128)S(1)} %collective-permute-done.2.refs_6_), channel_id=1, source_target_pairs={{0,1},{1,0},{2,3},{3,2},{4,5},{5,4},{6,7},{7,6},{8,9},{9,8},{10,11... | collective-permute-start | bytes 638984 | tf_op jit(solution)/shard_map/ppermute | solution.py:623
  24.3 5.3 %collective-permute-start.7 = (f32[4,32,128]{2,1,0:T(8,128)S(1)}, f32[4,32,128]{2,1,0:T(8,128)S(1)}, u32[]{:S(2)}, u32[]{:S(2)}) collective-permute-start(f32[4,32,128]{2,1,0:T(8,128)S(1)} %get-tuple-element.32.refs_0_), channel_id=1, source_target_pairs={{0,6},{2,4},{4,2},{6,0},{8,14},{10,12},{12,10},{14,8},{16,22},{18,... | collective-permute-start | bytes 196616 | tf_op jit(solution)/shard_map/ppermute | solution.py:640
  26.2 4.6 %collective-permute-start.6 = (f32[4,32,128]{2,1,0:T(8,128)S(1)}, f32[4,32,128]{2,1,0:T(8,128)S(1)}, u32[]{:S(2)}, u32[]{:S(2)}) collective-permute-start(f32[4,32,128]{2,1,0:T(8,128)S(1)} %get-tuple-element.32.refs_0_), channel_id=1, source_target_pairs={{0,4},{2,6},{4,0},{6,2},{8,12},{10,14},{12,8},{14,10},{16,20},{18,... | collective-permute-start | bytes 196616 | tf_op jit(solution)/shard_map/ppermute | solution.py:640
  27.3 4.3 %collective-permute-start.5 = (f32[4,32,128]{2,1,0:T(8,128)S(1)}, f32[4,32,128]{2,1,0:T(8,128)S(1)}, u32[]{:S(2)}, u32[]{:S(2)}) collective-permute-start(f32[4,32,128]{2,1,0:T(8,128)S(1)} %get-tuple-element.32.refs_0_), channel_id=1, source_target_pairs={{0,2},{2,0},{4,6},{6,4},{8,10},{10,8},{12,14},{14,12},{16,18},{18,... | collective-permute-start | bytes 196616 | tf_op jit(solution)/shard_map/ppermute | solution.py:640
  32.4 33.2 %collective-permute-start.11 = (f32[14,32,128]{2,1,0:T(8,128)S(1)}, f32[14,32,128]{2,1,0:T(8,128)S(1)}, u32[]{:S(2)}, u32[]{:S(2)}) collective-permute-start(f32[14,32,128]{2,1,0:T(8,128)S(1)} %get-tuple-element.38), channel_id=1, source_target_pairs={{0,2},{2,4},{4,6},{6,8},{8,10},{10,12},{12,14},{14,16},{16,18},{18... | collective-permute-start | bytes 688136 | tf_op jit(solution)/shard_map/ppermute | solution.py:618
  34.9 30.8 %collective-permute-start.12 = (f32[14,32,128]{2,1,0:T(8,128)S(1)}, f32[14,32,128]{2,1,0:T(8,128)S(1)}, u32[]{:S(2)}, u32[]{:S(2)}) collective-permute-start(f32[14,32,128]{2,1,0:T(8,128)S(1)} %get-tuple-element.39), channel_id=1, source_target_pairs={{2,0},{4,2},{6,4},{8,6},{10,8},{12,10},{14,12},{16,14},{18,16},{20... | collective-permute-start | bytes 688136 | tf_op jit(solution)/shard_map/ppermute | solution.py:618
  36.2 17.2 %collective-permute-start.10 = (f32[9,32,128]{2,1,0:T(8,128)S(1)}, f32[9,32,128]{2,1,0:T(8,128)S(1)}, u32[]{:S(2)}, u32[]{:S(2)}) collective-permute-start(f32[9,32,128]{2,1,0:T(8,128)S(1)} %merge.1.refs_0_), channel_id=1, source_target_pairs={{0,24},{2,26},{4,28},{6,30},{8,16},{10,18},{12,20},{14,22},{16,8},... | collective-permute-start | bytes 442376 | tf_op jit(solution)/shard_map/ppermute | solution.py:640
  43.8 15.8 %collective-permute-start.9 = (f32[9,32,128]{2,1,0:T(8,128)S(1)}, f32[9,32,128]{2,1,0:T(8,128)S(1)}, u32[]{:S(2)}, u32[]{:S(2)}) collective-permute-start(f32[9,32,128]{2,1,0:T(8,128)S(1)} %merge.1.refs_0_), channel_id=1, source_target_pairs={{0,16},{2,18},{4,20},{6,22},{8,24},{10,26},{12,28},{14,30},{16,0},... | collective-permute-start | bytes 442376 | tf_op jit(solution)/shard_map/ppermute | solution.py:640
  43.8 17.1 %collective-permute-start.8 = (f32[9,32,128]{2,1,0:T(8,128)S(1)}, f32[9,32,128]{2,1,0:T(8,128)S(1)}, u32[]{:S(2)}, u32[]{:S(2)}) collective-permute-start(f32[9,32,128]{2,1,0:T(8,128)S(1)} %merge.1.refs_0_), channel_id=1, source_target_pairs={{0,8},{2,10},{4,12},{6,14},{8,0},{10,2},{12,4},{14,6},{16,24},{18,... | collective-permute-start | bytes 442376 | tf_op jit(solution)/shard_map/ppermute | solution.py:640
  53.4 10.4 %collective-permute-start.13 = (f32[2,32,128]{2,1,0:T(8,128)S(1)}, f32[2,32,128]{2,1,0:T(8,128)S(1)}, u32[]{:S(2)}, u32[]{:S(2)}) collective-permute-start(f32[2,32,128]{2,1,0:T(8,128)S(1)} %get-tuple-element.40), channel_id=1, source_target_pairs={{0,4},{2,6},{4,8},{6,10},{8,12},{10,14},{12,16},{14,18},{16,20},{1... | collective-permute-start | bytes 98312 | tf_op jit(solution)/shard_map/ppermute | solution.py:618
  59.6 6.1 %collective-permute-start.14 = (f32[2,32,128]{2,1,0:T(8,128)S(1)}, f32[2,32,128]{2,1,0:T(8,128)S(1)}, u32[]{:S(2)}, u32[]{:S(2)}) collective-permute-start(f32[2,32,128]{2,1,0:T(8,128)S(1)} %get-tuple-element.41), channel_id=1, source_target_pairs={{4,0},{6,2},{8,4},{10,6},{12,8},{14,10},{16,12},{18,14},{20,16},{2... | collective-permute-start | bytes 98312 | tf_op jit(solution)/shard_map/ppermute | solution.py:618

commit v6 on v5

--- a/solution.py
+++ b/solution.py
@@ -701,11 +701,10 @@
             place,
             swap(blocks, stride, radix),
         )
-    blocks, *sent = lax.optimization_barrier((blocks, *ups, *fars))
     stride, radix = plan[-1]
     blocks = swap(blocks, stride, radix)
-    received = [along(sent[0], "span", 1), along(sent[1], "span", -1)]
-    received += [along(sent[2], "span", 2), along(sent[3], "span", -2)]
+    received = [along(ups[0], "span", 1), along(ups[1], "span", -1)]
+    received += [along(fars[0], "span", 2), along(fars[1], "span", -2)]
     scratch = [(sizes.span_count + 2, *tile), (max(sizes.span_count // 2, 2), *tile)]
     for index in range(3):
         count = sizes.span_count >> index

time: 69.1 us -> 64.8 us (0.938)
  waiting for transfers between devices: 28.8 us -> 24.5 us
    ppermute x6, waiting for transfers between devices: 17.6 us -> 13.2 us  [swap(): lax.ppermute(value, 'span', [(device, device ^ step * stride) for device...]
    ppermute x6, starting transfers between devices: 11.8 us -> 10.8 us  [swap(): lax.ppermute(value, 'span', [(device, device ^ step * stride) for device...]
    ppermute x6, starting transfers between devices: 12.5 us -> 13.4 us  [along(): lax.ppermute(value, axis, [(source, source + steps) for source in range(i...]
  transfers between devices with their start and end apart: 15 -> 15, of which waited for: 9 -> 6; matrix products, arithmetic and copies ran while one was open for 0% -> 0% of each run, Pallas kernels for 5% -> 7%
where the time goes in v6:
time: 64.8 us; the launch traced here: 64.4 us
  waiting for transfers between devices  24.5 us (38%)
  starting transfers between devices  24.3 us (38%)
  Pallas kernels  12.3 us (19%)
  local copies, waits for them, and re-layouts  3.12 us (5%)
    ppermute x6, starting transfers between devices, along(): lax.ppermute(value, axis, [(source, source + steps) for source in range(i...  13.4 us
    ppermute x6, waiting for transfers between devices, swap(): lax.ppermute(value, 'span', [(device, device ^ step * stride) for device...  13.2 us
    pallas_call x6, Pallas kernels, call(): pl.pallas_call(body, name=name, out_shape=[jax.ShapeDtypeStruct(shape, f3...  12.3 us
    ppermute x6, starting transfers between devices, swap(): lax.ppermute(value, 'span', [(device, device ^ step * stride) for device...  10.8 us
    ppermute x6, waiting for transfers between devices, along(): lax.ppermute(value, axis, [(source, source + steps) for source in range(i...  9.81 us
    unnamed x6, local copies, waits for them, and re-layouts  3.12 us
    ppermute x2, waiting for transfers between devices, beside(): lax.ppermute(value, 'width', [(0, 1), (1, 0)])  1.46 us
  transfers between devices with their start and end apart: 15, of which 6 were waited for; matrix products, arithmetic and copies ran while one was open for 0% of the time, Pallas kernels for 7%

profile of v6, /device:TPU:0, one launch (start us, length us, event | category | flops | bytes accessed | tf_op | source)
XLA Modules:
  0.0 64.4 jit_solution(12464941524327060781)
XLA Ops:
  0.1 1.0 %copy-done.1 = f32[32,8,512]{2,1,0:T(8,128)S(1)} copy-done((f32[32,8,512]{2,1,0:T(8,128)S(1)}, f32[32,8,512]{2,1,0:T(8,128)}, u32[]{:S(2)}) %copy-start.1) | copy-done | bytes 524312
  1.1 1.0 %copy-done.2 = f32[32,8,512]{2,1,0:T(8,128)S(1)} copy-done((f32[32,8,512]{2,1,0:T(8,128)S(1)}, f32[32,8,512]{2,1,0:T(8,128)}, u32[]{:S(2)}) %copy-start.2) | copy-done | bytes 524312
  2.2 1.1 %start.1 = (f32[2,8,32,512]{3,2,1,0:T(8,128)S(1)}, f32[8,32,256]{2,1,0:T(8,128)S(1)}, f32[4,32,128]{2,1,0:T(8,128)S(1)}, f32[13,32,128]{2,1,0:T(8,128)S(1)}, f32[13,32,128]{2,1,0:T(8,128)S(1)}) custom-call(s32[2]{0:T(128)S(1)} %pad_add_fusion.place, f32[32,8,512]{2,1,0:T(8,128)S(1)} %copy-done.1, f32[32,8,512]{2,1,0:T(8,128)S(1)} %copy-done.2), custom_call_target="tpu_custom_call" | custom-call | tf_op jit(solution)/shard_map/start/pallas_call | solution.py:604
  3.3 4.9 %collective-permute-start.1 = (f32[13,32,128]{2,1,0:T(8,128)S(1)}, f32[13,32,128]{2,1,0:T(8,128)S(1)}, u32[]{:S(2)}, u32[]{:S(2)}) collective-permute-start(f32[13,32,128]{2,1,0:T(8,128)S(1)} %get-tuple-element.25), channel_id=1, source_target_pairs={{0,2},{2,4},{4,6},{6,8},{8,10},{10,12},{12,14},{14,16},{16,18},{18... | collective-permute-start | bytes 638984 | tf_op jit(solution)/shard_map/ppermute | solution.py:618
  8.1 1.3 %collective-permute-start.2 = (f32[13,32,128]{2,1,0:T(8,128)S(1)}, f32[13,32,128]{2,1,0:T(8,128)S(1)}, u32[]{:S(2)}, u32[]{:S(2)}) collective-permute-start(f32[13,32,128]{2,1,0:T(8,128)S(1)} %get-tuple-element.26), channel_id=1, source_target_pairs={{2,0},{4,2},{6,4},{8,6},{10,8},{12,10},{14,12},{16,14},{18,16},{20... | collective-permute-start | bytes 638984 | tf_op jit(solution)/shard_map/ppermute | solution.py:618
  9.4 1.0 %copy-done = f32[32,8,512]{2,1,0:T(8,128)S(1)} copy-done((f32[32,8,512]{2,1,0:T(8,128)S(1)}, f32[32,8,512]{2,1,0:T(8,128)}, u32[]{:S(2)}) %copy-start) | copy-done | bytes 524312
  10.5 0.7 %turn.1 = (f32[8,32,512]{2,1,0:T(8,128)S(1)}, f32[3,8,32,128]{3,2,1,0:T(8,128)S(1)}) custom-call(s32[2]{0:T(128)S(1)} %pad_add_fusion.place, f32[32,8,512]{2,1,0:T(8,128)S(1)} %copy-done, f32[2,8,32,512]{3,2,1,0:T(8,128)S(1)} %get-tuple-element.20.own0.refs_0_.refs_7_), custom_call_target="tpu_custom_call" | custom-call | tf_op jit(solution)/shard_map/turn/pallas_call | solution.py:604
  11.2 1.4 %collective-permute-done.1.refs_5_ = f32[13,32,128]{2,1,0:T(8,128)S(1)} collective-permute-done((f32[13,32,128]{2,1,0:T(8,128)S(1)}, f32[13,32,128]{2,1,0:T(8,128)S(1)}, u32[]{:S(2)}, u32[]{:S(2)}) %collective-permute-start.1) | collective-permute-done | bytes 213024 | tf_op jit(solution)/shard_map/ppermute | solution.py:618
  12.6 6.5 %collective-permute-done.2.refs_6_ = f32[13,32,128]{2,1,0:T(8,128)S(1)} collective-permute-done((f32[13,32,128]{2,1,0:T(8,128)S(1)}, f32[13,32,128]{2,1,0:T(8,128)S(1)}, u32[]{:S(2)}, u32[]{:S(2)}) %collective-permute-start.2) | collective-permute-done | bytes 213024 | tf_op jit(solution)/shard_map/ppermute | solution.py:618
  19.1 1.5 %collective-permute-done.4.refs_8_ = f32[13,32,128]{2,1,0:T(8,128)S(1)} collective-permute-done((f32[13,32,128]{2,1,0:T(8,128)S(1)}, f32[13,32,128]{2,1,0:T(8,128)S(1)}, u32[]{:S(2)}, u32[]{:S(2)}) %collective-permute-start.4) | collective-permute-done | bytes 213024 | tf_op jit(solution)/shard_map/ppermute | solution.py:623
  20.6 3.7 %down.1 = (f32[41,32,640]{2,1,0:T(8,128)S(1)}, f32[43,32,384]{2,1,0:T(8,128)S(1)}, f32[29,32,256]{2,1,0:T(8,128)S(1)}, f32[4,32,128]{2,1,0:T(8,128)S(1)}, f32[14...) custom-call(s32[2]{0:T(128)S(1)} %pad_add_fusion.place, ...), custom_call_target="tpu_custom_call" | custom-call | tf_op jit(solution)/shard_map/down/pallas_call | solution.py:604
  24.3 1.9 %collective-permute-start.7 = (f32[4,32,128]{2,1,0:T(8,128)S(1)}, f32[4,32,128]{2,1,0:T(8,128)S(1)}, u32[]{:S(2)}, u32[]{:S(2)}) collective-permute-start(f32[4,32,128]{2,1,0:T(8,128)S(1)} %get-tuple-element.27.refs_0_), channel_id=1, source_target_pairs={{0,6},{2,4},{4,2},{6,0},{8,14},{10,12},{12,10},{14,8},{16,22},{18,... | collective-permute-start | bytes 196616 | tf_op jit(solution)/shard_map/ppermute | solution.py:640
  26.2 1.1 %collective-permute-start.6 = (f32[4,32,128]{2,1,0:T(8,128)S(1)}, f32[4,32,128]{2,1,0:T(8,128)S(1)}, u32[]{:S(2)}, u32[]{:S(2)}) collective-permute-start(f32[4,32,128]{2,1,0:T(8,128)S(1)} %get-tuple-element.27.refs_0_), channel_id=1, source_target_pairs={{0,4},{2,6},{4,0},{6,2},{8,12},{10,14},{12,8},{14,10},{16,20},{18,... | collective-permute-start | bytes 196616 | tf_op jit(solution)/shard_map/ppermute | solution.py:640
  27.8 3.4 %collective-permute-start.11 = (f32[14,32,128]{2,1,0:T(8,128)S(1)}, f32[14,32,128]{2,1,0:T(8,128)S(1)}, u32[]{:S(2)}, u32[]{:S(2)}) collective-permute-start(f32[14,32,128]{2,1,0:T(8,128)S(1)} %get-tuple-element.28), channel_id=1, source_target_pairs={{0,2},{2,4},{4,6},{6,8},{8,10},{10,12},{12,14},{14,16},{16,18},{18... | collective-permute-start | bytes 688136 | tf_op jit(solution)/shard_map/ppermute | solution.py:618
  31.2 1.3 %collective-permute-start.12 = (f32[14,32,128]{2,1,0:T(8,128)S(1)}, f32[14,32,128]{2,1,0:T(8,128)S(1)}, u32[]{:S(2)}, u32[]{:S(2)}) collective-permute-start(f32[14,32,128]{2,1,0:T(8,128)S(1)} %get-tuple-element.29), channel_id=1, source_target_pairs={{2,0},{4,2},{6,4},{8,6},{10,8},{12,10},{14,12},{16,14},{18,16},{20... | collective-permute-start | bytes 688136 | tf_op jit(solution)/shard_map/ppermute | solution.py:618
  32.6 0.9 %merge.1.refs_0_ = f32[9,32,128]{2,1,0:T(8,128)S(1)} custom-call(s32[2]{0:T(128)S(1)} %pad_add_fusion.place, f32[4,32,128]{2,1,0:T(8,128)S(1)} %get-tuple-element.27.refs_0_, f32[4,32,128]{2,1,0:T(8,128)S(1)} %collective-permute-done.5.refs_1_, f32[4,32,128]{2,1,0:T(8,128)S(1)} %collective-permute-done.6.refs_2_, ...), custom_call_target="tpu_custom_call" | custom-call | tf_op jit(solution)/shard_map/merge/pallas_call | solution.py:604
  33.4 6.6 %collective-permute-start.10 = (f32[9,32,128]{2,1,0:T(8,128)S(1)}, f32[9,32,128]{2,1,0:T(8,128)S(1)}, u32[]{:S(2)}, u32[]{:S(2)}) collective-permute-start(f32[9,32,128]{2,1,0:T(8,128)S(1)} %merge.1.refs_0_), channel_id=1, source_target_pairs={{0,24},{2,26},{4,28},{6,30},{8,16},{10,18},{12,20},{14,22},{16,8},... | collective-permute-start | bytes 442376 | tf_op jit(solution)/shard_map/ppermute | solution.py:640
  40.7 8.1 %collective-permute-done.10.refs_3_ = f32[9,32,128]{2,1,0:T(8,128)S(1)} collective-permute-done((f32[9,32,128]{2,1,0:T(8,128)S(1)}, f32[9,32,128]{2,1,0:T(8,128)S(1)}, u32[]{:S(2)}, u32[]{:S(2)}) %collective-permute-start.10) | collective-permute-done | bytes 147488 | tf_op jit(solution)/shard_map/ppermute | solution.py:640
  48.8 1.3 %collective-permute-start.13 = (f32[2,32,128]{2,1,0:T(8,128)S(1)}, f32[2,32,128]{2,1,0:T(8,128)S(1)}, u32[]{:S(2)}, u32[]{:S(2)}) collective-permute-start(f32[2,32,128]{2,1,0:T(8,128)S(1)} %get-tuple-element.30), channel_id=1, source_target_pairs={{0,4},{2,6},{4,8},{6,10},{8,12},{10,14},{12,16},{14,18},{16,20},{1... | collective-permute-start | bytes 98312 | tf_op jit(solution)/shard_map/ppermute | solution.py:618
  50.1 5.1 %collective-permute-done.9.refs_2_ = f32[9,32,128]{2,1,0:T(8,128)S(1)} collective-permute-done((f32[9,32,128]{2,1,0:T(8,128)S(1)}, f32[9,32,128]{2,1,0:T(8,128)S(1)}, u32[]{:S(2)}, u32[]{:S(2)}) %collective-permute-start.9) | collective-permute-done | bytes 147488 | tf_op jit(solution)/shard_map/ppermute | solution.py:640
  55.2 1.3 %collective-permute-start.14 = (f32[2,32,128]{2,1,0:T(8,128)S(1)}, f32[2,32,128]{2,1,0:T(8,128)S(1)}, u32[]{:S(2)}, u32[]{:S(2)}) collective-permute-start(f32[2,32,128]{2,1,0:T(8,128)S(1)} %get-tuple-element.31), channel_id=1, source_target_pairs={{4,0},{6,2},{8,4},{10,6},{12,8},{14,10},{16,12},{18,14},{20,16},{2... | collective-permute-start | bytes 98312 | tf_op jit(solution)/shard_map/ppermute | solution.py:618
  56.5 2.9 %coarse.1 = f32[3,32,128]{2,1,0:T(8,128)S(1)} custom-call(s32[2]{0:T(128)S(1)} %pad_add_fusion.place, f32[9,32,128]{2,1,0:T(8,128)S(1)} %merge.1.refs_0_, f32[9,32,128]{2,1,0:T(8,128)S(1)} %collective-permute-done.8.refs_1_, f32[9,32,128]{2,1,0:T(8,128)S(1)} %collective-permute-done.9.refs_2_, f32[9,32,128]{2,1,0:T(8,128)S(1)} %collective-permute-done.10.refs_3_), custom_call_target="tpu_custom_call" | custom-call | tf_op jit(solution)/shard_map/coarse/pallas_call | solution.py:604
  59.4 1.9 %collective-permute-done.14.refs_3_ = f32[2,32,128]{2,1,0:T(8,128)S(1)} collective-permute-done((f32[2,32,128]{2,1,0:T(8,128)S(1)}, f32[2,32,128]{2,1,0:T(8,128)S(1)}, u32[]{:S(2)}, u32[]{:S(2)}) %collective-permute-start.14) | collective-permute-done | bytes 32800 | tf_op jit(solution)/shard_map/ppermute | solution.py:618
  61.3 3.1 %up.1 = f32[32,8,512]{2,1,0:T(8,128)} custom-call(s32[2]{0:T(128)S(1)} %pad_add_fusion.place, f32[3,32,128]{2,1,0:T(8,128)S(1)} %coarse.1, f32[14,32,128]{2,1,0:T(8,128)S(1)} %collective-permute-done.11.refs_0_, f32[14,32,128]{2,1,0:T(8,128)S(1)} %collective-permute-done.12.refs_1_, f32[2,32,128]{2,1,0:T(8,128)S(1)} %collective-permute-done.13.refs_2_, ...), custom_call_target="tpu_custom_call" | custom-call | tf_op jit(solution)/shard_map/up/pallas_call | solution.py:604
  (19 shorter events, 1.4 us)
Async XLA Ops:
  0.1 1.0 %copy-start.1 = (f32[32,8,512]{2,1,0:T(8,128)S(1)}, f32[32,8,512]{2,1,0:T(8,128)}, u32[]{:S(2)}) copy-start(f32[32,8,512]{2,1,0:T(8,128)} %conduct.1) | copy-start | bytes 1572868
  1.1 1.0 %copy-start.2 = (f32[32,8,512]{2,1,0:T(8,128)S(1)}, f32[32,8,512]{2,1,0:T(8,128)}, u32[]{:S(2)}) copy-start(f32[32,8,512]{2,1,0:T(8,128)} %binding.1) | copy-start | bytes 1572868
  3.3 9.3 %collective-permute-start.1 = (f32[13,32,128]{2,1,0:T(8,128)S(1)}, f32[13,32,128]{2,1,0:T(8,128)S(1)}, u32[]{:S(2)}, u32[]{:S(2)}) collective-permute-start(f32[13,32,128]{2,1,0:T(8,128)S(1)} %get-tuple-element.25), channel_id=1, source_target_pairs={{0,2},{2,4},{4,6},{6,8},{8,10},{10,12},{12,14},{14,16},{16,18},{18... | collective-permute-start | bytes 638984 | tf_op jit(solution)/shard_map/ppermute | solution.py:618
  8.1 11.0 %collective-permute-start.2 = (f32[13,32,128]{2,1,0:T(8,128)S(1)}, f32[13,32,128]{2,1,0:T(8,128)S(1)}, u32[]{:S(2)}, u32[]{:S(2)}) collective-permute-start(f32[13,32,128]{2,1,0:T(8,128)S(1)} %get-tuple-element.26), channel_id=1, source_target_pairs={{2,0},{4,2},{6,4},{8,6},{10,8},{12,10},{14,12},{16,14},{18,16},{20... | collective-permute-start | bytes 638984 | tf_op jit(solution)/shard_map/ppermute | solution.py:618
  9.4 1.0 %copy-start = (f32[32,8,512]{2,1,0:T(8,128)S(1)}, f32[32,8,512]{2,1,0:T(8,128)}, u32[]{:S(2)}) copy-start(f32[32,8,512]{2,1,0:T(8,128)} %right_side.1) | copy-start | bytes 1572868
  11.2 8.0 %collective-permute-start = (f32[3,8,32,128]{3,2,1,0:T(8,128)S(1)}, f32[3,8,32,128]{3,2,1,0:T(8,128)S(1)}, u32[]{:S(2)}, u32[]{:S(2)}) collective-permute-start(f32[3,8,32,128]{3,2,1,0:T(8,128)S(1)} %get-tuple-element.24), channel_id=1, source_target_pairs={{0,1},{1,0},{2,3},{3,2},{4,5},{5,4},{6,7},{7,6},{8,9},{9,8},{10,11... | collective-permute-start | bytes 1179656 | tf_op jit(solution)/shard_map/ppermute | solution.py:674
  12.6 6.5 %collective-permute-start.3 = (f32[13,32,128]{2,1,0:T(8,128)S(1)}, f32[13,32,128]{2,1,0:T(8,128)S(1)}, u32[]{:S(2)}, u32[]{:S(2)}) collective-permute-start(f32[13,32,128]{2,1,0:T(8,128)S(1)} %collective-permute-done.1.refs_5_), channel_id=1, source_target_pairs={{0,1},{1,0},{2,3},{3,2},{4,5},{5,4},{6,7},{7,6},{8,9},{9,8},{10,11... | collective-permute-start | bytes 638984 | tf_op jit(solution)/shard_map/ppermute | solution.py:623
  19.1 1.5 %collective-permute-start.4 = (f32[13,32,128]{2,1,0:T(8,128)S(1)}, f32[13,32,128]{2,1,0:T(8,128)S(1)}, u32[]{:S(2)}, u32[]{:S(2)}) collective-permute-start(f32[13,32,128]{2,1,0:T(8,128)S(1)} %collective-permute-done.2.refs_6_), channel_id=1, source_target_pairs={{0,1},{1,0},{2,3},{3,2},{4,5},{5,4},{6,7},{7,6},{8,9},{9,8},{10,11... | collective-permute-start | bytes 638984 | tf_op jit(solution)/shard_map/ppermute | solution.py:623
  24.3 8.3 %collective-permute-start.7 = (f32[4,32,128]{2,1,0:T(8,128)S(1)}, f32[4,32,128]{2,1,0:T(8,128)S(1)}, u32[]{:S(2)}, u32[]{:S(2)}) collective-permute-start(f32[4,32,128]{2,1,0:T(8,128)S(1)} %get-tuple-element.27.refs_0_), channel_id=1, source_target_pairs={{0,6},{2,4},{4,2},{6,0},{8,14},{10,12},{12,10},{14,8},{16,22},{18,... | collective-permute-start | bytes 196616 | tf_op jit(solution)/shard_map/ppermute | solution.py:640
  26.2 6.4 %collective-permute-start.6 = (f32[4,32,128]{2,1,0:T(8,128)S(1)}, f32[4,32,128]{2,1,0:T(8,128)S(1)}, u32[]{:S(2)}, u32[]{:S(2)}) collective-permute-start(f32[4,32,128]{2,1,0:T(8,128)S(1)} %get-tuple-element.27.refs_0_), channel_id=1, source_target_pairs={{0,4},{2,6},{4,0},{6,2},{8,12},{10,14},{12,8},{14,10},{16,20},{18,... | collective-permute-start | bytes 196616 | tf_op jit(solution)/shard_map/ppermute | solution.py:640
  27.3 5.3 %collective-permute-start.5 = (f32[4,32,128]{2,1,0:T(8,128)S(1)}, f32[4,32,128]{2,1,0:T(8,128)S(1)}, u32[]{:S(2)}, u32[]{:S(2)}) collective-permute-start(f32[4,32,128]{2,1,0:T(8,128)S(1)} %get-tuple-element.27.refs_0_), channel_id=1, source_target_pairs={{0,2},{2,0},{4,6},{6,4},{8,10},{10,8},{12,14},{14,12},{16,18},{18,... | collective-permute-start | bytes 196616 | tf_op jit(solution)/shard_map/ppermute | solution.py:640
  27.8 33.5 %collective-permute-start.11 = (f32[14,32,128]{2,1,0:T(8,128)S(1)}, f32[14,32,128]{2,1,0:T(8,128)S(1)}, u32[]{:S(2)}, u32[]{:S(2)}) collective-permute-start(f32[14,32,128]{2,1,0:T(8,128)S(1)} %get-tuple-element.28), channel_id=1, source_target_pairs={{0,2},{2,4},{4,6},{6,8},{8,10},{10,12},{12,14},{14,16},{16,18},{18... | collective-permute-start | bytes 688136 | tf_op jit(solution)/shard_map/ppermute | solution.py:618
  31.2 30.1 %collective-permute-start.12 = (f32[14,32,128]{2,1,0:T(8,128)S(1)}, f32[14,32,128]{2,1,0:T(8,128)S(1)}, u32[]{:S(2)}, u32[]{:S(2)}) collective-permute-start(f32[14,32,128]{2,1,0:T(8,128)S(1)} %get-tuple-element.29), channel_id=1, source_target_pairs={{2,0},{4,2},{6,4},{8,6},{10,8},{12,10},{14,12},{16,14},{18,16},{20... | collective-permute-start | bytes 688136 | tf_op jit(solution)/shard_map/ppermute | solution.py:618
  33.4 15.3 %collective-permute-start.10 = (f32[9,32,128]{2,1,0:T(8,128)S(1)}, f32[9,32,128]{2,1,0:T(8,128)S(1)}, u32[]{:S(2)}, u32[]{:S(2)}) collective-permute-start(f32[9,32,128]{2,1,0:T(8,128)S(1)} %merge.1.refs_0_), channel_id=1, source_target_pairs={{0,24},{2,26},{4,28},{6,30},{8,16},{10,18},{12,20},{14,22},{16,8},... | collective-permute-start | bytes 442376 | tf_op jit(solution)/shard_map/ppermute | solution.py:640
  40.0 15.1 %collective-permute-start.9 = (f32[9,32,128]{2,1,0:T(8,128)S(1)}, f32[9,32,128]{2,1,0:T(8,128)S(1)}, u32[]{:S(2)}, u32[]{:S(2)}) collective-permute-start(f32[9,32,128]{2,1,0:T(8,128)S(1)} %merge.1.refs_0_), channel_id=1, source_target_pairs={{0,16},{2,18},{4,20},{6,22},{8,24},{10,26},{12,28},{14,30},{16,0},... | collective-permute-start | bytes 442376 | tf_op jit(solution)/shard_map/ppermute | solution.py:640
  40.1 16.4 %collective-permute-start.8 = (f32[9,32,128]{2,1,0:T(8,128)S(1)}, f32[9,32,128]{2,1,0:T(8,128)S(1)}, u32[]{:S(2)}, u32[]{:S(2)}) collective-permute-start(f32[9,32,128]{2,1,0:T(8,128)S(1)} %merge.1.refs_0_), channel_id=1, source_target_pairs={{0,8},{2,10},{4,12},{6,14},{8,0},{10,2},{12,4},{14,6},{16,24},{18,... | collective-permute-start | bytes 442376 | tf_op jit(solution)/shard_map/ppermute | solution.py:640
  48.8 10.6 %collective-permute-start.13 = (f32[2,32,128]{2,1,0:T(8,128)S(1)}, f32[2,32,128]{2,1,0:T(8,128)S(1)}, u32[]{:S(2)}, u32[]{:S(2)}) collective-permute-start(f32[2,32,128]{2,1,0:T(8,128)S(1)} %get-tuple-element.30), channel_id=1, source_target_pairs={{0,4},{2,6},{4,8},{6,10},{8,12},{10,14},{12,16},{14,18},{16,20},{1... | collective-permute-start | bytes 98312 | tf_op jit(solution)/shard_map/ppermute | solution.py:618
  55.2 6.2 %collective-permute-start.14 = (f32[2,32,128]{2,1,0:T(8,128)S(1)}, f32[2,32,128]{2,1,0:T(8,128)S(1)}, u32[]{:S(2)}, u32[]{:S(2)}) collective-permute-start(f32[2,32,128]{2,1,0:T(8,128)S(1)} %get-tuple-element.31), channel_id=1, source_target_pairs={{4,0},{6,2},{8,4},{10,6},{12,8},{14,10},{16,12},{18,14},{20,16},{2... | collective-permute-start | bytes 98312 | tf_op jit(solution)/shard_map/ppermute | solution.py:618

commit v7 on v6

--- a/solution.py
+++ b/solution.py
@@ -16,6 +16,7 @@
 relax_weight = 0.8
 f32 = jnp.float32
 VMEM_LIMIT = 32 * 1024 * 1024
+BYTES_A_MICRO = 3.69e6
 CHUNKS = 4
 
 
@@ -596,7 +597,7 @@
         copy.wait()
 
 
-def call(body, name, outputs, scratch, place, inputs, copies=0, far_out=False):
+def call(body, name, micros, outputs, scratch, place, inputs, copies=0, far_out=False):
     near, far = pl.BlockSpec(memory_space=pltpu.VMEM), pl.BlockSpec(memory_space=pl.ANY)
     scratch = [pltpu.VMEM(shape, f32) for shape in scratch]
     if copies:
@@ -608,6 +609,7 @@
         in_specs=[pl.BlockSpec(memory_space=pltpu.SMEM)] + [near] * len(inputs),
         out_specs=[far if far_out else near] * len(outputs),
         scratch_shapes=scratch,
+        cost_estimate=pl.CostEstimate(flops=int(micros * 1.15e9), bytes_accessed=int(micros * BYTES_A_MICRO), transcendentals=0),
         compiler_params=pltpu.CompilerParams(vmem_limit_bytes=VMEM_LIMIT),
     )(place, *inputs)
 
@@ -656,6 +658,7 @@
     own0, own1, own2, to_next, to_prev = call(
         functools.partial(start_kernel, sizes),
         "start",
+        1.1,
         [(2, n0, *own[0]), (2 * n1, *own[1]), (2 * n2, *own[2]), down_message, down_message],
         [(2 * n1, *own[0])],
         place,
@@ -665,6 +668,7 @@
     turned, *edges = call(
         functools.partial(turn_kernel, sizes),
         "turn",
+        0.7,
         [(n0, *own[0])] + [(3, n0, depth, BORDER)] * s,
         [],
         place,
@@ -685,26 +689,31 @@
     downs = call(
         functools.partial(down_kernel, sizes),
         "down",
+        3.6,
         [*coefs, (packing(sizes, 5)[2], *tile), up_message, up_message, far, far],
         [(2 * n1, *tile), (2 * n2, *tile), (5, *tile), (max(2 * n1, n1 + 2), *held[0])],
         place,
         [own0, own1, own2, turned, *borders, *halos, *sum(sides, [])],
     )
     coefs_out, blocks, ups, fars = downs[:3], downs[3], downs[4:6], downs[6:8]
+    far_rows = [along(fars[0], "span", 2), along(fars[1], "span", -2)]
     for stride, radix in plan[:-1]:
         count = stride * radix
+        blocks = swap(blocks, stride, radix)
+        blocks, far_rows = lax.optimization_barrier((blocks, far_rows))
         (blocks,) = call(
             functools.partial(merge_kernel, sizes, stride, radix),
             "merge",
+            0.9,
             [(packing(sizes, 3 * count + 2)[2], *tile)],
             [(count + 2, *tile), (count, *tile), (count, *tile)],
             place,
-            swap(blocks, stride, radix),
+            blocks,
         )
     stride, radix = plan[-1]
     blocks = swap(blocks, stride, radix)
     received = [along(ups[0], "span", 1), along(ups[1], "span", -1)]
-    received += [along(fars[0], "span", 2), along(fars[1], "span", -2)]
+    received += far_rows
     scratch = [(sizes.span_count + 2, *tile), (max(sizes.span_count // 2, 2), *tile)]
     for index in range(3):
         count = sizes.span_count >> index
@@ -713,6 +722,7 @@
     (coarse,) = call(
         functools.partial(coarse_kernel, sizes, stride, radix),
         "coarse",
+        2.9,
         [(n3 + 2, *tile)],
         scratch,
         place,
@@ -725,6 +735,7 @@
     (correction,) = call(
         functools.partial(up_kernel, sizes),
         "up",
+        3.0,
         [diffusivity.shape],
         scratch,
         place,

time: 64.8 us -> 60.3 us (0.931); the launches traced: 64.4 us -> 59.2 us
  waiting for transfers between devices: 24.5 us -> 22 us
  starting transfers between devices: 24.3 us -> 22.5 us
  local copies, waits for them, and re-layouts: 3.12 us -> 2.09 us
    ppermute x6, waiting for transfers between devices: 13.2 us -> 6.46 us  [swap(): lax.ppermute(value, 'span', [(device, device ^ step * stride) for device...]
    ppermute x6, waiting for transfers between devices: 9.81 us -> 14.1 us  [along(): lax.ppermute(value, axis, [(source, source + steps) for source in range(i...]
    ppermute x6, starting transfers between devices: 10.8 us -> 8.25 us  [swap(): lax.ppermute(value, 'span', [(device, device ^ step * stride) for device...]
    unnamed x6, local copies, waits for them, and re-layouts: 3.12 us -> 2.09 us
    ppermute x6, starting transfers between devices: 13.4 us -> 14.2 us  [along(): lax.ppermute(value, axis, [(source, source + steps) for source in range(i...]
  transfers between devices with their start and end apart: 15 -> 15, of which waited for: 6 -> 6; matrix products, arithmetic and copies ran while one was open for 0% -> 0% of each run, Pallas kernels for 7% -> 6%
where the time goes in v7:
time: 60.3 us; the launch traced here: 59.2 us
  starting transfers between devices  22.5 us (37%)
  waiting for transfers between devices  22 us (36%)
  Pallas kernels  12.4 us (21%)
  local copies, waits for them, and re-layouts  2.09 us (3%)
    ppermute x6, starting transfers between devices, along(): lax.ppermute(value, axis, [(source, source + steps) for source in range(i...  14.2 us
    ppermute x6, waiting for transfers between devices, along(): lax.ppermute(value, axis, [(source, source + steps) for source in range(i...  14.1 us
    pallas_call x6, Pallas kernels, call(): pl.pallas_call(body, name=name, out_shape=[jax.ShapeDtypeStruct(shape, f3...  12.4 us
    ppermute x6, starting transfers between devices, swap(): lax.ppermute(value, 'span', [(device, device ^ step * stride) for device...  8.25 us
    ppermute x6, waiting for transfers between devices, swap(): lax.ppermute(value, 'span', [(device, device ^ step * stride) for device...  6.46 us
    unnamed x6, local copies, waits for them, and re-layouts  2.09 us
    ppermute x2, waiting for transfers between devices, beside(): lax.ppermute(value, 'width', [(0, 1), (1, 0)])  1.46 us
  transfers between devices with their start and end apart: 15, of which 6 were waited for; matrix products, arithmetic and copies ran while one was open for 0% of the time, Pallas kernels for 6%

profile of v7, /device:TPU:0, one launch (start us, length us, event | category | flops | bytes accessed | tf_op | source)
XLA Modules:
  0.0 59.2 jit_solution(11362041988104392924)
XLA Ops:
  0.1 1.0 %copy-done = f32[32,8,512]{2,1,0:T(8,128)S(1)} copy-done((f32[32,8,512]{2,1,0:T(8,128)S(1)}, f32[32,8,512]{2,1,0:T(8,128)}, u32[]{:S(2)}) %copy-start) | copy-done | bytes 524312
  1.1 1.0 %copy-done.1 = f32[32,8,512]{2,1,0:T(8,128)S(1)} copy-done((f32[32,8,512]{2,1,0:T(8,128)S(1)}, f32[32,8,512]{2,1,0:T(8,128)}, u32[]{:S(2)}) %copy-start.1) | copy-done | bytes 524312
  2.2 1.1 %start.1 = (f32[2,8,32,512]{3,2,1,0:T(8,128)S(1)}, f32[8,32,256]{2,1,0:T(8,128)S(1)}, f32[4,32,128]{2,1,0:T(8,128)S(1)}, f32[13,32,128]{2,1,0:T(8,128)S(1)}, f32[13,32,128]{2,1,0:T(8,128)S(1)}) custom-call(s32[2]{0:T(128)S(1)} %pad_add_fusion.place, f32[32,8,512]{2,1,0:T(8,128)S(1)} %copy-done, f32[32,8,512]{2,1,0:T(8,128)S(1)} %copy-done.1), custom_call_target="tpu_custom_call" | custom-call | flops 1264999936 | bytes 4059000 | tf_op jit(solution)/shard_map/start/pallas_call | solution.py:605
  3.3 4.9 %collective-permute-start.1 = (f32[13,32,128]{2,1,0:T(8,128)S(1)}, f32[13,32,128]{2,1,0:T(8,128)S(1)}, u32[]{:S(2)}, u32[]{:S(2)}) collective-permute-start(f32[13,32,128]{2,1,0:T(8,128)S(1)} %get-tuple-element.31), channel_id=1, source_target_pairs={{0,2},{2,4},{4,6},{6,8},{8,10},{10,12},{12,14},{14,16},{16,18},{18... | collective-permute-start | bytes 638984 | tf_op jit(solution)/shard_map/ppermute | solution.py:620
  8.1 1.3 %collective-permute-start.2 = (f32[13,32,128]{2,1,0:T(8,128)S(1)}, f32[13,32,128]{2,1,0:T(8,128)S(1)}, u32[]{:S(2)}, u32[]{:S(2)}) collective-permute-start(f32[13,32,128]{2,1,0:T(8,128)S(1)} %get-tuple-element.32), channel_id=1, source_target_pairs={{2,0},{4,2},{6,4},{8,6},{10,8},{12,10},{14,12},{16,14},{18,16},{20... | collective-permute-start | bytes 638984 | tf_op jit(solution)/shard_map/ppermute | solution.py:620
  9.4 0.7 %turn.1 = (f32[8,32,512]{2,1,0:T(8,128)S(1)}, f32[3,8,32,128]{3,2,1,0:T(8,128)S(1)}) custom-call(s32[2]{0:T(128)S(1)} %pad_add_fusion.place, f32[32,8,512]{2,1,0:T(8,128)S(1)} %copy-done.2, f32[2,8,32,512]{3,2,1,0:T(8,128)S(1)} %get-tuple-element.26.own0.refs_0_.refs_7_), custom_call_target="tpu_custom_call" | custom-call | flops 805000000 | bytes 2583000 | tf_op jit(solution)/shard_map/turn/pallas_call | solution.py:605
  10.2 2.4 %collective-permute-done.1.refs_5_ = f32[13,32,128]{2,1,0:T(8,128)S(1)} collective-permute-done((f32[13,32,128]{2,1,0:T(8,128)S(1)}, f32[13,32,128]{2,1,0:T(8,128)S(1)}, u32[]{:S(2)}, u32[]{:S(2)}) %collective-permute-start.1) | collective-permute-done | bytes 213024 | tf_op jit(solution)/shard_map/ppermute | solution.py:620
  12.6 6.5 %collective-permute-done.2.refs_6_ = f32[13,32,128]{2,1,0:T(8,128)S(1)} collective-permute-done((f32[13,32,128]{2,1,0:T(8,128)S(1)}, f32[13,32,128]{2,1,0:T(8,128)S(1)}, u32[]{:S(2)}, u32[]{:S(2)}) %collective-permute-start.2) | collective-permute-done | bytes 213024 | tf_op jit(solution)/shard_map/ppermute | solution.py:620
  19.1 1.5 %collective-permute-done.4.refs_8_ = f32[13,32,128]{2,1,0:T(8,128)S(1)} collective-permute-done((f32[13,32,128]{2,1,0:T(8,128)S(1)}, f32[13,32,128]{2,1,0:T(8,128)S(1)}, u32[]{:S(2)}, u32[]{:S(2)}) %collective-permute-start.4) | collective-permute-done | bytes 213024 | tf_op jit(solution)/shard_map/ppermute | solution.py:625
  20.6 3.7 %down.1 = (f32[41,32,640]{2,1,0:T(8,128)S(1)}, f32[43,32,384]{2,1,0:T(8,128)S(1)}, f32[29,32,256]{2,1,0:T(8,128)S(1)}, f32[4,32,128]{2,1,0:T(8,128)S(1)}, f32[14...) custom-call(s32[2]{0:T(128)S(1)} %pad_add_fusion.place, ...), custom_call_target="tpu_custom_call" | custom-call | flops 4140000000 | bytes 13284000 | tf_op jit(solution)/shard_map/down/pallas_call | solution.py:605
  24.3 1.9 %collective-permute-start.7 = (f32[4,32,128]{2,1,0:T(8,128)S(1)}, f32[4,32,128]{2,1,0:T(8,128)S(1)}, u32[]{:S(2)}, u32[]{:S(2)}) collective-permute-start(f32[4,32,128]{2,1,0:T(8,128)S(1)} %get-tuple-element.36.refs_0_), channel_id=1, source_target_pairs={{0,6},{2,4},{4,2},{6,0},{8,14},{10,12},{12,10},{14,8},{16,22},{18,... | collective-permute-start | bytes 196616 | tf_op jit(solution)/shard_map/ppermute | solution.py:642
  26.2 1.1 %collective-permute-start.6 = (f32[4,32,128]{2,1,0:T(8,128)S(1)}, f32[4,32,128]{2,1,0:T(8,128)S(1)}, u32[]{:S(2)}, u32[]{:S(2)}) collective-permute-start(f32[4,32,128]{2,1,0:T(8,128)S(1)} %get-tuple-element.36.refs_0_), channel_id=1, source_target_pairs={{0,4},{2,6},{4,0},{6,2},{8,12},{10,14},{12,8},{14,10},{16,20},{18,... | collective-permute-start | bytes 196616 | tf_op jit(solution)/shard_map/ppermute | solution.py:642
  27.3 0.5 collective-permute-start.5
  27.9 2.3 %collective-permute-start.8 = (f32[2,32,128]{2,1,0:T(8,128)S(1)}, f32[2,32,128]{2,1,0:T(8,128)S(1)}, u32[]{:S(2)}, u32[]{:S(2)}) collective-permute-start(f32[2,32,128]{2,1,0:T(8,128)S(1)} %get-tuple-element.34), channel_id=1, source_target_pairs={{0,4},{2,6},{4,8},{6,10},{8,12},{10,14},{12,16},{14,18},{16,20},{1... | collective-permute-start | bytes 98312 | tf_op jit(solution)/shard_map/ppermute | solution.py:620
  30.2 1.3 %collective-permute-start.9 = (f32[2,32,128]{2,1,0:T(8,128)S(1)}, f32[2,32,128]{2,1,0:T(8,128)S(1)}, u32[]{:S(2)}, u32[]{:S(2)}) collective-permute-start(f32[2,32,128]{2,1,0:T(8,128)S(1)} %get-tuple-element.35), channel_id=1, source_target_pairs={{4,0},{6,2},{8,4},{10,6},{12,8},{14,10},{16,12},{18,14},{20,16},{2... | collective-permute-start | bytes 98312 | tf_op jit(solution)/shard_map/ppermute | solution.py:620
  31.7 4.9 %collective-permute-done.9.refs_3_ = f32[2,32,128]{2,1,0:T(8,128)S(1)} collective-permute-done((f32[2,32,128]{2,1,0:T(8,128)S(1)}, f32[2,32,128]{2,1,0:T(8,128)S(1)}, u32[]{:S(2)}, u32[]{:S(2)}) %collective-permute-start.9) | collective-permute-done | bytes 32800 | tf_op jit(solution)/shard_map/ppermute | solution.py:620
  36.6 0.9 %merge.1.refs_0_ = f32[9,32,128]{2,1,0:T(8,128)S(1)} custom-call(s32[2]{0:T(128)S(1)} %pad_add_fusion.place, f32[4,32,128]{2,1,0:T(8,128)S(1)} %get-tuple-element.36.refs_0_, f32[4,32,128]{2,1,0:T(8,128)S(1)} %collective-permute-done.5.refs_1_, f32[4,32,128]{2,1,0:T(8,128)S(1)} %collective-permute-done.6.refs_2_, ...), custom_call_target="tpu_custom_call" | custom-call | flops 1035000000 | bytes 3321000 | tf_op jit(solution)/shard_map/merge/pallas_call | solution.py:605
  37.5 4.0 %collective-permute-start.12 = (f32[9,32,128]{2,1,0:T(8,128)S(1)}, f32[9,32,128]{2,1,0:T(8,128)S(1)}, u32[]{:S(2)}, u32[]{:S(2)}) collective-permute-start(f32[9,32,128]{2,1,0:T(8,128)S(1)} %merge.1.refs_0_), channel_id=1, source_target_pairs={{0,24},{2,26},{4,28},{6,30},{8,16},{10,18},{12,20},{14,22},{16,8},... | collective-permute-start | bytes 442376 | tf_op jit(solution)/shard_map/ppermute | solution.py:642
  41.5 0.6 %collective-permute-start.10 = (f32[9,32,128]{2,1,0:T(8,128)S(1)}, f32[9,32,128]{2,1,0:T(8,128)S(1)}, u32[]{:S(2)}, u32[]{:S(2)}) collective-permute-start(f32[9,32,128]{2,1,0:T(8,128)S(1)} %merge.1.refs_0_), channel_id=1, source_target_pairs={{0,8},{2,10},{4,12},{6,14},{8,0},{10,2},{12,4},{14,6},{16,24},{18,... | collective-permute-start | bytes 442376 | tf_op jit(solution)/shard_map/ppermute | solution.py:642
  42.2 3.2 %collective-permute-start.13 = (f32[14,32,128]{2,1,0:T(8,128)S(1)}, f32[14,32,128]{2,1,0:T(8,128)S(1)}, u32[]{:S(2)}, u32[]{:S(2)}) collective-permute-start(f32[14,32,128]{2,1,0:T(8,128)S(1)} %get-tuple-element.40), channel_id=1, source_target_pairs={{0,2},{2,4},{4,6},{6,8},{8,10},{10,12},{12,14},{14,16},{16,18},{18... | collective-permute-start | bytes 688136 | tf_op jit(solution)/shard_map/ppermute | solution.py:620
  45.4 1.3 %collective-permute-start.14 = (f32[14,32,128]{2,1,0:T(8,128)S(1)}, f32[14,32,128]{2,1,0:T(8,128)S(1)}, u32[]{:S(2)}, u32[]{:S(2)}) collective-permute-start(f32[14,32,128]{2,1,0:T(8,128)S(1)} %get-tuple-element.41), channel_id=1, source_target_pairs={{2,0},{4,2},{6,4},{8,6},{10,8},{12,10},{14,12},{16,14},{18,16},{20... | collective-permute-start | bytes 688136 | tf_op jit(solution)/shard_map/ppermute | solution.py:620
  46.7 6.4 %collective-permute-done.11.refs_2_ = f32[9,32,128]{2,1,0:T(8,128)S(1)} collective-permute-done((f32[9,32,128]{2,1,0:T(8,128)S(1)}, f32[9,32,128]{2,1,0:T(8,128)S(1)}, u32[]{:S(2)}, u32[]{:S(2)}) %collective-permute-start.11) | collective-permute-done | bytes 147488 | tf_op jit(solution)/shard_map/ppermute | solution.py:642
  53.1 2.9 %coarse.1 = f32[3,32,128]{2,1,0:T(8,128)S(1)} custom-call(s32[2]{0:T(128)S(1)} %pad_add_fusion.place, f32[9,32,128]{2,1,0:T(8,128)S(1)} %merge.1.refs_0_, f32[9,32,128]{2,1,0:T(8,128)S(1)} %collective-permute-done.10.refs_1_, f32[9,32,128]{2,1,0:T(8,128)S(1)} %collective-permute-done.11.refs_2_, f32[9,32,128]{2,1,0:T(8,128)S(1)} %collective-permute-done.12.refs_3_), custom_call_target="tpu_custom_call" | custom-call | flops 3335000064 | bytes 10701000 | tf_op jit(solution)/shard_map/coarse/pallas_call | solution.py:605
  56.1 3.1 %up.1 = f32[32,8,512]{2,1,0:T(8,128)} custom-call(s32[2]{0:T(128)S(1)} %pad_add_fusion.place, f32[3,32,128]{2,1,0:T(8,128)S(1)} %coarse.1, f32[14,32,128]{2,1,0:T(8,128)S(1)} %collective-permute-done.13.refs_0_, f32[14,32,128]{2,1,0:T(8,128)S(1)} %collective-permute-done.14.refs_1_, f32[2,32,128]{2,1,0:T(8,128)S(1)} %collective-permute-done.8.refs_2_, ...), custom_call_target="tpu_custom_call" | custom-call | flops 3449999872 | bytes 11070000 | tf_op jit(solution)/shard_map/up/pallas_call | solution.py:605
  (19 shorter events, 0.5 us)
Async XLA Ops:
  0.1 1.0 %copy-start = (f32[32,8,512]{2,1,0:T(8,128)S(1)}, f32[32,8,512]{2,1,0:T(8,128)}, u32[]{:S(2)}) copy-start(f32[32,8,512]{2,1,0:T(8,128)} %conduct.1) | copy-start | bytes 1572868
  1.1 1.0 %copy-start.1 = (f32[32,8,512]{2,1,0:T(8,128)S(1)}, f32[32,8,512]{2,1,0:T(8,128)}, u32[]{:S(2)}) copy-start(f32[32,8,512]{2,1,0:T(8,128)} %binding.1) | copy-start | bytes 1572868
  2.2 7.3 %copy-start.2 = (f32[32,8,512]{2,1,0:T(8,128)S(1)}, f32[32,8,512]{2,1,0:T(8,128)}, u32[]{:S(2)}) copy-start(f32[32,8,512]{2,1,0:T(8,128)} %right_side.1) | copy-start | bytes 1572868
  3.3 9.3 %collective-permute-start.1 = (f32[13,32,128]{2,1,0:T(8,128)S(1)}, f32[13,32,128]{2,1,0:T(8,128)S(1)}, u32[]{:S(2)}, u32[]{:S(2)}) collective-permute-start(f32[13,32,128]{2,1,0:T(8,128)S(1)} %get-tuple-element.31), channel_id=1, source_target_pairs={{0,2},{2,4},{4,6},{6,8},{8,10},{10,12},{12,14},{14,16},{16,18},{18... | collective-permute-start | bytes 638984 | tf_op jit(solution)/shard_map/ppermute | solution.py:620
  8.1 11.0 %collective-permute-start.2 = (f32[13,32,128]{2,1,0:T(8,128)S(1)}, f32[13,32,128]{2,1,0:T(8,128)S(1)}, u32[]{:S(2)}, u32[]{:S(2)}) collective-permute-start(f32[13,32,128]{2,1,0:T(8,128)S(1)} %get-tuple-element.32), channel_id=1, source_target_pairs={{2,0},{4,2},{6,4},{8,6},{10,8},{12,10},{14,12},{16,14},{18,16},{20... | collective-permute-start | bytes 638984 | tf_op jit(solution)/shard_map/ppermute | solution.py:620
  10.1 9.0 %collective-permute-start = (f32[3,8,32,128]{3,2,1,0:T(8,128)S(1)}, f32[3,8,32,128]{3,2,1,0:T(8,128)S(1)}, u32[]{:S(2)}, u32[]{:S(2)}) collective-permute-start(f32[3,8,32,128]{3,2,1,0:T(8,128)S(1)} %get-tuple-element.30), channel_id=1, source_target_pairs={{0,1},{1,0},{2,3},{3,2},{4,5},{5,4},{6,7},{7,6},{8,9},{9,8},{10,11... | collective-permute-start | bytes 1179656 | tf_op jit(solution)/shard_map/ppermute | solution.py:678
  12.6 6.5 %collective-permute-start.3 = (f32[13,32,128]{2,1,0:T(8,128)S(1)}, f32[13,32,128]{2,1,0:T(8,128)S(1)}, u32[]{:S(2)}, u32[]{:S(2)}) collective-permute-start(f32[13,32,128]{2,1,0:T(8,128)S(1)} %collective-permute-done.1.refs_5_), channel_id=1, source_target_pairs={{0,1},{1,0},{2,3},{3,2},{4,5},{5,4},{6,7},{7,6},{8,9},{9,8},{10,11... | collective-permute-start | bytes 638984 | tf_op jit(solution)/shard_map/ppermute | solution.py:625
  19.1 1.5 %collective-permute-start.4 = (f32[13,32,128]{2,1,0:T(8,128)S(1)}, f32[13,32,128]{2,1,0:T(8,128)S(1)}, u32[]{:S(2)}, u32[]{:S(2)}) collective-permute-start(f32[13,32,128]{2,1,0:T(8,128)S(1)} %collective-permute-done.2.refs_6_), channel_id=1, source_target_pairs={{0,1},{1,0},{2,3},{3,2},{4,5},{5,4},{6,7},{7,6},{8,9},{9,8},{10,11... | collective-permute-start | bytes 638984 | tf_op jit(solution)/shard_map/ppermute | solution.py:625
  24.3 12.3 %collective-permute-start.7 = (f32[4,32,128]{2,1,0:T(8,128)S(1)}, f32[4,32,128]{2,1,0:T(8,128)S(1)}, u32[]{:S(2)}, u32[]{:S(2)}) collective-permute-start(f32[4,32,128]{2,1,0:T(8,128)S(1)} %get-tuple-element.36.refs_0_), channel_id=1, source_target_pairs={{0,6},{2,4},{4,2},{6,0},{8,14},{10,12},{12,10},{14,8},{16,22},{18,... | collective-permute-start | bytes 196616 | tf_op jit(solution)/shard_map/ppermute | solution.py:642
  26.2 10.4 %collective-permute-start.6 = (f32[4,32,128]{2,1,0:T(8,128)S(1)}, f32[4,32,128]{2,1,0:T(8,128)S(1)}, u32[]{:S(2)}, u32[]{:S(2)}) collective-permute-start(f32[4,32,128]{2,1,0:T(8,128)S(1)} %get-tuple-element.36.refs_0_), channel_id=1, source_target_pairs={{0,4},{2,6},{4,0},{6,2},{8,12},{10,14},{12,8},{14,10},{16,20},{18,... | collective-permute-start | bytes 196616 | tf_op jit(solution)/shard_map/ppermute | solution.py:642
  27.3 9.3 %collective-permute-start.5 = (f32[4,32,128]{2,1,0:T(8,128)S(1)}, f32[4,32,128]{2,1,0:T(8,128)S(1)}, u32[]{:S(2)}, u32[]{:S(2)}) collective-permute-start(f32[4,32,128]{2,1,0:T(8,128)S(1)} %get-tuple-element.36.refs_0_), channel_id=1, source_target_pairs={{0,2},{2,0},{4,6},{6,4},{8,10},{10,8},{12,14},{14,12},{16,18},{18,... | collective-permute-start | bytes 196616 | tf_op jit(solution)/shard_map/ppermute | solution.py:642
  27.9 3.9 %collective-permute-start.8 = (f32[2,32,128]{2,1,0:T(8,128)S(1)}, f32[2,32,128]{2,1,0:T(8,128)S(1)}, u32[]{:S(2)}, u32[]{:S(2)}) collective-permute-start(f32[2,32,128]{2,1,0:T(8,128)S(1)} %get-tuple-element.34), channel_id=1, source_target_pairs={{0,4},{2,6},{4,8},{6,10},{8,12},{10,14},{12,16},{14,18},{16,20},{1... | collective-permute-start | bytes 98312 | tf_op jit(solution)/shard_map/ppermute | solution.py:620
  30.2 6.4 %collective-permute-start.9 = (f32[2,32,128]{2,1,0:T(8,128)S(1)}, f32[2,32,128]{2,1,0:T(8,128)S(1)}, u32[]{:S(2)}, u32[]{:S(2)}) collective-permute-start(f32[2,32,128]{2,1,0:T(8,128)S(1)} %get-tuple-element.35), channel_id=1, source_target_pairs={{4,0},{6,2},{8,4},{10,6},{12,8},{14,10},{16,12},{18,14},{20,16},{2... | collective-permute-start | bytes 98312 | tf_op jit(solution)/shard_map/ppermute | solution.py:620
  37.5 9.2 %collective-permute-start.12 = (f32[9,32,128]{2,1,0:T(8,128)S(1)}, f32[9,32,128]{2,1,0:T(8,128)S(1)}, u32[]{:S(2)}, u32[]{:S(2)}) collective-permute-start(f32[9,32,128]{2,1,0:T(8,128)S(1)} %merge.1.refs_0_), channel_id=1, source_target_pairs={{0,24},{2,26},{4,28},{6,30},{8,16},{10,18},{12,20},{14,22},{16,8},... | collective-permute-start | bytes 442376 | tf_op jit(solution)/shard_map/ppermute | solution.py:642
  41.5 11.6 %collective-permute-start.11 = (f32[9,32,128]{2,1,0:T(8,128)S(1)}, f32[9,32,128]{2,1,0:T(8,128)S(1)}, u32[]{:S(2)}, u32[]{:S(2)}) collective-permute-start(f32[9,32,128]{2,1,0:T(8,128)S(1)} %merge.1.refs_0_), channel_id=1, source_target_pairs={{0,16},{2,18},{4,20},{6,22},{8,24},{10,26},{12,28},{14,30},{16,0},... | collective-permute-start | bytes 442376 | tf_op jit(solution)/shard_map/ppermute | solution.py:642
  41.5 11.6 %collective-permute-start.10 = (f32[9,32,128]{2,1,0:T(8,128)S(1)}, f32[9,32,128]{2,1,0:T(8,128)S(1)}, u32[]{:S(2)}, u32[]{:S(2)}) collective-permute-start(f32[9,32,128]{2,1,0:T(8,128)S(1)} %merge.1.refs_0_), channel_id=1, source_target_pairs={{0,8},{2,10},{4,12},{6,14},{8,0},{10,2},{12,4},{14,6},{16,24},{18,... | collective-permute-start | bytes 442376 | tf_op jit(solution)/shard_map/ppermute | solution.py:642
  42.2 13.9 %collective-permute-start.13 = (f32[14,32,128]{2,1,0:T(8,128)S(1)}, f32[14,32,128]{2,1,0:T(8,128)S(1)}, u32[]{:S(2)}, u32[]{:S(2)}) collective-permute-start(f32[14,32,128]{2,1,0:T(8,128)S(1)} %get-tuple-element.40), channel_id=1, source_target_pairs={{0,2},{2,4},{4,6},{6,8},{8,10},{10,12},{12,14},{14,16},{16,18},{18... | collective-permute-start | bytes 688136 | tf_op jit(solution)/shard_map/ppermute | solution.py:620
  45.4 10.7 %collective-permute-start.14 = (f32[14,32,128]{2,1,0:T(8,128)S(1)}, f32[14,32,128]{2,1,0:T(8,128)S(1)}, u32[]{:S(2)}, u32[]{:S(2)}) collective-permute-start(f32[14,32,128]{2,1,0:T(8,128)S(1)} %get-tuple-element.41), channel_id=1, source_target_pairs={{2,0},{4,2},{6,4},{8,6},{10,8},{12,10},{14,12},{16,14},{18,16},{20... | collective-permute-start | bytes 688136 | tf_op jit(solution)/shard_map/ppermute | solution.py:620

commit v8 on v7

--- a/solution.py
+++ b/solution.py
@@ -41,6 +41,21 @@
     start, tiles = slot
     for tile in range(tiles):
         message[start + tile] = row[:, tile * LANES : (tile + 1) * LANES]
+
+
+class Arrived:
+    def __init__(self, place, pair, forward, stride=1):
+        self.even = place[0] // stride % 2 == 0
+        self.first, self.second = (pair[0], pair[1]) if forward else (pair[1], pair[0])
+
+    def __getitem__(self, index):
+        return jnp.where(self.even, self.first[index], self.second[index])
+
+
+def put_pair(place, pair, slot, next_row, prev_row, stride=1):
+    even = place[0] // stride % 2 == 0
+    put(pair[0], slot, jnp.where(even, next_row, prev_row))
+    put(pair[1], slot, jnp.where(even, prev_row, next_row))
 
 
 def get(message, slot):
@@ -196,7 +211,7 @@
     return [n + 3] + [n + 2] * 6
 
 
-def start_kernel(sizes, place, conduct, binding, own0, own1, own2, to_next, to_prev, sums):
+def start_kernel(sizes, place, conduct, binding, own0, own1, own2, first, second, sums):
     n0, n1, n2 = sizes.rows[:3]
     for at, array in enumerate((conduct, binding)):
         own0[at] = jnp.swapaxes(array[...], 0, 1)
@@ -207,12 +222,13 @@
     for row in range(2 * n2):
         sums[row, :, : sizes.own[1] * LANES] = own1[2 * row] + own1[2 * row + 1]
     narrow(sizes, place, 1, sums, own2, 2 * n2, "own")
-    for message, low, at1, at0 in ((to_next, n1 - 2, n1 - 1, n0 - 1), (to_prev, 0, 0, 0)):
+    ends = []
+    for low, at1, at0 in ((n1 - 2, n1 - 1, n0 - 1), (0, 0, 0)):
         edge = n2 - 1 if at0 else 0
         rows = (own0[0, at0], own1[low], own1[low + 1], own1[n1 + at1])
-        rows += (own2[n2 - 2], own2[n2 - 1], own2[n2 + edge])
-        for slot, row in zip(sizes.slots, rows):
-            put(message, slot, row)
+        ends.append(rows + (own2[n2 - 2], own2[n2 - 1], own2[n2 + edge]))
+    for slot, next_row, prev_row in zip(sizes.slots, *ends):
+        put_pair(place, (first, second), slot, next_row, prev_row)
 
 
 def turn_kernel(sizes, place, right_side, own0, turned, *edges):
@@ -255,14 +271,14 @@
     return (lane < FRINGE) | (lane >= LANES - FRINGE)
 
 
-def put_fringes(sizes, message, rows):
+def fringes(sizes, rows):
     total = None
     for index, (level, row) in enumerate(rows):
         tile = row[:, sizes.own[level] * LANES :]
         tile = jnp.where(fringe_lanes(tile.shape), tile, 0.0)
         tile = roll(tile, SPREAD * index + SPREAD // 2, 1)
         total = tile if total is None else total + tile
-    message[sizes.tiles] = total
+    return total
 
 
 def fringed_row(sizes, level, index, message):
@@ -355,9 +371,11 @@
     s = sizes.sides
     owns, turned, refs = refs[:3], refs[3], refs[4:]
     borders0, refs = refs[:s], refs[s:]
-    from_prev, from_next, refs = refs[0], refs[1], refs[2:]
-    beside_prev, beside_next, refs = refs[: 2 * s : 2], refs[1 : 2 * s : 2], refs[2 * s :]
-    coefs, contribution, ups, fars, refs = refs[:3], refs[3], refs[4:6], refs[6:8], refs[8:]
+    pairs_of = [refs[2 * index : 2 * index + 2] for index in range(1 + s)]
+    refs = refs[2 * (1 + s) :]
+    from_prev, *beside_prev = (Arrived(place, pair, 0) for pair in pairs_of)
+    from_next, *beside_next = (Arrived(place, pair, 1) for pair in pairs_of)
+    coefs, contribution, with_far, ups, far, refs = refs[:3], refs[3], refs[4], refs[5:7], refs[7], refs[8:]
     border1, border2, level3, sums = refs
     slots = sizes.slots
     n0, n1, n2 = sizes.rows[:3]
@@ -431,19 +449,19 @@
     for at in (0, 1):
         sums[at, :, : sizes.held[2]] = held_row(2, at, 0) + held_row(2, at, 1)
     narrow(sizes, place, 2, sums.at[:, :, : sizes.held[2]], level3.at[3:5], 2)
+    tiles = packing(sizes, 5)[2]
     pack_rows(sizes, place, [level3[row] for row in range(5)], contribution)
+    with_far[0:tiles] = contribution[...]
     (s1, s2), (v1, v2) = sources, smooths
-    for at, rows in enumerate(
-        (
-            (v0[n0 - 1], s1[n1], s1[n1 + 1], v1[n1 - 1], s2[n2], s2[n2 + 1], v2[n2 - 1]),
-            (v0[0], s1[1], s1[0], v1[2], s2[1], s2[0], v2[2]),
-        )
-    ):
-        for slot, row in zip(slots, rows):
-            put(ups[at], slot, row)
-        if s:
-            put_fringes(sizes, ups[at], list(zip((1, 1, 1, 2, 2, 2), rows[1:])))
-        put(fars[at], (0, sizes.held[2] // LANES), v2[n2 + 1 if at == 0 else 0])
+    next_rows = (v0[n0 - 1], s1[n1], s1[n1 + 1], v1[n1 - 1], s2[n2], s2[n2 + 1], v2[n2 - 1])
+    prev_rows = (v0[0], s1[1], s1[0], v1[2], s2[1], s2[0], v2[2])
+    for slot, next_row, prev_row in zip(slots, next_rows, prev_rows):
+        put_pair(place, ups, slot, next_row, prev_row)
+    if s:
+        ends = [fringes(sizes, list(zip((1, 1, 1, 2, 2, 2), rows[1:]))) for rows in (next_rows, prev_rows)]
+        put_pair(place, ups, (sizes.tiles, 1), *ends)
+    far_tiles = sizes.held[2] // LANES
+    put_pair(place, (with_far.at[tiles : tiles + far_tiles], far), (0, far_tiles), v2[n2 + 1], v2[0], 2)
 
 
 def relax(count, field, refs_of, source, target):
@@ -531,7 +549,11 @@
 
 def up_kernel(sizes, place, coarse, *refs):
     s = sizes.sides
-    (from_prev, from_next), fars, coefs, (own0, turned) = refs[:2], refs[2:4], refs[4:7], refs[7:9]
+    pair, far_pair, coefs, (own0, turned) = refs[:2], refs[2:4], refs[4:7], refs[7:9]
+    from_prev, from_next = (Arrived(place, pair, forward) for forward in (0, 1))
+    tiles = packing(sizes, 5)[2]
+    far_pair = (far_pair[0].at[tiles : tiles + sizes.held[2] // LANES], far_pair[1])
+    fars = [Arrived(place, far_pair, forward, 2) for forward in (0, 1)]
     borders0, out, refs = refs[9 : 9 + s], refs[9 + s], refs[10 + s :]
     total1, total2, result = refs[:3]
     over2, over1, over0, lift2, lift1, lift0, it2, it1, it0, semaphores = refs[3:]
@@ -636,12 +658,21 @@
         stride *= radix
 
 
-def swap(value, stride, radix):
+def swap(value, stride, radix, others=None):
     count = lax.axis_size("span")
+    others = others or {}
     return [value] + [
-        lax.ppermute(value, "span", [(device, device ^ step * stride) for device in range(count)])
+        lax.ppermute(others.get(step, value), "span", [(device, device ^ step * stride) for device in range(count)])
         for step in range(1, radix)
     ]
+
+
+def exchange(pair, stride):
+    count = lax.axis_size("span")
+    routes = [[], []]
+    for low in range(count - stride):
+        routes[low // stride % 2] += [(low, low + stride), (low + stride, low)]
+    return [None if value is None else lax.ppermute(value, "span", route) for value, route in zip(pair, routes)]
 
 
 def on_device(right_side, diffusivity, reaction):
@@ -655,7 +686,7 @@
     held = [(depth, count) for count in sizes.held]
     down_message = (sizes.tiles, *tile)
     up_message = (sizes.tiles + 1, *tile)
-    own0, own1, own2, to_next, to_prev = call(
+    own0, own1, own2, *to_pairs = call(
         functools.partial(start_kernel, sizes),
         "start",
         1.1,
@@ -664,7 +695,7 @@
         place,
         [diffusivity, reaction],
     )
-    halos = [along(to_next, "span", 1), along(to_prev, "span", -1)]
+    halos = exchange(to_pairs, 1)
     turned, *edges = call(
         functools.partial(turn_kernel, sizes),
         "turn",
@@ -683,6 +714,7 @@
     plan = list(stages(sizes.span_count))
     sides = beside(halos, sizes)
 
+    part = packing(sizes, 5)[2]
     lengths = [sum(coefficient_rows(sizes, level)) for level in range(3)]
     far = (sizes.held[2] // LANES, *tile)
     coefs = [(lengths[level], *held[level]) for level in range(3)]
@@ -690,17 +722,21 @@
         functools.partial(down_kernel, sizes),
         "down",
         3.6,
-        [*coefs, (packing(sizes, 5)[2], *tile), up_message, up_message, far, far],
+        [*coefs, (part, *tile), (part + far[0], *tile), up_message, up_message, far],
         [(2 * n1, *tile), (2 * n2, *tile), (5, *tile), (max(2 * n1, n1 + 2), *held[0])],
         place,
         [own0, own1, own2, turned, *borders, *halos, *sum(sides, [])],
     )
-    coefs_out, blocks, ups, fars = downs[:3], downs[3], downs[4:6], downs[6:8]
-    far_rows = [along(fars[0], "span", 2), along(fars[1], "span", -2)]
+    coefs_out, blocks, with_far, ups, far_second = downs[:3], downs[3], downs[4], downs[5:7], downs[7]
+    far_rows = None
     for stride, radix in plan[:-1]:
         count = stride * radix
-        blocks = swap(blocks, stride, radix)
-        blocks, far_rows = lax.optimization_barrier((blocks, far_rows))
+        if far_rows is None:
+            blocks = swap(blocks, stride, radix, {2: with_far})
+            far_rows = [blocks[2], exchange([None, far_second], 2)[1]]
+            blocks, far_rows = lax.optimization_barrier((blocks, far_rows))
+        else:
+            blocks = swap(blocks, stride, radix)
         (blocks,) = call(
             functools.partial(merge_kernel, sizes, stride, radix),
             "merge",
@@ -712,8 +748,7 @@
         )
     stride, radix = plan[-1]
     blocks = swap(blocks, stride, radix)
-    received = [along(ups[0], "span", 1), along(ups[1], "span", -1)]
-    received += far_rows
+    received = exchange(ups, 1) + far_rows
     scratch = [(sizes.span_count + 2, *tile), (max(sizes.span_count // 2, 2), *tile)]
     for index in range(3):
         count = sizes.span_count >> index

time: 60.3 us -> 55.3 us (0.917); the launches traced: 59.2 us -> 55 us
  starting transfers between devices: 22.5 us -> 19 us
  waiting for transfers between devices: 22 us -> 21.3 us
    ppermute x12 -> x11, starting transfers between devices: 22.4 us -> 18.4 us  [the longest x6 11.4 us: swap(): lax.ppermute(others.get(step, value), 'span', [(device, device ^ step * s...]
    ppermute x12 -> x11, waiting for transfers between devices: 20.5 us -> 20.1 us  [the longest x6 12.4 us: swap(): lax.ppermute(others.get(step, value), 'span', [(device, device ^ step * s...]
  transfers between devices with their start and end apart: 15 -> 14, of which waited for: 6 -> 7; matrix products, arithmetic and copies ran while one was open for 0% -> 0% of each run, Pallas kernels for 6% -> 7%
where the time goes in v8:
time: 55.3 us; the launch traced here: 55 us
  waiting for transfers between devices  21.3 us (39%)
  starting transfers between devices  19 us (34%)
  Pallas kernels  12.5 us (23%)
  local copies, waits for them, and re-layouts  2.09 us (4%)
    pallas_call x6, Pallas kernels, call(): pl.pallas_call(body, name=name, out_shape=[jax.ShapeDtypeStruct(shape, f3...  12.5 us
    ppermute x6, waiting for transfers between devices, swap(): lax.ppermute(others.get(step, value), 'span', [(device, device ^ step * s...  12.4 us
    ppermute x6, starting transfers between devices, swap(): lax.ppermute(others.get(step, value), 'span', [(device, device ^ step * s...  11.4 us
    ppermute x5, waiting for transfers between devices, exchange(): lax.ppermute(value, 'span', route)  7.68 us
    ppermute x5, starting transfers between devices, exchange(): lax.ppermute(value, 'span', route)  6.99 us
    unnamed x6, local copies, waits for them, and re-layouts  2.09 us
    ppermute x2, waiting for transfers between devices, beside(): lax.ppermute(value, 'width', [(0, 1), (1, 0)])  1.25 us
  transfers between devices with their start and end apart: 14, of which 7 were waited for; matrix products, arithmetic and copies ran while one was open for 0% of the time, Pallas kernels for 7%

profile of v8, /device:TPU:0, one launch (start us, length us, event | category | flops | bytes accessed | tf_op | source)
XLA Modules:
  0.0 55.0 jit_solution(5453555587174952)
XLA Ops:
  0.1 1.0 %copy-done = f32[32,8,512]{2,1,0:T(8,128)S(1)} copy-done((f32[32,8,512]{2,1,0:T(8,128)S(1)}, f32[32,8,512]{2,1,0:T(8,128)}, u32[]{:S(2)}) %copy-start) | copy-done | bytes 524312
  1.1 1.0 %copy-done.1 = f32[32,8,512]{2,1,0:T(8,128)S(1)} copy-done((f32[32,8,512]{2,1,0:T(8,128)S(1)}, f32[32,8,512]{2,1,0:T(8,128)}, u32[]{:S(2)}) %copy-start.1) | copy-done | bytes 524312
  2.2 1.1 %start.1 = (f32[2,8,32,512]{3,2,1,0:T(8,128)S(1)}, f32[8,32,256]{2,1,0:T(8,128)S(1)}, f32[4,32,128]{2,1,0:T(8,128)S(1)}, f32[13,32,128]{2,1,0:T(8,128)S(1)}, f32[13,32,128]{2,1,0:T(8,128)S(1)}) custom-call(s32[2]{0:T(128)S(1)} %pad_add_fusion.place, f32[32,8,512]{2,1,0:T(8,128)S(1)} %copy-done, f32[32,8,512]{2,1,0:T(8,128)S(1)} %copy-done.1), custom_call_target="tpu_custom_call" | custom-call | flops 1264999936 | bytes 4059000 | tf_op jit(solution)/shard_map/start/pallas_call | solution.py:627
  3.3 3.0 %collective-permute-start.1 = (f32[13,32,128]{2,1,0:T(8,128)S(1)}, f32[13,32,128]{2,1,0:T(8,128)S(1)}, u32[]{:S(2)}, u32[]{:S(2)}) collective-permute-start(f32[13,32,128]{2,1,0:T(8,128)S(1)} %get-tuple-element.31), channel_id=1, source_target_pairs={{0,2},{2,0},{4,6},{6,4},{8,10},{10,8},{12,14},{14,12},{16,18},{18,... | collective-permute-start | bytes 638984 | tf_op jit(solution)/shard_map/ppermute | solution.py:675
  6.3 0.7 %collective-permute-start.2 = (f32[13,32,128]{2,1,0:T(8,128)S(1)}, f32[13,32,128]{2,1,0:T(8,128)S(1)}, u32[]{:S(2)}, u32[]{:S(2)}) collective-permute-start(f32[13,32,128]{2,1,0:T(8,128)S(1)} %get-tuple-element.32), channel_id=1, source_target_pairs={{2,4},{4,2},{6,8},{8,6},{10,12},{12,10},{14,16},{16,14},{18,20},{2... | collective-permute-start | bytes 638984 | tf_op jit(solution)/shard_map/ppermute | solution.py:675
  7.0 0.7 %turn.1 = (f32[8,32,512]{2,1,0:T(8,128)S(1)}, f32[3,8,32,128]{3,2,1,0:T(8,128)S(1)}) custom-call(s32[2]{0:T(128)S(1)} %pad_add_fusion.place, f32[32,8,512]{2,1,0:T(8,128)S(1)} %copy-done.2, f32[2,8,32,512]{3,2,1,0:T(8,128)S(1)} %get-tuple-element.26.own0.refs_0_.refs_7_), custom_call_target="tpu_custom_call" | custom-call | flops 805000000 | bytes 2583000 | tf_op jit(solution)/shard_map/turn/pallas_call | solution.py:627
  7.7 7.7 %collective-permute-done.1.refs_5_ = f32[13,32,128]{2,1,0:T(8,128)S(1)} collective-permute-done((f32[13,32,128]{2,1,0:T(8,128)S(1)}, f32[13,32,128]{2,1,0:T(8,128)S(1)}, u32[]{:S(2)}, u32[]{:S(2)}) %collective-permute-start.1) | collective-permute-done | bytes 213024 | tf_op jit(solution)/shard_map/ppermute | solution.py:675
  15.4 0.5 collective-permute-start.4
  15.9 0.9 %collective-permute-done.3.refs_7_ = f32[13,32,128]{2,1,0:T(8,128)S(1)} collective-permute-done((f32[13,32,128]{2,1,0:T(8,128)S(1)}, f32[13,32,128]{2,1,0:T(8,128)S(1)}, u32[]{:S(2)}, u32[]{:S(2)}) %collective-permute-start.3) | collective-permute-done | bytes 213024 | tf_op jit(solution)/shard_map/ppermute | solution.py:647
  17.2 3.8 %down.1 = (f32[41,32,640]{2,1,0:T(8,128)S(1)}, f32[43,32,384]{2,1,0:T(8,128)S(1)}, f32[29,32,256]{2,1,0:T(8,128)S(1)}, f32[4,32,128]{2,1,0:T(8,128)S(1)}, f32[6,...) custom-call(s32[2]{0:T(128)S(1)} %pad_add_fusion.place, ...), custom_call_target="tpu_custom_call" | custom-call | flops 4140000000 | bytes 13284000 | tf_op jit(solution)/shard_map/down/pallas_call | solution.py:627
  21.0 1.9 %collective-permute-start.6 = (f32[6,32,128]{2,1,0:T(8,128)S(1)}, f32[6,32,128]{2,1,0:T(8,128)S(1)}, u32[]{:S(2)}, u32[]{:S(2)}) collective-permute-start(f32[6,32,128]{2,1,0:T(8,128)S(1)} %get-tuple-element.34), channel_id=1, source_target_pairs={{0,4},{2,6},{4,0},{6,2},{8,12},{10,14},{12,8},{14,10},{16,20},{18,... | collective-permute-start | bytes 294920 | tf_op jit(solution)/shard_map/ppermute | solution.py:665
  22.9 2.7 %collective-permute-start.7 = (f32[4,32,128]{2,1,0:T(8,128)S(1)}, f32[4,32,128]{2,1,0:T(8,128)S(1)}, u32[]{:S(2)}, u32[]{:S(2)}) collective-permute-start(f32[4,32,128]{2,1,0:T(8,128)S(1)} %get-tuple-element.36.refs_0_), channel_id=1, source_target_pairs={{0,6},{2,4},{4,2},{6,0},{8,14},{10,12},{12,10},{14,8},{16,22},{18,... | collective-permute-start | bytes 196616 | tf_op jit(solution)/shard_map/ppermute | solution.py:665
  25.6 0.7 %collective-permute-start.8 = (f32[2,32,128]{2,1,0:T(8,128)S(1)}, f32[2,32,128]{2,1,0:T(8,128)S(1)}, u32[]{:S(2)}, u32[]{:S(2)}) collective-permute-start(f32[2,32,128]{2,1,0:T(8,128)S(1)} %get-tuple-element.35), channel_id=1, source_target_pairs={{4,8},{8,4},{6,10},{10,6},{12,16},{16,12},{14,18},{18,14},{20,24},... | collective-permute-start | bytes 98312 | tf_op jit(solution)/shard_map/ppermute | solution.py:675
  26.3 2.3 %collective-permute-done.7.refs_3_ = f32[4,32,128]{2,1,0:T(8,128)S(1)} collective-permute-done((f32[4,32,128]{2,1,0:T(8,128)S(1)}, f32[4,32,128]{2,1,0:T(8,128)S(1)}, u32[]{:S(2)}, u32[]{:S(2)}) %collective-permute-start.7) | collective-permute-done | bytes 65568 | tf_op jit(solution)/shard_map/ppermute | solution.py:665
  28.6 1.3 %collective-permute-done.5.refs_1_ = f32[4,32,128]{2,1,0:T(8,128)S(1)} collective-permute-done((f32[4,32,128]{2,1,0:T(8,128)S(1)}, f32[4,32,128]{2,1,0:T(8,128)S(1)}, u32[]{:S(2)}, u32[]{:S(2)}) %collective-permute-start.5) | collective-permute-done | bytes 65568 | tf_op jit(solution)/shard_map/ppermute | solution.py:665
  29.9 0.9 %merge.1.refs_0_ = f32[9,32,128]{2,1,0:T(8,128)S(1)} custom-call(s32[2]{0:T(128)S(1)} %pad_add_fusion.place, f32[4,32,128]{2,1,0:T(8,128)S(1)} %get-tuple-element.36.refs_0_, f32[4,32,128]{2,1,0:T(8,128)S(1)} %collective-permute-done.5.refs_1_, f32[6,32,128]{2,1,0:T(8,128)S(1)} %collective-permute-done.6.refs_2_, ...), custom_call_target="tpu_custom_call" | custom-call | flops 1035000000 | bytes 3321000 | tf_op jit(solution)/shard_map/merge/pallas_call | solution.py:627
  30.7 6.1 %collective-permute-start.11 = (f32[9,32,128]{2,1,0:T(8,128)S(1)}, f32[9,32,128]{2,1,0:T(8,128)S(1)}, u32[]{:S(2)}, u32[]{:S(2)}) collective-permute-start(f32[9,32,128]{2,1,0:T(8,128)S(1)} %merge.1.refs_0_), channel_id=1, source_target_pairs={{0,24},{2,26},{4,28},{6,30},{8,16},{10,18},{12,20},{14,22},{16,8},... | collective-permute-start | bytes 442376 | tf_op jit(solution)/shard_map/ppermute | solution.py:665
  36.9 0.6 %collective-permute-start.9 = (f32[9,32,128]{2,1,0:T(8,128)S(1)}, f32[9,32,128]{2,1,0:T(8,128)S(1)}, u32[]{:S(2)}, u32[]{:S(2)}) collective-permute-start(f32[9,32,128]{2,1,0:T(8,128)S(1)} %merge.1.refs_0_), channel_id=1, source_target_pairs={{0,8},{2,10},{4,12},{6,14},{8,0},{10,2},{12,4},{14,6},{16,24},{18,... | collective-permute-start | bytes 442376 | tf_op jit(solution)/shard_map/ppermute | solution.py:665
  37.5 2.0 %collective-permute-start.12 = (f32[14,32,128]{2,1,0:T(8,128)S(1)}, f32[14,32,128]{2,1,0:T(8,128)S(1)}, u32[]{:S(2)}, u32[]{:S(2)}) collective-permute-start(f32[14,32,128]{2,1,0:T(8,128)S(1)} %get-tuple-element.40), channel_id=1, source_target_pairs={{0,2},{2,0},{4,6},{6,4},{8,10},{10,8},{12,14},{14,12},{16,18},{18,... | collective-permute-start | bytes 688136 | tf_op jit(solution)/shard_map/ppermute | solution.py:675
  39.5 0.7 %collective-permute-start.13 = (f32[14,32,128]{2,1,0:T(8,128)S(1)}, f32[14,32,128]{2,1,0:T(8,128)S(1)}, u32[]{:S(2)}, u32[]{:S(2)}) collective-permute-start(f32[14,32,128]{2,1,0:T(8,128)S(1)} %get-tuple-element.41), channel_id=1, source_target_pairs={{2,4},{4,2},{6,8},{8,6},{10,12},{12,10},{14,16},{16,14},{18,20},{2... | collective-permute-start | bytes 688136 | tf_op jit(solution)/shard_map/ppermute | solution.py:675
  40.2 1.4 %collective-permute-done.11.refs_3_ = f32[9,32,128]{2,1,0:T(8,128)S(1)} collective-permute-done((f32[9,32,128]{2,1,0:T(8,128)S(1)}, f32[9,32,128]{2,1,0:T(8,128)S(1)}, u32[]{:S(2)}, u32[]{:S(2)}) %collective-permute-start.11) | collective-permute-done | bytes 147488 | tf_op jit(solution)/shard_map/ppermute | solution.py:665
  41.6 7.4 %collective-permute-done.10.refs_2_ = f32[9,32,128]{2,1,0:T(8,128)S(1)} collective-permute-done((f32[9,32,128]{2,1,0:T(8,128)S(1)}, f32[9,32,128]{2,1,0:T(8,128)S(1)}, u32[]{:S(2)}, u32[]{:S(2)}) %collective-permute-start.10) | collective-permute-done | bytes 147488 | tf_op jit(solution)/shard_map/ppermute | solution.py:665
  49.0 2.9 %coarse.1 = f32[3,32,128]{2,1,0:T(8,128)S(1)} custom-call(s32[2]{0:T(128)S(1)} %pad_add_fusion.place, f32[9,32,128]{2,1,0:T(8,128)S(1)} %merge.1.refs_0_, f32[9,32,128]{2,1,0:T(8,128)S(1)} %collective-permute-done.9.refs_1_, f32[9,32,128]{2,1,0:T(8,128)S(1)} %collective-permute-done.10.refs_2_, f32[9,32,128]{2,1,0:T(8,128)S(1)} %collective-permute-done.11.refs_3_), custom_call_target="tpu_custom_call" | custom-call | flops 3335000064 | bytes 10701000 | tf_op jit(solution)/shard_map/coarse/pallas_call | solution.py:627
  51.9 3.1 %up.1 = f32[32,8,512]{2,1,0:T(8,128)} custom-call(s32[2]{0:T(128)S(1)} %pad_add_fusion.place, f32[3,32,128]{2,1,0:T(8,128)S(1)} %coarse.1, f32[14,32,128]{2,1,0:T(8,128)S(1)} %collective-permute-done.12.refs_0_, f32[14,32,128]{2,1,0:T(8,128)S(1)} %collective-permute-done.13.refs_1_, f32[6,32,128]{2,1,0:T(8,128)S(1)} %collective-permute-done.6.refs_2_, ...), custom_call_target="tpu_custom_call" | custom-call | flops 3449999872 | bytes 11070000 | tf_op jit(solution)/shard_map/up/pallas_call | solution.py:627
  (17 shorter events, 0.5 us)
Async XLA Ops:
  0.1 1.0 %copy-start = (f32[32,8,512]{2,1,0:T(8,128)S(1)}, f32[32,8,512]{2,1,0:T(8,128)}, u32[]{:S(2)}) copy-start(f32[32,8,512]{2,1,0:T(8,128)} %conduct.1) | copy-start | bytes 1572868
  1.1 1.0 %copy-start.1 = (f32[32,8,512]{2,1,0:T(8,128)S(1)}, f32[32,8,512]{2,1,0:T(8,128)}, u32[]{:S(2)}) copy-start(f32[32,8,512]{2,1,0:T(8,128)} %binding.1) | copy-start | bytes 1572868
  2.2 4.8 %copy-start.2 = (f32[32,8,512]{2,1,0:T(8,128)S(1)}, f32[32,8,512]{2,1,0:T(8,128)}, u32[]{:S(2)}) copy-start(f32[32,8,512]{2,1,0:T(8,128)} %right_side.1) | copy-start | bytes 1572868
  3.3 12.1 %collective-permute-start.1 = (f32[13,32,128]{2,1,0:T(8,128)S(1)}, f32[13,32,128]{2,1,0:T(8,128)S(1)}, u32[]{:S(2)}, u32[]{:S(2)}) collective-permute-start(f32[13,32,128]{2,1,0:T(8,128)S(1)} %get-tuple-element.31), channel_id=1, source_target_pairs={{0,2},{2,0},{4,6},{6,4},{8,10},{10,8},{12,14},{14,12},{16,18},{18,... | collective-permute-start | bytes 638984 | tf_op jit(solution)/shard_map/ppermute | solution.py:675
  6.3 9.1 %collective-permute-start.2 = (f32[13,32,128]{2,1,0:T(8,128)S(1)}, f32[13,32,128]{2,1,0:T(8,128)S(1)}, u32[]{:S(2)}, u32[]{:S(2)}) collective-permute-start(f32[13,32,128]{2,1,0:T(8,128)S(1)} %get-tuple-element.32), channel_id=1, source_target_pairs={{2,4},{4,2},{6,8},{8,6},{10,12},{12,10},{14,16},{16,14},{18,20},{2... | collective-permute-start | bytes 638984 | tf_op jit(solution)/shard_map/ppermute | solution.py:675
  7.6 8.3 %collective-permute-start = (f32[3,8,32,128]{3,2,1,0:T(8,128)S(1)}, f32[3,8,32,128]{3,2,1,0:T(8,128)S(1)}, u32[]{:S(2)}, u32[]{:S(2)}) collective-permute-start(f32[3,8,32,128]{3,2,1,0:T(8,128)S(1)} %get-tuple-element.30), channel_id=1, source_target_pairs={{0,1},{1,0},{2,3},{3,2},{4,5},{5,4},{6,7},{7,6},{8,9},{9,8},{10,11... | collective-permute-start | bytes 1179656 | tf_op jit(solution)/shard_map/ppermute | solution.py:709
  15.4 1.5 %collective-permute-start.3 = (f32[13,32,128]{2,1,0:T(8,128)S(1)}, f32[13,32,128]{2,1,0:T(8,128)S(1)}, u32[]{:S(2)}, u32[]{:S(2)}) collective-permute-start(f32[13,32,128]{2,1,0:T(8,128)S(1)} %collective-permute-done.1.refs_5_), channel_id=1, source_target_pairs={{0,1},{1,0},{2,3},{3,2},{4,5},{5,4},{6,7},{7,6},{8,9},{9,8},{10,11... | collective-permute-start | bytes 638984 | tf_op jit(solution)/shard_map/ppermute | solution.py:647
  15.4 1.8 %collective-permute-start.4 = (f32[13,32,128]{2,1,0:T(8,128)S(1)}, f32[13,32,128]{2,1,0:T(8,128)S(1)}, u32[]{:S(2)}, u32[]{:S(2)}) collective-permute-start(f32[13,32,128]{2,1,0:T(8,128)S(1)} %collective-permute-done.2.refs_6_), channel_id=1, source_target_pairs={{0,1},{1,0},{2,3},{3,2},{4,5},{5,4},{6,7},{7,6},{8,9},{9,8},{10,11... | collective-permute-start | bytes 638984 | tf_op jit(solution)/shard_map/ppermute | solution.py:647
  21.0 8.9 %collective-permute-start.6 = (f32[6,32,128]{2,1,0:T(8,128)S(1)}, f32[6,32,128]{2,1,0:T(8,128)S(1)}, u32[]{:S(2)}, u32[]{:S(2)}) collective-permute-start(f32[6,32,128]{2,1,0:T(8,128)S(1)} %get-tuple-element.34), channel_id=1, source_target_pairs={{0,4},{2,6},{4,0},{6,2},{8,12},{10,14},{12,8},{14,10},{16,20},{18,... | collective-permute-start | bytes 294920 | tf_op jit(solution)/shard_map/ppermute | solution.py:665
  22.9 5.7 %collective-permute-start.7 = (f32[4,32,128]{2,1,0:T(8,128)S(1)}, f32[4,32,128]{2,1,0:T(8,128)S(1)}, u32[]{:S(2)}, u32[]{:S(2)}) collective-permute-start(f32[4,32,128]{2,1,0:T(8,128)S(1)} %get-tuple-element.36.refs_0_), channel_id=1, source_target_pairs={{0,6},{2,4},{4,2},{6,0},{8,14},{10,12},{12,10},{14,8},{16,22},{18,... | collective-permute-start | bytes 196616 | tf_op jit(solution)/shard_map/ppermute | solution.py:665
  25.6 4.3 %collective-permute-start.5 = (f32[4,32,128]{2,1,0:T(8,128)S(1)}, f32[4,32,128]{2,1,0:T(8,128)S(1)}, u32[]{:S(2)}, u32[]{:S(2)}) collective-permute-start(f32[4,32,128]{2,1,0:T(8,128)S(1)} %get-tuple-element.36.refs_0_), channel_id=1, source_target_pairs={{0,2},{2,0},{4,6},{6,4},{8,10},{10,8},{12,14},{14,12},{16,18},{18,... | collective-permute-start | bytes 196616 | tf_op jit(solution)/shard_map/ppermute | solution.py:665
  25.6 0.7 %collective-permute-start.8 = (f32[2,32,128]{2,1,0:T(8,128)S(1)}, f32[2,32,128]{2,1,0:T(8,128)S(1)}, u32[]{:S(2)}, u32[]{:S(2)}) collective-permute-start(f32[2,32,128]{2,1,0:T(8,128)S(1)} %get-tuple-element.35), channel_id=1, source_target_pairs={{4,8},{8,4},{6,10},{10,6},{12,16},{16,12},{14,18},{18,14},{20,24},... | collective-permute-start | bytes 98312 | tf_op jit(solution)/shard_map/ppermute | solution.py:675
  30.7 10.9 %collective-permute-start.11 = (f32[9,32,128]{2,1,0:T(8,128)S(1)}, f32[9,32,128]{2,1,0:T(8,128)S(1)}, u32[]{:S(2)}, u32[]{:S(2)}) collective-permute-start(f32[9,32,128]{2,1,0:T(8,128)S(1)} %merge.1.refs_0_), channel_id=1, source_target_pairs={{0,24},{2,26},{4,28},{6,30},{8,16},{10,18},{12,20},{14,22},{16,8},... | collective-permute-start | bytes 442376 | tf_op jit(solution)/shard_map/ppermute | solution.py:665
  36.9 12.1 %collective-permute-start.10 = (f32[9,32,128]{2,1,0:T(8,128)S(1)}, f32[9,32,128]{2,1,0:T(8,128)S(1)}, u32[]{:S(2)}, u32[]{:S(2)}) collective-permute-start(f32[9,32,128]{2,1,0:T(8,128)S(1)} %merge.1.refs_0_), channel_id=1, source_target_pairs={{0,16},{2,18},{4,20},{6,22},{8,24},{10,26},{12,28},{14,30},{16,0},... | collective-permute-start | bytes 442376 | tf_op jit(solution)/shard_map/ppermute | solution.py:665
  36.9 12.1 %collective-permute-start.9 = (f32[9,32,128]{2,1,0:T(8,128)S(1)}, f32[9,32,128]{2,1,0:T(8,128)S(1)}, u32[]{:S(2)}, u32[]{:S(2)}) collective-permute-start(f32[9,32,128]{2,1,0:T(8,128)S(1)} %merge.1.refs_0_), channel_id=1, source_target_pairs={{0,8},{2,10},{4,12},{6,14},{8,0},{10,2},{12,4},{14,6},{16,24},{18,... | collective-permute-start | bytes 442376 | tf_op jit(solution)/shard_map/ppermute | solution.py:665
  37.5 14.4 %collective-permute-start.12 = (f32[14,32,128]{2,1,0:T(8,128)S(1)}, f32[14,32,128]{2,1,0:T(8,128)S(1)}, u32[]{:S(2)}, u32[]{:S(2)}) collective-permute-start(f32[14,32,128]{2,1,0:T(8,128)S(1)} %get-tuple-element.40), channel_id=1, source_target_pairs={{0,2},{2,0},{4,6},{6,4},{8,10},{10,8},{12,14},{14,12},{16,18},{18,... | collective-permute-start | bytes 688136 | tf_op jit(solution)/shard_map/ppermute | solution.py:675
  39.5 12.4 %collective-permute-start.13 = (f32[14,32,128]{2,1,0:T(8,128)S(1)}, f32[14,32,128]{2,1,0:T(8,128)S(1)}, u32[]{:S(2)}, u32[]{:S(2)}) collective-permute-start(f32[14,32,128]{2,1,0:T(8,128)S(1)} %get-tuple-element.41), channel_id=1, source_target_pairs={{2,4},{4,2},{6,8},{8,6},{10,12},{12,10},{14,16},{16,14},{18,20},{2... | collective-permute-start | bytes 688136 | tf_op jit(solution)/shard_map/ppermute | solution.py:675

commit v9 on v8

--- a/solution.py
+++ b/solution.py
@@ -35,6 +35,7 @@
             self.slots.append((start, self.own[level]))
             start += self.own[level]
         self.tiles = start
+        self.last = list(stages(span_count))[-1][1]
 
 
 def put(message, slot, row):
@@ -211,7 +212,8 @@
     return [n + 3] + [n + 2] * 6
 
 
-def start_kernel(sizes, place, conduct, binding, own0, own1, own2, first, second, sums):
+def start_kernel(sizes, place, conduct, binding, own0, own1, own2, first, second, *refs):
+    edges, sums = refs[: sizes.sides], refs[-1]
     n0, n1, n2 = sizes.rows[:3]
     for at, array in enumerate((conduct, binding)):
         own0[at] = jnp.swapaxes(array[...], 0, 1)
@@ -229,18 +231,23 @@
         ends.append(rows + (own2[n2 - 2], own2[n2 - 1], own2[n2 + edge]))
     for slot, next_row, prev_row in zip(sizes.slots, *ends):
         put_pair(place, (first, second), slot, next_row, prev_row)
-
-
-def turn_kernel(sizes, place, right_side, own0, turned, *edges):
+    for at in (0, 1):
+        cut_edges(sizes, place, own0.at[at], [edge.at[at] for edge in edges])
+
+
+def cut_edges(sizes, place, array, edges):
+    last = sizes.extent_y - BORDER
+    if sizes.sides == 1:
+        at = pl.multiple_of(jnp.where(place[1] == 0, last, 0), LANES)
+        edges[0][...] = array[:, :, pl.ds(at, BORDER)]
+    elif sizes.sides == 2:
+        edges[0][...] = array[:, :, last:]
+        edges[1][...] = array[:, :, :BORDER]
+
+
+def turn_kernel(sizes, place, right_side, turned, *edges):
     turned[...] = jnp.swapaxes(right_side[...], 0, 1)
-    last = sizes.extent_y - BORDER
-    for index, array in enumerate((own0.at[0], own0.at[1], turned)):
-        if sizes.sides == 1:
-            at = pl.multiple_of(jnp.where(place[1] == 0, last, 0), LANES)
-            edges[0][index] = array[:, :, pl.ds(at, BORDER)]
-        elif sizes.sides == 2:
-            edges[0][index] = array[:, :, last:]
-            edges[1][index] = array[:, :, :BORDER]
+    cut_edges(sizes, place, turned, edges)
 
 
 def message_row(sizes, place, level, slot, message, beside):
@@ -294,9 +301,14 @@
 
 def packing(sizes, count):
     if sizes.sides != 1:
-        return False, count, count
+        return False, count, None
+    half, reach = LANES // 2, BORDER >> 3
     own = -(-count // 2)
-    return True, own, own - (-count * (BORDER >> 3) // LANES)
+    free = [(own - 1, column) for column in range(half, LANES, reach)] if count % 2 else []
+    while len(free) < count:
+        free += [(own, column) for column in range(0, LANES, reach)]
+        own += 1
+    return True, own, free[:count]
 
 
 def border_turn(place, goal):
@@ -304,82 +316,73 @@
 
 
 def pack_rows(sizes, place, rows, target):
-    packed, own, tiles = packing(sizes, len(rows))
+    packed, tiles, borders = packing(sizes, len(rows))
     if not packed:
         for index, row in enumerate(rows):
             target[index] = row
         return
     half, reach = LANES // 2, BORDER >> 3
     lane = lane_at(rows[0].shape)
-    for index in range(own):
-        held = rows[2 * index]
-        other = rows[2 * index + 1] if 2 * index + 1 < len(rows) else jnp.zeros(held.shape, f32)
-        target[index] = jnp.where(lane < half, held, pltpu.roll(other, half, axis=1))
-    for index in range(own, tiles):
+    for index in range(tiles):
         held = jnp.zeros(rows[0].shape, f32)
-        some = rows[(index - own) * (LANES // reach) :][: LANES // reach]
-        for place_at, row in enumerate(some):
-            goal = place_at * reach
-            moved = pltpu.roll(row, border_turn(place, goal), axis=1)
-            held = jnp.where((lane >= goal) & (lane < goal + reach), moved, held)
+        if 2 * index < len(rows):
+            held = jnp.where(lane < half, rows[2 * index], 0.0)
+        if 2 * index + 1 < len(rows):
+            held = jnp.where(lane < half, held, pltpu.roll(rows[2 * index + 1], half, axis=1))
+        for row, (tile, goal) in zip(rows, borders):
+            if tile == index:
+                moved = pltpu.roll(row, border_turn(place, goal), axis=1)
+                held = jnp.where((lane >= goal) & (lane < goal + reach), moved, held)
         target[index] = held
 
 
 def unpack_rows(sizes, place, blocks, count):
-    packed, own, _ = packing(sizes, count)
+    packed, _, borders = packing(sizes, count)
     if not packed:
         return [blocks[index] for index in range(count)]
     half, reach = LANES // 2, BORDER >> 3
     rows = []
-    for index in range(count):
+    for index, (tile, goal) in enumerate(borders):
         held = blocks[index // 2]
         lane = lane_at(held.shape)
         if index % 2:
             held = pltpu.roll(held, half, axis=1)
-        at, goal = index // (LANES // reach), index % (LANES // reach) * reach
         back = lax.rem(LANES - border_turn(place, goal), LANES)
-        beside = pltpu.roll(blocks[own + at], back, axis=1)
+        beside = pltpu.roll(blocks[tile], back, axis=1)
         start = jnp.where(place[1] == 0, half, LANES - reach)
         here = (lane >= start) & (lane < start + reach)
         rows.append(jnp.where(lane < half, held, jnp.where(here, beside, 0.0)))
     return rows
 
 
-def merge_into(sizes, place, stride, radix, arrays, source, conduct, binding, first):
+def merge_into(sizes, place, stride, radix, arrays, source, tops=None):
     position = (place[0] // stride) % radix
     source[...] = jnp.zeros(source.shape, f32)
+    kinds = 0 if tops is None else tops.shape[0]
     for step, array in enumerate(arrays):
         at = (position ^ step) * stride
-        rows = unpack_rows(sizes, place, array, 3 * stride + 2)
+        rows = unpack_rows(sizes, place, array, stride + 2 + kinds * stride)
         for index, row in enumerate(rows[: stride + 2]):
             source[at + index] = source[at + index] + row
-        for index in range(stride):
-            conduct[at + index + first] = rows[stride + 2 + index]
-            binding[at + index] = rows[2 * stride + 2 + index]
-
-
-def merge_kernel(sizes, stride, radix, place, *refs):
-    arrays, out, (source, conduct, binding) = refs[:radix], refs[radix], refs[radix + 1 :]
-    merge_into(sizes, place, stride, radix, arrays, source, conduct, binding, 0)
+        for kind in range(kinds):
+            for index in range(stride):
+                tops[kind, at + index] = rows[stride + 2 + kind * stride + index]
+
+
+def merge_kernel(sizes, stride, radix, final, place, *refs):
+    arrays, out, tops, source = refs[:radix], refs[radix], refs[radix + 1], refs[radix + 2]
+    merge_into(sizes, place, stride, radix, arrays, source, tops)
     count = stride * radix
     rows = [source[row] for row in range(count + 2)]
-    rows += [conduct[row] for row in range(count)] + [binding[row] for row in range(count)]
+    if not final:
+        rows += [tops[kind, row] for kind in range(tops.shape[0]) for row in range(count)]
     pack_rows(sizes, place, rows, out)
 
 
-def down_kernel(sizes, place, *refs):
+def top_kernel(sizes, place, own2, *refs):
     s = sizes.sides
-    owns, turned, refs = refs[:3], refs[3], refs[4:]
-    borders0, refs = refs[:s], refs[s:]
-    pairs_of = [refs[2 * index : 2 * index + 2] for index in range(1 + s)]
-    refs = refs[2 * (1 + s) :]
-    from_prev, *beside_prev = (Arrived(place, pair, 0) for pair in pairs_of)
-    from_next, *beside_next = (Arrived(place, pair, 1) for pair in pairs_of)
-    coefs, contribution, with_far, ups, far, refs = refs[:3], refs[3], refs[4], refs[5:7], refs[7], refs[8:]
-    border1, border2, level3, sums = refs
-    slots = sizes.slots
-    n0, n1, n2 = sizes.rows[:3]
-
+    borders0, (border1, border2, top, sums) = refs[:s], refs[s:]
+    n1, n2 = sizes.rows[1:3]
     if s:
         for row in range(2 * n1):
             for side in range(s):
@@ -390,10 +393,35 @@
         for row in range(2 * n2):
             sums[row, :, :LANES] = border1[2 * row] + border1[2 * row + 1]
         narrow(sizes, place, 1, sums, border2, 2 * n2, "border", sizes.own[1] * LANES)
+    for at in (0, 1):
+        row = at * n2
+        sums[at, :, :LANES] = own2[row] + own2[row + 1]
+        if s:
+            sums[at, :, LANES : 2 * LANES] = border2[row] + border2[row + 1]
+    narrow(sizes, place, 2, sums, top, 2)
+
+
+def down_kernel(sizes, place, *refs):
+    s = sizes.sides
+    owns, turned, refs = refs[:3], refs[3], refs[4:]
+    borders0, borders_r, refs = refs[:s], refs[s : 2 * s], refs[2 * s :]
+    pairs_of = [refs[2 * index : 2 * index + 2] for index in range(1 + s)]
+    refs = refs[2 * (1 + s) :]
+    from_prev, *beside_prev = (Arrived(place, pair, 0) for pair in pairs_of)
+    from_next, *beside_next = (Arrived(place, pair, 1) for pair in pairs_of)
+    (border1, border2), refs = refs[:2], refs[2:]
+    tops, refs = refs[: sizes.last], refs[sizes.last :]
+    coefs, contribution, with_far, ups, far, refs = refs[:3], refs[3], refs[4], refs[5:7], refs[7], refs[8:]
+    level3, sums = refs
+    slots = sizes.slots
+    n0, n1, n2 = sizes.rows[:3]
 
     def held_row(level, at, row):
         if level == 0:
-            tiles = [turned[row] if at == 2 else owns[0][at, row], *(array[at, row] for array in borders0)]
+            if at == 2:
+                tiles = [turned[row], *(array[row] for array in borders_r)]
+            else:
+                tiles = [owns[0][at, row], *(array[at, row] for array in borders0)]
         else:
             row = at * sizes.rows[level] + row
             tiles = [owns[level][row], *([(border1, border2)[level - 1][row]] if s else [])]
@@ -446,11 +474,9 @@
         sources.append(source)
     narrow(sizes, place, 2, sums.at[:, :, : sizes.held[2]], level3, 3)
 
-    for at in (0, 1):
-        sums[at, :, : sizes.held[2]] = held_row(2, at, 0) + held_row(2, at, 1)
-    narrow(sizes, place, 2, sums.at[:, :, : sizes.held[2]], level3.at[3:5], 2)
-    tiles = packing(sizes, 5)[2]
-    pack_rows(sizes, place, [level3[row] for row in range(5)], contribution)
+    rows = [level3[row] for row in range(3)] + [top[at] for top in tops for at in (0, 1)]
+    tiles = packing(sizes, len(rows))[1]
+    pack_rows(sizes, place, rows, contribution)
     with_far[0:tiles] = contribution[...]
     (s1, s2), (v1, v2) = sources, smooths
     next_rows = (v0[n0 - 1], s1[n1], s1[n1 + 1], v1[n1 - 1], s2[n2], s2[n2 + 1], v2[n2 - 1])
@@ -481,11 +507,16 @@
 
 
 def coarse_kernel(sizes, stride, radix, place, *refs):
-    blocks, refs = refs[:radix], refs[radix:]
+    blocks, tops, refs = refs[:radix], refs[radix], refs[radix + 1 :]
     out, merged, sums = refs[:3]
     coarse = [refs[3 + 9 * index : 12 + 9 * index] for index in range(3)]
     total = sizes.span_count
-    merge_into(sizes, place, stride, radix, blocks, merged, coarse[0][4], coarse[0][5], 1)
+    merge_into(sizes, place, stride, radix, blocks, merged)
+    position = (place[0] // stride) % radix
+    for step in range(radix):
+        at = (position ^ step) * stride
+        coarse[0][4][pl.ds(at + 1, stride)] = tops[2 * step]
+        coarse[0][5][pl.ds(at, stride)] = tops[2 * step + 1]
     zero = jnp.zeros((sizes.depth, LANES), f32)
     for index in range(3):
         level = 3 + index
@@ -551,10 +582,10 @@
     s = sizes.sides
     pair, far_pair, coefs, (own0, turned) = refs[:2], refs[2:4], refs[4:7], refs[7:9]
     from_prev, from_next = (Arrived(place, pair, forward) for forward in (0, 1))
-    tiles = packing(sizes, 5)[2]
+    tiles = far_pair[0].shape[0] - sizes.held[2] // LANES
     far_pair = (far_pair[0].at[tiles : tiles + sizes.held[2] // LANES], far_pair[1])
     fars = [Arrived(place, far_pair, forward, 2) for forward in (0, 1)]
-    borders0, out, refs = refs[9 : 9 + s], refs[9 + s], refs[10 + s :]
+    borders0, borders_r, out, refs = refs[9 : 9 + s], refs[9 + s : 9 + 2 * s], refs[9 + 2 * s], refs[10 + 2 * s :]
     total1, total2, result = refs[:3]
     over2, over1, over0, lift2, lift1, lift0, it2, it1, it0, semaphores = refs[3:]
     slots = sizes.slots
@@ -597,8 +628,11 @@
         widen(sizes, place, level - 1, target, upper, n + 2)
 
     def held_row(at, row):
-        own = turned[row - 1] if at == 2 else own0[at, row - 1]
-        return jnp.concatenate([own, *(array[at, row - 1] for array in borders0)], axis=1)
+        if at == 2:
+            tiles = [turned[row - 1], *(array[row - 1] for array in borders_r)]
+        else:
+            tiles = [own0[at, row - 1], *(array[at, row - 1] for array in borders0)]
+        return jnp.concatenate(tiles, axis=1)
 
     fx, fy, fz, weight, v0 = parts(coefs[0], coefficient_rows(sizes, 0))
     lift0[0] = fringed_row(sizes, 0, 0, from_prev) + over0[0]
@@ -650,6 +684,14 @@
     return []
 
 
+def edge_columns(edges, sizes):
+    if sizes.sides == 1:
+        return [lax.ppermute(edges[0], "width", [(0, 1), (1, 0)])]
+    if sizes.sides == 2:
+        return [along(edges[1], "width", -1), along(edges[0], "width", 1)]
+    return []
+
+
 def stages(count):
     stride = 1
     while stride < count:
@@ -686,35 +728,42 @@
     held = [(depth, count) for count in sizes.held]
     down_message = (sizes.tiles, *tile)
     up_message = (sizes.tiles + 1, *tile)
-    own0, own1, own2, *to_pairs = call(
+    own0, own1, own2, first, second, *edges = call(
         functools.partial(start_kernel, sizes),
         "start",
         1.1,
-        [(2, n0, *own[0]), (2 * n1, *own[1]), (2 * n2, *own[2]), down_message, down_message],
+        [(2, n0, *own[0]), (2 * n1, *own[1]), (2 * n2, *own[2]), down_message, down_message]
+        + [(2, n0, depth, BORDER)] * s,
         [(2 * n1, *own[0])],
         place,
         [diffusivity, reaction],
     )
-    halos = exchange(to_pairs, 1)
+    borders = edge_columns(edges, sizes)
+    halos = exchange([first, second], 1)
     turned, *edges = call(
         functools.partial(turn_kernel, sizes),
         "turn",
         0.7,
-        [(n0, *own[0])] + [(3, n0, depth, BORDER)] * s,
+        [(n0, *own[0])] + [(n0, depth, BORDER)] * s,
         [],
         place,
-        [right_side, own0],
+        [right_side],
     )
-    if s == 1:
-        borders = [lax.ppermute(edges[0], "width", [(0, 1), (1, 0)])]
-    elif s == 2:
-        borders = [along(edges[1], "width", -1), along(edges[0], "width", 1)]
-    else:
-        borders = []
+    borders_r = edge_columns(edges, sizes)
     plan = list(stages(sizes.span_count))
+    border1, border2, top = call(
+        functools.partial(top_kernel, sizes),
+        "top",
+        0.9,
+        [(2 * n1, *tile), (2 * n2, *tile), (2, *tile)],
+        [(2 * n1, depth, 2 * LANES)],
+        place,
+        [own2, *borders],
+    )
+    tops = swap(top, *plan[-1])
+    halos, tops, borders_r = lax.optimization_barrier((halos, tops, borders_r))
     sides = beside(halos, sizes)
-
-    part = packing(sizes, 5)[2]
+    part = packing(sizes, 3 + 2 * sizes.last)[1]
     lengths = [sum(coefficient_rows(sizes, level)) for level in range(3)]
     far = (sizes.held[2] // LANES, *tile)
     coefs = [(lengths[level], *held[level]) for level in range(3)]
@@ -723,32 +772,30 @@
         "down",
         3.6,
         [*coefs, (part, *tile), (part + far[0], *tile), up_message, up_message, far],
-        [(2 * n1, *tile), (2 * n2, *tile), (5, *tile), (max(2 * n1, n1 + 2), *held[0])],
+        [(3, *tile), (n1 + 2, *held[0])],
         place,
-        [own0, own1, own2, turned, *borders, *halos, *sum(sides, [])],
+        [own0, own1, own2, turned, *borders, *borders_r, *halos, *sum(sides, []), border1, border2, *tops],
     )
     coefs_out, blocks, with_far, ups, far_second = downs[:3], downs[3], downs[4], downs[5:7], downs[7]
-    far_rows = None
+    far_first = None
     for stride, radix in plan[:-1]:
         count = stride * radix
-        if far_rows is None:
-            blocks = swap(blocks, stride, radix, {2: with_far})
-            far_rows = [blocks[2], exchange([None, far_second], 2)[1]]
-            blocks, far_rows = lax.optimization_barrier((blocks, far_rows))
-        else:
-            blocks = swap(blocks, stride, radix)
-        (blocks,) = call(
-            functools.partial(merge_kernel, sizes, stride, radix),
+        blocks = swap(blocks, stride, radix, None if far_first is not None else {2: with_far})
+        far_first = blocks[2] if far_first is None else far_first
+        final = (stride, radix) == plan[-2]
+        rows = count + 2 + (0 if final else 2 * sizes.last * count)
+        blocks, top_rows = call(
+            functools.partial(merge_kernel, sizes, stride, radix, final),
             "merge",
             0.9,
-            [(packing(sizes, 3 * count + 2)[2], *tile)],
-            [(count + 2, *tile), (count, *tile), (count, *tile)],
+            [(packing(sizes, rows)[1], *tile), (2 * sizes.last, count, *tile)],
+            [(count + 2, *tile)],
             place,
             blocks,
         )
     stride, radix = plan[-1]
     blocks = swap(blocks, stride, radix)
-    received = exchange(ups, 1) + far_rows
+    received = exchange(ups, 1) + [far_first, exchange([None, far_second], 2)[1]]
     scratch = [(sizes.span_count + 2, *tile), (max(sizes.span_count // 2, 2), *tile)]
     for index in range(3):
         count = sizes.span_count >> index
@@ -761,7 +808,7 @@
         [(n3 + 2, *tile)],
         scratch,
         place,
-        blocks,
+        [*blocks, top_rows],
     )
     scratch = [(n1 + 2, *held[1]), (n2 + 2, *held[2]), diffusivity.shape]
     scratch += [(n3 + 2, *held[2]), (n2 + 2, *held[1]), (n1 + 2, *held[0])]
@@ -774,7 +821,7 @@
         [diffusivity.shape],
         scratch,
         place,
-        [coarse, *received, *coefs_out, own0, turned, *borders],
+        [coarse, *received, *coefs_out, own0, turned, *borders, *borders_r],
         copies=CHUNKS,
         far_out=True,
     )

time: 55.3 us -> 55.8 us (level)
  the two profiles are of different devices: /device:TPU:0 before, /device:TPU:10 now
where the time goes in v9:
time: 55.8 us; the launch traced here: 55.5 us
  starting transfers between devices  25.8 us (46%)
  waiting for transfers between devices  14 us (25%)
  Pallas kernels  13.4 us (24%)
  local copies, waits for them, and re-layouts  2.09 us (4%)
    pallas_call x7, Pallas kernels, call(): pl.pallas_call(body, name=name, out_shape=[jax.ShapeDtypeStruct(shape, f3...  13.4 us
    ppermute x5, starting transfers between devices, exchange(): lax.ppermute(value, 'span', route)  13.4 us
    ppermute x9, starting transfers between devices, swap(): lax.ppermute(others.get(step, value), 'span', [(device, device ^ step * s...  11.7 us
    ppermute x5, waiting for transfers between devices, exchange(): lax.ppermute(value, 'span', route)  6.4 us
    ppermute x9, waiting for transfers between devices, swap(): lax.ppermute(others.get(step, value), 'span', [(device, device ^ step * s...  6.35 us
    unnamed x6, local copies, waits for them, and re-layouts  2.09 us
    ppermute x2, waiting for transfers between devices, beside(): lax.ppermute(value, 'width', [(0, 1), (1, 0)])  1.26 us
  transfers between devices with their start and end apart: 18, of which 9 were waited for; matrix products, arithmetic and copies ran while one was open for 0% of the time, Pallas kernels for 8%

profile of v9, /device:TPU:10, one launch (start us, length us, event | category | flops | bytes accessed | tf_op | source)
XLA Modules:
  0.0 55.5 jit_solution(8127767532977039768)
XLA Ops:
  0.1 1.0 %copy-done = f32[32,8,512]{2,1,0:T(8,128)S(1)} copy-done((f32[32,8,512]{2,1,0:T(8,128)S(1)}, f32[32,8,512]{2,1,0:T(8,128)}, u32[]{:S(2)}) %copy-start) | copy-done | bytes 524312
  1.1 1.0 %copy-done.1 = f32[32,8,512]{2,1,0:T(8,128)S(1)} copy-done((f32[32,8,512]{2,1,0:T(8,128)S(1)}, f32[32,8,512]{2,1,0:T(8,128)}, u32[]{:S(2)}) %copy-start.1) | copy-done | bytes 524312
  2.2 1.1 %start.1 = (f32[2,8,32,512]{3,2,1,0:T(8,128)S(1)}, f32[8,32,256]{2,1,0:T(8,128)S(1)}, f32[4,32,128]{2,1,0:T(8,128)S(1)}, f32[13,32,128]{2,1,0:T(8,128)S(1)}, f32...) custom-call(s32[2]{0:T(128)S(1)} %pad_add_fusion.place, f32[32,8,512]{2,1,0:T(8,128)S(1)} %copy-done, ...), custom_call_target="tpu_custom_call" | custom-call | flops 1264999936 | bytes 4059000 | tf_op jit(solution)/shard_map/start/pallas_call | solution.py:661
  4.0 4.3 %collective-permute-start.2 = (f32[13,32,128]{2,1,0:T(8,128)S(1)}, f32[13,32,128]{2,1,0:T(8,128)S(1)}, u32[]{:S(2)}, u32[]{:S(2)}) collective-permute-start(f32[13,32,128]{2,1,0:T(8,128)S(1)} %get-tuple-element.39), channel_id=1, source_target_pairs={{2,4},{4,2},{6,8},{8,6},{10,12},{12,10},{14,16},{16,14},{18,20},{2... | collective-permute-start | bytes 638984 | tf_op jit(solution)/shard_map/ppermute | solution.py:717
  9.1 1.0 %top.1 = (f32[8,32,128]{2,1,0:T(8,128)S(1)}, f32[4,32,128]{2,1,0:T(8,128)S(1)}, f32[2,32,128]{2,1,0:T(8,128)S(1)}) custom-call(s32[2]{0:T(128)S(1)} %pad_add_fusion.place, f32[4,32,128]{2,1,0:T(8,128)S(1)} %get-tuple-element.35.own2.refs_2_, f32[2,8,32,128]{3,2,1,0:T(8,128)S(1)} %collective-permute-done.refs_0_.refs_4_.refs_9_), custom_call_target="tpu_custom_call" | custom-call | flops 1035000000 | bytes 3321000 | tf_op jit(solution)/shard_map/top/pallas_call | solution.py:661
  10.2 1.6 %collective-permute-start.5 = (f32[2,32,128]{2,1,0:T(8,128)S(1)}, f32[2,32,128]{2,1,0:T(8,128)S(1)}, u32[]{:S(2)}, u32[]{:S(2)}) collective-permute-start(f32[2,32,128]{2,1,0:T(8,128)S(1)} %get-tuple-element.47.refs_12_), channel_id=1, source_target_pairs={{0,24},{2,26},{4,28},{6,30},{8,16},{10,18},{12,20},{14,22},{16,8},... | collective-permute-start | bytes 98312 | tf_op jit(solution)/shard_map/ppermute | solution.py:707
  11.8 1.2 %collective-permute-start.4 = (f32[2,32,128]{2,1,0:T(8,128)S(1)}, f32[2,32,128]{2,1,0:T(8,128)S(1)}, u32[]{:S(2)}, u32[]{:S(2)}) collective-permute-start(f32[2,32,128]{2,1,0:T(8,128)S(1)} %get-tuple-element.47.refs_12_), channel_id=1, source_target_pairs={{0,16},{2,18},{4,20},{6,22},{8,24},{10,26},{12,28},{14,30},{16,0},... | collective-permute-start | bytes 98312 | tf_op jit(solution)/shard_map/ppermute | solution.py:707
  13.0 1.2 %collective-permute-start.3 = (f32[2,32,128]{2,1,0:T(8,128)S(1)}, f32[2,32,128]{2,1,0:T(8,128)S(1)}, u32[]{:S(2)}, u32[]{:S(2)}) collective-permute-start(f32[2,32,128]{2,1,0:T(8,128)S(1)} %get-tuple-element.47.refs_12_), channel_id=1, source_target_pairs={{0,8},{2,10},{4,12},{6,14},{8,0},{10,2},{12,4},{14,6},{16,24},{18,... | collective-permute-start | bytes 98312 | tf_op jit(solution)/shard_map/ppermute | solution.py:707
  14.3 1.4 %collective-permute-done.1.refs_6_ = f32[13,32,128]{2,1,0:T(8,128)S(1)} collective-permute-done((f32[13,32,128]{2,1,0:T(8,128)S(1)}, f32[13,32,128]{2,1,0:T(8,128)S(1)}, u32[]{:S(2)}, u32[]{:S(2)}) %collective-permute-start.1) | collective-permute-done | bytes 213024 | tf_op jit(solution)/shard_map/ppermute | solution.py:717
  15.6 1.0 %collective-permute-done.2.refs_7_ = f32[13,32,128]{2,1,0:T(8,128)S(1)} collective-permute-done((f32[13,32,128]{2,1,0:T(8,128)S(1)}, f32[13,32,128]{2,1,0:T(8,128)S(1)}, u32[]{:S(2)}, u32[]{:S(2)}) %collective-permute-start.2) | collective-permute-done | bytes 213024 | tf_op jit(solution)/shard_map/ppermute | solution.py:717
  19.2 3.8 %down.1 = (f32[41,32,640]{2,1,0:T(8,128)S(1)}, f32[43,32,384]{2,1,0:T(8,128)S(1)}, f32[29,32,256]{2,1,0:T(8,128)S(1)}, f32[7,32,128]{2,1,0:T(8,128)S(1)}, f32[9,...) custom-call(s32[2]{0:T(128)S(1)} %pad_add_fusion.place, ...), custom_call_target="tpu_custom_call" | custom-call | flops 4140000000 | bytes 13284000 | tf_op jit(solution)/shard_map/down/pallas_call | solution.py:661
  23.1 1.1 %collective-permute-start.10 = (f32[9,32,128]{2,1,0:T(8,128)S(1)}, f32[9,32,128]{2,1,0:T(8,128)S(1)}, u32[]{:S(2)}, u32[]{:S(2)}) collective-permute-start(f32[9,32,128]{2,1,0:T(8,128)S(1)} %get-tuple-element.52), channel_id=1, source_target_pairs={{0,4},{2,6},{4,0},{6,2},{8,12},{10,14},{12,8},{14,10},{16,20},{18,... | collective-permute-start | bytes 442376 | tf_op jit(solution)/shard_map/ppermute | solution.py:707
  24.1 1.2 %collective-permute-start.11 = (f32[7,32,128]{2,1,0:T(8,128)S(1)}, f32[7,32,128]{2,1,0:T(8,128)S(1)}, u32[]{:S(2)}, u32[]{:S(2)}) collective-permute-start(f32[7,32,128]{2,1,0:T(8,128)S(1)} %get-tuple-element.51.refs_0_), channel_id=1, source_target_pairs={{0,6},{2,4},{4,2},{6,0},{8,14},{10,12},{12,10},{14,8},{16,22},{18,... | collective-permute-start | bytes 344072 | tf_op jit(solution)/shard_map/ppermute | solution.py:707
  25.3 1.3 %collective-permute-start.9 = (f32[7,32,128]{2,1,0:T(8,128)S(1)}, f32[7,32,128]{2,1,0:T(8,128)S(1)}, u32[]{:S(2)}, u32[]{:S(2)}) collective-permute-start(f32[7,32,128]{2,1,0:T(8,128)S(1)} %get-tuple-element.51.refs_0_), channel_id=1, source_target_pairs={{0,2},{2,0},{4,6},{6,4},{8,10},{10,8},{12,14},{14,12},{16,18},{18,... | collective-permute-start | bytes 344072 | tf_op jit(solution)/shard_map/ppermute | solution.py:707
  26.6 4.4 %collective-permute-done.11.refs_3_ = f32[7,32,128]{2,1,0:T(8,128)S(1)} collective-permute-done((f32[7,32,128]{2,1,0:T(8,128)S(1)}, f32[7,32,128]{2,1,0:T(8,128)S(1)}, u32[]{:S(2)}, u32[]{:S(2)}) %collective-permute-start.11) | collective-permute-done | bytes 114720 | tf_op jit(solution)/shard_map/ppermute | solution.py:707
  31.0 1.0 %collective-permute-done.9.refs_1_ = f32[7,32,128]{2,1,0:T(8,128)S(1)} collective-permute-done((f32[7,32,128]{2,1,0:T(8,128)S(1)}, f32[7,32,128]{2,1,0:T(8,128)S(1)}, u32[]{:S(2)}, u32[]{:S(2)}) %collective-permute-start.9) | collective-permute-done | bytes 114720 | tf_op jit(solution)/shard_map/ppermute | solution.py:707
  33.0 2.2 %collective-permute-start.14 = (f32[4,32,128]{2,1,0:T(8,128)S(1)}, f32[4,32,128]{2,1,0:T(8,128)S(1)}, u32[]{:S(2)}, u32[]{:S(2)}) collective-permute-start(f32[4,32,128]{2,1,0:T(8,128)S(1)} %get-tuple-element.53.refs_0_), channel_id=1, source_target_pairs={{0,24},{2,26},{4,28},{6,30},{8,16},{10,18},{12,20},{14,22},{16,8},... | collective-permute-start | bytes 196616 | tf_op jit(solution)/shard_map/ppermute | solution.py:707
  35.3 1.8 %collective-permute-start.13 = (f32[4,32,128]{2,1,0:T(8,128)S(1)}, f32[4,32,128]{2,1,0:T(8,128)S(1)}, u32[]{:S(2)}, u32[]{:S(2)}) collective-permute-start(f32[4,32,128]{2,1,0:T(8,128)S(1)} %get-tuple-element.53.refs_0_), channel_id=1, source_target_pairs={{0,16},{2,18},{4,20},{6,22},{8,24},{10,26},{12,28},{14,30},{16,0},... | collective-permute-start | bytes 196616 | tf_op jit(solution)/shard_map/ppermute | solution.py:707
  37.1 3.7 %collective-permute-start.17 = (f32[2,32,128]{2,1,0:T(8,128)S(1)}, f32[2,32,128]{2,1,0:T(8,128)S(1)}, u32[]{:S(2)}, u32[]{:S(2)}) collective-permute-start(f32[2,32,128]{2,1,0:T(8,128)S(1)} %get-tuple-element.57), channel_id=1, source_target_pairs={{4,8},{8,4},{6,10},{10,6},{12,16},{16,12},{14,18},{18,14},{20,24},... | collective-permute-start | bytes 98312 | tf_op jit(solution)/shard_map/ppermute | solution.py:717
  40.8 1.0 %collective-permute-start.15 = (f32[14,32,128]{2,1,0:T(8,128)S(1)}, f32[14,32,128]{2,1,0:T(8,128)S(1)}, u32[]{:S(2)}, u32[]{:S(2)}) collective-permute-start(f32[14,32,128]{2,1,0:T(8,128)S(1)} %get-tuple-element.55), channel_id=1, source_target_pairs={{0,2},{2,0},{4,6},{6,4},{8,10},{10,8},{12,14},{14,12},{16,18},{18,... | collective-permute-start | bytes 688136 | tf_op jit(solution)/shard_map/ppermute | solution.py:717
  41.8 3.8 %collective-permute-start.16 = (f32[14,32,128]{2,1,0:T(8,128)S(1)}, f32[14,32,128]{2,1,0:T(8,128)S(1)}, u32[]{:S(2)}, u32[]{:S(2)}) collective-permute-start(f32[14,32,128]{2,1,0:T(8,128)S(1)} %get-tuple-element.56), channel_id=1, source_target_pairs={{2,4},{4,2},{6,8},{8,6},{10,12},{12,10},{14,16},{16,14},{18,20},{2... | collective-permute-start | bytes 688136 | tf_op jit(solution)/shard_map/ppermute | solution.py:717
  45.6 2.7 %coarse.1 = f32[3,32,128]{2,1,0:T(8,128)S(1)} custom-call(s32[2]{0:T(128)S(1)} %pad_add_fusion.place, f32[4,32,128]{2,1,0:T(8,128)S(1)} %get-tuple-element.53.refs_0_, f32[4,32,128]{2,1,0:T(8,128)S(1)} %collective-permute-done.12.refs_1_, f32[4,32,128]{2,1,0:T(8,128)S(1)} %collective-permute-done.13.refs_2_, ...), custom_call_target="tpu_custom_call" | custom-call | flops 3335000064 | bytes 10701000 | tf_op jit(solution)/shard_map/coarse/pallas_call | solution.py:661
  48.3 3.5 %collective-permute-done.15.refs_0_ = f32[14,32,128]{2,1,0:T(8,128)S(1)} collective-permute-done((f32[14,32,128]{2,1,0:T(8,128)S(1)}, f32[14,32,128]{2,1,0:T(8,128)S(1)}, u32[]{:S(2)}, u32[]{:S(2)}) %collective-permute-start.15) | collective-permute-done | bytes 229408 | tf_op jit(solution)/shard_map/ppermute | solution.py:717
  52.4 3.1 %up.1 = f32[32,8,512]{2,1,0:T(8,128)} custom-call(s32[2]{0:T(128)S(1)} %pad_add_fusion.place, f32[3,32,128]{2,1,0:T(8,128)S(1)} %coarse.1, f32[14,32,128]{2,1,0:T(8,128)S(1)} %collective-permute-done.15.refs_0_, f32[14,32,128]{2,1,0:T(8,128)S(1)} %collective-permute-done.16.refs_1_, f32[9,32,128]{2,1,0:T(8,128)S(1)} %collective-permute-done.10.refs_2_, ...), custom_call_target="tpu_custom_call" | custom-call | flops 3449999872 | bytes 11070000 | tf_op jit(solution)/shard_map/up/pallas_call | solution.py:661
  (26 shorter events, 5.7 us)
Async XLA Ops:
  0.1 1.0 %copy-start = (f32[32,8,512]{2,1,0:T(8,128)S(1)}, f32[32,8,512]{2,1,0:T(8,128)}, u32[]{:S(2)}) copy-start(f32[32,8,512]{2,1,0:T(8,128)} %conduct.1) | copy-start | bytes 1572868
  1.1 1.0 %copy-start.1 = (f32[32,8,512]{2,1,0:T(8,128)S(1)}, f32[32,8,512]{2,1,0:T(8,128)}, u32[]{:S(2)}) copy-start(f32[32,8,512]{2,1,0:T(8,128)} %binding.1) | copy-start | bytes 1572868
  2.2 6.2 %copy-start.2 = (f32[32,8,512]{2,1,0:T(8,128)S(1)}, f32[32,8,512]{2,1,0:T(8,128)}, u32[]{:S(2)}) copy-start(f32[32,8,512]{2,1,0:T(8,128)} %right_side.1) | copy-start | bytes 1572868
  3.3 5.8 %collective-permute-start = (f32[2,8,32,128]{3,2,1,0:T(8,128)S(1)}, f32[2,8,32,128]{3,2,1,0:T(8,128)S(1)}, u32[]{:S(2)}, u32[]{:S(2)}) collective-permute-start(f32[2,8,32,128]{3,2,1,0:T(8,128)S(1)} %get-tuple-element.37), channel_id=1, source_target_pairs={{0,1},{1,0},{2,3},{3,2},{4,5},{5,4},{6,7},{7,6},{8,9},{9,8},{10,11... | collective-permute-start | bytes 786440 | tf_op jit(solution)/shard_map/ppermute | solution.py:689
  3.4 12.2 %collective-permute-start.1 = (f32[13,32,128]{2,1,0:T(8,128)S(1)}, f32[13,32,128]{2,1,0:T(8,128)S(1)}, u32[]{:S(2)}, u32[]{:S(2)}) collective-permute-start(f32[13,32,128]{2,1,0:T(8,128)S(1)} %get-tuple-element.38), channel_id=1, source_target_pairs={{0,2},{2,0},{4,6},{6,4},{8,10},{10,8},{12,14},{14,12},{16,18},{18,... | collective-permute-start | bytes 638984 | tf_op jit(solution)/shard_map/ppermute | solution.py:717
  4.0 12.6 %collective-permute-start.2 = (f32[13,32,128]{2,1,0:T(8,128)S(1)}, f32[13,32,128]{2,1,0:T(8,128)S(1)}, u32[]{:S(2)}, u32[]{:S(2)}) collective-permute-start(f32[13,32,128]{2,1,0:T(8,128)S(1)} %get-tuple-element.39), channel_id=1, source_target_pairs={{2,4},{4,2},{6,8},{8,6},{10,12},{12,10},{14,16},{16,14},{18,20},{2... | collective-permute-start | bytes 638984 | tf_op jit(solution)/shard_map/ppermute | solution.py:717
  9.0 4.0 %collective-permute-start.6 = (f32[8,32,128]{2,1,0:T(8,128)S(1)}, f32[8,32,128]{2,1,0:T(8,128)S(1)}, u32[]{:S(2)}, u32[]{:S(2)}) collective-permute-start(f32[8,32,128]{2,1,0:T(8,128)S(1)} %get-tuple-element.41), channel_id=1, source_target_pairs={{0,1},{1,0},{2,3},{3,2},{4,5},{5,4},{6,7},{7,6},{8,9},{9,8},{10,11... | collective-permute-start | bytes 393224 | tf_op jit(solution)/shard_map/ppermute | solution.py:689
  10.2 6.4 %collective-permute-start.5 = (f32[2,32,128]{2,1,0:T(8,128)S(1)}, f32[2,32,128]{2,1,0:T(8,128)S(1)}, u32[]{:S(2)}, u32[]{:S(2)}) collective-permute-start(f32[2,32,128]{2,1,0:T(8,128)S(1)} %get-tuple-element.47.refs_12_), channel_id=1, source_target_pairs={{0,24},{2,26},{4,28},{6,30},{8,16},{10,18},{12,20},{14,22},{16,8},... | collective-permute-start | bytes 98312 | tf_op jit(solution)/shard_map/ppermute | solution.py:707
  11.8 4.8 %collective-permute-start.4 = (f32[2,32,128]{2,1,0:T(8,128)S(1)}, f32[2,32,128]{2,1,0:T(8,128)S(1)}, u32[]{:S(2)}, u32[]{:S(2)}) collective-permute-start(f32[2,32,128]{2,1,0:T(8,128)S(1)} %get-tuple-element.47.refs_12_), channel_id=1, source_target_pairs={{0,16},{2,18},{4,20},{6,22},{8,24},{10,26},{12,28},{14,30},{16,0},... | collective-permute-start | bytes 98312 | tf_op jit(solution)/shard_map/ppermute | solution.py:707
  13.0 4.4 %collective-permute-start.3 = (f32[2,32,128]{2,1,0:T(8,128)S(1)}, f32[2,32,128]{2,1,0:T(8,128)S(1)}, u32[]{:S(2)}, u32[]{:S(2)}) collective-permute-start(f32[2,32,128]{2,1,0:T(8,128)S(1)} %get-tuple-element.47.refs_12_), channel_id=1, source_target_pairs={{0,8},{2,10},{4,12},{6,14},{8,0},{10,2},{12,4},{14,6},{16,24},{18,... | collective-permute-start | bytes 98312 | tf_op jit(solution)/shard_map/ppermute | solution.py:707
  17.5 1.5 %collective-permute-start.7 = (f32[13,32,128]{2,1,0:T(8,128)S(1)}, f32[13,32,128]{2,1,0:T(8,128)S(1)}, u32[]{:S(2)}, u32[]{:S(2)}) collective-permute-start(f32[13,32,128]{2,1,0:T(8,128)S(1)} %collective-permute-done.1.refs_6_), channel_id=1, source_target_pairs={{0,1},{1,0},{2,3},{3,2},{4,5},{5,4},{6,7},{7,6},{8,9},{9,8},{10,11... | collective-permute-start | bytes 638984 | tf_op jit(solution)/shard_map/ppermute | solution.py:681
  17.5 1.8 %collective-permute-start.8 = (f32[13,32,128]{2,1,0:T(8,128)S(1)}, f32[13,32,128]{2,1,0:T(8,128)S(1)}, u32[]{:S(2)}, u32[]{:S(2)}) collective-permute-start(f32[13,32,128]{2,1,0:T(8,128)S(1)} %collective-permute-done.2.refs_7_), channel_id=1, source_target_pairs={{0,1},{1,0},{2,3},{3,2},{4,5},{5,4},{6,7},{7,6},{8,9},{9,8},{10,11... | collective-permute-start | bytes 638984 | tf_op jit(solution)/shard_map/ppermute | solution.py:681
  23.1 9.0 %collective-permute-start.10 = (f32[9,32,128]{2,1,0:T(8,128)S(1)}, f32[9,32,128]{2,1,0:T(8,128)S(1)}, u32[]{:S(2)}, u32[]{:S(2)}) collective-permute-start(f32[9,32,128]{2,1,0:T(8,128)S(1)} %get-tuple-element.52), channel_id=1, source_target_pairs={{0,4},{2,6},{4,0},{6,2},{8,12},{10,14},{12,8},{14,10},{16,20},{18,... | collective-permute-start | bytes 442376 | tf_op jit(solution)/shard_map/ppermute | solution.py:707
  24.1 6.9 %collective-permute-start.11 = (f32[7,32,128]{2,1,0:T(8,128)S(1)}, f32[7,32,128]{2,1,0:T(8,128)S(1)}, u32[]{:S(2)}, u32[]{:S(2)}) collective-permute-start(f32[7,32,128]{2,1,0:T(8,128)S(1)} %get-tuple-element.51.refs_0_), channel_id=1, source_target_pairs={{0,6},{2,4},{4,2},{6,0},{8,14},{10,12},{12,10},{14,8},{16,22},{18,... | collective-permute-start | bytes 344072 | tf_op jit(solution)/shard_map/ppermute | solution.py:707
  25.3 6.8 %collective-permute-start.9 = (f32[7,32,128]{2,1,0:T(8,128)S(1)}, f32[7,32,128]{2,1,0:T(8,128)S(1)}, u32[]{:S(2)}, u32[]{:S(2)}) collective-permute-start(f32[7,32,128]{2,1,0:T(8,128)S(1)} %get-tuple-element.51.refs_0_), channel_id=1, source_target_pairs={{0,2},{2,0},{4,6},{6,4},{8,10},{10,8},{12,14},{14,12},{16,18},{18,... | collective-permute-start | bytes 344072 | tf_op jit(solution)/shard_map/ppermute | solution.py:707
  33.0 8.7 %collective-permute-start.14 = (f32[4,32,128]{2,1,0:T(8,128)S(1)}, f32[4,32,128]{2,1,0:T(8,128)S(1)}, u32[]{:S(2)}, u32[]{:S(2)}) collective-permute-start(f32[4,32,128]{2,1,0:T(8,128)S(1)} %get-tuple-element.53.refs_0_), channel_id=1, source_target_pairs={{0,24},{2,26},{4,28},{6,30},{8,16},{10,18},{12,20},{14,22},{16,8},... | collective-permute-start | bytes 196616 | tf_op jit(solution)/shard_map/ppermute | solution.py:707
  35.3 10.3 %collective-permute-start.13 = (f32[4,32,128]{2,1,0:T(8,128)S(1)}, f32[4,32,128]{2,1,0:T(8,128)S(1)}, u32[]{:S(2)}, u32[]{:S(2)}) collective-permute-start(f32[4,32,128]{2,1,0:T(8,128)S(1)} %get-tuple-element.53.refs_0_), channel_id=1, source_target_pairs={{0,16},{2,18},{4,20},{6,22},{8,24},{10,26},{12,28},{14,30},{16,0},... | collective-permute-start | bytes 196616 | tf_op jit(solution)/shard_map/ppermute | solution.py:707
  37.1 8.5 %collective-permute-start.12 = (f32[4,32,128]{2,1,0:T(8,128)S(1)}, f32[4,32,128]{2,1,0:T(8,128)S(1)}, u32[]{:S(2)}, u32[]{:S(2)}) collective-permute-start(f32[4,32,128]{2,1,0:T(8,128)S(1)} %get-tuple-element.53.refs_0_), channel_id=1, source_target_pairs={{0,8},{2,10},{4,12},{6,14},{8,0},{10,2},{12,4},{14,6},{16,24},{18,... | collective-permute-start | bytes 196616 | tf_op jit(solution)/shard_map/ppermute | solution.py:707
  37.1 11.3 %collective-permute-start.17 = (f32[2,32,128]{2,1,0:T(8,128)S(1)}, f32[2,32,128]{2,1,0:T(8,128)S(1)}, u32[]{:S(2)}, u32[]{:S(2)}) collective-permute-start(f32[2,32,128]{2,1,0:T(8,128)S(1)} %get-tuple-element.57), channel_id=1, source_target_pairs={{4,8},{8,4},{6,10},{10,6},{12,16},{16,12},{14,18},{18,14},{20,24},... | collective-permute-start | bytes 98312 | tf_op jit(solution)/shard_map/ppermute | solution.py:717
  40.8 11.0 %collective-permute-start.15 = (f32[14,32,128]{2,1,0:T(8,128)S(1)}, f32[14,32,128]{2,1,0:T(8,128)S(1)}, u32[]{:S(2)}, u32[]{:S(2)}) collective-permute-start(f32[14,32,128]{2,1,0:T(8,128)S(1)} %get-tuple-element.55), channel_id=1, source_target_pairs={{0,2},{2,0},{4,6},{6,4},{8,10},{10,8},{12,14},{14,12},{16,18},{18,... | collective-permute-start | bytes 688136 | tf_op jit(solution)/shard_map/ppermute | solution.py:717
  41.8 10.7 %collective-permute-start.16 = (f32[14,32,128]{2,1,0:T(8,128)S(1)}, f32[14,32,128]{2,1,0:T(8,128)S(1)}, u32[]{:S(2)}, u32[]{:S(2)}) collective-permute-start(f32[14,32,128]{2,1,0:T(8,128)S(1)} %get-tuple-element.56), channel_id=1, source_target_pairs={{2,4},{4,2},{6,8},{8,6},{10,12},{12,10},{14,16},{16,14},{18,20},{2... | collective-permute-start | bytes 688136 | tf_op jit(solution)/shard_map/ppermute | solution.py:717

commit v10 on v9

--- a/solution.py
+++ b/solution.py
@@ -35,7 +35,6 @@
             self.slots.append((start, self.own[level]))
             start += self.own[level]
         self.tiles = start
-        self.last = list(stages(span_count))[-1][1]
 
 
 def put(message, slot, row):
@@ -355,28 +354,23 @@
     return rows
 
 
-def merge_into(sizes, place, stride, radix, arrays, source, tops=None):
+def merge_into(sizes, place, stride, radix, arrays, source, tops):
     position = (place[0] // stride) % radix
     source[...] = jnp.zeros(source.shape, f32)
-    kinds = 0 if tops is None else tops.shape[0]
     for step, array in enumerate(arrays):
         at = (position ^ step) * stride
-        rows = unpack_rows(sizes, place, array, stride + 2 + kinds * stride)
+        rows = unpack_rows(sizes, place, array, 3 * stride + 2)
         for index, row in enumerate(rows[: stride + 2]):
             source[at + index] = source[at + index] + row
-        for kind in range(kinds):
+        for kind, top in enumerate(tops):
             for index in range(stride):
-                tops[kind, at + index] = rows[stride + 2 + kind * stride + index]
-
-
-def merge_kernel(sizes, stride, radix, final, place, *refs):
-    arrays, out, tops, source = refs[:radix], refs[radix], refs[radix + 1], refs[radix + 2]
+                top[at + index] = rows[stride + 2 + kind * stride + index]
+
+
+def merge_kernel(sizes, stride, radix, place, *refs):
+    arrays, out, (source, *tops) = refs[:radix], refs[radix], refs[radix + 1 :]
     merge_into(sizes, place, stride, radix, arrays, source, tops)
-    count = stride * radix
-    rows = [source[row] for row in range(count + 2)]
-    if not final:
-        rows += [tops[kind, row] for kind in range(tops.shape[0]) for row in range(count)]
-    pack_rows(sizes, place, rows, out)
+    pack_rows(sizes, place, [array[row] for array in (source, *tops) for row in range(array.shape[0])], out)
 
 
 def top_kernel(sizes, place, own2, *refs):
@@ -410,7 +404,7 @@
     from_prev, *beside_prev = (Arrived(place, pair, 0) for pair in pairs_of)
     from_next, *beside_next = (Arrived(place, pair, 1) for pair in pairs_of)
     (border1, border2), refs = refs[:2], refs[2:]
-    tops, refs = refs[: sizes.last], refs[sizes.last :]
+    top, refs = refs[0], refs[1:]
     coefs, contribution, with_far, ups, far, refs = refs[:3], refs[3], refs[4], refs[5:7], refs[7], refs[8:]
     level3, sums = refs
     slots = sizes.slots
@@ -474,7 +468,7 @@
         sources.append(source)
     narrow(sizes, place, 2, sums.at[:, :, : sizes.held[2]], level3, 3)
 
-    rows = [level3[row] for row in range(3)] + [top[at] for top in tops for at in (0, 1)]
+    rows = [level3[row] for row in range(3)] + [top[0], top[1]]
     tiles = packing(sizes, len(rows))[1]
     pack_rows(sizes, place, rows, contribution)
     with_far[0:tiles] = contribution[...]
@@ -507,16 +501,11 @@
 
 
 def coarse_kernel(sizes, stride, radix, place, *refs):
-    blocks, tops, refs = refs[:radix], refs[radix], refs[radix + 1 :]
+    blocks, refs = refs[:radix], refs[radix:]
     out, merged, sums = refs[:3]
     coarse = [refs[3 + 9 * index : 12 + 9 * index] for index in range(3)]
     total = sizes.span_count
-    merge_into(sizes, place, stride, radix, blocks, merged)
-    position = (place[0] // stride) % radix
-    for step in range(radix):
-        at = (position ^ step) * stride
-        coarse[0][4][pl.ds(at + 1, stride)] = tops[2 * step]
-        coarse[0][5][pl.ds(at, stride)] = tops[2 * step + 1]
+    merge_into(sizes, place, stride, radix, blocks, merged, (coarse[0][4].at[1 : total + 1], coarse[0][5]))
     zero = jnp.zeros((sizes.depth, LANES), f32)
     for index in range(3):
         level = 3 + index
@@ -760,10 +749,9 @@
         place,
         [own2, *borders],
     )
-    tops = swap(top, *plan[-1])
-    halos, tops, borders_r = lax.optimization_barrier((halos, tops, borders_r))
+    halos, top, borders_r = lax.optimization_barrier((halos, top, borders_r))
     sides = beside(halos, sizes)
-    part = packing(sizes, 3 + 2 * sizes.last)[1]
+    part = packing(sizes, 5)[1]
     lengths = [sum(coefficient_rows(sizes, level)) for level in range(3)]
     far = (sizes.held[2] // LANES, *tile)
     coefs = [(lengths[level], *held[level]) for level in range(3)]
@@ -774,7 +762,7 @@
         [*coefs, (part, *tile), (part + far[0], *tile), up_message, up_message, far],
         [(3, *tile), (n1 + 2, *held[0])],
         place,
-        [own0, own1, own2, turned, *borders, *borders_r, *halos, *sum(sides, []), border1, border2, *tops],
+        [own0, own1, own2, turned, *borders, *borders_r, *halos, *sum(sides, []), border1, border2, top],
     )
     coefs_out, blocks, with_far, ups, far_second = downs[:3], downs[3], downs[4], downs[5:7], downs[7]
     far_first = None
@@ -782,14 +770,12 @@
         count = stride * radix
         blocks = swap(blocks, stride, radix, None if far_first is not None else {2: with_far})
         far_first = blocks[2] if far_first is None else far_first
-        final = (stride, radix) == plan[-2]
-        rows = count + 2 + (0 if final else 2 * sizes.last * count)
-        blocks, top_rows = call(
-            functools.partial(merge_kernel, sizes, stride, radix, final),
+        (blocks,) = call(
+            functools.partial(merge_kernel, sizes, stride, radix),
             "merge",
             0.9,
-            [(packing(sizes, rows)[1], *tile), (2 * sizes.last, count, *tile)],
-            [(count + 2, *tile)],
+            [(packing(sizes, 3 * count + 2)[1], *tile)],
+            [(count + 2, *tile), (count, *tile), (count, *tile)],
             place,
             blocks,
         )
@@ -808,7 +794,7 @@
         [(n3 + 2, *tile)],
         scratch,
         place,
-        [*blocks, top_rows],
+        blocks,
     )
     scratch = [(n1 + 2, *held[1]), (n2 + 2, *held[2]), diffusivity.shape]
     scratch += [(n3 + 2, *held[2]), (n2 + 2, *held[1]), (n1 + 2, *held[0])]

time: 55.8 us -> 55.9 us (level)
  the two profiles are of different devices: /device:TPU:10 before, /device:TPU:16 now
where the time goes in v10:
time: 55.9 us; the launch traced here: 55.7 us
  waiting for transfers between devices  20.5 us (37%)
  starting transfers between devices  19.3 us (35%)
  Pallas kernels  13.6 us (24%)
  local copies, waits for them, and re-layouts  2.09 us (4%)
    pallas_call x7, Pallas kernels, call(): pl.pallas_call(body, name=name, out_shape=[jax.ShapeDtypeStruct(shape, f3...  13.6 us
    ppermute x5, starting transfers between devices, exchange(): lax.ppermute(value, 'span', route)  11.1 us
    ppermute x5, waiting for transfers between devices, exchange(): lax.ppermute(value, 'span', route)  9.95 us
    ppermute x6, waiting for transfers between devices, swap(): lax.ppermute(others.get(step, value), 'span', [(device, device ^ step * s...  8.98 us
    ppermute x6, starting transfers between devices, swap(): lax.ppermute(others.get(step, value), 'span', [(device, device ^ step * s...  7.56 us
    unnamed x6, local copies, waits for them, and re-layouts  2.09 us
    ppermute x2, waiting for transfers between devices, beside(): lax.ppermute(value, 'width', [(0, 1), (1, 0)])  1.26 us
  transfers between devices with their start and end apart: 15, of which 9 were waited for; matrix products, arithmetic and copies ran while one was open for 0% of the time, Pallas kernels for 8%

profile of v10, /device:TPU:16, one launch (start us, length us, event | category | flops | bytes accessed | tf_op | source)
XLA Modules:
  0.0 55.7 jit_solution(6071421371617264254)
XLA Ops:
  0.1 1.0 %copy-done = f32[32,8,512]{2,1,0:T(8,128)S(1)} copy-done((f32[32,8,512]{2,1,0:T(8,128)S(1)}, f32[32,8,512]{2,1,0:T(8,128)}, u32[]{:S(2)}) %copy-start) | copy-done | bytes 524312
  1.1 1.0 %copy-done.1 = f32[32,8,512]{2,1,0:T(8,128)S(1)} copy-done((f32[32,8,512]{2,1,0:T(8,128)S(1)}, f32[32,8,512]{2,1,0:T(8,128)}, u32[]{:S(2)}) %copy-start.1) | copy-done | bytes 524312
  2.2 1.1 %start.1 = (f32[2,8,32,512]{3,2,1,0:T(8,128)S(1)}, f32[8,32,256]{2,1,0:T(8,128)S(1)}, f32[4,32,128]{2,1,0:T(8,128)S(1)}, f32[13,32,128]{2,1,0:T(8,128)S(1)}, f32...) custom-call(s32[2]{0:T(128)S(1)} %pad_add_fusion.place, f32[32,8,512]{2,1,0:T(8,128)S(1)} %copy-done, ...), custom_call_target="tpu_custom_call" | custom-call | flops 1264999936 | bytes 4059000 | tf_op jit(solution)/shard_map/start/pallas_call | solution.py:650
  3.4 1.6 %collective-permute-start.1 = (f32[13,32,128]{2,1,0:T(8,128)S(1)}, f32[13,32,128]{2,1,0:T(8,128)S(1)}, u32[]{:S(2)}, u32[]{:S(2)}) collective-permute-start(f32[13,32,128]{2,1,0:T(8,128)S(1)} %get-tuple-element.33), channel_id=1, source_target_pairs={{0,2},{2,0},{4,6},{6,4},{8,10},{10,8},{12,14},{14,12},{16,18},{18,... | collective-permute-start | bytes 638984 | tf_op jit(solution)/shard_map/ppermute | solution.py:706
  5.0 3.3 %collective-permute-start.2 = (f32[13,32,128]{2,1,0:T(8,128)S(1)}, f32[13,32,128]{2,1,0:T(8,128)S(1)}, u32[]{:S(2)}, u32[]{:S(2)}) collective-permute-start(f32[13,32,128]{2,1,0:T(8,128)S(1)} %get-tuple-element.34), channel_id=1, source_target_pairs={{2,4},{4,2},{6,8},{8,6},{10,12},{12,10},{14,16},{16,14},{18,20},{2... | collective-permute-start | bytes 638984 | tf_op jit(solution)/shard_map/ppermute | solution.py:706
  8.2 0.7 %turn.1 = (f32[8,32,512]{2,1,0:T(8,128)S(1)}, f32[8,32,128]{2,1,0:T(8,128)S(1)}) custom-call(s32[2]{0:T(128)S(1)} %pad_add_fusion.place, f32[32,8,512]{2,1,0:T(8,128)S(1)} %copy-done.2), custom_call_target="tpu_custom_call" | custom-call | flops 805000000 | bytes 2583000 | tf_op jit(solution)/shard_map/turn/pallas_call | solution.py:650
  9.0 1.0 %top.1 = (f32[8,32,128]{2,1,0:T(8,128)S(1)}, f32[4,32,128]{2,1,0:T(8,128)S(1)}, f32[2,32,128]{2,1,0:T(8,128)S(1)}) custom-call(s32[2]{0:T(128)S(1)} %pad_add_fusion.place, f32[4,32,128]{2,1,0:T(8,128)S(1)} %get-tuple-element.30.own2.refs_2_, f32[2,8,32,128]{3,2,1,0:T(8,128)S(1)} %collective-permute-done.refs_0_.refs_4_.refs_9_), custom_call_target="tpu_custom_call" | custom-call | flops 1035000000 | bytes 3321000 | tf_op jit(solution)/shard_map/top/pallas_call | solution.py:650
  10.3 4.3 %collective-permute-done.1.refs_6_ = f32[13,32,128]{2,1,0:T(8,128)S(1)} collective-permute-done((f32[13,32,128]{2,1,0:T(8,128)S(1)}, f32[13,32,128]{2,1,0:T(8,128)S(1)}, u32[]{:S(2)}, u32[]{:S(2)}) %collective-permute-start.1) | collective-permute-done | bytes 213024 | tf_op jit(solution)/shard_map/ppermute | solution.py:706
  14.7 1.4 %collective-permute-done.2.refs_7_ = f32[13,32,128]{2,1,0:T(8,128)S(1)} collective-permute-done((f32[13,32,128]{2,1,0:T(8,128)S(1)}, f32[13,32,128]{2,1,0:T(8,128)S(1)}, u32[]{:S(2)}, u32[]{:S(2)}) %collective-permute-start.2) | collective-permute-done | bytes 213024 | tf_op jit(solution)/shard_map/ppermute | solution.py:706
  16.6 1.0 %collective-permute-done.4.refs_8_ = f32[13,32,128]{2,1,0:T(8,128)S(1)} collective-permute-done((f32[13,32,128]{2,1,0:T(8,128)S(1)}, f32[13,32,128]{2,1,0:T(8,128)S(1)}, u32[]{:S(2)}, u32[]{:S(2)}) %collective-permute-start.4) | collective-permute-done | bytes 213024 | tf_op jit(solution)/shard_map/ppermute | solution.py:670
  17.8 3.8 %down.1 = (f32[41,32,640]{2,1,0:T(8,128)S(1)}, f32[43,32,384]{2,1,0:T(8,128)S(1)}, f32[29,32,256]{2,1,0:T(8,128)S(1)}, f32[4,32,128]{2,1,0:T(8,128)S(1)}, f32[6,...) custom-call(s32[2]{0:T(128)S(1)} %pad_add_fusion.place, ...), custom_call_target="tpu_custom_call" | custom-call | flops 4140000000 | bytes 13284000 | tf_op jit(solution)/shard_map/down/pallas_call | solution.py:650
  21.7 1.2 %collective-permute-start.7 = (f32[6,32,128]{2,1,0:T(8,128)S(1)}, f32[6,32,128]{2,1,0:T(8,128)S(1)}, u32[]{:S(2)}, u32[]{:S(2)}) collective-permute-start(f32[6,32,128]{2,1,0:T(8,128)S(1)} %get-tuple-element.44), channel_id=1, source_target_pairs={{0,4},{2,6},{4,0},{6,2},{8,12},{10,14},{12,8},{14,10},{16,20},{18,... | collective-permute-start | bytes 294920 | tf_op jit(solution)/shard_map/ppermute | solution.py:696
  22.8 2.4 %collective-permute-start.8 = (f32[4,32,128]{2,1,0:T(8,128)S(1)}, f32[4,32,128]{2,1,0:T(8,128)S(1)}, u32[]{:S(2)}, u32[]{:S(2)}) collective-permute-start(f32[4,32,128]{2,1,0:T(8,128)S(1)} %get-tuple-element.43.refs_0_), channel_id=1, source_target_pairs={{0,6},{2,4},{4,2},{6,0},{8,14},{10,12},{12,10},{14,8},{16,22},{18,... | collective-permute-start | bytes 196616 | tf_op jit(solution)/shard_map/ppermute | solution.py:696
  25.2 3.4 %collective-permute-done.8.refs_3_ = f32[4,32,128]{2,1,0:T(8,128)S(1)} collective-permute-done((f32[4,32,128]{2,1,0:T(8,128)S(1)}, f32[4,32,128]{2,1,0:T(8,128)S(1)}, u32[]{:S(2)}, u32[]{:S(2)}) %collective-permute-start.8) | collective-permute-done | bytes 65568 | tf_op jit(solution)/shard_map/ppermute | solution.py:696
  28.6 0.8 %collective-permute-done.6.refs_1_ = f32[4,32,128]{2,1,0:T(8,128)S(1)} collective-permute-done((f32[4,32,128]{2,1,0:T(8,128)S(1)}, f32[4,32,128]{2,1,0:T(8,128)S(1)}, u32[]{:S(2)}, u32[]{:S(2)}) %collective-permute-start.6) | collective-permute-done | bytes 65568 | tf_op jit(solution)/shard_map/ppermute | solution.py:696
  29.5 0.9 %merge.1.refs_0_ = f32[9,32,128]{2,1,0:T(8,128)S(1)} custom-call(s32[2]{0:T(128)S(1)} %pad_add_fusion.place, f32[4,32,128]{2,1,0:T(8,128)S(1)} %get-tuple-element.43.refs_0_, f32[4,32,128]{2,1,0:T(8,128)S(1)} %collective-permute-done.6.refs_1_, f32[6,32,128]{2,1,0:T(8,128)S(1)} %collective-permute-done.7.refs_2_, ...), custom_call_target="tpu_custom_call" | custom-call | flops 1035000000 | bytes 3321000 | tf_op jit(solution)/shard_map/merge/pallas_call | solution.py:650
  30.9 3.5 %collective-permute-start.10 = (f32[9,32,128]{2,1,0:T(8,128)S(1)}, f32[9,32,128]{2,1,0:T(8,128)S(1)}, u32[]{:S(2)}, u32[]{:S(2)}) collective-permute-start(f32[9,32,128]{2,1,0:T(8,128)S(1)} %merge.1.refs_0_), channel_id=1, source_target_pairs={{0,16},{2,18},{4,20},{6,22},{8,24},{10,26},{12,28},{14,30},{16,0},... | collective-permute-start | bytes 442376 | tf_op jit(solution)/shard_map/ppermute | solution.py:696
  34.4 2.3 %collective-permute-start.14 = (f32[2,32,128]{2,1,0:T(8,128)S(1)}, f32[2,32,128]{2,1,0:T(8,128)S(1)}, u32[]{:S(2)}, u32[]{:S(2)}) collective-permute-start(f32[2,32,128]{2,1,0:T(8,128)S(1)} %get-tuple-element.47), channel_id=1, source_target_pairs={{4,8},{8,4},{6,10},{10,6},{12,16},{16,12},{14,18},{18,14},{20,24},... | collective-permute-start | bytes 98312 | tf_op jit(solution)/shard_map/ppermute | solution.py:706
  36.7 1.4 %collective-permute-start.12 = (f32[14,32,128]{2,1,0:T(8,128)S(1)}, f32[14,32,128]{2,1,0:T(8,128)S(1)}, u32[]{:S(2)}, u32[]{:S(2)}) collective-permute-start(f32[14,32,128]{2,1,0:T(8,128)S(1)} %get-tuple-element.45), channel_id=1, source_target_pairs={{0,2},{2,0},{4,6},{6,4},{8,10},{10,8},{12,14},{14,12},{16,18},{18,... | collective-permute-start | bytes 688136 | tf_op jit(solution)/shard_map/ppermute | solution.py:706
  38.1 4.7 %collective-permute-done.11.refs_3_ = f32[9,32,128]{2,1,0:T(8,128)S(1)} collective-permute-done((f32[9,32,128]{2,1,0:T(8,128)S(1)}, f32[9,32,128]{2,1,0:T(8,128)S(1)}, u32[]{:S(2)}, u32[]{:S(2)}) %collective-permute-start.11) | collective-permute-done | bytes 147488 | tf_op jit(solution)/shard_map/ppermute | solution.py:696
  42.9 2.5 %collective-permute-start.13 = (f32[14,32,128]{2,1,0:T(8,128)S(1)}, f32[14,32,128]{2,1,0:T(8,128)S(1)}, u32[]{:S(2)}, u32[]{:S(2)}) collective-permute-start(f32[14,32,128]{2,1,0:T(8,128)S(1)} %get-tuple-element.46), channel_id=1, source_target_pairs={{2,4},{4,2},{6,8},{8,6},{10,12},{12,10},{14,16},{16,14},{18,20},{2... | collective-permute-start | bytes 688136 | tf_op jit(solution)/shard_map/ppermute | solution.py:706
  45.4 2.9 %coarse.1 = f32[3,32,128]{2,1,0:T(8,128)S(1)} custom-call(s32[2]{0:T(128)S(1)} %pad_add_fusion.place, f32[9,32,128]{2,1,0:T(8,128)S(1)} %merge.1.refs_0_, f32[9,32,128]{2,1,0:T(8,128)S(1)} %collective-permute-done.9.refs_1_, f32[9,32,128]{2,1,0:T(8,128)S(1)} %collective-permute-done.10.refs_2_, f32[9,32,128]{2,1,0:T(8,128)S(1)} %collective-permute-done.11.refs_3_), custom_call_target="tpu_custom_call" | custom-call | flops 3335000064 | bytes 10701000 | tf_op jit(solution)/shard_map/coarse/pallas_call | solution.py:650
  48.4 4.2 %collective-permute-done.13.refs_1_ = f32[14,32,128]{2,1,0:T(8,128)S(1)} collective-permute-done((f32[14,32,128]{2,1,0:T(8,128)S(1)}, f32[14,32,128]{2,1,0:T(8,128)S(1)}, u32[]{:S(2)}, u32[]{:S(2)}) %collective-permute-start.13) | collective-permute-done | bytes 229408 | tf_op jit(solution)/shard_map/ppermute | solution.py:706
  52.6 3.1 %up.1 = f32[32,8,512]{2,1,0:T(8,128)} custom-call(s32[2]{0:T(128)S(1)} %pad_add_fusion.place, f32[3,32,128]{2,1,0:T(8,128)S(1)} %coarse.1, f32[14,32,128]{2,1,0:T(8,128)S(1)} %collective-permute-done.12.refs_0_, f32[14,32,128]{2,1,0:T(8,128)S(1)} %collective-permute-done.13.refs_1_, f32[6,32,128]{2,1,0:T(8,128)S(1)} %collective-permute-done.7.refs_2_, ...), custom_call_target="tpu_custom_call" | custom-call | flops 3449999872 | bytes 11070000 | tf_op jit(solution)/shard_map/up/pallas_call | solution.py:650
  (20 shorter events, 1.9 us)
Async XLA Ops:
  0.1 1.0 %copy-start = (f32[32,8,512]{2,1,0:T(8,128)S(1)}, f32[32,8,512]{2,1,0:T(8,128)}, u32[]{:S(2)}) copy-start(f32[32,8,512]{2,1,0:T(8,128)} %conduct.1) | copy-start | bytes 1572868
  1.1 1.0 %copy-start.1 = (f32[32,8,512]{2,1,0:T(8,128)S(1)}, f32[32,8,512]{2,1,0:T(8,128)}, u32[]{:S(2)}) copy-start(f32[32,8,512]{2,1,0:T(8,128)} %binding.1) | copy-start | bytes 1572868
  2.2 6.1 %copy-start.2 = (f32[32,8,512]{2,1,0:T(8,128)S(1)}, f32[32,8,512]{2,1,0:T(8,128)}, u32[]{:S(2)}) copy-start(f32[32,8,512]{2,1,0:T(8,128)} %right_side.1) | copy-start | bytes 1572868
  3.3 5.7 %collective-permute-start = (f32[2,8,32,128]{3,2,1,0:T(8,128)S(1)}, f32[2,8,32,128]{3,2,1,0:T(8,128)S(1)}, u32[]{:S(2)}, u32[]{:S(2)}) collective-permute-start(f32[2,8,32,128]{3,2,1,0:T(8,128)S(1)} %get-tuple-element.32), channel_id=1, source_target_pairs={{0,1},{1,0},{2,3},{3,2},{4,5},{5,4},{6,7},{7,6},{8,9},{9,8},{10,11... | collective-permute-start | bytes 786440 | tf_op jit(solution)/shard_map/ppermute | solution.py:678
  3.4 11.3 %collective-permute-start.1 = (f32[13,32,128]{2,1,0:T(8,128)S(1)}, f32[13,32,128]{2,1,0:T(8,128)S(1)}, u32[]{:S(2)}, u32[]{:S(2)}) collective-permute-start(f32[13,32,128]{2,1,0:T(8,128)S(1)} %get-tuple-element.33), channel_id=1, source_target_pairs={{0,2},{2,0},{4,6},{6,4},{8,10},{10,8},{12,14},{14,12},{16,18},{18,... | collective-permute-start | bytes 638984 | tf_op jit(solution)/shard_map/ppermute | solution.py:706
  5.0 11.1 %collective-permute-start.2 = (f32[13,32,128]{2,1,0:T(8,128)S(1)}, f32[13,32,128]{2,1,0:T(8,128)S(1)}, u32[]{:S(2)}, u32[]{:S(2)}) collective-permute-start(f32[13,32,128]{2,1,0:T(8,128)S(1)} %get-tuple-element.34), channel_id=1, source_target_pairs={{2,4},{4,2},{6,8},{8,6},{10,12},{12,10},{14,16},{16,14},{18,20},{2... | collective-permute-start | bytes 638984 | tf_op jit(solution)/shard_map/ppermute | solution.py:706
  8.9 1.4 %collective-permute-start.3 = (f32[8,32,128]{2,1,0:T(8,128)S(1)}, f32[8,32,128]{2,1,0:T(8,128)S(1)}, u32[]{:S(2)}, u32[]{:S(2)}) collective-permute-start(f32[8,32,128]{2,1,0:T(8,128)S(1)} %get-tuple-element.36), channel_id=1, source_target_pairs={{0,1},{1,0},{2,3},{3,2},{4,5},{5,4},{6,7},{7,6},{8,9},{9,8},{10,11... | collective-permute-start | bytes 393224 | tf_op jit(solution)/shard_map/ppermute | solution.py:678
  16.1 1.5 %collective-permute-start.4 = (f32[13,32,128]{2,1,0:T(8,128)S(1)}, f32[13,32,128]{2,1,0:T(8,128)S(1)}, u32[]{:S(2)}, u32[]{:S(2)}) collective-permute-start(f32[13,32,128]{2,1,0:T(8,128)S(1)} %collective-permute-done.1.refs_6_), channel_id=1, source_target_pairs={{0,1},{1,0},{2,3},{3,2},{4,5},{5,4},{6,7},{7,6},{8,9},{9,8},{10,11... | collective-permute-start | bytes 638984 | tf_op jit(solution)/shard_map/ppermute | solution.py:670
  16.1 1.8 %collective-permute-start.5 = (f32[13,32,128]{2,1,0:T(8,128)S(1)}, f32[13,32,128]{2,1,0:T(8,128)S(1)}, u32[]{:S(2)}, u32[]{:S(2)}) collective-permute-start(f32[13,32,128]{2,1,0:T(8,128)S(1)} %collective-permute-done.2.refs_7_), channel_id=1, source_target_pairs={{0,1},{1,0},{2,3},{3,2},{4,5},{5,4},{6,7},{7,6},{8,9},{9,8},{10,11... | collective-permute-start | bytes 638984 | tf_op jit(solution)/shard_map/ppermute | solution.py:670
  21.7 7.8 %collective-permute-start.7 = (f32[6,32,128]{2,1,0:T(8,128)S(1)}, f32[6,32,128]{2,1,0:T(8,128)S(1)}, u32[]{:S(2)}, u32[]{:S(2)}) collective-permute-start(f32[6,32,128]{2,1,0:T(8,128)S(1)} %get-tuple-element.44), channel_id=1, source_target_pairs={{0,4},{2,6},{4,0},{6,2},{8,12},{10,14},{12,8},{14,10},{16,20},{18,... | collective-permute-start | bytes 294920 | tf_op jit(solution)/shard_map/ppermute | solution.py:696
  22.8 5.8 %collective-permute-start.8 = (f32[4,32,128]{2,1,0:T(8,128)S(1)}, f32[4,32,128]{2,1,0:T(8,128)S(1)}, u32[]{:S(2)}, u32[]{:S(2)}) collective-permute-start(f32[4,32,128]{2,1,0:T(8,128)S(1)} %get-tuple-element.43.refs_0_), channel_id=1, source_target_pairs={{0,6},{2,4},{4,2},{6,0},{8,14},{10,12},{12,10},{14,8},{16,22},{18,... | collective-permute-start | bytes 196616 | tf_op jit(solution)/shard_map/ppermute | solution.py:696
  25.2 4.3 %collective-permute-start.6 = (f32[4,32,128]{2,1,0:T(8,128)S(1)}, f32[4,32,128]{2,1,0:T(8,128)S(1)}, u32[]{:S(2)}, u32[]{:S(2)}) collective-permute-start(f32[4,32,128]{2,1,0:T(8,128)S(1)} %get-tuple-element.43.refs_0_), channel_id=1, source_target_pairs={{0,2},{2,0},{4,6},{6,4},{8,10},{10,8},{12,14},{14,12},{16,18},{18,... | collective-permute-start | bytes 196616 | tf_op jit(solution)/shard_map/ppermute | solution.py:696
  30.3 12.5 %collective-permute-start.11 = (f32[9,32,128]{2,1,0:T(8,128)S(1)}, f32[9,32,128]{2,1,0:T(8,128)S(1)}, u32[]{:S(2)}, u32[]{:S(2)}) collective-permute-start(f32[9,32,128]{2,1,0:T(8,128)S(1)} %merge.1.refs_0_), channel_id=1, source_target_pairs={{0,24},{2,26},{4,28},{6,30},{8,16},{10,18},{12,20},{14,22},{16,8},... | collective-permute-start | bytes 442376 | tf_op jit(solution)/shard_map/ppermute | solution.py:696
  30.9 14.5 %collective-permute-start.10 = (f32[9,32,128]{2,1,0:T(8,128)S(1)}, f32[9,32,128]{2,1,0:T(8,128)S(1)}, u32[]{:S(2)}, u32[]{:S(2)}) collective-permute-start(f32[9,32,128]{2,1,0:T(8,128)S(1)} %merge.1.refs_0_), channel_id=1, source_target_pairs={{0,16},{2,18},{4,20},{6,22},{8,24},{10,26},{12,28},{14,30},{16,0},... | collective-permute-start | bytes 442376 | tf_op jit(solution)/shard_map/ppermute | solution.py:696
  34.3 11.0 %collective-permute-start.9 = (f32[9,32,128]{2,1,0:T(8,128)S(1)}, f32[9,32,128]{2,1,0:T(8,128)S(1)}, u32[]{:S(2)}, u32[]{:S(2)}) collective-permute-start(f32[9,32,128]{2,1,0:T(8,128)S(1)} %merge.1.refs_0_), channel_id=1, source_target_pairs={{0,8},{2,10},{4,12},{6,14},{8,0},{10,2},{12,4},{14,6},{16,24},{18,... | collective-permute-start | bytes 442376 | tf_op jit(solution)/shard_map/ppermute | solution.py:696
  34.4 14.0 %collective-permute-start.14 = (f32[2,32,128]{2,1,0:T(8,128)S(1)}, f32[2,32,128]{2,1,0:T(8,128)S(1)}, u32[]{:S(2)}, u32[]{:S(2)}) collective-permute-start(f32[2,32,128]{2,1,0:T(8,128)S(1)} %get-tuple-element.47), channel_id=1, source_target_pairs={{4,8},{8,4},{6,10},{10,6},{12,16},{16,12},{14,18},{18,14},{20,24},... | collective-permute-start | bytes 98312 | tf_op jit(solution)/shard_map/ppermute | solution.py:706
  36.7 11.7 %collective-permute-start.12 = (f32[14,32,128]{2,1,0:T(8,128)S(1)}, f32[14,32,128]{2,1,0:T(8,128)S(1)}, u32[]{:S(2)}, u32[]{:S(2)}) collective-permute-start(f32[14,32,128]{2,1,0:T(8,128)S(1)} %get-tuple-element.45), channel_id=1, source_target_pairs={{0,2},{2,0},{4,6},{6,4},{8,10},{10,8},{12,14},{14,12},{16,18},{18,... | collective-permute-start | bytes 688136 | tf_op jit(solution)/shard_map/ppermute | solution.py:706
  42.9 9.7 %collective-permute-start.13 = (f32[14,32,128]{2,1,0:T(8,128)S(1)}, f32[14,32,128]{2,1,0:T(8,128)S(1)}, u32[]{:S(2)}, u32[]{:S(2)}) collective-permute-start(f32[14,32,128]{2,1,0:T(8,128)S(1)} %get-tuple-element.46), channel_id=1, source_target_pairs={{2,4},{4,2},{6,8},{8,6},{10,12},{12,10},{14,16},{16,14},{18,20},{2... | collective-permute-start | bytes 688136 | tf_op jit(solution)/shard_map/ppermute | solution.py:706

commit v11 on v10

--- a/solution.py
+++ b/solution.py
@@ -211,7 +211,7 @@
     return [n + 3] + [n + 2] * 6
 
 
-def start_kernel(sizes, place, conduct, binding, own0, own1, own2, first, second, *refs):
+def start_kernel(sizes, place, conduct, binding, own0, own1, own2, first, second, top, *refs):
     edges, sums = refs[: sizes.sides], refs[-1]
     n0, n1, n2 = sizes.rows[:3]
     for at, array in enumerate((conduct, binding)):
@@ -223,6 +223,9 @@
     for row in range(2 * n2):
         sums[row, :, : sizes.own[1] * LANES] = own1[2 * row] + own1[2 * row + 1]
     narrow(sizes, place, 1, sums, own2, 2 * n2, "own")
+    last = jnp.concatenate([own2[0] + own2[1], own2[n2] + own2[n2 + 1]], axis=0)
+    last = dot(split(last), pair_table(LANES, 0, None, 0.25))
+    top[0] = last[: sizes.depth] + roll(last[sizes.depth :], LANES // 2, 1)
     ends = []
     for low, at1, at0 in ((n1 - 2, n1 - 1, n0 - 1), (0, 0, 0)):
         edge = n2 - 1 if at0 else 0
@@ -354,28 +357,46 @@
     return rows
 
 
-def merge_into(sizes, place, stride, radix, arrays, source, tops):
+def merge_into(sizes, place, stride, radix, arrays, source):
     position = (place[0] // stride) % radix
     source[...] = jnp.zeros(source.shape, f32)
     for step, array in enumerate(arrays):
         at = (position ^ step) * stride
-        rows = unpack_rows(sizes, place, array, 3 * stride + 2)
-        for index, row in enumerate(rows[: stride + 2]):
+        for index, row in enumerate(unpack_rows(sizes, place, array, stride + 2)):
             source[at + index] = source[at + index] + row
-        for kind, top in enumerate(tops):
-            for index in range(stride):
-                top[at + index] = rows[stride + 2 + kind * stride + index]
 
 
 def merge_kernel(sizes, stride, radix, place, *refs):
-    arrays, out, (source, *tops) = refs[:radix], refs[radix], refs[radix + 1 :]
-    merge_into(sizes, place, stride, radix, arrays, source, tops)
-    pack_rows(sizes, place, [array[row] for array in (source, *tops) for row in range(array.shape[0])], out)
-
-
-def top_kernel(sizes, place, own2, *refs):
+    arrays, out, source = refs[:radix], refs[radix], refs[radix + 1]
+    merge_into(sizes, place, stride, radix, arrays, source)
+    pack_rows(sizes, place, [source[row] for row in range(source.shape[0])], out)
+
+
+def top_row(sizes, place, block, beside):
+    half, reach = LANES // 2, BORDER >> 3
+    lane = lane_at(block.shape)
+    values = [jnp.where(lane < half, block, 0.0), jnp.where(lane < half, pltpu.roll(block, half, axis=1), 0.0)]
+    for side, other in enumerate(beside):
+        first = LANES - reach if side else half
+        if sizes.sides == 1:
+            first = jnp.where(place[1] == 0, half, LANES - reach)
+        here = (lane >= first) & (lane < first + reach)
+        values[0] = jnp.where(here, pltpu.roll(other, half, axis=1), values[0])
+        values[1] = jnp.where(here, other, values[1])
+    return values
+
+
+def column_kernel(sizes, place, column, *refs):
+    beside, out = refs[: sizes.sides], refs[sizes.sides]
+    rows = []
+    for index in range(column.shape[0]):
+        rows += top_row(sizes, place, column[index], [other[index] for other in beside])
+    pack_rows(sizes, place, rows, out)
+
+
+def border_kernel(sizes, place, *refs):
     s = sizes.sides
-    borders0, (border1, border2, top, sums) = refs[:s], refs[s:]
+    borders0, (border1, border2, sums) = refs[:s], refs[s:]
     n1, n2 = sizes.rows[1:3]
     if s:
         for row in range(2 * n1):
@@ -387,12 +408,6 @@
         for row in range(2 * n2):
             sums[row, :, :LANES] = border1[2 * row] + border1[2 * row + 1]
         narrow(sizes, place, 1, sums, border2, 2 * n2, "border", sizes.own[1] * LANES)
-    for at in (0, 1):
-        row = at * n2
-        sums[at, :, :LANES] = own2[row] + own2[row + 1]
-        if s:
-            sums[at, :, LANES : 2 * LANES] = border2[row] + border2[row + 1]
-    narrow(sizes, place, 2, sums, top, 2)
 
 
 def down_kernel(sizes, place, *refs):
@@ -404,7 +419,6 @@
     from_prev, *beside_prev = (Arrived(place, pair, 0) for pair in pairs_of)
     from_next, *beside_next = (Arrived(place, pair, 1) for pair in pairs_of)
     (border1, border2), refs = refs[:2], refs[2:]
-    top, refs = refs[0], refs[1:]
     coefs, contribution, with_far, ups, far, refs = refs[:3], refs[3], refs[4], refs[5:7], refs[7], refs[8:]
     level3, sums = refs
     slots = sizes.slots
@@ -468,9 +482,8 @@
         sources.append(source)
     narrow(sizes, place, 2, sums.at[:, :, : sizes.held[2]], level3, 3)
 
-    rows = [level3[row] for row in range(3)] + [top[0], top[1]]
-    tiles = packing(sizes, len(rows))[1]
-    pack_rows(sizes, place, rows, contribution)
+    tiles = packing(sizes, 3)[1]
+    pack_rows(sizes, place, [level3[row] for row in range(3)], contribution)
     with_far[0:tiles] = contribution[...]
     (s1, s2), (v1, v2) = sources, smooths
     next_rows = (v0[n0 - 1], s1[n1], s1[n1 + 1], v1[n1 - 1], s2[n2], s2[n2 + 1], v2[n2 - 1])
@@ -500,12 +513,21 @@
     return put_row
 
 
-def coarse_kernel(sizes, stride, radix, place, *refs):
+def coarse_kernel(sizes, stride, radix, low_stride, place, *refs):
     blocks, refs = refs[:radix], refs[radix:]
+    groups, refs = refs[: stride // low_stride], refs[stride // low_stride :]
     out, merged, sums = refs[:3]
     coarse = [refs[3 + 9 * index : 12 + 9 * index] for index in range(3)]
     total = sizes.span_count
-    merge_into(sizes, place, stride, radix, blocks, merged, (coarse[0][4].at[1 : total + 1], coarse[0][5]))
+    merge_into(sizes, place, stride, radix, blocks, merged)
+    tiles = packing(sizes, 2 * radix)[1]
+    for step, group in enumerate(groups):
+        for low in range(low_stride):
+            rows = unpack_rows(sizes, place, group.at[low * tiles : (low + 1) * tiles], 2 * radix)
+            for high in range(radix):
+                row = place[0] ^ (step * low_stride + low + high * stride)
+                coarse[0][4][row + 1] = rows[2 * high]
+                coarse[0][5][row] = rows[2 * high + 1]
     zero = jnp.zeros((sizes.depth, LANES), f32)
     for index in range(3):
         level = 3 + index
@@ -717,17 +739,19 @@
     held = [(depth, count) for count in sizes.held]
     down_message = (sizes.tiles, *tile)
     up_message = (sizes.tiles + 1, *tile)
-    own0, own1, own2, first, second, *edges = call(
+    own0, own1, own2, first, second, top, *edges = call(
         functools.partial(start_kernel, sizes),
         "start",
         1.1,
-        [(2, n0, *own[0]), (2 * n1, *own[1]), (2 * n2, *own[2]), down_message, down_message]
+        [(2, n0, *own[0]), (2 * n1, *own[1]), (2 * n2, *own[2]), down_message, down_message, (1, *tile)]
         + [(2, n0, depth, BORDER)] * s,
         [(2 * n1, *own[0])],
         place,
         [diffusivity, reaction],
     )
     borders = edge_columns(edges, sizes)
+    plan = list(stages(sizes.span_count))
+    column = jnp.concatenate(swap(top, *plan[-1]))
     halos = exchange([first, second], 1)
     turned, *edges = call(
         functools.partial(turn_kernel, sizes),
@@ -739,19 +763,32 @@
         [right_side],
     )
     borders_r = edge_columns(edges, sizes)
-    plan = list(stages(sizes.span_count))
-    border1, border2, top = call(
-        functools.partial(top_kernel, sizes),
-        "top",
-        0.9,
-        [(2 * n1, *tile), (2 * n2, *tile), (2, *tile)],
+    border1, border2 = call(
+        functools.partial(border_kernel, sizes),
+        "border",
+        0.8,
+        [(2 * n1, *tile), (2 * n2, *tile)],
         [(2 * n1, depth, 2 * LANES)],
         place,
-        [own2, *borders],
+        borders,
     )
-    halos, top, borders_r = lax.optimization_barrier((halos, top, borders_r))
+    tiles = packing(sizes, 2 * plan[-1][1])[1]
+    (packed,) = call(
+        functools.partial(column_kernel, sizes),
+        "column",
+        0.6,
+        [(tiles, *tile)],
+        [],
+        place,
+        [column, *(side[0] for side in beside([column], sizes))],
+    )
+    halos, packed, border1, borders_r = lax.optimization_barrier((halos, packed, border1, borders_r))
     sides = beside(halos, sizes)
-    part = packing(sizes, 5)[1]
+    for stride, radix in plan[:-1]:
+        groups = swap(packed, stride, radix)
+        packed = jnp.concatenate(groups) if (stride, radix) != plan[-2] else packed
+    sides, groups = lax.optimization_barrier((sides, groups))
+    part = packing(sizes, 3)[1]
     lengths = [sum(coefficient_rows(sizes, level)) for level in range(3)]
     far = (sizes.held[2] // LANES, *tile)
     coefs = [(lengths[level], *held[level]) for level in range(3)]
@@ -762,39 +799,42 @@
         [*coefs, (part, *tile), (part + far[0], *tile), up_message, up_message, far],
         [(3, *tile), (n1 + 2, *held[0])],
         place,
-        [own0, own1, own2, turned, *borders, *borders_r, *halos, *sum(sides, []), border1, border2, top],
+        [own0, own1, own2, turned, *borders, *borders_r, *halos, *sum(sides, []), border1, border2],
     )
-    coefs_out, blocks, with_far, ups, far_second = downs[:3], downs[3], downs[4], downs[5:7], downs[7]
+    coefs_out, blocks, with_far, ups, far_second = downs[:3], downs[3], downs[4], list(downs[5:7]), downs[7]
     far_first = None
     for stride, radix in plan[:-1]:
         count = stride * radix
         blocks = swap(blocks, stride, radix, None if far_first is not None else {2: with_far})
-        far_first = blocks[2] if far_first is None else far_first
+        if far_first is None:
+            far_first = blocks[2]
+            blocks, ups[0] = lax.optimization_barrier((blocks, ups[0]))
         (blocks,) = call(
             functools.partial(merge_kernel, sizes, stride, radix),
             "merge",
             0.9,
-            [(packing(sizes, 3 * count + 2)[1], *tile)],
-            [(count + 2, *tile), (count, *tile), (count, *tile)],
+            [(packing(sizes, count + 2)[1], *tile)],
+            [(count + 2, *tile)],
             place,
             blocks,
         )
     stride, radix = plan[-1]
     blocks = swap(blocks, stride, radix)
     received = exchange(ups, 1) + [far_first, exchange([None, far_second], 2)[1]]
+    blocks, received[0] = lax.optimization_barrier((blocks, received[0]))
     scratch = [(sizes.span_count + 2, *tile), (max(sizes.span_count // 2, 2), *tile)]
     for index in range(3):
         count = sizes.span_count >> index
         scratch += [(count + 1, *tile)] + [(count, *tile)] * 3 + [(count + 2, *tile)] + [(count, *tile)] * 2
         scratch += [(count + 2, *tile)] * 2
     (coarse,) = call(
-        functools.partial(coarse_kernel, sizes, stride, radix),
+        functools.partial(coarse_kernel, sizes, stride, radix, plan[-2][0]),
         "coarse",
         2.9,
         [(n3 + 2, *tile)],
         scratch,
         place,
-        blocks,
+        [*blocks, *groups],
     )
     scratch = [(n1 + 2, *held[1]), (n2 + 2, *held[2]), diffusivity.shape]
     scratch += [(n3 + 2, *held[2]), (n2 + 2, *held[1]), (n1 + 2, *held[0])]

time: 55.9 us -> 59.6 us (1.066)
  the two profiles are of different devices: /device:TPU:16 before, /device:TPU:20 now
where the time goes in v11:
time: 59.6 us; the launch traced here: 59.4 us
  starting transfers between devices  27.9 us (47%)
  waiting for transfers between devices  14.9 us (25%)
  Pallas kernels  14.2 us (24%)
  local copies, waits for them, and re-layouts  2.1 us (4%)
    ppermute x12, starting transfers between devices, swap(): lax.ppermute(others.get(step, value), 'span', [(device, device ^ step * s...  15.2 us
    pallas_call x8, Pallas kernels, call(): pl.pallas_call(body, name=name, out_shape=[jax.ShapeDtypeStruct(shape, f3...  14.2 us
    ppermute x5, starting transfers between devices, exchange(): lax.ppermute(value, 'span', route)  11.5 us
    ppermute x5, waiting for transfers between devices, exchange(): lax.ppermute(value, 'span', route)  7.69 us
    ppermute x12, waiting for transfers between devices, swap(): lax.ppermute(others.get(step, value), 'span', [(device, device ^ step * s...  6.89 us
    unnamed x9, local copies, waits for them, and re-layouts  2.1 us
  transfers between devices with their start and end apart: 22, of which 7 were waited for; matrix products, arithmetic and copies ran while one was open for 0% of the time, Pallas kernels for 10%

profile of v11, /device:TPU:20, one launch (start us, length us, event | category | flops | bytes accessed | tf_op | source)
XLA Modules:
  0.0 59.4 jit_solution(9456977032049498679)
XLA Ops:
  0.1 1.0 %copy-done = f32[32,8,512]{2,1,0:T(8,128)S(1)} copy-done((f32[32,8,512]{2,1,0:T(8,128)S(1)}, f32[32,8,512]{2,1,0:T(8,128)}, u32[]{:S(2)}) %copy-start) | copy-done | bytes 524312
  1.1 1.0 %copy-done.1 = f32[32,8,512]{2,1,0:T(8,128)S(1)} copy-done((f32[32,8,512]{2,1,0:T(8,128)S(1)}, f32[32,8,512]{2,1,0:T(8,128)}, u32[]{:S(2)}) %copy-start.1) | copy-done | bytes 524312
  2.2 1.3 %start.1 = (f32[2,8,32,512]{3,2,1,0:T(8,128)S(1)}, f32[8,32,256]{2,1,0:T(8,128)S(1)}, f32[4,32,128]{2,1,0:T(8,128)S(1)}, f32[13,32,128]{2,1,0:T(8,128)S(1)}, f32...) custom-call(s32[2]{0:T(128)S(1)} %pad_add_fusion.place, ...), custom_call_target="tpu_custom_call" | custom-call | flops 1264999936 | bytes 4059000 | tf_op jit(solution)/shard_map/start/pallas_call | solution.py:672
  4.0 3.5 %collective-permute-start.4 = (f32[1,32,128]{2,1,0:T(8,128)S(1)}, f32[1,32,128]{2,1,0:T(8,128)S(1)}, u32[]{:S(2)}, u32[]{:S(2)}) collective-permute-start(f32[1,32,128]{2,1,0:T(8,128)S(1)} %get-tuple-element.52), channel_id=1, source_target_pairs={{0,16},{2,18},{4,20},{6,22},{8,24},{10,26},{12,28},{14,30},{16,0},... | collective-permute-start | bytes 49160 | tf_op jit(solution)/shard_map/ppermute | solution.py:718
  7.5 1.5 %collective-permute-start.1 = (f32[13,32,128]{2,1,0:T(8,128)S(1)}, f32[13,32,128]{2,1,0:T(8,128)S(1)}, u32[]{:S(2)}, u32[]{:S(2)}) collective-permute-start(f32[13,32,128]{2,1,0:T(8,128)S(1)} %get-tuple-element.50), channel_id=1, source_target_pairs={{0,2},{2,0},{4,6},{6,4},{8,10},{10,8},{12,14},{14,12},{16,18},{18,... | collective-permute-start | bytes 638984 | tf_op jit(solution)/shard_map/ppermute | solution.py:728
  8.9 2.4 %collective-permute-start.2 = (f32[13,32,128]{2,1,0:T(8,128)S(1)}, f32[13,32,128]{2,1,0:T(8,128)S(1)}, u32[]{:S(2)}, u32[]{:S(2)}) collective-permute-start(f32[13,32,128]{2,1,0:T(8,128)S(1)} %get-tuple-element.51), channel_id=1, source_target_pairs={{2,4},{4,2},{6,8},{8,6},{10,12},{12,10},{14,16},{16,14},{18,20},{2... | collective-permute-start | bytes 638984 | tf_op jit(solution)/shard_map/ppermute | solution.py:728
  13.0 0.7 %column.1.refs_4_ = f32[5,32,128]{2,1,0:T(8,128)S(1)} custom-call(s32[2]{0:T(128)S(1)} %pad_add_fusion.place, f32[4,32,128]{2,1,0:T(8,128)S(1)} %constant_dynamic-update-slice_fusion.column, f32[4,32,128]{2,1,0:T(8,128)S(1)} %collective-permute-done.6.refs_0_), custom_call_target="tpu_custom_call" | custom-call | flops 690000000 | bytes 2214000 | tf_op jit(solution)/shard_map/column/pallas_call | solution.py:672
  13.8 0.9 %border.1 = (f32[8,32,128]{2,1,0:T(8,128)S(1)}, f32[4,32,128]{2,1,0:T(8,128)S(1)}) custom-call(s32[2]{0:T(128)S(1)} %pad_add_fusion.place, f32[2,8,32,128]{3,2,1,0:T(8,128)S(1)} %collective-permute-done.refs_0_.refs_4_.refs_9_), custom_call_target="tpu_custom_call" | custom-call | flops 920000000 | bytes 2952000 | tf_op jit(solution)/shard_map/border/pallas_call | solution.py:672
  14.7 3.8 %collective-permute-done.1.refs_6_ = f32[13,32,128]{2,1,0:T(8,128)S(1)} collective-permute-done((f32[13,32,128]{2,1,0:T(8,128)S(1)}, f32[13,32,128]{2,1,0:T(8,128)S(1)}, u32[]{:S(2)}, u32[]{:S(2)}) %collective-permute-start.1) | collective-permute-done | bytes 213024 | tf_op jit(solution)/shard_map/ppermute | solution.py:728
  19.0 2.4 %collective-permute-start.12 = (f32[5,32,128]{2,1,0:T(8,128)S(1)}, f32[5,32,128]{2,1,0:T(8,128)S(1)}, u32[]{:S(2)}, u32[]{:S(2)}) collective-permute-start(f32[5,32,128]{2,1,0:T(8,128)S(1)} %column.1.refs_4_), channel_id=1, source_target_pairs={{0,6},{2,4},{4,2},{6,0},{8,14},{10,12},{12,10},{14,8},{16,22},{18,... | collective-permute-start | bytes 245768 | tf_op jit(solution)/shard_map/ppermute | solution.py:718
  21.4 1.1 %collective-permute-start.10 = (f32[5,32,128]{2,1,0:T(8,128)S(1)}, f32[5,32,128]{2,1,0:T(8,128)S(1)}, u32[]{:S(2)}, u32[]{:S(2)}) collective-permute-start(f32[5,32,128]{2,1,0:T(8,128)S(1)} %column.1.refs_4_), channel_id=1, source_target_pairs={{0,2},{2,0},{4,6},{6,4},{8,10},{10,8},{12,14},{14,12},{16,18},{18,... | collective-permute-start | bytes 245768 | tf_op jit(solution)/shard_map/ppermute | solution.py:718
  22.5 1.9 %collective-permute-done.12.refs_7_ = f32[5,32,128]{2,1,0:T(8,128)S(1)} collective-permute-done((f32[5,32,128]{2,1,0:T(8,128)S(1)}, f32[5,32,128]{2,1,0:T(8,128)S(1)}, u32[]{:S(2)}, u32[]{:S(2)}) %collective-permute-start.12) | collective-permute-done | bytes 81952 | tf_op jit(solution)/shard_map/ppermute | solution.py:718
  24.4 1.7 %collective-permute-done.11.refs_6_ = f32[5,32,128]{2,1,0:T(8,128)S(1)} collective-permute-done((f32[5,32,128]{2,1,0:T(8,128)S(1)}, f32[5,32,128]{2,1,0:T(8,128)S(1)}, u32[]{:S(2)}, u32[]{:S(2)}) %collective-permute-start.11) | collective-permute-done | bytes 81952 | tf_op jit(solution)/shard_map/ppermute | solution.py:718
  26.1 3.8 %down.1 = (f32[41,32,640]{2,1,0:T(8,128)S(1)}, f32[43,32,384]{2,1,0:T(8,128)S(1)}, f32[29,32,256]{2,1,0:T(8,128)S(1)}, f32[2,32,128]{2,1,0:T(8,128)S(1)}, f32[4,...) custom-call(s32[2]{0:T(128)S(1)} %pad_add_fusion.place, ...), custom_call_target="tpu_custom_call" | custom-call | flops 4140000000 | bytes 13284000 | tf_op jit(solution)/shard_map/down/pallas_call | solution.py:672
  29.9 1.8 %collective-permute-start.14 = (f32[4,32,128]{2,1,0:T(8,128)S(1)}, f32[4,32,128]{2,1,0:T(8,128)S(1)}, u32[]{:S(2)}, u32[]{:S(2)}) collective-permute-start(f32[4,32,128]{2,1,0:T(8,128)S(1)} %get-tuple-element.64), channel_id=1, source_target_pairs={{0,4},{2,6},{4,0},{6,2},{8,12},{10,14},{12,8},{14,10},{16,20},{18,... | collective-permute-start | bytes 196616 | tf_op jit(solution)/shard_map/ppermute | solution.py:718
  31.7 1.1 %collective-permute-start.15 = (f32[2,32,128]{2,1,0:T(8,128)S(1)}, f32[2,32,128]{2,1,0:T(8,128)S(1)}, u32[]{:S(2)}, u32[]{:S(2)}) collective-permute-start(f32[2,32,128]{2,1,0:T(8,128)S(1)} %get-tuple-element.66.refs_0_), channel_id=1, source_target_pairs={{0,6},{2,4},{4,2},{6,0},{8,14},{10,12},{12,10},{14,8},{16,22},{18,... | collective-permute-start | bytes 98312 | tf_op jit(solution)/shard_map/ppermute | solution.py:718
  33.4 3.1 %collective-permute-done.15.refs_3_ = f32[2,32,128]{2,1,0:T(8,128)S(1)} collective-permute-done((f32[2,32,128]{2,1,0:T(8,128)S(1)}, f32[2,32,128]{2,1,0:T(8,128)S(1)}, u32[]{:S(2)}, u32[]{:S(2)}) %collective-permute-start.15) | collective-permute-done | bytes 32800 | tf_op jit(solution)/shard_map/ppermute | solution.py:718
  37.3 0.8 %merge.1.refs_0_ = f32[4,32,128]{2,1,0:T(8,128)S(1)} custom-call(s32[2]{0:T(128)S(1)} %pad_add_fusion.place, f32[2,32,128]{2,1,0:T(8,128)S(1)} %get-tuple-element.66.refs_0_, f32[2,32,128]{2,1,0:T(8,128)S(1)} %collective-permute-done.13.refs_1_, f32[4,32,128]{2,1,0:T(8,128)S(1)} %collective-permute-done.14.refs_2_, ...), custom_call_target="tpu_custom_call" | custom-call | flops 1035000000 | bytes 3321000 | tf_op jit(solution)/shard_map/merge/pallas_call | solution.py:672
  38.8 3.5 %collective-permute-start.17 = (f32[4,32,128]{2,1,0:T(8,128)S(1)}, f32[4,32,128]{2,1,0:T(8,128)S(1)}, u32[]{:S(2)}, u32[]{:S(2)}) collective-permute-start(f32[4,32,128]{2,1,0:T(8,128)S(1)} %merge.1.refs_0_), channel_id=1, source_target_pairs={{0,16},{2,18},{4,20},{6,22},{8,24},{10,26},{12,28},{14,30},{16,0},... | collective-permute-start | bytes 196616 | tf_op jit(solution)/shard_map/ppermute | solution.py:718
  42.3 5.1 %collective-permute-start.21 = (f32[2,32,128]{2,1,0:T(8,128)S(1)}, f32[2,32,128]{2,1,0:T(8,128)S(1)}, u32[]{:S(2)}, u32[]{:S(2)}) collective-permute-start(f32[2,32,128]{2,1,0:T(8,128)S(1)} %get-tuple-element.81), channel_id=1, source_target_pairs={{4,8},{8,4},{6,10},{10,6},{12,16},{16,12},{14,18},{18,14},{20,24},... | collective-permute-start | bytes 98312 | tf_op jit(solution)/shard_map/ppermute | solution.py:728
  47.4 1.9 %collective-permute-start.20 = (f32[14,32,128]{2,1,0:T(8,128)S(1)}, f32[14,32,128]{2,1,0:T(8,128)S(1)}, u32[]{:S(2)}, u32[]{:S(2)}) collective-permute-start(f32[14,32,128]{2,1,0:T(8,128)S(1)} %get-tuple-element.80), channel_id=1, source_target_pairs={{2,4},{4,2},{6,8},{8,6},{10,12},{12,10},{14,16},{16,14},{18,20},{2... | collective-permute-start | bytes 688136 | tf_op jit(solution)/shard_map/ppermute | solution.py:728
  49.4 2.9 %coarse.1 = f32[3,32,128]{2,1,0:T(8,128)S(1)} custom-call(s32[2]{0:T(128)S(1)} %pad_add_fusion.place, f32[4,32,128]{2,1,0:T(8,128)S(1)} %merge.1.refs_0_, f32[4,32,128]{2,1,0:T(8,128)S(1)} %collective-permute-done.16.refs_1_, f32[4,32,128]{2,1,0:T(8,128)S(1)} %collective-permute-done.17.refs_2_, f32[4,32,128]{2,1,0:T(8,128)S(1)} %collective-permute-done.18.refs_3_, ...), custom_call_target="tpu_custom_call" | custom-call | flops 3335000064 | bytes 10701000 | tf_op jit(solution)/shard_map/coarse/pallas_call | solution.py:672
  52.3 3.9 %collective-permute-done.20.refs_1_ = f32[14,32,128]{2,1,0:T(8,128)S(1)} collective-permute-done((f32[14,32,128]{2,1,0:T(8,128)S(1)}, f32[14,32,128]{2,1,0:T(8,128)S(1)}, u32[]{:S(2)}, u32[]{:S(2)}) %collective-permute-start.20) | collective-permute-done | bytes 229408 | tf_op jit(solution)/shard_map/ppermute | solution.py:728
  56.2 3.1 %up.1 = f32[32,8,512]{2,1,0:T(8,128)} custom-call(s32[2]{0:T(128)S(1)} %pad_add_fusion.place, f32[3,32,128]{2,1,0:T(8,128)S(1)} %coarse.1, f32[14,32,128]{2,1,0:T(8,128)S(1)} %collective-permute-done.19.refs_0_, f32[14,32,128]{2,1,0:T(8,128)S(1)} %collective-permute-done.20.refs_1_, f32[4,32,128]{2,1,0:T(8,128)S(1)} %collective-permute-done.14.refs_2_, ...), custom_call_target="tpu_custom_call" | custom-call | flops 3449999872 | bytes 11070000 | tf_op jit(solution)/shard_map/up/pallas_call | solution.py:672
  (39 shorter events, 4.9 us)
Async XLA Ops:
  0.1 1.0 %copy-start = (f32[32,8,512]{2,1,0:T(8,128)S(1)}, f32[32,8,512]{2,1,0:T(8,128)}, u32[]{:S(2)}) copy-start(f32[32,8,512]{2,1,0:T(8,128)} %conduct.1) | copy-start | bytes 1572868
  2.2 9.9 %copy-start.2 = (f32[32,8,512]{2,1,0:T(8,128)S(1)}, f32[32,8,512]{2,1,0:T(8,128)}, u32[]{:S(2)}) copy-start(f32[32,8,512]{2,1,0:T(8,128)} %right_side.1) | copy-start | bytes 1572868
  3.5 8.0 %collective-permute-start.5 = (f32[1,32,128]{2,1,0:T(8,128)S(1)}, f32[1,32,128]{2,1,0:T(8,128)S(1)}, u32[]{:S(2)}, u32[]{:S(2)}) collective-permute-start(f32[1,32,128]{2,1,0:T(8,128)S(1)} %get-tuple-element.52), channel_id=1, source_target_pairs={{0,24},{2,26},{4,28},{6,30},{8,16},{10,18},{12,20},{14,22},{16,8},... | collective-permute-start | bytes 49160 | tf_op jit(solution)/shard_map/ppermute | solution.py:718
  4.0 7.5 %collective-permute-start.4 = (f32[1,32,128]{2,1,0:T(8,128)S(1)}, f32[1,32,128]{2,1,0:T(8,128)S(1)}, u32[]{:S(2)}, u32[]{:S(2)}) collective-permute-start(f32[1,32,128]{2,1,0:T(8,128)S(1)} %get-tuple-element.52), channel_id=1, source_target_pairs={{0,16},{2,18},{4,20},{6,22},{8,24},{10,26},{12,28},{14,30},{16,0},... | collective-permute-start | bytes 49160 | tf_op jit(solution)/shard_map/ppermute | solution.py:718
  7.4 3.9 %collective-permute-start.3 = (f32[1,32,128]{2,1,0:T(8,128)S(1)}, f32[1,32,128]{2,1,0:T(8,128)S(1)}, u32[]{:S(2)}, u32[]{:S(2)}) collective-permute-start(f32[1,32,128]{2,1,0:T(8,128)S(1)} %get-tuple-element.52), channel_id=1, source_target_pairs={{0,8},{2,10},{4,12},{6,14},{8,0},{10,2},{12,4},{14,6},{16,24},{18,... | collective-permute-start | bytes 49160 | tf_op jit(solution)/shard_map/ppermute | solution.py:718
  7.5 11.0 %collective-permute-start.1 = (f32[13,32,128]{2,1,0:T(8,128)S(1)}, f32[13,32,128]{2,1,0:T(8,128)S(1)}, u32[]{:S(2)}, u32[]{:S(2)}) collective-permute-start(f32[13,32,128]{2,1,0:T(8,128)S(1)} %get-tuple-element.50), channel_id=1, source_target_pairs={{0,2},{2,0},{4,6},{6,4},{8,10},{10,8},{12,14},{14,12},{16,18},{18,... | collective-permute-start | bytes 638984 | tf_op jit(solution)/shard_map/ppermute | solution.py:728
  8.9 9.5 %collective-permute-start.2 = (f32[13,32,128]{2,1,0:T(8,128)S(1)}, f32[13,32,128]{2,1,0:T(8,128)S(1)}, u32[]{:S(2)}, u32[]{:S(2)}) collective-permute-start(f32[13,32,128]{2,1,0:T(8,128)S(1)} %get-tuple-element.51), channel_id=1, source_target_pairs={{2,4},{4,2},{6,8},{8,6},{10,12},{12,10},{14,16},{16,14},{18,20},{2... | collective-permute-start | bytes 638984 | tf_op jit(solution)/shard_map/ppermute | solution.py:728
  11.3 2.4 %collective-permute-start = (f32[2,8,32,128]{3,2,1,0:T(8,128)S(1)}, f32[2,8,32,128]{3,2,1,0:T(8,128)S(1)}, u32[]{:S(2)}, u32[]{:S(2)}) collective-permute-start(f32[2,8,32,128]{3,2,1,0:T(8,128)S(1)} %get-tuple-element.49), channel_id=1, source_target_pairs={{0,1},{1,0},{2,3},{3,2},{4,5},{5,4},{6,7},{7,6},{8,9},{9,8},{10,11... | collective-permute-start | bytes 786440 | tf_op jit(solution)/shard_map/ppermute | solution.py:700
  11.5 1.6 %collective-permute-start.6 = (f32[4,32,128]{2,1,0:T(8,128)S(1)}, f32[4,32,128]{2,1,0:T(8,128)S(1)}, u32[]{:S(2)}, u32[]{:S(2)}) collective-permute-start(f32[4,32,128]{2,1,0:T(8,128)S(1)} %constant_dynamic-update-slice_fusion.column), channel_id=1, source_target_pairs={{0,1},{1,0},{2,3},{3,2},{4,5},{5,4},{6,7},{7,6},{8,9},{9,8},{10,11... | collective-permute-start | bytes 196616 | tf_op jit(solution)/shard_map/ppermute | solution.py:692
  12.7 2.0 %collective-permute-start.7 = (f32[8,32,128]{2,1,0:T(8,128)S(1)}, f32[8,32,128]{2,1,0:T(8,128)S(1)}, u32[]{:S(2)}, u32[]{:S(2)}) collective-permute-start(f32[8,32,128]{2,1,0:T(8,128)S(1)} %get-tuple-element.54), channel_id=1, source_target_pairs={{0,1},{1,0},{2,3},{3,2},{4,5},{5,4},{6,7},{7,6},{8,9},{9,8},{10,11... | collective-permute-start | bytes 393224 | tf_op jit(solution)/shard_map/ppermute | solution.py:700
  18.5 7.6 %collective-permute-start.8 = (f32[13,32,128]{2,1,0:T(8,128)S(1)}, f32[13,32,128]{2,1,0:T(8,128)S(1)}, u32[]{:S(2)}, u32[]{:S(2)}) collective-permute-start(f32[13,32,128]{2,1,0:T(8,128)S(1)} %collective-permute-done.1.refs_6_), channel_id=1, source_target_pairs={{0,1},{1,0},{2,3},{3,2},{4,5},{5,4},{6,7},{7,6},{8,9},{9,8},{10,11... | collective-permute-start | bytes 638984 | tf_op jit(solution)/shard_map/ppermute | solution.py:692
  18.5 7.6 %collective-permute-start.9 = (f32[13,32,128]{2,1,0:T(8,128)S(1)}, f32[13,32,128]{2,1,0:T(8,128)S(1)}, u32[]{:S(2)}, u32[]{:S(2)}) collective-permute-start(f32[13,32,128]{2,1,0:T(8,128)S(1)} %collective-permute-done.2.refs_7_), channel_id=1, source_target_pairs={{0,1},{1,0},{2,3},{3,2},{4,5},{5,4},{6,7},{7,6},{8,9},{9,8},{10,11... | collective-permute-start | bytes 638984 | tf_op jit(solution)/shard_map/ppermute | solution.py:692
  19.0 5.4 %collective-permute-start.12 = (f32[5,32,128]{2,1,0:T(8,128)S(1)}, f32[5,32,128]{2,1,0:T(8,128)S(1)}, u32[]{:S(2)}, u32[]{:S(2)}) collective-permute-start(f32[5,32,128]{2,1,0:T(8,128)S(1)} %column.1.refs_4_), channel_id=1, source_target_pairs={{0,6},{2,4},{4,2},{6,0},{8,14},{10,12},{12,10},{14,8},{16,22},{18,... | collective-permute-start | bytes 245768 | tf_op jit(solution)/shard_map/ppermute | solution.py:718
  21.4 4.7 %collective-permute-start.11 = (f32[5,32,128]{2,1,0:T(8,128)S(1)}, f32[5,32,128]{2,1,0:T(8,128)S(1)}, u32[]{:S(2)}, u32[]{:S(2)}) collective-permute-start(f32[5,32,128]{2,1,0:T(8,128)S(1)} %column.1.refs_4_), channel_id=1, source_target_pairs={{0,4},{2,6},{4,0},{6,2},{8,12},{10,14},{12,8},{14,10},{16,20},{18,... | collective-permute-start | bytes 245768 | tf_op jit(solution)/shard_map/ppermute | solution.py:718
  21.4 4.7 %collective-permute-start.10 = (f32[5,32,128]{2,1,0:T(8,128)S(1)}, f32[5,32,128]{2,1,0:T(8,128)S(1)}, u32[]{:S(2)}, u32[]{:S(2)}) collective-permute-start(f32[5,32,128]{2,1,0:T(8,128)S(1)} %column.1.refs_4_), channel_id=1, source_target_pairs={{0,2},{2,0},{4,6},{6,4},{8,10},{10,8},{12,14},{14,12},{16,18},{18,... | collective-permute-start | bytes 245768 | tf_op jit(solution)/shard_map/ppermute | solution.py:718
  29.9 6.8 %collective-permute-start.14 = (f32[4,32,128]{2,1,0:T(8,128)S(1)}, f32[4,32,128]{2,1,0:T(8,128)S(1)}, u32[]{:S(2)}, u32[]{:S(2)}) collective-permute-start(f32[4,32,128]{2,1,0:T(8,128)S(1)} %get-tuple-element.64), channel_id=1, source_target_pairs={{0,4},{2,6},{4,0},{6,2},{8,12},{10,14},{12,8},{14,10},{16,20},{18,... | collective-permute-start | bytes 196616 | tf_op jit(solution)/shard_map/ppermute | solution.py:718
  31.7 4.8 %collective-permute-start.15 = (f32[2,32,128]{2,1,0:T(8,128)S(1)}, f32[2,32,128]{2,1,0:T(8,128)S(1)}, u32[]{:S(2)}, u32[]{:S(2)}) collective-permute-start(f32[2,32,128]{2,1,0:T(8,128)S(1)} %get-tuple-element.66.refs_0_), channel_id=1, source_target_pairs={{0,6},{2,4},{4,2},{6,0},{8,14},{10,12},{12,10},{14,8},{16,22},{18,... | collective-permute-start | bytes 98312 | tf_op jit(solution)/shard_map/ppermute | solution.py:718
  32.8 3.9 %collective-permute-start.13 = (f32[2,32,128]{2,1,0:T(8,128)S(1)}, f32[2,32,128]{2,1,0:T(8,128)S(1)}, u32[]{:S(2)}, u32[]{:S(2)}) collective-permute-start(f32[2,32,128]{2,1,0:T(8,128)S(1)} %get-tuple-element.66.refs_0_), channel_id=1, source_target_pairs={{0,2},{2,0},{4,6},{6,4},{8,10},{10,8},{12,14},{14,12},{16,18},{18,... | collective-permute-start | bytes 98312 | tf_op jit(solution)/shard_map/ppermute | solution.py:718
  36.7 12.7 %collective-permute-start.19 = (f32[14,32,128]{2,1,0:T(8,128)S(1)}, f32[14,32,128]{2,1,0:T(8,128)S(1)}, u32[]{:S(2)}, u32[]{:S(2)}) collective-permute-start(f32[14,32,128]{2,1,0:T(8,128)S(1)} %get-tuple-element.70), channel_id=1, source_target_pairs={{0,2},{2,0},{4,6},{6,4},{8,10},{10,8},{12,14},{14,12},{16,18},{18,... | collective-permute-start | bytes 688136 | tf_op jit(solution)/shard_map/ppermute | solution.py:728
  38.1 9.3 %collective-permute-start.18 = (f32[4,32,128]{2,1,0:T(8,128)S(1)}, f32[4,32,128]{2,1,0:T(8,128)S(1)}, u32[]{:S(2)}, u32[]{:S(2)}) collective-permute-start(f32[4,32,128]{2,1,0:T(8,128)S(1)} %merge.1.refs_0_), channel_id=1, source_target_pairs={{0,24},{2,26},{4,28},{6,30},{8,16},{10,18},{12,20},{14,22},{16,8},... | collective-permute-start | bytes 196616 | tf_op jit(solution)/shard_map/ppermute | solution.py:718
  38.8 10.6 %collective-permute-start.17 = (f32[4,32,128]{2,1,0:T(8,128)S(1)}, f32[4,32,128]{2,1,0:T(8,128)S(1)}, u32[]{:S(2)}, u32[]{:S(2)}) collective-permute-start(f32[4,32,128]{2,1,0:T(8,128)S(1)} %merge.1.refs_0_), channel_id=1, source_target_pairs={{0,16},{2,18},{4,20},{6,22},{8,24},{10,26},{12,28},{14,30},{16,0},... | collective-permute-start | bytes 196616 | tf_op jit(solution)/shard_map/ppermute | solution.py:718
  42.3 7.1 %collective-permute-start.16 = (f32[4,32,128]{2,1,0:T(8,128)S(1)}, f32[4,32,128]{2,1,0:T(8,128)S(1)}, u32[]{:S(2)}, u32[]{:S(2)}) collective-permute-start(f32[4,32,128]{2,1,0:T(8,128)S(1)} %merge.1.refs_0_), channel_id=1, source_target_pairs={{0,8},{2,10},{4,12},{6,14},{8,0},{10,2},{12,4},{14,6},{16,24},{18,... | collective-permute-start | bytes 196616 | tf_op jit(solution)/shard_map/ppermute | solution.py:718
  42.3 10.0 %collective-permute-start.21 = (f32[2,32,128]{2,1,0:T(8,128)S(1)}, f32[2,32,128]{2,1,0:T(8,128)S(1)}, u32[]{:S(2)}, u32[]{:S(2)}) collective-permute-start(f32[2,32,128]{2,1,0:T(8,128)S(1)} %get-tuple-element.81), channel_id=1, source_target_pairs={{4,8},{8,4},{6,10},{10,6},{12,16},{16,12},{14,18},{18,14},{20,24},... | collective-permute-start | bytes 98312 | tf_op jit(solution)/shard_map/ppermute | solution.py:728
  47.4 8.8 %collective-permute-start.20 = (f32[14,32,128]{2,1,0:T(8,128)S(1)}, f32[14,32,128]{2,1,0:T(8,128)S(1)}, u32[]{:S(2)}, u32[]{:S(2)}) collective-permute-start(f32[14,32,128]{2,1,0:T(8,128)S(1)} %get-tuple-element.80), channel_id=1, source_target_pairs={{2,4},{4,2},{6,8},{8,6},{10,12},{12,10},{14,16},{16,14},{18,20},{2... | collective-permute-start | bytes 688136 | tf_op jit(solution)/shard_map/ppermute | solution.py:728
  (1 other events, 1.0 us)

commit v12 on v8

--- a/solution.py
+++ b/solution.py
@@ -727,14 +727,14 @@
         place,
         [own0, own1, own2, turned, *borders, *halos, *sum(sides, [])],
     )
-    coefs_out, blocks, with_far, ups, far_second = downs[:3], downs[3], downs[4], downs[5:7], downs[7]
+    coefs_out, blocks, with_far, ups, far_second = downs[:3], downs[3], downs[4], list(downs[5:7]), downs[7]
     far_rows = None
     for stride, radix in plan[:-1]:
         count = stride * radix
         if far_rows is None:
             blocks = swap(blocks, stride, radix, {2: with_far})
             far_rows = [blocks[2], exchange([None, far_second], 2)[1]]
-            blocks, far_rows = lax.optimization_barrier((blocks, far_rows))
+            blocks, ups[0] = lax.optimization_barrier((blocks, ups[0]))
         else:
             blocks = swap(blocks, stride, radix)
         (blocks,) = call(
@@ -748,7 +748,8 @@
         )
     stride, radix = plan[-1]
     blocks = swap(blocks, stride, radix)
-    received = exchange(ups, 1) + far_rows
+    received = lax.optimization_barrier([exchange([ups[0], None], 1)[0], ups[1]])
+    received = [received[0], exchange([None, received[1]], 1)[1]] + far_rows
     scratch = [(sizes.span_count + 2, *tile), (max(sizes.span_count // 2, 2), *tile)]
     for index in range(3):
         count = sizes.span_count >> index

time: 55.3 us -> 54.1 us (0.978)
  starting transfers between devices: 19 us -> 15.6 us
  waiting for transfers between devices: 21.3 us -> 23.5 us
    ppermute x6, starting transfers between devices: 11.4 us -> 9.08 us  [swap(): lax.ppermute(others.get(step, value), 'span', [(device, device ^ step * s...]
    ppermute x6, waiting for transfers between devices: 12.4 us -> 14.5 us  [swap(): lax.ppermute(others.get(step, value), 'span', [(device, device ^ step * s...]
    ppermute x5, starting transfers between devices: 6.99 us -> 5.99 us  [exchange(): lax.ppermute(value, 'span', route)]
  transfers between devices with their start and end apart: 14 -> 14, of which waited for: 7 -> 7; matrix products, arithmetic and copies ran while one was open for 0% -> 0% of each run, Pallas kernels for 7% -> 8%
where the time goes in v12:
time: 54.1 us; the launch traced here: 53.9 us
  waiting for transfers between devices  23.5 us (43%)
  starting transfers between devices  15.6 us (29%)
  Pallas kernels  12.5 us (23%)
  local copies, waits for them, and re-layouts  2.09 us (4%)
    ppermute x6, waiting for transfers between devices, swap(): lax.ppermute(others.get(step, value), 'span', [(device, device ^ step * s...  14.5 us
    pallas_call x6, Pallas kernels, call(): pl.pallas_call(body, name=name, out_shape=[jax.ShapeDtypeStruct(shape, f3...  12.5 us
    ppermute x6, starting transfers between devices, swap(): lax.ppermute(others.get(step, value), 'span', [(device, device ^ step * s...  9.08 us
    ppermute x5, waiting for transfers between devices, exchange(): lax.ppermute(value, 'span', route)  7.68 us
    ppermute x5, starting transfers between devices, exchange(): lax.ppermute(value, 'span', route)  5.99 us
    unnamed x6, local copies, waits for them, and re-layouts  2.09 us
    ppermute x2, waiting for transfers between devices, beside(): lax.ppermute(value, 'width', [(0, 1), (1, 0)])  1.25 us
  transfers between devices with their start and end apart: 14, of which 7 were waited for; matrix products, arithmetic and copies ran while one was open for 0% of the time, Pallas kernels for 8%

profile of v12, /device:TPU:0, one launch (start us, length us, event | category | flops | bytes accessed | tf_op | source)
XLA Modules:
  0.0 53.9 jit_solution(8758731822717393996)
XLA Ops:
  0.1 1.0 %copy-done = f32[32,8,512]{2,1,0:T(8,128)S(1)} copy-done((f32[32,8,512]{2,1,0:T(8,128)S(1)}, f32[32,8,512]{2,1,0:T(8,128)}, u32[]{:S(2)}) %copy-start) | copy-done | bytes 524312
  1.1 1.0 %copy-done.1 = f32[32,8,512]{2,1,0:T(8,128)S(1)} copy-done((f32[32,8,512]{2,1,0:T(8,128)S(1)}, f32[32,8,512]{2,1,0:T(8,128)}, u32[]{:S(2)}) %copy-start.1) | copy-done | bytes 524312
  2.2 1.1 %start.1 = (f32[2,8,32,512]{3,2,1,0:T(8,128)S(1)}, f32[8,32,256]{2,1,0:T(8,128)S(1)}, f32[4,32,128]{2,1,0:T(8,128)S(1)}, f32[13,32,128]{2,1,0:T(8,128)S(1)}, f32[13,32,128]{2,1,0:T(8,128)S(1)}) custom-call(s32[2]{0:T(128)S(1)} %pad_add_fusion.place, f32[32,8,512]{2,1,0:T(8,128)S(1)} %copy-done, f32[32,8,512]{2,1,0:T(8,128)S(1)} %copy-done.1), custom_call_target="tpu_custom_call" | custom-call | flops 1264999936 | bytes 4059000 | tf_op jit(solution)/shard_map/start/pallas_call | solution.py:627
  3.3 3.0 %collective-permute-start.1 = (f32[13,32,128]{2,1,0:T(8,128)S(1)}, f32[13,32,128]{2,1,0:T(8,128)S(1)}, u32[]{:S(2)}, u32[]{:S(2)}) collective-permute-start(f32[13,32,128]{2,1,0:T(8,128)S(1)} %get-tuple-element.32), channel_id=1, source_target_pairs={{0,2},{2,0},{4,6},{6,4},{8,10},{10,8},{12,14},{14,12},{16,18},{18,... | collective-permute-start | bytes 638984 | tf_op jit(solution)/shard_map/ppermute | solution.py:675
  6.3 0.7 %collective-permute-start.2 = (f32[13,32,128]{2,1,0:T(8,128)S(1)}, f32[13,32,128]{2,1,0:T(8,128)S(1)}, u32[]{:S(2)}, u32[]{:S(2)}) collective-permute-start(f32[13,32,128]{2,1,0:T(8,128)S(1)} %get-tuple-element.33), channel_id=1, source_target_pairs={{2,4},{4,2},{6,8},{8,6},{10,12},{12,10},{14,16},{16,14},{18,20},{2... | collective-permute-start | bytes 638984 | tf_op jit(solution)/shard_map/ppermute | solution.py:675
  7.0 0.7 %turn.1 = (f32[8,32,512]{2,1,0:T(8,128)S(1)}, f32[3,8,32,128]{3,2,1,0:T(8,128)S(1)}) custom-call(s32[2]{0:T(128)S(1)} %pad_add_fusion.place, f32[32,8,512]{2,1,0:T(8,128)S(1)} %copy-done.2, f32[2,8,32,512]{3,2,1,0:T(8,128)S(1)} %get-tuple-element.27.own0.refs_0_.refs_7_), custom_call_target="tpu_custom_call" | custom-call | flops 805000000 | bytes 2583000 | tf_op jit(solution)/shard_map/turn/pallas_call | solution.py:627
  7.7 7.7 %collective-permute-done.1.refs_5_ = f32[13,32,128]{2,1,0:T(8,128)S(1)} collective-permute-done((f32[13,32,128]{2,1,0:T(8,128)S(1)}, f32[13,32,128]{2,1,0:T(8,128)S(1)}, u32[]{:S(2)}, u32[]{:S(2)}) %collective-permute-start.1) | collective-permute-done | bytes 213024 | tf_op jit(solution)/shard_map/ppermute | solution.py:675
  15.4 0.5 collective-permute-start.4
  15.9 0.9 %collective-permute-done.3.refs_7_ = f32[13,32,128]{2,1,0:T(8,128)S(1)} collective-permute-done((f32[13,32,128]{2,1,0:T(8,128)S(1)}, f32[13,32,128]{2,1,0:T(8,128)S(1)}, u32[]{:S(2)}, u32[]{:S(2)}) %collective-permute-start.3) | collective-permute-done | bytes 213024 | tf_op jit(solution)/shard_map/ppermute | solution.py:647
  17.2 3.8 %down.1 = (f32[41,32,640]{2,1,0:T(8,128)S(1)}, f32[43,32,384]{2,1,0:T(8,128)S(1)}, f32[29,32,256]{2,1,0:T(8,128)S(1)}, f32[4,32,128]{2,1,0:T(8,128)S(1)}, f32[6,...) custom-call(s32[2]{0:T(128)S(1)} %pad_add_fusion.place, ...), custom_call_target="tpu_custom_call" | custom-call | flops 4140000000 | bytes 13284000 | tf_op jit(solution)/shard_map/down/pallas_call | solution.py:627
  21.0 1.9 %collective-permute-start.6 = (f32[6,32,128]{2,1,0:T(8,128)S(1)}, f32[6,32,128]{2,1,0:T(8,128)S(1)}, u32[]{:S(2)}, u32[]{:S(2)}) collective-permute-start(f32[6,32,128]{2,1,0:T(8,128)S(1)} %get-tuple-element.35), channel_id=1, source_target_pairs={{0,4},{2,6},{4,0},{6,2},{8,12},{10,14},{12,8},{14,10},{16,20},{18,... | collective-permute-start | bytes 294920 | tf_op jit(solution)/shard_map/ppermute | solution.py:665
  22.9 2.7 %collective-permute-start.7 = (f32[4,32,128]{2,1,0:T(8,128)S(1)}, f32[4,32,128]{2,1,0:T(8,128)S(1)}, u32[]{:S(2)}, u32[]{:S(2)}) collective-permute-start(f32[4,32,128]{2,1,0:T(8,128)S(1)} %get-tuple-element.37.refs_0_), channel_id=1, source_target_pairs={{0,6},{2,4},{4,2},{6,0},{8,14},{10,12},{12,10},{14,8},{16,22},{18,... | collective-permute-start | bytes 196616 | tf_op jit(solution)/shard_map/ppermute | solution.py:665
  25.6 3.0 %collective-permute-done.7.refs_3_ = f32[4,32,128]{2,1,0:T(8,128)S(1)} collective-permute-done((f32[4,32,128]{2,1,0:T(8,128)S(1)}, f32[4,32,128]{2,1,0:T(8,128)S(1)}, u32[]{:S(2)}, u32[]{:S(2)}) %collective-permute-start.7) | collective-permute-done | bytes 65568 | tf_op jit(solution)/shard_map/ppermute | solution.py:665
  28.6 1.3 %collective-permute-done.5.refs_1_ = f32[4,32,128]{2,1,0:T(8,128)S(1)} collective-permute-done((f32[4,32,128]{2,1,0:T(8,128)S(1)}, f32[4,32,128]{2,1,0:T(8,128)S(1)}, u32[]{:S(2)}, u32[]{:S(2)}) %collective-permute-start.5) | collective-permute-done | bytes 65568 | tf_op jit(solution)/shard_map/ppermute | solution.py:665
  29.9 1.0 %collective-permute-start.11 = (f32[14,32,128]{2,1,0:T(8,128)S(1)}, f32[14,32,128]{2,1,0:T(8,128)S(1)}, u32[]{:S(2)}, u32[]{:S(2)}) collective-permute-start(f32[14,32,128]{2,1,0:T(8,128)S(1)} %get-tuple-element.41), channel_id=1, source_target_pairs={{0,2},{2,0},{4,6},{6,4},{8,10},{10,8},{12,14},{14,12},{16,18},{18,... | collective-permute-start | bytes 688136 | tf_op jit(solution)/shard_map/ppermute | solution.py:675
  30.9 0.9 %merge.1.refs_0_ = f32[9,32,128]{2,1,0:T(8,128)S(1)} custom-call(s32[2]{0:T(128)S(1)} %pad_add_fusion.place, f32[4,32,128]{2,1,0:T(8,128)S(1)} %get-tuple-element.37.refs_0_, f32[4,32,128]{2,1,0:T(8,128)S(1)} %collective-permute-done.5.refs_1_, f32[6,32,128]{2,1,0:T(8,128)S(1)} %collective-permute-done.6.refs_2_, ...), custom_call_target="tpu_custom_call" | custom-call | flops 1035000000 | bytes 3321000 | tf_op jit(solution)/shard_map/merge/pallas_call | solution.py:627
  31.7 3.7 %collective-permute-start.10 = (f32[9,32,128]{2,1,0:T(8,128)S(1)}, f32[9,32,128]{2,1,0:T(8,128)S(1)}, u32[]{:S(2)}, u32[]{:S(2)}) collective-permute-start(f32[9,32,128]{2,1,0:T(8,128)S(1)} %merge.1.refs_0_), channel_id=1, source_target_pairs={{0,24},{2,26},{4,28},{6,30},{8,16},{10,18},{12,20},{14,22},{16,8},... | collective-permute-start | bytes 442376 | tf_op jit(solution)/shard_map/ppermute | solution.py:665
  35.4 0.8 %collective-permute-start.8 = (f32[9,32,128]{2,1,0:T(8,128)S(1)}, f32[9,32,128]{2,1,0:T(8,128)S(1)}, u32[]{:S(2)}, u32[]{:S(2)}) collective-permute-start(f32[9,32,128]{2,1,0:T(8,128)S(1)} %merge.1.refs_0_), channel_id=1, source_target_pairs={{0,8},{2,10},{4,12},{6,14},{8,0},{10,2},{12,4},{14,6},{16,24},{18,... | collective-permute-start | bytes 442376 | tf_op jit(solution)/shard_map/ppermute | solution.py:665
  36.2 0.7 %collective-permute-start.13 = (f32[2,32,128]{2,1,0:T(8,128)S(1)}, f32[2,32,128]{2,1,0:T(8,128)S(1)}, u32[]{:S(2)}, u32[]{:S(2)}) collective-permute-start(f32[2,32,128]{2,1,0:T(8,128)S(1)} %get-tuple-element.45), channel_id=1, source_target_pairs={{4,8},{8,4},{6,10},{10,6},{12,16},{16,12},{14,18},{18,14},{20,24},... | collective-permute-start | bytes 98312 | tf_op jit(solution)/shard_map/ppermute | solution.py:675
  36.9 0.7 %collective-permute-start.12 = (f32[14,32,128]{2,1,0:T(8,128)S(1)}, f32[14,32,128]{2,1,0:T(8,128)S(1)}, u32[]{:S(2)}, u32[]{:S(2)}) collective-permute-start(f32[14,32,128]{2,1,0:T(8,128)S(1)} %get-tuple-element.44), channel_id=1, source_target_pairs={{2,4},{4,2},{6,8},{8,6},{10,12},{12,10},{14,16},{16,14},{18,20},{2... | collective-permute-start | bytes 688136 | tf_op jit(solution)/shard_map/ppermute | solution.py:675
  37.5 2.8 %collective-permute-done.10.refs_3_ = f32[9,32,128]{2,1,0:T(8,128)S(1)} collective-permute-done((f32[9,32,128]{2,1,0:T(8,128)S(1)}, f32[9,32,128]{2,1,0:T(8,128)S(1)}, u32[]{:S(2)}, u32[]{:S(2)}) %collective-permute-start.10) | collective-permute-done | bytes 147488 | tf_op jit(solution)/shard_map/ppermute | solution.py:665
  40.4 7.4 %collective-permute-done.9.refs_2_ = f32[9,32,128]{2,1,0:T(8,128)S(1)} collective-permute-done((f32[9,32,128]{2,1,0:T(8,128)S(1)}, f32[9,32,128]{2,1,0:T(8,128)S(1)}, u32[]{:S(2)}, u32[]{:S(2)}) %collective-permute-start.9) | collective-permute-done | bytes 147488 | tf_op jit(solution)/shard_map/ppermute | solution.py:665
  47.8 2.9 %coarse.1 = f32[3,32,128]{2,1,0:T(8,128)S(1)} custom-call(s32[2]{0:T(128)S(1)} %pad_add_fusion.place, f32[9,32,128]{2,1,0:T(8,128)S(1)} %merge.1.refs_0_, f32[9,32,128]{2,1,0:T(8,128)S(1)} %collective-permute-done.8.refs_1_, f32[9,32,128]{2,1,0:T(8,128)S(1)} %collective-permute-done.9.refs_2_, f32[9,32,128]{2,1,0:T(8,128)S(1)} %collective-permute-done.10.refs_3_), custom_call_target="tpu_custom_call" | custom-call | flops 3335000064 | bytes 10701000 | tf_op jit(solution)/shard_map/coarse/pallas_call | solution.py:627
  50.8 3.1 %up.1 = f32[32,8,512]{2,1,0:T(8,128)} custom-call(s32[2]{0:T(128)S(1)} %pad_add_fusion.place, f32[3,32,128]{2,1,0:T(8,128)S(1)} %coarse.1, f32[14,32,128]{2,1,0:T(8,128)S(1)} %collective-permute-done.11.refs_0_, f32[14,32,128]{2,1,0:T(8,128)S(1)} %collective-permute-done.12.refs_1_, f32[6,32,128]{2,1,0:T(8,128)S(1)} %collective-permute-done.6.refs_2_, ...), custom_call_target="tpu_custom_call" | custom-call | flops 3449999872 | bytes 11070000 | tf_op jit(solution)/shard_map/up/pallas_call | solution.py:627
  (17 shorter events, 0.5 us)
Async XLA Ops:
  0.1 1.0 %copy-start = (f32[32,8,512]{2,1,0:T(8,128)S(1)}, f32[32,8,512]{2,1,0:T(8,128)}, u32[]{:S(2)}) copy-start(f32[32,8,512]{2,1,0:T(8,128)} %conduct.1) | copy-start | bytes 1572868
  1.1 1.0 %copy-start.1 = (f32[32,8,512]{2,1,0:T(8,128)S(1)}, f32[32,8,512]{2,1,0:T(8,128)}, u32[]{:S(2)}) copy-start(f32[32,8,512]{2,1,0:T(8,128)} %binding.1) | copy-start | bytes 1572868
  2.2 4.8 %copy-start.2 = (f32[32,8,512]{2,1,0:T(8,128)S(1)}, f32[32,8,512]{2,1,0:T(8,128)}, u32[]{:S(2)}) copy-start(f32[32,8,512]{2,1,0:T(8,128)} %right_side.1) | copy-start | bytes 1572868
  3.3 12.1 %collective-permute-start.1 = (f32[13,32,128]{2,1,0:T(8,128)S(1)}, f32[13,32,128]{2,1,0:T(8,128)S(1)}, u32[]{:S(2)}, u32[]{:S(2)}) collective-permute-start(f32[13,32,128]{2,1,0:T(8,128)S(1)} %get-tuple-element.32), channel_id=1, source_target_pairs={{0,2},{2,0},{4,6},{6,4},{8,10},{10,8},{12,14},{14,12},{16,18},{18,... | collective-permute-start | bytes 638984 | tf_op jit(solution)/shard_map/ppermute | solution.py:675
  6.3 9.1 %collective-permute-start.2 = (f32[13,32,128]{2,1,0:T(8,128)S(1)}, f32[13,32,128]{2,1,0:T(8,128)S(1)}, u32[]{:S(2)}, u32[]{:S(2)}) collective-permute-start(f32[13,32,128]{2,1,0:T(8,128)S(1)} %get-tuple-element.33), channel_id=1, source_target_pairs={{2,4},{4,2},{6,8},{8,6},{10,12},{12,10},{14,16},{16,14},{18,20},{2... | collective-permute-start | bytes 638984 | tf_op jit(solution)/shard_map/ppermute | solution.py:675
  7.6 8.3 %collective-permute-start = (f32[3,8,32,128]{3,2,1,0:T(8,128)S(1)}, f32[3,8,32,128]{3,2,1,0:T(8,128)S(1)}, u32[]{:S(2)}, u32[]{:S(2)}) collective-permute-start(f32[3,8,32,128]{3,2,1,0:T(8,128)S(1)} %get-tuple-element.31), channel_id=1, source_target_pairs={{0,1},{1,0},{2,3},{3,2},{4,5},{5,4},{6,7},{7,6},{8,9},{9,8},{10,11... | collective-permute-start | bytes 1179656 | tf_op jit(solution)/shard_map/ppermute | solution.py:709
  15.4 1.5 %collective-permute-start.3 = (f32[13,32,128]{2,1,0:T(8,128)S(1)}, f32[13,32,128]{2,1,0:T(8,128)S(1)}, u32[]{:S(2)}, u32[]{:S(2)}) collective-permute-start(f32[13,32,128]{2,1,0:T(8,128)S(1)} %collective-permute-done.1.refs_5_), channel_id=1, source_target_pairs={{0,1},{1,0},{2,3},{3,2},{4,5},{5,4},{6,7},{7,6},{8,9},{9,8},{10,11... | collective-permute-start | bytes 638984 | tf_op jit(solution)/shard_map/ppermute | solution.py:647
  15.4 1.8 %collective-permute-start.4 = (f32[13,32,128]{2,1,0:T(8,128)S(1)}, f32[13,32,128]{2,1,0:T(8,128)S(1)}, u32[]{:S(2)}, u32[]{:S(2)}) collective-permute-start(f32[13,32,128]{2,1,0:T(8,128)S(1)} %collective-permute-done.2.refs_6_), channel_id=1, source_target_pairs={{0,1},{1,0},{2,3},{3,2},{4,5},{5,4},{6,7},{7,6},{8,9},{9,8},{10,11... | collective-permute-start | bytes 638984 | tf_op jit(solution)/shard_map/ppermute | solution.py:647
  21.0 8.9 %collective-permute-start.6 = (f32[6,32,128]{2,1,0:T(8,128)S(1)}, f32[6,32,128]{2,1,0:T(8,128)S(1)}, u32[]{:S(2)}, u32[]{:S(2)}) collective-permute-start(f32[6,32,128]{2,1,0:T(8,128)S(1)} %get-tuple-element.35), channel_id=1, source_target_pairs={{0,4},{2,6},{4,0},{6,2},{8,12},{10,14},{12,8},{14,10},{16,20},{18,... | collective-permute-start | bytes 294920 | tf_op jit(solution)/shard_map/ppermute | solution.py:665
  22.9 5.7 %collective-permute-start.7 = (f32[4,32,128]{2,1,0:T(8,128)S(1)}, f32[4,32,128]{2,1,0:T(8,128)S(1)}, u32[]{:S(2)}, u32[]{:S(2)}) collective-permute-start(f32[4,32,128]{2,1,0:T(8,128)S(1)} %get-tuple-element.37.refs_0_), channel_id=1, source_target_pairs={{0,6},{2,4},{4,2},{6,0},{8,14},{10,12},{12,10},{14,8},{16,22},{18,... | collective-permute-start | bytes 196616 | tf_op jit(solution)/shard_map/ppermute | solution.py:665
  25.6 4.3 %collective-permute-start.5 = (f32[4,32,128]{2,1,0:T(8,128)S(1)}, f32[4,32,128]{2,1,0:T(8,128)S(1)}, u32[]{:S(2)}, u32[]{:S(2)}) collective-permute-start(f32[4,32,128]{2,1,0:T(8,128)S(1)} %get-tuple-element.37.refs_0_), channel_id=1, source_target_pairs={{0,2},{2,0},{4,6},{6,4},{8,10},{10,8},{12,14},{14,12},{16,18},{18,... | collective-permute-start | bytes 196616 | tf_op jit(solution)/shard_map/ppermute | solution.py:665
  29.9 7.0 %collective-permute-start.11 = (f32[14,32,128]{2,1,0:T(8,128)S(1)}, f32[14,32,128]{2,1,0:T(8,128)S(1)}, u32[]{:S(2)}, u32[]{:S(2)}) collective-permute-start(f32[14,32,128]{2,1,0:T(8,128)S(1)} %get-tuple-element.41), channel_id=1, source_target_pairs={{0,2},{2,0},{4,6},{6,4},{8,10},{10,8},{12,14},{14,12},{16,18},{18,... | collective-permute-start | bytes 688136 | tf_op jit(solution)/shard_map/ppermute | solution.py:675
  31.7 8.6 %collective-permute-start.10 = (f32[9,32,128]{2,1,0:T(8,128)S(1)}, f32[9,32,128]{2,1,0:T(8,128)S(1)}, u32[]{:S(2)}, u32[]{:S(2)}) collective-permute-start(f32[9,32,128]{2,1,0:T(8,128)S(1)} %merge.1.refs_0_), channel_id=1, source_target_pairs={{0,24},{2,26},{4,28},{6,30},{8,16},{10,18},{12,20},{14,22},{16,8},... | collective-permute-start | bytes 442376 | tf_op jit(solution)/shard_map/ppermute | solution.py:665
  35.4 12.4 %collective-permute-start.9 = (f32[9,32,128]{2,1,0:T(8,128)S(1)}, f32[9,32,128]{2,1,0:T(8,128)S(1)}, u32[]{:S(2)}, u32[]{:S(2)}) collective-permute-start(f32[9,32,128]{2,1,0:T(8,128)S(1)} %merge.1.refs_0_), channel_id=1, source_target_pairs={{0,16},{2,18},{4,20},{6,22},{8,24},{10,26},{12,28},{14,30},{16,0},... | collective-permute-start | bytes 442376 | tf_op jit(solution)/shard_map/ppermute | solution.py:665
  35.4 12.4 %collective-permute-start.8 = (f32[9,32,128]{2,1,0:T(8,128)S(1)}, f32[9,32,128]{2,1,0:T(8,128)S(1)}, u32[]{:S(2)}, u32[]{:S(2)}) collective-permute-start(f32[9,32,128]{2,1,0:T(8,128)S(1)} %merge.1.refs_0_), channel_id=1, source_target_pairs={{0,8},{2,10},{4,12},{6,14},{8,0},{10,2},{12,4},{14,6},{16,24},{18,... | collective-permute-start | bytes 442376 | tf_op jit(solution)/shard_map/ppermute | solution.py:665
  36.2 14.6 %collective-permute-start.13 = (f32[2,32,128]{2,1,0:T(8,128)S(1)}, f32[2,32,128]{2,1,0:T(8,128)S(1)}, u32[]{:S(2)}, u32[]{:S(2)}) collective-permute-start(f32[2,32,128]{2,1,0:T(8,128)S(1)} %get-tuple-element.45), channel_id=1, source_target_pairs={{4,8},{8,4},{6,10},{10,6},{12,16},{16,12},{14,18},{18,14},{20,24},... | collective-permute-start | bytes 98312 | tf_op jit(solution)/shard_map/ppermute | solution.py:675
  36.9 13.9 %collective-permute-start.12 = (f32[14,32,128]{2,1,0:T(8,128)S(1)}, f32[14,32,128]{2,1,0:T(8,128)S(1)}, u32[]{:S(2)}, u32[]{:S(2)}) collective-permute-start(f32[14,32,128]{2,1,0:T(8,128)S(1)} %get-tuple-element.44), channel_id=1, source_target_pairs={{2,4},{4,2},{6,8},{8,6},{10,12},{12,10},{14,16},{16,14},{18,20},{2... | collective-permute-start | bytes 688136 | tf_op jit(solution)/shard_map/ppermute | solution.py:675

commit v13 on v12

--- a/solution.py
+++ b/solution.py
@@ -145,30 +145,89 @@
         target[0:rows, :, start:stop] = result.reshape(rows, depth, stop - start)
 
 
-def coefficients(sizes, place, level, count, conduct, binding, fx, fy, fz, weight):
+class Joined:
+    def __init__(self, inner, outer, first):
+        self.inner, self.outer, self.first = inner, outer, first
+
+    def find(self, row):
+        place, count = row - self.first, 0 if self.inner is None else self.inner.shape[0]
+        if 0 <= place < count:
+            return self.inner, place
+        return self.outer, row if place < 0 else row - count
+
+    def __getitem__(self, row):
+        array, place = self.find(row)
+        return array[place]
+
+    def __setitem__(self, row, value):
+        array, place = self.find(row)
+        array[place] = value
+
+
+class Level:
+    def __init__(self, sizes, level, inner, outer):
+        self.n, self.halo = sizes.rows[level], 1 if level == 0 else 2
+        counts = inner_rows(sizes, level)
+        fx, fy, fz, *rest = parts(inner, counts)
+        weight, source, smooth = (None, None, None) if level == 2 else (rest[0], None, rest[1])
+        if level == 1:
+            weight, source, smooth = rest
+        others = [None] * 7 if outer is None else parts(outer, outer_rows(sizes, level))
+        if level == 0 and outer is not None:
+            others = [others[0], None, None, others[1], None, others[2], None]
+        h = self.halo
+        self.fx = Joined(fx, others[0], h)
+        self.fy, self.fz = Joined(fy, others[1], h - 1), Joined(fz, others[2], h - 1)
+        self.weight, self.source, self.smooth = (
+            Joined(array, other, h) for array, other in zip((weight, source, smooth), others[3:6])
+        )
+        self.binding = others[6]
+
+    def inner(self):
+        first, last = self.halo, self.halo + self.n - 1
+        return range(first + 1, last + 1), range(first, last + 1), range(first + 1, last)
+
+    def outer(self):
+        count = self.n + 2 * self.halo
+        every = (range(1, count), range(1, count - 1), range(1, count - 1))
+        return tuple([row for row in rows if row not in mine] for rows, mine in zip(every, self.inner()))
+
+
+def inner_rows(sizes, level):
+    n = sizes.rows[level]
+    return [n - 1, n, n] + [[n - 2] * 2, [n - 2] * 3, []][level]
+
+
+def outer_rows(sizes, level):
+    n = sizes.rows[level]
+    return [[2, 2, 2], [4, 2, 2, 4, 4, 4, n + 2], [4, 2, 2] + [n + 2] * 4][level]
+
+
+def coefficients(sizes, place, level, conduct, binding, fx, fy, fz, weight, rows):
     guard = level > 0 or sizes.sides > 1
-    for row in range(1, count):
+    for row in rows[0]:
         fx[row - 1] = harmonic(conduct(row - 1), conduct(row), guard)
-    for row in range(1, count - 1):
+    for row in rows[1]:
         mine = conduct(row)
         south = harmonic(mine, roll(mine, 1, 1), guard)
         if level == 0 and sizes.sides < 2:
             cut = 0 if sizes.sides == 0 else jnp.where(place[1] == 0, 0, sizes.extent_y)
             south = jnp.where(lane_at(mine.shape) == cut, 0.0, south)
         below = harmonic(mine, roll(mine, 1, 0), guard)
-        below = jnp.where(lax.broadcasted_iota(jnp.int32, mine.shape, 0) == 0, 0.0, below)
+        fy[row - 1] = south
+        fz[row - 1] = jnp.where(lax.broadcasted_iota(jnp.int32, mine.shape, 0) == 0, 0.0, below)
+    for row in rows[2]:
+        south, below = fy[row - 1], fz[row - 1]
         diagonal = fx[row - 1] + fx[row] + binding(row)
         diagonal = diagonal + (south + roll(south, -1, 1)) + (below + roll(below, -1, 0))
         if guard:
             diagonal = jnp.maximum(diagonal, 1e-6)
-        fy[row - 1] = south
-        fz[row - 1] = below
         weight[row - 1] = relax_weight * reciprocal(diagonal)
 
 
-def sweep(count, field, binding, fx, fy, fz, emit):
-    lower = fx[0] * (field(1) - field(0))
-    for row in range(1, count - 1):
+def sweep(first, last, field, binding, fx, fy, fz, emit):
+    lower = fx[first - 1] * (field(first) - field(first - 1))
+    for row in range(first, last + 1):
         mine = field(row)
         upper = fx[row] * (field(row + 1) - mine)
         south = fy[row - 1] * (mine - roll(mine, 1, 1))
@@ -178,22 +237,15 @@
         lower = upper
 
 
-def own_defect(count, smooth, source, binding, fx, fy, fz, sums, first):
-    zero = jnp.zeros(smooth.shape[1:], f32)
-
-    def field(row):
-        return smooth[row - 1] if 0 < row < count - 1 else zero
-
+def in_pairs(sums, slot_of):
     def add(row, value):
-        slot = (row + first) // 2
-        if (row + first) % 2 == 0 or row == 0:
+        slot, first = slot_of(row)
+        if first:
             sums[slot] = value
         else:
             sums[slot] = sums[slot] + value
 
-    add(0, fx[0] * field(1))
-    sweep(count, field, binding, fx, fy, fz, lambda row, result: add(row, source(row) - result))
-    add(count - 1, fx[count - 2] * field(count - 2))
+    return add
 
 
 def parts(array, counts):
@@ -204,14 +256,8 @@
     return views
 
 
-def coefficient_rows(sizes, level):
-    n = sizes.rows[level]
-    if level == 0:
-        return [n + 1, n, n, n, n]
-    return [n + 3] + [n + 2] * 6
-
-
-def start_kernel(sizes, place, conduct, binding, own0, own1, own2, first, second, sums):
+def start_kernel(sizes, place, conduct, binding, own0, own1, own2, first, second, *refs):
+    edges, sums = refs[: sizes.sides], refs[-1]
     n0, n1, n2 = sizes.rows[:3]
     for at, array in enumerate((conduct, binding)):
         own0[at] = jnp.swapaxes(array[...], 0, 1)
@@ -229,18 +275,23 @@
         ends.append(rows + (own2[n2 - 2], own2[n2 - 1], own2[n2 + edge]))
     for slot, next_row, prev_row in zip(sizes.slots, *ends):
         put_pair(place, (first, second), slot, next_row, prev_row)
-
-
-def turn_kernel(sizes, place, right_side, own0, turned, *edges):
+    for at in (0, 1):
+        cut_edges(sizes, place, own0.at[at], [edge.at[at] for edge in edges])
+
+
+def cut_edges(sizes, place, array, edges):
+    last = sizes.extent_y - BORDER
+    if sizes.sides == 1:
+        at = pl.multiple_of(jnp.where(place[1] == 0, last, 0), LANES)
+        edges[0][...] = array[:, :, pl.ds(at, BORDER)]
+    elif sizes.sides == 2:
+        edges[0][...] = array[:, :, last:]
+        edges[1][...] = array[:, :, :BORDER]
+
+
+def turn_kernel(sizes, place, right_side, turned, *edges):
     turned[...] = jnp.swapaxes(right_side[...], 0, 1)
-    last = sizes.extent_y - BORDER
-    for index, array in enumerate((own0.at[0], own0.at[1], turned)):
-        if sizes.sides == 1:
-            at = pl.multiple_of(jnp.where(place[1] == 0, last, 0), LANES)
-            edges[0][index] = array[:, :, pl.ds(at, BORDER)]
-        elif sizes.sides == 2:
-            edges[0][index] = array[:, :, last:]
-            edges[1][index] = array[:, :, :BORDER]
+    cut_edges(sizes, place, turned, edges)
 
 
 def message_row(sizes, place, level, slot, message, beside):
@@ -367,19 +418,24 @@
     pack_rows(sizes, place, rows, out)
 
 
-def down_kernel(sizes, place, *refs):
+def held_rows(sizes, owns, borders):
+    def held_row(level, at, row):
+        if level > 0:
+            row = at * sizes.rows[level] + row
+            return jnp.concatenate([owns[level][row], *(array[row] for array in borders[level])], axis=1)
+        sides = len(borders[0]) // 2
+        if at == 2:
+            return jnp.concatenate([owns[3][row], *(array[row] for array in borders[0][sides:])], axis=1)
+        return jnp.concatenate([owns[0][at, row], *(array[at, row] for array in borders[0][:sides])], axis=1)
+
+    return held_row
+
+
+def inner_kernel(sizes, place, *refs):
     s = sizes.sides
-    owns, turned, refs = refs[:3], refs[3], refs[4:]
-    borders0, refs = refs[:s], refs[s:]
-    pairs_of = [refs[2 * index : 2 * index + 2] for index in range(1 + s)]
-    refs = refs[2 * (1 + s) :]
-    from_prev, *beside_prev = (Arrived(place, pair, 0) for pair in pairs_of)
-    from_next, *beside_next = (Arrived(place, pair, 1) for pair in pairs_of)
-    coefs, contribution, with_far, ups, far, refs = refs[:3], refs[3], refs[4], refs[5:7], refs[7], refs[8:]
-    border1, border2, level3, sums = refs
-    slots = sizes.slots
+    owns, borders0, refs = refs[:4], refs[4 : 4 + 2 * s], refs[4 + 2 * s :]
+    border1, border2, inner0, inner1, inner2, sums = refs
     n0, n1, n2 = sizes.rows[:3]
-
     if s:
         for row in range(2 * n1):
             for side in range(s):
@@ -390,14 +446,42 @@
         for row in range(2 * n2):
             sums[row, :, :LANES] = border1[2 * row] + border1[2 * row + 1]
         narrow(sizes, place, 1, sums, border2, 2 * n2, "border", sizes.own[1] * LANES)
-
-    def held_row(level, at, row):
-        if level == 0:
-            tiles = [turned[row] if at == 2 else owns[0][at, row], *(array[at, row] for array in borders0)]
-        else:
-            row = at * sizes.rows[level] + row
-            tiles = [owns[level][row], *([(border1, border2)[level - 1][row]] if s else [])]
-        return jnp.concatenate(tiles, axis=1)
+    held_row = held_rows(sizes, owns, [borders0, [border1][:s], [border2][:s]])
+    levels = [Level(sizes, level, inner, None) for level, inner in enumerate((inner0, inner1, inner2))]
+    for index, level in enumerate(levels):
+        conduct = lambda row, index=index, level=level: held_row(index, 0, row - level.halo)
+        bound = lambda row, index=index, level=level: held_row(index, 1, row - level.halo)
+        coefficients(
+            sizes, place, index, conduct, bound, level.fx, level.fy, level.fz, level.weight, level.inner()
+        )
+        if index == 0:
+            right = lambda row: held_row(0, 2, row - 1)
+            for row in range(2, n0):
+                level.smooth[row - 1] = level.weight[row - 1] * right(row)
+            add = in_pairs(sums, lambda row: ((row - 3) // 2, row % 2 == 1))
+            field = lambda row, level=level: level.smooth[row - 1]
+            emit = lambda row, value: add(row, right(row) - value)
+            sweep(3, n0 - 2, field, bound, level.fx, level.fy, level.fz, emit)
+        if index == 1:
+            narrow(sizes, place, 0, sums, level.source.inner, n1 - 2)
+            for row in range(2, n1):
+                level.smooth[row] = level.weight[row] * level.source[row]
+
+
+def down_kernel(sizes, place, *refs):
+    s = sizes.sides
+    owns, borders0, refs = refs[:4], refs[4 : 4 + 2 * s], refs[4 + 2 * s :]
+    pairs_of = [refs[2 * index : 2 * index + 2] for index in range(1 + s)]
+    refs = refs[2 * (1 + s) :]
+    from_prev, *beside_prev = (Arrived(place, pair, 0) for pair in pairs_of)
+    from_next, *beside_next = (Arrived(place, pair, 1) for pair in pairs_of)
+    (border1, border2), inners, refs = refs[:2], refs[2:5], refs[5:]
+    outers, contribution, with_far, ups, far, refs = refs[:3], refs[3], refs[4], refs[5:7], refs[7], refs[8:]
+    level3, sums = refs
+    slots = sizes.slots
+    n0, n1, n2 = sizes.rows[:3]
+    levels = [Level(sizes, index, inner, outer) for index, (inner, outer) in enumerate(zip(inners, outers))]
+    held_row = held_rows(sizes, owns, [borders0, [border1][:s], [border2][:s]])
 
     def prev_row(level, index):
         return message_row(sizes, place, level, slots[index], from_prev, beside_prev)
@@ -412,47 +496,69 @@
             return next_row(0, 0)
         return held_row(0, 0, row - 1)
 
+    zero = jnp.zeros((sizes.depth, sizes.held[0]), f32)
+    level = levels[0]
     bound0 = lambda row: held_row(0, 1, row - 1)
-    fx, fy, fz, weight, v0 = parts(coefs[0], coefficient_rows(sizes, 0))
-    coefficients(sizes, place, 0, n0 + 2, conduct0, bound0, fx, fy, fz, weight)
-    for row in range(n0):
-        v0[row] = weight[row] * held_row(0, 2, row)
-    own_defect(n0 + 2, v0, lambda row: held_row(0, 2, row - 1), bound0, fx, fy, fz, sums, 1)
-    smooths, sources = [], []
-    for level, first in ((1, 1), (2, 4)):
-        n = sizes.rows[level]
-        fx, fy, fz, weight, binding, source, smooth = parts(coefs[level], coefficient_rows(sizes, level))
-        held = sizes.held[level]
-        narrow(sizes, place, level - 1, sums.at[:, :, : sizes.held[level - 1]], source, n + 2)
-        binding[0] = prev_row(level, first + 2)
-        binding[n + 1] = next_row(level, first + 2)
+    right = lambda row: held_row(0, 2, row - 1)
+    coefficients(
+        sizes, place, 0, conduct0, bound0, level.fx, level.fy, level.fz, level.weight, level.outer()
+    )
+    for row in (1, n0):
+        level.smooth[row - 1] = level.weight[row - 1] * right(row)
+    first_slot = lambda row: (row + 1) // 2
+    add = in_pairs(
+        sums,
+        lambda row: (first_slot(row) - (n1 - 2 if row > n0 // 2 else 0), row % 2 == 1 or row == 0),
+    )
+    field = lambda row, level=level: level.smooth[row - 1] if 0 < row < n0 + 1 else zero
+    emit = lambda row, value: add(row, right(row) - value)
+    add(0, level.fx[0] * field(1))
+    sweep(1, 2, field, bound0, level.fx, level.fy, level.fz, emit)
+    sweep(n0 - 1, n0, field, bound0, level.fx, level.fy, level.fz, emit)
+    add(n0 + 1, level.fx[n0] * field(n0))
+    fine_held = sizes.held[0]
+    for index, first in ((1, 1), (2, 4)):
+        level, n = levels[index], sizes.rows[index]
+        held = sizes.held[index]
+        narrow(
+            sizes, place, index - 1, sums.at[:, :, :fine_held], level.source.outer, level.source.outer.shape[0]
+        )
+        binding = level.binding
+        binding[0] = prev_row(index, first + 2)
+        binding[n + 1] = next_row(index, first + 2)
         for row in range(n):
-            binding[row + 1] = held_row(level, 1, row)
-
-        def conduct(row, n=n, level=level, first=first):
+            binding[row + 1] = held_row(index, 1, row)
+
+        def conduct(row, n=n, index=index, first=first):
             if row < 2:
-                return prev_row(level, first + row)
+                return prev_row(index, first + row)
             if row >= n + 2:
-                return next_row(level, first + row - n - 2)
-            return held_row(level, 0, row - 2)
+                return next_row(index, first + row - n - 2)
+            return held_row(index, 0, row - 2)
 
         bound = lambda row, binding=binding: binding[row - 1]
-        coefficients(sizes, place, level, n + 4, conduct, bound, fx, fy, fz, weight)
-        for row in range(n + 2):
-            smooth[row] = weight[row] * source[row]
-        mine = lambda row, source=source: source[row - 1]
-        own_defect(n + 4, smooth, mine, bound, fx, fy, fz, sums.at[:, :, :held], 0)
-        smooths.append(smooth)
-        sources.append(source)
+        coefficients(
+            sizes, place, index, conduct, bound, level.fx, level.fy, level.fz, level.weight, level.outer()
+        )
+        for row in level.outer()[2] if index == 1 else range(1, n + 3):
+            level.smooth[row - 1] = level.weight[row - 1] * level.source[row - 1]
+        zero = jnp.zeros((sizes.depth, held), f32)
+        field = lambda row, level=level, n=n, zero=zero: level.smooth[row - 1] if 0 < row < n + 3 else zero
+        add = in_pairs(sums.at[:, :, :held], lambda row: (row // 2, row % 2 == 0))
+        emit = lambda row, value, level=level, add=add: add(row, level.source[row - 1] - value)
+        add(0, level.fx[0] * field(1))
+        sweep(1, n + 2, field, bound, level.fx, level.fy, level.fz, emit)
+        add(n + 3, level.fx[n + 2] * field(n + 2))
+        fine_held = held
     narrow(sizes, place, 2, sums.at[:, :, : sizes.held[2]], level3, 3)
-
     for at in (0, 1):
         sums[at, :, : sizes.held[2]] = held_row(2, at, 0) + held_row(2, at, 1)
     narrow(sizes, place, 2, sums.at[:, :, : sizes.held[2]], level3.at[3:5], 2)
     tiles = packing(sizes, 5)[2]
     pack_rows(sizes, place, [level3[row] for row in range(5)], contribution)
     with_far[0:tiles] = contribution[...]
-    (s1, s2), (v1, v2) = sources, smooths
+    v0, s1, v1 = levels[0].smooth, levels[1].source, levels[1].smooth
+    s2, v2 = levels[2].source, levels[2].smooth
     next_rows = (v0[n0 - 1], s1[n1], s1[n1 + 1], v1[n1 - 1], s2[n2], s2[n2 + 1], v2[n2 - 1])
     prev_rows = (v0[0], s1[1], s1[0], v1[2], s2[1], s2[0], v2[2])
     for slot, next_row, prev_row in zip(slots, next_rows, prev_rows):
@@ -470,7 +576,7 @@
     def update(row, value):
         target(row, field(row) + weight[row - 1] * (source(row) - value))
 
-    sweep(count, field, binding, fx, fy, fz, update)
+    sweep(1, count - 2, field, binding, fx, fy, fz, update)
 
 
 def store(array, first):
@@ -498,7 +604,8 @@
             source = merged.at[1 : count + 1]
         bound = lambda row, binding=binding: binding[row - 1]
         at_row = lambda row, conduct=conduct: conduct[row]
-        coefficients(sizes, place, level, count + 2, at_row, bound, fx, fy, fz, weight)
+        every = (range(1, count + 2), range(1, count + 1), range(1, count + 1))
+        coefficients(sizes, place, level, at_row, bound, fx, fy, fz, weight, every)
         for row in range(count):
             smooth[row + 1] = weight[row] * source[row]
         if index < 2:
@@ -519,7 +626,7 @@
                 else:
                     sums[slot, :, :LANES] = sums[slot, :, :LANES] + value
 
-            sweep(count + 2, lambda row, smooth=smooth: smooth[row], bound, fx, fy, fz, add)
+            sweep(1, count, lambda row, smooth=smooth: smooth[row], bound, fx, fy, fz, add)
             narrow(sizes, place, level, sums, source_next, half)
 
     fx, fy, fz, weight, conduct, binding, source, smooth, iterate = coarse[2]
@@ -549,12 +656,13 @@
 
 def up_kernel(sizes, place, coarse, *refs):
     s = sizes.sides
-    pair, far_pair, coefs, (own0, turned) = refs[:2], refs[2:4], refs[4:7], refs[7:9]
+    pair, far_pair, inners, outers, owns = refs[:2], refs[2:4], refs[4:7], refs[7:10], refs[10:12]
+    levels = [Level(sizes, index, inner, outer) for index, (inner, outer) in enumerate(zip(inners, outers))]
     from_prev, from_next = (Arrived(place, pair, forward) for forward in (0, 1))
     tiles = packing(sizes, 5)[2]
     far_pair = (far_pair[0].at[tiles : tiles + sizes.held[2] // LANES], far_pair[1])
     fars = [Arrived(place, far_pair, forward, 2) for forward in (0, 1)]
-    borders0, out, refs = refs[9 : 9 + s], refs[9 + s], refs[10 + s :]
+    borders0, out, refs = refs[12 : 12 + 2 * s], refs[12 + 2 * s], refs[13 + 2 * s :]
     total1, total2, result = refs[:3]
     over2, over1, over0, lift2, lift1, lift0, it2, it1, it0, semaphores = refs[3:]
     slots = sizes.slots
@@ -562,12 +670,13 @@
     width = sizes.own[0] * LANES
 
     widen(sizes, place, 2, coarse, over2, 3)
-    for level, array, first, totals, over, lift, target, upper in (
-        (2, coefs[2], 4, total2, over2, lift2, it2, over1),
-        (1, coefs[1], 1, total1, over1, lift1, it1, over0),
+    for level, first, totals, over, lift, target, upper in (
+        (2, 4, total2, over2, lift2, it2, over1),
+        (1, 1, total1, over1, lift1, it1, over0),
     ):
-        n = sizes.rows[level]
-        fx, fy, fz, weight, binding, own, smooth = parts(array, coefficient_rows(sizes, level))
+        n, kept = sizes.rows[level], levels[level]
+        fx, fy, fz, weight, binding = kept.fx, kept.fy, kept.fz, kept.weight, kept.binding
+        own, smooth = kept.source, kept.smooth
         edge = {}
         for row, message, index in (
             (1, from_prev, first),
@@ -596,18 +705,15 @@
         relax(n + 4, field, (fx, fy, fz, weight, bound), mine, store(target, 1))
         widen(sizes, place, level - 1, target, upper, n + 2)
 
-    def held_row(at, row):
-        own = turned[row - 1] if at == 2 else own0[at, row - 1]
-        return jnp.concatenate([own, *(array[at, row - 1] for array in borders0)], axis=1)
-
-    fx, fy, fz, weight, v0 = parts(coefs[0], coefficient_rows(sizes, 0))
+    held_row = held_rows(sizes, [owns[0], None, None, owns[1]], [borders0])
+    fx, fy, fz, weight, v0 = levels[0].fx, levels[0].fy, levels[0].fz, levels[0].weight, levels[0].smooth
     lift0[0] = fringed_row(sizes, 0, 0, from_prev) + over0[0]
     lift0[n0 + 1] = fringed_row(sizes, 0, 0, from_next) + over0[n1 + 1]
     for row in range(1, n0 + 1):
         lift0[row] = v0[row - 1] + over0[(row + 1) // 2]
     field = lambda row: lift0[row]
-    bound = lambda row: held_row(1, row)
-    relax(n0 + 2, field, (fx, fy, fz, weight, bound), lambda row: held_row(2, row), store(it0, 1))
+    bound = lambda row: held_row(0, 1, row - 1)
+    relax(n0 + 2, field, (fx, fy, fz, weight, bound), lambda row: held_row(0, 2, row - 1), store(it0, 1))
     step = sizes.depth // CHUNKS
     copies = []
     for chunk in range(CHUNKS):
@@ -650,6 +756,14 @@
     return []
 
 
+def edge_columns(edges, sizes):
+    if sizes.sides == 1:
+        return [lax.ppermute(edges[0], "width", [(0, 1), (1, 0)])]
+    if sizes.sides == 2:
+        return [along(edges[1], "width", -1), along(edges[0], "width", 1)]
+    return []
+
+
 def stages(count):
     stride = 1
     while stride < count:
@@ -686,48 +800,55 @@
     held = [(depth, count) for count in sizes.held]
     down_message = (sizes.tiles, *tile)
     up_message = (sizes.tiles + 1, *tile)
-    own0, own1, own2, *to_pairs = call(
+    own0, own1, own2, first, second, *edges = call(
         functools.partial(start_kernel, sizes),
         "start",
         1.1,
-        [(2, n0, *own[0]), (2 * n1, *own[1]), (2 * n2, *own[2]), down_message, down_message],
+        [(2, n0, *own[0]), (2 * n1, *own[1]), (2 * n2, *own[2]), down_message, down_message]
+        + [(2, n0, depth, BORDER)] * s,
         [(2 * n1, *own[0])],
         place,
         [diffusivity, reaction],
     )
-    halos = exchange(to_pairs, 1)
+    borders = edge_columns(edges, sizes)
+    halos = exchange([first, second], 1)
     turned, *edges = call(
         functools.partial(turn_kernel, sizes),
         "turn",
         0.7,
-        [(n0, *own[0])] + [(3, n0, depth, BORDER)] * s,
+        [(n0, *own[0])] + [(n0, depth, BORDER)] * s,
         [],
         place,
-        [right_side, own0],
+        [right_side],
     )
-    if s == 1:
-        borders = [lax.ppermute(edges[0], "width", [(0, 1), (1, 0)])]
-    elif s == 2:
-        borders = [along(edges[1], "width", -1), along(edges[0], "width", 1)]
-    else:
-        borders = []
+    borders += edge_columns(edges, sizes)
     plan = list(stages(sizes.span_count))
+
+    part = packing(sizes, 5)[2]
+    far = (sizes.held[2] // LANES, *tile)
+    inners = [(sum(inner_rows(sizes, level)), *held[level]) for level in range(3)]
+    outers = [(sum(outer_rows(sizes, level)), *held[level]) for level in range(3)]
+    inner = call(
+        functools.partial(inner_kernel, sizes),
+        "inner",
+        0.5,
+        [(2 * n1, *tile), (2 * n2, *tile), *inners],
+        [(2 * n1, *held[0])],
+        place,
+        [own0, own1, own2, turned, *borders],
+    )
+    halos, inner = lax.optimization_barrier((halos, inner))
     sides = beside(halos, sizes)
-
-    part = packing(sizes, 5)[2]
-    lengths = [sum(coefficient_rows(sizes, level)) for level in range(3)]
-    far = (sizes.held[2] // LANES, *tile)
-    coefs = [(lengths[level], *held[level]) for level in range(3)]
     downs = call(
         functools.partial(down_kernel, sizes),
         "down",
-        3.6,
-        [*coefs, (part, *tile), (part + far[0], *tile), up_message, up_message, far],
-        [(2 * n1, *tile), (2 * n2, *tile), (5, *tile), (max(2 * n1, n1 + 2), *held[0])],
+        2.5,
+        [*outers, (part, *tile), (part + far[0], *tile), up_message, up_message, far],
+        [(5, *tile), (n1 + 2, *held[0])],
         place,
-        [own0, own1, own2, turned, *borders, *halos, *sum(sides, [])],
+        [own0, own1, own2, turned, *borders, *halos, *sum(sides, []), *inner],
     )
-    coefs_out, blocks, with_far, ups, far_second = downs[:3], downs[3], downs[4], list(downs[5:7]), downs[7]
+    outer, blocks, with_far, ups, far_second = downs[:3], downs[3], downs[4], list(downs[5:7]), downs[7]
     far_rows = None
     for stride, radix in plan[:-1]:
         count = stride * radix
@@ -775,7 +896,7 @@
         [diffusivity.shape],
         scratch,
         place,
-        [coarse, *received, *coefs_out, own0, turned, *borders],
+        [coarse, *received, *inner[2:], *outer, own0, turned, *borders],
         copies=CHUNKS,
         far_out=True,
     )

time: 54.1 us -> 53.8 us (level)
  waiting for transfers between devices: 23.5 us -> 22.2 us
  starting transfers between devices: 15.6 us -> 16.2 us
    ppermute x5, waiting for transfers between devices: 7.68 us -> 5.14 us  [exchange(): lax.ppermute(value, 'span', route)]
    ppermute x1 -> x2, waiting for transfers between devices: 0.01 us -> 1.19 us  [edge_columns(): return [lax.ppermute(edges[0], 'width', [(0, 1), (1, 0)])]]
    ppermute x1 -> x2, starting transfers between devices: 0.07 us -> 0.74 us  [edge_columns(): return [lax.ppermute(edges[0], 'width', [(0, 1), (1, 0)])]]
    pallas_call x6 -> x7, Pallas kernels: 12.5 us -> 12.8 us  [call(): pl.pallas_call(body, name=name, out_shape=[jax.ShapeDtypeStruct(shape, f3...]
  transfers between devices with their start and end apart: 14 -> 15, of which waited for: 7 -> 8; matrix products, arithmetic and copies ran while one was open for 0% -> 0% of each run, Pallas kernels for 8% -> 12%
where the time goes in v13:
time: 53.8 us; the launch traced here: 53.5 us
  waiting for transfers between devices  22.2 us (41%)
  starting transfers between devices  16.2 us (30%)
  Pallas kernels  12.8 us (24%)
  local copies, waits for them, and re-layouts  2.09 us (4%)
    ppermute x6, waiting for transfers between devices, swap(): lax.ppermute(others.get(step, value), 'span', [(device, device ^ step * s...  14.6 us
    pallas_call x7, Pallas kernels, call(): pl.pallas_call(body, name=name, out_shape=[jax.ShapeDtypeStruct(shape, f3...  12.8 us
    ppermute x6, starting transfers between devices, swap(): lax.ppermute(others.get(step, value), 'span', [(device, device ^ step * s...  9.38 us
    ppermute x5, starting transfers between devices, exchange(): lax.ppermute(value, 'span', route)  5.61 us
    ppermute x5, waiting for transfers between devices, exchange(): lax.ppermute(value, 'span', route)  5.14 us
    unnamed x6, local copies, waits for them, and re-layouts  2.09 us
    ppermute x2, waiting for transfers between devices, beside(): lax.ppermute(value, 'width', [(0, 1), (1, 0)])  1.26 us
    ppermute x2, waiting for transfers between devices, edge_columns(): return [lax.ppermute(edges[0], 'width', [(0, 1), (1, 0)])]  1.19 us
  transfers between devices with their start and end apart: 15, of which 8 were waited for; matrix products, arithmetic and copies ran while one was open for 0% of the time, Pallas kernels for 12%

profile of v13, /device:TPU:0, one launch (start us, length us, event | category | flops | bytes accessed | tf_op | source)
XLA Modules:
  0.0 53.5 jit_solution(2838424452102064467)
XLA Ops:
  0.1 1.0 %copy-done = f32[32,8,512]{2,1,0:T(8,128)S(1)} copy-done((f32[32,8,512]{2,1,0:T(8,128)S(1)}, f32[32,8,512]{2,1,0:T(8,128)}, u32[]{:S(2)}) %copy-start) | copy-done | bytes 524312
  1.1 1.0 %copy-done.1 = f32[32,8,512]{2,1,0:T(8,128)S(1)} copy-done((f32[32,8,512]{2,1,0:T(8,128)S(1)}, f32[32,8,512]{2,1,0:T(8,128)}, u32[]{:S(2)}) %copy-start.1) | copy-done | bytes 524312
  2.2 1.1 %start.1 = (f32[2,8,32,512]{3,2,1,0:T(8,128)S(1)}, f32[8,32,256]{2,1,0:T(8,128)S(1)}, f32[4,32,128]{2,1,0:T(8,128)S(1)}, f32[13,32,128]{2,1,0:T(8,128)S(1)}, f32...) custom-call(s32[2]{0:T(128)S(1)} %pad_add_fusion.place, f32[32,8,512]{2,1,0:T(8,128)S(1)} %copy-done, ...), custom_call_target="tpu_custom_call" | custom-call | flops 1264999936 | bytes 4059000 | tf_op jit(solution)/shard_map/start/pallas_call | solution.py:733
  3.8 2.6 %collective-permute-start.2 = (f32[13,32,128]{2,1,0:T(8,128)S(1)}, f32[13,32,128]{2,1,0:T(8,128)S(1)}, u32[]{:S(2)}, u32[]{:S(2)}) collective-permute-start(f32[13,32,128]{2,1,0:T(8,128)S(1)} %get-tuple-element.46), channel_id=1, source_target_pairs={{0,2},{2,0},{4,6},{6,4},{8,10},{10,8},{12,14},{14,12},{16,18},{18,... | collective-permute-start | bytes 638984 | tf_op jit(solution)/shard_map/ppermute | solution.py:789
  6.4 0.7 %collective-permute-start.3 = (f32[13,32,128]{2,1,0:T(8,128)S(1)}, f32[13,32,128]{2,1,0:T(8,128)S(1)}, u32[]{:S(2)}, u32[]{:S(2)}) collective-permute-start(f32[13,32,128]{2,1,0:T(8,128)S(1)} %get-tuple-element.47), channel_id=1, source_target_pairs={{2,4},{4,2},{6,8},{8,6},{10,12},{12,10},{14,16},{16,14},{18,20},{2... | collective-permute-start | bytes 638984 | tf_op jit(solution)/shard_map/ppermute | solution.py:789
  7.1 0.7 %turn.1 = (f32[8,32,512]{2,1,0:T(8,128)S(1)}, f32[8,32,128]{2,1,0:T(8,128)S(1)}) custom-call(s32[2]{0:T(128)S(1)} %pad_add_fusion.place, f32[32,8,512]{2,1,0:T(8,128)S(1)} %copy-done.2), custom_call_target="tpu_custom_call" | custom-call | flops 805000000 | bytes 2583000 | tf_op jit(solution)/shard_map/turn/pallas_call | solution.py:733
  8.0 1.2 %collective-permute-done.1.refs_5_.refs_13_ = f32[8,32,128]{2,1,0:T(8,128)S(1)} collective-permute-done((f32[8,32,128]{2,1,0:T(8,128)S(1)}, f32[8,32,128]{2,1,0:T(8,128)S(1)}, u32[]{:S(2)}, u32[]{:S(2)}) %collective-permute-start.1) | collective-permute-done | bytes 131104 | tf_op jit(solution)/shard_map/ppermute | solution.py:761
  9.2 1.8 %inner.1 = (f32[8,32,128]{2,1,0:T(8,128)S(1)}, f32[4,32,128]{2,1,0:T(8,128)S(1)}, f32[35,32,640]{2,1,0:T(8,128)S(1)}, f32[17,32,384]{2,1,0:T(8,128)S(1)}, f32[5,32,256]{2,1,0:T(8,128)S(1)}) custom-call(s32[2]{0:T(128)S(1)} %pad_add_fusion.place, f32[2,8,32,512]{3,2,1,0:T(8,128)S(1)} %get-tuple-element.40.refs_0_.refs_10_, ...), custom_call_target="tpu_custom_call" | custom-call | flops 575000000 | bytes 1845000 | tf_op jit(solution)/shard_map/inner/pallas_call | solution.py:733
  11.0 5.1 %collective-permute-done.2.refs_6_ = f32[13,32,128]{2,1,0:T(8,128)S(1)} collective-permute-done((f32[13,32,128]{2,1,0:T(8,128)S(1)}, f32[13,32,128]{2,1,0:T(8,128)S(1)}, u32[]{:S(2)}, u32[]{:S(2)}) %collective-permute-start.2) | collective-permute-done | bytes 213024 | tf_op jit(solution)/shard_map/ppermute | solution.py:789
  16.6 1.0 %collective-permute-done.4.refs_8_ = f32[13,32,128]{2,1,0:T(8,128)S(1)} collective-permute-done((f32[13,32,128]{2,1,0:T(8,128)S(1)}, f32[13,32,128]{2,1,0:T(8,128)S(1)}, u32[]{:S(2)}, u32[]{:S(2)}) %collective-permute-start.4) | collective-permute-done | bytes 213024 | tf_op jit(solution)/shard_map/ppermute | solution.py:753
  17.9 2.3 %down.1 = (f32[6,32,640]{2,1,0:T(8,128)S(1)}, f32[26,32,384]{2,1,0:T(8,128)S(1)}, f32[24,32,256]{2,1,0:T(8,128)S(1)}, f32[4,32,128]{2,1,0:T(8,128)S(1)}, f32[6,3...) custom-call(s32[2]{0:T(128)S(1)} %pad_add_fusion.place, ...), custom_call_target="tpu_custom_call" | custom-call | flops 2875000064 | bytes 9225000 | tf_op jit(solution)/shard_map/down/pallas_call | solution.py:733
  20.2 2.2 %collective-permute-start.7 = (f32[6,32,128]{2,1,0:T(8,128)S(1)}, f32[6,32,128]{2,1,0:T(8,128)S(1)}, u32[]{:S(2)}, u32[]{:S(2)}) collective-permute-start(f32[6,32,128]{2,1,0:T(8,128)S(1)} %get-tuple-element.61), channel_id=1, source_target_pairs={{0,4},{2,6},{4,0},{6,2},{8,12},{10,14},{12,8},{14,10},{16,20},{18,... | collective-permute-start | bytes 294920 | tf_op jit(solution)/shard_map/ppermute | solution.py:779
  22.4 2.7 %collective-permute-start.8 = (f32[4,32,128]{2,1,0:T(8,128)S(1)}, f32[4,32,128]{2,1,0:T(8,128)S(1)}, u32[]{:S(2)}, u32[]{:S(2)}) collective-permute-start(f32[4,32,128]{2,1,0:T(8,128)S(1)} %get-tuple-element.63.refs_0_), channel_id=1, source_target_pairs={{0,6},{2,4},{4,2},{6,0},{8,14},{10,12},{12,10},{14,8},{16,22},{18,... | collective-permute-start | bytes 196616 | tf_op jit(solution)/shard_map/ppermute | solution.py:779
  25.1 2.9 %collective-permute-done.8.refs_3_ = f32[4,32,128]{2,1,0:T(8,128)S(1)} collective-permute-done((f32[4,32,128]{2,1,0:T(8,128)S(1)}, f32[4,32,128]{2,1,0:T(8,128)S(1)}, u32[]{:S(2)}, u32[]{:S(2)}) %collective-permute-start.8) | collective-permute-done | bytes 65568 | tf_op jit(solution)/shard_map/ppermute | solution.py:779
  28.0 1.4 %collective-permute-done.6.refs_1_ = f32[4,32,128]{2,1,0:T(8,128)S(1)} collective-permute-done((f32[4,32,128]{2,1,0:T(8,128)S(1)}, f32[4,32,128]{2,1,0:T(8,128)S(1)}, u32[]{:S(2)}, u32[]{:S(2)}) %collective-permute-start.6) | collective-permute-done | bytes 65568 | tf_op jit(solution)/shard_map/ppermute | solution.py:779
  29.4 1.1 %collective-permute-start.12 = (f32[14,32,128]{2,1,0:T(8,128)S(1)}, f32[14,32,128]{2,1,0:T(8,128)S(1)}, u32[]{:S(2)}, u32[]{:S(2)}) collective-permute-start(f32[14,32,128]{2,1,0:T(8,128)S(1)} %get-tuple-element.67), channel_id=1, source_target_pairs={{0,2},{2,0},{4,6},{6,4},{8,10},{10,8},{12,14},{14,12},{16,18},{18,... | collective-permute-start | bytes 688136 | tf_op jit(solution)/shard_map/ppermute | solution.py:789
  30.4 0.9 %merge.1.refs_0_ = f32[9,32,128]{2,1,0:T(8,128)S(1)} custom-call(s32[2]{0:T(128)S(1)} %pad_add_fusion.place, f32[4,32,128]{2,1,0:T(8,128)S(1)} %get-tuple-element.63.refs_0_, f32[4,32,128]{2,1,0:T(8,128)S(1)} %collective-permute-done.6.refs_1_, f32[6,32,128]{2,1,0:T(8,128)S(1)} %collective-permute-done.7.refs_2_, ...), custom_call_target="tpu_custom_call" | custom-call | flops 1035000000 | bytes 3321000 | tf_op jit(solution)/shard_map/merge/pallas_call | solution.py:733
  31.3 3.7 %collective-permute-start.11 = (f32[9,32,128]{2,1,0:T(8,128)S(1)}, f32[9,32,128]{2,1,0:T(8,128)S(1)}, u32[]{:S(2)}, u32[]{:S(2)}) collective-permute-start(f32[9,32,128]{2,1,0:T(8,128)S(1)} %merge.1.refs_0_), channel_id=1, source_target_pairs={{0,24},{2,26},{4,28},{6,30},{8,16},{10,18},{12,20},{14,22},{16,8},... | collective-permute-start | bytes 442376 | tf_op jit(solution)/shard_map/ppermute | solution.py:779
  35.0 0.8 %collective-permute-start.9 = (f32[9,32,128]{2,1,0:T(8,128)S(1)}, f32[9,32,128]{2,1,0:T(8,128)S(1)}, u32[]{:S(2)}, u32[]{:S(2)}) collective-permute-start(f32[9,32,128]{2,1,0:T(8,128)S(1)} %merge.1.refs_0_), channel_id=1, source_target_pairs={{0,8},{2,10},{4,12},{6,14},{8,0},{10,2},{12,4},{14,6},{16,24},{18,... | collective-permute-start | bytes 442376 | tf_op jit(solution)/shard_map/ppermute | solution.py:779
  36.4 0.7 %collective-permute-start.13 = (f32[14,32,128]{2,1,0:T(8,128)S(1)}, f32[14,32,128]{2,1,0:T(8,128)S(1)}, u32[]{:S(2)}, u32[]{:S(2)}) collective-permute-start(f32[14,32,128]{2,1,0:T(8,128)S(1)} %get-tuple-element.70), channel_id=1, source_target_pairs={{2,4},{4,2},{6,8},{8,6},{10,12},{12,10},{14,16},{16,14},{18,20},{2... | collective-permute-start | bytes 688136 | tf_op jit(solution)/shard_map/ppermute | solution.py:789
  37.1 2.8 %collective-permute-done.11.refs_3_ = f32[9,32,128]{2,1,0:T(8,128)S(1)} collective-permute-done((f32[9,32,128]{2,1,0:T(8,128)S(1)}, f32[9,32,128]{2,1,0:T(8,128)S(1)}, u32[]{:S(2)}, u32[]{:S(2)}) %collective-permute-start.11) | collective-permute-done | bytes 147488 | tf_op jit(solution)/shard_map/ppermute | solution.py:779
  40.0 7.5 %collective-permute-done.10.refs_2_ = f32[9,32,128]{2,1,0:T(8,128)S(1)} collective-permute-done((f32[9,32,128]{2,1,0:T(8,128)S(1)}, f32[9,32,128]{2,1,0:T(8,128)S(1)}, u32[]{:S(2)}, u32[]{:S(2)}) %collective-permute-start.10) | collective-permute-done | bytes 147488 | tf_op jit(solution)/shard_map/ppermute | solution.py:779
  47.5 2.9 %coarse.1 = f32[3,32,128]{2,1,0:T(8,128)S(1)} custom-call(s32[2]{0:T(128)S(1)} %pad_add_fusion.place, f32[9,32,128]{2,1,0:T(8,128)S(1)} %merge.1.refs_0_, f32[9,32,128]{2,1,0:T(8,128)S(1)} %collective-permute-done.9.refs_1_, f32[9,32,128]{2,1,0:T(8,128)S(1)} %collective-permute-done.10.refs_2_, f32[9,32,128]{2,1,0:T(8,128)S(1)} %collective-permute-done.11.refs_3_), custom_call_target="tpu_custom_call" | custom-call | flops 3335000064 | bytes 10701000 | tf_op jit(solution)/shard_map/coarse/pallas_call | solution.py:733
  50.4 3.1 %up.1 = f32[32,8,512]{2,1,0:T(8,128)} custom-call(s32[2]{0:T(128)S(1)} %pad_add_fusion.place, f32[3,32,128]{2,1,0:T(8,128)S(1)} %coarse.1, f32[14,32,128]{2,1,0:T(8,128)S(1)} %collective-permute-done.12.refs_0_, f32[14,32,128]{2,1,0:T(8,128)S(1)} %collective-permute-done.13.refs_1_, f32[6,32,128]{2,1,0:T(8,128)S(1)} %collective-permute-done.7.refs_2_, ...), custom_call_target="tpu_custom_call" | custom-call | flops 3449999872 | bytes 11070000 | tf_op jit(solution)/shard_map/up/pallas_call | solution.py:733
  (20 shorter events, 2.3 us)
Async XLA Ops:
  0.1 1.0 %copy-start = (f32[32,8,512]{2,1,0:T(8,128)S(1)}, f32[32,8,512]{2,1,0:T(8,128)}, u32[]{:S(2)}) copy-start(f32[32,8,512]{2,1,0:T(8,128)} %conduct.1) | copy-start | bytes 1572868
  1.1 1.0 %copy-start.1 = (f32[32,8,512]{2,1,0:T(8,128)S(1)}, f32[32,8,512]{2,1,0:T(8,128)}, u32[]{:S(2)}) copy-start(f32[32,8,512]{2,1,0:T(8,128)} %binding.1) | copy-start | bytes 1572868
  2.2 4.9 %copy-start.2 = (f32[32,8,512]{2,1,0:T(8,128)S(1)}, f32[32,8,512]{2,1,0:T(8,128)}, u32[]{:S(2)}) copy-start(f32[32,8,512]{2,1,0:T(8,128)} %right_side.1) | copy-start | bytes 1572868
  3.3 5.9 %collective-permute-start = (f32[2,8,32,128]{3,2,1,0:T(8,128)S(1)}, f32[2,8,32,128]{3,2,1,0:T(8,128)S(1)}, u32[]{:S(2)}, u32[]{:S(2)}) collective-permute-start(f32[2,8,32,128]{3,2,1,0:T(8,128)S(1)} %get-tuple-element.44), channel_id=1, source_target_pairs={{0,1},{1,0},{2,3},{3,2},{4,5},{5,4},{6,7},{7,6},{8,9},{9,8},{10,11... | collective-permute-start | bytes 786440 | tf_op jit(solution)/shard_map/ppermute | solution.py:761
  3.8 12.3 %collective-permute-start.2 = (f32[13,32,128]{2,1,0:T(8,128)S(1)}, f32[13,32,128]{2,1,0:T(8,128)S(1)}, u32[]{:S(2)}, u32[]{:S(2)}) collective-permute-start(f32[13,32,128]{2,1,0:T(8,128)S(1)} %get-tuple-element.46), channel_id=1, source_target_pairs={{0,2},{2,0},{4,6},{6,4},{8,10},{10,8},{12,14},{14,12},{16,18},{18,... | collective-permute-start | bytes 638984 | tf_op jit(solution)/shard_map/ppermute | solution.py:789
  6.4 9.7 %collective-permute-start.3 = (f32[13,32,128]{2,1,0:T(8,128)S(1)}, f32[13,32,128]{2,1,0:T(8,128)S(1)}, u32[]{:S(2)}, u32[]{:S(2)}) collective-permute-start(f32[13,32,128]{2,1,0:T(8,128)S(1)} %get-tuple-element.47), channel_id=1, source_target_pairs={{2,4},{4,2},{6,8},{8,6},{10,12},{12,10},{14,16},{16,14},{18,20},{2... | collective-permute-start | bytes 638984 | tf_op jit(solution)/shard_map/ppermute | solution.py:789
  7.7 1.4 %collective-permute-start.1 = (f32[8,32,128]{2,1,0:T(8,128)S(1)}, f32[8,32,128]{2,1,0:T(8,128)S(1)}, u32[]{:S(2)}, u32[]{:S(2)}) collective-permute-start(f32[8,32,128]{2,1,0:T(8,128)S(1)} %get-tuple-element.45), channel_id=1, source_target_pairs={{0,1},{1,0},{2,3},{3,2},{4,5},{5,4},{6,7},{7,6},{8,9},{9,8},{10,11... | collective-permute-start | bytes 393224 | tf_op jit(solution)/shard_map/ppermute | solution.py:761
  16.1 1.5 %collective-permute-start.4 = (f32[13,32,128]{2,1,0:T(8,128)S(1)}, f32[13,32,128]{2,1,0:T(8,128)S(1)}, u32[]{:S(2)}, u32[]{:S(2)}) collective-permute-start(f32[13,32,128]{2,1,0:T(8,128)S(1)} %collective-permute-done.2.refs_6_), channel_id=1, source_target_pairs={{0,1},{1,0},{2,3},{3,2},{4,5},{5,4},{6,7},{7,6},{8,9},{9,8},{10,11... | collective-permute-start | bytes 638984 | tf_op jit(solution)/shard_map/ppermute | solution.py:753
  16.1 1.8 %collective-permute-start.5 = (f32[13,32,128]{2,1,0:T(8,128)S(1)}, f32[13,32,128]{2,1,0:T(8,128)S(1)}, u32[]{:S(2)}, u32[]{:S(2)}) collective-permute-start(f32[13,32,128]{2,1,0:T(8,128)S(1)} %collective-permute-done.3.refs_7_), channel_id=1, source_target_pairs={{0,1},{1,0},{2,3},{3,2},{4,5},{5,4},{6,7},{7,6},{8,9},{9,8},{10,11... | collective-permute-start | bytes 638984 | tf_op jit(solution)/shard_map/ppermute | solution.py:753
  20.2 9.2 %collective-permute-start.7 = (f32[6,32,128]{2,1,0:T(8,128)S(1)}, f32[6,32,128]{2,1,0:T(8,128)S(1)}, u32[]{:S(2)}, u32[]{:S(2)}) collective-permute-start(f32[6,32,128]{2,1,0:T(8,128)S(1)} %get-tuple-element.61), channel_id=1, source_target_pairs={{0,4},{2,6},{4,0},{6,2},{8,12},{10,14},{12,8},{14,10},{16,20},{18,... | collective-permute-start | bytes 294920 | tf_op jit(solution)/shard_map/ppermute | solution.py:779
  22.4 5.6 %collective-permute-start.8 = (f32[4,32,128]{2,1,0:T(8,128)S(1)}, f32[4,32,128]{2,1,0:T(8,128)S(1)}, u32[]{:S(2)}, u32[]{:S(2)}) collective-permute-start(f32[4,32,128]{2,1,0:T(8,128)S(1)} %get-tuple-element.63.refs_0_), channel_id=1, source_target_pairs={{0,6},{2,4},{4,2},{6,0},{8,14},{10,12},{12,10},{14,8},{16,22},{18,... | collective-permute-start | bytes 196616 | tf_op jit(solution)/shard_map/ppermute | solution.py:779
  25.1 4.3 %collective-permute-start.6 = (f32[4,32,128]{2,1,0:T(8,128)S(1)}, f32[4,32,128]{2,1,0:T(8,128)S(1)}, u32[]{:S(2)}, u32[]{:S(2)}) collective-permute-start(f32[4,32,128]{2,1,0:T(8,128)S(1)} %get-tuple-element.63.refs_0_), channel_id=1, source_target_pairs={{0,2},{2,0},{4,6},{6,4},{8,10},{10,8},{12,14},{14,12},{16,18},{18,... | collective-permute-start | bytes 196616 | tf_op jit(solution)/shard_map/ppermute | solution.py:779
  29.4 7.1 %collective-permute-start.12 = (f32[14,32,128]{2,1,0:T(8,128)S(1)}, f32[14,32,128]{2,1,0:T(8,128)S(1)}, u32[]{:S(2)}, u32[]{:S(2)}) collective-permute-start(f32[14,32,128]{2,1,0:T(8,128)S(1)} %get-tuple-element.67), channel_id=1, source_target_pairs={{0,2},{2,0},{4,6},{6,4},{8,10},{10,8},{12,14},{14,12},{16,18},{18,... | collective-permute-start | bytes 688136 | tf_op jit(solution)/shard_map/ppermute | solution.py:789
  31.3 8.7 %collective-permute-start.11 = (f32[9,32,128]{2,1,0:T(8,128)S(1)}, f32[9,32,128]{2,1,0:T(8,128)S(1)}, u32[]{:S(2)}, u32[]{:S(2)}) collective-permute-start(f32[9,32,128]{2,1,0:T(8,128)S(1)} %merge.1.refs_0_), channel_id=1, source_target_pairs={{0,24},{2,26},{4,28},{6,30},{8,16},{10,18},{12,20},{14,22},{16,8},... | collective-permute-start | bytes 442376 | tf_op jit(solution)/shard_map/ppermute | solution.py:779
  35.0 12.5 %collective-permute-start.10 = (f32[9,32,128]{2,1,0:T(8,128)S(1)}, f32[9,32,128]{2,1,0:T(8,128)S(1)}, u32[]{:S(2)}, u32[]{:S(2)}) collective-permute-start(f32[9,32,128]{2,1,0:T(8,128)S(1)} %merge.1.refs_0_), channel_id=1, source_target_pairs={{0,16},{2,18},{4,20},{6,22},{8,24},{10,26},{12,28},{14,30},{16,0},... | collective-permute-start | bytes 442376 | tf_op jit(solution)/shard_map/ppermute | solution.py:779
  35.0 12.5 %collective-permute-start.9 = (f32[9,32,128]{2,1,0:T(8,128)S(1)}, f32[9,32,128]{2,1,0:T(8,128)S(1)}, u32[]{:S(2)}, u32[]{:S(2)}) collective-permute-start(f32[9,32,128]{2,1,0:T(8,128)S(1)} %merge.1.refs_0_), channel_id=1, source_target_pairs={{0,8},{2,10},{4,12},{6,14},{8,0},{10,2},{12,4},{14,6},{16,24},{18,... | collective-permute-start | bytes 442376 | tf_op jit(solution)/shard_map/ppermute | solution.py:779
  35.8 14.6 %collective-permute-start.14 = (f32[2,32,128]{2,1,0:T(8,128)S(1)}, f32[2,32,128]{2,1,0:T(8,128)S(1)}, u32[]{:S(2)}, u32[]{:S(2)}) collective-permute-start(f32[2,32,128]{2,1,0:T(8,128)S(1)} %get-tuple-element.71), channel_id=1, source_target_pairs={{4,8},{8,4},{6,10},{10,6},{12,16},{16,12},{14,18},{18,14},{20,24},... | collective-permute-start | bytes 98312 | tf_op jit(solution)/shard_map/ppermute | solution.py:789
  36.4 14.0 %collective-permute-start.13 = (f32[14,32,128]{2,1,0:T(8,128)S(1)}, f32[14,32,128]{2,1,0:T(8,128)S(1)}, u32[]{:S(2)}, u32[]{:S(2)}) collective-permute-start(f32[14,32,128]{2,1,0:T(8,128)S(1)} %get-tuple-element.70), channel_id=1, source_target_pairs={{2,4},{4,2},{6,8},{8,6},{10,12},{12,10},{14,16},{16,14},{18,20},{2... | collective-permute-start | bytes 688136 | tf_op jit(solution)/shard_map/ppermute | solution.py:789

commit v14 on v13

--- a/solution.py
+++ b/solution.py
@@ -257,7 +257,7 @@
 
 
 def start_kernel(sizes, place, conduct, binding, own0, own1, own2, first, second, *refs):
-    edges, sums = refs[: sizes.sides], refs[-1]
+    edges, sums = refs[: 2 * sizes.sides], refs[-1]
     n0, n1, n2 = sizes.rows[:3]
     for at, array in enumerate((conduct, binding)):
         own0[at] = jnp.swapaxes(array[...], 0, 1)
@@ -276,7 +276,7 @@
     for slot, next_row, prev_row in zip(sizes.slots, *ends):
         put_pair(place, (first, second), slot, next_row, prev_row)
     for at in (0, 1):
-        cut_edges(sizes, place, own0.at[at], [edge.at[at] for edge in edges])
+        cut_edges(sizes, place, own0.at[at], edges[at * sizes.sides : (at + 1) * sizes.sides])
 
 
 def cut_edges(sizes, place, array, edges):
@@ -343,65 +343,44 @@
     return jnp.concatenate(row, axis=1)
 
 
-def packing(sizes, count):
-    if sizes.sides != 1:
-        return False, count, count
-    own = -(-count // 2)
-    return True, own, own - (-count * (BORDER >> 3) // LANES)
-
-
-def border_turn(place, goal):
-    return jnp.where(place[1] == 0, (goal - LANES // 2) % LANES, (goal + (BORDER >> 3)) % LANES)
-
-
-def pack_rows(sizes, place, rows, target):
-    packed, own, tiles = packing(sizes, len(rows))
-    if not packed:
-        for index, row in enumerate(rows):
-            target[index] = row
-        return
+def packing(count):
+    return -(-count // 2)
+
+
+def pack_rows(rows, target):
+    half = LANES // 2
+    lane = lane_at(rows[0].shape)
+    for index in range(packing(len(rows))):
+        held = jnp.where(lane < half, rows[2 * index], 0.0)
+        if 2 * index + 1 < len(rows):
+            held = jnp.where(lane < half, held, pltpu.roll(rows[2 * index + 1], half, axis=1))
+        target[index] = held
+
+
+def unpack_rows(sizes, place, tiles, count, others=()):
     half, reach = LANES // 2, BORDER >> 3
-    lane = lane_at(rows[0].shape)
-    for index in range(own):
-        held = rows[2 * index]
-        other = rows[2 * index + 1] if 2 * index + 1 < len(rows) else jnp.zeros(held.shape, f32)
-        target[index] = jnp.where(lane < half, held, pltpu.roll(other, half, axis=1))
-    for index in range(own, tiles):
-        held = jnp.zeros(rows[0].shape, f32)
-        some = rows[(index - own) * (LANES // reach) :][: LANES // reach]
-        for place_at, row in enumerate(some):
-            goal = place_at * reach
-            moved = pltpu.roll(row, border_turn(place, goal), axis=1)
-            held = jnp.where((lane >= goal) & (lane < goal + reach), moved, held)
-        target[index] = held
-
-
-def unpack_rows(sizes, place, blocks, count):
-    packed, own, _ = packing(sizes, count)
-    if not packed:
-        return [blocks[index] for index in range(count)]
-    half, reach = LANES // 2, BORDER >> 3
+    lane = lane_at(tiles.shape[1:])
     rows = []
     for index in range(count):
-        held = blocks[index // 2]
-        lane = lane_at(held.shape)
-        if index % 2:
-            held = pltpu.roll(held, half, axis=1)
-        at, goal = index // (LANES // reach), index % (LANES // reach) * reach
-        back = lax.rem(LANES - border_turn(place, goal), LANES)
-        beside = pltpu.roll(blocks[own + at], back, axis=1)
-        start = jnp.where(place[1] == 0, half, LANES - reach)
-        here = (lane >= start) & (lane < start + reach)
-        rows.append(jnp.where(lane < half, held, jnp.where(here, beside, 0.0)))
+        held = tiles[index // 2]
+        row = jnp.where(lane < half, pltpu.roll(held, half, axis=1) if index % 2 else held, 0.0)
+        for side, other in enumerate(others):
+            first = LANES - reach if side else half
+            if sizes.sides == 1:
+                first = jnp.where(place[1] == 0, half, LANES - reach)
+            beside = other[index // 2]
+            beside = beside if index % 2 else pltpu.roll(beside, half, axis=1)
+            row = jnp.where((lane >= first) & (lane < first + reach), beside, row)
+        rows.append(row)
     return rows
 
 
-def merge_into(sizes, place, stride, radix, arrays, source, conduct, binding, first):
+def merge_into(sizes, place, stride, radix, arrays, source, conduct, binding, first, others=()):
     position = (place[0] // stride) % radix
     source[...] = jnp.zeros(source.shape, f32)
     for step, array in enumerate(arrays):
         at = (position ^ step) * stride
-        rows = unpack_rows(sizes, place, array, 3 * stride + 2)
+        rows = unpack_rows(sizes, place, array, 3 * stride + 2, [other[step] for other in others])
         for index, row in enumerate(rows[: stride + 2]):
             source[at + index] = source[at + index] + row
         for index in range(stride):
@@ -415,7 +394,7 @@
     count = stride * radix
     rows = [source[row] for row in range(count + 2)]
     rows += [conduct[row] for row in range(count)] + [binding[row] for row in range(count)]
-    pack_rows(sizes, place, rows, out)
+    pack_rows(rows, out)
 
 
 def held_rows(sizes, owns, borders):
@@ -423,17 +402,16 @@
         if level > 0:
             row = at * sizes.rows[level] + row
             return jnp.concatenate([owns[level][row], *(array[row] for array in borders[level])], axis=1)
-        sides = len(borders[0]) // 2
-        if at == 2:
-            return jnp.concatenate([owns[3][row], *(array[row] for array in borders[0][sides:])], axis=1)
-        return jnp.concatenate([owns[0][at, row], *(array[at, row] for array in borders[0][:sides])], axis=1)
+        own = owns[3][row] if at == 2 else owns[0][at, row]
+        sides = len(borders[0]) // 3
+        return jnp.concatenate([own, *(array[row] for array in borders[0][at * sides : (at + 1) * sides])], axis=1)
 
     return held_row
 
 
 def inner_kernel(sizes, place, *refs):
     s = sizes.sides
-    owns, borders0, refs = refs[:4], refs[4 : 4 + 2 * s], refs[4 + 2 * s :]
+    owns, borders0, refs = refs[:4], refs[4 : 4 + 3 * s], refs[4 + 3 * s :]
     border1, border2, inner0, inner1, inner2, sums = refs
     n0, n1, n2 = sizes.rows[:3]
     if s:
@@ -441,7 +419,7 @@
             for side in range(s):
                 columns = slice(side * LANES, (side + 1) * LANES)
                 at, low = row // n1, 2 * (row % n1)
-                sums[row, :, columns] = borders0[side][at, low] + borders0[side][at, low + 1]
+                sums[row, :, columns] = borders0[at * s + side][low] + borders0[at * s + side][low + 1]
         narrow(sizes, place, 0, sums, border1, 2 * n1, "border", sizes.own[0] * LANES)
         for row in range(2 * n2):
             sums[row, :, :LANES] = border1[2 * row] + border1[2 * row + 1]
@@ -470,7 +448,7 @@
 
 def down_kernel(sizes, place, *refs):
     s = sizes.sides
-    owns, borders0, refs = refs[:4], refs[4 : 4 + 2 * s], refs[4 + 2 * s :]
+    owns, borders0, refs = refs[:4], refs[4 : 4 + 3 * s], refs[4 + 3 * s :]
     pairs_of = [refs[2 * index : 2 * index + 2] for index in range(1 + s)]
     refs = refs[2 * (1 + s) :]
     from_prev, *beside_prev = (Arrived(place, pair, 0) for pair in pairs_of)
@@ -554,8 +532,8 @@
     for at in (0, 1):
         sums[at, :, : sizes.held[2]] = held_row(2, at, 0) + held_row(2, at, 1)
     narrow(sizes, place, 2, sums.at[:, :, : sizes.held[2]], level3.at[3:5], 2)
-    tiles = packing(sizes, 5)[2]
-    pack_rows(sizes, place, [level3[row] for row in range(5)], contribution)
+    tiles = packing(5)
+    pack_rows([level3[row] for row in range(5)], contribution)
     with_far[0:tiles] = contribution[...]
     v0, s1, v1 = levels[0].smooth, levels[1].source, levels[1].smooth
     s2, v2 = levels[2].source, levels[2].smooth
@@ -588,10 +566,11 @@
 
 def coarse_kernel(sizes, stride, radix, place, *refs):
     blocks, refs = refs[:radix], refs[radix:]
+    others, refs = [refs[side * radix : (side + 1) * radix] for side in range(sizes.sides)], refs[sizes.sides * radix :]
     out, merged, sums = refs[:3]
     coarse = [refs[3 + 9 * index : 12 + 9 * index] for index in range(3)]
     total = sizes.span_count
-    merge_into(sizes, place, stride, radix, blocks, merged, coarse[0][4], coarse[0][5], 1)
+    merge_into(sizes, place, stride, radix, blocks, merged, coarse[0][4], coarse[0][5], 1, others)
     zero = jnp.zeros((sizes.depth, LANES), f32)
     for index in range(3):
         level = 3 + index
@@ -659,10 +638,10 @@
     pair, far_pair, inners, outers, owns = refs[:2], refs[2:4], refs[4:7], refs[7:10], refs[10:12]
     levels = [Level(sizes, index, inner, outer) for index, (inner, outer) in enumerate(zip(inners, outers))]
     from_prev, from_next = (Arrived(place, pair, forward) for forward in (0, 1))
-    tiles = packing(sizes, 5)[2]
+    tiles = packing(5)
     far_pair = (far_pair[0].at[tiles : tiles + sizes.held[2] // LANES], far_pair[1])
     fars = [Arrived(place, far_pair, forward, 2) for forward in (0, 1)]
-    borders0, out, refs = refs[12 : 12 + 2 * s], refs[12 + 2 * s], refs[13 + 2 * s :]
+    borders0, out, refs = refs[12 : 12 + 3 * s], refs[12 + 3 * s], refs[13 + 3 * s :]
     total1, total2, result = refs[:3]
     over2, over1, over0, lift2, lift1, lift0, it2, it1, it0, semaphores = refs[3:]
     slots = sizes.slots
@@ -805,12 +784,12 @@
         "start",
         1.1,
         [(2, n0, *own[0]), (2 * n1, *own[1]), (2 * n2, *own[2]), down_message, down_message]
-        + [(2, n0, depth, BORDER)] * s,
+        + [(n0, depth, BORDER)] * 2 * s,
         [(2 * n1, *own[0])],
         place,
         [diffusivity, reaction],
     )
-    borders = edge_columns(edges, sizes)
+    borders = edge_columns(edges[:s], sizes) + edge_columns(edges[s:], sizes)
     halos = exchange([first, second], 1)
     turned, *edges = call(
         functools.partial(turn_kernel, sizes),
@@ -824,7 +803,7 @@
     borders += edge_columns(edges, sizes)
     plan = list(stages(sizes.span_count))
 
-    part = packing(sizes, 5)[2]
+    part = packing(5)
     far = (sizes.held[2] // LANES, *tile)
     inners = [(sum(inner_rows(sizes, level)), *held[level]) for level in range(3)]
     outers = [(sum(outer_rows(sizes, level)), *held[level]) for level in range(3)]
@@ -862,7 +841,7 @@
             functools.partial(merge_kernel, sizes, stride, radix),
             "merge",
             0.9,
-            [(packing(sizes, 3 * count + 2)[2], *tile)],
+            [(packing(3 * count + 2), *tile)],
             [(count + 2, *tile), (count, *tile), (count, *tile)],
             place,
             blocks,
@@ -876,14 +855,15 @@
         count = sizes.span_count >> index
         scratch += [(count + 1, *tile)] + [(count, *tile)] * 3 + [(count + 2, *tile)] + [(count, *tile)] * 2
         scratch += [(count + 2, *tile)] * 2
+    blocks, received[3] = lax.optimization_barrier((blocks, received[3]))
     (coarse,) = call(
         functools.partial(coarse_kernel, sizes, stride, radix),
         "coarse",
-        2.9,
+        0.7,
         [(n3 + 2, *tile)],
         scratch,
         place,
-        blocks,
+        [*blocks, *sum(beside(blocks, sizes), [])],
     )
     scratch = [(n1 + 2, *held[1]), (n2 + 2, *held[2]), diffusivity.shape]
     scratch += [(n3 + 2, *held[2]), (n2 + 2, *held[1]), (n1 + 2, *held[0])]

time: 53.8 us -> 54 us (level)
  the two profiles are of different devices: /device:TPU:0 before, /device:TPU:13 now
where the time goes in v14:
time: 54 us; the launch traced here: 53.7 us
  starting transfers between devices  21.2 us (39%)
  waiting for transfers between devices  17.6 us (33%)
  Pallas kernels  12.6 us (23%)
  local copies, waits for them, and re-layouts  2.09 us (4%)
    pallas_call x7, Pallas kernels, call(): pl.pallas_call(body, name=name, out_shape=[jax.ShapeDtypeStruct(shape, f3...  12.6 us
    ppermute x5, waiting for transfers between devices, exchange(): lax.ppermute(value, 'span', route)  10.7 us
    ppermute x5, starting transfers between devices, exchange(): lax.ppermute(value, 'span', route)  9.37 us
    ppermute x6, starting transfers between devices, swap(): lax.ppermute(others.get(step, value), 'span', [(device, device ^ step * s...  6.27 us
    ppermute x6, starting transfers between devices, beside(): lax.ppermute(value, 'width', [(0, 1), (1, 0)])  3.78 us
    ppermute x6, waiting for transfers between devices, swap(): lax.ppermute(others.get(step, value), 'span', [(device, device ^ step * s...  3.2 us
    ppermute x6, waiting for transfers between devices, beside(): lax.ppermute(value, 'width', [(0, 1), (1, 0)])  2.71 us
    unnamed x6, local copies, waits for them, and re-layouts  2.09 us
  transfers between devices with their start and end apart: 20, of which 14 were waited for; matrix products, arithmetic and copies ran while one was open for 0% of the time, Pallas kernels for 11%

profile of v14, /device:TPU:13, one launch (start us, length us, event | category | flops | bytes accessed | tf_op | source)
XLA Modules:
  0.0 53.7 jit_solution(13159649381088622668)
XLA Ops:
  0.1 1.0 %copy-done = f32[32,8,512]{2,1,0:T(8,128)S(1)} copy-done((f32[32,8,512]{2,1,0:T(8,128)S(1)}, f32[32,8,512]{2,1,0:T(8,128)}, u32[]{:S(2)}) %copy-start) | copy-done | bytes 524312
  1.1 1.0 %copy-done.1 = f32[32,8,512]{2,1,0:T(8,128)S(1)} copy-done((f32[32,8,512]{2,1,0:T(8,128)S(1)}, f32[32,8,512]{2,1,0:T(8,128)}, u32[]{:S(2)}) %copy-start.1) | copy-done | bytes 524312
  2.2 1.1 %start.1 = (f32[2,8,32,512]{3,2,1,0:T(8,128)S(1)}, f32[8,32,256]{2,1,0:T(8,128)S(1)}, f32[4,32,128]{2,1,0:T(8,128)S(1)}, f32[13,32,128]{2,1,0:T(8,128)S(1)}, f32...) custom-call(s32[2]{0:T(128)S(1)} %pad_add_fusion.place, f32[32,8,512]{2,1,0:T(8,128)S(1)} %copy-done, ...), custom_call_target="tpu_custom_call" | custom-call | flops 1264999936 | bytes 4059000 | tf_op jit(solution)/shard_map/start/pallas_call | solution.py:712
  3.3 1.3 %collective-permute-start.3 = (f32[13,32,128]{2,1,0:T(8,128)S(1)}, f32[13,32,128]{2,1,0:T(8,128)S(1)}, u32[]{:S(2)}, u32[]{:S(2)}) collective-permute-start(f32[13,32,128]{2,1,0:T(8,128)S(1)} %get-tuple-element.53), channel_id=1, source_target_pairs={{0,2},{2,0},{4,6},{6,4},{8,10},{10,8},{12,14},{14,12},{16,18},{18,... | collective-permute-start | bytes 638984 | tf_op jit(solution)/shard_map/ppermute | solution.py:768
  4.6 2.1 %collective-permute-start.4 = (f32[13,32,128]{2,1,0:T(8,128)S(1)}, f32[13,32,128]{2,1,0:T(8,128)S(1)}, u32[]{:S(2)}, u32[]{:S(2)}) collective-permute-start(f32[13,32,128]{2,1,0:T(8,128)S(1)} %get-tuple-element.54), channel_id=1, source_target_pairs={{2,4},{4,2},{6,8},{8,6},{10,12},{12,10},{14,16},{16,14},{18,20},{2... | collective-permute-start | bytes 638984 | tf_op jit(solution)/shard_map/ppermute | solution.py:768
  7.4 1.3 %collective-permute-start.2 = (f32[8,32,128]{2,1,0:T(8,128)S(1)}, f32[8,32,128]{2,1,0:T(8,128)S(1)}, u32[]{:S(2)}, u32[]{:S(2)}) collective-permute-start(f32[8,32,128]{2,1,0:T(8,128)S(1)} %get-tuple-element.52), channel_id=1, source_target_pairs={{0,1},{1,0},{2,3},{3,2},{4,5},{5,4},{6,7},{7,6},{8,9},{9,8},{10,11... | collective-permute-start | bytes 393224 | tf_op jit(solution)/shard_map/ppermute | solution.py:740
  10.2 1.8 %inner.1 = (f32[8,32,128]{2,1,0:T(8,128)S(1)}, f32[4,32,128]{2,1,0:T(8,128)S(1)}, f32[35,32,640]{2,1,0:T(8,128)S(1)}, f32[17,32,384]{2,1,0:T(8,128)S(1)}, f32[5,32,256]{2,1,0:T(8,128)S(1)}) custom-call(s32[2]{0:T(128)S(1)} %pad_add_fusion.place, f32[2,8,32,512]{3,2,1,0:T(8,128)S(1)} %get-tuple-element.46.refs_0_.refs_10_, ...), custom_call_target="tpu_custom_call" | custom-call | flops 575000000 | bytes 1845000 | tf_op jit(solution)/shard_map/inner/pallas_call | solution.py:712
  12.0 2.2 %collective-permute-done.4.refs_8_ = f32[13,32,128]{2,1,0:T(8,128)S(1)} collective-permute-done((f32[13,32,128]{2,1,0:T(8,128)S(1)}, f32[13,32,128]{2,1,0:T(8,128)S(1)}, u32[]{:S(2)}, u32[]{:S(2)}) %collective-permute-start.4) | collective-permute-done | bytes 213024 | tf_op jit(solution)/shard_map/ppermute | solution.py:768
  14.2 1.4 %collective-permute-start.5 = (f32[13,32,128]{2,1,0:T(8,128)S(1)}, f32[13,32,128]{2,1,0:T(8,128)S(1)}, u32[]{:S(2)}, u32[]{:S(2)}) collective-permute-start(f32[13,32,128]{2,1,0:T(8,128)S(1)} %collective-permute-done.3.refs_7_), channel_id=1, source_target_pairs={{0,1},{1,0},{2,3},{3,2},{4,5},{5,4},{6,7},{7,6},{8,9},{9,8},{10,11... | collective-permute-start | bytes 638984 | tf_op jit(solution)/shard_map/ppermute | solution.py:732
  15.6 1.1 %collective-permute-done.5.refs_9_ = f32[13,32,128]{2,1,0:T(8,128)S(1)} collective-permute-done((f32[13,32,128]{2,1,0:T(8,128)S(1)}, f32[13,32,128]{2,1,0:T(8,128)S(1)}, u32[]{:S(2)}, u32[]{:S(2)}) %collective-permute-start.5) | collective-permute-done | bytes 213024 | tf_op jit(solution)/shard_map/ppermute | solution.py:732
  17.1 2.3 %down.1 = (f32[6,32,640]{2,1,0:T(8,128)S(1)}, f32[26,32,384]{2,1,0:T(8,128)S(1)}, f32[24,32,256]{2,1,0:T(8,128)S(1)}, f32[3,32,128]{2,1,0:T(8,128)S(1)}, f32[5,3...) custom-call(s32[2]{0:T(128)S(1)} %pad_add_fusion.place, ...), custom_call_target="tpu_custom_call" | custom-call | flops 2875000064 | bytes 9225000 | tf_op jit(solution)/shard_map/down/pallas_call | solution.py:712
  20.1 1.5 %collective-permute-start.9 = (f32[3,32,128]{2,1,0:T(8,128)S(1)}, f32[3,32,128]{2,1,0:T(8,128)S(1)}, u32[]{:S(2)}, u32[]{:S(2)}) collective-permute-start(f32[3,32,128]{2,1,0:T(8,128)S(1)} %get-tuple-element.70.refs_0_), channel_id=1, source_target_pairs={{0,6},{2,4},{4,2},{6,0},{8,14},{10,12},{12,10},{14,8},{16,22},{18,... | collective-permute-start | bytes 147464 | tf_op jit(solution)/shard_map/ppermute | solution.py:758
  22.1 2.0 %collective-permute-done.9.refs_3_ = f32[3,32,128]{2,1,0:T(8,128)S(1)} collective-permute-done((f32[3,32,128]{2,1,0:T(8,128)S(1)}, f32[3,32,128]{2,1,0:T(8,128)S(1)}, u32[]{:S(2)}, u32[]{:S(2)}) %collective-permute-start.9) | collective-permute-done | bytes 49184 | tf_op jit(solution)/shard_map/ppermute | solution.py:758
  24.0 1.2 %collective-permute-done.7.refs_1_ = f32[3,32,128]{2,1,0:T(8,128)S(1)} collective-permute-done((f32[3,32,128]{2,1,0:T(8,128)S(1)}, f32[3,32,128]{2,1,0:T(8,128)S(1)}, u32[]{:S(2)}, u32[]{:S(2)}) %collective-permute-start.7) | collective-permute-done | bytes 49184 | tf_op jit(solution)/shard_map/ppermute | solution.py:758
  26.4 1.4 %collective-permute-start.12 = (f32[7,32,128]{2,1,0:T(8,128)S(1)}, f32[7,32,128]{2,1,0:T(8,128)S(1)}, u32[]{:S(2)}, u32[]{:S(2)}) collective-permute-start(f32[7,32,128]{2,1,0:T(8,128)S(1)} %merge.1.refs_0_), channel_id=1, source_target_pairs={{0,24},{2,26},{4,28},{6,30},{8,16},{10,18},{12,20},{14,22},{16,8},... | collective-permute-start | bytes 344072 | tf_op jit(solution)/shard_map/ppermute | solution.py:758
  27.8 1.1 %collective-permute-start.11 = (f32[7,32,128]{2,1,0:T(8,128)S(1)}, f32[7,32,128]{2,1,0:T(8,128)S(1)}, u32[]{:S(2)}, u32[]{:S(2)}) collective-permute-start(f32[7,32,128]{2,1,0:T(8,128)S(1)} %merge.1.refs_0_), channel_id=1, source_target_pairs={{0,16},{2,18},{4,20},{6,22},{8,24},{10,26},{12,28},{14,30},{16,0},... | collective-permute-start | bytes 344072 | tf_op jit(solution)/shard_map/ppermute | solution.py:758
  28.9 1.1 %collective-permute-start.10 = (f32[7,32,128]{2,1,0:T(8,128)S(1)}, f32[7,32,128]{2,1,0:T(8,128)S(1)}, u32[]{:S(2)}, u32[]{:S(2)}) collective-permute-start(f32[7,32,128]{2,1,0:T(8,128)S(1)} %merge.1.refs_0_), channel_id=1, source_target_pairs={{0,8},{2,10},{4,12},{6,14},{8,0},{10,2},{12,4},{14,6},{16,24},{18,... | collective-permute-start | bytes 344072 | tf_op jit(solution)/shard_map/ppermute | solution.py:758
  30.0 1.4 %collective-permute-done.18.refs_0_ = f32[14,32,128]{2,1,0:T(8,128)S(1)} collective-permute-done((f32[14,32,128]{2,1,0:T(8,128)S(1)}, f32[14,32,128]{2,1,0:T(8,128)S(1)}, u32[]{:S(2)}, u32[]{:S(2)}) %collective-permute-start.18) | collective-permute-done | bytes 229408 | tf_op jit(solution)/shard_map/ppermute | solution.py:768
  31.3 2.7 %collective-permute-start.19 = (f32[14,32,128]{2,1,0:T(8,128)S(1)}, f32[14,32,128]{2,1,0:T(8,128)S(1)}, u32[]{:S(2)}, u32[]{:S(2)}) collective-permute-start(f32[14,32,128]{2,1,0:T(8,128)S(1)} %get-tuple-element.82), channel_id=1, source_target_pairs={{2,4},{4,2},{6,8},{8,6},{10,12},{12,10},{14,16},{16,14},{18,20},{2... | collective-permute-start | bytes 688136 | tf_op jit(solution)/shard_map/ppermute | solution.py:768
  34.0 2.9 %collective-permute-start.13 = (f32[2,32,128]{2,1,0:T(8,128)S(1)}, f32[2,32,128]{2,1,0:T(8,128)S(1)}, u32[]{:S(2)}, u32[]{:S(2)}) collective-permute-start(f32[2,32,128]{2,1,0:T(8,128)S(1)} %get-tuple-element.74), channel_id=1, source_target_pairs={{4,8},{8,4},{6,10},{10,6},{12,16},{16,12},{14,18},{18,14},{20,24},... | collective-permute-start | bytes 98312 | tf_op jit(solution)/shard_map/ppermute | solution.py:768
  36.9 7.2 %collective-permute-done.13.refs_3_ = f32[2,32,128]{2,1,0:T(8,128)S(1)} collective-permute-done((f32[2,32,128]{2,1,0:T(8,128)S(1)}, f32[2,32,128]{2,1,0:T(8,128)S(1)}, u32[]{:S(2)}, u32[]{:S(2)}) %collective-permute-start.13) | collective-permute-done | bytes 32800 | tf_op jit(solution)/shard_map/ppermute | solution.py:768
  44.1 1.8 %collective-permute-start.14 = (f32[7,32,128]{2,1,0:T(8,128)S(1)}, f32[7,32,128]{2,1,0:T(8,128)S(1)}, u32[]{:S(2)}, u32[]{:S(2)}) collective-permute-start(f32[7,32,128]{2,1,0:T(8,128)S(1)} %merge.1.refs_0_), channel_id=1, source_target_pairs={{0,1},{1,0},{2,3},{3,2},{4,5},{5,4},{6,7},{7,6},{8,9},{9,8},{10,11... | collective-permute-start | bytes 344072 | tf_op jit(solution)/shard_map/ppermute | solution.py:732
  47.8 2.9 %coarse.1 = f32[3,32,128]{2,1,0:T(8,128)S(1)} custom-call(s32[2]{0:T(128)S(1)} %pad_add_fusion.place, f32[7,32,128]{2,1,0:T(8,128)S(1)} %merge.1.refs_0_, f32[7,32,128]{2,1,0:T(8,128)S(1)} %collective-permute-done.10.refs_1_, f32[7,32,128]{2,1,0:T(8,128)S(1)} %collective-permute-done.11.refs_2_, f32[7,32,128]{2,1,0:T(8,128)S(1)} %collective-permute-done.12.refs_3_, ...), custom_call_target="tpu_custom_call" | custom-call | flops 805000000 | bytes 2583000 | tf_op jit(solution)/shard_map/coarse/pallas_call | solution.py:712
  50.6 3.1 %up.1 = f32[32,8,512]{2,1,0:T(8,128)} custom-call(s32[2]{0:T(128)S(1)} %pad_add_fusion.place, f32[3,32,128]{2,1,0:T(8,128)S(1)} %coarse.1, f32[14,32,128]{2,1,0:T(8,128)S(1)} %collective-permute-done.18.refs_0_, f32[14,32,128]{2,1,0:T(8,128)S(1)} %collective-permute-done.19.refs_1_, f32[5,32,128]{2,1,0:T(8,128)S(1)} %collective-permute-done.8.refs_2_, ...), custom_call_target="tpu_custom_call" | custom-call | flops 3449999872 | bytes 11070000 | tf_op jit(solution)/shard_map/up/pallas_call | solution.py:712
  (30 shorter events, 6.8 us)
Async XLA Ops:
  0.1 1.0 %copy-start = (f32[32,8,512]{2,1,0:T(8,128)S(1)}, f32[32,8,512]{2,1,0:T(8,128)}, u32[]{:S(2)}) copy-start(f32[32,8,512]{2,1,0:T(8,128)} %conduct.1) | copy-start | bytes 1572868
  1.1 1.0 %copy-start.1 = (f32[32,8,512]{2,1,0:T(8,128)S(1)}, f32[32,8,512]{2,1,0:T(8,128)}, u32[]{:S(2)}) copy-start(f32[32,8,512]{2,1,0:T(8,128)} %binding.1) | copy-start | bytes 1572868
  2.2 4.5 %copy-start.2 = (f32[32,8,512]{2,1,0:T(8,128)S(1)}, f32[32,8,512]{2,1,0:T(8,128)}, u32[]{:S(2)}) copy-start(f32[32,8,512]{2,1,0:T(8,128)} %right_side.1) | copy-start | bytes 1572868
  3.3 8.7 %collective-permute-start.3 = (f32[13,32,128]{2,1,0:T(8,128)S(1)}, f32[13,32,128]{2,1,0:T(8,128)S(1)}, u32[]{:S(2)}, u32[]{:S(2)}) collective-permute-start(f32[13,32,128]{2,1,0:T(8,128)S(1)} %get-tuple-element.53), channel_id=1, source_target_pairs={{0,2},{2,0},{4,6},{6,4},{8,10},{10,8},{12,14},{14,12},{16,18},{18,... | collective-permute-start | bytes 638984 | tf_op jit(solution)/shard_map/ppermute | solution.py:768
  4.6 9.6 %collective-permute-start.4 = (f32[13,32,128]{2,1,0:T(8,128)S(1)}, f32[13,32,128]{2,1,0:T(8,128)S(1)}, u32[]{:S(2)}, u32[]{:S(2)}) collective-permute-start(f32[13,32,128]{2,1,0:T(8,128)S(1)} %get-tuple-element.54), channel_id=1, source_target_pairs={{2,4},{4,2},{6,8},{8,6},{10,12},{12,10},{14,16},{16,14},{18,20},{2... | collective-permute-start | bytes 638984 | tf_op jit(solution)/shard_map/ppermute | solution.py:768
  7.4 2.3 %collective-permute-start.2 = (f32[8,32,128]{2,1,0:T(8,128)S(1)}, f32[8,32,128]{2,1,0:T(8,128)S(1)}, u32[]{:S(2)}, u32[]{:S(2)}) collective-permute-start(f32[8,32,128]{2,1,0:T(8,128)S(1)} %get-tuple-element.52), channel_id=1, source_target_pairs={{0,1},{1,0},{2,3},{3,2},{4,5},{5,4},{6,7},{7,6},{8,9},{9,8},{10,11... | collective-permute-start | bytes 393224 | tf_op jit(solution)/shard_map/ppermute | solution.py:740
  8.7 1.3 %collective-permute-start = (f32[8,32,128]{2,1,0:T(8,128)S(1)}, f32[8,32,128]{2,1,0:T(8,128)S(1)}, u32[]{:S(2)}, u32[]{:S(2)}) collective-permute-start(f32[8,32,128]{2,1,0:T(8,128)S(1)} %get-tuple-element.50), channel_id=1, source_target_pairs={{0,1},{1,0},{2,3},{3,2},{4,5},{5,4},{6,7},{7,6},{8,9},{9,8},{10,11... | collective-permute-start | bytes 393224 | tf_op jit(solution)/shard_map/ppermute | solution.py:740
  8.8 1.5 %collective-permute-start.1 = (f32[8,32,128]{2,1,0:T(8,128)S(1)}, f32[8,32,128]{2,1,0:T(8,128)S(1)}, u32[]{:S(2)}, u32[]{:S(2)}) collective-permute-start(f32[8,32,128]{2,1,0:T(8,128)S(1)} %get-tuple-element.51), channel_id=1, source_target_pairs={{0,1},{1,0},{2,3},{3,2},{4,5},{5,4},{6,7},{7,6},{8,9},{9,8},{10,11... | collective-permute-start | bytes 393224 | tf_op jit(solution)/shard_map/ppermute | solution.py:740
  14.2 2.5 %collective-permute-start.5 = (f32[13,32,128]{2,1,0:T(8,128)S(1)}, f32[13,32,128]{2,1,0:T(8,128)S(1)}, u32[]{:S(2)}, u32[]{:S(2)}) collective-permute-start(f32[13,32,128]{2,1,0:T(8,128)S(1)} %collective-permute-done.3.refs_7_), channel_id=1, source_target_pairs={{0,1},{1,0},{2,3},{3,2},{4,5},{5,4},{6,7},{7,6},{8,9},{9,8},{10,11... | collective-permute-start | bytes 638984 | tf_op jit(solution)/shard_map/ppermute | solution.py:732
  15.6 1.5 %collective-permute-start.6 = (f32[13,32,128]{2,1,0:T(8,128)S(1)}, f32[13,32,128]{2,1,0:T(8,128)S(1)}, u32[]{:S(2)}, u32[]{:S(2)}) collective-permute-start(f32[13,32,128]{2,1,0:T(8,128)S(1)} %collective-permute-done.4.refs_8_), channel_id=1, source_target_pairs={{0,1},{1,0},{2,3},{3,2},{4,5},{5,4},{6,7},{7,6},{8,9},{9,8},{10,11... | collective-permute-start | bytes 638984 | tf_op jit(solution)/shard_map/ppermute | solution.py:732
  19.4 5.9 %collective-permute-start.8 = (f32[5,32,128]{2,1,0:T(8,128)S(1)}, f32[5,32,128]{2,1,0:T(8,128)S(1)}, u32[]{:S(2)}, u32[]{:S(2)}) collective-permute-start(f32[5,32,128]{2,1,0:T(8,128)S(1)} %get-tuple-element.68), channel_id=1, source_target_pairs={{0,4},{2,6},{4,0},{6,2},{8,12},{10,14},{12,8},{14,10},{16,20},{18,... | collective-permute-start | bytes 245768 | tf_op jit(solution)/shard_map/ppermute | solution.py:758
  20.1 3.9 %collective-permute-start.9 = (f32[3,32,128]{2,1,0:T(8,128)S(1)}, f32[3,32,128]{2,1,0:T(8,128)S(1)}, u32[]{:S(2)}, u32[]{:S(2)}) collective-permute-start(f32[3,32,128]{2,1,0:T(8,128)S(1)} %get-tuple-element.70.refs_0_), channel_id=1, source_target_pairs={{0,6},{2,4},{4,2},{6,0},{8,14},{10,12},{12,10},{14,8},{16,22},{18,... | collective-permute-start | bytes 147464 | tf_op jit(solution)/shard_map/ppermute | solution.py:758
  21.6 3.7 %collective-permute-start.7 = (f32[3,32,128]{2,1,0:T(8,128)S(1)}, f32[3,32,128]{2,1,0:T(8,128)S(1)}, u32[]{:S(2)}, u32[]{:S(2)}) collective-permute-start(f32[3,32,128]{2,1,0:T(8,128)S(1)} %get-tuple-element.70.refs_0_), channel_id=1, source_target_pairs={{0,2},{2,0},{4,6},{6,4},{8,10},{10,8},{12,14},{14,12},{16,18},{18,... | collective-permute-start | bytes 147464 | tf_op jit(solution)/shard_map/ppermute | solution.py:758
  25.3 6.1 %collective-permute-start.18 = (f32[14,32,128]{2,1,0:T(8,128)S(1)}, f32[14,32,128]{2,1,0:T(8,128)S(1)}, u32[]{:S(2)}, u32[]{:S(2)}) collective-permute-start(f32[14,32,128]{2,1,0:T(8,128)S(1)} %get-tuple-element.79), channel_id=1, source_target_pairs={{0,2},{2,0},{4,6},{6,4},{8,10},{10,8},{12,14},{14,12},{16,18},{18,... | collective-permute-start | bytes 688136 | tf_op jit(solution)/shard_map/ppermute | solution.py:768
  26.4 17.7 %collective-permute-start.12 = (f32[7,32,128]{2,1,0:T(8,128)S(1)}, f32[7,32,128]{2,1,0:T(8,128)S(1)}, u32[]{:S(2)}, u32[]{:S(2)}) collective-permute-start(f32[7,32,128]{2,1,0:T(8,128)S(1)} %merge.1.refs_0_), channel_id=1, source_target_pairs={{0,24},{2,26},{4,28},{6,30},{8,16},{10,18},{12,20},{14,22},{16,8},... | collective-permute-start | bytes 344072 | tf_op jit(solution)/shard_map/ppermute | solution.py:758
  27.8 16.4 %collective-permute-start.11 = (f32[7,32,128]{2,1,0:T(8,128)S(1)}, f32[7,32,128]{2,1,0:T(8,128)S(1)}, u32[]{:S(2)}, u32[]{:S(2)}) collective-permute-start(f32[7,32,128]{2,1,0:T(8,128)S(1)} %merge.1.refs_0_), channel_id=1, source_target_pairs={{0,16},{2,18},{4,20},{6,22},{8,24},{10,26},{12,28},{14,30},{16,0},... | collective-permute-start | bytes 344072 | tf_op jit(solution)/shard_map/ppermute | solution.py:758
  28.9 15.3 %collective-permute-start.10 = (f32[7,32,128]{2,1,0:T(8,128)S(1)}, f32[7,32,128]{2,1,0:T(8,128)S(1)}, u32[]{:S(2)}, u32[]{:S(2)}) collective-permute-start(f32[7,32,128]{2,1,0:T(8,128)S(1)} %merge.1.refs_0_), channel_id=1, source_target_pairs={{0,8},{2,10},{4,12},{6,14},{8,0},{10,2},{12,4},{14,6},{16,24},{18,... | collective-permute-start | bytes 344072 | tf_op jit(solution)/shard_map/ppermute | solution.py:758
  31.3 19.3 %collective-permute-start.19 = (f32[14,32,128]{2,1,0:T(8,128)S(1)}, f32[14,32,128]{2,1,0:T(8,128)S(1)}, u32[]{:S(2)}, u32[]{:S(2)}) collective-permute-start(f32[14,32,128]{2,1,0:T(8,128)S(1)} %get-tuple-element.82), channel_id=1, source_target_pairs={{2,4},{4,2},{6,8},{8,6},{10,12},{12,10},{14,16},{16,14},{18,20},{2... | collective-permute-start | bytes 688136 | tf_op jit(solution)/shard_map/ppermute | solution.py:768
  34.0 10.1 %collective-permute-start.13 = (f32[2,32,128]{2,1,0:T(8,128)S(1)}, f32[2,32,128]{2,1,0:T(8,128)S(1)}, u32[]{:S(2)}, u32[]{:S(2)}) collective-permute-start(f32[2,32,128]{2,1,0:T(8,128)S(1)} %get-tuple-element.74), channel_id=1, source_target_pairs={{4,8},{8,4},{6,10},{10,6},{12,16},{16,12},{14,18},{18,14},{20,24},... | collective-permute-start | bytes 98312 | tf_op jit(solution)/shard_map/ppermute | solution.py:768
  44.1 2.7 %collective-permute-start.14 = (f32[7,32,128]{2,1,0:T(8,128)S(1)}, f32[7,32,128]{2,1,0:T(8,128)S(1)}, u32[]{:S(2)}, u32[]{:S(2)}) collective-permute-start(f32[7,32,128]{2,1,0:T(8,128)S(1)} %merge.1.refs_0_), channel_id=1, source_target_pairs={{0,1},{1,0},{2,3},{3,2},{4,5},{5,4},{6,7},{7,6},{8,9},{9,8},{10,11... | collective-permute-start | bytes 344072 | tf_op jit(solution)/shard_map/ppermute | solution.py:732
  45.9 1.3 %collective-permute-start.15 = (f32[7,32,128]{2,1,0:T(8,128)S(1)}, f32[7,32,128]{2,1,0:T(8,128)S(1)}, u32[]{:S(2)}, u32[]{:S(2)}) collective-permute-start(f32[7,32,128]{2,1,0:T(8,128)S(1)} %collective-permute-done.10.refs_1_), channel_id=1, source_target_pairs={{0,1},{1,0},{2,3},{3,2},{4,5},{5,4},{6,7},{7,6},{8,9},{9,8},{10,11... | collective-permute-start | bytes 344072 | tf_op jit(solution)/shard_map/ppermute | solution.py:732
  46.0 1.4 %collective-permute-start.16 = (f32[7,32,128]{2,1,0:T(8,128)S(1)}, f32[7,32,128]{2,1,0:T(8,128)S(1)}, u32[]{:S(2)}, u32[]{:S(2)}) collective-permute-start(f32[7,32,128]{2,1,0:T(8,128)S(1)} %collective-permute-done.11.refs_2_), channel_id=1, source_target_pairs={{0,1},{1,0},{2,3},{3,2},{4,5},{5,4},{6,7},{7,6},{8,9},{9,8},{10,11... | collective-permute-start | bytes 344072 | tf_op jit(solution)/shard_map/ppermute | solution.py:732
  46.4 1.3 %collective-permute-start.17 = (f32[7,32,128]{2,1,0:T(8,128)S(1)}, f32[7,32,128]{2,1,0:T(8,128)S(1)}, u32[]{:S(2)}, u32[]{:S(2)}) collective-permute-start(f32[7,32,128]{2,1,0:T(8,128)S(1)} %collective-permute-done.12.refs_3_), channel_id=1, source_target_pairs={{0,1},{1,0},{2,3},{3,2},{4,5},{5,4},{6,7},{7,6},{8,9},{9,8},{10,11... | collective-permute-start | bytes 344072 | tf_op jit(solution)/shard_map/ppermute | solution.py:732

commit v15 on v14

--- a/solution.py
+++ b/solution.py
@@ -35,6 +35,12 @@
             self.slots.append((start, self.own[level]))
             start += self.own[level]
         self.tiles = start
+        self.up_slots = []
+        start = 0
+        for level in (0, 1, 1, 2, 2, 2):
+            self.up_slots.append((start, self.own[level]))
+            start += self.own[level]
+        self.up_tiles = start
 
 
 def put(message, slot, row):
@@ -325,21 +331,24 @@
 def fringes(sizes, rows):
     total = None
     for index, (level, row) in enumerate(rows):
-        tile = row[:, sizes.own[level] * LANES :]
-        tile = jnp.where(fringe_lanes(tile.shape), tile, 0.0)
+        border = row[:, sizes.own[level] * LANES :]
+        tile = border[:, :LANES]
+        lane = lane_at(tile.shape)
+        if border.shape[1] > LANES:
+            tile = jnp.where(lane < FRINGE, tile, border[:, LANES:])
+        tile = jnp.where((lane < FRINGE) | (lane >= LANES - FRINGE), tile, 0.0)
         tile = roll(tile, SPREAD * index + SPREAD // 2, 1)
         total = tile if total is None else total + tile
     return total
 
 
 def fringed_row(sizes, level, index, message):
-    row = get(message, sizes.slots[index])
+    row = get(message, sizes.up_slots[index])
     if sizes.border[level]:
-        if level == 0:
-            row += [jnp.zeros(row[0].shape, f32)] * sizes.border[0]
-        else:
-            tile = roll(message[sizes.tiles], -(SPREAD * (index - 1) + SPREAD // 2), 1)
-            row.append(jnp.where(fringe_lanes(tile.shape), tile, 0.0))
+        tile = roll(message[sizes.up_tiles], -(SPREAD * index + SPREAD // 2), 1)
+        lane = lane_at(tile.shape)
+        right, left = jnp.where(lane < FRINGE, tile, 0.0), jnp.where(lane >= LANES - FRINGE, tile, 0.0)
+        row += [right, left] if sizes.border[level] == 2 else [right + left]
     return jnp.concatenate(row, axis=1)
 
 
@@ -537,13 +546,13 @@
     with_far[0:tiles] = contribution[...]
     v0, s1, v1 = levels[0].smooth, levels[1].source, levels[1].smooth
     s2, v2 = levels[2].source, levels[2].smooth
-    next_rows = (v0[n0 - 1], s1[n1], s1[n1 + 1], v1[n1 - 1], s2[n2], s2[n2 + 1], v2[n2 - 1])
-    prev_rows = (v0[0], s1[1], s1[0], v1[2], s2[1], s2[0], v2[2])
-    for slot, next_row, prev_row in zip(slots, next_rows, prev_rows):
+    next_rows = (v0[n0 - 1], s1[n1], v1[n1 - 1], s2[n2], s2[n2 + 1], v2[n2 - 1])
+    prev_rows = (v0[0], s1[1], v1[2], s2[1], s2[0], v2[2])
+    for slot, next_row, prev_row in zip(sizes.up_slots, next_rows, prev_rows):
         put_pair(place, ups, slot, next_row, prev_row)
     if s:
-        ends = [fringes(sizes, list(zip((1, 1, 1, 2, 2, 2), rows[1:]))) for rows in (next_rows, prev_rows)]
-        put_pair(place, ups, (sizes.tiles, 1), *ends)
+        ends = [fringes(sizes, list(zip((0, 1, 1, 2, 2, 2), rows))) for rows in (next_rows, prev_rows)]
+        put_pair(place, ups, (sizes.up_tiles, 1), *ends)
     far_tiles = sizes.held[2] // LANES
     put_pair(place, (with_far.at[tiles : tiles + far_tiles], far), (0, far_tiles), v2[n2 + 1], v2[0], 2)
 
@@ -642,34 +651,39 @@
     far_pair = (far_pair[0].at[tiles : tiles + sizes.held[2] // LANES], far_pair[1])
     fars = [Arrived(place, far_pair, forward, 2) for forward in (0, 1)]
     borders0, out, refs = refs[12 : 12 + 3 * s], refs[12 + 3 * s], refs[13 + 3 * s :]
-    total1, total2, result = refs[:3]
-    over2, over1, over0, lift2, lift1, lift0, it2, it1, it0, semaphores = refs[3:]
+    total1, total2, result, edges0, edges1 = refs[:5]
+    over2, over1, over0, lift2, lift1, lift0, it2, it1, it0, semaphores = refs[5:]
     slots = sizes.slots
     n0, n1, n2 = sizes.rows[:3]
     width = sizes.own[0] * LANES
 
+    before, behind = fringed_row(sizes, 0, 0, from_prev), fringed_row(sizes, 0, 0, from_next)
+    lift0[0], lift0[n0 + 1] = before, behind
+    edges0[0], edges0[1] = levels[0].fx[0] * before, levels[0].fx[n0] * behind
+    narrow(sizes, place, 0, edges0, edges1, 2)
+
     widen(sizes, place, 2, coarse, over2, 3)
     for level, first, totals, over, lift, target, upper in (
-        (2, 4, total2, over2, lift2, it2, over1),
+        (2, 3, total2, over2, lift2, it2, over1),
         (1, 1, total1, over1, lift1, it1, over0),
     ):
         n, kept = sizes.rows[level], levels[level]
         fx, fy, fz, weight, binding = kept.fx, kept.fy, kept.fz, kept.weight, kept.binding
         own, smooth = kept.source, kept.smooth
-        edge = {}
-        for row, message, index in (
-            (1, from_prev, first),
-            (2, from_prev, first + 1),
-            (n + 2, from_next, first),
-            (n + 1, from_next, first + 1),
-        ):
-            value = edge.get(row, own[row - 1])
-            edge[row] = value + fringed_row(sizes, level, index, message)
+        fringed = lambda index, message, level=level: fringed_row(sizes, level, index, message)
+        if level == 1:
+            smooth_at = first + 1
+            edge = {2: own[1] + edges1[0], n + 1: own[n] + edges1[1]}
+        else:
+            smooth_at = first + 2
+            edge = {2: own[1] + fringed(first + 1, from_prev)}
+            edge[n + 1] = own[n] + fringed(first + 1, from_next)
+        edge[1], edge[n + 2] = own[0] + fringed(first, from_prev), own[n + 1] + fringed(first, from_next)
         for row, value in edge.items():
             totals[row - 1] = value
         for row in range(n + 4):
             if row in (0, n + 3):
-                value = fringed_row(sizes, level, first + 2, from_next if row else from_prev)
+                value = fringed(smooth_at, from_next if row else from_prev)
                 if level == 2:
                     far = fars[1 if row else 0]
                     value = value + jnp.concatenate(get(far, (0, sizes.held[2] // LANES)), axis=1)
@@ -686,8 +700,8 @@
 
     held_row = held_rows(sizes, [owns[0], None, None, owns[1]], [borders0])
     fx, fy, fz, weight, v0 = levels[0].fx, levels[0].fy, levels[0].fz, levels[0].weight, levels[0].smooth
-    lift0[0] = fringed_row(sizes, 0, 0, from_prev) + over0[0]
-    lift0[n0 + 1] = fringed_row(sizes, 0, 0, from_next) + over0[n1 + 1]
+    lift0[0] = lift0[0] + over0[0]
+    lift0[n0 + 1] = lift0[n0 + 1] + over0[n1 + 1]
     for row in range(1, n0 + 1):
         lift0[row] = v0[row - 1] + over0[(row + 1) // 2]
     field = lambda row: lift0[row]
@@ -778,7 +792,7 @@
     own = [(depth, count * LANES) for count in sizes.own]
     held = [(depth, count) for count in sizes.held]
     down_message = (sizes.tiles, *tile)
-    up_message = (sizes.tiles + 1, *tile)
+    up_message = (sizes.up_tiles + 1, *tile)
     own0, own1, own2, first, second, *edges = call(
         functools.partial(start_kernel, sizes),
         "start",
@@ -834,7 +848,6 @@
         if far_rows is None:
             blocks = swap(blocks, stride, radix, {2: with_far})
             far_rows = [blocks[2], exchange([None, far_second], 2)[1]]
-            blocks, ups[0] = lax.optimization_barrier((blocks, ups[0]))
         else:
             blocks = swap(blocks, stride, radix)
         (blocks,) = call(
@@ -865,7 +878,7 @@
         place,
         [*blocks, *sum(beside(blocks, sizes), [])],
     )
-    scratch = [(n1 + 2, *held[1]), (n2 + 2, *held[2]), diffusivity.shape]
+    scratch = [(n1 + 2, *held[1]), (n2 + 2, *held[2]), diffusivity.shape, (2, *held[0]), (2, *held[1])]
     scratch += [(n3 + 2, *held[2]), (n2 + 2, *held[1]), (n1 + 2, *held[0])]
     scratch += [(n2 + 4, *held[2]), (n1 + 4, *held[1]), (n0 + 2, *held[0])]
     scratch += [(n2 + 2, *held[2]), (n1 + 2, *held[1]), (n0, *held[0])]

time: 54 us -> 50.6 us (0.937)
  the two profiles are of different devices: /device:TPU:13 before, /device:TPU:0 now
where the time goes in v15:
time: 50.6 us; the launch traced here: 50.4 us
  starting transfers between devices  18.6 us (37%)
  waiting for transfers between devices  16.9 us (33%)
  Pallas kernels  12.6 us (25%)
  local copies, waits for them, and re-layouts  2.09 us (4%)
    pallas_call x7, Pallas kernels, call(): pl.pallas_call(body, name=name, out_shape=[jax.ShapeDtypeStruct(shape, f3...  12.6 us
    ppermute x6, waiting for transfers between devices, swap(): lax.ppermute(others.get(step, value), 'span', [(device, device ^ step * s...  9.39 us
    ppermute x6, starting transfers between devices, swap(): lax.ppermute(others.get(step, value), 'span', [(device, device ^ step * s...  9.38 us
    ppermute x5, starting transfers between devices, exchange(): lax.ppermute(value, 'span', route)  7.01 us
    ppermute x5, waiting for transfers between devices, exchange(): lax.ppermute(value, 'span', route)  4.02 us
    ppermute x6, waiting for transfers between devices, beside(): lax.ppermute(value, 'width', [(0, 1), (1, 0)])  2.23 us
    unnamed x6, local copies, waits for them, and re-layouts  2.09 us
    ppermute x6, starting transfers between devices, beside(): lax.ppermute(value, 'width', [(0, 1), (1, 0)])  1.53 us
  transfers between devices with their start and end apart: 20, of which 14 were waited for; matrix products, arithmetic and copies ran while one was open for 0% of the time, Pallas kernels for 12%

profile of v15, /device:TPU:0, one launch (start us, length us, event | category | flops | bytes accessed | tf_op | source)
XLA Modules:
  0.0 50.4 jit_solution(1404393205725471356)
XLA Ops:
  0.1 1.0 %copy-done = f32[32,8,512]{2,1,0:T(8,128)S(1)} copy-done((f32[32,8,512]{2,1,0:T(8,128)S(1)}, f32[32,8,512]{2,1,0:T(8,128)}, u32[]{:S(2)}) %copy-start) | copy-done | bytes 524312
  1.1 1.0 %copy-done.1 = f32[32,8,512]{2,1,0:T(8,128)S(1)} copy-done((f32[32,8,512]{2,1,0:T(8,128)S(1)}, f32[32,8,512]{2,1,0:T(8,128)}, u32[]{:S(2)}) %copy-start.1) | copy-done | bytes 524312
  2.2 1.1 %start.1 = (f32[2,8,32,512]{3,2,1,0:T(8,128)S(1)}, f32[8,32,256]{2,1,0:T(8,128)S(1)}, f32[4,32,128]{2,1,0:T(8,128)S(1)}, f32[13,32,128]{2,1,0:T(8,128)S(1)}, f32...) custom-call(s32[2]{0:T(128)S(1)} %pad_add_fusion.place, f32[32,8,512]{2,1,0:T(8,128)S(1)} %copy-done, ...), custom_call_target="tpu_custom_call" | custom-call | flops 1264999936 | bytes 4059000 | tf_op jit(solution)/shard_map/start/pallas_call | solution.py:726
  3.3 3.0 %collective-permute-start.3 = (f32[13,32,128]{2,1,0:T(8,128)S(1)}, f32[13,32,128]{2,1,0:T(8,128)S(1)}, u32[]{:S(2)}, u32[]{:S(2)}) collective-permute-start(f32[13,32,128]{2,1,0:T(8,128)S(1)} %get-tuple-element.48), channel_id=1, source_target_pairs={{0,2},{2,0},{4,6},{6,4},{8,10},{10,8},{12,14},{14,12},{16,18},{18,... | collective-permute-start | bytes 638984 | tf_op jit(solution)/shard_map/ppermute | solution.py:782
  6.3 0.7 %collective-permute-start.4 = (f32[13,32,128]{2,1,0:T(8,128)S(1)}, f32[13,32,128]{2,1,0:T(8,128)S(1)}, u32[]{:S(2)}, u32[]{:S(2)}) collective-permute-start(f32[13,32,128]{2,1,0:T(8,128)S(1)} %get-tuple-element.49), channel_id=1, source_target_pairs={{2,4},{4,2},{6,8},{8,6},{10,12},{12,10},{14,16},{16,14},{18,20},{2... | collective-permute-start | bytes 638984 | tf_op jit(solution)/shard_map/ppermute | solution.py:782
  7.0 0.7 %turn.1 = (f32[8,32,512]{2,1,0:T(8,128)S(1)}, f32[8,32,128]{2,1,0:T(8,128)S(1)}) custom-call(s32[2]{0:T(128)S(1)} %pad_add_fusion.place, f32[32,8,512]{2,1,0:T(8,128)S(1)} %copy-done.2), custom_call_target="tpu_custom_call" | custom-call | flops 805000000 | bytes 2583000 | tf_op jit(solution)/shard_map/turn/pallas_call | solution.py:726
  8.3 0.8 %collective-permute-done.2.refs_6_.refs_14_ = f32[8,32,128]{2,1,0:T(8,128)S(1)} collective-permute-done((f32[8,32,128]{2,1,0:T(8,128)S(1)}, f32[8,32,128]{2,1,0:T(8,128)S(1)}, u32[]{:S(2)}, u32[]{:S(2)}) %collective-permute-start.2) | collective-permute-done | bytes 131104 | tf_op jit(solution)/shard_map/ppermute | solution.py:754
  9.6 1.8 %inner.1 = (f32[8,32,128]{2,1,0:T(8,128)S(1)}, f32[4,32,128]{2,1,0:T(8,128)S(1)}, f32[35,32,640]{2,1,0:T(8,128)S(1)}, f32[17,32,384]{2,1,0:T(8,128)S(1)}, f32[5,32,256]{2,1,0:T(8,128)S(1)}) custom-call(s32[2]{0:T(128)S(1)} %pad_add_fusion.place, f32[2,8,32,512]{3,2,1,0:T(8,128)S(1)} %get-tuple-element.41.refs_0_.refs_10_, ...), custom_call_target="tpu_custom_call" | custom-call | flops 575000000 | bytes 1845000 | tf_op jit(solution)/shard_map/inner/pallas_call | solution.py:726
  11.4 4.0 %collective-permute-done.3.refs_7_ = f32[13,32,128]{2,1,0:T(8,128)S(1)} collective-permute-done((f32[13,32,128]{2,1,0:T(8,128)S(1)}, f32[13,32,128]{2,1,0:T(8,128)S(1)}, u32[]{:S(2)}, u32[]{:S(2)}) %collective-permute-start.3) | collective-permute-done | bytes 213024 | tf_op jit(solution)/shard_map/ppermute | solution.py:782
  15.9 1.0 %collective-permute-done.5.refs_9_ = f32[13,32,128]{2,1,0:T(8,128)S(1)} collective-permute-done((f32[13,32,128]{2,1,0:T(8,128)S(1)}, f32[13,32,128]{2,1,0:T(8,128)S(1)}, u32[]{:S(2)}, u32[]{:S(2)}) %collective-permute-start.5) | collective-permute-done | bytes 213024 | tf_op jit(solution)/shard_map/ppermute | solution.py:746
  17.2 2.3 %down.1 = (f32[6,32,640]{2,1,0:T(8,128)S(1)}, f32[26,32,384]{2,1,0:T(8,128)S(1)}, f32[24,32,256]{2,1,0:T(8,128)S(1)}, f32[3,32,128]{2,1,0:T(8,128)S(1)}, f32[5,3...) custom-call(s32[2]{0:T(128)S(1)} %pad_add_fusion.place, ...), custom_call_target="tpu_custom_call" | custom-call | flops 2875000064 | bytes 9225000 | tf_op jit(solution)/shard_map/down/pallas_call | solution.py:726
  19.5 2.2 %collective-permute-start.8 = (f32[5,32,128]{2,1,0:T(8,128)S(1)}, f32[5,32,128]{2,1,0:T(8,128)S(1)}, u32[]{:S(2)}, u32[]{:S(2)}) collective-permute-start(f32[5,32,128]{2,1,0:T(8,128)S(1)} %get-tuple-element.63), channel_id=1, source_target_pairs={{0,4},{2,6},{4,0},{6,2},{8,12},{10,14},{12,8},{14,10},{16,20},{18,... | collective-permute-start | bytes 245768 | tf_op jit(solution)/shard_map/ppermute | solution.py:772
  21.7 2.7 %collective-permute-start.9 = (f32[3,32,128]{2,1,0:T(8,128)S(1)}, f32[3,32,128]{2,1,0:T(8,128)S(1)}, u32[]{:S(2)}, u32[]{:S(2)}) collective-permute-start(f32[3,32,128]{2,1,0:T(8,128)S(1)} %get-tuple-element.62.refs_0_), channel_id=1, source_target_pairs={{0,6},{2,4},{4,2},{6,0},{8,14},{10,12},{12,10},{14,8},{16,22},{18,... | collective-permute-start | bytes 147464 | tf_op jit(solution)/shard_map/ppermute | solution.py:772
  24.4 2.0 %collective-permute-start.18 = (f32[12,32,128]{2,1,0:T(8,128)S(1)}, f32[12,32,128]{2,1,0:T(8,128)S(1)}, u32[]{:S(2)}, u32[]{:S(2)}) collective-permute-start(f32[12,32,128]{2,1,0:T(8,128)S(1)} %get-tuple-element.69), channel_id=1, source_target_pairs={{0,2},{2,0},{4,6},{6,4},{8,10},{10,8},{12,14},{14,12},{16,18},{18,... | collective-permute-start | bytes 589832 | tf_op jit(solution)/shard_map/ppermute | solution.py:782
  27.0 2.1 %collective-permute-done.7.refs_1_ = f32[3,32,128]{2,1,0:T(8,128)S(1)} collective-permute-done((f32[3,32,128]{2,1,0:T(8,128)S(1)}, f32[3,32,128]{2,1,0:T(8,128)S(1)}, u32[]{:S(2)}, u32[]{:S(2)}) %collective-permute-start.7) | collective-permute-done | bytes 49184 | tf_op jit(solution)/shard_map/ppermute | solution.py:772
  29.1 0.7 %merge.1.refs_0_ = f32[7,32,128]{2,1,0:T(8,128)S(1)} custom-call(s32[2]{0:T(128)S(1)} %pad_add_fusion.place, f32[3,32,128]{2,1,0:T(8,128)S(1)} %get-tuple-element.62.refs_0_, f32[3,32,128]{2,1,0:T(8,128)S(1)} %collective-permute-done.7.refs_1_, f32[5,32,128]{2,1,0:T(8,128)S(1)} %collective-permute-done.8.refs_2_, ...), custom_call_target="tpu_custom_call" | custom-call | flops 1035000000 | bytes 3321000 | tf_op jit(solution)/shard_map/merge/pallas_call | solution.py:726
  29.8 3.7 %collective-permute-start.12 = (f32[7,32,128]{2,1,0:T(8,128)S(1)}, f32[7,32,128]{2,1,0:T(8,128)S(1)}, u32[]{:S(2)}, u32[]{:S(2)}) collective-permute-start(f32[7,32,128]{2,1,0:T(8,128)S(1)} %merge.1.refs_0_), channel_id=1, source_target_pairs={{0,24},{2,26},{4,28},{6,30},{8,16},{10,18},{12,20},{14,22},{16,8},... | collective-permute-start | bytes 344072 | tf_op jit(solution)/shard_map/ppermute | solution.py:772
  33.5 0.8 %collective-permute-start.10 = (f32[7,32,128]{2,1,0:T(8,128)S(1)}, f32[7,32,128]{2,1,0:T(8,128)S(1)}, u32[]{:S(2)}, u32[]{:S(2)}) collective-permute-start(f32[7,32,128]{2,1,0:T(8,128)S(1)} %merge.1.refs_0_), channel_id=1, source_target_pairs={{0,8},{2,10},{4,12},{6,14},{8,0},{10,2},{12,4},{14,6},{16,24},{18,... | collective-permute-start | bytes 344072 | tf_op jit(solution)/shard_map/ppermute | solution.py:772
  34.3 0.7 %collective-permute-start.13 = (f32[2,32,128]{2,1,0:T(8,128)S(1)}, f32[2,32,128]{2,1,0:T(8,128)S(1)}, u32[]{:S(2)}, u32[]{:S(2)}) collective-permute-start(f32[2,32,128]{2,1,0:T(8,128)S(1)} %get-tuple-element.64), channel_id=1, source_target_pairs={{4,8},{8,4},{6,10},{10,6},{12,16},{16,12},{14,18},{18,14},{20,24},... | collective-permute-start | bytes 98312 | tf_op jit(solution)/shard_map/ppermute | solution.py:782
  34.9 0.7 %collective-permute-start.19 = (f32[12,32,128]{2,1,0:T(8,128)S(1)}, f32[12,32,128]{2,1,0:T(8,128)S(1)}, u32[]{:S(2)}, u32[]{:S(2)}) collective-permute-start(f32[12,32,128]{2,1,0:T(8,128)S(1)} %get-tuple-element.72), channel_id=1, source_target_pairs={{2,4},{4,2},{6,8},{8,6},{10,12},{12,10},{14,16},{16,14},{18,20},{2... | collective-permute-start | bytes 589832 | tf_op jit(solution)/shard_map/ppermute | solution.py:782
  35.6 1.2 %collective-permute-done.12.refs_3_ = f32[7,32,128]{2,1,0:T(8,128)S(1)} collective-permute-done((f32[7,32,128]{2,1,0:T(8,128)S(1)}, f32[7,32,128]{2,1,0:T(8,128)S(1)}, u32[]{:S(2)}, u32[]{:S(2)}) %collective-permute-start.12) | collective-permute-done | bytes 114720 | tf_op jit(solution)/shard_map/ppermute | solution.py:772
  36.8 5.5 %collective-permute-done.11.refs_2_ = f32[7,32,128]{2,1,0:T(8,128)S(1)} collective-permute-done((f32[7,32,128]{2,1,0:T(8,128)S(1)}, f32[7,32,128]{2,1,0:T(8,128)S(1)}, u32[]{:S(2)}, u32[]{:S(2)}) %collective-permute-start.11) | collective-permute-done | bytes 114720 | tf_op jit(solution)/shard_map/ppermute | solution.py:772
  44.4 2.9 %coarse.1 = f32[3,32,128]{2,1,0:T(8,128)S(1)} custom-call(s32[2]{0:T(128)S(1)} %pad_add_fusion.place, f32[7,32,128]{2,1,0:T(8,128)S(1)} %merge.1.refs_0_, f32[7,32,128]{2,1,0:T(8,128)S(1)} %collective-permute-done.10.refs_1_, f32[7,32,128]{2,1,0:T(8,128)S(1)} %collective-permute-done.11.refs_2_, f32[7,32,128]{2,1,0:T(8,128)S(1)} %collective-permute-done.12.refs_3_, ...), custom_call_target="tpu_custom_call" | custom-call | flops 805000000 | bytes 2583000 | tf_op jit(solution)/shard_map/coarse/pallas_call | solution.py:726
  47.3 3.1 %up.1 = f32[32,8,512]{2,1,0:T(8,128)} custom-call(s32[2]{0:T(128)S(1)} %pad_add_fusion.place, f32[3,32,128]{2,1,0:T(8,128)S(1)} %coarse.1, f32[12,32,128]{2,1,0:T(8,128)S(1)} %collective-permute-done.18.refs_0_, f32[12,32,128]{2,1,0:T(8,128)S(1)} %collective-permute-done.19.refs_1_, f32[5,32,128]{2,1,0:T(8,128)S(1)} %collective-permute-done.8.refs_2_, ...), custom_call_target="tpu_custom_call" | custom-call | flops 3449999872 | bytes 11070000 | tf_op jit(solution)/shard_map/up/pallas_call | solution.py:726
  (30 shorter events, 4.6 us)
Async XLA Ops:
  0.1 1.0 %copy-start = (f32[32,8,512]{2,1,0:T(8,128)S(1)}, f32[32,8,512]{2,1,0:T(8,128)}, u32[]{:S(2)}) copy-start(f32[32,8,512]{2,1,0:T(8,128)} %conduct.1) | copy-start | bytes 1572868
  1.1 1.0 %copy-start.1 = (f32[32,8,512]{2,1,0:T(8,128)S(1)}, f32[32,8,512]{2,1,0:T(8,128)}, u32[]{:S(2)}) copy-start(f32[32,8,512]{2,1,0:T(8,128)} %binding.1) | copy-start | bytes 1572868
  2.2 4.8 %copy-start.2 = (f32[32,8,512]{2,1,0:T(8,128)S(1)}, f32[32,8,512]{2,1,0:T(8,128)}, u32[]{:S(2)}) copy-start(f32[32,8,512]{2,1,0:T(8,128)} %right_side.1) | copy-start | bytes 1572868
  3.3 12.1 %collective-permute-start.3 = (f32[13,32,128]{2,1,0:T(8,128)S(1)}, f32[13,32,128]{2,1,0:T(8,128)S(1)}, u32[]{:S(2)}, u32[]{:S(2)}) collective-permute-start(f32[13,32,128]{2,1,0:T(8,128)S(1)} %get-tuple-element.48), channel_id=1, source_target_pairs={{0,2},{2,0},{4,6},{6,4},{8,10},{10,8},{12,14},{14,12},{16,18},{18,... | collective-permute-start | bytes 638984 | tf_op jit(solution)/shard_map/ppermute | solution.py:782
  6.3 9.1 %collective-permute-start.4 = (f32[13,32,128]{2,1,0:T(8,128)S(1)}, f32[13,32,128]{2,1,0:T(8,128)S(1)}, u32[]{:S(2)}, u32[]{:S(2)}) collective-permute-start(f32[13,32,128]{2,1,0:T(8,128)S(1)} %get-tuple-element.49), channel_id=1, source_target_pairs={{2,4},{4,2},{6,8},{8,6},{10,12},{12,10},{14,16},{16,14},{18,20},{2... | collective-permute-start | bytes 638984 | tf_op jit(solution)/shard_map/ppermute | solution.py:782
  7.7 1.4 %collective-permute-start.2 = (f32[8,32,128]{2,1,0:T(8,128)S(1)}, f32[8,32,128]{2,1,0:T(8,128)S(1)}, u32[]{:S(2)}, u32[]{:S(2)}) collective-permute-start(f32[8,32,128]{2,1,0:T(8,128)S(1)} %get-tuple-element.47), channel_id=1, source_target_pairs={{0,1},{1,0},{2,3},{3,2},{4,5},{5,4},{6,7},{7,6},{8,9},{9,8},{10,11... | collective-permute-start | bytes 393224 | tf_op jit(solution)/shard_map/ppermute | solution.py:754
  7.8 1.5 %collective-permute-start = (f32[8,32,128]{2,1,0:T(8,128)S(1)}, f32[8,32,128]{2,1,0:T(8,128)S(1)}, u32[]{:S(2)}, u32[]{:S(2)}) collective-permute-start(f32[8,32,128]{2,1,0:T(8,128)S(1)} %get-tuple-element.45), channel_id=1, source_target_pairs={{0,1},{1,0},{2,3},{3,2},{4,5},{5,4},{6,7},{7,6},{8,9},{9,8},{10,11... | collective-permute-start | bytes 393224 | tf_op jit(solution)/shard_map/ppermute | solution.py:754
  8.2 1.3 %collective-permute-start.1 = (f32[8,32,128]{2,1,0:T(8,128)S(1)}, f32[8,32,128]{2,1,0:T(8,128)S(1)}, u32[]{:S(2)}, u32[]{:S(2)}) collective-permute-start(f32[8,32,128]{2,1,0:T(8,128)S(1)} %get-tuple-element.46), channel_id=1, source_target_pairs={{0,1},{1,0},{2,3},{3,2},{4,5},{5,4},{6,7},{7,6},{8,9},{9,8},{10,11... | collective-permute-start | bytes 393224 | tf_op jit(solution)/shard_map/ppermute | solution.py:754
  15.4 1.5 %collective-permute-start.5 = (f32[13,32,128]{2,1,0:T(8,128)S(1)}, f32[13,32,128]{2,1,0:T(8,128)S(1)}, u32[]{:S(2)}, u32[]{:S(2)}) collective-permute-start(f32[13,32,128]{2,1,0:T(8,128)S(1)} %collective-permute-done.3.refs_7_), channel_id=1, source_target_pairs={{0,1},{1,0},{2,3},{3,2},{4,5},{5,4},{6,7},{7,6},{8,9},{9,8},{10,11... | collective-permute-start | bytes 638984 | tf_op jit(solution)/shard_map/ppermute | solution.py:746
  15.4 1.8 %collective-permute-start.6 = (f32[13,32,128]{2,1,0:T(8,128)S(1)}, f32[13,32,128]{2,1,0:T(8,128)S(1)}, u32[]{:S(2)}, u32[]{:S(2)}) collective-permute-start(f32[13,32,128]{2,1,0:T(8,128)S(1)} %collective-permute-done.4.refs_8_), channel_id=1, source_target_pairs={{0,1},{1,0},{2,3},{3,2},{4,5},{5,4},{6,7},{7,6},{8,9},{9,8},{10,11... | collective-permute-start | bytes 638984 | tf_op jit(solution)/shard_map/ppermute | solution.py:746
  19.5 9.6 %collective-permute-start.8 = (f32[5,32,128]{2,1,0:T(8,128)S(1)}, f32[5,32,128]{2,1,0:T(8,128)S(1)}, u32[]{:S(2)}, u32[]{:S(2)}) collective-permute-start(f32[5,32,128]{2,1,0:T(8,128)S(1)} %get-tuple-element.63), channel_id=1, source_target_pairs={{0,4},{2,6},{4,0},{6,2},{8,12},{10,14},{12,8},{14,10},{16,20},{18,... | collective-permute-start | bytes 245768 | tf_op jit(solution)/shard_map/ppermute | solution.py:772
  21.7 5.2 %collective-permute-start.9 = (f32[3,32,128]{2,1,0:T(8,128)S(1)}, f32[3,32,128]{2,1,0:T(8,128)S(1)}, u32[]{:S(2)}, u32[]{:S(2)}) collective-permute-start(f32[3,32,128]{2,1,0:T(8,128)S(1)} %get-tuple-element.62.refs_0_), channel_id=1, source_target_pairs={{0,6},{2,4},{4,2},{6,0},{8,14},{10,12},{12,10},{14,8},{16,22},{18,... | collective-permute-start | bytes 147464 | tf_op jit(solution)/shard_map/ppermute | solution.py:772
  24.4 4.7 %collective-permute-start.7 = (f32[3,32,128]{2,1,0:T(8,128)S(1)}, f32[3,32,128]{2,1,0:T(8,128)S(1)}, u32[]{:S(2)}, u32[]{:S(2)}) collective-permute-start(f32[3,32,128]{2,1,0:T(8,128)S(1)} %get-tuple-element.62.refs_0_), channel_id=1, source_target_pairs={{0,2},{2,0},{4,6},{6,4},{8,10},{10,8},{12,14},{14,12},{16,18},{18,... | collective-permute-start | bytes 147464 | tf_op jit(solution)/shard_map/ppermute | solution.py:772
  24.4 10.5 %collective-permute-start.18 = (f32[12,32,128]{2,1,0:T(8,128)S(1)}, f32[12,32,128]{2,1,0:T(8,128)S(1)}, u32[]{:S(2)}, u32[]{:S(2)}) collective-permute-start(f32[12,32,128]{2,1,0:T(8,128)S(1)} %get-tuple-element.69), channel_id=1, source_target_pairs={{0,2},{2,0},{4,6},{6,4},{8,10},{10,8},{12,14},{14,12},{16,18},{18,... | collective-permute-start | bytes 589832 | tf_op jit(solution)/shard_map/ppermute | solution.py:782
  29.8 7.0 %collective-permute-start.12 = (f32[7,32,128]{2,1,0:T(8,128)S(1)}, f32[7,32,128]{2,1,0:T(8,128)S(1)}, u32[]{:S(2)}, u32[]{:S(2)}) collective-permute-start(f32[7,32,128]{2,1,0:T(8,128)S(1)} %merge.1.refs_0_), channel_id=1, source_target_pairs={{0,24},{2,26},{4,28},{6,30},{8,16},{10,18},{12,20},{14,22},{16,8},... | collective-permute-start | bytes 344072 | tf_op jit(solution)/shard_map/ppermute | solution.py:772
  33.5 8.9 %collective-permute-start.11 = (f32[7,32,128]{2,1,0:T(8,128)S(1)}, f32[7,32,128]{2,1,0:T(8,128)S(1)}, u32[]{:S(2)}, u32[]{:S(2)}) collective-permute-start(f32[7,32,128]{2,1,0:T(8,128)S(1)} %merge.1.refs_0_), channel_id=1, source_target_pairs={{0,16},{2,18},{4,20},{6,22},{8,24},{10,26},{12,28},{14,30},{16,0},... | collective-permute-start | bytes 344072 | tf_op jit(solution)/shard_map/ppermute | solution.py:772
  33.5 8.9 %collective-permute-start.10 = (f32[7,32,128]{2,1,0:T(8,128)S(1)}, f32[7,32,128]{2,1,0:T(8,128)S(1)}, u32[]{:S(2)}, u32[]{:S(2)}) collective-permute-start(f32[7,32,128]{2,1,0:T(8,128)S(1)} %merge.1.refs_0_), channel_id=1, source_target_pairs={{0,8},{2,10},{4,12},{6,14},{8,0},{10,2},{12,4},{14,6},{16,24},{18,... | collective-permute-start | bytes 344072 | tf_op jit(solution)/shard_map/ppermute | solution.py:772
  34.3 1.4 %collective-permute-start.13 = (f32[2,32,128]{2,1,0:T(8,128)S(1)}, f32[2,32,128]{2,1,0:T(8,128)S(1)}, u32[]{:S(2)}, u32[]{:S(2)}) collective-permute-start(f32[2,32,128]{2,1,0:T(8,128)S(1)} %get-tuple-element.64), channel_id=1, source_target_pairs={{4,8},{8,4},{6,10},{10,6},{12,16},{16,12},{14,18},{18,14},{20,24},... | collective-permute-start | bytes 98312 | tf_op jit(solution)/shard_map/ppermute | solution.py:782
  34.9 12.3 %collective-permute-start.19 = (f32[12,32,128]{2,1,0:T(8,128)S(1)}, f32[12,32,128]{2,1,0:T(8,128)S(1)}, u32[]{:S(2)}, u32[]{:S(2)}) collective-permute-start(f32[12,32,128]{2,1,0:T(8,128)S(1)} %get-tuple-element.72), channel_id=1, source_target_pairs={{2,4},{4,2},{6,8},{8,6},{10,12},{12,10},{14,16},{16,14},{18,20},{2... | collective-permute-start | bytes 589832 | tf_op jit(solution)/shard_map/ppermute | solution.py:782
  42.4 1.3 %collective-permute-start.14 = (f32[7,32,128]{2,1,0:T(8,128)S(1)}, f32[7,32,128]{2,1,0:T(8,128)S(1)}, u32[]{:S(2)}, u32[]{:S(2)}) collective-permute-start(f32[7,32,128]{2,1,0:T(8,128)S(1)} %merge.1.refs_0_), channel_id=1, source_target_pairs={{0,1},{1,0},{2,3},{3,2},{4,5},{5,4},{6,7},{7,6},{8,9},{9,8},{10,11... | collective-permute-start | bytes 344072 | tf_op jit(solution)/shard_map/ppermute | solution.py:746
  42.4 1.5 %collective-permute-start.15 = (f32[7,32,128]{2,1,0:T(8,128)S(1)}, f32[7,32,128]{2,1,0:T(8,128)S(1)}, u32[]{:S(2)}, u32[]{:S(2)}) collective-permute-start(f32[7,32,128]{2,1,0:T(8,128)S(1)} %collective-permute-done.10.refs_1_), channel_id=1, source_target_pairs={{0,1},{1,0},{2,3},{3,2},{4,5},{5,4},{6,7},{7,6},{8,9},{9,8},{10,11... | collective-permute-start | bytes 344072 | tf_op jit(solution)/shard_map/ppermute | solution.py:746
  42.9 1.3 %collective-permute-start.16 = (f32[7,32,128]{2,1,0:T(8,128)S(1)}, f32[7,32,128]{2,1,0:T(8,128)S(1)}, u32[]{:S(2)}, u32[]{:S(2)}) collective-permute-start(f32[7,32,128]{2,1,0:T(8,128)S(1)} %collective-permute-done.11.refs_2_), channel_id=1, source_target_pairs={{0,1},{1,0},{2,3},{3,2},{4,5},{5,4},{6,7},{7,6},{8,9},{9,8},{10,11... | collective-permute-start | bytes 344072 | tf_op jit(solution)/shard_map/ppermute | solution.py:746
  42.9 1.5 %collective-permute-start.17 = (f32[7,32,128]{2,1,0:T(8,128)S(1)}, f32[7,32,128]{2,1,0:T(8,128)S(1)}, u32[]{:S(2)}, u32[]{:S(2)}) collective-permute-start(f32[7,32,128]{2,1,0:T(8,128)S(1)} %collective-permute-done.12.refs_3_), channel_id=1, source_target_pairs={{0,1},{1,0},{2,3},{3,2},{4,5},{5,4},{6,7},{7,6},{8,9},{9,8},{10,11... | collective-permute-start | bytes 344072 | tf_op jit(solution)/shard_map/ppermute | solution.py:746

commit v16 on v15

--- a/solution.py
+++ b/solution.py
@@ -41,6 +41,7 @@
             self.up_slots.append((start, self.own[level]))
             start += self.own[level]
         self.up_tiles = start
+        self.last = list(stages(span_count))[-1][1]
 
 
 def put(message, slot, row):
@@ -262,7 +263,7 @@
     return views
 
 
-def start_kernel(sizes, place, conduct, binding, own0, own1, own2, first, second, *refs):
+def start_kernel(sizes, place, conduct, binding, own0, own1, own2, first, second, top, *refs):
     edges, sums = refs[: 2 * sizes.sides], refs[-1]
     n0, n1, n2 = sizes.rows[:3]
     for at, array in enumerate((conduct, binding)):
@@ -274,6 +275,9 @@
     for row in range(2 * n2):
         sums[row, :, : sizes.own[1] * LANES] = own1[2 * row] + own1[2 * row + 1]
     narrow(sizes, place, 1, sums, own2, 2 * n2, "own")
+    last = jnp.concatenate([own2[0] + own2[1], own2[n2] + own2[n2 + 1]], axis=0)
+    last = dot(split(last), pair_table(LANES, 0, None, 0.25))
+    top[0] = last[: sizes.depth] + roll(last[sizes.depth :], LANES // 2, 1)
     ends = []
     for low, at1, at0 in ((n1 - 2, n1 - 1, n0 - 1), (0, 0, 0)):
         edge = n2 - 1 if at0 else 0
@@ -384,26 +388,30 @@
     return rows
 
 
-def merge_into(sizes, place, stride, radix, arrays, source, conduct, binding, first, others=()):
+def merge_into(sizes, place, stride, radix, arrays, source, others=()):
     position = (place[0] // stride) % radix
     source[...] = jnp.zeros(source.shape, f32)
     for step, array in enumerate(arrays):
         at = (position ^ step) * stride
-        rows = unpack_rows(sizes, place, array, 3 * stride + 2, [other[step] for other in others])
-        for index, row in enumerate(rows[: stride + 2]):
+        rows = unpack_rows(sizes, place, array, stride + 2, [other[step] for other in others])
+        for index, row in enumerate(rows):
             source[at + index] = source[at + index] + row
-        for index in range(stride):
-            conduct[at + index + first] = rows[stride + 2 + index]
-            binding[at + index] = rows[2 * stride + 2 + index]
-
-
-def merge_kernel(sizes, stride, radix, place, *refs):
-    arrays, out, (source, conduct, binding) = refs[:radix], refs[radix], refs[radix + 1 :]
-    merge_into(sizes, place, stride, radix, arrays, source, conduct, binding, 0)
-    count = stride * radix
-    rows = [source[row] for row in range(count + 2)]
-    rows += [conduct[row] for row in range(count)] + [binding[row] for row in range(count)]
+
+
+def merge_kernel(sizes, stride, radix, final, place, *refs):
+    arrays, out, tops, source = refs[:radix], refs[radix], refs[radix + 1], refs[radix + 2]
+    merge_into(sizes, place, stride, radix, arrays, source)
+    rows = [source[row] for row in range(source.shape[0])]
     pack_rows(rows, out)
+    position, start = (place[0] // stride) % radix, packing(stride + 2)
+    for step, array in enumerate(arrays):
+        for kind in range(tops.shape[0]):
+            first = start + kind * stride
+            tops[kind, pl.ds((position ^ step) * stride, stride)] = array[first : first + stride]
+    if not final:
+        start, count = packing(len(rows)), stride * radix
+        for kind in range(tops.shape[0]):
+            out[start + kind * count : start + (kind + 1) * count] = tops[kind]
 
 
 def held_rows(sizes, owns, borders):
@@ -463,6 +471,7 @@
     from_prev, *beside_prev = (Arrived(place, pair, 0) for pair in pairs_of)
     from_next, *beside_next = (Arrived(place, pair, 1) for pair in pairs_of)
     (border1, border2), inners, refs = refs[:2], refs[2:5], refs[5:]
+    tops, refs = refs[: sizes.last], refs[sizes.last :]
     outers, contribution, with_far, ups, far, refs = refs[:3], refs[3], refs[4], refs[5:7], refs[7], refs[8:]
     level3, sums = refs
     slots = sizes.slots
@@ -538,11 +547,10 @@
         add(n + 3, level.fx[n + 2] * field(n + 2))
         fine_held = held
     narrow(sizes, place, 2, sums.at[:, :, : sizes.held[2]], level3, 3)
-    for at in (0, 1):
-        sums[at, :, : sizes.held[2]] = held_row(2, at, 0) + held_row(2, at, 1)
-    narrow(sizes, place, 2, sums.at[:, :, : sizes.held[2]], level3.at[3:5], 2)
-    tiles = packing(5)
-    pack_rows([level3[row] for row in range(5)], contribution)
+    tiles = packing(3) + sizes.last
+    pack_rows([level3[row] for row in range(3)], contribution)
+    for kind, top in enumerate(tops):
+        contribution[packing(3) + kind] = top[0]
     with_far[0:tiles] = contribution[...]
     v0, s1, v1 = levels[0].smooth, levels[1].source, levels[1].smooth
     s2, v2 = levels[2].source, levels[2].smooth
@@ -576,10 +584,18 @@
 def coarse_kernel(sizes, stride, radix, place, *refs):
     blocks, refs = refs[:radix], refs[radix:]
     others, refs = [refs[side * radix : (side + 1) * radix] for side in range(sizes.sides)], refs[sizes.sides * radix :]
+    tops, beside_tops, refs = refs[0], refs[1 : 1 + sizes.sides], refs[1 + sizes.sides :]
     out, merged, sums = refs[:3]
     coarse = [refs[3 + 9 * index : 12 + 9 * index] for index in range(3)]
     total = sizes.span_count
-    merge_into(sizes, place, stride, radix, blocks, merged, coarse[0][4], coarse[0][5], 1, others)
+    merge_into(sizes, place, stride, radix, blocks, merged, others)
+    position = (place[0] // stride) % radix
+    for kind in range(radix):
+        for low in range(stride):
+            tile, beside_tiles = tops[kind, low], [array[kind, low] for array in beside_tops]
+            rows = unpack_rows(sizes, place, tile[None], 2, [other[None] for other in beside_tiles])
+            row = (position ^ kind) * stride + low
+            coarse[0][4][row + 1], coarse[0][5][row] = rows
     zero = jnp.zeros((sizes.depth, LANES), f32)
     for index in range(3):
         level = 3 + index
@@ -647,7 +663,7 @@
     pair, far_pair, inners, outers, owns = refs[:2], refs[2:4], refs[4:7], refs[7:10], refs[10:12]
     levels = [Level(sizes, index, inner, outer) for index, (inner, outer) in enumerate(zip(inners, outers))]
     from_prev, from_next = (Arrived(place, pair, forward) for forward in (0, 1))
-    tiles = packing(5)
+    tiles = packing(3) + sizes.last
     far_pair = (far_pair[0].at[tiles : tiles + sizes.held[2] // LANES], far_pair[1])
     fars = [Arrived(place, far_pair, forward, 2) for forward in (0, 1)]
     borders0, out, refs = refs[12 : 12 + 3 * s], refs[12 + 3 * s], refs[13 + 3 * s :]
@@ -793,11 +809,11 @@
     held = [(depth, count) for count in sizes.held]
     down_message = (sizes.tiles, *tile)
     up_message = (sizes.up_tiles + 1, *tile)
-    own0, own1, own2, first, second, *edges = call(
+    own0, own1, own2, first, second, top, *edges = call(
         functools.partial(start_kernel, sizes),
         "start",
         1.1,
-        [(2, n0, *own[0]), (2 * n1, *own[1]), (2 * n2, *own[2]), down_message, down_message]
+        [(2, n0, *own[0]), (2 * n1, *own[1]), (2 * n2, *own[2]), down_message, down_message, (1, *tile)]
         + [(n0, depth, BORDER)] * 2 * s,
         [(2 * n1, *own[0])],
         place,
@@ -817,7 +833,7 @@
     borders += edge_columns(edges, sizes)
     plan = list(stages(sizes.span_count))
 
-    part = packing(5)
+    part = packing(3) + sizes.last
     far = (sizes.held[2] // LANES, *tile)
     inners = [(sum(inner_rows(sizes, level)), *held[level]) for level in range(3)]
     outers = [(sum(outer_rows(sizes, level)), *held[level]) for level in range(3)]
@@ -830,16 +846,18 @@
         place,
         [own0, own1, own2, turned, *borders],
     )
-    halos, inner = lax.optimization_barrier((halos, inner))
+    inner, top = lax.optimization_barrier((inner, top))
+    tops = swap(top, *plan[-1])
+    halos, inner, tops = lax.optimization_barrier((halos, inner, tops))
     sides = beside(halos, sizes)
     downs = call(
         functools.partial(down_kernel, sizes),
         "down",
         2.5,
         [*outers, (part, *tile), (part + far[0], *tile), up_message, up_message, far],
-        [(5, *tile), (n1 + 2, *held[0])],
+        [(3, *tile), (n1 + 2, *held[0])],
         place,
-        [own0, own1, own2, turned, *borders, *halos, *sum(sides, []), *inner],
+        [own0, own1, own2, turned, *borders, *halos, *sum(sides, []), *inner, *tops],
     )
     outer, blocks, with_far, ups, far_second = downs[:3], downs[3], downs[4], list(downs[5:7]), downs[7]
     far_rows = None
@@ -847,36 +865,40 @@
         count = stride * radix
         if far_rows is None:
             blocks = swap(blocks, stride, radix, {2: with_far})
-            far_rows = [blocks[2], exchange([None, far_second], 2)[1]]
+            far_rows = [blocks[2]]
+            blocks[1], ups[0] = lax.optimization_barrier((blocks[1], ups[0]))
         else:
             blocks = swap(blocks, stride, radix)
-        (blocks,) = call(
-            functools.partial(merge_kernel, sizes, stride, radix),
+        final = (stride, radix) == plan[-2]
+        rows = packing(count + 2) + (0 if final else sizes.last * count)
+        blocks, top_tiles = call(
+            functools.partial(merge_kernel, sizes, stride, radix, final),
             "merge",
-            0.9,
-            [(packing(3 * count + 2), *tile)],
-            [(count + 2, *tile), (count, *tile), (count, *tile)],
+            0.7,
+            [(rows, *tile), (sizes.last, count, *tile)],
+            [(count + 2, *tile)],
             place,
             blocks,
         )
     stride, radix = plan[-1]
     blocks = swap(blocks, stride, radix)
     received = lax.optimization_barrier([exchange([ups[0], None], 1)[0], ups[1]])
+    far_rows.append(exchange([None, far_second], 2)[1])
     received = [received[0], exchange([None, received[1]], 1)[1]] + far_rows
     scratch = [(sizes.span_count + 2, *tile), (max(sizes.span_count // 2, 2), *tile)]
     for index in range(3):
         count = sizes.span_count >> index
         scratch += [(count + 1, *tile)] + [(count, *tile)] * 3 + [(count + 2, *tile)] + [(count, *tile)] * 2
         scratch += [(count + 2, *tile)] * 2
-    blocks, received[3] = lax.optimization_barrier((blocks, received[3]))
+    blocks, received[3], top_tiles = lax.optimization_barrier((blocks, received[3], top_tiles))
     (coarse,) = call(
         functools.partial(coarse_kernel, sizes, stride, radix),
         "coarse",
-        0.7,
+        0.01,
         [(n3 + 2, *tile)],
         scratch,
         place,
-        [*blocks, *sum(beside(blocks, sizes), [])],
+        [*blocks, *sum(beside(blocks, sizes), []), top_tiles, *sum(beside([top_tiles], sizes), [])],
     )
     scratch = [(n1 + 2, *held[1]), (n2 + 2, *held[2]), diffusivity.shape, (2, *held[0]), (2, *held[1])]
     scratch += [(n3 + 2, *held[2]), (n2 + 2, *held[1]), (n1 + 2, *held[0])]

time: 50.6 us -> 59 us (1.17)
  the two profiles are of different devices: /device:TPU:0 before, /device:TPU:4 now
where the time goes in v16:
time: 59 us; the launch traced here: 58.7 us
  starting transfers between devices  24.5 us (42%)
  waiting for transfers between devices  19.2 us (33%)
  Pallas kernels  12.7 us (22%)
  local copies, waits for them, and re-layouts  2.09 us (4%)
    ppermute x9, starting transfers between devices, swap(): lax.ppermute(others.get(step, value), 'span', [(device, device ^ step * s...  12.8 us
    pallas_call x7, Pallas kernels, call(): pl.pallas_call(body, name=name, out_shape=[jax.ShapeDtypeStruct(shape, f3...  12.7 us
    ppermute x5, starting transfers between devices, exchange(): lax.ppermute(value, 'span', route)  9.02 us
    ppermute x9, waiting for transfers between devices, swap(): lax.ppermute(others.get(step, value), 'span', [(device, device ^ step * s...  8.15 us
    ppermute x5, waiting for transfers between devices, exchange(): lax.ppermute(value, 'span', route)  7.3 us
    ppermute x7, waiting for transfers between devices, beside(): lax.ppermute(value, 'width', [(0, 1), (1, 0)])  2.51 us
    unnamed x6, local copies, waits for them, and re-layouts  2.09 us
    ppermute x7, starting transfers between devices, beside(): lax.ppermute(value, 'width', [(0, 1), (1, 0)])  2.04 us
  transfers between devices with their start and end apart: 24, of which 14 were waited for; matrix products, arithmetic and copies ran while one was open for 0% of the time, Pallas kernels for 10%

profile of v16, /device:TPU:4, one launch (start us, length us, event | category | flops | bytes accessed | tf_op | source)
XLA Modules:
  0.0 58.7 jit_solution(16003288526739001027)
XLA Ops:
  0.1 1.0 %copy-done = f32[32,8,512]{2,1,0:T(8,128)S(1)} copy-done((f32[32,8,512]{2,1,0:T(8,128)S(1)}, f32[32,8,512]{2,1,0:T(8,128)}, u32[]{:S(2)}) %copy-start) | copy-done | bytes 524312
  1.1 1.0 %copy-done.1 = f32[32,8,512]{2,1,0:T(8,128)S(1)} copy-done((f32[32,8,512]{2,1,0:T(8,128)S(1)}, f32[32,8,512]{2,1,0:T(8,128)}, u32[]{:S(2)}) %copy-start.1) | copy-done | bytes 524312
  2.2 1.3 %start.1 = (f32[2,8,32,512]{3,2,1,0:T(8,128)S(1)}, f32[8,32,256]{2,1,0:T(8,128)S(1)}, f32[4,32,128]{2,1,0:T(8,128)S(1)}, f32[13,32,128]{2,1,0:T(8,128)S(1)}, f32...) custom-call(s32[2]{0:T(128)S(1)} %pad_add_fusion.place, ...), custom_call_target="tpu_custom_call" | custom-call | flops 1264999936 | bytes 4059000 | tf_op jit(solution)/shard_map/start/pallas_call | solution.py:742
  3.5 1.5 %collective-permute-start.3 = (f32[13,32,128]{2,1,0:T(8,128)S(1)}, f32[13,32,128]{2,1,0:T(8,128)S(1)}, u32[]{:S(2)}, u32[]{:S(2)}) collective-permute-start(f32[13,32,128]{2,1,0:T(8,128)S(1)} %get-tuple-element.64), channel_id=1, source_target_pairs={{0,2},{2,0},{4,6},{6,4},{8,10},{10,8},{12,14},{14,12},{16,18},{18,... | collective-permute-start | bytes 638984 | tf_op jit(solution)/shard_map/ppermute | solution.py:798
  5.0 1.9 %collective-permute-start.4 = (f32[13,32,128]{2,1,0:T(8,128)S(1)}, f32[13,32,128]{2,1,0:T(8,128)S(1)}, u32[]{:S(2)}, u32[]{:S(2)}) collective-permute-start(f32[13,32,128]{2,1,0:T(8,128)S(1)} %get-tuple-element.65), channel_id=1, source_target_pairs={{2,4},{4,2},{6,8},{8,6},{10,12},{12,10},{14,16},{16,14},{18,20},{2... | collective-permute-start | bytes 638984 | tf_op jit(solution)/shard_map/ppermute | solution.py:798
  9.5 1.8 %inner.1 = (f32[8,32,128]{2,1,0:T(8,128)S(1)}, f32[4,32,128]{2,1,0:T(8,128)S(1)}, f32[35,32,640]{2,1,0:T(8,128)S(1)}, f32[17,32,384]{2,1,0:T(8,128)S(1)}, f32[5,32,256]{2,1,0:T(8,128)S(1)}) custom-call(s32[2]{0:T(128)S(1)} %pad_add_fusion.place, f32[2,8,32,512]{3,2,1,0:T(8,128)S(1)} %get-tuple-element.57.refs_0_.refs_10_, ...), custom_call_target="tpu_custom_call" | custom-call | flops 575000000 | bytes 1845000 | tf_op jit(solution)/shard_map/inner/pallas_call | solution.py:742
  11.3 4.1 %collective-permute-start.7 = (f32[1,32,128]{2,1,0:T(8,128)S(1)}, f32[1,32,128]{2,1,0:T(8,128)S(1)}, u32[]{:S(2)}, u32[]{:S(2)}) collective-permute-start(f32[1,32,128]{2,1,0:T(8,128)S(1)} %get-tuple-element.85.refs_16_), channel_id=1, source_target_pairs={{0,24},{2,26},{4,28},{6,30},{8,16},{10,18},{12,20},{14,22},{16,8},... | collective-permute-start | bytes 49160 | tf_op jit(solution)/shard_map/ppermute | solution.py:788
  16.1 1.1 %collective-permute-done.7.refs_19_ = f32[1,32,128]{2,1,0:T(8,128)S(1)} collective-permute-done((f32[1,32,128]{2,1,0:T(8,128)S(1)}, f32[1,32,128]{2,1,0:T(8,128)S(1)}, u32[]{:S(2)}, u32[]{:S(2)}) %collective-permute-start.7) | collective-permute-done | bytes 16416 | tf_op jit(solution)/shard_map/ppermute | solution.py:788
  17.2 2.9 %collective-permute-done.6.refs_18_ = f32[1,32,128]{2,1,0:T(8,128)S(1)} collective-permute-done((f32[1,32,128]{2,1,0:T(8,128)S(1)}, f32[1,32,128]{2,1,0:T(8,128)S(1)}, u32[]{:S(2)}, u32[]{:S(2)}) %collective-permute-start.6) | collective-permute-done | bytes 16416 | tf_op jit(solution)/shard_map/ppermute | solution.py:788
  20.7 1.0 %collective-permute-done.8.refs_9_ = f32[13,32,128]{2,1,0:T(8,128)S(1)} collective-permute-done((f32[13,32,128]{2,1,0:T(8,128)S(1)}, f32[13,32,128]{2,1,0:T(8,128)S(1)}, u32[]{:S(2)}, u32[]{:S(2)}) %collective-permute-start.8) | collective-permute-done | bytes 213024 | tf_op jit(solution)/shard_map/ppermute | solution.py:762
  22.0 2.2 %down.1 = (f32[6,32,640]{2,1,0:T(8,128)S(1)}, f32[26,32,384]{2,1,0:T(8,128)S(1)}, f32[24,32,256]{2,1,0:T(8,128)S(1)}, f32[6,32,128]{2,1,0:T(8,128)S(1)}, f32[8,3...) custom-call(s32[2]{0:T(128)S(1)} %pad_add_fusion.place, ...), custom_call_target="tpu_custom_call" | custom-call | flops 2875000064 | bytes 9225000 | tf_op jit(solution)/shard_map/down/pallas_call | solution.py:742
  24.2 1.5 %collective-permute-start.11 = (f32[8,32,128]{2,1,0:T(8,128)S(1)}, f32[8,32,128]{2,1,0:T(8,128)S(1)}, u32[]{:S(2)}, u32[]{:S(2)}) collective-permute-start(f32[8,32,128]{2,1,0:T(8,128)S(1)} %get-tuple-element.92), channel_id=1, source_target_pairs={{0,4},{2,6},{4,0},{6,2},{8,12},{10,14},{12,8},{14,10},{16,20},{18,... | collective-permute-start | bytes 393224 | tf_op jit(solution)/shard_map/ppermute | solution.py:788
  25.7 1.6 %collective-permute-start.10 = (f32[6,32,128]{2,1,0:T(8,128)S(1)}, f32[6,32,128]{2,1,0:T(8,128)S(1)}, u32[]{:S(2)}, u32[]{:S(2)}) collective-permute-start(f32[6,32,128]{2,1,0:T(8,128)S(1)} %get-tuple-element.89.refs_0_), channel_id=1, source_target_pairs={{0,2},{2,0},{4,6},{6,4},{8,10},{10,8},{12,14},{14,12},{16,18},{18,... | collective-permute-start | bytes 294920 | tf_op jit(solution)/shard_map/ppermute | solution.py:788
  27.8 3.5 %collective-permute-done.10.refs_1_ = f32[6,32,128]{2,1,0:T(8,128)S(1)} collective-permute-done((f32[6,32,128]{2,1,0:T(8,128)S(1)}, f32[6,32,128]{2,1,0:T(8,128)S(1)}, u32[]{:S(2)}, u32[]{:S(2)}) %collective-permute-start.10) | collective-permute-done | bytes 98336 | tf_op jit(solution)/shard_map/ppermute | solution.py:788
  31.3 1.7 %collective-permute-start.22 = (f32[12,32,128]{2,1,0:T(8,128)S(1)}, f32[12,32,128]{2,1,0:T(8,128)S(1)}, u32[]{:S(2)}, u32[]{:S(2)}) collective-permute-start(f32[12,32,128]{2,1,0:T(8,128)S(1)} %get-tuple-element.101), channel_id=1, source_target_pairs={{0,2},{2,0},{4,6},{6,4},{8,10},{10,8},{12,14},{14,12},{16,18},{18,... | collective-permute-start | bytes 589832 | tf_op jit(solution)/shard_map/ppermute | solution.py:798
  34.3 0.9 %collective-permute-start.15 = (f32[3,32,128]{2,1,0:T(8,128)S(1)}, f32[3,32,128]{2,1,0:T(8,128)S(1)}, u32[]{:S(2)}, u32[]{:S(2)}) collective-permute-start(f32[3,32,128]{2,1,0:T(8,128)S(1)} %get-tuple-element.96.refs_0_), channel_id=1, source_target_pairs={{0,24},{2,26},{4,28},{6,30},{8,16},{10,18},{12,20},{14,22},{16,8},... | collective-permute-start | bytes 147464 | tf_op jit(solution)/shard_map/ppermute | solution.py:788
  35.2 1.2 %collective-permute-start.14 = (f32[3,32,128]{2,1,0:T(8,128)S(1)}, f32[3,32,128]{2,1,0:T(8,128)S(1)}, u32[]{:S(2)}, u32[]{:S(2)}) collective-permute-start(f32[3,32,128]{2,1,0:T(8,128)S(1)} %get-tuple-element.96.refs_0_), channel_id=1, source_target_pairs={{0,16},{2,18},{4,20},{6,22},{8,24},{10,26},{12,28},{14,30},{16,0},... | collective-permute-start | bytes 147464 | tf_op jit(solution)/shard_map/ppermute | solution.py:788
  36.4 2.4 %collective-permute-start.13 = (f32[3,32,128]{2,1,0:T(8,128)S(1)}, f32[3,32,128]{2,1,0:T(8,128)S(1)}, u32[]{:S(2)}, u32[]{:S(2)}) collective-permute-start(f32[3,32,128]{2,1,0:T(8,128)S(1)} %get-tuple-element.96.refs_0_), channel_id=1, source_target_pairs={{0,8},{2,10},{4,12},{6,14},{8,0},{10,2},{12,4},{14,6},{16,24},{18,... | collective-permute-start | bytes 147464 | tf_op jit(solution)/shard_map/ppermute | solution.py:788
  38.8 2.0 %collective-permute-start.16 = (f32[2,32,128]{2,1,0:T(8,128)S(1)}, f32[2,32,128]{2,1,0:T(8,128)S(1)}, u32[]{:S(2)}, u32[]{:S(2)}) collective-permute-start(f32[2,32,128]{2,1,0:T(8,128)S(1)} %get-tuple-element.94), channel_id=1, source_target_pairs={{4,8},{8,4},{6,10},{10,6},{12,16},{16,12},{14,18},{18,14},{20,24},... | collective-permute-start | bytes 98312 | tf_op jit(solution)/shard_map/ppermute | solution.py:798
  40.8 4.7 %collective-permute-done.16.refs_3_ = f32[2,32,128]{2,1,0:T(8,128)S(1)} collective-permute-done((f32[2,32,128]{2,1,0:T(8,128)S(1)}, f32[2,32,128]{2,1,0:T(8,128)S(1)}, u32[]{:S(2)}, u32[]{:S(2)}) %collective-permute-start.16) | collective-permute-done | bytes 32800 | tf_op jit(solution)/shard_map/ppermute | solution.py:798
  45.6 1.9 %collective-permute-start.23 = (f32[12,32,128]{2,1,0:T(8,128)S(1)}, f32[12,32,128]{2,1,0:T(8,128)S(1)}, u32[]{:S(2)}, u32[]{:S(2)}) collective-permute-start(f32[12,32,128]{2,1,0:T(8,128)S(1)} %get-tuple-element.104), channel_id=1, source_target_pairs={{2,4},{4,2},{6,8},{8,6},{10,12},{12,10},{14,16},{16,14},{18,20},{2... | collective-permute-start | bytes 589832 | tf_op jit(solution)/shard_map/ppermute | solution.py:798
  50.1 2.9 %coarse.1 = f32[3,32,128]{2,1,0:T(8,128)S(1)} custom-call(s32[2]{0:T(128)S(1)} %pad_add_fusion.place, f32[3,32,128]{2,1,0:T(8,128)S(1)} %get-tuple-element.96.refs_0_, f32[3,32,128]{2,1,0:T(8,128)S(1)} %collective-permute-done.13.refs_1_, f32[3,32,128]{2,1,0:T(8,128)S(1)} %collective-permute-done.14.refs_2_, ...), custom_call_target="tpu_custom_call" | custom-call | flops 11500000 | bytes 36900 | tf_op jit(solution)/shard_map/coarse/pallas_call | solution.py:742
  53.0 2.6 %collective-permute-done.23.refs_1_ = f32[12,32,128]{2,1,0:T(8,128)S(1)} collective-permute-done((f32[12,32,128]{2,1,0:T(8,128)S(1)}, f32[12,32,128]{2,1,0:T(8,128)S(1)}, u32[]{:S(2)}, u32[]{:S(2)}) %collective-permute-start.23) | collective-permute-done | bytes 196640 | tf_op jit(solution)/shard_map/ppermute | solution.py:798
  55.6 3.1 %up.1 = f32[32,8,512]{2,1,0:T(8,128)} custom-call(s32[2]{0:T(128)S(1)} %pad_add_fusion.place, f32[3,32,128]{2,1,0:T(8,128)S(1)} %coarse.1, f32[12,32,128]{2,1,0:T(8,128)S(1)} %collective-permute-done.22.refs_0_, f32[12,32,128]{2,1,0:T(8,128)S(1)} %collective-permute-done.23.refs_1_, f32[8,32,128]{2,1,0:T(8,128)S(1)} %collective-permute-done.11.refs_2_, ...), custom_call_target="tpu_custom_call" | custom-call | flops 3449999872 | bytes 11070000 | tf_op jit(solution)/shard_map/up/pallas_call | solution.py:742
  (38 shorter events, 8.7 us)
Async XLA Ops:
  3.5 16.6 %collective-permute-start.3 = (f32[13,32,128]{2,1,0:T(8,128)S(1)}, f32[13,32,128]{2,1,0:T(8,128)S(1)}, u32[]{:S(2)}, u32[]{:S(2)}) collective-permute-start(f32[13,32,128]{2,1,0:T(8,128)S(1)} %get-tuple-element.64), channel_id=1, source_target_pairs={{0,2},{2,0},{4,6},{6,4},{8,10},{10,8},{12,14},{14,12},{16,18},{18,... | collective-permute-start | bytes 638984 | tf_op jit(solution)/shard_map/ppermute | solution.py:798
  5.0 15.1 %collective-permute-start.4 = (f32[13,32,128]{2,1,0:T(8,128)S(1)}, f32[13,32,128]{2,1,0:T(8,128)S(1)}, u32[]{:S(2)}, u32[]{:S(2)}) collective-permute-start(f32[13,32,128]{2,1,0:T(8,128)S(1)} %get-tuple-element.65), channel_id=1, source_target_pairs={{2,4},{4,2},{6,8},{8,6},{10,12},{12,10},{14,16},{16,14},{18,20},{2... | collective-permute-start | bytes 638984 | tf_op jit(solution)/shard_map/ppermute | solution.py:798
  7.6 1.4 %collective-permute-start.2 = (f32[8,32,128]{2,1,0:T(8,128)S(1)}, f32[8,32,128]{2,1,0:T(8,128)S(1)}, u32[]{:S(2)}, u32[]{:S(2)}) collective-permute-start(f32[8,32,128]{2,1,0:T(8,128)S(1)} %get-tuple-element.63), channel_id=1, source_target_pairs={{0,1},{1,0},{2,3},{3,2},{4,5},{5,4},{6,7},{7,6},{8,9},{9,8},{10,11... | collective-permute-start | bytes 393224 | tf_op jit(solution)/shard_map/ppermute | solution.py:770
  7.7 1.5 %collective-permute-start = (f32[8,32,128]{2,1,0:T(8,128)S(1)}, f32[8,32,128]{2,1,0:T(8,128)S(1)}, u32[]{:S(2)}, u32[]{:S(2)}) collective-permute-start(f32[8,32,128]{2,1,0:T(8,128)S(1)} %get-tuple-element.61), channel_id=1, source_target_pairs={{0,1},{1,0},{2,3},{3,2},{4,5},{5,4},{6,7},{7,6},{8,9},{9,8},{10,11... | collective-permute-start | bytes 393224 | tf_op jit(solution)/shard_map/ppermute | solution.py:770
  8.2 1.3 %collective-permute-start.1 = (f32[8,32,128]{2,1,0:T(8,128)S(1)}, f32[8,32,128]{2,1,0:T(8,128)S(1)}, u32[]{:S(2)}, u32[]{:S(2)}) collective-permute-start(f32[8,32,128]{2,1,0:T(8,128)S(1)} %get-tuple-element.62), channel_id=1, source_target_pairs={{0,1},{1,0},{2,3},{3,2},{4,5},{5,4},{6,7},{7,6},{8,9},{9,8},{10,11... | collective-permute-start | bytes 393224 | tf_op jit(solution)/shard_map/ppermute | solution.py:770
  11.3 5.9 %collective-permute-start.7 = (f32[1,32,128]{2,1,0:T(8,128)S(1)}, f32[1,32,128]{2,1,0:T(8,128)S(1)}, u32[]{:S(2)}, u32[]{:S(2)}) collective-permute-start(f32[1,32,128]{2,1,0:T(8,128)S(1)} %get-tuple-element.85.refs_16_), channel_id=1, source_target_pairs={{0,24},{2,26},{4,28},{6,30},{8,16},{10,18},{12,20},{14,22},{16,8},... | collective-permute-start | bytes 49160 | tf_op jit(solution)/shard_map/ppermute | solution.py:788
  15.5 4.6 %collective-permute-start.6 = (f32[1,32,128]{2,1,0:T(8,128)S(1)}, f32[1,32,128]{2,1,0:T(8,128)S(1)}, u32[]{:S(2)}, u32[]{:S(2)}) collective-permute-start(f32[1,32,128]{2,1,0:T(8,128)S(1)} %get-tuple-element.85.refs_16_), channel_id=1, source_target_pairs={{0,16},{2,18},{4,20},{6,22},{8,24},{10,26},{12,28},{14,30},{16,0},... | collective-permute-start | bytes 49160 | tf_op jit(solution)/shard_map/ppermute | solution.py:788
  15.5 4.6 %collective-permute-start.5 = (f32[1,32,128]{2,1,0:T(8,128)S(1)}, f32[1,32,128]{2,1,0:T(8,128)S(1)}, u32[]{:S(2)}, u32[]{:S(2)}) collective-permute-start(f32[1,32,128]{2,1,0:T(8,128)S(1)} %get-tuple-element.85.refs_16_), channel_id=1, source_target_pairs={{0,8},{2,10},{4,12},{6,14},{8,0},{10,2},{12,4},{14,6},{16,24},{18,... | collective-permute-start | bytes 49160 | tf_op jit(solution)/shard_map/ppermute | solution.py:788
  20.1 1.5 %collective-permute-start.8 = (f32[13,32,128]{2,1,0:T(8,128)S(1)}, f32[13,32,128]{2,1,0:T(8,128)S(1)}, u32[]{:S(2)}, u32[]{:S(2)}) collective-permute-start(f32[13,32,128]{2,1,0:T(8,128)S(1)} %collective-permute-done.3.refs_7_), channel_id=1, source_target_pairs={{0,1},{1,0},{2,3},{3,2},{4,5},{5,4},{6,7},{7,6},{8,9},{9,8},{10,11... | collective-permute-start | bytes 638984 | tf_op jit(solution)/shard_map/ppermute | solution.py:762
  20.2 1.8 %collective-permute-start.9 = (f32[13,32,128]{2,1,0:T(8,128)S(1)}, f32[13,32,128]{2,1,0:T(8,128)S(1)}, u32[]{:S(2)}, u32[]{:S(2)}) collective-permute-start(f32[13,32,128]{2,1,0:T(8,128)S(1)} %collective-permute-done.4.refs_8_), channel_id=1, source_target_pairs={{0,1},{1,0},{2,3},{3,2},{4,5},{5,4},{6,7},{7,6},{8,9},{9,8},{10,11... | collective-permute-start | bytes 638984 | tf_op jit(solution)/shard_map/ppermute | solution.py:762
  24.2 9.4 %collective-permute-start.11 = (f32[8,32,128]{2,1,0:T(8,128)S(1)}, f32[8,32,128]{2,1,0:T(8,128)S(1)}, u32[]{:S(2)}, u32[]{:S(2)}) collective-permute-start(f32[8,32,128]{2,1,0:T(8,128)S(1)} %get-tuple-element.92), channel_id=1, source_target_pairs={{0,4},{2,6},{4,0},{6,2},{8,12},{10,14},{12,8},{14,10},{16,20},{18,... | collective-permute-start | bytes 393224 | tf_op jit(solution)/shard_map/ppermute | solution.py:788
  25.7 5.6 %collective-permute-start.10 = (f32[6,32,128]{2,1,0:T(8,128)S(1)}, f32[6,32,128]{2,1,0:T(8,128)S(1)}, u32[]{:S(2)}, u32[]{:S(2)}) collective-permute-start(f32[6,32,128]{2,1,0:T(8,128)S(1)} %get-tuple-element.89.refs_0_), channel_id=1, source_target_pairs={{0,2},{2,0},{4,6},{6,4},{8,10},{10,8},{12,14},{14,12},{16,18},{18,... | collective-permute-start | bytes 294920 | tf_op jit(solution)/shard_map/ppermute | solution.py:788
  27.3 6.3 %collective-permute-start.12 = (f32[6,32,128]{2,1,0:T(8,128)S(1)}, f32[6,32,128]{2,1,0:T(8,128)S(1)}, u32[]{:S(2)}, u32[]{:S(2)}) collective-permute-start(f32[6,32,128]{2,1,0:T(8,128)S(1)} %get-tuple-element.89.refs_0_), channel_id=1, source_target_pairs={{0,6},{2,4},{4,2},{6,0},{8,14},{10,12},{12,10},{14,8},{16,22},{18,... | collective-permute-start | bytes 294920 | tf_op jit(solution)/shard_map/ppermute | solution.py:788
  31.3 14.3 %collective-permute-start.22 = (f32[12,32,128]{2,1,0:T(8,128)S(1)}, f32[12,32,128]{2,1,0:T(8,128)S(1)}, u32[]{:S(2)}, u32[]{:S(2)}) collective-permute-start(f32[12,32,128]{2,1,0:T(8,128)S(1)} %get-tuple-element.101), channel_id=1, source_target_pairs={{0,2},{2,0},{4,6},{6,4},{8,10},{10,8},{12,14},{14,12},{16,18},{18,... | collective-permute-start | bytes 589832 | tf_op jit(solution)/shard_map/ppermute | solution.py:798
  34.3 11.2 %collective-permute-start.15 = (f32[3,32,128]{2,1,0:T(8,128)S(1)}, f32[3,32,128]{2,1,0:T(8,128)S(1)}, u32[]{:S(2)}, u32[]{:S(2)}) collective-permute-start(f32[3,32,128]{2,1,0:T(8,128)S(1)} %get-tuple-element.96.refs_0_), channel_id=1, source_target_pairs={{0,24},{2,26},{4,28},{6,30},{8,16},{10,18},{12,20},{14,22},{16,8},... | collective-permute-start | bytes 147464 | tf_op jit(solution)/shard_map/ppermute | solution.py:788
  35.2 10.3 %collective-permute-start.14 = (f32[3,32,128]{2,1,0:T(8,128)S(1)}, f32[3,32,128]{2,1,0:T(8,128)S(1)}, u32[]{:S(2)}, u32[]{:S(2)}) collective-permute-start(f32[3,32,128]{2,1,0:T(8,128)S(1)} %get-tuple-element.96.refs_0_), channel_id=1, source_target_pairs={{0,16},{2,18},{4,20},{6,22},{8,24},{10,26},{12,28},{14,30},{16,0},... | collective-permute-start | bytes 147464 | tf_op jit(solution)/shard_map/ppermute | solution.py:788
  36.4 9.1 %collective-permute-start.13 = (f32[3,32,128]{2,1,0:T(8,128)S(1)}, f32[3,32,128]{2,1,0:T(8,128)S(1)}, u32[]{:S(2)}, u32[]{:S(2)}) collective-permute-start(f32[3,32,128]{2,1,0:T(8,128)S(1)} %get-tuple-element.96.refs_0_), channel_id=1, source_target_pairs={{0,8},{2,10},{4,12},{6,14},{8,0},{10,2},{12,4},{14,6},{16,24},{18,... | collective-permute-start | bytes 147464 | tf_op jit(solution)/shard_map/ppermute | solution.py:788
  38.8 6.7 %collective-permute-start.16 = (f32[2,32,128]{2,1,0:T(8,128)S(1)}, f32[2,32,128]{2,1,0:T(8,128)S(1)}, u32[]{:S(2)}, u32[]{:S(2)}) collective-permute-start(f32[2,32,128]{2,1,0:T(8,128)S(1)} %get-tuple-element.94), channel_id=1, source_target_pairs={{4,8},{8,4},{6,10},{10,6},{12,16},{16,12},{14,18},{18,14},{20,24},... | collective-permute-start | bytes 98312 | tf_op jit(solution)/shard_map/ppermute | solution.py:798
  45.5 4.7 %collective-permute-start.21 = (f32[4,4,32,128]{3,2,1,0:T(8,128)S(1)}, f32[4,4,32,128]{3,2,1,0:T(8,128)S(1)}, u32[]{:S(2)}, u32[]{:S(2)}) collective-permute-start(f32[4,4,32,128]{3,2,1,0:T(8,128)S(1)} %get-tuple-element.100.refs_8_), channel_id=1, source_target_pairs={{0,1},{1,0},{2,3},{3,2},{4,5},{5,4},{6,7},{7,6},{8,9},{9,8},{10,11... | collective-permute-start | bytes 786440 | tf_op jit(solution)/shard_map/ppermute | solution.py:762
  45.6 10.1 %collective-permute-start.23 = (f32[12,32,128]{2,1,0:T(8,128)S(1)}, f32[12,32,128]{2,1,0:T(8,128)S(1)}, u32[]{:S(2)}, u32[]{:S(2)}) collective-permute-start(f32[12,32,128]{2,1,0:T(8,128)S(1)} %get-tuple-element.104), channel_id=1, source_target_pairs={{2,4},{4,2},{6,8},{8,6},{10,12},{12,10},{14,16},{16,14},{18,20},{2... | collective-permute-start | bytes 589832 | tf_op jit(solution)/shard_map/ppermute | solution.py:798
  47.5 1.4 %collective-permute-start.17 = (f32[3,32,128]{2,1,0:T(8,128)S(1)}, f32[3,32,128]{2,1,0:T(8,128)S(1)}, u32[]{:S(2)}, u32[]{:S(2)}) collective-permute-start(f32[3,32,128]{2,1,0:T(8,128)S(1)} %get-tuple-element.96.refs_0_), channel_id=1, source_target_pairs={{0,1},{1,0},{2,3},{3,2},{4,5},{5,4},{6,7},{7,6},{8,9},{9,8},{10,11... | collective-permute-start | bytes 147464 | tf_op jit(solution)/shard_map/ppermute | solution.py:762
  48.0 1.2 %collective-permute-start.18 = (f32[3,32,128]{2,1,0:T(8,128)S(1)}, f32[3,32,128]{2,1,0:T(8,128)S(1)}, u32[]{:S(2)}, u32[]{:S(2)}) collective-permute-start(f32[3,32,128]{2,1,0:T(8,128)S(1)} %collective-permute-done.13.refs_1_), channel_id=1, source_target_pairs={{0,1},{1,0},{2,3},{3,2},{4,5},{5,4},{6,7},{7,6},{8,9},{9,8},{10,11... | collective-permute-start | bytes 147464 | tf_op jit(solution)/shard_map/ppermute | solution.py:762
  48.1 1.3 %collective-permute-start.19 = (f32[3,32,128]{2,1,0:T(8,128)S(1)}, f32[3,32,128]{2,1,0:T(8,128)S(1)}, u32[]{:S(2)}, u32[]{:S(2)}) collective-permute-start(f32[3,32,128]{2,1,0:T(8,128)S(1)} %collective-permute-done.14.refs_2_), channel_id=1, source_target_pairs={{0,1},{1,0},{2,3},{3,2},{4,5},{5,4},{6,7},{7,6},{8,9},{9,8},{10,11... | collective-permute-start | bytes 147464 | tf_op jit(solution)/shard_map/ppermute | solution.py:762
  48.9 1.2 %collective-permute-start.20 = (f32[3,32,128]{2,1,0:T(8,128)S(1)}, f32[3,32,128]{2,1,0:T(8,128)S(1)}, u32[]{:S(2)}, u32[]{:S(2)}) collective-permute-start(f32[3,32,128]{2,1,0:T(8,128)S(1)} %collective-permute-done.15.refs_3_), channel_id=1, source_target_pairs={{0,1},{1,0},{2,3},{3,2},{4,5},{5,4},{6,7},{7,6},{8,9},{9,8},{10,11... | collective-permute-start | bytes 147464 | tf_op jit(solution)/shard_map/ppermute | solution.py:762
  (3 other events, 6.8 us)

commit v17 on v15

--- a/solution.py
+++ b/solution.py
@@ -31,7 +31,7 @@
         self.rows = [extent_x >> level for level in range(4)]
         self.slots = []
         start = 0
-        for level in (0, 1, 1, 1, 2, 2, 2):
+        for level in (0, 1, 1, 1, 2, 2):
             self.slots.append((start, self.own[level]))
             start += self.own[level]
         self.tiles = start
@@ -276,9 +276,9 @@
     narrow(sizes, place, 1, sums, own2, 2 * n2, "own")
     ends = []
     for low, at1, at0 in ((n1 - 2, n1 - 1, n0 - 1), (0, 0, 0)):
-        edge = n2 - 1 if at0 else 0
-        rows = (own0[0, at0], own1[low], own1[low + 1], own1[n1 + at1])
-        ends.append(rows + (own2[n2 - 2], own2[n2 - 1], own2[n2 + edge]))
+        near, far = (n2 - 1, n2 - 2) if at0 else (0, 1)
+        rows = (own0[0, at0], own1[low], own1[low + 1], own1[n1 + at1], own2[far], own2[n2 + near])
+        ends.append(rows)
     for slot, next_row, prev_row in zip(sizes.slots, *ends):
         put_pair(place, (first, second), slot, next_row, prev_row)
     for at in (0, 1):
@@ -464,7 +464,7 @@
     from_next, *beside_next = (Arrived(place, pair, 1) for pair in pairs_of)
     (border1, border2), inners, refs = refs[:2], refs[2:5], refs[5:]
     outers, contribution, with_far, ups, far, refs = refs[:3], refs[3], refs[4], refs[5:7], refs[7], refs[8:]
-    level3, sums = refs
+    level3, near, sums = refs
     slots = sizes.slots
     n0, n1, n2 = sizes.rows[:3]
     levels = [Level(sizes, index, inner, outer) for index, (inner, outer) in enumerate(zip(inners, outers))]
@@ -483,6 +483,9 @@
             return next_row(0, 0)
         return held_row(0, 0, row - 1)
 
+    for at, row_of in enumerate((prev_row, next_row)):
+        sums[at, :, : sizes.held[1]] = row_of(1, 1) + row_of(1, 2)
+    narrow(sizes, place, 1, sums.at[:, :, : sizes.held[1]], near, 2)
     zero = jnp.zeros((sizes.depth, sizes.held[0]), f32)
     level = levels[0]
     bound0 = lambda row: held_row(0, 1, row - 1)
@@ -504,24 +507,26 @@
     sweep(n0 - 1, n0, field, bound0, level.fx, level.fy, level.fz, emit)
     add(n0 + 1, level.fx[n0] * field(n0))
     fine_held = sizes.held[0]
-    for index, first in ((1, 1), (2, 4)):
+    for index in (1, 2):
         level, n = levels[index], sizes.rows[index]
         held = sizes.held[index]
         narrow(
             sizes, place, index - 1, sums.at[:, :, :fine_held], level.source.outer, level.source.outer.shape[0]
         )
         binding = level.binding
-        binding[0] = prev_row(index, first + 2)
-        binding[n + 1] = next_row(index, first + 2)
+        binding[0] = prev_row(index, 3 if index == 1 else 5)
+        binding[n + 1] = next_row(index, 3 if index == 1 else 5)
         for row in range(n):
             binding[row + 1] = held_row(index, 1, row)
 
-        def conduct(row, n=n, index=index, first=first):
-            if row < 2:
-                return prev_row(index, first + row)
-            if row >= n + 2:
-                return next_row(index, first + row - n - 2)
-            return held_row(index, 0, row - 2)
+        def conduct(row, n=n, index=index):
+            if 2 <= row < n + 2:
+                return held_row(index, 0, row - 2)
+            if index == 1:
+                return prev_row(1, 1 + row) if row < 2 else next_row(1, row - n - 1)
+            if row in (1, n + 2):
+                return near[0 if row == 1 else 1]
+            return (prev_row if row == 0 else next_row)(2, 4)
 
         bound = lambda row, binding=binding: binding[row - 1]
         coefficients(
@@ -576,46 +581,44 @@
 def coarse_kernel(sizes, stride, radix, place, *refs):
     blocks, refs = refs[:radix], refs[radix:]
     others, refs = [refs[side * radix : (side + 1) * radix] for side in range(sizes.sides)], refs[sizes.sides * radix :]
-    out, merged, sums = refs[:3]
-    coarse = [refs[3 + 9 * index : 12 + 9 * index] for index in range(3)]
+    out, merged, sums, both, defects = refs[:5]
+    coarse = [refs[5 + 9 * index : 14 + 9 * index] for index in range(3)]
     total = sizes.span_count
     merge_into(sizes, place, stride, radix, blocks, merged, coarse[0][4], coarse[0][5], 1, others)
     zero = jnp.zeros((sizes.depth, LANES), f32)
     for index in range(3):
         level = 3 + index
         fx, fy, fz, weight, conduct, binding, source, smooth, iterate = coarse[index]
-        count = total >> index
+        count, half = total >> index, total >> index + 1
         for array in (conduct, smooth, iterate):
             array[0] = zero
             array[count + 1] = zero
-        if index == 0:
-            source = merged.at[1 : count + 1]
+        if index < 2:
+            conduct_next, binding_next = coarse[index + 1][4:6]
+            for row in range(half):
+                sums[row] = conduct[2 * row + 1] + conduct[2 * row + 2]
+                sums[half + row] = binding[2 * row] + binding[2 * row + 1]
+            narrow(sizes, place, level, sums, both, 2 * half)
+            for row in range(half):
+                conduct_next[row + 1], binding_next[row] = both[row], both[half + row]
         bound = lambda row, binding=binding: binding[row - 1]
         at_row = lambda row, conduct=conduct: conduct[row]
         every = (range(1, count + 2), range(1, count + 1), range(1, count + 1))
         coefficients(sizes, place, level, at_row, bound, fx, fy, fz, weight, every)
+    for index in range(3):
+        level = 3 + index
+        fx, fy, fz, weight, conduct, binding, source, smooth, iterate = coarse[index]
+        count = total >> index
+        bound = lambda row, binding=binding: binding[row - 1]
+        if index == 0:
+            source = merged.at[1 : count + 1]
         for row in range(count):
             smooth[row + 1] = weight[row] * source[row]
         if index < 2:
-            conduct_next, binding_next, source_next = coarse[index + 1][4:7]
-            half = count // 2
-            for row in range(half):
-                sums[row, :, :LANES] = conduct[2 * row + 1] + conduct[2 * row + 2]
-            narrow(sizes, place, level, sums, conduct_next.at[1 : half + 1], half)
-            for row in range(half):
-                sums[row, :, :LANES] = binding[2 * row] + binding[2 * row + 1]
-            narrow(sizes, place, level, sums, binding_next, half)
-
-            def add(row, value, source=source):
-                value = source[row - 1] - value
-                slot = (row - 1) // 2
-                if row % 2 == 1:
-                    sums[slot, :, :LANES] = value
-                else:
-                    sums[slot, :, :LANES] = sums[slot, :, :LANES] + value
-
-            sweep(1, count, lambda row, smooth=smooth: smooth[row], bound, fx, fy, fz, add)
-            narrow(sizes, place, level, sums, source_next, half)
+            add = in_pairs(defects, lambda row: ((row - 1) // 2, row % 2 == 1))
+            emit = lambda row, value, source=source, add=add: add(row, source[row - 1] - value)
+            sweep(1, count, lambda row, smooth=smooth: smooth[row], bound, fx, fy, fz, emit)
+            narrow(sizes, place, level, defects, coarse[index + 1][6], count // 2)
 
     fx, fy, fz, weight, conduct, binding, source, smooth, iterate = coarse[2]
     held, other = smooth, iterate
@@ -837,7 +840,7 @@
         "down",
         2.5,
         [*outers, (part, *tile), (part + far[0], *tile), up_message, up_message, far],
-        [(5, *tile), (n1 + 2, *held[0])],
+        [(5, *tile), (2, *held[2]), (n1 + 2, *held[0])],
         place,
         [own0, own1, own2, turned, *borders, *halos, *sum(sides, []), *inner],
     )
@@ -863,7 +866,7 @@
     blocks = swap(blocks, stride, radix)
     received = lax.optimization_barrier([exchange([ups[0], None], 1)[0], ups[1]])
     received = [received[0], exchange([None, received[1]], 1)[1]] + far_rows
-    scratch = [(sizes.span_count + 2, *tile), (max(sizes.span_count // 2, 2), *tile)]
+    scratch = [(sizes.span_count + 2, *tile)] + [(sizes.span_count, *tile)] * 3
     for index in range(3):
         count = sizes.span_count >> index
         scratch += [(count + 1, *tile)] + [(count, *tile)] * 3 + [(count + 2, *tile)] + [(count, *tile)] * 2

time: 50.6 us -> 50.2 us (level)
  waiting for transfers between devices: 16.9 us -> 13.2 us
  starting transfers between devices: 18.6 us -> 21.9 us
    ppermute x5, waiting for transfers between devices: 4.02 us -> 0.01 us  [exchange(): lax.ppermute(value, 'span', route)]
    ppermute x6, starting transfers between devices: 9.38 us -> 12.6 us  [swap(): lax.ppermute(others.get(step, value), 'span', [(device, device ^ step * s...]
  transfers between devices with their start and end apart: 20 -> 20, of which waited for: 14 -> 13; matrix products, arithmetic and copies ran while one was open for 0% -> 0% of each run, Pallas kernels for 12% -> 12%
where the time goes in v17:
time: 50.2 us; the launch traced here: 49.9 us
  starting transfers between devices  21.9 us (44%)
  waiting for transfers between devices  13.2 us (26%)
  Pallas kernels  12.6 us (25%)
  local copies, waits for them, and re-layouts  2.09 us (4%)
    ppermute x6, starting transfers between devices, swap(): lax.ppermute(others.get(step, value), 'span', [(device, device ^ step * s...  12.6 us
    pallas_call x7, Pallas kernels, call(): pl.pallas_call(body, name=name, out_shape=[jax.ShapeDtypeStruct(shape, f3...  12.6 us
    ppermute x6, waiting for transfers between devices, swap(): lax.ppermute(others.get(step, value), 'span', [(device, device ^ step * s...  9.71 us
    ppermute x5, starting transfers between devices, exchange(): lax.ppermute(value, 'span', route)  7.01 us
    ppermute x6, waiting for transfers between devices, beside(): lax.ppermute(value, 'width', [(0, 1), (1, 0)])  2.19 us
    unnamed x6, local copies, waits for them, and re-layouts  2.09 us
    ppermute x6, starting transfers between devices, beside(): lax.ppermute(value, 'width', [(0, 1), (1, 0)])  1.6 us
    ppermute x3, waiting for transfers between devices, edge_columns(): return [lax.ppermute(edges[0], 'width', [(0, 1), (1, 0)])]  1.27 us
  transfers between devices with their start and end apart: 20, of which 13 were waited for; matrix products, arithmetic and copies ran while one was open for 0% of the time, Pallas kernels for 12%

profile of v17, /device:TPU:0, one launch (start us, length us, event | category | flops | bytes accessed | tf_op | source)
XLA Modules:
  0.0 49.9 jit_solution(5025694891907650153)
XLA Ops:
  0.1 1.0 %copy-done = f32[32,8,512]{2,1,0:T(8,128)S(1)} copy-done((f32[32,8,512]{2,1,0:T(8,128)S(1)}, f32[32,8,512]{2,1,0:T(8,128)}, u32[]{:S(2)}) %copy-start) | copy-done | bytes 524312
  1.1 1.0 %copy-done.1 = f32[32,8,512]{2,1,0:T(8,128)S(1)} copy-done((f32[32,8,512]{2,1,0:T(8,128)S(1)}, f32[32,8,512]{2,1,0:T(8,128)}, u32[]{:S(2)}) %copy-start.1) | copy-done | bytes 524312
  2.2 1.1 %start.1 = (f32[2,8,32,512]{3,2,1,0:T(8,128)S(1)}, f32[8,32,256]{2,1,0:T(8,128)S(1)}, f32[4,32,128]{2,1,0:T(8,128)S(1)}, f32[12,32,128]{2,1,0:T(8,128)S(1)}, f32...) custom-call(s32[2]{0:T(128)S(1)} %pad_add_fusion.place, f32[32,8,512]{2,1,0:T(8,128)S(1)} %copy-done, ...), custom_call_target="tpu_custom_call" | custom-call | flops 1264999936 | bytes 4059000 | tf_op jit(solution)/shard_map/start/pallas_call | solution.py:729
  3.3 3.0 %collective-permute-start.3 = (f32[12,32,128]{2,1,0:T(8,128)S(1)}, f32[12,32,128]{2,1,0:T(8,128)S(1)}, u32[]{:S(2)}, u32[]{:S(2)}) collective-permute-start(f32[12,32,128]{2,1,0:T(8,128)S(1)} %get-tuple-element.48), channel_id=1, source_target_pairs={{0,2},{2,0},{4,6},{6,4},{8,10},{10,8},{12,14},{14,12},{16,18},{18,... | collective-permute-start | bytes 589832 | tf_op jit(solution)/shard_map/ppermute | solution.py:785
  6.3 0.7 %collective-permute-start.4 = (f32[12,32,128]{2,1,0:T(8,128)S(1)}, f32[12,32,128]{2,1,0:T(8,128)S(1)}, u32[]{:S(2)}, u32[]{:S(2)}) collective-permute-start(f32[12,32,128]{2,1,0:T(8,128)S(1)} %get-tuple-element.49), channel_id=1, source_target_pairs={{2,4},{4,2},{6,8},{8,6},{10,12},{12,10},{14,16},{16,14},{18,20},{2... | collective-permute-start | bytes 589832 | tf_op jit(solution)/shard_map/ppermute | solution.py:785
  7.0 0.7 %turn.1 = (f32[8,32,512]{2,1,0:T(8,128)S(1)}, f32[8,32,128]{2,1,0:T(8,128)S(1)}) custom-call(s32[2]{0:T(128)S(1)} %pad_add_fusion.place, f32[32,8,512]{2,1,0:T(8,128)S(1)} %copy-done.2), custom_call_target="tpu_custom_call" | custom-call | flops 805000000 | bytes 2583000 | tf_op jit(solution)/shard_map/turn/pallas_call | solution.py:729
  8.3 0.8 %collective-permute-done.2.refs_6_.refs_14_ = f32[8,32,128]{2,1,0:T(8,128)S(1)} collective-permute-done((f32[8,32,128]{2,1,0:T(8,128)S(1)}, f32[8,32,128]{2,1,0:T(8,128)S(1)}, u32[]{:S(2)}, u32[]{:S(2)}) %collective-permute-start.2) | collective-permute-done | bytes 131104 | tf_op jit(solution)/shard_map/ppermute | solution.py:757
  9.6 1.8 %inner.1 = (f32[8,32,128]{2,1,0:T(8,128)S(1)}, f32[4,32,128]{2,1,0:T(8,128)S(1)}, f32[35,32,640]{2,1,0:T(8,128)S(1)}, f32[17,32,384]{2,1,0:T(8,128)S(1)}, f32[5,32,256]{2,1,0:T(8,128)S(1)}) custom-call(s32[2]{0:T(128)S(1)} %pad_add_fusion.place, f32[2,8,32,512]{3,2,1,0:T(8,128)S(1)} %get-tuple-element.41.refs_0_.refs_10_, ...), custom_call_target="tpu_custom_call" | custom-call | flops 575000000 | bytes 1845000 | tf_op jit(solution)/shard_map/inner/pallas_call | solution.py:729
  12.0 0.9 %collective-permute-done.5.refs_9_ = f32[12,32,128]{2,1,0:T(8,128)S(1)} collective-permute-done((f32[12,32,128]{2,1,0:T(8,128)S(1)}, f32[12,32,128]{2,1,0:T(8,128)S(1)}, u32[]{:S(2)}, u32[]{:S(2)}) %collective-permute-start.5) | collective-permute-done | bytes 196640 | tf_op jit(solution)/shard_map/ppermute | solution.py:749
  13.2 2.3 %down.1 = (f32[6,32,640]{2,1,0:T(8,128)S(1)}, f32[26,32,384]{2,1,0:T(8,128)S(1)}, f32[24,32,256]{2,1,0:T(8,128)S(1)}, f32[3,32,128]{2,1,0:T(8,128)S(1)}, f32[5,3...) custom-call(s32[2]{0:T(128)S(1)} %pad_add_fusion.place, ...), custom_call_target="tpu_custom_call" | custom-call | flops 2875000064 | bytes 9225000 | tf_op jit(solution)/shard_map/down/pallas_call | solution.py:729
  15.5 5.5 %collective-permute-start.8 = (f32[5,32,128]{2,1,0:T(8,128)S(1)}, f32[5,32,128]{2,1,0:T(8,128)S(1)}, u32[]{:S(2)}, u32[]{:S(2)}) collective-permute-start(f32[5,32,128]{2,1,0:T(8,128)S(1)} %get-tuple-element.63), channel_id=1, source_target_pairs={{0,4},{2,6},{4,0},{6,2},{8,12},{10,14},{12,8},{14,10},{16,20},{18,... | collective-permute-start | bytes 245768 | tf_op jit(solution)/shard_map/ppermute | solution.py:775
  21.1 2.6 %collective-permute-start.9 = (f32[3,32,128]{2,1,0:T(8,128)S(1)}, f32[3,32,128]{2,1,0:T(8,128)S(1)}, u32[]{:S(2)}, u32[]{:S(2)}) collective-permute-start(f32[3,32,128]{2,1,0:T(8,128)S(1)} %get-tuple-element.62.refs_0_), channel_id=1, source_target_pairs={{0,6},{2,4},{4,2},{6,0},{8,14},{10,12},{12,10},{14,8},{16,22},{18,... | collective-permute-start | bytes 147464 | tf_op jit(solution)/shard_map/ppermute | solution.py:775
  23.7 2.0 %collective-permute-start.18 = (f32[12,32,128]{2,1,0:T(8,128)S(1)}, f32[12,32,128]{2,1,0:T(8,128)S(1)}, u32[]{:S(2)}, u32[]{:S(2)}) collective-permute-start(f32[12,32,128]{2,1,0:T(8,128)S(1)} %get-tuple-element.69), channel_id=1, source_target_pairs={{0,2},{2,0},{4,6},{6,4},{8,10},{10,8},{12,14},{14,12},{16,18},{18,... | collective-permute-start | bytes 589832 | tf_op jit(solution)/shard_map/ppermute | solution.py:785
  25.7 0.6 %collective-permute-done.9.refs_3_ = f32[3,32,128]{2,1,0:T(8,128)S(1)} collective-permute-done((f32[3,32,128]{2,1,0:T(8,128)S(1)}, f32[3,32,128]{2,1,0:T(8,128)S(1)}, u32[]{:S(2)}, u32[]{:S(2)}) %collective-permute-start.9) | collective-permute-done | bytes 49184 | tf_op jit(solution)/shard_map/ppermute | solution.py:775
  26.4 2.0 %collective-permute-done.7.refs_1_ = f32[3,32,128]{2,1,0:T(8,128)S(1)} collective-permute-done((f32[3,32,128]{2,1,0:T(8,128)S(1)}, f32[3,32,128]{2,1,0:T(8,128)S(1)}, u32[]{:S(2)}, u32[]{:S(2)}) %collective-permute-start.7) | collective-permute-done | bytes 49184 | tf_op jit(solution)/shard_map/ppermute | solution.py:775
  28.3 0.7 %merge.1.refs_0_ = f32[7,32,128]{2,1,0:T(8,128)S(1)} custom-call(s32[2]{0:T(128)S(1)} %pad_add_fusion.place, f32[3,32,128]{2,1,0:T(8,128)S(1)} %get-tuple-element.62.refs_0_, f32[3,32,128]{2,1,0:T(8,128)S(1)} %collective-permute-done.7.refs_1_, f32[5,32,128]{2,1,0:T(8,128)S(1)} %collective-permute-done.8.refs_2_, ...), custom_call_target="tpu_custom_call" | custom-call | flops 1035000000 | bytes 3321000 | tf_op jit(solution)/shard_map/merge/pallas_call | solution.py:729
  29.1 3.7 %collective-permute-start.12 = (f32[7,32,128]{2,1,0:T(8,128)S(1)}, f32[7,32,128]{2,1,0:T(8,128)S(1)}, u32[]{:S(2)}, u32[]{:S(2)}) collective-permute-start(f32[7,32,128]{2,1,0:T(8,128)S(1)} %merge.1.refs_0_), channel_id=1, source_target_pairs={{0,24},{2,26},{4,28},{6,30},{8,16},{10,18},{12,20},{14,22},{16,8},... | collective-permute-start | bytes 344072 | tf_op jit(solution)/shard_map/ppermute | solution.py:775
  32.8 0.8 %collective-permute-start.10 = (f32[7,32,128]{2,1,0:T(8,128)S(1)}, f32[7,32,128]{2,1,0:T(8,128)S(1)}, u32[]{:S(2)}, u32[]{:S(2)}) collective-permute-start(f32[7,32,128]{2,1,0:T(8,128)S(1)} %merge.1.refs_0_), channel_id=1, source_target_pairs={{0,8},{2,10},{4,12},{6,14},{8,0},{10,2},{12,4},{14,6},{16,24},{18,... | collective-permute-start | bytes 344072 | tf_op jit(solution)/shard_map/ppermute | solution.py:775
  33.5 0.7 %collective-permute-start.13 = (f32[2,32,128]{2,1,0:T(8,128)S(1)}, f32[2,32,128]{2,1,0:T(8,128)S(1)}, u32[]{:S(2)}, u32[]{:S(2)}) collective-permute-start(f32[2,32,128]{2,1,0:T(8,128)S(1)} %get-tuple-element.64), channel_id=1, source_target_pairs={{4,8},{8,4},{6,10},{10,6},{12,16},{16,12},{14,18},{18,14},{20,24},... | collective-permute-start | bytes 98312 | tf_op jit(solution)/shard_map/ppermute | solution.py:785
  34.2 0.7 %collective-permute-start.19 = (f32[12,32,128]{2,1,0:T(8,128)S(1)}, f32[12,32,128]{2,1,0:T(8,128)S(1)}, u32[]{:S(2)}, u32[]{:S(2)}) collective-permute-start(f32[12,32,128]{2,1,0:T(8,128)S(1)} %get-tuple-element.72), channel_id=1, source_target_pairs={{2,4},{4,2},{6,8},{8,6},{10,12},{12,10},{14,16},{16,14},{18,20},{2... | collective-permute-start | bytes 589832 | tf_op jit(solution)/shard_map/ppermute | solution.py:785
  34.9 1.3 %collective-permute-done.12.refs_3_ = f32[7,32,128]{2,1,0:T(8,128)S(1)} collective-permute-done((f32[7,32,128]{2,1,0:T(8,128)S(1)}, f32[7,32,128]{2,1,0:T(8,128)S(1)}, u32[]{:S(2)}, u32[]{:S(2)}) %collective-permute-start.12) | collective-permute-done | bytes 114720 | tf_op jit(solution)/shard_map/ppermute | solution.py:775
  36.3 5.7 %collective-permute-done.11.refs_2_ = f32[7,32,128]{2,1,0:T(8,128)S(1)} collective-permute-done((f32[7,32,128]{2,1,0:T(8,128)S(1)}, f32[7,32,128]{2,1,0:T(8,128)S(1)}, u32[]{:S(2)}, u32[]{:S(2)}) %collective-permute-start.11) | collective-permute-done | bytes 114720 | tf_op jit(solution)/shard_map/ppermute | solution.py:775
  44.0 2.8 %coarse.1 = f32[3,32,128]{2,1,0:T(8,128)S(1)} custom-call(s32[2]{0:T(128)S(1)} %pad_add_fusion.place, f32[7,32,128]{2,1,0:T(8,128)S(1)} %merge.1.refs_0_, f32[7,32,128]{2,1,0:T(8,128)S(1)} %collective-permute-done.10.refs_1_, f32[7,32,128]{2,1,0:T(8,128)S(1)} %collective-permute-done.11.refs_2_, f32[7,32,128]{2,1,0:T(8,128)S(1)} %collective-permute-done.12.refs_3_, ...), custom_call_target="tpu_custom_call" | custom-call | flops 805000000 | bytes 2583000 | tf_op jit(solution)/shard_map/coarse/pallas_call | solution.py:729
  46.8 3.1 %up.1 = f32[32,8,512]{2,1,0:T(8,128)} custom-call(s32[2]{0:T(128)S(1)} %pad_add_fusion.place, f32[3,32,128]{2,1,0:T(8,128)S(1)} %coarse.1, f32[12,32,128]{2,1,0:T(8,128)S(1)} %collective-permute-done.18.refs_0_, f32[12,32,128]{2,1,0:T(8,128)S(1)} %collective-permute-done.19.refs_1_, f32[5,32,128]{2,1,0:T(8,128)S(1)} %collective-permute-done.8.refs_2_, ...), custom_call_target="tpu_custom_call" | custom-call | flops 3449999872 | bytes 11070000 | tf_op jit(solution)/shard_map/up/pallas_call | solution.py:729
  (30 shorter events, 4.1 us)
Async XLA Ops:
  0.1 1.0 %copy-start = (f32[32,8,512]{2,1,0:T(8,128)S(1)}, f32[32,8,512]{2,1,0:T(8,128)}, u32[]{:S(2)}) copy-start(f32[32,8,512]{2,1,0:T(8,128)} %conduct.1) | copy-start | bytes 1572868
  1.1 1.0 %copy-start.1 = (f32[32,8,512]{2,1,0:T(8,128)S(1)}, f32[32,8,512]{2,1,0:T(8,128)}, u32[]{:S(2)}) copy-start(f32[32,8,512]{2,1,0:T(8,128)} %binding.1) | copy-start | bytes 1572868
  2.2 4.8 %copy-start.2 = (f32[32,8,512]{2,1,0:T(8,128)S(1)}, f32[32,8,512]{2,1,0:T(8,128)}, u32[]{:S(2)}) copy-start(f32[32,8,512]{2,1,0:T(8,128)} %right_side.1) | copy-start | bytes 1572868
  3.3 8.1 %collective-permute-start.3 = (f32[12,32,128]{2,1,0:T(8,128)S(1)}, f32[12,32,128]{2,1,0:T(8,128)S(1)}, u32[]{:S(2)}, u32[]{:S(2)}) collective-permute-start(f32[12,32,128]{2,1,0:T(8,128)S(1)} %get-tuple-element.48), channel_id=1, source_target_pairs={{0,2},{2,0},{4,6},{6,4},{8,10},{10,8},{12,14},{14,12},{16,18},{18,... | collective-permute-start | bytes 589832 | tf_op jit(solution)/shard_map/ppermute | solution.py:785
  6.3 5.1 %collective-permute-start.4 = (f32[12,32,128]{2,1,0:T(8,128)S(1)}, f32[12,32,128]{2,1,0:T(8,128)S(1)}, u32[]{:S(2)}, u32[]{:S(2)}) collective-permute-start(f32[12,32,128]{2,1,0:T(8,128)S(1)} %get-tuple-element.49), channel_id=1, source_target_pairs={{2,4},{4,2},{6,8},{8,6},{10,12},{12,10},{14,16},{16,14},{18,20},{2... | collective-permute-start | bytes 589832 | tf_op jit(solution)/shard_map/ppermute | solution.py:785
  7.7 1.4 %collective-permute-start.2 = (f32[8,32,128]{2,1,0:T(8,128)S(1)}, f32[8,32,128]{2,1,0:T(8,128)S(1)}, u32[]{:S(2)}, u32[]{:S(2)}) collective-permute-start(f32[8,32,128]{2,1,0:T(8,128)S(1)} %get-tuple-element.47), channel_id=1, source_target_pairs={{0,1},{1,0},{2,3},{3,2},{4,5},{5,4},{6,7},{7,6},{8,9},{9,8},{10,11... | collective-permute-start | bytes 393224 | tf_op jit(solution)/shard_map/ppermute | solution.py:757
  7.7 1.5 %collective-permute-start = (f32[8,32,128]{2,1,0:T(8,128)S(1)}, f32[8,32,128]{2,1,0:T(8,128)S(1)}, u32[]{:S(2)}, u32[]{:S(2)}) collective-permute-start(f32[8,32,128]{2,1,0:T(8,128)S(1)} %get-tuple-element.45), channel_id=1, source_target_pairs={{0,1},{1,0},{2,3},{3,2},{4,5},{5,4},{6,7},{7,6},{8,9},{9,8},{10,11... | collective-permute-start | bytes 393224 | tf_op jit(solution)/shard_map/ppermute | solution.py:757
  8.2 1.3 %collective-permute-start.1 = (f32[8,32,128]{2,1,0:T(8,128)S(1)}, f32[8,32,128]{2,1,0:T(8,128)S(1)}, u32[]{:S(2)}, u32[]{:S(2)}) collective-permute-start(f32[8,32,128]{2,1,0:T(8,128)S(1)} %get-tuple-element.46), channel_id=1, source_target_pairs={{0,1},{1,0},{2,3},{3,2},{4,5},{5,4},{6,7},{7,6},{8,9},{9,8},{10,11... | collective-permute-start | bytes 393224 | tf_op jit(solution)/shard_map/ppermute | solution.py:757
  11.4 1.5 %collective-permute-start.5 = (f32[12,32,128]{2,1,0:T(8,128)S(1)}, f32[12,32,128]{2,1,0:T(8,128)S(1)}, u32[]{:S(2)}, u32[]{:S(2)}) collective-permute-start(f32[12,32,128]{2,1,0:T(8,128)S(1)} %collective-permute-done.3.refs_7_), channel_id=1, source_target_pairs={{0,1},{1,0},{2,3},{3,2},{4,5},{5,4},{6,7},{7,6},{8,9},{9,8},{10,11... | collective-permute-start | bytes 589832 | tf_op jit(solution)/shard_map/ppermute | solution.py:749
  11.7 1.5 %collective-permute-start.6 = (f32[12,32,128]{2,1,0:T(8,128)S(1)}, f32[12,32,128]{2,1,0:T(8,128)S(1)}, u32[]{:S(2)}, u32[]{:S(2)}) collective-permute-start(f32[12,32,128]{2,1,0:T(8,128)S(1)} %collective-permute-done.4.refs_8_), channel_id=1, source_target_pairs={{0,1},{1,0},{2,3},{3,2},{4,5},{5,4},{6,7},{7,6},{8,9},{9,8},{10,11... | collective-permute-start | bytes 589832 | tf_op jit(solution)/shard_map/ppermute | solution.py:749
  15.5 12.8 %collective-permute-start.8 = (f32[5,32,128]{2,1,0:T(8,128)S(1)}, f32[5,32,128]{2,1,0:T(8,128)S(1)}, u32[]{:S(2)}, u32[]{:S(2)}) collective-permute-start(f32[5,32,128]{2,1,0:T(8,128)S(1)} %get-tuple-element.63), channel_id=1, source_target_pairs={{0,4},{2,6},{4,0},{6,2},{8,12},{10,14},{12,8},{14,10},{16,20},{18,... | collective-permute-start | bytes 245768 | tf_op jit(solution)/shard_map/ppermute | solution.py:775
  21.1 5.3 %collective-permute-start.9 = (f32[3,32,128]{2,1,0:T(8,128)S(1)}, f32[3,32,128]{2,1,0:T(8,128)S(1)}, u32[]{:S(2)}, u32[]{:S(2)}) collective-permute-start(f32[3,32,128]{2,1,0:T(8,128)S(1)} %get-tuple-element.62.refs_0_), channel_id=1, source_target_pairs={{0,6},{2,4},{4,2},{6,0},{8,14},{10,12},{12,10},{14,8},{16,22},{18,... | collective-permute-start | bytes 147464 | tf_op jit(solution)/shard_map/ppermute | solution.py:775
  23.7 4.7 %collective-permute-start.7 = (f32[3,32,128]{2,1,0:T(8,128)S(1)}, f32[3,32,128]{2,1,0:T(8,128)S(1)}, u32[]{:S(2)}, u32[]{:S(2)}) collective-permute-start(f32[3,32,128]{2,1,0:T(8,128)S(1)} %get-tuple-element.62.refs_0_), channel_id=1, source_target_pairs={{0,2},{2,0},{4,6},{6,4},{8,10},{10,8},{12,14},{14,12},{16,18},{18,... | collective-permute-start | bytes 147464 | tf_op jit(solution)/shard_map/ppermute | solution.py:775
  23.7 10.5 %collective-permute-start.18 = (f32[12,32,128]{2,1,0:T(8,128)S(1)}, f32[12,32,128]{2,1,0:T(8,128)S(1)}, u32[]{:S(2)}, u32[]{:S(2)}) collective-permute-start(f32[12,32,128]{2,1,0:T(8,128)S(1)} %get-tuple-element.69), channel_id=1, source_target_pairs={{0,2},{2,0},{4,6},{6,4},{8,10},{10,8},{12,14},{14,12},{16,18},{18,... | collective-permute-start | bytes 589832 | tf_op jit(solution)/shard_map/ppermute | solution.py:785
  29.1 7.2 %collective-permute-start.12 = (f32[7,32,128]{2,1,0:T(8,128)S(1)}, f32[7,32,128]{2,1,0:T(8,128)S(1)}, u32[]{:S(2)}, u32[]{:S(2)}) collective-permute-start(f32[7,32,128]{2,1,0:T(8,128)S(1)} %merge.1.refs_0_), channel_id=1, source_target_pairs={{0,24},{2,26},{4,28},{6,30},{8,16},{10,18},{12,20},{14,22},{16,8},... | collective-permute-start | bytes 344072 | tf_op jit(solution)/shard_map/ppermute | solution.py:775
  32.8 9.2 %collective-permute-start.11 = (f32[7,32,128]{2,1,0:T(8,128)S(1)}, f32[7,32,128]{2,1,0:T(8,128)S(1)}, u32[]{:S(2)}, u32[]{:S(2)}) collective-permute-start(f32[7,32,128]{2,1,0:T(8,128)S(1)} %merge.1.refs_0_), channel_id=1, source_target_pairs={{0,16},{2,18},{4,20},{6,22},{8,24},{10,26},{12,28},{14,30},{16,0},... | collective-permute-start | bytes 344072 | tf_op jit(solution)/shard_map/ppermute | solution.py:775
  32.8 9.2 %collective-permute-start.10 = (f32[7,32,128]{2,1,0:T(8,128)S(1)}, f32[7,32,128]{2,1,0:T(8,128)S(1)}, u32[]{:S(2)}, u32[]{:S(2)}) collective-permute-start(f32[7,32,128]{2,1,0:T(8,128)S(1)} %merge.1.refs_0_), channel_id=1, source_target_pairs={{0,8},{2,10},{4,12},{6,14},{8,0},{10,2},{12,4},{14,6},{16,24},{18,... | collective-permute-start | bytes 344072 | tf_op jit(solution)/shard_map/ppermute | solution.py:775
  33.5 1.4 %collective-permute-start.13 = (f32[2,32,128]{2,1,0:T(8,128)S(1)}, f32[2,32,128]{2,1,0:T(8,128)S(1)}, u32[]{:S(2)}, u32[]{:S(2)}) collective-permute-start(f32[2,32,128]{2,1,0:T(8,128)S(1)} %get-tuple-element.64), channel_id=1, source_target_pairs={{4,8},{8,4},{6,10},{10,6},{12,16},{16,12},{14,18},{18,14},{20,24},... | collective-permute-start | bytes 98312 | tf_op jit(solution)/shard_map/ppermute | solution.py:785
  34.2 12.6 %collective-permute-start.19 = (f32[12,32,128]{2,1,0:T(8,128)S(1)}, f32[12,32,128]{2,1,0:T(8,128)S(1)}, u32[]{:S(2)}, u32[]{:S(2)}) collective-permute-start(f32[12,32,128]{2,1,0:T(8,128)S(1)} %get-tuple-element.72), channel_id=1, source_target_pairs={{2,4},{4,2},{6,8},{8,6},{10,12},{12,10},{14,16},{16,14},{18,20},{2... | collective-permute-start | bytes 589832 | tf_op jit(solution)/shard_map/ppermute | solution.py:785
  42.0 1.3 %collective-permute-start.14 = (f32[7,32,128]{2,1,0:T(8,128)S(1)}, f32[7,32,128]{2,1,0:T(8,128)S(1)}, u32[]{:S(2)}, u32[]{:S(2)}) collective-permute-start(f32[7,32,128]{2,1,0:T(8,128)S(1)} %merge.1.refs_0_), channel_id=1, source_target_pairs={{0,1},{1,0},{2,3},{3,2},{4,5},{5,4},{6,7},{7,6},{8,9},{9,8},{10,11... | collective-permute-start | bytes 344072 | tf_op jit(solution)/shard_map/ppermute | solution.py:749
  42.0 1.5 %collective-permute-start.15 = (f32[7,32,128]{2,1,0:T(8,128)S(1)}, f32[7,32,128]{2,1,0:T(8,128)S(1)}, u32[]{:S(2)}, u32[]{:S(2)}) collective-permute-start(f32[7,32,128]{2,1,0:T(8,128)S(1)} %collective-permute-done.10.refs_1_), channel_id=1, source_target_pairs={{0,1},{1,0},{2,3},{3,2},{4,5},{5,4},{6,7},{7,6},{8,9},{9,8},{10,11... | collective-permute-start | bytes 344072 | tf_op jit(solution)/shard_map/ppermute | solution.py:749
  42.5 1.3 %collective-permute-start.16 = (f32[7,32,128]{2,1,0:T(8,128)S(1)}, f32[7,32,128]{2,1,0:T(8,128)S(1)}, u32[]{:S(2)}, u32[]{:S(2)}) collective-permute-start(f32[7,32,128]{2,1,0:T(8,128)S(1)} %collective-permute-done.11.refs_2_), channel_id=1, source_target_pairs={{0,1},{1,0},{2,3},{3,2},{4,5},{5,4},{6,7},{7,6},{8,9},{9,8},{10,11... | collective-permute-start | bytes 344072 | tf_op jit(solution)/shard_map/ppermute | solution.py:749
  42.5 1.5 %collective-permute-start.17 = (f32[7,32,128]{2,1,0:T(8,128)S(1)}, f32[7,32,128]{2,1,0:T(8,128)S(1)}, u32[]{:S(2)}, u32[]{:S(2)}) collective-permute-start(f32[7,32,128]{2,1,0:T(8,128)S(1)} %collective-permute-done.12.refs_3_), channel_id=1, source_target_pairs={{0,1},{1,0},{2,3},{3,2},{4,5},{5,4},{6,7},{7,6},{8,9},{9,8},{10,11... | collective-permute-start | bytes 344072 | tf_op jit(solution)/shard_map/ppermute | solution.py:749

commit v18 on v17

--- a/solution.py
+++ b/solution.py
@@ -398,7 +398,7 @@
 
 
 def merge_kernel(sizes, stride, radix, place, *refs):
-    arrays, out, (source, conduct, binding) = refs[:radix], refs[radix], refs[radix + 1 :]
+    arrays, out, (source, conduct, binding) = refs[:radix][::-1], refs[radix], refs[radix + 1 :]
     merge_into(sizes, place, stride, radix, arrays, source, conduct, binding, 0)
     count = stride * radix
     rows = [source[row] for row in range(count + 2)]
@@ -860,7 +860,7 @@
             [(packing(3 * count + 2), *tile)],
             [(count + 2, *tile), (count, *tile), (count, *tile)],
             place,
-            blocks,
+            blocks[::-1],
         )
     stride, radix = plan[-1]
     blocks = swap(blocks, stride, radix)
@@ -871,7 +871,8 @@
         count = sizes.span_count >> index
         scratch += [(count + 1, *tile)] + [(count, *tile)] * 3 + [(count + 2, *tile)] + [(count, *tile)] * 2
         scratch += [(count + 2, *tile)] * 2
-    blocks, received[3] = lax.optimization_barrier((blocks, received[3]))
+    blocks, received[3] = lax.optimization_barrier((blocks[::-1], received[3]))
+    blocks = blocks[::-1]
     (coarse,) = call(
         functools.partial(coarse_kernel, sizes, stride, radix),
         "coarse",

time: 50.2 us -> 51 us (1.016)
  the two profiles are of different devices: /device:TPU:0 before, /device:TPU:13 now
where the time goes in v18:
time: 51 us; the launch traced here: 50.7 us
  starting transfers between devices  24.6 us (48%)
  Pallas kernels  12.6 us (25%)
  waiting for transfers between devices  11.3 us (22%)
  local copies, waits for them, and re-layouts  2.09 us (4%)
    pallas_call x7, Pallas kernels, call(): pl.pallas_call(body, name=name, out_shape=[jax.ShapeDtypeStruct(shape, f3...  12.6 us
    ppermute x5, starting transfers between devices, exchange(): lax.ppermute(value, 'span', route)  10.7 us
    ppermute x6, starting transfers between devices, beside(): lax.ppermute(value, 'width', [(0, 1), (1, 0)])  6.69 us
    ppermute x6, starting transfers between devices, swap(): lax.ppermute(others.get(step, value), 'span', [(device, device ^ step * s...  5.43 us
    ppermute x5, waiting for transfers between devices, exchange(): lax.ppermute(value, 'span', route)  5.05 us
    ppermute x6, waiting for transfers between devices, beside(): lax.ppermute(value, 'width', [(0, 1), (1, 0)])  2.68 us
    ppermute x6, waiting for transfers between devices, swap(): lax.ppermute(others.get(step, value), 'span', [(device, device ^ step * s...  2.56 us
    unnamed x6, local copies, waits for them, and re-layouts  2.09 us
  transfers between devices with their start and end apart: 20, of which 13 were waited for; matrix products, arithmetic and copies ran while one was open for 0% of the time, Pallas kernels for 12%

profile of v18, /device:TPU:13, one launch (start us, length us, event | category | flops | bytes accessed | tf_op | source)
XLA Modules:
  0.0 50.7 jit_solution(8358331838311022347)
XLA Ops:
  0.1 1.0 %copy-done = f32[32,8,512]{2,1,0:T(8,128)S(1)} copy-done((f32[32,8,512]{2,1,0:T(8,128)S(1)}, f32[32,8,512]{2,1,0:T(8,128)}, u32[]{:S(2)}) %copy-start) | copy-done | bytes 524312
  1.1 1.0 %copy-done.1 = f32[32,8,512]{2,1,0:T(8,128)S(1)} copy-done((f32[32,8,512]{2,1,0:T(8,128)S(1)}, f32[32,8,512]{2,1,0:T(8,128)}, u32[]{:S(2)}) %copy-start.1) | copy-done | bytes 524312
  2.2 1.1 %start.1 = (f32[2,8,32,512]{3,2,1,0:T(8,128)S(1)}, f32[8,32,256]{2,1,0:T(8,128)S(1)}, f32[4,32,128]{2,1,0:T(8,128)S(1)}, f32[12,32,128]{2,1,0:T(8,128)S(1)}, f32...) custom-call(s32[2]{0:T(128)S(1)} %pad_add_fusion.place, f32[32,8,512]{2,1,0:T(8,128)S(1)} %copy-done, ...), custom_call_target="tpu_custom_call" | custom-call | flops 1264999936 | bytes 4059000 | tf_op jit(solution)/shard_map/start/pallas_call | solution.py:729
  3.3 1.3 %collective-permute-start.3 = (f32[12,32,128]{2,1,0:T(8,128)S(1)}, f32[12,32,128]{2,1,0:T(8,128)S(1)}, u32[]{:S(2)}, u32[]{:S(2)}) collective-permute-start(f32[12,32,128]{2,1,0:T(8,128)S(1)} %get-tuple-element.48), channel_id=1, source_target_pairs={{0,2},{2,0},{4,6},{6,4},{8,10},{10,8},{12,14},{14,12},{16,18},{18,... | collective-permute-start | bytes 589832 | tf_op jit(solution)/shard_map/ppermute | solution.py:785
  4.6 2.1 %collective-permute-start.4 = (f32[12,32,128]{2,1,0:T(8,128)S(1)}, f32[12,32,128]{2,1,0:T(8,128)S(1)}, u32[]{:S(2)}, u32[]{:S(2)}) collective-permute-start(f32[12,32,128]{2,1,0:T(8,128)S(1)} %get-tuple-element.49), channel_id=1, source_target_pairs={{2,4},{4,2},{6,8},{8,6},{10,12},{12,10},{14,16},{16,14},{18,20},{2... | collective-permute-start | bytes 589832 | tf_op jit(solution)/shard_map/ppermute | solution.py:785
  6.7 0.7 %turn.1 = (f32[8,32,512]{2,1,0:T(8,128)S(1)}, f32[8,32,128]{2,1,0:T(8,128)S(1)}) custom-call(s32[2]{0:T(128)S(1)} %pad_add_fusion.place, f32[32,8,512]{2,1,0:T(8,128)S(1)} %copy-done.2), custom_call_target="tpu_custom_call" | custom-call | flops 805000000 | bytes 2583000 | tf_op jit(solution)/shard_map/turn/pallas_call | solution.py:729
  7.4 1.3 %collective-permute-start.2 = (f32[8,32,128]{2,1,0:T(8,128)S(1)}, f32[8,32,128]{2,1,0:T(8,128)S(1)}, u32[]{:S(2)}, u32[]{:S(2)}) collective-permute-start(f32[8,32,128]{2,1,0:T(8,128)S(1)} %get-tuple-element.47), channel_id=1, source_target_pairs={{0,1},{1,0},{2,3},{3,2},{4,5},{5,4},{6,7},{7,6},{8,9},{9,8},{10,11... | collective-permute-start | bytes 393224 | tf_op jit(solution)/shard_map/ppermute | solution.py:757
  10.2 1.8 %inner.1 = (f32[8,32,128]{2,1,0:T(8,128)S(1)}, f32[4,32,128]{2,1,0:T(8,128)S(1)}, f32[35,32,640]{2,1,0:T(8,128)S(1)}, f32[17,32,384]{2,1,0:T(8,128)S(1)}, f32[5,32,256]{2,1,0:T(8,128)S(1)}) custom-call(s32[2]{0:T(128)S(1)} %pad_add_fusion.place, f32[2,8,32,512]{3,2,1,0:T(8,128)S(1)} %get-tuple-element.41.refs_0_.refs_10_, ...), custom_call_target="tpu_custom_call" | custom-call | flops 575000000 | bytes 1845000 | tf_op jit(solution)/shard_map/inner/pallas_call | solution.py:729
  12.0 1.1 %collective-permute-done.4.refs_8_ = f32[12,32,128]{2,1,0:T(8,128)S(1)} collective-permute-done((f32[12,32,128]{2,1,0:T(8,128)S(1)}, f32[12,32,128]{2,1,0:T(8,128)S(1)}, u32[]{:S(2)}, u32[]{:S(2)}) %collective-permute-start.4) | collective-permute-done | bytes 196640 | tf_op jit(solution)/shard_map/ppermute | solution.py:785
  13.2 1.8 %collective-permute-start.5 = (f32[12,32,128]{2,1,0:T(8,128)S(1)}, f32[12,32,128]{2,1,0:T(8,128)S(1)}, u32[]{:S(2)}, u32[]{:S(2)}) collective-permute-start(f32[12,32,128]{2,1,0:T(8,128)S(1)} %collective-permute-done.3.refs_7_), channel_id=1, source_target_pairs={{0,1},{1,0},{2,3},{3,2},{4,5},{5,4},{6,7},{7,6},{8,9},{9,8},{10,11... | collective-permute-start | bytes 589832 | tf_op jit(solution)/shard_map/ppermute | solution.py:749
  14.9 1.1 %collective-permute-done.5.refs_9_ = f32[12,32,128]{2,1,0:T(8,128)S(1)} collective-permute-done((f32[12,32,128]{2,1,0:T(8,128)S(1)}, f32[12,32,128]{2,1,0:T(8,128)S(1)}, u32[]{:S(2)}, u32[]{:S(2)}) %collective-permute-start.5) | collective-permute-done | bytes 196640 | tf_op jit(solution)/shard_map/ppermute | solution.py:749
  16.4 2.3 %down.1 = (f32[6,32,640]{2,1,0:T(8,128)S(1)}, f32[26,32,384]{2,1,0:T(8,128)S(1)}, f32[24,32,256]{2,1,0:T(8,128)S(1)}, f32[3,32,128]{2,1,0:T(8,128)S(1)}, f32[5,3...) custom-call(s32[2]{0:T(128)S(1)} %pad_add_fusion.place, ...), custom_call_target="tpu_custom_call" | custom-call | flops 2875000064 | bytes 9225000 | tf_op jit(solution)/shard_map/down/pallas_call | solution.py:729
  18.7 1.1 %collective-permute-start.8 = (f32[5,32,128]{2,1,0:T(8,128)S(1)}, f32[5,32,128]{2,1,0:T(8,128)S(1)}, u32[]{:S(2)}, u32[]{:S(2)}) collective-permute-start(f32[5,32,128]{2,1,0:T(8,128)S(1)} %get-tuple-element.63), channel_id=1, source_target_pairs={{0,4},{2,6},{4,0},{6,2},{8,12},{10,14},{12,8},{14,10},{16,20},{18,... | collective-permute-start | bytes 245768 | tf_op jit(solution)/shard_map/ppermute | solution.py:775
  19.7 1.4 %collective-permute-start.9 = (f32[3,32,128]{2,1,0:T(8,128)S(1)}, f32[3,32,128]{2,1,0:T(8,128)S(1)}, u32[]{:S(2)}, u32[]{:S(2)}) collective-permute-start(f32[3,32,128]{2,1,0:T(8,128)S(1)} %get-tuple-element.62.refs_3_), channel_id=1, source_target_pairs={{0,2},{2,0},{4,6},{6,4},{8,10},{10,8},{12,14},{14,12},{16,18},{18,... | collective-permute-start | bytes 147464 | tf_op jit(solution)/shard_map/ppermute | solution.py:775
  21.4 1.0 %collective-permute-start.18 = (f32[12,32,128]{2,1,0:T(8,128)S(1)}, f32[12,32,128]{2,1,0:T(8,128)S(1)}, u32[]{:S(2)}, u32[]{:S(2)}) collective-permute-start(f32[12,32,128]{2,1,0:T(8,128)S(1)} %get-tuple-element.69), channel_id=1, source_target_pairs={{0,2},{2,0},{4,6},{6,4},{8,10},{10,8},{12,14},{14,12},{16,18},{18,... | collective-permute-start | bytes 589832 | tf_op jit(solution)/shard_map/ppermute | solution.py:785
  23.0 2.0 %collective-permute-done.7.refs_0_ = f32[3,32,128]{2,1,0:T(8,128)S(1)} collective-permute-done((f32[3,32,128]{2,1,0:T(8,128)S(1)}, f32[3,32,128]{2,1,0:T(8,128)S(1)}, u32[]{:S(2)}, u32[]{:S(2)}) %collective-permute-start.7) | collective-permute-done | bytes 49184 | tf_op jit(solution)/shard_map/ppermute | solution.py:775
  25.0 0.7 %merge.1.refs_0_ = f32[7,32,128]{2,1,0:T(8,128)S(1)} custom-call(s32[2]{0:T(128)S(1)} %pad_add_fusion.place, f32[3,32,128]{2,1,0:T(8,128)S(1)} %collective-permute-done.7.refs_0_, f32[5,32,128]{2,1,0:T(8,128)S(1)} %collective-permute-done.8.refs_1_.refs_2_, f32[3,32,128]{2,1,0:T(8,128)S(1)} %collective-permute-done.9.refs_2_, ...), custom_call_target="tpu_custom_call" | custom-call | flops 1035000000 | bytes 3321000 | tf_op jit(solution)/shard_map/merge/pallas_call | solution.py:729
  25.9 2.3 %collective-permute-start.11 = (f32[7,32,128]{2,1,0:T(8,128)S(1)}, f32[7,32,128]{2,1,0:T(8,128)S(1)}, u32[]{:S(2)}, u32[]{:S(2)}) collective-permute-start(f32[7,32,128]{2,1,0:T(8,128)S(1)} %merge.1.refs_0_), channel_id=1, source_target_pairs={{0,16},{2,18},{4,20},{6,22},{8,24},{10,26},{12,28},{14,30},{16,0},... | collective-permute-start | bytes 344072 | tf_op jit(solution)/shard_map/ppermute | solution.py:775
  28.4 3.4 %collective-permute-start.13 = (f32[2,32,128]{2,1,0:T(8,128)S(1)}, f32[2,32,128]{2,1,0:T(8,128)S(1)}, u32[]{:S(2)}, u32[]{:S(2)}) collective-permute-start(f32[2,32,128]{2,1,0:T(8,128)S(1)} %get-tuple-element.64), channel_id=1, source_target_pairs={{4,8},{8,4},{6,10},{10,6},{12,16},{16,12},{14,18},{18,14},{20,24},... | collective-permute-start | bytes 98312 | tf_op jit(solution)/shard_map/ppermute | solution.py:785
  31.8 2.9 %collective-permute-start.19 = (f32[12,32,128]{2,1,0:T(8,128)S(1)}, f32[12,32,128]{2,1,0:T(8,128)S(1)}, u32[]{:S(2)}, u32[]{:S(2)}) collective-permute-start(f32[12,32,128]{2,1,0:T(8,128)S(1)} %get-tuple-element.72), channel_id=1, source_target_pairs={{2,4},{4,2},{6,8},{8,6},{10,12},{12,10},{14,16},{16,14},{18,20},{2... | collective-permute-start | bytes 589832 | tf_op jit(solution)/shard_map/ppermute | solution.py:785
  34.7 3.9 %collective-permute-done.13.refs_3_ = f32[2,32,128]{2,1,0:T(8,128)S(1)} collective-permute-done((f32[2,32,128]{2,1,0:T(8,128)S(1)}, f32[2,32,128]{2,1,0:T(8,128)S(1)}, u32[]{:S(2)}, u32[]{:S(2)}) %collective-permute-start.13) | collective-permute-done | bytes 32800 | tf_op jit(solution)/shard_map/ppermute | solution.py:785
  38.6 4.3 %collective-permute-start.14 = (f32[7,32,128]{2,1,0:T(8,128)S(1)}, f32[7,32,128]{2,1,0:T(8,128)S(1)}, u32[]{:S(2)}, u32[]{:S(2)}) collective-permute-start(f32[7,32,128]{2,1,0:T(8,128)S(1)} %merge.1.refs_0_), channel_id=1, source_target_pairs={{0,1},{1,0},{2,3},{3,2},{4,5},{5,4},{6,7},{7,6},{8,9},{9,8},{10,11... | collective-permute-start | bytes 344072 | tf_op jit(solution)/shard_map/ppermute | solution.py:749
  44.8 2.8 %coarse.1 = f32[3,32,128]{2,1,0:T(8,128)S(1)} custom-call(s32[2]{0:T(128)S(1)} %pad_add_fusion.place, f32[7,32,128]{2,1,0:T(8,128)S(1)} %merge.1.refs_0_, f32[7,32,128]{2,1,0:T(8,128)S(1)} %collective-permute-done.12.refs_1_, f32[7,32,128]{2,1,0:T(8,128)S(1)} %collective-permute-done.11.refs_2_, f32[7,32,128]{2,1,0:T(8,128)S(1)} %collective-permute-done.10.refs_3_, ...), custom_call_target="tpu_custom_call" | custom-call | flops 805000000 | bytes 2583000 | tf_op jit(solution)/shard_map/coarse/pallas_call | solution.py:729
  47.6 3.1 %up.1 = f32[32,8,512]{2,1,0:T(8,128)} custom-call(s32[2]{0:T(128)S(1)} %pad_add_fusion.place, f32[3,32,128]{2,1,0:T(8,128)S(1)} %coarse.1, f32[12,32,128]{2,1,0:T(8,128)S(1)} %collective-permute-done.18.refs_0_, f32[12,32,128]{2,1,0:T(8,128)S(1)} %collective-permute-done.19.refs_1_, f32[5,32,128]{2,1,0:T(8,128)S(1)} %collective-permute-done.8.refs_1_.refs_2_, ...), custom_call_target="tpu_custom_call" | custom-call | flops 3449999872 | bytes 11070000 | tf_op jit(solution)/shard_map/up/pallas_call | solution.py:729
  (30 shorter events, 5.1 us)
Async XLA Ops:
  0.1 1.0 %copy-start = (f32[32,8,512]{2,1,0:T(8,128)S(1)}, f32[32,8,512]{2,1,0:T(8,128)}, u32[]{:S(2)}) copy-start(f32[32,8,512]{2,1,0:T(8,128)} %conduct.1) | copy-start | bytes 1572868
  1.1 1.0 %copy-start.1 = (f32[32,8,512]{2,1,0:T(8,128)S(1)}, f32[32,8,512]{2,1,0:T(8,128)}, u32[]{:S(2)}) copy-start(f32[32,8,512]{2,1,0:T(8,128)} %binding.1) | copy-start | bytes 1572868
  2.2 4.5 %copy-start.2 = (f32[32,8,512]{2,1,0:T(8,128)S(1)}, f32[32,8,512]{2,1,0:T(8,128)}, u32[]{:S(2)}) copy-start(f32[32,8,512]{2,1,0:T(8,128)} %right_side.1) | copy-start | bytes 1572868
  3.3 8.7 %collective-permute-start.3 = (f32[12,32,128]{2,1,0:T(8,128)S(1)}, f32[12,32,128]{2,1,0:T(8,128)S(1)}, u32[]{:S(2)}, u32[]{:S(2)}) collective-permute-start(f32[12,32,128]{2,1,0:T(8,128)S(1)} %get-tuple-element.48), channel_id=1, source_target_pairs={{0,2},{2,0},{4,6},{6,4},{8,10},{10,8},{12,14},{14,12},{16,18},{18,... | collective-permute-start | bytes 589832 | tf_op jit(solution)/shard_map/ppermute | solution.py:785
  4.6 8.6 %collective-permute-start.4 = (f32[12,32,128]{2,1,0:T(8,128)S(1)}, f32[12,32,128]{2,1,0:T(8,128)S(1)}, u32[]{:S(2)}, u32[]{:S(2)}) collective-permute-start(f32[12,32,128]{2,1,0:T(8,128)S(1)} %get-tuple-element.49), channel_id=1, source_target_pairs={{2,4},{4,2},{6,8},{8,6},{10,12},{12,10},{14,16},{16,14},{18,20},{2... | collective-permute-start | bytes 589832 | tf_op jit(solution)/shard_map/ppermute | solution.py:785
  7.4 2.3 %collective-permute-start.2 = (f32[8,32,128]{2,1,0:T(8,128)S(1)}, f32[8,32,128]{2,1,0:T(8,128)S(1)}, u32[]{:S(2)}, u32[]{:S(2)}) collective-permute-start(f32[8,32,128]{2,1,0:T(8,128)S(1)} %get-tuple-element.47), channel_id=1, source_target_pairs={{0,1},{1,0},{2,3},{3,2},{4,5},{5,4},{6,7},{7,6},{8,9},{9,8},{10,11... | collective-permute-start | bytes 393224 | tf_op jit(solution)/shard_map/ppermute | solution.py:757
  8.7 1.3 %collective-permute-start = (f32[8,32,128]{2,1,0:T(8,128)S(1)}, f32[8,32,128]{2,1,0:T(8,128)S(1)}, u32[]{:S(2)}, u32[]{:S(2)}) collective-permute-start(f32[8,32,128]{2,1,0:T(8,128)S(1)} %get-tuple-element.45), channel_id=1, source_target_pairs={{0,1},{1,0},{2,3},{3,2},{4,5},{5,4},{6,7},{7,6},{8,9},{9,8},{10,11... | collective-permute-start | bytes 393224 | tf_op jit(solution)/shard_map/ppermute | solution.py:757
  8.8 1.5 %collective-permute-start.1 = (f32[8,32,128]{2,1,0:T(8,128)S(1)}, f32[8,32,128]{2,1,0:T(8,128)S(1)}, u32[]{:S(2)}, u32[]{:S(2)}) collective-permute-start(f32[8,32,128]{2,1,0:T(8,128)S(1)} %get-tuple-element.46), channel_id=1, source_target_pairs={{0,1},{1,0},{2,3},{3,2},{4,5},{5,4},{6,7},{7,6},{8,9},{9,8},{10,11... | collective-permute-start | bytes 393224 | tf_op jit(solution)/shard_map/ppermute | solution.py:757
  13.2 2.8 %collective-permute-start.5 = (f32[12,32,128]{2,1,0:T(8,128)S(1)}, f32[12,32,128]{2,1,0:T(8,128)S(1)}, u32[]{:S(2)}, u32[]{:S(2)}) collective-permute-start(f32[12,32,128]{2,1,0:T(8,128)S(1)} %collective-permute-done.3.refs_7_), channel_id=1, source_target_pairs={{0,1},{1,0},{2,3},{3,2},{4,5},{5,4},{6,7},{7,6},{8,9},{9,8},{10,11... | collective-permute-start | bytes 589832 | tf_op jit(solution)/shard_map/ppermute | solution.py:749
  14.9 1.4 %collective-permute-start.6 = (f32[12,32,128]{2,1,0:T(8,128)S(1)}, f32[12,32,128]{2,1,0:T(8,128)S(1)}, u32[]{:S(2)}, u32[]{:S(2)}) collective-permute-start(f32[12,32,128]{2,1,0:T(8,128)S(1)} %collective-permute-done.4.refs_8_), channel_id=1, source_target_pairs={{0,1},{1,0},{2,3},{3,2},{4,5},{5,4},{6,7},{7,6},{8,9},{9,8},{10,11... | collective-permute-start | bytes 589832 | tf_op jit(solution)/shard_map/ppermute | solution.py:749
  18.7 6.3 %collective-permute-start.8 = (f32[5,32,128]{2,1,0:T(8,128)S(1)}, f32[5,32,128]{2,1,0:T(8,128)S(1)}, u32[]{:S(2)}, u32[]{:S(2)}) collective-permute-start(f32[5,32,128]{2,1,0:T(8,128)S(1)} %get-tuple-element.63), channel_id=1, source_target_pairs={{0,4},{2,6},{4,0},{6,2},{8,12},{10,14},{12,8},{14,10},{16,20},{18,... | collective-permute-start | bytes 245768 | tf_op jit(solution)/shard_map/ppermute | solution.py:775
  19.7 3.2 %collective-permute-start.9 = (f32[3,32,128]{2,1,0:T(8,128)S(1)}, f32[3,32,128]{2,1,0:T(8,128)S(1)}, u32[]{:S(2)}, u32[]{:S(2)}) collective-permute-start(f32[3,32,128]{2,1,0:T(8,128)S(1)} %get-tuple-element.62.refs_3_), channel_id=1, source_target_pairs={{0,2},{2,0},{4,6},{6,4},{8,10},{10,8},{12,14},{14,12},{16,18},{18,... | collective-permute-start | bytes 147464 | tf_op jit(solution)/shard_map/ppermute | solution.py:775
  21.1 3.8 %collective-permute-start.7 = (f32[3,32,128]{2,1,0:T(8,128)S(1)}, f32[3,32,128]{2,1,0:T(8,128)S(1)}, u32[]{:S(2)}, u32[]{:S(2)}) collective-permute-start(f32[3,32,128]{2,1,0:T(8,128)S(1)} %get-tuple-element.62.refs_3_), channel_id=1, source_target_pairs={{0,6},{2,4},{4,2},{6,0},{8,14},{10,12},{12,10},{14,8},{16,22},{18,... | collective-permute-start | bytes 147464 | tf_op jit(solution)/shard_map/ppermute | solution.py:775
  21.4 10.4 %collective-permute-start.18 = (f32[12,32,128]{2,1,0:T(8,128)S(1)}, f32[12,32,128]{2,1,0:T(8,128)S(1)}, u32[]{:S(2)}, u32[]{:S(2)}) collective-permute-start(f32[12,32,128]{2,1,0:T(8,128)S(1)} %get-tuple-element.69), channel_id=1, source_target_pairs={{0,2},{2,0},{4,6},{6,4},{8,10},{10,8},{12,14},{14,12},{16,18},{18,... | collective-permute-start | bytes 589832 | tf_op jit(solution)/shard_map/ppermute | solution.py:785
  25.7 12.9 %collective-permute-start.12 = (f32[7,32,128]{2,1,0:T(8,128)S(1)}, f32[7,32,128]{2,1,0:T(8,128)S(1)}, u32[]{:S(2)}, u32[]{:S(2)}) collective-permute-start(f32[7,32,128]{2,1,0:T(8,128)S(1)} %merge.1.refs_0_), channel_id=1, source_target_pairs={{0,8},{2,10},{4,12},{6,14},{8,0},{10,2},{12,4},{14,6},{16,24},{18,... | collective-permute-start | bytes 344072 | tf_op jit(solution)/shard_map/ppermute | solution.py:775
  25.9 12.7 %collective-permute-start.11 = (f32[7,32,128]{2,1,0:T(8,128)S(1)}, f32[7,32,128]{2,1,0:T(8,128)S(1)}, u32[]{:S(2)}, u32[]{:S(2)}) collective-permute-start(f32[7,32,128]{2,1,0:T(8,128)S(1)} %merge.1.refs_0_), channel_id=1, source_target_pairs={{0,16},{2,18},{4,20},{6,22},{8,24},{10,26},{12,28},{14,30},{16,0},... | collective-permute-start | bytes 344072 | tf_op jit(solution)/shard_map/ppermute | solution.py:775
  28.3 10.4 %collective-permute-start.10 = (f32[7,32,128]{2,1,0:T(8,128)S(1)}, f32[7,32,128]{2,1,0:T(8,128)S(1)}, u32[]{:S(2)}, u32[]{:S(2)}) collective-permute-start(f32[7,32,128]{2,1,0:T(8,128)S(1)} %merge.1.refs_0_), channel_id=1, source_target_pairs={{0,24},{2,26},{4,28},{6,30},{8,16},{10,18},{12,20},{14,22},{16,8},... | collective-permute-start | bytes 344072 | tf_op jit(solution)/shard_map/ppermute | solution.py:775
  28.4 10.2 %collective-permute-start.13 = (f32[2,32,128]{2,1,0:T(8,128)S(1)}, f32[2,32,128]{2,1,0:T(8,128)S(1)}, u32[]{:S(2)}, u32[]{:S(2)}) collective-permute-start(f32[2,32,128]{2,1,0:T(8,128)S(1)} %get-tuple-element.64), channel_id=1, source_target_pairs={{4,8},{8,4},{6,10},{10,6},{12,16},{16,12},{14,18},{18,14},{20,24},... | collective-permute-start | bytes 98312 | tf_op jit(solution)/shard_map/ppermute | solution.py:785
  31.8 15.8 %collective-permute-start.19 = (f32[12,32,128]{2,1,0:T(8,128)S(1)}, f32[12,32,128]{2,1,0:T(8,128)S(1)}, u32[]{:S(2)}, u32[]{:S(2)}) collective-permute-start(f32[12,32,128]{2,1,0:T(8,128)S(1)} %get-tuple-element.72), channel_id=1, source_target_pairs={{2,4},{4,2},{6,8},{8,6},{10,12},{12,10},{14,16},{16,14},{18,20},{2... | collective-permute-start | bytes 589832 | tf_op jit(solution)/shard_map/ppermute | solution.py:785
  38.6 5.3 %collective-permute-start.14 = (f32[7,32,128]{2,1,0:T(8,128)S(1)}, f32[7,32,128]{2,1,0:T(8,128)S(1)}, u32[]{:S(2)}, u32[]{:S(2)}) collective-permute-start(f32[7,32,128]{2,1,0:T(8,128)S(1)} %merge.1.refs_0_), channel_id=1, source_target_pairs={{0,1},{1,0},{2,3},{3,2},{4,5},{5,4},{6,7},{7,6},{8,9},{9,8},{10,11... | collective-permute-start | bytes 344072 | tf_op jit(solution)/shard_map/ppermute | solution.py:749
  43.0 1.3 %collective-permute-start.15 = (f32[7,32,128]{2,1,0:T(8,128)S(1)}, f32[7,32,128]{2,1,0:T(8,128)S(1)}, u32[]{:S(2)}, u32[]{:S(2)}) collective-permute-start(f32[7,32,128]{2,1,0:T(8,128)S(1)} %collective-permute-done.12.refs_1_), channel_id=1, source_target_pairs={{0,1},{1,0},{2,3},{3,2},{4,5},{5,4},{6,7},{7,6},{8,9},{9,8},{10,11... | collective-permute-start | bytes 344072 | tf_op jit(solution)/shard_map/ppermute | solution.py:749
  43.1 1.4 %collective-permute-start.16 = (f32[7,32,128]{2,1,0:T(8,128)S(1)}, f32[7,32,128]{2,1,0:T(8,128)S(1)}, u32[]{:S(2)}, u32[]{:S(2)}) collective-permute-start(f32[7,32,128]{2,1,0:T(8,128)S(1)} %collective-permute-done.11.refs_2_), channel_id=1, source_target_pairs={{0,1},{1,0},{2,3},{3,2},{4,5},{5,4},{6,7},{7,6},{8,9},{9,8},{10,11... | collective-permute-start | bytes 344072 | tf_op jit(solution)/shard_map/ppermute | solution.py:749
  43.5 1.3 %collective-permute-start.17 = (f32[7,32,128]{2,1,0:T(8,128)S(1)}, f32[7,32,128]{2,1,0:T(8,128)S(1)}, u32[]{:S(2)}, u32[]{:S(2)}) collective-permute-start(f32[7,32,128]{2,1,0:T(8,128)S(1)} %collective-permute-done.10.refs_3_), channel_id=1, source_target_pairs={{0,1},{1,0},{2,3},{3,2},{4,5},{5,4},{6,7},{7,6},{8,9},{9,8},{10,11... | collective-permute-start | bytes 344072 | tf_op jit(solution)/shard_map/ppermute | solution.py:749

commit v19 on v17

--- a/solution.py
+++ b/solution.py
@@ -231,14 +231,17 @@
         weight[row - 1] = relax_weight * reciprocal(diagonal)
 
 
-def sweep(first, last, field, binding, fx, fy, fz, emit):
-    lower = fx[first - 1] * (field(first) - field(first - 1))
+def sweep(first, last, field, binding, fx, fy, fz, emit, width=None):
+    cut = lambda value: value if width is None else value[:, :width]
+    lower = cut(fx[first - 1]) * (cut(field(first)) - cut(field(first - 1)))
     for row in range(first, last + 1):
         mine = field(row)
-        upper = fx[row] * (field(row + 1) - mine)
         south = fy[row - 1] * (mine - roll(mine, 1, 1))
-        below = fz[row - 1] * (mine - roll(mine, 1, 0))
-        across = (south - roll(south, -1, 1)) + (below - roll(below, -1, 0))
+        across = cut(south - roll(south, -1, 1))
+        mine = cut(mine)
+        upper = cut(fx[row]) * (cut(field(row + 1)) - mine)
+        below = cut(fz[row - 1]) * (mine - roll(mine, 1, 0))
+        across = across + (below - roll(below, -1, 0))
         emit(row, binding(row) * mine + (lower - upper) + across)
         lower = upper
 
@@ -636,13 +639,24 @@
         widen(sizes, place, 3 + index, held.at[1 : count // 2 + 1], sums, count // 2)
         for row in range(count):
             smooth[row + 1] = smooth[row + 1] + sums[row // 2, :, :LANES]
+        if index == 0:
+            break
         field = lambda row, smooth=smooth: smooth[row]
         mine = lambda row, source=source: source[row - 1]
         bound = lambda row, binding=binding: binding[row - 1]
         relax(count + 2, field, (fx, fy, fz, weight, bound), mine, store(iterate, 0))
         held = iterate
 
-    out[...] = held[pl.ds(place[0], 3)]
+    for at in range(3):
+        row = jnp.clip(place[0] + at, 1, total)
+        mine = smooth[row]
+        lower, upper = fx[row - 1] * (mine - smooth[row - 1]), fx[row] * (smooth[row + 1] - mine)
+        south = fy[row - 1] * (mine - roll(mine, 1, 1))
+        below = fz[row - 1] * (mine - roll(mine, 1, 0))
+        across = (south - roll(south, -1, 1)) + (below - roll(below, -1, 0))
+        value = binding[row - 1] * mine + (lower - upper) + across
+        value = mine + weight[row - 1] * (source[row - 1] - value)
+        out[at] = jnp.where(row == place[0] + at, value, 0.0)
 
 
 def up_kernel(sizes, place, coarse, *refs):
@@ -701,15 +715,17 @@
         relax(n + 4, field, (fx, fy, fz, weight, bound), mine, store(target, 1))
         widen(sizes, place, level - 1, target, upper, n + 2)
 
-    held_row = held_rows(sizes, [owns[0], None, None, owns[1]], [borders0])
     fx, fy, fz, weight, v0 = levels[0].fx, levels[0].fy, levels[0].fz, levels[0].weight, levels[0].smooth
     lift0[0] = lift0[0] + over0[0]
     lift0[n0 + 1] = lift0[n0 + 1] + over0[n1 + 1]
     for row in range(1, n0 + 1):
         lift0[row] = v0[row - 1] + over0[(row + 1) // 2]
     field = lambda row: lift0[row]
-    bound = lambda row: held_row(0, 1, row - 1)
-    relax(n0 + 2, field, (fx, fy, fz, weight, bound), lambda row: held_row(0, 2, row - 1), store(it0, 1))
+
+    def relax_own(row, value):
+        it0[row - 1] = lift0[row, :, :width] + weight[row - 1][:, :width] * (owns[1][row - 1] - value)
+
+    sweep(1, n0, field, lambda row: owns[0][1, row - 1], fx, fy, fz, relax_own, width)
     step = sizes.depth // CHUNKS
     copies = []
     for chunk in range(CHUNKS):
@@ -884,7 +900,7 @@
     scratch = [(n1 + 2, *held[1]), (n2 + 2, *held[2]), diffusivity.shape, (2, *held[0]), (2, *held[1])]
     scratch += [(n3 + 2, *held[2]), (n2 + 2, *held[1]), (n1 + 2, *held[0])]
     scratch += [(n2 + 4, *held[2]), (n1 + 4, *held[1]), (n0 + 2, *held[0])]
-    scratch += [(n2 + 2, *held[2]), (n1 + 2, *held[1]), (n0, *held[0])]
+    scratch += [(n2 + 2, *held[2]), (n1 + 2, *held[1]), (n0, *own[0])]
     (correction,) = call(
         functools.partial(up_kernel, sizes),
         "up",

time: 50.2 us -> 50.1 us (level)
  no operation moved by 1% of the time
where the time goes in v19:
time: 50.1 us; the launch traced here: 49.9 us
  starting transfers between devices  21.9 us (44%)
  waiting for transfers between devices  13.2 us (26%)
  Pallas kernels  12.5 us (25%)
  local copies, waits for them, and re-layouts  2.09 us (4%)
    ppermute x6, starting transfers between devices, swap(): lax.ppermute(others.get(step, value), 'span', [(device, device ^ step * s...  12.6 us
    pallas_call x7, Pallas kernels, call(): pl.pallas_call(body, name=name, out_shape=[jax.ShapeDtypeStruct(shape, f3...  12.5 us
    ppermute x6, waiting for transfers between devices, swap(): lax.ppermute(others.get(step, value), 'span', [(device, device ^ step * s...  9.71 us
    ppermute x5, starting transfers between devices, exchange(): lax.ppermute(value, 'span', route)  7.01 us
    ppermute x6, waiting for transfers between devices, beside(): lax.ppermute(value, 'width', [(0, 1), (1, 0)])  2.19 us
    unnamed x6, local copies, waits for them, and re-layouts  2.09 us
    ppermute x6, starting transfers between devices, beside(): lax.ppermute(value, 'width', [(0, 1), (1, 0)])  1.6 us
    ppermute x3, waiting for transfers between devices, edge_columns(): return [lax.ppermute(edges[0], 'width', [(0, 1), (1, 0)])]  1.27 us
  transfers between devices with their start and end apart: 20, of which 13 were waited for; matrix products, arithmetic and copies ran while one was open for 0% of the time, Pallas kernels for 12%

profile of v19, /device:TPU:0, one launch (start us, length us, event | category | flops | bytes accessed | tf_op | source)
XLA Modules:
  0.0 49.9 jit_solution(8465924800170223106)
XLA Ops:
  0.1 1.0 %copy-done = f32[32,8,512]{2,1,0:T(8,128)S(1)} copy-done((f32[32,8,512]{2,1,0:T(8,128)S(1)}, f32[32,8,512]{2,1,0:T(8,128)}, u32[]{:S(2)}) %copy-start) | copy-done | bytes 524312
  1.1 1.0 %copy-done.1 = f32[32,8,512]{2,1,0:T(8,128)S(1)} copy-done((f32[32,8,512]{2,1,0:T(8,128)S(1)}, f32[32,8,512]{2,1,0:T(8,128)}, u32[]{:S(2)}) %copy-start.1) | copy-done | bytes 524312
  2.2 1.1 %start.1 = (f32[2,8,32,512]{3,2,1,0:T(8,128)S(1)}, f32[8,32,256]{2,1,0:T(8,128)S(1)}, f32[4,32,128]{2,1,0:T(8,128)S(1)}, f32[12,32,128]{2,1,0:T(8,128)S(1)}, f32...) custom-call(s32[2]{0:T(128)S(1)} %pad_add_fusion.place, f32[32,8,512]{2,1,0:T(8,128)S(1)} %copy-done, ...), custom_call_target="tpu_custom_call" | custom-call | flops 1264999936 | bytes 4059000 | tf_op jit(solution)/shard_map/start/pallas_call | solution.py:745
  3.3 3.0 %collective-permute-start.3 = (f32[12,32,128]{2,1,0:T(8,128)S(1)}, f32[12,32,128]{2,1,0:T(8,128)S(1)}, u32[]{:S(2)}, u32[]{:S(2)}) collective-permute-start(f32[12,32,128]{2,1,0:T(8,128)S(1)} %get-tuple-element.48), channel_id=1, source_target_pairs={{0,2},{2,0},{4,6},{6,4},{8,10},{10,8},{12,14},{14,12},{16,18},{18,... | collective-permute-start | bytes 589832 | tf_op jit(solution)/shard_map/ppermute | solution.py:801
  6.3 0.7 %collective-permute-start.4 = (f32[12,32,128]{2,1,0:T(8,128)S(1)}, f32[12,32,128]{2,1,0:T(8,128)S(1)}, u32[]{:S(2)}, u32[]{:S(2)}) collective-permute-start(f32[12,32,128]{2,1,0:T(8,128)S(1)} %get-tuple-element.49), channel_id=1, source_target_pairs={{2,4},{4,2},{6,8},{8,6},{10,12},{12,10},{14,16},{16,14},{18,20},{2... | collective-permute-start | bytes 589832 | tf_op jit(solution)/shard_map/ppermute | solution.py:801
  7.0 0.7 %turn.1 = (f32[8,32,512]{2,1,0:T(8,128)S(1)}, f32[8,32,128]{2,1,0:T(8,128)S(1)}) custom-call(s32[2]{0:T(128)S(1)} %pad_add_fusion.place, f32[32,8,512]{2,1,0:T(8,128)S(1)} %copy-done.2), custom_call_target="tpu_custom_call" | custom-call | flops 805000000 | bytes 2583000 | tf_op jit(solution)/shard_map/turn/pallas_call | solution.py:745
  8.3 0.8 %collective-permute-done.2.refs_6_.refs_14_ = f32[8,32,128]{2,1,0:T(8,128)S(1)} collective-permute-done((f32[8,32,128]{2,1,0:T(8,128)S(1)}, f32[8,32,128]{2,1,0:T(8,128)S(1)}, u32[]{:S(2)}, u32[]{:S(2)}) %collective-permute-start.2) | collective-permute-done | bytes 131104 | tf_op jit(solution)/shard_map/ppermute | solution.py:773
  9.6 1.8 %inner.1 = (f32[8,32,128]{2,1,0:T(8,128)S(1)}, f32[4,32,128]{2,1,0:T(8,128)S(1)}, f32[35,32,640]{2,1,0:T(8,128)S(1)}, f32[17,32,384]{2,1,0:T(8,128)S(1)}, f32[5,32,256]{2,1,0:T(8,128)S(1)}) custom-call(s32[2]{0:T(128)S(1)} %pad_add_fusion.place, f32[2,8,32,512]{3,2,1,0:T(8,128)S(1)} %get-tuple-element.41.refs_0_.refs_10_, ...), custom_call_target="tpu_custom_call" | custom-call | flops 575000000 | bytes 1845000 | tf_op jit(solution)/shard_map/inner/pallas_call | solution.py:745
  12.0 0.9 %collective-permute-done.5.refs_9_ = f32[12,32,128]{2,1,0:T(8,128)S(1)} collective-permute-done((f32[12,32,128]{2,1,0:T(8,128)S(1)}, f32[12,32,128]{2,1,0:T(8,128)S(1)}, u32[]{:S(2)}, u32[]{:S(2)}) %collective-permute-start.5) | collective-permute-done | bytes 196640 | tf_op jit(solution)/shard_map/ppermute | solution.py:765
  13.2 2.3 %down.1 = (f32[6,32,640]{2,1,0:T(8,128)S(1)}, f32[26,32,384]{2,1,0:T(8,128)S(1)}, f32[24,32,256]{2,1,0:T(8,128)S(1)}, f32[3,32,128]{2,1,0:T(8,128)S(1)}, f32[5,3...) custom-call(s32[2]{0:T(128)S(1)} %pad_add_fusion.place, ...), custom_call_target="tpu_custom_call" | custom-call | flops 2875000064 | bytes 9225000 | tf_op jit(solution)/shard_map/down/pallas_call | solution.py:745
  15.5 5.5 %collective-permute-start.8 = (f32[5,32,128]{2,1,0:T(8,128)S(1)}, f32[5,32,128]{2,1,0:T(8,128)S(1)}, u32[]{:S(2)}, u32[]{:S(2)}) collective-permute-start(f32[5,32,128]{2,1,0:T(8,128)S(1)} %get-tuple-element.63), channel_id=1, source_target_pairs={{0,4},{2,6},{4,0},{6,2},{8,12},{10,14},{12,8},{14,10},{16,20},{18,... | collective-permute-start | bytes 245768 | tf_op jit(solution)/shard_map/ppermute | solution.py:791
  21.1 2.6 %collective-permute-start.9 = (f32[3,32,128]{2,1,0:T(8,128)S(1)}, f32[3,32,128]{2,1,0:T(8,128)S(1)}, u32[]{:S(2)}, u32[]{:S(2)}) collective-permute-start(f32[3,32,128]{2,1,0:T(8,128)S(1)} %get-tuple-element.62.refs_0_), channel_id=1, source_target_pairs={{0,6},{2,4},{4,2},{6,0},{8,14},{10,12},{12,10},{14,8},{16,22},{18,... | collective-permute-start | bytes 147464 | tf_op jit(solution)/shard_map/ppermute | solution.py:791
  23.7 2.0 %collective-permute-start.18 = (f32[12,32,128]{2,1,0:T(8,128)S(1)}, f32[12,32,128]{2,1,0:T(8,128)S(1)}, u32[]{:S(2)}, u32[]{:S(2)}) collective-permute-start(f32[12,32,128]{2,1,0:T(8,128)S(1)} %get-tuple-element.69), channel_id=1, source_target_pairs={{0,2},{2,0},{4,6},{6,4},{8,10},{10,8},{12,14},{14,12},{16,18},{18,... | collective-permute-start | bytes 589832 | tf_op jit(solution)/shard_map/ppermute | solution.py:801
  25.7 0.6 %collective-permute-done.9.refs_3_ = f32[3,32,128]{2,1,0:T(8,128)S(1)} collective-permute-done((f32[3,32,128]{2,1,0:T(8,128)S(1)}, f32[3,32,128]{2,1,0:T(8,128)S(1)}, u32[]{:S(2)}, u32[]{:S(2)}) %collective-permute-start.9) | collective-permute-done | bytes 49184 | tf_op jit(solution)/shard_map/ppermute | solution.py:791
  26.4 2.0 %collective-permute-done.7.refs_1_ = f32[3,32,128]{2,1,0:T(8,128)S(1)} collective-permute-done((f32[3,32,128]{2,1,0:T(8,128)S(1)}, f32[3,32,128]{2,1,0:T(8,128)S(1)}, u32[]{:S(2)}, u32[]{:S(2)}) %collective-permute-start.7) | collective-permute-done | bytes 49184 | tf_op jit(solution)/shard_map/ppermute | solution.py:791
  28.3 0.7 %merge.1.refs_0_ = f32[7,32,128]{2,1,0:T(8,128)S(1)} custom-call(s32[2]{0:T(128)S(1)} %pad_add_fusion.place, f32[3,32,128]{2,1,0:T(8,128)S(1)} %get-tuple-element.62.refs_0_, f32[3,32,128]{2,1,0:T(8,128)S(1)} %collective-permute-done.7.refs_1_, f32[5,32,128]{2,1,0:T(8,128)S(1)} %collective-permute-done.8.refs_2_, ...), custom_call_target="tpu_custom_call" | custom-call | flops 1035000000 | bytes 3321000 | tf_op jit(solution)/shard_map/merge/pallas_call | solution.py:745
  29.1 3.7 %collective-permute-start.12 = (f32[7,32,128]{2,1,0:T(8,128)S(1)}, f32[7,32,128]{2,1,0:T(8,128)S(1)}, u32[]{:S(2)}, u32[]{:S(2)}) collective-permute-start(f32[7,32,128]{2,1,0:T(8,128)S(1)} %merge.1.refs_0_), channel_id=1, source_target_pairs={{0,24},{2,26},{4,28},{6,30},{8,16},{10,18},{12,20},{14,22},{16,8},... | collective-permute-start | bytes 344072 | tf_op jit(solution)/shard_map/ppermute | solution.py:791
  32.8 0.8 %collective-permute-start.10 = (f32[7,32,128]{2,1,0:T(8,128)S(1)}, f32[7,32,128]{2,1,0:T(8,128)S(1)}, u32[]{:S(2)}, u32[]{:S(2)}) collective-permute-start(f32[7,32,128]{2,1,0:T(8,128)S(1)} %merge.1.refs_0_), channel_id=1, source_target_pairs={{0,8},{2,10},{4,12},{6,14},{8,0},{10,2},{12,4},{14,6},{16,24},{18,... | collective-permute-start | bytes 344072 | tf_op jit(solution)/shard_map/ppermute | solution.py:791
  33.5 0.7 %collective-permute-start.13 = (f32[2,32,128]{2,1,0:T(8,128)S(1)}, f32[2,32,128]{2,1,0:T(8,128)S(1)}, u32[]{:S(2)}, u32[]{:S(2)}) collective-permute-start(f32[2,32,128]{2,1,0:T(8,128)S(1)} %get-tuple-element.64), channel_id=1, source_target_pairs={{4,8},{8,4},{6,10},{10,6},{12,16},{16,12},{14,18},{18,14},{20,24},... | collective-permute-start | bytes 98312 | tf_op jit(solution)/shard_map/ppermute | solution.py:801
  34.2 0.7 %collective-permute-start.19 = (f32[12,32,128]{2,1,0:T(8,128)S(1)}, f32[12,32,128]{2,1,0:T(8,128)S(1)}, u32[]{:S(2)}, u32[]{:S(2)}) collective-permute-start(f32[12,32,128]{2,1,0:T(8,128)S(1)} %get-tuple-element.72), channel_id=1, source_target_pairs={{2,4},{4,2},{6,8},{8,6},{10,12},{12,10},{14,16},{16,14},{18,20},{2... | collective-permute-start | bytes 589832 | tf_op jit(solution)/shard_map/ppermute | solution.py:801
  34.9 1.3 %collective-permute-done.12.refs_3_ = f32[7,32,128]{2,1,0:T(8,128)S(1)} collective-permute-done((f32[7,32,128]{2,1,0:T(8,128)S(1)}, f32[7,32,128]{2,1,0:T(8,128)S(1)}, u32[]{:S(2)}, u32[]{:S(2)}) %collective-permute-start.12) | collective-permute-done | bytes 114720 | tf_op jit(solution)/shard_map/ppermute | solution.py:791
  36.3 5.7 %collective-permute-done.11.refs_2_ = f32[7,32,128]{2,1,0:T(8,128)S(1)} collective-permute-done((f32[7,32,128]{2,1,0:T(8,128)S(1)}, f32[7,32,128]{2,1,0:T(8,128)S(1)}, u32[]{:S(2)}, u32[]{:S(2)}) %collective-permute-start.11) | collective-permute-done | bytes 114720 | tf_op jit(solution)/shard_map/ppermute | solution.py:791
  44.0 2.7 %coarse.1 = f32[3,32,128]{2,1,0:T(8,128)S(1)} custom-call(s32[2]{0:T(128)S(1)} %pad_add_fusion.place, f32[7,32,128]{2,1,0:T(8,128)S(1)} %merge.1.refs_0_, f32[7,32,128]{2,1,0:T(8,128)S(1)} %collective-permute-done.10.refs_1_, f32[7,32,128]{2,1,0:T(8,128)S(1)} %collective-permute-done.11.refs_2_, f32[7,32,128]{2,1,0:T(8,128)S(1)} %collective-permute-done.12.refs_3_, ...), custom_call_target="tpu_custom_call" | custom-call | flops 805000000 | bytes 2583000 | tf_op jit(solution)/shard_map/coarse/pallas_call | solution.py:745
  46.7 3.1 %up.1 = f32[32,8,512]{2,1,0:T(8,128)} custom-call(s32[2]{0:T(128)S(1)} %pad_add_fusion.place, f32[3,32,128]{2,1,0:T(8,128)S(1)} %coarse.1, f32[12,32,128]{2,1,0:T(8,128)S(1)} %collective-permute-done.18.refs_0_, f32[12,32,128]{2,1,0:T(8,128)S(1)} %collective-permute-done.19.refs_1_, f32[5,32,128]{2,1,0:T(8,128)S(1)} %collective-permute-done.8.refs_2_, ...), custom_call_target="tpu_custom_call" | custom-call | flops 3449999872 | bytes 11070000 | tf_op jit(solution)/shard_map/up/pallas_call | solution.py:745
  (30 shorter events, 4.1 us)
Async XLA Ops:
  0.1 1.0 %copy-start = (f32[32,8,512]{2,1,0:T(8,128)S(1)}, f32[32,8,512]{2,1,0:T(8,128)}, u32[]{:S(2)}) copy-start(f32[32,8,512]{2,1,0:T(8,128)} %conduct.1) | copy-start | bytes 1572868
  1.1 1.0 %copy-start.1 = (f32[32,8,512]{2,1,0:T(8,128)S(1)}, f32[32,8,512]{2,1,0:T(8,128)}, u32[]{:S(2)}) copy-start(f32[32,8,512]{2,1,0:T(8,128)} %binding.1) | copy-start | bytes 1572868
  2.2 4.8 %copy-start.2 = (f32[32,8,512]{2,1,0:T(8,128)S(1)}, f32[32,8,512]{2,1,0:T(8,128)}, u32[]{:S(2)}) copy-start(f32[32,8,512]{2,1,0:T(8,128)} %right_side.1) | copy-start | bytes 1572868
  3.3 8.1 %collective-permute-start.3 = (f32[12,32,128]{2,1,0:T(8,128)S(1)}, f32[12,32,128]{2,1,0:T(8,128)S(1)}, u32[]{:S(2)}, u32[]{:S(2)}) collective-permute-start(f32[12,32,128]{2,1,0:T(8,128)S(1)} %get-tuple-element.48), channel_id=1, source_target_pairs={{0,2},{2,0},{4,6},{6,4},{8,10},{10,8},{12,14},{14,12},{16,18},{18,... | collective-permute-start | bytes 589832 | tf_op jit(solution)/shard_map/ppermute | solution.py:801
  6.3 5.1 %collective-permute-start.4 = (f32[12,32,128]{2,1,0:T(8,128)S(1)}, f32[12,32,128]{2,1,0:T(8,128)S(1)}, u32[]{:S(2)}, u32[]{:S(2)}) collective-permute-start(f32[12,32,128]{2,1,0:T(8,128)S(1)} %get-tuple-element.49), channel_id=1, source_target_pairs={{2,4},{4,2},{6,8},{8,6},{10,12},{12,10},{14,16},{16,14},{18,20},{2... | collective-permute-start | bytes 589832 | tf_op jit(solution)/shard_map/ppermute | solution.py:801
  7.7 1.4 %collective-permute-start.2 = (f32[8,32,128]{2,1,0:T(8,128)S(1)}, f32[8,32,128]{2,1,0:T(8,128)S(1)}, u32[]{:S(2)}, u32[]{:S(2)}) collective-permute-start(f32[8,32,128]{2,1,0:T(8,128)S(1)} %get-tuple-element.47), channel_id=1, source_target_pairs={{0,1},{1,0},{2,3},{3,2},{4,5},{5,4},{6,7},{7,6},{8,9},{9,8},{10,11... | collective-permute-start | bytes 393224 | tf_op jit(solution)/shard_map/ppermute | solution.py:773
  7.7 1.5 %collective-permute-start = (f32[8,32,128]{2,1,0:T(8,128)S(1)}, f32[8,32,128]{2,1,0:T(8,128)S(1)}, u32[]{:S(2)}, u32[]{:S(2)}) collective-permute-start(f32[8,32,128]{2,1,0:T(8,128)S(1)} %get-tuple-element.45), channel_id=1, source_target_pairs={{0,1},{1,0},{2,3},{3,2},{4,5},{5,4},{6,7},{7,6},{8,9},{9,8},{10,11... | collective-permute-start | bytes 393224 | tf_op jit(solution)/shard_map/ppermute | solution.py:773
  8.2 1.3 %collective-permute-start.1 = (f32[8,32,128]{2,1,0:T(8,128)S(1)}, f32[8,32,128]{2,1,0:T(8,128)S(1)}, u32[]{:S(2)}, u32[]{:S(2)}) collective-permute-start(f32[8,32,128]{2,1,0:T(8,128)S(1)} %get-tuple-element.46), channel_id=1, source_target_pairs={{0,1},{1,0},{2,3},{3,2},{4,5},{5,4},{6,7},{7,6},{8,9},{9,8},{10,11... | collective-permute-start | bytes 393224 | tf_op jit(solution)/shard_map/ppermute | solution.py:773
  11.4 1.5 %collective-permute-start.5 = (f32[12,32,128]{2,1,0:T(8,128)S(1)}, f32[12,32,128]{2,1,0:T(8,128)S(1)}, u32[]{:S(2)}, u32[]{:S(2)}) collective-permute-start(f32[12,32,128]{2,1,0:T(8,128)S(1)} %collective-permute-done.3.refs_7_), channel_id=1, source_target_pairs={{0,1},{1,0},{2,3},{3,2},{4,5},{5,4},{6,7},{7,6},{8,9},{9,8},{10,11... | collective-permute-start | bytes 589832 | tf_op jit(solution)/shard_map/ppermute | solution.py:765
  11.7 1.5 %collective-permute-start.6 = (f32[12,32,128]{2,1,0:T(8,128)S(1)}, f32[12,32,128]{2,1,0:T(8,128)S(1)}, u32[]{:S(2)}, u32[]{:S(2)}) collective-permute-start(f32[12,32,128]{2,1,0:T(8,128)S(1)} %collective-permute-done.4.refs_8_), channel_id=1, source_target_pairs={{0,1},{1,0},{2,3},{3,2},{4,5},{5,4},{6,7},{7,6},{8,9},{9,8},{10,11... | collective-permute-start | bytes 589832 | tf_op jit(solution)/shard_map/ppermute | solution.py:765
  15.5 12.8 %collective-permute-start.8 = (f32[5,32,128]{2,1,0:T(8,128)S(1)}, f32[5,32,128]{2,1,0:T(8,128)S(1)}, u32[]{:S(2)}, u32[]{:S(2)}) collective-permute-start(f32[5,32,128]{2,1,0:T(8,128)S(1)} %get-tuple-element.63), channel_id=1, source_target_pairs={{0,4},{2,6},{4,0},{6,2},{8,12},{10,14},{12,8},{14,10},{16,20},{18,... | collective-permute-start | bytes 245768 | tf_op jit(solution)/shard_map/ppermute | solution.py:791
  21.1 5.3 %collective-permute-start.9 = (f32[3,32,128]{2,1,0:T(8,128)S(1)}, f32[3,32,128]{2,1,0:T(8,128)S(1)}, u32[]{:S(2)}, u32[]{:S(2)}) collective-permute-start(f32[3,32,128]{2,1,0:T(8,128)S(1)} %get-tuple-element.62.refs_0_), channel_id=1, source_target_pairs={{0,6},{2,4},{4,2},{6,0},{8,14},{10,12},{12,10},{14,8},{16,22},{18,... | collective-permute-start | bytes 147464 | tf_op jit(solution)/shard_map/ppermute | solution.py:791
  23.7 4.7 %collective-permute-start.7 = (f32[3,32,128]{2,1,0:T(8,128)S(1)}, f32[3,32,128]{2,1,0:T(8,128)S(1)}, u32[]{:S(2)}, u32[]{:S(2)}) collective-permute-start(f32[3,32,128]{2,1,0:T(8,128)S(1)} %get-tuple-element.62.refs_0_), channel_id=1, source_target_pairs={{0,2},{2,0},{4,6},{6,4},{8,10},{10,8},{12,14},{14,12},{16,18},{18,... | collective-permute-start | bytes 147464 | tf_op jit(solution)/shard_map/ppermute | solution.py:791
  23.7 10.5 %collective-permute-start.18 = (f32[12,32,128]{2,1,0:T(8,128)S(1)}, f32[12,32,128]{2,1,0:T(8,128)S(1)}, u32[]{:S(2)}, u32[]{:S(2)}) collective-permute-start(f32[12,32,128]{2,1,0:T(8,128)S(1)} %get-tuple-element.69), channel_id=1, source_target_pairs={{0,2},{2,0},{4,6},{6,4},{8,10},{10,8},{12,14},{14,12},{16,18},{18,... | collective-permute-start | bytes 589832 | tf_op jit(solution)/shard_map/ppermute | solution.py:801
  29.1 7.2 %collective-permute-start.12 = (f32[7,32,128]{2,1,0:T(8,128)S(1)}, f32[7,32,128]{2,1,0:T(8,128)S(1)}, u32[]{:S(2)}, u32[]{:S(2)}) collective-permute-start(f32[7,32,128]{2,1,0:T(8,128)S(1)} %merge.1.refs_0_), channel_id=1, source_target_pairs={{0,24},{2,26},{4,28},{6,30},{8,16},{10,18},{12,20},{14,22},{16,8},... | collective-permute-start | bytes 344072 | tf_op jit(solution)/shard_map/ppermute | solution.py:791
  32.8 9.2 %collective-permute-start.11 = (f32[7,32,128]{2,1,0:T(8,128)S(1)}, f32[7,32,128]{2,1,0:T(8,128)S(1)}, u32[]{:S(2)}, u32[]{:S(2)}) collective-permute-start(f32[7,32,128]{2,1,0:T(8,128)S(1)} %merge.1.refs_0_), channel_id=1, source_target_pairs={{0,16},{2,18},{4,20},{6,22},{8,24},{10,26},{12,28},{14,30},{16,0},... | collective-permute-start | bytes 344072 | tf_op jit(solution)/shard_map/ppermute | solution.py:791
  32.8 9.2 %collective-permute-start.10 = (f32[7,32,128]{2,1,0:T(8,128)S(1)}, f32[7,32,128]{2,1,0:T(8,128)S(1)}, u32[]{:S(2)}, u32[]{:S(2)}) collective-permute-start(f32[7,32,128]{2,1,0:T(8,128)S(1)} %merge.1.refs_0_), channel_id=1, source_target_pairs={{0,8},{2,10},{4,12},{6,14},{8,0},{10,2},{12,4},{14,6},{16,24},{18,... | collective-permute-start | bytes 344072 | tf_op jit(solution)/shard_map/ppermute | solution.py:791
  33.5 1.4 %collective-permute-start.13 = (f32[2,32,128]{2,1,0:T(8,128)S(1)}, f32[2,32,128]{2,1,0:T(8,128)S(1)}, u32[]{:S(2)}, u32[]{:S(2)}) collective-permute-start(f32[2,32,128]{2,1,0:T(8,128)S(1)} %get-tuple-element.64), channel_id=1, source_target_pairs={{4,8},{8,4},{6,10},{10,6},{12,16},{16,12},{14,18},{18,14},{20,24},... | collective-permute-start | bytes 98312 | tf_op jit(solution)/shard_map/ppermute | solution.py:801
  34.2 12.5 %collective-permute-start.19 = (f32[12,32,128]{2,1,0:T(8,128)S(1)}, f32[12,32,128]{2,1,0:T(8,128)S(1)}, u32[]{:S(2)}, u32[]{:S(2)}) collective-permute-start(f32[12,32,128]{2,1,0:T(8,128)S(1)} %get-tuple-element.72), channel_id=1, source_target_pairs={{2,4},{4,2},{6,8},{8,6},{10,12},{12,10},{14,16},{16,14},{18,20},{2... | collective-permute-start | bytes 589832 | tf_op jit(solution)/shard_map/ppermute | solution.py:801
  42.0 1.3 %collective-permute-start.14 = (f32[7,32,128]{2,1,0:T(8,128)S(1)}, f32[7,32,128]{2,1,0:T(8,128)S(1)}, u32[]{:S(2)}, u32[]{:S(2)}) collective-permute-start(f32[7,32,128]{2,1,0:T(8,128)S(1)} %merge.1.refs_0_), channel_id=1, source_target_pairs={{0,1},{1,0},{2,3},{3,2},{4,5},{5,4},{6,7},{7,6},{8,9},{9,8},{10,11... | collective-permute-start | bytes 344072 | tf_op jit(solution)/shard_map/ppermute | solution.py:765
  42.0 1.5 %collective-permute-start.15 = (f32[7,32,128]{2,1,0:T(8,128)S(1)}, f32[7,32,128]{2,1,0:T(8,128)S(1)}, u32[]{:S(2)}, u32[]{:S(2)}) collective-permute-start(f32[7,32,128]{2,1,0:T(8,128)S(1)} %collective-permute-done.10.refs_1_), channel_id=1, source_target_pairs={{0,1},{1,0},{2,3},{3,2},{4,5},{5,4},{6,7},{7,6},{8,9},{9,8},{10,11... | collective-permute-start | bytes 344072 | tf_op jit(solution)/shard_map/ppermute | solution.py:765
  42.5 1.3 %collective-permute-start.16 = (f32[7,32,128]{2,1,0:T(8,128)S(1)}, f32[7,32,128]{2,1,0:T(8,128)S(1)}, u32[]{:S(2)}, u32[]{:S(2)}) collective-permute-start(f32[7,32,128]{2,1,0:T(8,128)S(1)} %collective-permute-done.11.refs_2_), channel_id=1, source_target_pairs={{0,1},{1,0},{2,3},{3,2},{4,5},{5,4},{6,7},{7,6},{8,9},{9,8},{10,11... | collective-permute-start | bytes 344072 | tf_op jit(solution)/shard_map/ppermute | solution.py:765
  42.5 1.5 %collective-permute-start.17 = (f32[7,32,128]{2,1,0:T(8,128)S(1)}, f32[7,32,128]{2,1,0:T(8,128)S(1)}, u32[]{:S(2)}, u32[]{:S(2)}) collective-permute-start(f32[7,32,128]{2,1,0:T(8,128)S(1)} %collective-permute-done.12.refs_3_), channel_id=1, source_target_pairs={{0,1},{1,0},{2,3},{3,2},{4,5},{5,4},{6,7},{7,6},{8,9},{9,8},{10,11... | collective-permute-start | bytes 344072 | tf_op jit(solution)/shard_map/ppermute | solution.py:765

commit v20 on v19

--- a/solution.py
+++ b/solution.py
@@ -18,6 +18,7 @@
 VMEM_LIMIT = 32 * 1024 * 1024
 BYTES_A_MICRO = 3.69e6
 CHUNKS = 4
+PIECES = 4
 
 
 class Sizes:
@@ -730,9 +731,12 @@
     copies = []
     for chunk in range(CHUNKS):
         part = slice(chunk * step, (chunk + 1) * step)
-        result[part] = jnp.swapaxes(it0[:, part, :width], 0, 1)
-        copies.append(pltpu.make_async_copy(result.at[part], out.at[part], semaphores.at[chunk]))
-        copies[-1].start()
+        result[part] = jnp.swapaxes(it0[:, part], 0, 1)
+        for piece in range(PIECES):
+            start = chunk * step + piece * (step // PIECES)
+            part = slice(start, start + step // PIECES)
+            copies.append(pltpu.make_async_copy(result.at[part], out.at[part], semaphores.at[len(copies)]))
+            copies[-1].start()
     for copy in copies:
         copy.wait()
 
@@ -909,7 +913,7 @@
         scratch,
         place,
         [coarse, *received, *inner[2:], *outer, own0, turned, *borders],
-        copies=CHUNKS,
+        copies=CHUNKS * PIECES,
         far_out=True,
     )
     return correction

time: 50.1 us -> 50.2 us (level)
  no operation moved by 1% of the time
where the time goes in v20:
time: 50.2 us; the launch traced here: 49.9 us
  starting transfers between devices  21.9 us (44%)
  waiting for transfers between devices  13.2 us (26%)
  Pallas kernels  12.6 us (25%)
  local copies, waits for them, and re-layouts  2.09 us (4%)
    ppermute x6, starting transfers between devices, swap(): lax.ppermute(others.get(step, value), 'span', [(device, device ^ step * s...  12.6 us
    pallas_call x7, Pallas kernels, call(): pl.pallas_call(body, name=name, out_shape=[jax.ShapeDtypeStruct(shape, f3...  12.6 us
    ppermute x6, waiting for transfers between devices, swap(): lax.ppermute(others.get(step, value), 'span', [(device, device ^ step * s...  9.71 us
    ppermute x5, starting transfers between devices, exchange(): lax.ppermute(value, 'span', route)  7.01 us
    ppermute x6, waiting for transfers between devices, beside(): lax.ppermute(value, 'width', [(0, 1), (1, 0)])  2.19 us
    unnamed x6, local copies, waits for them, and re-layouts  2.09 us
    ppermute x6, starting transfers between devices, beside(): lax.ppermute(value, 'width', [(0, 1), (1, 0)])  1.6 us
    ppermute x3, waiting for transfers between devices, edge_columns(): return [lax.ppermute(edges[0], 'width', [(0, 1), (1, 0)])]  1.27 us
  transfers between devices with their start and end apart: 20, of which 13 were waited for; matrix products, arithmetic and copies ran while one was open for 0% of the time, Pallas kernels for 12%

profile of v20, /device:TPU:0, one launch (start us, length us, event | category | flops | bytes accessed | tf_op | source)
XLA Modules:
  0.0 49.9 jit_solution(9468984648578424361)
XLA Ops:
  0.1 1.0 %copy-done = f32[32,8,512]{2,1,0:T(8,128)S(1)} copy-done((f32[32,8,512]{2,1,0:T(8,128)S(1)}, f32[32,8,512]{2,1,0:T(8,128)}, u32[]{:S(2)}) %copy-start) | copy-done | bytes 524312
  1.1 1.0 %copy-done.1 = f32[32,8,512]{2,1,0:T(8,128)S(1)} copy-done((f32[32,8,512]{2,1,0:T(8,128)S(1)}, f32[32,8,512]{2,1,0:T(8,128)}, u32[]{:S(2)}) %copy-start.1) | copy-done | bytes 524312
  2.2 1.1 %start.1 = (f32[2,8,32,512]{3,2,1,0:T(8,128)S(1)}, f32[8,32,256]{2,1,0:T(8,128)S(1)}, f32[4,32,128]{2,1,0:T(8,128)S(1)}, f32[12,32,128]{2,1,0:T(8,128)S(1)}, f32...) custom-call(s32[2]{0:T(128)S(1)} %pad_add_fusion.place, f32[32,8,512]{2,1,0:T(8,128)S(1)} %copy-done, ...), custom_call_target="tpu_custom_call" | custom-call | flops 1264999936 | bytes 4059000 | tf_op jit(solution)/shard_map/start/pallas_call | solution.py:749
  3.3 3.0 %collective-permute-start.3 = (f32[12,32,128]{2,1,0:T(8,128)S(1)}, f32[12,32,128]{2,1,0:T(8,128)S(1)}, u32[]{:S(2)}, u32[]{:S(2)}) collective-permute-start(f32[12,32,128]{2,1,0:T(8,128)S(1)} %get-tuple-element.48), channel_id=1, source_target_pairs={{0,2},{2,0},{4,6},{6,4},{8,10},{10,8},{12,14},{14,12},{16,18},{18,... | collective-permute-start | bytes 589832 | tf_op jit(solution)/shard_map/ppermute | solution.py:805
  6.3 0.7 %collective-permute-start.4 = (f32[12,32,128]{2,1,0:T(8,128)S(1)}, f32[12,32,128]{2,1,0:T(8,128)S(1)}, u32[]{:S(2)}, u32[]{:S(2)}) collective-permute-start(f32[12,32,128]{2,1,0:T(8,128)S(1)} %get-tuple-element.49), channel_id=1, source_target_pairs={{2,4},{4,2},{6,8},{8,6},{10,12},{12,10},{14,16},{16,14},{18,20},{2... | collective-permute-start | bytes 589832 | tf_op jit(solution)/shard_map/ppermute | solution.py:805
  7.0 0.7 %turn.1 = (f32[8,32,512]{2,1,0:T(8,128)S(1)}, f32[8,32,128]{2,1,0:T(8,128)S(1)}) custom-call(s32[2]{0:T(128)S(1)} %pad_add_fusion.place, f32[32,8,512]{2,1,0:T(8,128)S(1)} %copy-done.2), custom_call_target="tpu_custom_call" | custom-call | flops 805000000 | bytes 2583000 | tf_op jit(solution)/shard_map/turn/pallas_call | solution.py:749
  8.3 0.8 %collective-permute-done.2.refs_6_.refs_14_ = f32[8,32,128]{2,1,0:T(8,128)S(1)} collective-permute-done((f32[8,32,128]{2,1,0:T(8,128)S(1)}, f32[8,32,128]{2,1,0:T(8,128)S(1)}, u32[]{:S(2)}, u32[]{:S(2)}) %collective-permute-start.2) | collective-permute-done | bytes 131104 | tf_op jit(solution)/shard_map/ppermute | solution.py:777
  9.6 1.8 %inner.1 = (f32[8,32,128]{2,1,0:T(8,128)S(1)}, f32[4,32,128]{2,1,0:T(8,128)S(1)}, f32[35,32,640]{2,1,0:T(8,128)S(1)}, f32[17,32,384]{2,1,0:T(8,128)S(1)}, f32[5,32,256]{2,1,0:T(8,128)S(1)}) custom-call(s32[2]{0:T(128)S(1)} %pad_add_fusion.place, f32[2,8,32,512]{3,2,1,0:T(8,128)S(1)} %get-tuple-element.41.refs_0_.refs_10_, ...), custom_call_target="tpu_custom_call" | custom-call | flops 575000000 | bytes 1845000 | tf_op jit(solution)/shard_map/inner/pallas_call | solution.py:749
  12.0 0.9 %collective-permute-done.5.refs_9_ = f32[12,32,128]{2,1,0:T(8,128)S(1)} collective-permute-done((f32[12,32,128]{2,1,0:T(8,128)S(1)}, f32[12,32,128]{2,1,0:T(8,128)S(1)}, u32[]{:S(2)}, u32[]{:S(2)}) %collective-permute-start.5) | collective-permute-done | bytes 196640 | tf_op jit(solution)/shard_map/ppermute | solution.py:769
  13.2 2.3 %down.1 = (f32[6,32,640]{2,1,0:T(8,128)S(1)}, f32[26,32,384]{2,1,0:T(8,128)S(1)}, f32[24,32,256]{2,1,0:T(8,128)S(1)}, f32[3,32,128]{2,1,0:T(8,128)S(1)}, f32[5,3...) custom-call(s32[2]{0:T(128)S(1)} %pad_add_fusion.place, ...), custom_call_target="tpu_custom_call" | custom-call | flops 2875000064 | bytes 9225000 | tf_op jit(solution)/shard_map/down/pallas_call | solution.py:749
  15.5 5.5 %collective-permute-start.8 = (f32[5,32,128]{2,1,0:T(8,128)S(1)}, f32[5,32,128]{2,1,0:T(8,128)S(1)}, u32[]{:S(2)}, u32[]{:S(2)}) collective-permute-start(f32[5,32,128]{2,1,0:T(8,128)S(1)} %get-tuple-element.63), channel_id=1, source_target_pairs={{0,4},{2,6},{4,0},{6,2},{8,12},{10,14},{12,8},{14,10},{16,20},{18,... | collective-permute-start | bytes 245768 | tf_op jit(solution)/shard_map/ppermute | solution.py:795
  21.1 2.6 %collective-permute-start.9 = (f32[3,32,128]{2,1,0:T(8,128)S(1)}, f32[3,32,128]{2,1,0:T(8,128)S(1)}, u32[]{:S(2)}, u32[]{:S(2)}) collective-permute-start(f32[3,32,128]{2,1,0:T(8,128)S(1)} %get-tuple-element.62.refs_0_), channel_id=1, source_target_pairs={{0,6},{2,4},{4,2},{6,0},{8,14},{10,12},{12,10},{14,8},{16,22},{18,... | collective-permute-start | bytes 147464 | tf_op jit(solution)/shard_map/ppermute | solution.py:795
  23.7 2.0 %collective-permute-start.18 = (f32[12,32,128]{2,1,0:T(8,128)S(1)}, f32[12,32,128]{2,1,0:T(8,128)S(1)}, u32[]{:S(2)}, u32[]{:S(2)}) collective-permute-start(f32[12,32,128]{2,1,0:T(8,128)S(1)} %get-tuple-element.69), channel_id=1, source_target_pairs={{0,2},{2,0},{4,6},{6,4},{8,10},{10,8},{12,14},{14,12},{16,18},{18,... | collective-permute-start | bytes 589832 | tf_op jit(solution)/shard_map/ppermute | solution.py:805
  25.7 0.6 %collective-permute-done.9.refs_3_ = f32[3,32,128]{2,1,0:T(8,128)S(1)} collective-permute-done((f32[3,32,128]{2,1,0:T(8,128)S(1)}, f32[3,32,128]{2,1,0:T(8,128)S(1)}, u32[]{:S(2)}, u32[]{:S(2)}) %collective-permute-start.9) | collective-permute-done | bytes 49184 | tf_op jit(solution)/shard_map/ppermute | solution.py:795
  26.4 2.0 %collective-permute-done.7.refs_1_ = f32[3,32,128]{2,1,0:T(8,128)S(1)} collective-permute-done((f32[3,32,128]{2,1,0:T(8,128)S(1)}, f32[3,32,128]{2,1,0:T(8,128)S(1)}, u32[]{:S(2)}, u32[]{:S(2)}) %collective-permute-start.7) | collective-permute-done | bytes 49184 | tf_op jit(solution)/shard_map/ppermute | solution.py:795
  28.3 0.7 %merge.1.refs_0_ = f32[7,32,128]{2,1,0:T(8,128)S(1)} custom-call(s32[2]{0:T(128)S(1)} %pad_add_fusion.place, f32[3,32,128]{2,1,0:T(8,128)S(1)} %get-tuple-element.62.refs_0_, f32[3,32,128]{2,1,0:T(8,128)S(1)} %collective-permute-done.7.refs_1_, f32[5,32,128]{2,1,0:T(8,128)S(1)} %collective-permute-done.8.refs_2_, ...), custom_call_target="tpu_custom_call" | custom-call | flops 1035000000 | bytes 3321000 | tf_op jit(solution)/shard_map/merge/pallas_call | solution.py:749
  29.1 3.7 %collective-permute-start.12 = (f32[7,32,128]{2,1,0:T(8,128)S(1)}, f32[7,32,128]{2,1,0:T(8,128)S(1)}, u32[]{:S(2)}, u32[]{:S(2)}) collective-permute-start(f32[7,32,128]{2,1,0:T(8,128)S(1)} %merge.1.refs_0_), channel_id=1, source_target_pairs={{0,24},{2,26},{4,28},{6,30},{8,16},{10,18},{12,20},{14,22},{16,8},... | collective-permute-start | bytes 344072 | tf_op jit(solution)/shard_map/ppermute | solution.py:795
  32.8 0.8 %collective-permute-start.10 = (f32[7,32,128]{2,1,0:T(8,128)S(1)}, f32[7,32,128]{2,1,0:T(8,128)S(1)}, u32[]{:S(2)}, u32[]{:S(2)}) collective-permute-start(f32[7,32,128]{2,1,0:T(8,128)S(1)} %merge.1.refs_0_), channel_id=1, source_target_pairs={{0,8},{2,10},{4,12},{6,14},{8,0},{10,2},{12,4},{14,6},{16,24},{18,... | collective-permute-start | bytes 344072 | tf_op jit(solution)/shard_map/ppermute | solution.py:795
  33.5 0.7 %collective-permute-start.13 = (f32[2,32,128]{2,1,0:T(8,128)S(1)}, f32[2,32,128]{2,1,0:T(8,128)S(1)}, u32[]{:S(2)}, u32[]{:S(2)}) collective-permute-start(f32[2,32,128]{2,1,0:T(8,128)S(1)} %get-tuple-element.64), channel_id=1, source_target_pairs={{4,8},{8,4},{6,10},{10,6},{12,16},{16,12},{14,18},{18,14},{20,24},... | collective-permute-start | bytes 98312 | tf_op jit(solution)/shard_map/ppermute | solution.py:805
  34.2 0.7 %collective-permute-start.19 = (f32[12,32,128]{2,1,0:T(8,128)S(1)}, f32[12,32,128]{2,1,0:T(8,128)S(1)}, u32[]{:S(2)}, u32[]{:S(2)}) collective-permute-start(f32[12,32,128]{2,1,0:T(8,128)S(1)} %get-tuple-element.72), channel_id=1, source_target_pairs={{2,4},{4,2},{6,8},{8,6},{10,12},{12,10},{14,16},{16,14},{18,20},{2... | collective-permute-start | bytes 589832 | tf_op jit(solution)/shard_map/ppermute | solution.py:805
  34.9 1.3 %collective-permute-done.12.refs_3_ = f32[7,32,128]{2,1,0:T(8,128)S(1)} collective-permute-done((f32[7,32,128]{2,1,0:T(8,128)S(1)}, f32[7,32,128]{2,1,0:T(8,128)S(1)}, u32[]{:S(2)}, u32[]{:S(2)}) %collective-permute-start.12) | collective-permute-done | bytes 114720 | tf_op jit(solution)/shard_map/ppermute | solution.py:795
  36.3 5.7 %collective-permute-done.11.refs_2_ = f32[7,32,128]{2,1,0:T(8,128)S(1)} collective-permute-done((f32[7,32,128]{2,1,0:T(8,128)S(1)}, f32[7,32,128]{2,1,0:T(8,128)S(1)}, u32[]{:S(2)}, u32[]{:S(2)}) %collective-permute-start.11) | collective-permute-done | bytes 114720 | tf_op jit(solution)/shard_map/ppermute | solution.py:795
  44.0 2.7 %coarse.1 = f32[3,32,128]{2,1,0:T(8,128)S(1)} custom-call(s32[2]{0:T(128)S(1)} %pad_add_fusion.place, f32[7,32,128]{2,1,0:T(8,128)S(1)} %merge.1.refs_0_, f32[7,32,128]{2,1,0:T(8,128)S(1)} %collective-permute-done.10.refs_1_, f32[7,32,128]{2,1,0:T(8,128)S(1)} %collective-permute-done.11.refs_2_, f32[7,32,128]{2,1,0:T(8,128)S(1)} %collective-permute-done.12.refs_3_, ...), custom_call_target="tpu_custom_call" | custom-call | flops 805000000 | bytes 2583000 | tf_op jit(solution)/shard_map/coarse/pallas_call | solution.py:749
  46.7 3.2 %up.1 = f32[32,8,512]{2,1,0:T(8,128)} custom-call(s32[2]{0:T(128)S(1)} %pad_add_fusion.place, f32[3,32,128]{2,1,0:T(8,128)S(1)} %coarse.1, f32[12,32,128]{2,1,0:T(8,128)S(1)} %collective-permute-done.18.refs_0_, f32[12,32,128]{2,1,0:T(8,128)S(1)} %collective-permute-done.19.refs_1_, f32[5,32,128]{2,1,0:T(8,128)S(1)} %collective-permute-done.8.refs_2_, ...), custom_call_target="tpu_custom_call" | custom-call | flops 3449999872 | bytes 11070000 | tf_op jit(solution)/shard_map/up/pallas_call | solution.py:749
  (30 shorter events, 4.1 us)
Async XLA Ops:
  0.1 1.0 %copy-start = (f32[32,8,512]{2,1,0:T(8,128)S(1)}, f32[32,8,512]{2,1,0:T(8,128)}, u32[]{:S(2)}) copy-start(f32[32,8,512]{2,1,0:T(8,128)} %conduct.1) | copy-start | bytes 1572868
  1.1 1.0 %copy-start.1 = (f32[32,8,512]{2,1,0:T(8,128)S(1)}, f32[32,8,512]{2,1,0:T(8,128)}, u32[]{:S(2)}) copy-start(f32[32,8,512]{2,1,0:T(8,128)} %binding.1) | copy-start | bytes 1572868
  2.2 4.8 %copy-start.2 = (f32[32,8,512]{2,1,0:T(8,128)S(1)}, f32[32,8,512]{2,1,0:T(8,128)}, u32[]{:S(2)}) copy-start(f32[32,8,512]{2,1,0:T(8,128)} %right_side.1) | copy-start | bytes 1572868
  3.3 8.1 %collective-permute-start.3 = (f32[12,32,128]{2,1,0:T(8,128)S(1)}, f32[12,32,128]{2,1,0:T(8,128)S(1)}, u32[]{:S(2)}, u32[]{:S(2)}) collective-permute-start(f32[12,32,128]{2,1,0:T(8,128)S(1)} %get-tuple-element.48), channel_id=1, source_target_pairs={{0,2},{2,0},{4,6},{6,4},{8,10},{10,8},{12,14},{14,12},{16,18},{18,... | collective-permute-start | bytes 589832 | tf_op jit(solution)/shard_map/ppermute | solution.py:805
  6.3 5.1 %collective-permute-start.4 = (f32[12,32,128]{2,1,0:T(8,128)S(1)}, f32[12,32,128]{2,1,0:T(8,128)S(1)}, u32[]{:S(2)}, u32[]{:S(2)}) collective-permute-start(f32[12,32,128]{2,1,0:T(8,128)S(1)} %get-tuple-element.49), channel_id=1, source_target_pairs={{2,4},{4,2},{6,8},{8,6},{10,12},{12,10},{14,16},{16,14},{18,20},{2... | collective-permute-start | bytes 589832 | tf_op jit(solution)/shard_map/ppermute | solution.py:805
  7.7 1.4 %collective-permute-start.2 = (f32[8,32,128]{2,1,0:T(8,128)S(1)}, f32[8,32,128]{2,1,0:T(8,128)S(1)}, u32[]{:S(2)}, u32[]{:S(2)}) collective-permute-start(f32[8,32,128]{2,1,0:T(8,128)S(1)} %get-tuple-element.47), channel_id=1, source_target_pairs={{0,1},{1,0},{2,3},{3,2},{4,5},{5,4},{6,7},{7,6},{8,9},{9,8},{10,11... | collective-permute-start | bytes 393224 | tf_op jit(solution)/shard_map/ppermute | solution.py:777
  7.7 1.5 %collective-permute-start = (f32[8,32,128]{2,1,0:T(8,128)S(1)}, f32[8,32,128]{2,1,0:T(8,128)S(1)}, u32[]{:S(2)}, u32[]{:S(2)}) collective-permute-start(f32[8,32,128]{2,1,0:T(8,128)S(1)} %get-tuple-element.45), channel_id=1, source_target_pairs={{0,1},{1,0},{2,3},{3,2},{4,5},{5,4},{6,7},{7,6},{8,9},{9,8},{10,11... | collective-permute-start | bytes 393224 | tf_op jit(solution)/shard_map/ppermute | solution.py:777
  8.2 1.3 %collective-permute-start.1 = (f32[8,32,128]{2,1,0:T(8,128)S(1)}, f32[8,32,128]{2,1,0:T(8,128)S(1)}, u32[]{:S(2)}, u32[]{:S(2)}) collective-permute-start(f32[8,32,128]{2,1,0:T(8,128)S(1)} %get-tuple-element.46), channel_id=1, source_target_pairs={{0,1},{1,0},{2,3},{3,2},{4,5},{5,4},{6,7},{7,6},{8,9},{9,8},{10,11... | collective-permute-start | bytes 393224 | tf_op jit(solution)/shard_map/ppermute | solution.py:777
  11.4 1.5 %collective-permute-start.5 = (f32[12,32,128]{2,1,0:T(8,128)S(1)}, f32[12,32,128]{2,1,0:T(8,128)S(1)}, u32[]{:S(2)}, u32[]{:S(2)}) collective-permute-start(f32[12,32,128]{2,1,0:T(8,128)S(1)} %collective-permute-done.3.refs_7_), channel_id=1, source_target_pairs={{0,1},{1,0},{2,3},{3,2},{4,5},{5,4},{6,7},{7,6},{8,9},{9,8},{10,11... | collective-permute-start | bytes 589832 | tf_op jit(solution)/shard_map/ppermute | solution.py:769
  11.7 1.5 %collective-permute-start.6 = (f32[12,32,128]{2,1,0:T(8,128)S(1)}, f32[12,32,128]{2,1,0:T(8,128)S(1)}, u32[]{:S(2)}, u32[]{:S(2)}) collective-permute-start(f32[12,32,128]{2,1,0:T(8,128)S(1)} %collective-permute-done.4.refs_8_), channel_id=1, source_target_pairs={{0,1},{1,0},{2,3},{3,2},{4,5},{5,4},{6,7},{7,6},{8,9},{9,8},{10,11... | collective-permute-start | bytes 589832 | tf_op jit(solution)/shard_map/ppermute | solution.py:769
  15.5 12.8 %collective-permute-start.8 = (f32[5,32,128]{2,1,0:T(8,128)S(1)}, f32[5,32,128]{2,1,0:T(8,128)S(1)}, u32[]{:S(2)}, u32[]{:S(2)}) collective-permute-start(f32[5,32,128]{2,1,0:T(8,128)S(1)} %get-tuple-element.63), channel_id=1, source_target_pairs={{0,4},{2,6},{4,0},{6,2},{8,12},{10,14},{12,8},{14,10},{16,20},{18,... | collective-permute-start | bytes 245768 | tf_op jit(solution)/shard_map/ppermute | solution.py:795
  21.1 5.3 %collective-permute-start.9 = (f32[3,32,128]{2,1,0:T(8,128)S(1)}, f32[3,32,128]{2,1,0:T(8,128)S(1)}, u32[]{:S(2)}, u32[]{:S(2)}) collective-permute-start(f32[3,32,128]{2,1,0:T(8,128)S(1)} %get-tuple-element.62.refs_0_), channel_id=1, source_target_pairs={{0,6},{2,4},{4,2},{6,0},{8,14},{10,12},{12,10},{14,8},{16,22},{18,... | collective-permute-start | bytes 147464 | tf_op jit(solution)/shard_map/ppermute | solution.py:795
  23.7 4.7 %collective-permute-start.7 = (f32[3,32,128]{2,1,0:T(8,128)S(1)}, f32[3,32,128]{2,1,0:T(8,128)S(1)}, u32[]{:S(2)}, u32[]{:S(2)}) collective-permute-start(f32[3,32,128]{2,1,0:T(8,128)S(1)} %get-tuple-element.62.refs_0_), channel_id=1, source_target_pairs={{0,2},{2,0},{4,6},{6,4},{8,10},{10,8},{12,14},{14,12},{16,18},{18,... | collective-permute-start | bytes 147464 | tf_op jit(solution)/shard_map/ppermute | solution.py:795
  23.7 10.5 %collective-permute-start.18 = (f32[12,32,128]{2,1,0:T(8,128)S(1)}, f32[12,32,128]{2,1,0:T(8,128)S(1)}, u32[]{:S(2)}, u32[]{:S(2)}) collective-permute-start(f32[12,32,128]{2,1,0:T(8,128)S(1)} %get-tuple-element.69), channel_id=1, source_target_pairs={{0,2},{2,0},{4,6},{6,4},{8,10},{10,8},{12,14},{14,12},{16,18},{18,... | collective-permute-start | bytes 589832 | tf_op jit(solution)/shard_map/ppermute | solution.py:805
  29.1 7.2 %collective-permute-start.12 = (f32[7,32,128]{2,1,0:T(8,128)S(1)}, f32[7,32,128]{2,1,0:T(8,128)S(1)}, u32[]{:S(2)}, u32[]{:S(2)}) collective-permute-start(f32[7,32,128]{2,1,0:T(8,128)S(1)} %merge.1.refs_0_), channel_id=1, source_target_pairs={{0,24},{2,26},{4,28},{6,30},{8,16},{10,18},{12,20},{14,22},{16,8},... | collective-permute-start | bytes 344072 | tf_op jit(solution)/shard_map/ppermute | solution.py:795
  32.8 9.2 %collective-permute-start.11 = (f32[7,32,128]{2,1,0:T(8,128)S(1)}, f32[7,32,128]{2,1,0:T(8,128)S(1)}, u32[]{:S(2)}, u32[]{:S(2)}) collective-permute-start(f32[7,32,128]{2,1,0:T(8,128)S(1)} %merge.1.refs_0_), channel_id=1, source_target_pairs={{0,16},{2,18},{4,20},{6,22},{8,24},{10,26},{12,28},{14,30},{16,0},... | collective-permute-start | bytes 344072 | tf_op jit(solution)/shard_map/ppermute | solution.py:795
  32.8 9.2 %collective-permute-start.10 = (f32[7,32,128]{2,1,0:T(8,128)S(1)}, f32[7,32,128]{2,1,0:T(8,128)S(1)}, u32[]{:S(2)}, u32[]{:S(2)}) collective-permute-start(f32[7,32,128]{2,1,0:T(8,128)S(1)} %merge.1.refs_0_), channel_id=1, source_target_pairs={{0,8},{2,10},{4,12},{6,14},{8,0},{10,2},{12,4},{14,6},{16,24},{18,... | collective-permute-start | bytes 344072 | tf_op jit(solution)/shard_map/ppermute | solution.py:795
  33.5 1.4 %collective-permute-start.13 = (f32[2,32,128]{2,1,0:T(8,128)S(1)}, f32[2,32,128]{2,1,0:T(8,128)S(1)}, u32[]{:S(2)}, u32[]{:S(2)}) collective-permute-start(f32[2,32,128]{2,1,0:T(8,128)S(1)} %get-tuple-element.64), channel_id=1, source_target_pairs={{4,8},{8,4},{6,10},{10,6},{12,16},{16,12},{14,18},{18,14},{20,24},... | collective-permute-start | bytes 98312 | tf_op jit(solution)/shard_map/ppermute | solution.py:805
  34.2 12.5 %collective-permute-start.19 = (f32[12,32,128]{2,1,0:T(8,128)S(1)}, f32[12,32,128]{2,1,0:T(8,128)S(1)}, u32[]{:S(2)}, u32[]{:S(2)}) collective-permute-start(f32[12,32,128]{2,1,0:T(8,128)S(1)} %get-tuple-element.72), channel_id=1, source_target_pairs={{2,4},{4,2},{6,8},{8,6},{10,12},{12,10},{14,16},{16,14},{18,20},{2... | collective-permute-start | bytes 589832 | tf_op jit(solution)/shard_map/ppermute | solution.py:805
  42.0 1.3 %collective-permute-start.14 = (f32[7,32,128]{2,1,0:T(8,128)S(1)}, f32[7,32,128]{2,1,0:T(8,128)S(1)}, u32[]{:S(2)}, u32[]{:S(2)}) collective-permute-start(f32[7,32,128]{2,1,0:T(8,128)S(1)} %merge.1.refs_0_), channel_id=1, source_target_pairs={{0,1},{1,0},{2,3},{3,2},{4,5},{5,4},{6,7},{7,6},{8,9},{9,8},{10,11... | collective-permute-start | bytes 344072 | tf_op jit(solution)/shard_map/ppermute | solution.py:769
  42.0 1.5 %collective-permute-start.15 = (f32[7,32,128]{2,1,0:T(8,128)S(1)}, f32[7,32,128]{2,1,0:T(8,128)S(1)}, u32[]{:S(2)}, u32[]{:S(2)}) collective-permute-start(f32[7,32,128]{2,1,0:T(8,128)S(1)} %collective-permute-done.10.refs_1_), channel_id=1, source_target_pairs={{0,1},{1,0},{2,3},{3,2},{4,5},{5,4},{6,7},{7,6},{8,9},{9,8},{10,11... | collective-permute-start | bytes 344072 | tf_op jit(solution)/shard_map/ppermute | solution.py:769
  42.5 1.3 %collective-permute-start.16 = (f32[7,32,128]{2,1,0:T(8,128)S(1)}, f32[7,32,128]{2,1,0:T(8,128)S(1)}, u32[]{:S(2)}, u32[]{:S(2)}) collective-permute-start(f32[7,32,128]{2,1,0:T(8,128)S(1)} %collective-permute-done.11.refs_2_), channel_id=1, source_target_pairs={{0,1},{1,0},{2,3},{3,2},{4,5},{5,4},{6,7},{7,6},{8,9},{9,8},{10,11... | collective-permute-start | bytes 344072 | tf_op jit(solution)/shard_map/ppermute | solution.py:769
  42.5 1.5 %collective-permute-start.17 = (f32[7,32,128]{2,1,0:T(8,128)S(1)}, f32[7,32,128]{2,1,0:T(8,128)S(1)}, u32[]{:S(2)}, u32[]{:S(2)}) collective-permute-start(f32[7,32,128]{2,1,0:T(8,128)S(1)} %collective-permute-done.12.refs_3_), channel_id=1, source_target_pairs={{0,1},{1,0},{2,3},{3,2},{4,5},{5,4},{6,7},{7,6},{8,9},{9,8},{10,11... | collective-permute-start | bytes 344072 | tf_op jit(solution)/shard_map/ppermute | solution.py:769

commit v21 on v19

--- a/solution.py
+++ b/solution.py
@@ -887,7 +887,9 @@
         count = sizes.span_count >> index
         scratch += [(count + 1, *tile)] + [(count, *tile)] * 3 + [(count + 2, *tile)] + [(count, *tile)] * 2
         scratch += [(count + 2, *tile)] * 2
-    blocks, received[3] = lax.optimization_barrier((blocks, received[3]))
+    own_part = beside(blocks[:1], sizes)
+    blocks, received[3], own_part = lax.optimization_barrier((blocks, received[3], own_part))
+    swapped = [first + rest for first, rest in zip(own_part, beside(blocks[1:], sizes))]
     (coarse,) = call(
         functools.partial(coarse_kernel, sizes, stride, radix),
         "coarse",
@@ -895,7 +897,7 @@
         [(n3 + 2, *tile)],
         scratch,
         place,
-        [*blocks, *sum(beside(blocks, sizes), [])],
+        [*blocks, *sum(swapped, [])],
     )
     scratch = [(n1 + 2, *held[1]), (n2 + 2, *held[2]), diffusivity.shape, (2, *held[0]), (2, *held[1])]
     scratch += [(n3 + 2, *held[2]), (n2 + 2, *held[1]), (n1 + 2, *held[0])]

time: 50.1 us -> 54.4 us (1.086)
  the two profiles are of different devices: /device:TPU:0 before, /device:TPU:16 now
where the time goes in v21:
time: 54.4 us; the launch traced here: 54.2 us
  starting transfers between devices  21.5 us (40%)
  waiting for transfers between devices  17.9 us (33%)
  Pallas kernels  12.5 us (23%)
  local copies, waits for them, and re-layouts  2.09 us (4%)
    pallas_call x7, Pallas kernels, call(): pl.pallas_call(body, name=name, out_shape=[jax.ShapeDtypeStruct(shape, f3...  12.5 us
    ppermute x5, starting transfers between devices, exchange(): lax.ppermute(value, 'span', route)  12 us
    ppermute x5, waiting for transfers between devices, exchange(): lax.ppermute(value, 'span', route)  11.5 us
    ppermute x6, starting transfers between devices, swap(): lax.ppermute(others.get(step, value), 'span', [(device, device ^ step * s...  7.56 us
    ppermute x6, waiting for transfers between devices, swap(): lax.ppermute(others.get(step, value), 'span', [(device, device ^ step * s...  2.63 us
    ppermute x6, waiting for transfers between devices, beside(): lax.ppermute(value, 'width', [(0, 1), (1, 0)])  2.46 us
    unnamed x6, local copies, waits for them, and re-layouts  2.09 us
    ppermute x3, waiting for transfers between devices, edge_columns(): return [lax.ppermute(edges[0], 'width', [(0, 1), (1, 0)])]  1.27 us
  transfers between devices with their start and end apart: 20, of which 13 were waited for; matrix products, arithmetic and copies ran while one was open for 0% of the time, Pallas kernels for 11%

profile of v21, /device:TPU:16, one launch (start us, length us, event | category | flops | bytes accessed | tf_op | source)
XLA Modules:
  0.0 54.2 jit_solution(5530014507481763224)
XLA Ops:
  0.1 1.0 %copy-done = f32[32,8,512]{2,1,0:T(8,128)S(1)} copy-done((f32[32,8,512]{2,1,0:T(8,128)S(1)}, f32[32,8,512]{2,1,0:T(8,128)}, u32[]{:S(2)}) %copy-start) | copy-done | bytes 524312
  1.1 1.0 %copy-done.1 = f32[32,8,512]{2,1,0:T(8,128)S(1)} copy-done((f32[32,8,512]{2,1,0:T(8,128)S(1)}, f32[32,8,512]{2,1,0:T(8,128)}, u32[]{:S(2)}) %copy-start.1) | copy-done | bytes 524312
  2.2 1.1 %start.1 = (f32[2,8,32,512]{3,2,1,0:T(8,128)S(1)}, f32[8,32,256]{2,1,0:T(8,128)S(1)}, f32[4,32,128]{2,1,0:T(8,128)S(1)}, f32[12,32,128]{2,1,0:T(8,128)S(1)}, f32...) custom-call(s32[2]{0:T(128)S(1)} %pad_add_fusion.place, f32[32,8,512]{2,1,0:T(8,128)S(1)} %copy-done, ...), custom_call_target="tpu_custom_call" | custom-call | flops 1264999936 | bytes 4059000 | tf_op jit(solution)/shard_map/start/pallas_call | solution.py:745
  3.3 1.6 %collective-permute-start.3 = (f32[12,32,128]{2,1,0:T(8,128)S(1)}, f32[12,32,128]{2,1,0:T(8,128)S(1)}, u32[]{:S(2)}, u32[]{:S(2)}) collective-permute-start(f32[12,32,128]{2,1,0:T(8,128)S(1)} %get-tuple-element.49), channel_id=1, source_target_pairs={{0,2},{2,0},{4,6},{6,4},{8,10},{10,8},{12,14},{14,12},{16,18},{18,... | collective-permute-start | bytes 589832 | tf_op jit(solution)/shard_map/ppermute | solution.py:801
  4.9 3.3 %collective-permute-start.4 = (f32[12,32,128]{2,1,0:T(8,128)S(1)}, f32[12,32,128]{2,1,0:T(8,128)S(1)}, u32[]{:S(2)}, u32[]{:S(2)}) collective-permute-start(f32[12,32,128]{2,1,0:T(8,128)S(1)} %get-tuple-element.50), channel_id=1, source_target_pairs={{2,4},{4,2},{6,8},{8,6},{10,12},{12,10},{14,16},{16,14},{18,20},{2... | collective-permute-start | bytes 589832 | tf_op jit(solution)/shard_map/ppermute | solution.py:801
  9.5 0.8 %collective-permute-done.2.refs_6_.refs_14_ = f32[8,32,128]{2,1,0:T(8,128)S(1)} collective-permute-done((f32[8,32,128]{2,1,0:T(8,128)S(1)}, f32[8,32,128]{2,1,0:T(8,128)S(1)}, u32[]{:S(2)}, u32[]{:S(2)}) %collective-permute-start.2) | collective-permute-done | bytes 131104 | tf_op jit(solution)/shard_map/ppermute | solution.py:773
  10.8 1.8 %inner.1 = (f32[8,32,128]{2,1,0:T(8,128)S(1)}, f32[4,32,128]{2,1,0:T(8,128)S(1)}, f32[35,32,640]{2,1,0:T(8,128)S(1)}, f32[17,32,384]{2,1,0:T(8,128)S(1)}, f32[5,32,256]{2,1,0:T(8,128)S(1)}) custom-call(s32[2]{0:T(128)S(1)} %pad_add_fusion.place, f32[2,8,32,512]{3,2,1,0:T(8,128)S(1)} %get-tuple-element.42.refs_0_.refs_10_, ...), custom_call_target="tpu_custom_call" | custom-call | flops 575000000 | bytes 1845000 | tf_op jit(solution)/shard_map/inner/pallas_call | solution.py:745
  12.6 2.4 %collective-permute-done.4.refs_8_ = f32[12,32,128]{2,1,0:T(8,128)S(1)} collective-permute-done((f32[12,32,128]{2,1,0:T(8,128)S(1)}, f32[12,32,128]{2,1,0:T(8,128)S(1)}, u32[]{:S(2)}, u32[]{:S(2)}) %collective-permute-start.4) | collective-permute-done | bytes 196640 | tf_op jit(solution)/shard_map/ppermute | solution.py:801
  15.5 0.9 %collective-permute-done.5.refs_9_ = f32[12,32,128]{2,1,0:T(8,128)S(1)} collective-permute-done((f32[12,32,128]{2,1,0:T(8,128)S(1)}, f32[12,32,128]{2,1,0:T(8,128)S(1)}, u32[]{:S(2)}, u32[]{:S(2)}) %collective-permute-start.5) | collective-permute-done | bytes 196640 | tf_op jit(solution)/shard_map/ppermute | solution.py:765
  16.7 2.3 %down.1 = (f32[6,32,640]{2,1,0:T(8,128)S(1)}, f32[26,32,384]{2,1,0:T(8,128)S(1)}, f32[24,32,256]{2,1,0:T(8,128)S(1)}, f32[3,32,128]{2,1,0:T(8,128)S(1)}, f32[5,3...) custom-call(s32[2]{0:T(128)S(1)} %pad_add_fusion.place, ...), custom_call_target="tpu_custom_call" | custom-call | flops 2875000064 | bytes 9225000 | tf_op jit(solution)/shard_map/down/pallas_call | solution.py:745
  19.1 0.8 %collective-permute-start.8 = (f32[5,32,128]{2,1,0:T(8,128)S(1)}, f32[5,32,128]{2,1,0:T(8,128)S(1)}, u32[]{:S(2)}, u32[]{:S(2)}) collective-permute-start(f32[5,32,128]{2,1,0:T(8,128)S(1)} %get-tuple-element.64), channel_id=1, source_target_pairs={{0,4},{2,6},{4,0},{6,2},{8,12},{10,14},{12,8},{14,10},{16,20},{18,... | collective-permute-start | bytes 245768 | tf_op jit(solution)/shard_map/ppermute | solution.py:791
  19.9 2.4 %collective-permute-start.9 = (f32[3,32,128]{2,1,0:T(8,128)S(1)}, f32[3,32,128]{2,1,0:T(8,128)S(1)}, u32[]{:S(2)}, u32[]{:S(2)}) collective-permute-start(f32[3,32,128]{2,1,0:T(8,128)S(1)} %get-tuple-element.63.refs_0_), channel_id=1, source_target_pairs={{0,6},{2,4},{4,2},{6,0},{8,14},{10,12},{12,10},{14,8},{16,22},{18,... | collective-permute-start | bytes 147464 | tf_op jit(solution)/shard_map/ppermute | solution.py:791
  22.6 1.7 %collective-permute-start.18 = (f32[12,32,128]{2,1,0:T(8,128)S(1)}, f32[12,32,128]{2,1,0:T(8,128)S(1)}, u32[]{:S(2)}, u32[]{:S(2)}) collective-permute-start(f32[12,32,128]{2,1,0:T(8,128)S(1)} %get-tuple-element.71), channel_id=1, source_target_pairs={{0,2},{2,0},{4,6},{6,4},{8,10},{10,8},{12,14},{14,12},{16,18},{18,... | collective-permute-start | bytes 589832 | tf_op jit(solution)/shard_map/ppermute | solution.py:801
  24.3 1.1 %collective-permute-done.9.refs_3_ = f32[3,32,128]{2,1,0:T(8,128)S(1)} collective-permute-done((f32[3,32,128]{2,1,0:T(8,128)S(1)}, f32[3,32,128]{2,1,0:T(8,128)S(1)}, u32[]{:S(2)}, u32[]{:S(2)}) %collective-permute-start.9) | collective-permute-done | bytes 49184 | tf_op jit(solution)/shard_map/ppermute | solution.py:791
  25.4 1.5 %collective-permute-done.7.refs_1_ = f32[3,32,128]{2,1,0:T(8,128)S(1)} collective-permute-done((f32[3,32,128]{2,1,0:T(8,128)S(1)}, f32[3,32,128]{2,1,0:T(8,128)S(1)}, u32[]{:S(2)}, u32[]{:S(2)}) %collective-permute-start.7) | collective-permute-done | bytes 49184 | tf_op jit(solution)/shard_map/ppermute | solution.py:791
  26.9 0.7 %merge.1.refs_0_ = f32[7,32,128]{2,1,0:T(8,128)S(1)} custom-call(s32[2]{0:T(128)S(1)} %pad_add_fusion.place, f32[3,32,128]{2,1,0:T(8,128)S(1)} %get-tuple-element.63.refs_0_, f32[3,32,128]{2,1,0:T(8,128)S(1)} %collective-permute-done.7.refs_1_, f32[5,32,128]{2,1,0:T(8,128)S(1)} %collective-permute-done.8.refs_2_, ...), custom_call_target="tpu_custom_call" | custom-call | flops 1035000000 | bytes 3321000 | tf_op jit(solution)/shard_map/merge/pallas_call | solution.py:745
  28.2 3.5 %collective-permute-start.11 = (f32[7,32,128]{2,1,0:T(8,128)S(1)}, f32[7,32,128]{2,1,0:T(8,128)S(1)}, u32[]{:S(2)}, u32[]{:S(2)}) collective-permute-start(f32[7,32,128]{2,1,0:T(8,128)S(1)} %merge.1.refs_0_), channel_id=1, source_target_pairs={{0,16},{2,18},{4,20},{6,22},{8,24},{10,26},{12,28},{14,30},{16,0},... | collective-permute-start | bytes 344072 | tf_op jit(solution)/shard_map/ppermute | solution.py:791
  31.7 2.0 %collective-permute-start.13 = (f32[2,32,128]{2,1,0:T(8,128)S(1)}, f32[2,32,128]{2,1,0:T(8,128)S(1)}, u32[]{:S(2)}, u32[]{:S(2)}) collective-permute-start(f32[2,32,128]{2,1,0:T(8,128)S(1)} %get-tuple-element.65), channel_id=1, source_target_pairs={{4,8},{8,4},{6,10},{10,6},{12,16},{16,12},{14,18},{18,14},{20,24},... | collective-permute-start | bytes 98312 | tf_op jit(solution)/shard_map/ppermute | solution.py:801
  33.7 7.5 %collective-permute-done.13.refs_3_ = f32[2,32,128]{2,1,0:T(8,128)S(1)} collective-permute-done((f32[2,32,128]{2,1,0:T(8,128)S(1)}, f32[2,32,128]{2,1,0:T(8,128)S(1)}, u32[]{:S(2)}, u32[]{:S(2)}) %collective-permute-start.13) | collective-permute-done | bytes 32800 | tf_op jit(solution)/shard_map/ppermute | solution.py:801
  41.2 3.6 %collective-permute-start.19 = (f32[12,32,128]{2,1,0:T(8,128)S(1)}, f32[12,32,128]{2,1,0:T(8,128)S(1)}, u32[]{:S(2)}, u32[]{:S(2)}) collective-permute-start(f32[12,32,128]{2,1,0:T(8,128)S(1)} %get-tuple-element.74), channel_id=1, source_target_pairs={{2,4},{4,2},{6,8},{8,6},{10,12},{12,10},{14,16},{16,14},{18,20},{2... | collective-permute-start | bytes 589832 | tf_op jit(solution)/shard_map/ppermute | solution.py:801
  45.5 0.7 %collective-permute-done.15.refs_5_ = f32[7,32,128]{2,1,0:T(8,128)S(1)} collective-permute-done((f32[7,32,128]{2,1,0:T(8,128)S(1)}, f32[7,32,128]{2,1,0:T(8,128)S(1)}, u32[]{:S(2)}, u32[]{:S(2)}) %collective-permute-start.15) | collective-permute-done | bytes 114720 | tf_op jit(solution)/shard_map/ppermute | solution.py:765
  46.7 2.7 %coarse.1 = f32[3,32,128]{2,1,0:T(8,128)S(1)} custom-call(s32[2]{0:T(128)S(1)} %pad_add_fusion.place, f32[7,32,128]{2,1,0:T(8,128)S(1)} %merge.1.refs_0_, f32[7,32,128]{2,1,0:T(8,128)S(1)} %collective-permute-done.10.refs_1_, f32[7,32,128]{2,1,0:T(8,128)S(1)} %collective-permute-done.11.refs_2_, f32[7,32,128]{2,1,0:T(8,128)S(1)} %collective-permute-done.12.refs_3_, ...), custom_call_target="tpu_custom_call" | custom-call | flops 805000000 | bytes 2583000 | tf_op jit(solution)/shard_map/coarse/pallas_call | solution.py:745
  49.4 1.6 %collective-permute-done.19.refs_1_ = f32[12,32,128]{2,1,0:T(8,128)S(1)} collective-permute-done((f32[12,32,128]{2,1,0:T(8,128)S(1)}, f32[12,32,128]{2,1,0:T(8,128)S(1)}, u32[]{:S(2)}, u32[]{:S(2)}) %collective-permute-start.19) | collective-permute-done | bytes 196640 | tf_op jit(solution)/shard_map/ppermute | solution.py:801
  51.0 3.1 %up.1 = f32[32,8,512]{2,1,0:T(8,128)} custom-call(s32[2]{0:T(128)S(1)} %pad_add_fusion.place, f32[3,32,128]{2,1,0:T(8,128)S(1)} %coarse.1, f32[12,32,128]{2,1,0:T(8,128)S(1)} %collective-permute-done.18.refs_0_, f32[12,32,128]{2,1,0:T(8,128)S(1)} %collective-permute-done.19.refs_1_, f32[5,32,128]{2,1,0:T(8,128)S(1)} %collective-permute-done.8.refs_2_, ...), custom_call_target="tpu_custom_call" | custom-call | flops 3449999872 | bytes 11070000 | tf_op jit(solution)/shard_map/up/pallas_call | solution.py:745
  (30 shorter events, 4.8 us)
Async XLA Ops:
  0.1 1.0 %copy-start = (f32[32,8,512]{2,1,0:T(8,128)S(1)}, f32[32,8,512]{2,1,0:T(8,128)}, u32[]{:S(2)}) copy-start(f32[32,8,512]{2,1,0:T(8,128)} %conduct.1) | copy-start | bytes 1572868
  1.1 1.0 %copy-start.1 = (f32[32,8,512]{2,1,0:T(8,128)S(1)}, f32[32,8,512]{2,1,0:T(8,128)}, u32[]{:S(2)}) copy-start(f32[32,8,512]{2,1,0:T(8,128)} %binding.1) | copy-start | bytes 1572868
  2.2 6.0 %copy-start.2 = (f32[32,8,512]{2,1,0:T(8,128)S(1)}, f32[32,8,512]{2,1,0:T(8,128)}, u32[]{:S(2)}) copy-start(f32[32,8,512]{2,1,0:T(8,128)} %right_side.1) | copy-start | bytes 1572868
  3.3 9.3 %collective-permute-start.3 = (f32[12,32,128]{2,1,0:T(8,128)S(1)}, f32[12,32,128]{2,1,0:T(8,128)S(1)}, u32[]{:S(2)}, u32[]{:S(2)}) collective-permute-start(f32[12,32,128]{2,1,0:T(8,128)S(1)} %get-tuple-element.49), channel_id=1, source_target_pairs={{0,2},{2,0},{4,6},{6,4},{8,10},{10,8},{12,14},{14,12},{16,18},{18,... | collective-permute-start | bytes 589832 | tf_op jit(solution)/shard_map/ppermute | solution.py:801
  4.9 10.1 %collective-permute-start.4 = (f32[12,32,128]{2,1,0:T(8,128)S(1)}, f32[12,32,128]{2,1,0:T(8,128)S(1)}, u32[]{:S(2)}, u32[]{:S(2)}) collective-permute-start(f32[12,32,128]{2,1,0:T(8,128)S(1)} %get-tuple-element.50), channel_id=1, source_target_pairs={{2,4},{4,2},{6,8},{8,6},{10,12},{12,10},{14,16},{16,14},{18,20},{2... | collective-permute-start | bytes 589832 | tf_op jit(solution)/shard_map/ppermute | solution.py:801
  8.8 1.4 %collective-permute-start.2 = (f32[8,32,128]{2,1,0:T(8,128)S(1)}, f32[8,32,128]{2,1,0:T(8,128)S(1)}, u32[]{:S(2)}, u32[]{:S(2)}) collective-permute-start(f32[8,32,128]{2,1,0:T(8,128)S(1)} %get-tuple-element.48), channel_id=1, source_target_pairs={{0,1},{1,0},{2,3},{3,2},{4,5},{5,4},{6,7},{7,6},{8,9},{9,8},{10,11... | collective-permute-start | bytes 393224 | tf_op jit(solution)/shard_map/ppermute | solution.py:773
  8.9 1.5 %collective-permute-start = (f32[8,32,128]{2,1,0:T(8,128)S(1)}, f32[8,32,128]{2,1,0:T(8,128)S(1)}, u32[]{:S(2)}, u32[]{:S(2)}) collective-permute-start(f32[8,32,128]{2,1,0:T(8,128)S(1)} %get-tuple-element.46), channel_id=1, source_target_pairs={{0,1},{1,0},{2,3},{3,2},{4,5},{5,4},{6,7},{7,6},{8,9},{9,8},{10,11... | collective-permute-start | bytes 393224 | tf_op jit(solution)/shard_map/ppermute | solution.py:773
  9.4 1.3 %collective-permute-start.1 = (f32[8,32,128]{2,1,0:T(8,128)S(1)}, f32[8,32,128]{2,1,0:T(8,128)S(1)}, u32[]{:S(2)}, u32[]{:S(2)}) collective-permute-start(f32[8,32,128]{2,1,0:T(8,128)S(1)} %get-tuple-element.47), channel_id=1, source_target_pairs={{0,1},{1,0},{2,3},{3,2},{4,5},{5,4},{6,7},{7,6},{8,9},{9,8},{10,11... | collective-permute-start | bytes 393224 | tf_op jit(solution)/shard_map/ppermute | solution.py:773
  15.0 1.4 %collective-permute-start.5 = (f32[12,32,128]{2,1,0:T(8,128)S(1)}, f32[12,32,128]{2,1,0:T(8,128)S(1)}, u32[]{:S(2)}, u32[]{:S(2)}) collective-permute-start(f32[12,32,128]{2,1,0:T(8,128)S(1)} %collective-permute-done.3.refs_7_), channel_id=1, source_target_pairs={{0,1},{1,0},{2,3},{3,2},{4,5},{5,4},{6,7},{7,6},{8,9},{9,8},{10,11... | collective-permute-start | bytes 589832 | tf_op jit(solution)/shard_map/ppermute | solution.py:765
  15.0 1.7 %collective-permute-start.6 = (f32[12,32,128]{2,1,0:T(8,128)S(1)}, f32[12,32,128]{2,1,0:T(8,128)S(1)}, u32[]{:S(2)}, u32[]{:S(2)}) collective-permute-start(f32[12,32,128]{2,1,0:T(8,128)S(1)} %collective-permute-done.4.refs_8_), channel_id=1, source_target_pairs={{0,1},{1,0},{2,3},{3,2},{4,5},{5,4},{6,7},{7,6},{8,9},{9,8},{10,11... | collective-permute-start | bytes 589832 | tf_op jit(solution)/shard_map/ppermute | solution.py:765
  19.1 7.8 %collective-permute-start.8 = (f32[5,32,128]{2,1,0:T(8,128)S(1)}, f32[5,32,128]{2,1,0:T(8,128)S(1)}, u32[]{:S(2)}, u32[]{:S(2)}) collective-permute-start(f32[5,32,128]{2,1,0:T(8,128)S(1)} %get-tuple-element.64), channel_id=1, source_target_pairs={{0,4},{2,6},{4,0},{6,2},{8,12},{10,14},{12,8},{14,10},{16,20},{18,... | collective-permute-start | bytes 245768 | tf_op jit(solution)/shard_map/ppermute | solution.py:791
  19.9 5.5 %collective-permute-start.9 = (f32[3,32,128]{2,1,0:T(8,128)S(1)}, f32[3,32,128]{2,1,0:T(8,128)S(1)}, u32[]{:S(2)}, u32[]{:S(2)}) collective-permute-start(f32[3,32,128]{2,1,0:T(8,128)S(1)} %get-tuple-element.63.refs_0_), channel_id=1, source_target_pairs={{0,6},{2,4},{4,2},{6,0},{8,14},{10,12},{12,10},{14,8},{16,22},{18,... | collective-permute-start | bytes 147464 | tf_op jit(solution)/shard_map/ppermute | solution.py:791
  22.2 4.7 %collective-permute-start.7 = (f32[3,32,128]{2,1,0:T(8,128)S(1)}, f32[3,32,128]{2,1,0:T(8,128)S(1)}, u32[]{:S(2)}, u32[]{:S(2)}) collective-permute-start(f32[3,32,128]{2,1,0:T(8,128)S(1)} %get-tuple-element.63.refs_0_), channel_id=1, source_target_pairs={{0,2},{2,0},{4,6},{6,4},{8,10},{10,8},{12,14},{14,12},{16,18},{18,... | collective-permute-start | bytes 147464 | tf_op jit(solution)/shard_map/ppermute | solution.py:791
  22.6 9.1 %collective-permute-start.18 = (f32[12,32,128]{2,1,0:T(8,128)S(1)}, f32[12,32,128]{2,1,0:T(8,128)S(1)}, u32[]{:S(2)}, u32[]{:S(2)}) collective-permute-start(f32[12,32,128]{2,1,0:T(8,128)S(1)} %get-tuple-element.71), channel_id=1, source_target_pairs={{0,2},{2,0},{4,6},{6,4},{8,10},{10,8},{12,14},{14,12},{16,18},{18,... | collective-permute-start | bytes 589832 | tf_op jit(solution)/shard_map/ppermute | solution.py:801
  27.6 17.1 %collective-permute-start.14 = (f32[7,32,128]{2,1,0:T(8,128)S(1)}, f32[7,32,128]{2,1,0:T(8,128)S(1)}, u32[]{:S(2)}, u32[]{:S(2)}) collective-permute-start(f32[7,32,128]{2,1,0:T(8,128)S(1)} %merge.1.refs_0_), channel_id=1, source_target_pairs={{0,1},{1,0},{2,3},{3,2},{4,5},{5,4},{6,7},{7,6},{8,9},{9,8},{10,11... | collective-permute-start | bytes 344072 | tf_op jit(solution)/shard_map/ppermute | solution.py:765
  27.7 17.1 %collective-permute-start.12 = (f32[7,32,128]{2,1,0:T(8,128)S(1)}, f32[7,32,128]{2,1,0:T(8,128)S(1)}, u32[]{:S(2)}, u32[]{:S(2)}) collective-permute-start(f32[7,32,128]{2,1,0:T(8,128)S(1)} %merge.1.refs_0_), channel_id=1, source_target_pairs={{0,24},{2,26},{4,28},{6,30},{8,16},{10,18},{12,20},{14,22},{16,8},... | collective-permute-start | bytes 344072 | tf_op jit(solution)/shard_map/ppermute | solution.py:791
  28.2 16.6 %collective-permute-start.11 = (f32[7,32,128]{2,1,0:T(8,128)S(1)}, f32[7,32,128]{2,1,0:T(8,128)S(1)}, u32[]{:S(2)}, u32[]{:S(2)}) collective-permute-start(f32[7,32,128]{2,1,0:T(8,128)S(1)} %merge.1.refs_0_), channel_id=1, source_target_pairs={{0,16},{2,18},{4,20},{6,22},{8,24},{10,26},{12,28},{14,30},{16,0},... | collective-permute-start | bytes 344072 | tf_op jit(solution)/shard_map/ppermute | solution.py:791
  31.7 13.1 %collective-permute-start.10 = (f32[7,32,128]{2,1,0:T(8,128)S(1)}, f32[7,32,128]{2,1,0:T(8,128)S(1)}, u32[]{:S(2)}, u32[]{:S(2)}) collective-permute-start(f32[7,32,128]{2,1,0:T(8,128)S(1)} %merge.1.refs_0_), channel_id=1, source_target_pairs={{0,8},{2,10},{4,12},{6,14},{8,0},{10,2},{12,4},{14,6},{16,24},{18,... | collective-permute-start | bytes 344072 | tf_op jit(solution)/shard_map/ppermute | solution.py:791
  31.7 9.5 %collective-permute-start.13 = (f32[2,32,128]{2,1,0:T(8,128)S(1)}, f32[2,32,128]{2,1,0:T(8,128)S(1)}, u32[]{:S(2)}, u32[]{:S(2)}) collective-permute-start(f32[2,32,128]{2,1,0:T(8,128)S(1)} %get-tuple-element.65), channel_id=1, source_target_pairs={{4,8},{8,4},{6,10},{10,6},{12,16},{16,12},{14,18},{18,14},{20,24},... | collective-permute-start | bytes 98312 | tf_op jit(solution)/shard_map/ppermute | solution.py:801
  41.2 9.9 %collective-permute-start.19 = (f32[12,32,128]{2,1,0:T(8,128)S(1)}, f32[12,32,128]{2,1,0:T(8,128)S(1)}, u32[]{:S(2)}, u32[]{:S(2)}) collective-permute-start(f32[12,32,128]{2,1,0:T(8,128)S(1)} %get-tuple-element.74), channel_id=1, source_target_pairs={{2,4},{4,2},{6,8},{8,6},{10,12},{12,10},{14,16},{16,14},{18,20},{2... | collective-permute-start | bytes 589832 | tf_op jit(solution)/shard_map/ppermute | solution.py:801
  44.8 1.4 %collective-permute-start.15 = (f32[7,32,128]{2,1,0:T(8,128)S(1)}, f32[7,32,128]{2,1,0:T(8,128)S(1)}, u32[]{:S(2)}, u32[]{:S(2)}) collective-permute-start(f32[7,32,128]{2,1,0:T(8,128)S(1)} %collective-permute-done.10.refs_1_), channel_id=1, source_target_pairs={{0,1},{1,0},{2,3},{3,2},{4,5},{5,4},{6,7},{7,6},{8,9},{9,8},{10,11... | collective-permute-start | bytes 344072 | tf_op jit(solution)/shard_map/ppermute | solution.py:765
  44.9 1.5 %collective-permute-start.16 = (f32[7,32,128]{2,1,0:T(8,128)S(1)}, f32[7,32,128]{2,1,0:T(8,128)S(1)}, u32[]{:S(2)}, u32[]{:S(2)}) collective-permute-start(f32[7,32,128]{2,1,0:T(8,128)S(1)} %collective-permute-done.11.refs_2_), channel_id=1, source_target_pairs={{0,1},{1,0},{2,3},{3,2},{4,5},{5,4},{6,7},{7,6},{8,9},{9,8},{10,11... | collective-permute-start | bytes 344072 | tf_op jit(solution)/shard_map/ppermute | solution.py:765
  45.4 1.3 %collective-permute-start.17 = (f32[7,32,128]{2,1,0:T(8,128)S(1)}, f32[7,32,128]{2,1,0:T(8,128)S(1)}, u32[]{:S(2)}, u32[]{:S(2)}) collective-permute-start(f32[7,32,128]{2,1,0:T(8,128)S(1)} %collective-permute-done.12.refs_3_), channel_id=1, source_target_pairs={{0,1},{1,0},{2,3},{3,2},{4,5},{5,4},{6,7},{7,6},{8,9},{9,8},{10,11... | collective-permute-start | bytes 344072 | tf_op jit(solution)/shard_map/ppermute | solution.py:765

commit v22 on v19

--- a/solution.py
+++ b/solution.py
@@ -849,8 +849,11 @@
         place,
         [own0, own1, own2, turned, *borders],
     )
-    halos, inner = lax.optimization_barrier((halos, inner))
-    sides = beside(halos, sizes)
+    early, inner = lax.optimization_barrier((halos[0], inner))
+    first_sides = beside([early], sizes)
+    second, first_sides = lax.optimization_barrier((halos[1], first_sides))
+    halos = [early, second]
+    sides = [one + two for one, two in zip(first_sides, beside([second], sizes))]
     downs = call(
         functools.partial(down_kernel, sizes),
         "down",

time: 50.1 us -> 50.6 us (level)
  waiting for transfers between devices: 13.2 us -> 14.2 us
    ppermute x6, waiting for transfers between devices: 2.19 us -> 3.71 us  [beside(): lax.ppermute(value, 'width', [(0, 1), (1, 0)])]
    ppermute x3, waiting for transfers between devices: 1.27 us -> 0.6 us  [edge_columns(): return [lax.ppermute(edges[0], 'width', [(0, 1), (1, 0)])]]
    ppermute x5, starting transfers between devices: 7.01 us -> 6.42 us  [exchange(): lax.ppermute(value, 'span', route)]
    ppermute x6, starting transfers between devices: 12.6 us -> 13.1 us  [swap(): lax.ppermute(others.get(step, value), 'span', [(device, device ^ step * s...]
  transfers between devices with their start and end apart: 20 -> 20, of which waited for: 13 -> 14; matrix products, arithmetic and copies ran while one was open for 0% -> 0% of each run, Pallas kernels for 12% -> 12%
where the time goes in v22:
time: 50.6 us; the launch traced here: 50.3 us
  starting transfers between devices  21.4 us (42%)
  waiting for transfers between devices  14.2 us (28%)
  Pallas kernels  12.5 us (25%)
  local copies, waits for them, and re-layouts  2.09 us (4%)
    ppermute x6, starting transfers between devices, swap(): lax.ppermute(others.get(step, value), 'span', [(device, device ^ step * s...  13.1 us
    pallas_call x7, Pallas kernels, call(): pl.pallas_call(body, name=name, out_shape=[jax.ShapeDtypeStruct(shape, f3...  12.5 us
    ppermute x6, waiting for transfers between devices, swap(): lax.ppermute(others.get(step, value), 'span', [(device, device ^ step * s...  9.38 us
    ppermute x5, starting transfers between devices, exchange(): lax.ppermute(value, 'span', route)  6.42 us
    ppermute x6, waiting for transfers between devices, beside(): lax.ppermute(value, 'width', [(0, 1), (1, 0)])  3.71 us
    unnamed x6, local copies, waits for them, and re-layouts  2.09 us
    ppermute x6, starting transfers between devices, beside(): lax.ppermute(value, 'width', [(0, 1), (1, 0)])  1.16 us
  transfers between devices with their start and end apart: 20, of which 14 were waited for; matrix products, arithmetic and copies ran while one was open for 0% of the time, Pallas kernels for 12%

profile of v22, /device:TPU:0, one launch (start us, length us, event | category | flops | bytes accessed | tf_op | source)
XLA Modules:
  0.0 50.3 jit_solution(12926145708240493024)
XLA Ops:
  0.1 1.0 %copy-done = f32[32,8,512]{2,1,0:T(8,128)S(1)} copy-done((f32[32,8,512]{2,1,0:T(8,128)S(1)}, f32[32,8,512]{2,1,0:T(8,128)}, u32[]{:S(2)}) %copy-start) | copy-done | bytes 524312
  1.1 1.0 %copy-done.1 = f32[32,8,512]{2,1,0:T(8,128)S(1)} copy-done((f32[32,8,512]{2,1,0:T(8,128)S(1)}, f32[32,8,512]{2,1,0:T(8,128)}, u32[]{:S(2)}) %copy-start.1) | copy-done | bytes 524312
  2.2 1.1 %start.1 = (f32[2,8,32,512]{3,2,1,0:T(8,128)S(1)}, f32[8,32,256]{2,1,0:T(8,128)S(1)}, f32[4,32,128]{2,1,0:T(8,128)S(1)}, f32[12,32,128]{2,1,0:T(8,128)S(1)}, f32...) custom-call(s32[2]{0:T(128)S(1)} %pad_add_fusion.place, f32[32,8,512]{2,1,0:T(8,128)S(1)} %copy-done, ...), custom_call_target="tpu_custom_call" | custom-call | flops 1264999936 | bytes 4059000 | tf_op jit(solution)/shard_map/start/pallas_call | solution.py:745
  3.3 3.0 %collective-permute-start.3 = (f32[12,32,128]{2,1,0:T(8,128)S(1)}, f32[12,32,128]{2,1,0:T(8,128)S(1)}, u32[]{:S(2)}, u32[]{:S(2)}) collective-permute-start(f32[12,32,128]{2,1,0:T(8,128)S(1)} %get-tuple-element.49), channel_id=1, source_target_pairs={{0,2},{2,0},{4,6},{6,4},{8,10},{10,8},{12,14},{14,12},{16,18},{18,... | collective-permute-start | bytes 589832 | tf_op jit(solution)/shard_map/ppermute | solution.py:801
  6.3 0.7 %turn.1 = (f32[8,32,512]{2,1,0:T(8,128)S(1)}, f32[8,32,128]{2,1,0:T(8,128)S(1)}) custom-call(s32[2]{0:T(128)S(1)} %pad_add_fusion.place, f32[32,8,512]{2,1,0:T(8,128)S(1)} %copy-done.2), custom_call_target="tpu_custom_call" | custom-call | flops 805000000 | bytes 2583000 | tf_op jit(solution)/shard_map/turn/pallas_call | solution.py:745
  7.6 0.7 %collective-permute-start.4 = (f32[12,32,128]{2,1,0:T(8,128)S(1)}, f32[12,32,128]{2,1,0:T(8,128)S(1)}, u32[]{:S(2)}, u32[]{:S(2)}) collective-permute-start(f32[12,32,128]{2,1,0:T(8,128)S(1)} %get-tuple-element.56), channel_id=1, source_target_pairs={{2,4},{4,2},{6,8},{8,6},{10,12},{12,10},{14,16},{16,14},{18,20},{2... | collective-permute-start | bytes 589832 | tf_op jit(solution)/shard_map/ppermute | solution.py:801
  8.9 1.8 %inner.1 = (f32[8,32,128]{2,1,0:T(8,128)S(1)}, f32[4,32,128]{2,1,0:T(8,128)S(1)}, f32[35,32,640]{2,1,0:T(8,128)S(1)}, f32[17,32,384]{2,1,0:T(8,128)S(1)}, f32[5,32,256]{2,1,0:T(8,128)S(1)}) custom-call(s32[2]{0:T(128)S(1)} %pad_add_fusion.place, f32[2,8,32,512]{3,2,1,0:T(8,128)S(1)} %get-tuple-element.42.refs_0_.refs_10_, ...), custom_call_target="tpu_custom_call" | custom-call | flops 575000000 | bytes 1845000 | tf_op jit(solution)/shard_map/inner/pallas_call | solution.py:745
  11.2 1.4 %collective-permute-done.5.refs_9_ = f32[12,32,128]{2,1,0:T(8,128)S(1)} collective-permute-done((f32[12,32,128]{2,1,0:T(8,128)S(1)}, f32[12,32,128]{2,1,0:T(8,128)S(1)}, u32[]{:S(2)}, u32[]{:S(2)}) %collective-permute-start.5) | collective-permute-done | bytes 196640 | tf_op jit(solution)/shard_map/ppermute | solution.py:765
  12.8 1.3 %collective-permute-done.6.refs_10_ = f32[12,32,128]{2,1,0:T(8,128)S(1)} collective-permute-done((f32[12,32,128]{2,1,0:T(8,128)S(1)}, f32[12,32,128]{2,1,0:T(8,128)S(1)}, u32[]{:S(2)}, u32[]{:S(2)}) %collective-permute-start.6) | collective-permute-done | bytes 196640 | tf_op jit(solution)/shard_map/ppermute | solution.py:765
  14.1 2.3 %down.1 = (f32[6,32,640]{2,1,0:T(8,128)S(1)}, f32[26,32,384]{2,1,0:T(8,128)S(1)}, f32[24,32,256]{2,1,0:T(8,128)S(1)}, f32[3,32,128]{2,1,0:T(8,128)S(1)}, f32[5,3...) custom-call(s32[2]{0:T(128)S(1)} %pad_add_fusion.place, ...), custom_call_target="tpu_custom_call" | custom-call | flops 2875000064 | bytes 9225000 | tf_op jit(solution)/shard_map/down/pallas_call | solution.py:745
  16.4 6.6 %collective-permute-start.8 = (f32[5,32,128]{2,1,0:T(8,128)S(1)}, f32[5,32,128]{2,1,0:T(8,128)S(1)}, u32[]{:S(2)}, u32[]{:S(2)}) collective-permute-start(f32[5,32,128]{2,1,0:T(8,128)S(1)} %get-tuple-element.65), channel_id=1, source_target_pairs={{0,4},{2,6},{4,0},{6,2},{8,12},{10,14},{12,8},{14,10},{16,20},{18,... | collective-permute-start | bytes 245768 | tf_op jit(solution)/shard_map/ppermute | solution.py:791
  23.0 0.9 %collective-permute-start.9 = (f32[3,32,128]{2,1,0:T(8,128)S(1)}, f32[3,32,128]{2,1,0:T(8,128)S(1)}, u32[]{:S(2)}, u32[]{:S(2)}) collective-permute-start(f32[3,32,128]{2,1,0:T(8,128)S(1)} %get-tuple-element.64.refs_0_), channel_id=1, source_target_pairs={{0,6},{2,4},{4,2},{6,0},{8,14},{10,12},{12,10},{14,8},{16,22},{18,... | collective-permute-start | bytes 147464 | tf_op jit(solution)/shard_map/ppermute | solution.py:791
  24.0 0.6 %collective-permute-start.7 = (f32[3,32,128]{2,1,0:T(8,128)S(1)}, f32[3,32,128]{2,1,0:T(8,128)S(1)}, u32[]{:S(2)}, u32[]{:S(2)}) collective-permute-start(f32[3,32,128]{2,1,0:T(8,128)S(1)} %get-tuple-element.64.refs_0_), channel_id=1, source_target_pairs={{0,2},{2,0},{4,6},{6,4},{8,10},{10,8},{12,14},{14,12},{16,18},{18,... | collective-permute-start | bytes 147464 | tf_op jit(solution)/shard_map/ppermute | solution.py:791
  24.6 1.4 %collective-permute-start.18 = (f32[12,32,128]{2,1,0:T(8,128)S(1)}, f32[12,32,128]{2,1,0:T(8,128)S(1)}, u32[]{:S(2)}, u32[]{:S(2)}) collective-permute-start(f32[12,32,128]{2,1,0:T(8,128)S(1)} %get-tuple-element.71), channel_id=1, source_target_pairs={{0,2},{2,0},{4,6},{6,4},{8,10},{10,8},{12,14},{14,12},{16,18},{18,... | collective-permute-start | bytes 589832 | tf_op jit(solution)/shard_map/ppermute | solution.py:801
  26.0 2.5 %collective-permute-done.9.refs_3_ = f32[3,32,128]{2,1,0:T(8,128)S(1)} collective-permute-done((f32[3,32,128]{2,1,0:T(8,128)S(1)}, f32[3,32,128]{2,1,0:T(8,128)S(1)}, u32[]{:S(2)}, u32[]{:S(2)}) %collective-permute-start.9) | collective-permute-done | bytes 49184 | tf_op jit(solution)/shard_map/ppermute | solution.py:791
  28.6 0.7 %merge.1.refs_0_ = f32[7,32,128]{2,1,0:T(8,128)S(1)} custom-call(s32[2]{0:T(128)S(1)} %pad_add_fusion.place, f32[3,32,128]{2,1,0:T(8,128)S(1)} %get-tuple-element.64.refs_0_, f32[3,32,128]{2,1,0:T(8,128)S(1)} %collective-permute-done.7.refs_1_, f32[5,32,128]{2,1,0:T(8,128)S(1)} %collective-permute-done.8.refs_2_, ...), custom_call_target="tpu_custom_call" | custom-call | flops 1035000000 | bytes 3321000 | tf_op jit(solution)/shard_map/merge/pallas_call | solution.py:745
  29.3 4.3 %collective-permute-start.12 = (f32[7,32,128]{2,1,0:T(8,128)S(1)}, f32[7,32,128]{2,1,0:T(8,128)S(1)}, u32[]{:S(2)}, u32[]{:S(2)}) collective-permute-start(f32[7,32,128]{2,1,0:T(8,128)S(1)} %merge.1.refs_0_), channel_id=1, source_target_pairs={{0,24},{2,26},{4,28},{6,30},{8,16},{10,18},{12,20},{14,22},{16,8},... | collective-permute-start | bytes 344072 | tf_op jit(solution)/shard_map/ppermute | solution.py:791
  33.7 0.6 %collective-permute-start.10 = (f32[7,32,128]{2,1,0:T(8,128)S(1)}, f32[7,32,128]{2,1,0:T(8,128)S(1)}, u32[]{:S(2)}, u32[]{:S(2)}) collective-permute-start(f32[7,32,128]{2,1,0:T(8,128)S(1)} %merge.1.refs_0_), channel_id=1, source_target_pairs={{0,8},{2,10},{4,12},{6,14},{8,0},{10,2},{12,4},{14,6},{16,24},{18,... | collective-permute-start | bytes 344072 | tf_op jit(solution)/shard_map/ppermute | solution.py:791
  34.3 0.7 %collective-permute-start.13 = (f32[2,32,128]{2,1,0:T(8,128)S(1)}, f32[2,32,128]{2,1,0:T(8,128)S(1)}, u32[]{:S(2)}, u32[]{:S(2)}) collective-permute-start(f32[2,32,128]{2,1,0:T(8,128)S(1)} %get-tuple-element.66), channel_id=1, source_target_pairs={{4,8},{8,4},{6,10},{10,6},{12,16},{16,12},{14,18},{18,14},{20,24},... | collective-permute-start | bytes 98312 | tf_op jit(solution)/shard_map/ppermute | solution.py:801
  35.0 0.7 %collective-permute-start.19 = (f32[12,32,128]{2,1,0:T(8,128)S(1)}, f32[12,32,128]{2,1,0:T(8,128)S(1)}, u32[]{:S(2)}, u32[]{:S(2)}) collective-permute-start(f32[12,32,128]{2,1,0:T(8,128)S(1)} %get-tuple-element.74), channel_id=1, source_target_pairs={{2,4},{4,2},{6,8},{8,6},{10,12},{12,10},{14,16},{16,14},{18,20},{2... | collective-permute-start | bytes 589832 | tf_op jit(solution)/shard_map/ppermute | solution.py:801
  35.7 1.3 %collective-permute-done.12.refs_3_ = f32[7,32,128]{2,1,0:T(8,128)S(1)} collective-permute-done((f32[7,32,128]{2,1,0:T(8,128)S(1)}, f32[7,32,128]{2,1,0:T(8,128)S(1)}, u32[]{:S(2)}, u32[]{:S(2)}) %collective-permute-start.12) | collective-permute-done | bytes 114720 | tf_op jit(solution)/shard_map/ppermute | solution.py:791
  37.0 5.5 %collective-permute-done.11.refs_2_ = f32[7,32,128]{2,1,0:T(8,128)S(1)} collective-permute-done((f32[7,32,128]{2,1,0:T(8,128)S(1)}, f32[7,32,128]{2,1,0:T(8,128)S(1)}, u32[]{:S(2)}, u32[]{:S(2)}) %collective-permute-start.11) | collective-permute-done | bytes 114720 | tf_op jit(solution)/shard_map/ppermute | solution.py:791
  44.5 2.7 %coarse.1 = f32[3,32,128]{2,1,0:T(8,128)S(1)} custom-call(s32[2]{0:T(128)S(1)} %pad_add_fusion.place, f32[7,32,128]{2,1,0:T(8,128)S(1)} %merge.1.refs_0_, f32[7,32,128]{2,1,0:T(8,128)S(1)} %collective-permute-done.10.refs_1_, f32[7,32,128]{2,1,0:T(8,128)S(1)} %collective-permute-done.11.refs_2_, f32[7,32,128]{2,1,0:T(8,128)S(1)} %collective-permute-done.12.refs_3_, ...), custom_call_target="tpu_custom_call" | custom-call | flops 805000000 | bytes 2583000 | tf_op jit(solution)/shard_map/coarse/pallas_call | solution.py:745
  47.2 3.1 %up.1 = f32[32,8,512]{2,1,0:T(8,128)} custom-call(s32[2]{0:T(128)S(1)} %pad_add_fusion.place, f32[3,32,128]{2,1,0:T(8,128)S(1)} %coarse.1, f32[12,32,128]{2,1,0:T(8,128)S(1)} %collective-permute-done.18.refs_0_, f32[12,32,128]{2,1,0:T(8,128)S(1)} %collective-permute-done.19.refs_1_, f32[5,32,128]{2,1,0:T(8,128)S(1)} %collective-permute-done.8.refs_2_, ...), custom_call_target="tpu_custom_call" | custom-call | flops 3449999872 | bytes 11070000 | tf_op jit(solution)/shard_map/up/pallas_call | solution.py:745
  (30 shorter events, 4.1 us)
Async XLA Ops:
  0.1 1.0 %copy-start = (f32[32,8,512]{2,1,0:T(8,128)S(1)}, f32[32,8,512]{2,1,0:T(8,128)}, u32[]{:S(2)}) copy-start(f32[32,8,512]{2,1,0:T(8,128)} %conduct.1) | copy-start | bytes 1572868
  1.1 1.0 %copy-start.1 = (f32[32,8,512]{2,1,0:T(8,128)S(1)}, f32[32,8,512]{2,1,0:T(8,128)}, u32[]{:S(2)}) copy-start(f32[32,8,512]{2,1,0:T(8,128)} %binding.1) | copy-start | bytes 1572868
  2.2 4.2 %copy-start.2 = (f32[32,8,512]{2,1,0:T(8,128)S(1)}, f32[32,8,512]{2,1,0:T(8,128)}, u32[]{:S(2)}) copy-start(f32[32,8,512]{2,1,0:T(8,128)} %right_side.1) | copy-start | bytes 1572868
  3.3 7.9 %collective-permute-start.3 = (f32[12,32,128]{2,1,0:T(8,128)S(1)}, f32[12,32,128]{2,1,0:T(8,128)S(1)}, u32[]{:S(2)}, u32[]{:S(2)}) collective-permute-start(f32[12,32,128]{2,1,0:T(8,128)S(1)} %get-tuple-element.49), channel_id=1, source_target_pairs={{0,2},{2,0},{4,6},{6,4},{8,10},{10,8},{12,14},{14,12},{16,18},{18,... | collective-permute-start | bytes 589832 | tf_op jit(solution)/shard_map/ppermute | solution.py:801
  7.0 1.4 %collective-permute-start.2 = (f32[8,32,128]{2,1,0:T(8,128)S(1)}, f32[8,32,128]{2,1,0:T(8,128)S(1)}, u32[]{:S(2)}, u32[]{:S(2)}) collective-permute-start(f32[8,32,128]{2,1,0:T(8,128)S(1)} %get-tuple-element.48), channel_id=1, source_target_pairs={{0,1},{1,0},{2,3},{3,2},{4,5},{5,4},{6,7},{7,6},{8,9},{9,8},{10,11... | collective-permute-start | bytes 393224 | tf_op jit(solution)/shard_map/ppermute | solution.py:773
  7.1 1.5 %collective-permute-start = (f32[8,32,128]{2,1,0:T(8,128)S(1)}, f32[8,32,128]{2,1,0:T(8,128)S(1)}, u32[]{:S(2)}, u32[]{:S(2)}) collective-permute-start(f32[8,32,128]{2,1,0:T(8,128)S(1)} %get-tuple-element.46), channel_id=1, source_target_pairs={{0,1},{1,0},{2,3},{3,2},{4,5},{5,4},{6,7},{7,6},{8,9},{9,8},{10,11... | collective-permute-start | bytes 393224 | tf_op jit(solution)/shard_map/ppermute | solution.py:773
  7.6 1.3 %collective-permute-start.1 = (f32[8,32,128]{2,1,0:T(8,128)S(1)}, f32[8,32,128]{2,1,0:T(8,128)S(1)}, u32[]{:S(2)}, u32[]{:S(2)}) collective-permute-start(f32[8,32,128]{2,1,0:T(8,128)S(1)} %get-tuple-element.47), channel_id=1, source_target_pairs={{0,1},{1,0},{2,3},{3,2},{4,5},{5,4},{6,7},{7,6},{8,9},{9,8},{10,11... | collective-permute-start | bytes 393224 | tf_op jit(solution)/shard_map/ppermute | solution.py:773
  7.6 3.6 %collective-permute-start.4 = (f32[12,32,128]{2,1,0:T(8,128)S(1)}, f32[12,32,128]{2,1,0:T(8,128)S(1)}, u32[]{:S(2)}, u32[]{:S(2)}) collective-permute-start(f32[12,32,128]{2,1,0:T(8,128)S(1)} %get-tuple-element.56), channel_id=1, source_target_pairs={{2,4},{4,2},{6,8},{8,6},{10,12},{12,10},{14,16},{16,14},{18,20},{2... | collective-permute-start | bytes 589832 | tf_op jit(solution)/shard_map/ppermute | solution.py:801
  11.2 1.4 %collective-permute-start.5 = (f32[12,32,128]{2,1,0:T(8,128)S(1)}, f32[12,32,128]{2,1,0:T(8,128)S(1)}, u32[]{:S(2)}, u32[]{:S(2)}) collective-permute-start(f32[12,32,128]{2,1,0:T(8,128)S(1)} %collective-permute-done.3.refs_7_), channel_id=1, source_target_pairs={{0,1},{1,0},{2,3},{3,2},{4,5},{5,4},{6,7},{7,6},{8,9},{9,8},{10,11... | collective-permute-start | bytes 589832 | tf_op jit(solution)/shard_map/ppermute | solution.py:765
  12.7 1.4 %collective-permute-start.6 = (f32[12,32,128]{2,1,0:T(8,128)S(1)}, f32[12,32,128]{2,1,0:T(8,128)S(1)}, u32[]{:S(2)}, u32[]{:S(2)}) collective-permute-start(f32[12,32,128]{2,1,0:T(8,128)S(1)} %collective-permute-done.4.refs_8_), channel_id=1, source_target_pairs={{0,1},{1,0},{2,3},{3,2},{4,5},{5,4},{6,7},{7,6},{8,9},{9,8},{10,11... | collective-permute-start | bytes 589832 | tf_op jit(solution)/shard_map/ppermute | solution.py:765
  16.4 12.2 %collective-permute-start.8 = (f32[5,32,128]{2,1,0:T(8,128)S(1)}, f32[5,32,128]{2,1,0:T(8,128)S(1)}, u32[]{:S(2)}, u32[]{:S(2)}) collective-permute-start(f32[5,32,128]{2,1,0:T(8,128)S(1)} %get-tuple-element.65), channel_id=1, source_target_pairs={{0,4},{2,6},{4,0},{6,2},{8,12},{10,14},{12,8},{14,10},{16,20},{18,... | collective-permute-start | bytes 245768 | tf_op jit(solution)/shard_map/ppermute | solution.py:791
  23.0 5.5 %collective-permute-start.9 = (f32[3,32,128]{2,1,0:T(8,128)S(1)}, f32[3,32,128]{2,1,0:T(8,128)S(1)}, u32[]{:S(2)}, u32[]{:S(2)}) collective-permute-start(f32[3,32,128]{2,1,0:T(8,128)S(1)} %get-tuple-element.64.refs_0_), channel_id=1, source_target_pairs={{0,6},{2,4},{4,2},{6,0},{8,14},{10,12},{12,10},{14,8},{16,22},{18,... | collective-permute-start | bytes 147464 | tf_op jit(solution)/shard_map/ppermute | solution.py:791
  24.0 4.6 %collective-permute-start.7 = (f32[3,32,128]{2,1,0:T(8,128)S(1)}, f32[3,32,128]{2,1,0:T(8,128)S(1)}, u32[]{:S(2)}, u32[]{:S(2)}) collective-permute-start(f32[3,32,128]{2,1,0:T(8,128)S(1)} %get-tuple-element.64.refs_0_), channel_id=1, source_target_pairs={{0,2},{2,0},{4,6},{6,4},{8,10},{10,8},{12,14},{14,12},{16,18},{18,... | collective-permute-start | bytes 147464 | tf_op jit(solution)/shard_map/ppermute | solution.py:791
  24.6 10.4 %collective-permute-start.18 = (f32[12,32,128]{2,1,0:T(8,128)S(1)}, f32[12,32,128]{2,1,0:T(8,128)S(1)}, u32[]{:S(2)}, u32[]{:S(2)}) collective-permute-start(f32[12,32,128]{2,1,0:T(8,128)S(1)} %get-tuple-element.71), channel_id=1, source_target_pairs={{0,2},{2,0},{4,6},{6,4},{8,10},{10,8},{12,14},{14,12},{16,18},{18,... | collective-permute-start | bytes 589832 | tf_op jit(solution)/shard_map/ppermute | solution.py:801
  29.3 7.6 %collective-permute-start.12 = (f32[7,32,128]{2,1,0:T(8,128)S(1)}, f32[7,32,128]{2,1,0:T(8,128)S(1)}, u32[]{:S(2)}, u32[]{:S(2)}) collective-permute-start(f32[7,32,128]{2,1,0:T(8,128)S(1)} %merge.1.refs_0_), channel_id=1, source_target_pairs={{0,24},{2,26},{4,28},{6,30},{8,16},{10,18},{12,20},{14,22},{16,8},... | collective-permute-start | bytes 344072 | tf_op jit(solution)/shard_map/ppermute | solution.py:791
  33.7 8.8 %collective-permute-start.11 = (f32[7,32,128]{2,1,0:T(8,128)S(1)}, f32[7,32,128]{2,1,0:T(8,128)S(1)}, u32[]{:S(2)}, u32[]{:S(2)}) collective-permute-start(f32[7,32,128]{2,1,0:T(8,128)S(1)} %merge.1.refs_0_), channel_id=1, source_target_pairs={{0,16},{2,18},{4,20},{6,22},{8,24},{10,26},{12,28},{14,30},{16,0},... | collective-permute-start | bytes 344072 | tf_op jit(solution)/shard_map/ppermute | solution.py:791
  33.7 8.8 %collective-permute-start.10 = (f32[7,32,128]{2,1,0:T(8,128)S(1)}, f32[7,32,128]{2,1,0:T(8,128)S(1)}, u32[]{:S(2)}, u32[]{:S(2)}) collective-permute-start(f32[7,32,128]{2,1,0:T(8,128)S(1)} %merge.1.refs_0_), channel_id=1, source_target_pairs={{0,8},{2,10},{4,12},{6,14},{8,0},{10,2},{12,4},{14,6},{16,24},{18,... | collective-permute-start | bytes 344072 | tf_op jit(solution)/shard_map/ppermute | solution.py:791
  34.3 1.4 %collective-permute-start.13 = (f32[2,32,128]{2,1,0:T(8,128)S(1)}, f32[2,32,128]{2,1,0:T(8,128)S(1)}, u32[]{:S(2)}, u32[]{:S(2)}) collective-permute-start(f32[2,32,128]{2,1,0:T(8,128)S(1)} %get-tuple-element.66), channel_id=1, source_target_pairs={{4,8},{8,4},{6,10},{10,6},{12,16},{16,12},{14,18},{18,14},{20,24},... | collective-permute-start | bytes 98312 | tf_op jit(solution)/shard_map/ppermute | solution.py:801
  35.0 12.2 %collective-permute-start.19 = (f32[12,32,128]{2,1,0:T(8,128)S(1)}, f32[12,32,128]{2,1,0:T(8,128)S(1)}, u32[]{:S(2)}, u32[]{:S(2)}) collective-permute-start(f32[12,32,128]{2,1,0:T(8,128)S(1)} %get-tuple-element.74), channel_id=1, source_target_pairs={{2,4},{4,2},{6,8},{8,6},{10,12},{12,10},{14,16},{16,14},{18,20},{2... | collective-permute-start | bytes 589832 | tf_op jit(solution)/shard_map/ppermute | solution.py:801
  42.5 1.3 %collective-permute-start.14 = (f32[7,32,128]{2,1,0:T(8,128)S(1)}, f32[7,32,128]{2,1,0:T(8,128)S(1)}, u32[]{:S(2)}, u32[]{:S(2)}) collective-permute-start(f32[7,32,128]{2,1,0:T(8,128)S(1)} %merge.1.refs_0_), channel_id=1, source_target_pairs={{0,1},{1,0},{2,3},{3,2},{4,5},{5,4},{6,7},{7,6},{8,9},{9,8},{10,11... | collective-permute-start | bytes 344072 | tf_op jit(solution)/shard_map/ppermute | solution.py:765
  42.5 1.5 %collective-permute-start.15 = (f32[7,32,128]{2,1,0:T(8,128)S(1)}, f32[7,32,128]{2,1,0:T(8,128)S(1)}, u32[]{:S(2)}, u32[]{:S(2)}) collective-permute-start(f32[7,32,128]{2,1,0:T(8,128)S(1)} %collective-permute-done.10.refs_1_), channel_id=1, source_target_pairs={{0,1},{1,0},{2,3},{3,2},{4,5},{5,4},{6,7},{7,6},{8,9},{9,8},{10,11... | collective-permute-start | bytes 344072 | tf_op jit(solution)/shard_map/ppermute | solution.py:765
  43.0 1.3 %collective-permute-start.16 = (f32[7,32,128]{2,1,0:T(8,128)S(1)}, f32[7,32,128]{2,1,0:T(8,128)S(1)}, u32[]{:S(2)}, u32[]{:S(2)}) collective-permute-start(f32[7,32,128]{2,1,0:T(8,128)S(1)} %collective-permute-done.11.refs_2_), channel_id=1, source_target_pairs={{0,1},{1,0},{2,3},{3,2},{4,5},{5,4},{6,7},{7,6},{8,9},{9,8},{10,11... | collective-permute-start | bytes 344072 | tf_op jit(solution)/shard_map/ppermute | solution.py:765
  43.0 1.5 %collective-permute-start.17 = (f32[7,32,128]{2,1,0:T(8,128)S(1)}, f32[7,32,128]{2,1,0:T(8,128)S(1)}, u32[]{:S(2)}, u32[]{:S(2)}) collective-permute-start(f32[7,32,128]{2,1,0:T(8,128)S(1)} %collective-permute-done.12.refs_3_), channel_id=1, source_target_pairs={{0,1},{1,0},{2,3},{3,2},{4,5},{5,4},{6,7},{7,6},{8,9},{9,8},{10,11... | collective-permute-start | bytes 344072 | tf_op jit(solution)/shard_map/ppermute | solution.py:765

commit v23 on v19

--- a/solution.py
+++ b/solution.py
@@ -401,7 +401,7 @@
 
 
 def merge_kernel(sizes, stride, radix, place, *refs):
-    arrays, out, (source, conduct, binding) = refs[:radix], refs[radix], refs[radix + 1 :]
+    arrays, out, (source, conduct, binding) = refs[:radix][::-1], refs[radix], refs[radix + 1 :]
     merge_into(sizes, place, stride, radix, arrays, source, conduct, binding, 0)
     count = stride * radix
     rows = [source[row] for row in range(count + 2)]
@@ -876,7 +876,7 @@
             [(packing(3 * count + 2), *tile)],
             [(count + 2, *tile), (count, *tile), (count, *tile)],
             place,
-            blocks,
+            blocks[::-1],
         )
     stride, radix = plan[-1]
     blocks = swap(blocks, stride, radix)

time: 50.1 us -> 49.8 us (level)
  transfers between devices with their start and end apart: 20 -> 20, of which waited for: 13 -> 12; matrix products, arithmetic and copies ran while one was open for 0% -> 0% of each run, Pallas kernels for 12% -> 12%
where the time goes in v23:
time: 49.8 us; the launch traced here: 49.6 us
  starting transfers between devices  21.9 us (44%)
  waiting for transfers between devices  12.9 us (26%)
  Pallas kernels  12.5 us (25%)
  local copies, waits for them, and re-layouts  2.09 us (4%)
    ppermute x6, starting transfers between devices, swap(): lax.ppermute(others.get(step, value), 'span', [(device, device ^ step * s...  12.6 us
    pallas_call x7, Pallas kernels, call(): pl.pallas_call(body, name=name, out_shape=[jax.ShapeDtypeStruct(shape, f3...  12.5 us
    ppermute x6, waiting for transfers between devices, swap(): lax.ppermute(others.get(step, value), 'span', [(device, device ^ step * s...  9.39 us
    ppermute x5, starting transfers between devices, exchange(): lax.ppermute(value, 'span', route)  7.01 us
    ppermute x6, waiting for transfers between devices, beside(): lax.ppermute(value, 'width', [(0, 1), (1, 0)])  2.19 us
    unnamed x6, local copies, waits for them, and re-layouts  2.09 us
    ppermute x6, starting transfers between devices, beside(): lax.ppermute(value, 'width', [(0, 1), (1, 0)])  1.6 us
    ppermute x3, waiting for transfers between devices, edge_columns(): return [lax.ppermute(edges[0], 'width', [(0, 1), (1, 0)])]  1.27 us
  transfers between devices with their start and end apart: 20, of which 12 were waited for; matrix products, arithmetic and copies ran while one was open for 0% of the time, Pallas kernels for 12%

profile of v23, /device:TPU:0, one launch (start us, length us, event | category | flops | bytes accessed | tf_op | source)
XLA Modules:
  0.0 49.6 jit_solution(15968917714272041088)
XLA Ops:
  0.1 1.0 %copy-done = f32[32,8,512]{2,1,0:T(8,128)S(1)} copy-done((f32[32,8,512]{2,1,0:T(8,128)S(1)}, f32[32,8,512]{2,1,0:T(8,128)}, u32[]{:S(2)}) %copy-start) | copy-done | bytes 524312
  1.1 1.0 %copy-done.1 = f32[32,8,512]{2,1,0:T(8,128)S(1)} copy-done((f32[32,8,512]{2,1,0:T(8,128)S(1)}, f32[32,8,512]{2,1,0:T(8,128)}, u32[]{:S(2)}) %copy-start.1) | copy-done | bytes 524312
  2.2 1.1 %start.1 = (f32[2,8,32,512]{3,2,1,0:T(8,128)S(1)}, f32[8,32,256]{2,1,0:T(8,128)S(1)}, f32[4,32,128]{2,1,0:T(8,128)S(1)}, f32[12,32,128]{2,1,0:T(8,128)S(1)}, f32...) custom-call(s32[2]{0:T(128)S(1)} %pad_add_fusion.place, f32[32,8,512]{2,1,0:T(8,128)S(1)} %copy-done, ...), custom_call_target="tpu_custom_call" | custom-call | flops 1264999936 | bytes 4059000 | tf_op jit(solution)/shard_map/start/pallas_call | solution.py:745
  3.3 3.0 %collective-permute-start.3 = (f32[12,32,128]{2,1,0:T(8,128)S(1)}, f32[12,32,128]{2,1,0:T(8,128)S(1)}, u32[]{:S(2)}, u32[]{:S(2)}) collective-permute-start(f32[12,32,128]{2,1,0:T(8,128)S(1)} %get-tuple-element.48), channel_id=1, source_target_pairs={{0,2},{2,0},{4,6},{6,4},{8,10},{10,8},{12,14},{14,12},{16,18},{18,... | collective-permute-start | bytes 589832 | tf_op jit(solution)/shard_map/ppermute | solution.py:801
  6.3 0.7 %collective-permute-start.4 = (f32[12,32,128]{2,1,0:T(8,128)S(1)}, f32[12,32,128]{2,1,0:T(8,128)S(1)}, u32[]{:S(2)}, u32[]{:S(2)}) collective-permute-start(f32[12,32,128]{2,1,0:T(8,128)S(1)} %get-tuple-element.49), channel_id=1, source_target_pairs={{2,4},{4,2},{6,8},{8,6},{10,12},{12,10},{14,16},{16,14},{18,20},{2... | collective-permute-start | bytes 589832 | tf_op jit(solution)/shard_map/ppermute | solution.py:801
  7.0 0.7 %turn.1 = (f32[8,32,512]{2,1,0:T(8,128)S(1)}, f32[8,32,128]{2,1,0:T(8,128)S(1)}) custom-call(s32[2]{0:T(128)S(1)} %pad_add_fusion.place, f32[32,8,512]{2,1,0:T(8,128)S(1)} %copy-done.2), custom_call_target="tpu_custom_call" | custom-call | flops 805000000 | bytes 2583000 | tf_op jit(solution)/shard_map/turn/pallas_call | solution.py:745
  8.3 0.8 %collective-permute-done.2.refs_6_.refs_14_ = f32[8,32,128]{2,1,0:T(8,128)S(1)} collective-permute-done((f32[8,32,128]{2,1,0:T(8,128)S(1)}, f32[8,32,128]{2,1,0:T(8,128)S(1)}, u32[]{:S(2)}, u32[]{:S(2)}) %collective-permute-start.2) | collective-permute-done | bytes 131104 | tf_op jit(solution)/shard_map/ppermute | solution.py:773
  9.6 1.8 %inner.1 = (f32[8,32,128]{2,1,0:T(8,128)S(1)}, f32[4,32,128]{2,1,0:T(8,128)S(1)}, f32[35,32,640]{2,1,0:T(8,128)S(1)}, f32[17,32,384]{2,1,0:T(8,128)S(1)}, f32[5,32,256]{2,1,0:T(8,128)S(1)}) custom-call(s32[2]{0:T(128)S(1)} %pad_add_fusion.place, f32[2,8,32,512]{3,2,1,0:T(8,128)S(1)} %get-tuple-element.41.refs_0_.refs_10_, ...), custom_call_target="tpu_custom_call" | custom-call | flops 575000000 | bytes 1845000 | tf_op jit(solution)/shard_map/inner/pallas_call | solution.py:745
  12.0 0.9 %collective-permute-done.5.refs_9_ = f32[12,32,128]{2,1,0:T(8,128)S(1)} collective-permute-done((f32[12,32,128]{2,1,0:T(8,128)S(1)}, f32[12,32,128]{2,1,0:T(8,128)S(1)}, u32[]{:S(2)}, u32[]{:S(2)}) %collective-permute-start.5) | collective-permute-done | bytes 196640 | tf_op jit(solution)/shard_map/ppermute | solution.py:765
  13.2 2.3 %down.1 = (f32[6,32,640]{2,1,0:T(8,128)S(1)}, f32[26,32,384]{2,1,0:T(8,128)S(1)}, f32[24,32,256]{2,1,0:T(8,128)S(1)}, f32[3,32,128]{2,1,0:T(8,128)S(1)}, f32[5,3...) custom-call(s32[2]{0:T(128)S(1)} %pad_add_fusion.place, ...), custom_call_target="tpu_custom_call" | custom-call | flops 2875000064 | bytes 9225000 | tf_op jit(solution)/shard_map/down/pallas_call | solution.py:745
  15.5 5.5 %collective-permute-start.8 = (f32[5,32,128]{2,1,0:T(8,128)S(1)}, f32[5,32,128]{2,1,0:T(8,128)S(1)}, u32[]{:S(2)}, u32[]{:S(2)}) collective-permute-start(f32[5,32,128]{2,1,0:T(8,128)S(1)} %get-tuple-element.63), channel_id=1, source_target_pairs={{0,4},{2,6},{4,0},{6,2},{8,12},{10,14},{12,8},{14,10},{16,20},{18,... | collective-permute-start | bytes 245768 | tf_op jit(solution)/shard_map/ppermute | solution.py:791
  21.1 1.5 %collective-permute-start.9 = (f32[3,32,128]{2,1,0:T(8,128)S(1)}, f32[3,32,128]{2,1,0:T(8,128)S(1)}, u32[]{:S(2)}, u32[]{:S(2)}) collective-permute-start(f32[3,32,128]{2,1,0:T(8,128)S(1)} %get-tuple-element.62.refs_3_), channel_id=1, source_target_pairs={{0,2},{2,0},{4,6},{6,4},{8,10},{10,8},{12,14},{14,12},{16,18},{18,... | collective-permute-start | bytes 147464 | tf_op jit(solution)/shard_map/ppermute | solution.py:791
  22.6 1.1 %collective-permute-start.7 = (f32[3,32,128]{2,1,0:T(8,128)S(1)}, f32[3,32,128]{2,1,0:T(8,128)S(1)}, u32[]{:S(2)}, u32[]{:S(2)}) collective-permute-start(f32[3,32,128]{2,1,0:T(8,128)S(1)} %get-tuple-element.62.refs_3_), channel_id=1, source_target_pairs={{0,6},{2,4},{4,2},{6,0},{8,14},{10,12},{12,10},{14,8},{16,22},{18,... | collective-permute-start | bytes 147464 | tf_op jit(solution)/shard_map/ppermute | solution.py:791
  23.7 2.0 %collective-permute-start.18 = (f32[12,32,128]{2,1,0:T(8,128)S(1)}, f32[12,32,128]{2,1,0:T(8,128)S(1)}, u32[]{:S(2)}, u32[]{:S(2)}) collective-permute-start(f32[12,32,128]{2,1,0:T(8,128)S(1)} %get-tuple-element.69), channel_id=1, source_target_pairs={{0,2},{2,0},{4,6},{6,4},{8,10},{10,8},{12,14},{14,12},{16,18},{18,... | collective-permute-start | bytes 589832 | tf_op jit(solution)/shard_map/ppermute | solution.py:801
  25.7 2.5 %collective-permute-done.7.refs_0_ = f32[3,32,128]{2,1,0:T(8,128)S(1)} collective-permute-done((f32[3,32,128]{2,1,0:T(8,128)S(1)}, f32[3,32,128]{2,1,0:T(8,128)S(1)}, u32[]{:S(2)}, u32[]{:S(2)}) %collective-permute-start.7) | collective-permute-done | bytes 49184 | tf_op jit(solution)/shard_map/ppermute | solution.py:791
  28.2 0.7 %merge.1.refs_0_ = f32[7,32,128]{2,1,0:T(8,128)S(1)} custom-call(s32[2]{0:T(128)S(1)} %pad_add_fusion.place, f32[3,32,128]{2,1,0:T(8,128)S(1)} %collective-permute-done.7.refs_0_, f32[5,32,128]{2,1,0:T(8,128)S(1)} %collective-permute-done.8.refs_1_.refs_2_, f32[3,32,128]{2,1,0:T(8,128)S(1)} %collective-permute-done.9.refs_2_, ...), custom_call_target="tpu_custom_call" | custom-call | flops 1035000000 | bytes 3321000 | tf_op jit(solution)/shard_map/merge/pallas_call | solution.py:745
  28.9 3.3 %collective-permute-start.12 = (f32[7,32,128]{2,1,0:T(8,128)S(1)}, f32[7,32,128]{2,1,0:T(8,128)S(1)}, u32[]{:S(2)}, u32[]{:S(2)}) collective-permute-start(f32[7,32,128]{2,1,0:T(8,128)S(1)} %merge.1.refs_0_), channel_id=1, source_target_pairs={{0,24},{2,26},{4,28},{6,30},{8,16},{10,18},{12,20},{14,22},{16,8},... | collective-permute-start | bytes 344072 | tf_op jit(solution)/shard_map/ppermute | solution.py:791
  32.2 1.1 %collective-permute-start.10 = (f32[7,32,128]{2,1,0:T(8,128)S(1)}, f32[7,32,128]{2,1,0:T(8,128)S(1)}, u32[]{:S(2)}, u32[]{:S(2)}) collective-permute-start(f32[7,32,128]{2,1,0:T(8,128)S(1)} %merge.1.refs_0_), channel_id=1, source_target_pairs={{0,8},{2,10},{4,12},{6,14},{8,0},{10,2},{12,4},{14,6},{16,24},{18,... | collective-permute-start | bytes 344072 | tf_op jit(solution)/shard_map/ppermute | solution.py:791
  33.4 0.7 %collective-permute-start.13 = (f32[2,32,128]{2,1,0:T(8,128)S(1)}, f32[2,32,128]{2,1,0:T(8,128)S(1)}, u32[]{:S(2)}, u32[]{:S(2)}) collective-permute-start(f32[2,32,128]{2,1,0:T(8,128)S(1)} %get-tuple-element.64), channel_id=1, source_target_pairs={{4,8},{8,4},{6,10},{10,6},{12,16},{16,12},{14,18},{18,14},{20,24},... | collective-permute-start | bytes 98312 | tf_op jit(solution)/shard_map/ppermute | solution.py:801
  34.0 0.7 %collective-permute-start.19 = (f32[12,32,128]{2,1,0:T(8,128)S(1)}, f32[12,32,128]{2,1,0:T(8,128)S(1)}, u32[]{:S(2)}, u32[]{:S(2)}) collective-permute-start(f32[12,32,128]{2,1,0:T(8,128)S(1)} %get-tuple-element.72), channel_id=1, source_target_pairs={{2,4},{4,2},{6,8},{8,6},{10,12},{12,10},{14,16},{16,14},{18,20},{2... | collective-permute-start | bytes 589832 | tf_op jit(solution)/shard_map/ppermute | solution.py:801
  34.7 1.2 %collective-permute-done.12.refs_3_ = f32[7,32,128]{2,1,0:T(8,128)S(1)} collective-permute-done((f32[7,32,128]{2,1,0:T(8,128)S(1)}, f32[7,32,128]{2,1,0:T(8,128)S(1)}, u32[]{:S(2)}, u32[]{:S(2)}) %collective-permute-start.12) | collective-permute-done | bytes 114720 | tf_op jit(solution)/shard_map/ppermute | solution.py:791
  35.9 5.8 %collective-permute-done.11.refs_2_ = f32[7,32,128]{2,1,0:T(8,128)S(1)} collective-permute-done((f32[7,32,128]{2,1,0:T(8,128)S(1)}, f32[7,32,128]{2,1,0:T(8,128)S(1)}, u32[]{:S(2)}, u32[]{:S(2)}) %collective-permute-start.11) | collective-permute-done | bytes 114720 | tf_op jit(solution)/shard_map/ppermute | solution.py:791
  43.7 2.7 %coarse.1 = f32[3,32,128]{2,1,0:T(8,128)S(1)} custom-call(s32[2]{0:T(128)S(1)} %pad_add_fusion.place, f32[7,32,128]{2,1,0:T(8,128)S(1)} %merge.1.refs_0_, f32[7,32,128]{2,1,0:T(8,128)S(1)} %collective-permute-done.10.refs_1_, f32[7,32,128]{2,1,0:T(8,128)S(1)} %collective-permute-done.11.refs_2_, f32[7,32,128]{2,1,0:T(8,128)S(1)} %collective-permute-done.12.refs_3_, ...), custom_call_target="tpu_custom_call" | custom-call | flops 805000000 | bytes 2583000 | tf_op jit(solution)/shard_map/coarse/pallas_call | solution.py:745
  46.4 3.1 %up.1 = f32[32,8,512]{2,1,0:T(8,128)} custom-call(s32[2]{0:T(128)S(1)} %pad_add_fusion.place, f32[3,32,128]{2,1,0:T(8,128)S(1)} %coarse.1, f32[12,32,128]{2,1,0:T(8,128)S(1)} %collective-permute-done.18.refs_0_, f32[12,32,128]{2,1,0:T(8,128)S(1)} %collective-permute-done.19.refs_1_, f32[5,32,128]{2,1,0:T(8,128)S(1)} %collective-permute-done.8.refs_1_.refs_2_, ...), custom_call_target="tpu_custom_call" | custom-call | flops 3449999872 | bytes 11070000 | tf_op jit(solution)/shard_map/up/pallas_call | solution.py:745
  (30 shorter events, 4.1 us)
Async XLA Ops:
  0.1 1.0 %copy-start = (f32[32,8,512]{2,1,0:T(8,128)S(1)}, f32[32,8,512]{2,1,0:T(8,128)}, u32[]{:S(2)}) copy-start(f32[32,8,512]{2,1,0:T(8,128)} %conduct.1) | copy-start | bytes 1572868
  1.1 1.0 %copy-start.1 = (f32[32,8,512]{2,1,0:T(8,128)S(1)}, f32[32,8,512]{2,1,0:T(8,128)}, u32[]{:S(2)}) copy-start(f32[32,8,512]{2,1,0:T(8,128)} %binding.1) | copy-start | bytes 1572868
  2.2 4.8 %copy-start.2 = (f32[32,8,512]{2,1,0:T(8,128)S(1)}, f32[32,8,512]{2,1,0:T(8,128)}, u32[]{:S(2)}) copy-start(f32[32,8,512]{2,1,0:T(8,128)} %right_side.1) | copy-start | bytes 1572868
  3.3 8.1 %collective-permute-start.3 = (f32[12,32,128]{2,1,0:T(8,128)S(1)}, f32[12,32,128]{2,1,0:T(8,128)S(1)}, u32[]{:S(2)}, u32[]{:S(2)}) collective-permute-start(f32[12,32,128]{2,1,0:T(8,128)S(1)} %get-tuple-element.48), channel_id=1, source_target_pairs={{0,2},{2,0},{4,6},{6,4},{8,10},{10,8},{12,14},{14,12},{16,18},{18,... | collective-permute-start | bytes 589832 | tf_op jit(solution)/shard_map/ppermute | solution.py:801
  6.3 5.1 %collective-permute-start.4 = (f32[12,32,128]{2,1,0:T(8,128)S(1)}, f32[12,32,128]{2,1,0:T(8,128)S(1)}, u32[]{:S(2)}, u32[]{:S(2)}) collective-permute-start(f32[12,32,128]{2,1,0:T(8,128)S(1)} %get-tuple-element.49), channel_id=1, source_target_pairs={{2,4},{4,2},{6,8},{8,6},{10,12},{12,10},{14,16},{16,14},{18,20},{2... | collective-permute-start | bytes 589832 | tf_op jit(solution)/shard_map/ppermute | solution.py:801
  7.7 1.4 %collective-permute-start.2 = (f32[8,32,128]{2,1,0:T(8,128)S(1)}, f32[8,32,128]{2,1,0:T(8,128)S(1)}, u32[]{:S(2)}, u32[]{:S(2)}) collective-permute-start(f32[8,32,128]{2,1,0:T(8,128)S(1)} %get-tuple-element.47), channel_id=1, source_target_pairs={{0,1},{1,0},{2,3},{3,2},{4,5},{5,4},{6,7},{7,6},{8,9},{9,8},{10,11... | collective-permute-start | bytes 393224 | tf_op jit(solution)/shard_map/ppermute | solution.py:773
  7.7 1.5 %collective-permute-start = (f32[8,32,128]{2,1,0:T(8,128)S(1)}, f32[8,32,128]{2,1,0:T(8,128)S(1)}, u32[]{:S(2)}, u32[]{:S(2)}) collective-permute-start(f32[8,32,128]{2,1,0:T(8,128)S(1)} %get-tuple-element.45), channel_id=1, source_target_pairs={{0,1},{1,0},{2,3},{3,2},{4,5},{5,4},{6,7},{7,6},{8,9},{9,8},{10,11... | collective-permute-start | bytes 393224 | tf_op jit(solution)/shard_map/ppermute | solution.py:773
  8.2 1.3 %collective-permute-start.1 = (f32[8,32,128]{2,1,0:T(8,128)S(1)}, f32[8,32,128]{2,1,0:T(8,128)S(1)}, u32[]{:S(2)}, u32[]{:S(2)}) collective-permute-start(f32[8,32,128]{2,1,0:T(8,128)S(1)} %get-tuple-element.46), channel_id=1, source_target_pairs={{0,1},{1,0},{2,3},{3,2},{4,5},{5,4},{6,7},{7,6},{8,9},{9,8},{10,11... | collective-permute-start | bytes 393224 | tf_op jit(solution)/shard_map/ppermute | solution.py:773
  11.4 1.5 %collective-permute-start.5 = (f32[12,32,128]{2,1,0:T(8,128)S(1)}, f32[12,32,128]{2,1,0:T(8,128)S(1)}, u32[]{:S(2)}, u32[]{:S(2)}) collective-permute-start(f32[12,32,128]{2,1,0:T(8,128)S(1)} %collective-permute-done.3.refs_7_), channel_id=1, source_target_pairs={{0,1},{1,0},{2,3},{3,2},{4,5},{5,4},{6,7},{7,6},{8,9},{9,8},{10,11... | collective-permute-start | bytes 589832 | tf_op jit(solution)/shard_map/ppermute | solution.py:765
  11.7 1.5 %collective-permute-start.6 = (f32[12,32,128]{2,1,0:T(8,128)S(1)}, f32[12,32,128]{2,1,0:T(8,128)S(1)}, u32[]{:S(2)}, u32[]{:S(2)}) collective-permute-start(f32[12,32,128]{2,1,0:T(8,128)S(1)} %collective-permute-done.4.refs_8_), channel_id=1, source_target_pairs={{0,1},{1,0},{2,3},{3,2},{4,5},{5,4},{6,7},{7,6},{8,9},{9,8},{10,11... | collective-permute-start | bytes 589832 | tf_op jit(solution)/shard_map/ppermute | solution.py:765
  15.5 12.6 %collective-permute-start.8 = (f32[5,32,128]{2,1,0:T(8,128)S(1)}, f32[5,32,128]{2,1,0:T(8,128)S(1)}, u32[]{:S(2)}, u32[]{:S(2)}) collective-permute-start(f32[5,32,128]{2,1,0:T(8,128)S(1)} %get-tuple-element.63), channel_id=1, source_target_pairs={{0,4},{2,6},{4,0},{6,2},{8,12},{10,14},{12,8},{14,10},{16,20},{18,... | collective-permute-start | bytes 245768 | tf_op jit(solution)/shard_map/ppermute | solution.py:791
  21.1 4.6 %collective-permute-start.9 = (f32[3,32,128]{2,1,0:T(8,128)S(1)}, f32[3,32,128]{2,1,0:T(8,128)S(1)}, u32[]{:S(2)}, u32[]{:S(2)}) collective-permute-start(f32[3,32,128]{2,1,0:T(8,128)S(1)} %get-tuple-element.62.refs_3_), channel_id=1, source_target_pairs={{0,2},{2,0},{4,6},{6,4},{8,10},{10,8},{12,14},{14,12},{16,18},{18,... | collective-permute-start | bytes 147464 | tf_op jit(solution)/shard_map/ppermute | solution.py:791
  22.6 5.6 %collective-permute-start.7 = (f32[3,32,128]{2,1,0:T(8,128)S(1)}, f32[3,32,128]{2,1,0:T(8,128)S(1)}, u32[]{:S(2)}, u32[]{:S(2)}) collective-permute-start(f32[3,32,128]{2,1,0:T(8,128)S(1)} %get-tuple-element.62.refs_3_), channel_id=1, source_target_pairs={{0,6},{2,4},{4,2},{6,0},{8,14},{10,12},{12,10},{14,8},{16,22},{18,... | collective-permute-start | bytes 147464 | tf_op jit(solution)/shard_map/ppermute | solution.py:791
  23.7 10.3 %collective-permute-start.18 = (f32[12,32,128]{2,1,0:T(8,128)S(1)}, f32[12,32,128]{2,1,0:T(8,128)S(1)}, u32[]{:S(2)}, u32[]{:S(2)}) collective-permute-start(f32[12,32,128]{2,1,0:T(8,128)S(1)} %get-tuple-element.69), channel_id=1, source_target_pairs={{0,2},{2,0},{4,6},{6,4},{8,10},{10,8},{12,14},{14,12},{16,18},{18,... | collective-permute-start | bytes 589832 | tf_op jit(solution)/shard_map/ppermute | solution.py:801
  28.9 7.0 %collective-permute-start.12 = (f32[7,32,128]{2,1,0:T(8,128)S(1)}, f32[7,32,128]{2,1,0:T(8,128)S(1)}, u32[]{:S(2)}, u32[]{:S(2)}) collective-permute-start(f32[7,32,128]{2,1,0:T(8,128)S(1)} %merge.1.refs_0_), channel_id=1, source_target_pairs={{0,24},{2,26},{4,28},{6,30},{8,16},{10,18},{12,20},{14,22},{16,8},... | collective-permute-start | bytes 344072 | tf_op jit(solution)/shard_map/ppermute | solution.py:791
  32.2 9.4 %collective-permute-start.11 = (f32[7,32,128]{2,1,0:T(8,128)S(1)}, f32[7,32,128]{2,1,0:T(8,128)S(1)}, u32[]{:S(2)}, u32[]{:S(2)}) collective-permute-start(f32[7,32,128]{2,1,0:T(8,128)S(1)} %merge.1.refs_0_), channel_id=1, source_target_pairs={{0,16},{2,18},{4,20},{6,22},{8,24},{10,26},{12,28},{14,30},{16,0},... | collective-permute-start | bytes 344072 | tf_op jit(solution)/shard_map/ppermute | solution.py:791
  32.2 9.4 %collective-permute-start.10 = (f32[7,32,128]{2,1,0:T(8,128)S(1)}, f32[7,32,128]{2,1,0:T(8,128)S(1)}, u32[]{:S(2)}, u32[]{:S(2)}) collective-permute-start(f32[7,32,128]{2,1,0:T(8,128)S(1)} %merge.1.refs_0_), channel_id=1, source_target_pairs={{0,8},{2,10},{4,12},{6,14},{8,0},{10,2},{12,4},{14,6},{16,24},{18,... | collective-permute-start | bytes 344072 | tf_op jit(solution)/shard_map/ppermute | solution.py:791
  33.4 1.4 %collective-permute-start.13 = (f32[2,32,128]{2,1,0:T(8,128)S(1)}, f32[2,32,128]{2,1,0:T(8,128)S(1)}, u32[]{:S(2)}, u32[]{:S(2)}) collective-permute-start(f32[2,32,128]{2,1,0:T(8,128)S(1)} %get-tuple-element.64), channel_id=1, source_target_pairs={{4,8},{8,4},{6,10},{10,6},{12,16},{16,12},{14,18},{18,14},{20,24},... | collective-permute-start | bytes 98312 | tf_op jit(solution)/shard_map/ppermute | solution.py:801
  34.0 12.4 %collective-permute-start.19 = (f32[12,32,128]{2,1,0:T(8,128)S(1)}, f32[12,32,128]{2,1,0:T(8,128)S(1)}, u32[]{:S(2)}, u32[]{:S(2)}) collective-permute-start(f32[12,32,128]{2,1,0:T(8,128)S(1)} %get-tuple-element.72), channel_id=1, source_target_pairs={{2,4},{4,2},{6,8},{8,6},{10,12},{12,10},{14,16},{16,14},{18,20},{2... | collective-permute-start | bytes 589832 | tf_op jit(solution)/shard_map/ppermute | solution.py:801
  41.7 1.3 %collective-permute-start.14 = (f32[7,32,128]{2,1,0:T(8,128)S(1)}, f32[7,32,128]{2,1,0:T(8,128)S(1)}, u32[]{:S(2)}, u32[]{:S(2)}) collective-permute-start(f32[7,32,128]{2,1,0:T(8,128)S(1)} %merge.1.refs_0_), channel_id=1, source_target_pairs={{0,1},{1,0},{2,3},{3,2},{4,5},{5,4},{6,7},{7,6},{8,9},{9,8},{10,11... | collective-permute-start | bytes 344072 | tf_op jit(solution)/shard_map/ppermute | solution.py:765
  41.7 1.5 %collective-permute-start.15 = (f32[7,32,128]{2,1,0:T(8,128)S(1)}, f32[7,32,128]{2,1,0:T(8,128)S(1)}, u32[]{:S(2)}, u32[]{:S(2)}) collective-permute-start(f32[7,32,128]{2,1,0:T(8,128)S(1)} %collective-permute-done.10.refs_1_), channel_id=1, source_target_pairs={{0,1},{1,0},{2,3},{3,2},{4,5},{5,4},{6,7},{7,6},{8,9},{9,8},{10,11... | collective-permute-start | bytes 344072 | tf_op jit(solution)/shard_map/ppermute | solution.py:765
  42.2 1.3 %collective-permute-start.16 = (f32[7,32,128]{2,1,0:T(8,128)S(1)}, f32[7,32,128]{2,1,0:T(8,128)S(1)}, u32[]{:S(2)}, u32[]{:S(2)}) collective-permute-start(f32[7,32,128]{2,1,0:T(8,128)S(1)} %collective-permute-done.11.refs_2_), channel_id=1, source_target_pairs={{0,1},{1,0},{2,3},{3,2},{4,5},{5,4},{6,7},{7,6},{8,9},{9,8},{10,11... | collective-permute-start | bytes 344072 | tf_op jit(solution)/shard_map/ppermute | solution.py:765
  42.2 1.5 %collective-permute-start.17 = (f32[7,32,128]{2,1,0:T(8,128)S(1)}, f32[7,32,128]{2,1,0:T(8,128)S(1)}, u32[]{:S(2)}, u32[]{:S(2)}) collective-permute-start(f32[7,32,128]{2,1,0:T(8,128)S(1)} %collective-permute-done.12.refs_3_), channel_id=1, source_target_pairs={{0,1},{1,0},{2,3},{3,2},{4,5},{5,4},{6,7},{7,6},{8,9},{9,8},{10,11... | collective-permute-start | bytes 344072 | tf_op jit(solution)/shard_map/ppermute | solution.py:765
